TPU v7x, 32 devices: a whole 2x2x4 slice. The times are simulated.
32 devices in a mesh: groups: 2 (over x), cache: 8 (over z, y), serve: 2 (over core).
Axes of the slice: x: 2, y: 2, z: 4, core: 2. Of those that a mesh axis runs over, the one named last changes fastest.
Arguments:
- candidates: bfloat16 [128, 16, 1024], P(('groups', 'cache'), 'serve'), parts along dimension 0
- input_gain: bfloat16 [1024], replicated, may hold values from 0.5 to 1.5
- w_in: bfloat16 [1024, 4, 1024], P(None, None, 'serve'), may hold values from -0.1875 to 0.1875
- w_out: bfloat16 [1024, 1024], P('serve'), may hold values from -0.1875 to 0.1875
- hist_keys: bfloat16 [16, 2048, 1024], P(('groups', 'cache'), None, 'serve'), parts along dimension 0, may hold values from -6 to 6
- hist_values: bfloat16 [16, 2048, 1024], P(('groups', 'cache'), None, 'serve'), parts along dimension 0, may hold values from -0.59765625 to 0.59765625
- request_session: int32 [128, 1], P('groups'), parts along dimension 0, may hold values from 0 to 7; in each aligned block of 8 rows (0 to 7, 8 to 15, ...) at most 2 rows name the same one
- hist_len: int32 [16], P('groups'), parts along dimension 0, may hold values from 1 to 2048, as said below
- block_mask: int32 [128, 32], P('groups'), parts along dimension 0, may hold values 0 or 1
Outputs:
- layer_out: bfloat16 [128, 16, 1024], P(('groups', 'cache'), 'serve'), parts along dimension 0
There are 2 independent parts, one for each index of `groups`. A program takes and returns all parts, laid end to end along the dimension named above; an argument that names none is the same for every part. Nothing has to cross between parts.
Inputs may be any that keep to these rules, and one draw needn't show every extreme that they name: `request_session`: among the 8 requests of one index of cache no session is named more than 2 times, and in some such block one session is named exactly 2 times. `hist_len`: some session has all 2048 rows valid.
All inputs are finite; a program needn't handle non-finite values.
Results may differ from a plain program's by a relative error of at most 0.005.
Values may be sent and summed in bfloat16 or wider, within the bound.
No kernel may reach another device: no remote copies, remote signals or barrier semaphores. Data moves between devices by JAX's collectives and lax.ppermute only.
A program may use at most 128 MiB of HBM per device.

v0:
```python
import jax
import jax.numpy as jnp
from jax import lax
from jax.sharding import PartitionSpec as P

HD = 128
BLK = 64
CAP = 2


def slot_table(matches):
    row_count = matches.shape[1]
    flags = matches.astype(jnp.int32)
    earlier = jnp.cumsum(flags, axis=1) - flags
    row_ids = jnp.arange(row_count, dtype=jnp.int32)
    locals_list = []
    valids_list = []
    for place in range(CAP):
        picked = flags * (earlier == place).astype(jnp.int32)
        locals_list.append(jnp.sum(picked * row_ids[None, :], axis=1))
        valids_list.append(jnp.sum(picked, axis=1))
    return (jnp.stack(locals_list, axis=1), jnp.stack(valids_list, axis=1))


def history_term(slot_queries, keys, values, visible):
    slot_count, cand_count, local_heads, head_size = slot_queries.shape
    hist_rows = keys.shape[0]
    block_span = max((size for size in range(1, min(hist_rows, 512) + 1) if hist_rows % size == 0))
    block_count = hist_rows // block_span
    score_scale = HD ** (-0.5)

    def one_block(block_index, running):
        row_start = block_index * block_span
        key_block = lax.dynamic_slice_in_dim(keys, row_start, block_span, 0).reshape(
            block_span, local_heads, HD
        )
        value_block = lax.dynamic_slice_in_dim(values, row_start, block_span, 0).reshape(
            block_span, local_heads, HD
        )
        visible_block = lax.dynamic_slice_in_dim(visible, row_start, block_span, 1)
        scores = (
            jnp.einsum(
                "schd,khd->shck", slot_queries, key_block, preferred_element_type=jnp.float32
            )
            * score_scale
        )
        weights = jnp.where(visible_block[:, None, None, :], jax.nn.silu(scores), 0.0).astype(
            jnp.bfloat16
        )
        return running + jnp.einsum(
            "shck,khd->schd", weights, value_block, preferred_element_type=jnp.float32
        )

    zeros_init = jnp.zeros(slot_queries.shape, jnp.float32)
    return lax.fori_loop(0, block_count, one_block, zeros_init)


def body(
    candidates,
    input_gain,
    w_in,
    w_out,
    hist_keys,
    hist_values,
    request_session,
    hist_len,
    block_mask,
):
    own_rows = candidates.astype(jnp.float32)
    mean_square = jnp.mean(own_rows * own_rows, axis=-1, keepdims=True)
    normed = (own_rows * lax.rsqrt(mean_square + 1e-06) * input_gain.astype(jnp.float32)).astype(
        jnp.bfloat16
    )
    gathered = lax.all_gather(normed, "serve", axis=1, tiled=True)
    req_count, cand_count, model_width = gathered.shape
    local_width = w_in.shape[2]
    local_heads = local_width // HD
    projected = jnp.dot(
        gathered.reshape(req_count * cand_count, model_width),
        w_in.reshape(model_width, 4 * local_width),
        preferred_element_type=jnp.float32,
    )
    activated = (
        jax.nn.silu(projected)
        .astype(jnp.bfloat16)
        .reshape(req_count, cand_count, 4, local_heads, HD)
    )
    queries = activated[:, :, 0]
    keys_self = activated[:, :, 1]
    values_self = activated[:, :, 2]
    gate_values = activated[:, :, 3]
    owner_count = lax.axis_size("cache")
    cache_place = lax.axis_index("cache")
    all_sessions = request_session[:, 0]
    own_sessions = lax.dynamic_slice_in_dim(all_sessions, cache_place * req_count, req_count, 0)
    flat_queries = queries.reshape(req_count, cand_count, local_width)
    block_sessions = all_sessions.reshape(owner_count, req_count)
    slot_local, slot_valid = slot_table(block_sessions == cache_place)
    slot_rows = (
        jnp.arange(owner_count, dtype=jnp.int32)[:, None] * req_count + slot_local
    ).reshape(owner_count * CAP)
    slot_live = slot_valid.reshape(owner_count * CAP) == 1
    all_queries = lax.all_gather(flat_queries, "cache", axis=0, tiled=True)
    slot_queries = jnp.take(all_queries, slot_rows, axis=0).reshape(
        owner_count * CAP, cand_count, local_heads, HD
    )
    hist_rows = hist_keys.shape[1]
    length_here = lax.dynamic_index_in_dim(hist_len, cache_place, 0, keepdims=False)
    slot_marks = jnp.take(block_mask, slot_rows, axis=0)
    positions = jnp.arange(hist_rows, dtype=jnp.int32)
    visible = (
        (positions[None, :] < length_here)
        & (jnp.repeat(slot_marks, BLK, axis=1) == 1)
        & slot_live[:, None]
    )
    slot_result = history_term(slot_queries, hist_keys[0], hist_values[0], visible)
    slot_result = slot_result.reshape(owner_count, CAP, cand_count, local_width)
    returned = lax.all_to_all(
        slot_result.astype(jnp.bfloat16), "cache", split_axis=0, concat_axis=0, tiled=True
    ).astype(slot_result.dtype)
    returned = returned.reshape(owner_count * CAP, cand_count, local_width)
    request_ids = jnp.arange(req_count, dtype=jnp.int32)
    same_before = (own_sessions[:, None] == own_sessions[None, :]) & (
        request_ids[None, :] < request_ids[:, None]
    )
    occurrence = jnp.sum(same_before.astype(jnp.int32), axis=1)
    attended = jnp.take(returned, own_sessions * CAP + occurrence, axis=0).reshape(
        req_count, cand_count, local_heads, HD
    )
    score_scale = HD ** (-0.5)
    self_score = (
        jnp.sum(queries.astype(jnp.float32) * keys_self.astype(jnp.float32), axis=-1, keepdims=True)
        * score_scale
    )
    attended = attended + jax.nn.silu(self_score) * values_self.astype(jnp.float32)
    level = lax.rsqrt(jnp.mean(attended * attended, axis=-1, keepdims=True) + 1e-06)
    mixed = (
        (attended * level * gate_values.astype(jnp.float32))
        .astype(jnp.bfloat16)
        .reshape(req_count * cand_count, local_width)
    )
    partial_out = jnp.dot(mixed, w_out, preferred_element_type=jnp.float32).reshape(
        req_count, cand_count, model_width
    )
    summed = lax.psum_scatter(
        partial_out.astype(jnp.bfloat16), "serve", scatter_dimension=1, tiled=True
    ).astype(jnp.float32)
    return (summed + own_rows).astype(jnp.bfloat16)


def solution(mesh):
    placed = (
        P(("groups", "cache"), "serve", None),
        P(),
        P(None, None, "serve"),
        P("serve", None),
        P(("groups", "cache"), None, "serve"),
        P(("groups", "cache"), None, "serve"),
        P("groups", None),
        P("groups"),
        P("groups", None),
    )
    return jax.shard_map(
        body,
        mesh=mesh,
        in_specs=placed,
        out_specs=P(("groups", "cache"), "serve", None),
        check_vma=False,
    )
```

profile of v0, /device:TPU:0, one launch (start us, length us, event | category | flops | bytes accessed | tf_op | source)
XLA Modules:
  0.0 116.8 jit_solution(13456846530133513794)
XLA Ops:
  6.5 3.7 %copy.73 = bf16[128,8,4,512]{3,1,2,0:T(8,128)(2,1)S(1)} copy(bf16[128,8,4,512]{3,2,1,0:T(4,128)(2,1)} %bitcast.107) | data formatting | bytes 8388608
  10.2 0.1 fusion.12
  10.4 0.1 fusion.14
  10.5 2.1 %all_gather.6 = bf16[8,16,1024]{2,1,0:T(8,128)(2,1)S(1)} all-gather(bf16[8,8,1024]{2,1,0:T(8,128)(2,1)S(1)} %fusion.14), channel_id=1, replica_groups=mesh['groups'=2,'cache'=8,'serve'=2] {'serve'}, dimensions={1}, use_global_device_ids=true | all-gather | bytes 393216 | tf_op jit(solution)/shard_map/all_gather | solution.py:74
  12.6 0.8 multiply_convert_fusion
  13.4 0.4 reshape.194
  13.8 1.0 slice_convert_fusion.1
  14.8 0.7 reshape_squeeze.4
  15.7 0.2 reduce_window_sum.11
  15.8 0.2 fusion.22
  16.4 0.6 gather_fusion
  17.0 0.1 broadcast_in_dim.84
  17.2 0.2 eq.98
  17.3 0.1 copy.61
  17.4 0.1 eq.100
  17.5 4.0 %copy.62 = bf16[1,2048,512]{1,2,0:T(8,128)(2,1)} copy(bf16[1,2048,512]{2,1,0:T(8,128)(2,1)} %param.15) | data formatting | bytes 4194304 | tf_op args[4]
  21.5 4.0 %copy.57 = bf16[1,2048,512]{1,2,0:T(8,128)(2,1)} copy(bf16[1,2048,512]{2,1,0:T(8,128)(2,1)} %param.16) | data formatting | bytes 4194304 | tf_op args[5]
  25.5 0.2 multiply_reduce_fusion
  25.7 0.1 copy.65
  25.8 0.7 dynamic_slice.29
  26.5 0.7 iota_compare_fusion
  27.2 0.6 divide_multiply_fusion
  27.8 0.7 and_and_fusion
  28.5 29.9 %all-gather.2.cloned.1.call-done = bf16[64,16,512]{2,1,0:T(8,128)(2,1)} async-done(((bf16[8,16,512]{2,1,0:T(8,128)(2,1)}), bf16[64,16,512]{2,1,0:T(8,128)(2,1)}) %all-gather.2.cloned.1.call-update) | async-done | bytes 1048592 | tf_op jit(solution)/shard_map/all_gather | solution.py:103
  58.4 1.8 %gather_fusion.1 = bf16[16,16,512]{2,1,0:T(8,128)(2,1)S(1)} fusion(bf16[64,16,512]{2,1,0:T(8,128)(2,1)} %all-gather.2.cloned.1.call-done, s32[1024]{0:T(1024)S(1)} %pad_clamp_fusion.1), kind=kCustom, calls=%fused_computation.1 | custom fusion | bytes 524352 | tf_op jit(solution)/shard_map/jit(_take)/gather | solution.py:104
  60.3 0.2 broadcast_select_fusion
  60.5 23.7 %while.14 = (s32[]{:T(128)}, f32[16,16,4,128]{3,1,0,2:T(8,128)}, bf16[2048,512]{0,1:T(8,128)(2,1)}, pred[16,2048]{1,0:T(8,128)(4,1)}, bf16[2048,512]{0,1:T(8,128...) while((s32[]{:T(128)}, f32[16,16,4,128]{3,1,0,2:T(8,128)}, ...), condition=%wide.region_8.9_spmd.clone, body=%wide.region_7.8_spmd.clone.sunk | while | flops 272367616 | bytes 8675493 | solution.py:55
  60.6 2.1 %constant_dynamic-slice_fusion.6 = (bf16[512,512]{0,1:T(8,128)(2,1)S(1)}, bf16[512,512]{0,1:T(8,128)(2,1)}) fusion(bf16[2048,512]{0,1:T(8,128)(2,1)} %get-tuple-element.254, s32[]{:T(128)S(6)} %select_n.100, bf16[2048,512]{0,1:T(8,128)(2,1)} %get-tuple-element.252), kind=kLoop, calls=%fused_computation.13.clone.1 | loop fusion | bytes 2097156 | tf_op jit(solution)/shard_map/while/body/eval_jaxpr/dynamic_slice | solution.py:34
  62.6 0.4 fusion.47
  63.1 0.7 constant_dynamic-slice_fusion.7
  63.8 2.6 %fusion.48 = f32[16,16,4,128]{3,1,0,2:T(8,128)} fusion(bf16[512,4,128,1]{0,2,3,1:T(8,128)(2,1)} %bitcast.105, f32[4,512,16,16]{1,3,2,0:T(8,128)S(1)} %bitcast.103, pred[16,512]{1,0:T(8,128)(4,1)S(1)} %constant_dynamic-slice_fusion.7, f32[16,16,4,128]{3,1,0,2:T(8,128)} %get-tuple-element.241, pred[]{:T(512)S(6)} %compare.3), kind=kOutput, calls=%fused_computation.11.clone.1 | convolution fusion | flops 138149888 | bytes 3678209 | tf_op jit(solution)/shard_map/while/body/eval_jaxpr/shck,khd->schd/dot_general | solution.py:50
  66.4 2.1 %constant_dynamic-slice_fusion.6 = (bf16[512,512]{0,1:T(8,128)(2,1)S(1)}, bf16[512,512]{0,1:T(8,128)(2,1)}) fusion(bf16[2048,512]{0,1:T(8,128)(2,1)} %get-tuple-element.254, s32[]{:T(128)S(6)} %select_n.100, bf16[2048,512]{0,1:T(8,128)(2,1)} %get-tuple-element.252), kind=kLoop, calls=%fused_computation.13.clone.1 | loop fusion | bytes 2097156 | tf_op jit(solution)/shard_map/while/body/eval_jaxpr/dynamic_slice | solution.py:34
  68.4 0.4 fusion.47
  68.9 0.7 constant_dynamic-slice_fusion.7
  69.6 2.8 %fusion.48 = f32[16,16,4,128]{3,1,0,2:T(8,128)} fusion(bf16[512,4,128,1]{0,2,3,1:T(8,128)(2,1)} %bitcast.105, f32[4,512,16,16]{1,3,2,0:T(8,128)S(1)} %bitcast.103, pred[16,512]{1,0:T(8,128)(4,1)S(1)} %constant_dynamic-slice_fusion.7, f32[16,16,4,128]{3,1,0,2:T(8,128)} %get-tuple-element.241, pred[]{:T(512)S(6)} %compare.3), kind=kOutput, calls=%fused_computation.11.clone.1 | convolution fusion | flops 138149888 | bytes 3678209 | tf_op jit(solution)/shard_map/while/body/eval_jaxpr/shck,khd->schd/dot_general | solution.py:50
  72.3 2.1 %constant_dynamic-slice_fusion.6 = (bf16[512,512]{0,1:T(8,128)(2,1)S(1)}, bf16[512,512]{0,1:T(8,128)(2,1)}) fusion(bf16[2048,512]{0,1:T(8,128)(2,1)} %get-tuple-element.254, s32[]{:T(128)S(6)} %select_n.100, bf16[2048,512]{0,1:T(8,128)(2,1)} %get-tuple-element.252), kind=kLoop, calls=%fused_computation.13.clone.1 | loop fusion | bytes 2097156 | tf_op jit(solution)/shard_map/while/body/eval_jaxpr/dynamic_slice | solution.py:34
  74.4 0.4 fusion.47
  74.8 0.7 constant_dynamic-slice_fusion.7
  75.5 2.8 %fusion.48 = f32[16,16,4,128]{3,1,0,2:T(8,128)} fusion(bf16[512,4,128,1]{0,2,3,1:T(8,128)(2,1)} %bitcast.105, f32[4,512,16,16]{1,3,2,0:T(8,128)S(1)} %bitcast.103, pred[16,512]{1,0:T(8,128)(4,1)S(1)} %constant_dynamic-slice_fusion.7, f32[16,16,4,128]{3,1,0,2:T(8,128)} %get-tuple-element.241, pred[]{:T(512)S(6)} %compare.3), kind=kOutput, calls=%fused_computation.11.clone.1 | convolution fusion | flops 138149888 | bytes 3678209 | tf_op jit(solution)/shard_map/while/body/eval_jaxpr/shck,khd->schd/dot_general | solution.py:50
  78.3 2.1 %constant_dynamic-slice_fusion.6 = (bf16[512,512]{0,1:T(8,128)(2,1)S(1)}, bf16[512,512]{0,1:T(8,128)(2,1)}) fusion(bf16[2048,512]{0,1:T(8,128)(2,1)} %get-tuple-element.254, s32[]{:T(128)S(6)} %select_n.100, bf16[2048,512]{0,1:T(8,128)(2,1)} %get-tuple-element.252), kind=kLoop, calls=%fused_computation.13.clone.1 | loop fusion | bytes 2097156 | tf_op jit(solution)/shard_map/while/body/eval_jaxpr/dynamic_slice | solution.py:34
  80.3 0.4 fusion.47
  80.8 0.7 constant_dynamic-slice_fusion.7
  81.5 2.8 %fusion.48 = f32[16,16,4,128]{3,1,0,2:T(8,128)} fusion(bf16[512,4,128,1]{0,2,3,1:T(8,128)(2,1)} %bitcast.105, f32[4,512,16,16]{1,3,2,0:T(8,128)S(1)} %bitcast.103, pred[16,512]{1,0:T(8,128)(4,1)S(1)} %constant_dynamic-slice_fusion.7, f32[16,16,4,128]{3,1,0,2:T(8,128)} %get-tuple-element.241, pred[]{:T(512)S(6)} %compare.3), kind=kOutput, calls=%fused_computation.11.clone.1 | convolution fusion | flops 138149888 | bytes 3678209 | tf_op jit(solution)/shard_map/while/body/eval_jaxpr/shck,khd->schd/dot_general | solution.py:50
  84.2 1.1 convert_element_type.103
  85.4 0.2 copy.64
  85.6 0.8 convert_element_type.104
  86.4 3.4 %all-to-all-start = ((bf16[8,2,16,512]{3,2,1,0:T(8,128)(2,1)}), bf16[8,2,16,512]{3,2,1,0:T(8,128)(2,1)S(1)}, u32[]{:S(2)}, u32[]{:S(2)}) async-start(bf16[8,2,16,512]{3,2,1,0:T(8,128)(2,1)} %convert_element_type.104), calls=%async_computation | async-start | bytes 524288 | tf_op jit(solution)/shard_map/all_to_all | solution.py:118
  90.0 0.1 copy.66
  90.1 0.1 reshape.200
  90.2 0.1 reshape.202
  90.3 0.2 mul.165
  90.5 0.1 mul.166
  90.6 0.2 convert_reduce_fusion
  90.9 7.2 %all-to-all-done = bf16[8,2,16,512]{3,2,1,0:T(8,128)(2,1)S(1)} async-done(((bf16[8,2,16,512]{3,2,1,0:T(8,128)(2,1)}), bf16[8,2,16,512]{3,2,1,0:T(8,128)(2,1)S(1)}, u32[]{:S(2)}, u32[]{:S(2)}) %all-to-all-start) | async-done | bytes 262176 | tf_op jit(solution)/shard_map/all_to_all | solution.py:118
  98.2 0.6 gather_fusion.2
  98.8 0.1 gather.20
  98.9 1.3 %fusion.18 = f32[8,16,4]{2,1,0:T(8,128)S(1)} fusion(f32[8,16,4,128]{3,2,1,0:T(4,128)S(1)} %gather.20, f32[8,16,4]{2,1,0:T(8,128)S(1)} %copy.66, pred[8]{0:T(512)(128)(4,1)S(1)} %get-tuple-element.182, bf16[8,16,4,4,128]{4,3,2,1,0:T(4,128)(2,1)} %copy-done.1), kind=kLoop, calls=%fused_computation.33 | loop fusion | flops 392704 | bytes 397320 | tf_op jit(solution)/shard_map/reduce_sum | solution.py:136
  100.2 0.2 mul.170
  100.4 0.1 mul.171
  100.5 0.4 fusion.28
  100.9 0.7 copy.74
  101.6 6.6 %reduce-scatter.4.cloned.1.call-done = bf16[8,8192]{1,0:T(8,128)(2,1)} async-done(((bf16[16,8192]{1,0:T(8,128)(2,1)}), bf16[8,8192]{1,0:T(8,128)(2,1)}) %reduce-scatter.4.cloned.1.call-update) | async-done | bytes 131088
  108.3 1.0 copy.79
  109.3 0.7 fusion.15
  (47 shorter events, 1.0 us)
Async XLA Ops:
  6.5 94.0 %copy-start = (bf16[512,1024]{1,0:T(8,128)(2,1)S(1)}, bf16[512,1024]{1,0:T(8,128)(2,1)}, u32[]{:S(2)}) copy-start(bf16[512,1024]{1,0:T(8,128)(2,1)} %param.14) | copy-start | bytes 3145732
  6.5 51.9 %all-gather.2.cloned.1.call-start = ((), (), s32[]{:S(2)}) async-start(), calls=%async_computation.2 | async-start | bytes 1179648 | tf_op jit(solution)/shard_map/all_gather | solution.py:103
  6.5 3.7 %copy-start.2 = (bf16[8,8,1024]{2,1,0:T(8,128)(2,1)S(1)}, bf16[8,8,1024]{2,1,0:T(8,128)(2,1)}, u32[]{:S(2)}) copy-start(bf16[8,8,1024]{2,1,0:T(8,128)(2,1)} %param.11) | copy-start | bytes 393220
  6.5 3.8 %copy-start.7 = (bf16[1024]{0:T(1024)(128)(2,1)S(1)}, bf16[1024]{0:T(1024)(128)(2,1)}, u32[]{:S(2)}) copy-start(bf16[1024]{0:T(1024)(128)(2,1)} %param.12) | copy-start | bytes 6148
  13.4 2.2 %copy-start.8 = (s32[64,1]{0,1:T(1,128)S(1)}, s32[64,1]{0,1:T(1,128)}, u32[]{:S(2)}) copy-start(s32[64,1]{0,1:T(1,128)} %param.17) | copy-start | bytes 772
  13.4 2.8 %copy-start.6 = (s32[64,32]{0,1:T(8,128)S(1)}, s32[64,32]{0,1:T(8,128)}, u32[]{:S(2)}) copy-start(s32[64,32]{0,1:T(8,128)} %param.19) | copy-start | bytes 24580
  13.8 11.7 %copy-start.1 = (bf16[8,16,4,4,128]{4,3,2,1,0:T(4,128)(2,1)}, bf16[8,16,4,4,128]{4,3,2,1,0:T(4,128)(2,1)S(1)}, u32[]{:S(2)}) copy-start(bf16[8,16,4,4,128]{4,3,2,1,0:T(4,128)(2,1)S(1)} %reshape.194) | copy-start | bytes 1572868
  21.5 4.3 %copy-start.9 = (s32[8]{0:T(128)S(1)}, s32[8]{0:T(128)}, u32[]{:S(2)}) copy-start(s32[8]{0:T(128)} %param.18) | copy-start | bytes 100
  84.2 5.7 %copy-start.5 = (f32[8,16,4]{1,0,2:T(8,128)S(1)}, f32[8,16,4]{1,0,2:T(8,128)}, u32[]{:S(2)}) copy-start(f32[8,16,4]{1,0,2:T(8,128)} %divide_multiply_fusion) | copy-start | bytes 6148
  84.2 5.8 %copy-start.4 = (f32[8,16,1,4,128]{4,3,2,1,0:T(4,128)S(1)}, f32[8,16,1,4,128]{4,3,2,1,0:T(4,128)}, u32[]{:S(2)}) copy-start(f32[8,16,1,4,128]{4,3,2,1,0:T(4,128)} %get-tuple-element.186) | copy-start | bytes 786436
  84.2 6.0 %copy-start.3 = (f32[8,16,1,4,128]{4,3,2,1,0:T(4,128)S(1)}, f32[8,16,1,4,128]{4,3,2,1,0:T(4,128)}, u32[]{:S(2)}) copy-start(f32[8,16,1,4,128]{4,3,2,1,0:T(4,128)} %get-tuple-element.187) | copy-start | bytes 786436
  86.4 11.7 %all-to-all-start = ((bf16[8,2,16,512]{3,2,1,0:T(8,128)(2,1)}), bf16[8,2,16,512]{3,2,1,0:T(8,128)(2,1)S(1)}, u32[]{:S(2)}, u32[]{:S(2)}) async-start(bf16[8,2,16,512]{3,2,1,0:T(8,128)(2,1)} %convert_element_type.104), calls=%async_computation | async-start | bytes 524288 | tf_op jit(solution)/shard_map/all_to_all | solution.py:118
  89.8 18.5 %reduce-scatter.4.cloned.1.call-start = ((), (), s32[]{:S(2)}) async-start(), calls=%async_computation.3 | async-start | bytes 393216
Sparse Core Ops, SparseCore 0:
  15.7 42.7 all-gather.1
  101.8 6.4 reduce-scatter.3
where the time goes:
time: 118 us; the launch traced here: 117 us
  waiting for transfers between devices  43.8 us (37%)
  local copies, waits for them, and re-layouts  32.4 us (27%)
  matrix products  13.8 us (12%)
  between operations  13.7 us (12%)
  other arithmetic  7.63 us (6%)
  starting transfers between devices  3.45 us (3%)
  blocking collectives  2.09 us (2%)
    all_gather x1, waiting for transfers between devices, body(): all_queries = lax.all_gather(flat_queries, 'cache', axis=0, tiled=True)  29.9 us
    unnamed x27, local copies, waits for them, and re-layouts  13.5 us
    dot_general x4, matrix products, one_block(): jnp.einsum('shck,khd->schd', weights, value_block, preferred_element_type...  10.9 us
    dynamic_slice x4, local copies, waits for them, and re-layouts, one_block(): lax.dynamic_slice_in_dim(keys, row_start, block_span, 0)  8.26 us
    all_to_all x1, waiting for transfers between devices, body(): lax.all_to_all(slot_result.astype(jnp.bfloat16), 'cache', split_axis=0, c...  7.19 us
    unnamed x3, waiting for transfers between devices  6.66 us
    all_to_all x1, starting transfers between devices, body(): lax.all_to_all(slot_result.astype(jnp.bfloat16), 'cache', split_axis=0, c...  3.41 us
    dynamic_slice x4, local copies, waits for them, and re-layouts, one_block(): visible_block = lax.dynamic_slice_in_dim(visible, row_start, block_span, 1)  2.82 us
  transfers between devices with their start and end apart: 3, of which 3 were waited for; matrix products, arithmetic and copies ran while one was open for 12% of the time, Pallas kernels for 0%

commit v1 on v0

v1 whole, which is shorter than its diff:
```python
import functools

import jax
import jax.numpy as jnp
from jax import lax
from jax.experimental import pallas as pl
from jax.experimental.pallas import tpu as pltpu
from jax.sharding import PartitionSpec as P

HD = 128
BLK = 64
CAP = 2
EPS = 1e-06
SCALE = HD ** (-0.5)
HIDE = -1e30
VMEM_LIMIT = 48 * 1024 * 1024

vmem = pl.BlockSpec(memory_space=pltpu.VMEM)
smem = pl.BlockSpec(memory_space=pltpu.SMEM)


def silu(x):
    half = x * 0.5
    return half + half * jnp.tanh(half)


def kernel_call(body, out_shape, in_specs, scratch_shapes=(), flops=0, moved=0):
    return pl.pallas_call(
        body,
        out_shape=out_shape,
        in_specs=in_specs,
        out_specs=jax.tree.map(lambda _: vmem, out_shape),
        scratch_shapes=scratch_shapes,
        cost_estimate=pl.CostEstimate(flops=flops, bytes_accessed=moved, transcendentals=0),
        compiler_params=pltpu.CompilerParams(vmem_limit_bytes=VMEM_LIMIT),
    )


def normed_rows(rows_ref, gain):
    rows = rows_ref[...].astype(jnp.float32)
    count, cands, width = rows.shape
    rows = rows.reshape(count * cands, width)
    mean_square = jnp.mean(rows * rows, axis=-1, keepdims=True)
    return (rows * lax.rsqrt(mean_square + EPS) * gain).astype(jnp.bfloat16)


def own_slots(sess_ref, req_count):
    base = lax.axis_index("cache") * req_count
    sessions = [sess_ref[base + request] for request in range(req_count)]
    slots = []
    for request in range(req_count):
        place = 0
        for earlier in range(request):
            place = place + (sessions[earlier] == sessions[request]).astype(jnp.int32)
        slots.append((sessions[request], place))
    return slots


def query_kernel(sess_ref, own_ref, other_ref, gain_ref, wq_ref, slots_ref, queries_ref, normed_ref):
    req_count, half_cands, _ = own_ref.shape
    rows = req_count * half_cands
    gain = gain_ref[...].astype(jnp.float32)
    normed_ref[:rows, :] = normed_rows(own_ref, gain)
    normed_ref[rows:, :] = normed_rows(other_ref, gain)
    slots_ref[...] = jnp.zeros_like(slots_ref)
    queries = silu(jnp.dot(normed_ref[...], wq_ref[...], preferred_element_type=jnp.float32))
    queries_ref[...] = queries.astype(jnp.bfloat16)
    slots = own_slots(sess_ref, req_count)
    for request in range(req_count):
        session, place = slots[request]
        low = request * half_cands
        slot = jnp.concatenate([queries[low : low + half_cands], queries[rows + low : rows + low + half_cands]], axis=0)
        slots_ref[session * CAP + place] = slot.astype(jnp.bfloat16)


def self_kernel(
    sess_ref, len_ref, mask_ref, normed_ref, queries_ref, wkvu_ref,
    keep_ref, send_ref, hide_rows_ref, hide_cols_ref, seen_ref, marks_ref,
):
    rows2, width = queries_ref.shape
    rows = rows2 // 2
    normed = normed_ref[...]
    me = lax.axis_index("cache")
    keys = silu(jnp.dot(normed, wkvu_ref[0], preferred_element_type=jnp.float32)).astype(jnp.bfloat16)
    products = queries_ref[...].astype(jnp.float32) * keys.astype(jnp.float32)
    values = silu(jnp.dot(normed, wkvu_ref[1], preferred_element_type=jnp.float32)).astype(jnp.bfloat16)
    gates = silu(jnp.dot(normed, wkvu_ref[2], preferred_element_type=jnp.float32)).astype(jnp.bfloat16)
    for low in range(0, width, HD):
        score = jnp.sum(products[:, low : low + HD], axis=-1, keepdims=True) * SCALE
        own_term = (silu(score) * values[:, low : low + HD].astype(jnp.float32)).astype(jnp.bfloat16)
        keep_ref[0, :, low : low + HD] = own_term[:rows]
        send_ref[0, :, low : low + HD] = own_term[rows:]
    keep_ref[1] = gates[:rows]
    send_ref[1] = gates[rows:]

    owners = seen_ref.shape[0]
    requests, blocks = mask_ref.shape
    per_owner = requests // owners
    marks_ref[...] = jnp.zeros_like(marks_ref)
    lane = lax.broadcasted_iota(jnp.int32, (1, HD), 1)
    for owner in range(owners):
        seen_ref[owner] = 0

    def one_request(request, carry):
        owner = request // per_owner

        @pl.when(sess_ref[request] == me)
        def _():
            place = seen_ref[owner]
            seen_ref[owner] = place + 1
            marks_ref[pl.ds(owner * CAP + place, 1), :blocks] = mask_ref[pl.ds(request, 1), :]

        return carry

    lax.fori_loop(0, requests, one_request, 0)
    hidden = jnp.where(lane == blocks, 1.0, jnp.where(lane < blocks, 1.0 - marks_ref[...].astype(jnp.float32), 0.0))
    slots = owners * CAP
    per_slot = hide_rows_ref.shape[0] // slots
    hide_rows_ref[...] = (
        jnp.broadcast_to((hidden * HIDE)[:, None, :], (slots, per_slot, HD)).reshape(slots * per_slot, HD)
    ).astype(jnp.bfloat16)
    hist_rows = hide_cols_ref.shape[0]
    at_row = lax.broadcasted_iota(jnp.int32, (hist_rows, HD), 0)
    at_lane = lax.broadcasted_iota(jnp.int32, (hist_rows, HD), 1)
    length = len_ref[me]
    hide_cols_ref[...] = jnp.where(
        (at_lane == at_row // BLK) | ((at_lane == blocks) & (at_row >= length)), 1.0, 0.0
    ).astype(jnp.bfloat16)


def history_kernel(slots_ref, hide_rows_ref, hide_cols_ref, keys_ref, values_ref, out_ref):
    owners, rows_per_owner, width = slots_ref.shape
    hist_rows = keys_ref.shape[0]
    serve = lax.axis_index("serve")
    span = min(256, hist_rows)
    per_step = max(1, min(owners, 256 // rows_per_owner))
    rows = per_step * rows_per_owner
    half = rows_per_owner // CAP // 2

    def one_step(step):
        first = step * per_step
        queries = slots_ref[pl.ds(first, per_step)].reshape(rows, width)
        hide_rows = hide_rows_ref[pl.ds(pl.multiple_of(step * rows, rows), rows), :]
        for low in range(0, width, HD):
            lhs = jnp.concatenate([queries[:, low : low + HD], hide_rows], axis=1)
            total = None
            for start in range(0, hist_rows, span):
                rhs = jnp.concatenate(
                    [keys_ref[start : start + span, low : low + HD], hide_cols_ref[start : start + span, :]], axis=1
                )
                scores = lax.dot_general(lhs, rhs, (((1,), (1,)), ((), ())), preferred_element_type=jnp.float32)
                weights = silu(scores * SCALE).astype(jnp.bfloat16)
                term = jnp.dot(
                    weights, values_ref[start : start + span, low : low + HD], preferred_element_type=jnp.float32
                )
                total = term if total is None else total + term
            parts = total.reshape(per_step, CAP, 2, half, HD)
            for owner in range(per_step):
                own = parts[owner, :, 0].reshape(CAP * half, HD)
                other = parts[owner, :, 1].reshape(CAP * half, HD)
                out_ref[first + owner, 0, :, low : low + HD] = jnp.where(serve == 0, own, other).astype(jnp.bfloat16)
                out_ref[first + owner, 1, :, low : low + HD] = jnp.where(serve == 0, other, own).astype(jnp.bfloat16)

    if owners == per_step:
        one_step(0)
    else:
        pl.loop(0, owners // per_step)(one_step)


def output_kernel(sess_ref, own_ref, returned_ref, keep_ref, got_ref, w_own_ref, w_other_ref, out_ref):
    req_count, half_cands, model_width = own_ref.shape
    width = keep_ref.shape[2]
    slots = own_slots(sess_ref, req_count)
    serve = lax.axis_index("serve")
    picked = ([], [])
    for request in range(req_count):
        session, place = slots[request]
        halves = [returned_ref[session, side].astype(jnp.float32) for side in range(2)]
        for side in range(2):
            both = jnp.where(serve == side, halves[0], halves[1])
            rows = both[:half_cands]
            for at in range(1, CAP):
                rows = jnp.where(place == at, both[at * half_cands : (at + 1) * half_cands], rows)
            picked[side].append(rows)
    total = own_ref[...].astype(jnp.float32).reshape(req_count * half_cands, model_width)
    for side, (extra_ref, w_ref) in enumerate(((keep_ref, w_own_ref), (got_ref, w_other_ref))):
        attended = jnp.concatenate(picked[side], axis=0) + extra_ref[0].astype(jnp.float32)
        gates = extra_ref[1].astype(jnp.float32)
        mixed = []
        for low in range(0, width, HD):
            head = attended[:, low : low + HD]
            level = lax.rsqrt(jnp.mean(head * head, axis=-1, keepdims=True) + EPS)
            mixed.append((head * level * gates[:, low : low + HD]).astype(jnp.bfloat16))
        total = total + jnp.dot(jnp.concatenate(mixed, axis=1), w_ref[...], preferred_element_type=jnp.float32)
    out_ref[...] = total.reshape(req_count, half_cands, model_width).astype(jnp.bfloat16)


def body(candidates, input_gain, w_in, w_out, hist_keys, hist_values, request_session, hist_len, block_mask):
    owners = lax.axis_size("cache")
    req_count, half_cands, model_width = candidates.shape
    width = w_in.shape[2]
    cand_count = 2 * half_cands
    rows = req_count * half_cands
    hist_rows = hist_keys.shape[1]
    swap = [(0, 1), (1, 0)]
    bf16 = functools.partial(jax.ShapeDtypeStruct, dtype=jnp.bfloat16)
    sessions = request_session.reshape(-1)

    other = lax.ppermute(candidates, "serve", swap)
    slots, queries, normed = kernel_call(
        query_kernel,
        (bf16((owners * CAP, cand_count, width)), bf16((2 * rows, width)), bf16((2 * rows, model_width))),
        [smem, vmem, vmem, vmem, vmem],
        flops=4 * rows * model_width * width,
        moved=2 * model_width * width,
    )(sessions, candidates, other, input_gain.reshape(1, -1), w_in[:, 0, :])
    sent = lax.all_to_all(
        slots.reshape(owners, CAP * cand_count, width), "cache", split_axis=0, concat_axis=0, tiled=True
    )
    slot_rows = owners * CAP * cand_count
    keep, send, hide_rows, hide_cols = kernel_call(
        self_kernel,
        (bf16((2, rows, width)), bf16((2, rows, width)), bf16((slot_rows, HD)), bf16((hist_rows, HD))),
        [smem, smem, vmem, vmem, vmem, vmem],
        [pltpu.SMEM((owners,), jnp.int32), pltpu.VMEM((owners * CAP, HD), jnp.int32)],
        flops=12 * rows * model_width * width,
        moved=6 * model_width * width,
    )(sessions, hist_len, block_mask, normed, queries, jnp.transpose(w_in[:, 1:, :], (1, 0, 2)))
    got = lax.ppermute(send, "serve", swap)
    w_other = lax.ppermute(w_out, "serve", swap)
    attended = kernel_call(
        history_kernel,
        bf16((owners, 2, CAP * half_cands, width)),
        [vmem] * 5,
        flops=8 * slot_rows * hist_rows * width,
        moved=4 * hist_rows * width,
    )(sent, hide_rows, hide_cols, hist_keys.reshape(hist_rows, width), hist_values.reshape(hist_rows, width))
    returned = lax.all_to_all(
        attended.reshape(owners * 2, CAP * half_cands, width), ("cache", "serve"), split_axis=0, concat_axis=0, tiled=True
    ).reshape(owners, 2, CAP * half_cands, width)
    return kernel_call(
        output_kernel,
        bf16((req_count, half_cands, model_width)),
        [smem] + [vmem] * 6,
        flops=8 * rows * model_width * width,
        moved=4 * model_width * width,
    )(sessions, candidates, returned, keep, got, w_out, w_other)


def solution(mesh):
    placed = (
        P(("groups", "cache"), "serve", None),
        P(),
        P(None, None, "serve"),
        P("serve", None),
        P(("groups", "cache"), None, "serve"),
        P(("groups", "cache"), None, "serve"),
        P("groups", None),
        P("groups"),
        P("groups", None),
    )
    return jax.shard_map(
        body,
        mesh=mesh,
        in_specs=placed,
        out_specs=P(("groups", "cache"), "serve", None),
        check_vma=False,
    )
```

time: 118 us -> 57.8 us (0.49)
  waiting for transfers between devices: 43.8 us -> 9.57 us
  matrix products: 13.8 us -> 0 us
  between operations: 13.7 us -> 0.12 us
  Pallas kernels: 0 us -> 10.9 us
  starting transfers between devices: 3.45 us -> 14.1 us
  local copies, waits for them, and re-layouts: 32.4 us -> 22.4 us
  other arithmetic: 7.63 us -> 0 us
  blocking collectives: 2.09 us -> 0 us
    all_gather x1 -> x0, waiting for transfers between devices: 29.9 us -> none  [body(): all_queries = lax.all_gather(flat_queries, 'cache', axis=0, tiled=True)]
    dot_general x6 -> x0, matrix products: 12.1 us -> none  [the longest x4 10.9 us: one_block(): jnp.einsum('shck,khd->schd', weights, value_block, preferred_element_type...]
    dynamic_slice x9 -> x0, local copies, waits for them, and re-layouts: 11.8 us -> none  [the longest x4 8.26 us: one_block(): lax.dynamic_slice_in_dim(keys, row_start, block_span, 0)]
    pallas_call x0 -> x4, Pallas kernels: none -> 10.9 us  [the longest x1 3.89 us: body(): kernel_call(history_kernel, bf16((owners, 2, CAP * half_cands, width)), [...]
    all_to_all x1 -> x2, starting transfers between devices: 3.41 us -> 12.9 us  [the longest x1 6.85 us: body(): lax.all_to_all(slots.reshape(owners, CAP * cand_count, width), 'cache', s...]
    slice x0 -> x2, local copies, waits for them, and re-layouts: none -> 8.15 us  [the longest x1 4.53 us: body(): w_in[:, 1:, :]]
    unnamed x3 -> x0, waiting for transfers between devices: 6.66 us -> none
    gather x5 -> x0, local copies, waits for them, and re-layouts: 3.07 us -> none  [the longest x2 1.85 us: body(): jnp.take(all_queries, slot_rows, axis=0)]
  transfers between devices with their start and end apart: 3 -> 5, of which waited for: 3 -> 2; matrix products, arithmetic and copies ran while one was open for 12% -> 19% of each run, Pallas kernels for 0% -> 11%
where the time goes in v1:
time: 57.8 us; the launch traced here: 57 us
  local copies, waits for them, and re-layouts  22.4 us (39%)
  starting transfers between devices  14.1 us (24%)
  Pallas kernels  10.9 us (19%)
  waiting for transfers between devices  9.57 us (17%)
    unnamed x41, local copies, waits for them, and re-layouts  14.2 us
    all_to_all x1, waiting for transfers between devices, body(): lax.all_to_all(attended.reshape(owners * 2, CAP * half_cands, width), ('c...  8.58 us
    all_to_all x1, starting transfers between devices, body(): lax.all_to_all(slots.reshape(owners, CAP * cand_count, width), 'cache', s...  6.85 us
    all_to_all x1, starting transfers between devices, body(): lax.all_to_all(attended.reshape(owners * 2, CAP * half_cands, width), ('c...  6.01 us
    slice x1, local copies, waits for them, and re-layouts, body(): w_in[:, 1:, :]  4.53 us
    pallas_call x1, Pallas kernels, body(): kernel_call(history_kernel, bf16((owners, 2, CAP * half_cands, width)), [...  3.89 us
    slice x1, local copies, waits for them, and re-layouts, body(): w_in[:, 0, :]  3.63 us
    pallas_call x1, Pallas kernels, body(): kernel_call(output_kernel, bf16((req_count, half_cands, model_width)), [s...  2.8 us
  transfers between devices with their start and end apart: 5, of which 2 were waited for; matrix products, arithmetic and copies ran while one was open for 19% of the time, Pallas kernels for 11%

profile of v1, /device:TPU:0, one launch (start us, length us, event | category | flops | bytes accessed | tf_op | source)
XLA Modules:
  0.0 57.0 jit_solution(5251220884368560010)
XLA Ops:
  0.0 0.0 copy-start
  0.0 0.0 copy-start.18
  0.0 0.0 copy-start.8
  0.0 0.5 collective-permute-start
  0.5 3.6 %slice.6 = bf16[1024,1,512]{2,1,0:T(2,128)(2,1)S(1)} slice(bf16[1024,4,512]{2,1,0:T(4,128)(2,1)} %param.11), slice={[0:1024], [0:1], [0:512]} | slice | bytes 2097152 | tf_op jit(solution)/shard_map/slice | solution.py:216
  4.2 0.3 copy.18
  4.5 0.0 copy-done.18
  4.5 0.0 collective-permute-done.other_ref
  4.5 0.0 copy-done
  4.5 0.0 copy-done.8
  4.5 1.7 %shard_map.91 = (bf16[16,16,512]{2,1,0:T(8,128)(2,1)}, bf16[128,512]{1,0:T(8,128)(2,1)S(1)}, bf16[128,1024]{1,0:T(8,128)(2,1)S(1)}) custom-call(s32[64]{0:T(128)S(1)} %bitcast.15, bf16[8,8,1024]{2,1,0:T(8,128)(2,1)S(1)} %copy-done, bf16[8,8,1024]{2,1,0:T(8,128)(2,1)S(1)} %collective-permute-done.other_ref, bf16[1,1024]{1,0:T(2,128)(2,1)S(1)} %reshape.22.gain_ref, ...), custom_call_target="tpu_custom_call" | custom-call | flops 134217728 | bytes 1048576 | tf_op jit(solution)/shard_map/pallas_call | solution.py:210
  6.2 0.0 copy-start.1
  6.2 0.7 %copy-done.1 = bf16[128,1024]{1,0:T(8,128)(2,1)} copy-done((bf16[128,1024]{1,0:T(8,128)(2,1)}, bf16[128,1024]{1,0:T(8,128)(2,1)S(1)}, u32[]{:S(2)}) %copy-start.1) | copy-done | bytes 262168
  6.9 0.0 copy-start.6
  6.9 0.7 %copy-done.6 = bf16[128,512]{1,0:T(8,128)(2,1)} copy-done((bf16[128,512]{1,0:T(8,128)(2,1)}, bf16[128,512]{1,0:T(8,128)(2,1)S(1)}, u32[]{:S(2)}) %copy-start.6) | copy-done | bytes 131096
  7.5 6.9 %all-to-all-start = ((bf16[8,32,512]{2,1,0:T(8,128)(2,1)}), bf16[8,32,512]{2,1,0:T(8,128)(2,1)S(1)}, u32[]{:S(2)}, u32[]{:S(2)}) async-start(bf16[8,32,512]{2,1,0:T(8,128)(2,1)} %bitcast.2), calls=%async_computation | async-start | bytes 524288 | tf_op jit(solution)/shard_map/all_to_all | solution.py:217
  14.4 0.2 collective-permute-start.2
  14.6 4.5 %slice.7 = bf16[1024,3,512]{2,1,0:T(4,128)(2,1)S(1)} slice(bf16[1024,4,512]{2,1,0:T(4,128)(2,1)} %param.11), slice={[0:1024], [1:4], [0:512]} | slice | bytes 6291456 | tf_op jit(solution)/shard_map/slice | solution.py:228
  19.1 0.0 copy-start.9
  19.1 0.8 %copy.17 = bf16[1024,3,512]{2,0,1:T(8,128)(2,1)S(1)} copy(bf16[1024,3,512]{2,1,0:T(4,128)(2,1)S(1)} %slice.7) | data formatting | bytes 6291456
  19.9 1.4 %copy.12.mask_ref = s32[64,32]{1,0:T(8,128)} copy(s32[64,32]{0,1:T(8,128)} %param.17) | data formatting | bytes 16384 | tf_op args[8]
  21.3 0.0 copy-done.9
  21.3 0.0 copy-start.2
  21.3 0.9 %copy-done.2 = bf16[128,1024]{1,0:T(8,128)(2,1)S(1)} copy-done((bf16[128,1024]{1,0:T(8,128)(2,1)S(1)}, bf16[128,1024]{1,0:T(8,128)(2,1)}, u32[]{:S(2)}) %copy-start.2) | copy-done | bytes 262168
  22.3 0.0 copy-start.3
  22.3 0.8 %copy-done.3 = s32[64,32]{1,0:T(8,128)S(1)} copy-done((s32[64,32]{1,0:T(8,128)S(1)}, s32[64,32]{1,0:T(8,128)}, u32[]{:S(2)}) %copy-start.3) | copy-done | bytes 8216
  23.0 0.0 copy-start.7
  23.0 0.9 %copy-done.7 = bf16[128,512]{1,0:T(8,128)(2,1)S(1)} copy-done((bf16[128,512]{1,0:T(8,128)(2,1)S(1)}, bf16[128,512]{1,0:T(8,128)(2,1)}, u32[]{:S(2)}) %copy-start.7) | copy-done | bytes 131096
  23.9 2.5 %shard_map.92 = (bf16[2,64,512]{2,1,0:T(8,128)(2,1)S(1)}, bf16[2,64,512]{2,1,0:T(8,128)(2,1)S(1)}, bf16[256,128]{1,0:T(8,128)(2,1)S(1)}, bf16[2048,128]{1,0:T(8,128)(2,1)S(1)}) custom-call(s32[64]{0:T(128)S(1)} %bitcast.16, s32[8]{0:T(128)S(1)} %copy-done.9, s32[64,32]{1,0:T(8,128)S(1)} %copy-done.3, bf16[128,1024]{1,0:T(8,128)(2,1)S(1)} %copy-done.2, ...), custom_call_target="tpu_custom_call" | custom-call | flops 402653184 | bytes 3145728 | tf_op jit(solution)/shard_map/pallas_call | solution.py:221
  26.5 0.0 copy-start.4
  26.5 0.6 %copy-done.4 = bf16[2,64,512]{2,1,0:T(8,128)(2,1)} copy-done((bf16[2,64,512]{2,1,0:T(8,128)(2,1)}, bf16[2,64,512]{2,1,0:T(8,128)(2,1)S(1)}, u32[]{:S(2)}) %copy-start.4) | copy-done | bytes 131096
  27.1 0.0 copy-start.12
  27.1 0.8 %copy-done.12 = bf16[2048,128]{1,0:T(8,128)(2,1)} copy-done((bf16[2048,128]{1,0:T(8,128)(2,1)}, bf16[2048,128]{1,0:T(8,128)(2,1)S(1)}, u32[]{:S(2)}) %copy-start.12) | copy-done | bytes 524312
  27.9 0.0 copy-start.14
  27.9 0.6 %copy-done.14 = bf16[2,64,512]{2,1,0:T(8,128)(2,1)} copy-done((bf16[2,64,512]{2,1,0:T(8,128)(2,1)}, bf16[2,64,512]{2,1,0:T(8,128)(2,1)S(1)}, u32[]{:S(2)}) %copy-start.14) | copy-done | bytes 131096
  28.6 0.0 copy-start.16
  28.6 0.6 %copy-done.16 = bf16[256,128]{1,0:T(8,128)(2,1)} copy-done((bf16[256,128]{1,0:T(8,128)(2,1)}, bf16[256,128]{1,0:T(8,128)(2,1)S(1)}, u32[]{:S(2)}) %copy-start.16) | copy-done | bytes 65560
  29.2 0.0 all-to-all-done.slots_ref
  29.2 0.0 copy-start.10
  29.2 1.6 %copy-done.10 = bf16[1,2048,512]{2,1,0:T(8,128)(2,1)S(1)} copy-done((bf16[1,2048,512]{2,1,0:T(8,128)(2,1)S(1)}, bf16[1,2048,512]{2,1,0:T(8,128)(2,1)}, u32[]{:S(2)}) %copy-start.10) | copy-done | bytes 2097176
  30.8 0.0 copy-start.11
  30.8 1.6 %copy-done.11 = bf16[1,2048,512]{2,1,0:T(8,128)(2,1)S(1)} copy-done((bf16[1,2048,512]{2,1,0:T(8,128)(2,1)S(1)}, bf16[1,2048,512]{2,1,0:T(8,128)(2,1)}, u32[]{:S(2)}) %copy-start.11) | copy-done | bytes 2097176
  32.4 0.0 copy-start.13
  32.4 1.0 %copy-done.13 = bf16[2048,128]{1,0:T(8,128)(2,1)S(1)} copy-done((bf16[2048,128]{1,0:T(8,128)(2,1)S(1)}, bf16[2048,128]{1,0:T(8,128)(2,1)}, u32[]{:S(2)}) %copy-start.13) | copy-done | bytes 524312
  33.4 0.0 copy-start.17
  33.4 0.8 %copy-done.17 = bf16[256,128]{1,0:T(8,128)(2,1)S(1)} copy-done((bf16[256,128]{1,0:T(8,128)(2,1)S(1)}, bf16[256,128]{1,0:T(8,128)(2,1)}, u32[]{:S(2)}) %copy-start.17) | copy-done | bytes 65560
  34.3 0.0 copy-start.15
  34.3 0.0 copy-start.5
  34.3 3.9 %shard_map.93 = bf16[8,2,16,512]{3,2,1,0:T(8,128)(2,1)} custom-call(bf16[8,32,512]{2,1,0:T(8,128)(2,1)S(1)} %all-to-all-done.slots_ref, bf16[256,128]{1,0:T(8,128)(2,1)S(1)} %copy-done.17, bf16[2048,128]{1,0:T(8,128)(2,1)S(1)} %copy-done.13, bf16[2048,512]{1,0:T(8,128)(2,1)S(1)} %bitcast.18, bf16[2048,512]{1,0:T(8,128)(2,1)S(1)} %bitcast.19), custom_call_target="tpu_custom_call" | custom-call | flops 2147483648 | bytes 4194304 | tf_op jit(solution)/shard_map/pallas_call | solution.py:231
  38.2 6.0 %all-to-all-start.1 = ((bf16[16,16,512]{2,1,0:T(8,128)(2,1)}), bf16[16,16,512]{2,1,0:T(8,128)(2,1)S(1)}, u32[]{:S(2)}, u32[]{:S(2)}) async-start(bf16[16,16,512]{2,1,0:T(8,128)(2,1)} %bitcast.6), calls=%async_computation.1 | async-start | bytes 524288 | tf_op jit(solution)/shard_map/all_to_all | solution.py:238
  44.2 0.0 copy-done.15
  44.2 0.5 collective-permute-start.1
  44.7 1.0 %collective-permute-done.1.got_ref = bf16[2,64,512]{2,1,0:T(8,128)(2,1)S(1)} collective-permute-done((bf16[2,64,512]{2,1,0:T(8,128)(2,1)S(1)}, bf16[2,64,512]{2,1,0:T(8,128)(2,1)S(1)}, u32[]{:S(2)}, u32[]{:S(2)}) %collective-permute-start.1) | collective-permute-done | bytes 131104 | tf_op jit(solution)/shard_map/ppermute | solution.py:229
  45.7 0.0 collective-permute-done.2.w_other_ref
  45.7 8.6 %all-to-all-done.1 = bf16[16,16,512]{2,1,0:T(8,128)(2,1)S(1)} async-done(((bf16[16,16,512]{2,1,0:T(8,128)(2,1)}), bf16[16,16,512]{2,1,0:T(8,128)(2,1)S(1)}, u32[]{:S(2)}, u32[]{:S(2)}) %all-to-all-start.1) | async-done | bytes 262176 | tf_op jit(solution)/shard_map/all_to_all | solution.py:238
  54.2 0.0 copy-done.5
  54.2 2.8 %shard_map.94 = bf16[8,8,1024]{2,1,0:T(8,128)(2,1)} custom-call(s32[64]{0:T(128)S(1)} %bitcast.17, bf16[8,8,1024]{2,1,0:T(8,128)(2,1)S(1)} %copy-done, bf16[8,2,16,512]{3,2,1,0:T(8,128)(2,1)S(1)} %bitcast.14, bf16[2,64,512]{2,1,0:T(8,128)(2,1)S(1)} %copy-done.5, bf16[2,64,512]{2,1,0:T(8,128)(2,1)S(1)} %collective-permute-done.1.got_ref, ...), custom_call_target="tpu_custom_call" | custom-call | flops 268435456 | bytes 2097152 | tf_op jit(solution)/shard_map/pallas_call | solution.py:241
  (1 shorter events, 0.0 us)
Async XLA Ops:
  0.0 4.5 %copy-start = (bf16[8,8,1024]{2,1,0:T(8,128)(2,1)S(1)}, bf16[8,8,1024]{2,1,0:T(8,128)(2,1)}, u32[]{:S(2)}) copy-start(bf16[8,8,1024]{2,1,0:T(8,128)(2,1)} %own_ref.3) | copy-start | bytes 393220
  0.0 4.4 %copy-start.18 = (bf16[1024]{0:T(1024)(128)(2,1)S(1)}, bf16[1024]{0:T(1024)(128)(2,1)}, u32[]{:S(2)}) copy-start(bf16[1024]{0:T(1024)(128)(2,1)} %param.10) | copy-start | bytes 6148
  0.0 4.5 %copy-start.8 = (s32[64,1]{0,1:T(1,128)S(1)}, s32[64,1]{0,1:T(1,128)}, u32[]{:S(2)}) copy-start(s32[64,1]{0,1:T(1,128)} %param.15) | copy-start | bytes 772
  0.0 4.5 %collective-permute-start = (bf16[8,8,1024]{2,1,0:T(8,128)(2,1)}, bf16[8,8,1024]{2,1,0:T(8,128)(2,1)S(1)}, u32[]{:S(2)}, u32[]{:S(2)}) collective-permute-start(bf16[8,8,1024]{2,1,0:T(8,128)(2,1)} %own_ref.3), channel_id=1, source_target_pairs={{0,1},{1,0},{2,3},{3,2},{4,5},{5,4},{6,7},{7,6},{8,9},{9,8},{10,11... | collective-permute-start | bytes 393224 | tf_op jit(solution)/shard_map/ppermute | solution.py:209
  6.2 0.7 %copy-start.1 = (bf16[128,1024]{1,0:T(8,128)(2,1)}, bf16[128,1024]{1,0:T(8,128)(2,1)S(1)}, u32[]{:S(2)}) copy-start(bf16[128,1024]{1,0:T(8,128)(2,1)S(1)} %get-tuple-element.13.normed_ref) | copy-start | bytes 786436
  6.9 0.7 %copy-start.6 = (bf16[128,512]{1,0:T(8,128)(2,1)}, bf16[128,512]{1,0:T(8,128)(2,1)S(1)}, u32[]{:S(2)}) copy-start(bf16[128,512]{1,0:T(8,128)(2,1)S(1)} %get-tuple-element.14.queries_ref) | copy-start | bytes 393220
  7.5 21.7 %all-to-all-start = ((bf16[8,32,512]{2,1,0:T(8,128)(2,1)}), bf16[8,32,512]{2,1,0:T(8,128)(2,1)S(1)}, u32[]{:S(2)}, u32[]{:S(2)}) async-start(bf16[8,32,512]{2,1,0:T(8,128)(2,1)} %bitcast.2), calls=%async_computation | async-start | bytes 524288 | tf_op jit(solution)/shard_map/all_to_all | solution.py:217
  14.4 31.3 %collective-permute-start.2 = (bf16[512,1024]{1,0:T(8,128)(2,1)}, bf16[512,1024]{1,0:T(8,128)(2,1)}, u32[]{:S(2)}, u32[]{:S(2)}) collective-permute-start(bf16[512,1024]{1,0:T(8,128)(2,1)} %w_own_ref.1), channel_id=1, source_target_pairs={{0,1},{1,0},{2,3},{3,2},{4,5},{5,4},{6,7},{7,6},{8,9},{9,8},{10,11... | collective-permute-start | bytes 3145736 | tf_op jit(solution)/shard_map/ppermute | solution.py:230
  19.1 2.2 %copy-start.9 = (s32[8]{0:T(128)S(1)}, s32[8]{0:T(128)}, u32[]{:S(2)}) copy-start(s32[8]{0:T(128)} %len_ref.1) | copy-start | bytes 100
  21.3 1.0 %copy-start.2 = (bf16[128,1024]{1,0:T(8,128)(2,1)S(1)}, bf16[128,1024]{1,0:T(8,128)(2,1)}, u32[]{:S(2)}) copy-start(bf16[128,1024]{1,0:T(8,128)(2,1)} %copy-done.1) | copy-start | bytes 786436
  22.3 0.8 %copy-start.3 = (s32[64,32]{1,0:T(8,128)S(1)}, s32[64,32]{1,0:T(8,128)}, u32[]{:S(2)}) copy-start(s32[64,32]{1,0:T(8,128)} %copy.12.mask_ref) | copy-start | bytes 24580
  23.0 0.9 %copy-start.7 = (bf16[128,512]{1,0:T(8,128)(2,1)S(1)}, bf16[128,512]{1,0:T(8,128)(2,1)}, u32[]{:S(2)}) copy-start(bf16[128,512]{1,0:T(8,128)(2,1)} %copy-done.6) | copy-start | bytes 393220
  26.5 0.7 %copy-start.4 = (bf16[2,64,512]{2,1,0:T(8,128)(2,1)}, bf16[2,64,512]{2,1,0:T(8,128)(2,1)S(1)}, u32[]{:S(2)}) copy-start(bf16[2,64,512]{2,1,0:T(8,128)(2,1)S(1)} %get-tuple-element.17.keep_ref) | copy-start | bytes 393220
  27.1 0.8 %copy-start.12 = (bf16[2048,128]{1,0:T(8,128)(2,1)}, bf16[2048,128]{1,0:T(8,128)(2,1)S(1)}, u32[]{:S(2)}) copy-start(bf16[2048,128]{1,0:T(8,128)(2,1)S(1)} %get-tuple-element.16.hide_cols_ref) | copy-start | bytes 1572868
  27.9 0.7 %copy-start.14 = (bf16[2,64,512]{2,1,0:T(8,128)(2,1)}, bf16[2,64,512]{2,1,0:T(8,128)(2,1)S(1)}, u32[]{:S(2)}) copy-start(bf16[2,64,512]{2,1,0:T(8,128)(2,1)S(1)} %get-tuple-element.18) | copy-start | bytes 393220
  28.6 0.6 %copy-start.16 = (bf16[256,128]{1,0:T(8,128)(2,1)}, bf16[256,128]{1,0:T(8,128)(2,1)S(1)}, u32[]{:S(2)}) copy-start(bf16[256,128]{1,0:T(8,128)(2,1)S(1)} %get-tuple-element.15.hide_rows_ref) | copy-start | bytes 196612
  29.2 1.6 %copy-start.10 = (bf16[1,2048,512]{2,1,0:T(8,128)(2,1)S(1)}, bf16[1,2048,512]{2,1,0:T(8,128)(2,1)}, u32[]{:S(2)}) copy-start(bf16[1,2048,512]{2,1,0:T(8,128)(2,1)} %param.13) | copy-start | bytes 6291460
  30.8 1.6 %copy-start.11 = (bf16[1,2048,512]{2,1,0:T(8,128)(2,1)S(1)}, bf16[1,2048,512]{2,1,0:T(8,128)(2,1)}, u32[]{:S(2)}) copy-start(bf16[1,2048,512]{2,1,0:T(8,128)(2,1)} %param.14) | copy-start | bytes 6291460
  32.4 1.0 %copy-start.13 = (bf16[2048,128]{1,0:T(8,128)(2,1)S(1)}, bf16[2048,128]{1,0:T(8,128)(2,1)}, u32[]{:S(2)}) copy-start(bf16[2048,128]{1,0:T(8,128)(2,1)} %copy-done.12) | copy-start | bytes 1572868
  33.4 0.8 %copy-start.17 = (bf16[256,128]{1,0:T(8,128)(2,1)S(1)}, bf16[256,128]{1,0:T(8,128)(2,1)}, u32[]{:S(2)}) copy-start(bf16[256,128]{1,0:T(8,128)(2,1)} %copy-done.16) | copy-start | bytes 196612
  34.3 9.9 %copy-start.15 = (bf16[2,64,512]{2,1,0:T(8,128)(2,1)S(1)}, bf16[2,64,512]{2,1,0:T(8,128)(2,1)}, u32[]{:S(2)}) copy-start(bf16[2,64,512]{2,1,0:T(8,128)(2,1)} %copy-done.14) | copy-start | bytes 393220
  34.3 20.0 %copy-start.5 = (bf16[2,64,512]{2,1,0:T(8,128)(2,1)S(1)}, bf16[2,64,512]{2,1,0:T(8,128)(2,1)}, u32[]{:S(2)}) copy-start(bf16[2,64,512]{2,1,0:T(8,128)(2,1)} %copy-done.4) | copy-start | bytes 393220
  38.2 16.1 %all-to-all-start.1 = ((bf16[16,16,512]{2,1,0:T(8,128)(2,1)}), bf16[16,16,512]{2,1,0:T(8,128)(2,1)S(1)}, u32[]{:S(2)}, u32[]{:S(2)}) async-start(bf16[16,16,512]{2,1,0:T(8,128)(2,1)} %bitcast.6), calls=%async_computation.1 | async-start | bytes 524288 | tf_op jit(solution)/shard_map/all_to_all | solution.py:238
  44.2 1.5 %collective-permute-start.1 = (bf16[2,64,512]{2,1,0:T(8,128)(2,1)S(1)}, bf16[2,64,512]{2,1,0:T(8,128)(2,1)S(1)}, u32[]{:S(2)}, u32[]{:S(2)}) collective-permute-start(bf16[2,64,512]{2,1,0:T(8,128)(2,1)S(1)} %copy-done.15), channel_id=1, source_target_pairs={{0,1},{1,0},{2,3},{3,2},{4,5},{5,4},{6,7},{7,6},{8,9},{9,8},{10,11... | collective-permute-start | bytes 393224 | tf_op jit(solution)/shard_map/ppermute | solution.py:229

commit v2 on v1

v2 whole, which is shorter than its diff:
```python
import functools

import jax
import jax.numpy as jnp
from jax import lax
from jax.experimental import pallas as pl
from jax.experimental.pallas import tpu as pltpu
from jax.sharding import PartitionSpec as P

HD = 128
BLK = 64
CAP = 2
EPS = 1e-06
SCALE = HD ** (-0.5)
HIDE = -1e30
VMEM_LIMIT = 16 * 1024 * 1024

vmem = pl.BlockSpec(memory_space=pltpu.VMEM)
smem = pl.BlockSpec(memory_space=pltpu.SMEM)


def silu(x):
    half = x * 0.5
    return half + half * jnp.tanh(half)


def kernel_call(body, out_shape, in_specs, scratch_shapes=(), flops=0, moved=0):
    return pl.pallas_call(
        body,
        out_shape=out_shape,
        in_specs=in_specs,
        out_specs=jax.tree.map(lambda _: vmem, out_shape),
        scratch_shapes=scratch_shapes,
        cost_estimate=pl.CostEstimate(flops=flops, bytes_accessed=moved, transcendentals=0),
        compiler_params=pltpu.CompilerParams(vmem_limit_bytes=VMEM_LIMIT),
    )


def normed_rows(rows_ref, gain):
    rows = rows_ref[...].astype(jnp.float32)
    count, cands, width = rows.shape
    rows = rows.reshape(count * cands, width)
    mean_square = jnp.mean(rows * rows, axis=-1, keepdims=True)
    return (rows * lax.rsqrt(mean_square + EPS) * gain).astype(jnp.bfloat16)


def own_slots(sess_ref, req_count):
    me = lax.axis_index("cache")
    base = me * req_count
    sessions = [sess_ref[base + request] for request in range(req_count)]
    slots = []
    for request in range(req_count):
        place = 0
        for earlier in range(request):
            place = place + (sessions[earlier] == sessions[request]).astype(jnp.int32)
        slots.append((sessions[request] ^ me) * CAP + place)
    return slots


def query_kernel(sess_ref, own_ref, other_ref, gain_ref, w_ref, *refs):
    *slot_refs, queries_ref, normed_ref, table_ref = refs
    req_count, half_cands, _ = own_ref.shape
    rows = req_count * half_cands
    gain = gain_ref[...].astype(jnp.float32)
    normed_ref[:rows, :] = normed_rows(own_ref, gain)
    normed_ref[rows:, :] = normed_rows(other_ref, gain)
    table_ref[...] = jnp.zeros_like(table_ref)
    queries = silu(jnp.dot(normed_ref[...], w_ref[0], preferred_element_type=jnp.float32))
    queries_ref[...] = queries.astype(jnp.bfloat16)
    for request, slot in enumerate(own_slots(sess_ref, req_count)):
        low = request * half_cands
        both = jnp.concatenate([queries[low : low + half_cands], queries[rows + low : rows + low + half_cands]], axis=0)
        table_ref[slot] = both.astype(jnp.bfloat16)
    for distance, slot_ref in enumerate(slot_refs):
        slot_ref[...] = table_ref[distance * CAP : (distance + 1) * CAP].reshape(slot_ref.shape)


def self_kernel(sess_ref, len_ref, mask_ref, normed_ref, queries_ref, w_ref, own_ref, gates_ref, hide_rows_ref, hide_cols_ref, marks_ref):
    width = queries_ref.shape[1]
    normed = normed_ref[...]
    me = lax.axis_index("cache")
    keys = silu(jnp.dot(normed, w_ref[1], preferred_element_type=jnp.float32)).astype(jnp.bfloat16)
    products = queries_ref[...].astype(jnp.float32) * keys.astype(jnp.float32)
    values = silu(jnp.dot(normed, w_ref[2], preferred_element_type=jnp.float32)).astype(jnp.bfloat16)
    gates_ref[...] = silu(jnp.dot(normed, w_ref[3], preferred_element_type=jnp.float32)).astype(jnp.bfloat16)
    for low in range(0, width, HD):
        score = jnp.sum(products[:, low : low + HD], axis=-1, keepdims=True) * SCALE
        own_ref[:, low : low + HD] = silu(score) * values[:, low : low + HD].astype(jnp.float32)

    blocks, requests = mask_ref.shape
    owners = len_ref.shape[0]
    per_owner = requests // owners
    sessions = sess_ref[...]
    lane = lax.broadcasted_iota(jnp.int32, (1, requests), 1)
    place = jnp.zeros((1, requests), jnp.int32)
    for back in range(1, per_owner):
        same = (pltpu.roll(sessions, back, 1) == sessions) & (lane % per_owner >= back)
        place = place + same.astype(jnp.int32)
    slot_of = jnp.where(sessions == me, ((lane // per_owner) ^ me) * CAP + place, -1)
    slots = owners * CAP
    at_slot = lax.broadcasted_iota(jnp.int32, (slots, requests), 0)
    chosen = (at_slot == slot_of).astype(jnp.float32).astype(jnp.bfloat16)
    marks_ref[...] = jnp.zeros_like(marks_ref)
    marks_ref[:blocks, :] = mask_ref[...].astype(jnp.float32).astype(jnp.bfloat16)
    seen = lax.dot_general(chosen, marks_ref[...], (((1,), (1,)), ((), ())), preferred_element_type=jnp.float32)
    at_lane = lax.broadcasted_iota(jnp.int32, (slots, HD), 1)
    hidden = jnp.where(at_lane < blocks, (1.0 - seen) * HIDE, jnp.where(at_lane == blocks, HIDE, 0.0))
    per_slot = hide_rows_ref.shape[0] // slots
    hide_rows_ref[...] = (
        jnp.broadcast_to(hidden[:, None, :], (slots, per_slot, HD)).reshape(slots * per_slot, HD).astype(jnp.bfloat16)
    )
    hist_rows = hide_cols_ref.shape[0]
    at_row = lax.broadcasted_iota(jnp.int32, (hist_rows, HD), 0)
    at_lane = lax.broadcasted_iota(jnp.int32, (hist_rows, HD), 1)
    hide_cols_ref[...] = jnp.where(
        (at_lane == at_row // BLK) | ((at_lane == blocks) & (at_row >= len_ref[me])), 1.0, 0.0
    ).astype(jnp.bfloat16)


def history_kernel(owners, hide_rows_ref, hide_cols_ref, keys_ref, values_ref, *refs):
    slot_refs, out_refs = refs[:owners], refs[owners:]
    per_owner, width = slot_refs[0].shape
    hist_rows = keys_ref.shape[0]
    span = min(256, hist_rows)
    per_step = max(1, min(owners, 256 // per_owner))
    for first in range(0, owners, per_step):
        group = range(first, min(first + per_step, owners))
        queries = jnp.concatenate([slot_refs[at][...] for at in group], axis=0)
        hide_rows = hide_rows_ref[first * per_owner : first * per_owner + queries.shape[0], :]
        for low in range(0, width, HD):
            lhs = jnp.concatenate([queries[:, low : low + HD], hide_rows], axis=1)
            total = None
            for start in range(0, hist_rows, span):
                rhs = jnp.concatenate(
                    [keys_ref[start : start + span, low : low + HD], hide_cols_ref[start : start + span, :]], axis=1
                )
                scores = lax.dot_general(lhs, rhs, (((1,), (1,)), ((), ())), preferred_element_type=jnp.float32)
                weights = silu(scores * SCALE).astype(jnp.bfloat16)
                term = jnp.dot(
                    weights, values_ref[start : start + span, low : low + HD], preferred_element_type=jnp.float32
                )
                total = term if total is None else total + term
            total = total.astype(jnp.bfloat16)
            for place, at in enumerate(group):
                out_refs[at][:, low : low + HD] = total[place * per_owner : (place + 1) * per_owner]


def mix_kernel(owners, req_count, sess_ref, own_ref, gates_ref, *refs):
    back_refs, (keep_ref, send_ref, table_ref) = refs[:owners], refs[owners:]
    rows, width = keep_ref.shape
    half_cands = rows // req_count
    for distance, back_ref in enumerate(back_refs):
        table_ref[distance * CAP : (distance + 1) * CAP] = back_ref[...].reshape((CAP,) + table_ref.shape[1:])
    picked = [table_ref[slot].astype(jnp.float32) for slot in own_slots(sess_ref, req_count)]
    for side, out_ref in enumerate((keep_ref, send_ref)):
        history = jnp.concatenate([both[side * half_cands : (side + 1) * half_cands] for both in picked], axis=0)
        attended = history + own_ref[side * rows : (side + 1) * rows, :]
        gates = gates_ref[side * rows : (side + 1) * rows, :].astype(jnp.float32)
        for low in range(0, width, HD):
            head = attended[:, low : low + HD]
            level = lax.rsqrt(jnp.mean(head * head, axis=-1, keepdims=True) + EPS)
            out_ref[:, low : low + HD] = (head * level * gates[:, low : low + HD]).astype(jnp.bfloat16)


def output_kernel(own_ref, keep_ref, got_ref, w_own_ref, w_other_ref, out_ref):
    req_count, half_cands, model_width = own_ref.shape
    total = own_ref[...].astype(jnp.float32).reshape(req_count * half_cands, model_width)
    total = total + jnp.dot(keep_ref[...], w_own_ref[...], preferred_element_type=jnp.float32)
    total = total + jnp.dot(got_ref[...], w_other_ref[...], preferred_element_type=jnp.float32)
    out_ref[...] = total.reshape(req_count, half_cands, model_width).astype(jnp.bfloat16)


def exchange(pieces):
    count = len(pieces)
    return [pieces[0]] + [
        lax.ppermute(pieces[distance], "cache", [(place, place ^ distance) for place in range(count)])
        for distance in range(1, count)
    ]


def body(candidates, input_gain, w_in, w_out, hist_keys, hist_values, request_session, hist_len, block_mask):
    owners = lax.axis_size("cache")
    req_count, half_cands, model_width = candidates.shape
    width = w_in.shape[2]
    cand_count = 2 * half_cands
    rows = req_count * half_cands
    hist_rows = hist_keys.shape[1]
    blocks = block_mask.shape[1]
    swap = [(0, 1), (1, 0)]
    bf16 = functools.partial(jax.ShapeDtypeStruct, dtype=jnp.bfloat16)
    sessions = request_session.reshape(-1)
    piece = bf16((CAP * cand_count, width))
    table = pltpu.VMEM((owners * CAP, cand_count, width), jnp.bfloat16)

    other = lax.ppermute(candidates, "serve", swap)
    weights = jnp.transpose(w_in, (1, 0, 2))
    *pieces, queries, normed = kernel_call(
        query_kernel,
        [piece] * owners + [bf16((2 * rows, width)), bf16((2 * rows, model_width))],
        [smem, vmem, vmem, vmem, vmem],
        [table],
        flops=4 * rows * model_width * width,
        moved=2 * model_width * width,
    )(sessions, candidates, other, input_gain.reshape(1, -1), weights)
    slots = exchange(pieces)
    slot_rows = owners * CAP * cand_count
    own_term, gates, hide_rows, hide_cols = kernel_call(
        self_kernel,
        [
            jax.ShapeDtypeStruct((2 * rows, width), jnp.float32),
            bf16((2 * rows, width)),
            bf16((slot_rows, HD)),
            bf16((hist_rows, HD)),
        ],
        [vmem, smem, vmem, vmem, vmem, vmem],
        [pltpu.VMEM((HD, owners * req_count), jnp.bfloat16)],
        flops=12 * rows * model_width * width,
        moved=6 * model_width * width,
    )(request_session.reshape(1, -1), hist_len, block_mask.T, normed, queries, weights)
    w_other = lax.ppermute(w_out, "serve", swap)
    backs = exchange(
        kernel_call(
            functools.partial(history_kernel, owners),
            [piece] * owners,
            [vmem] * (4 + owners),
            flops=8 * slot_rows * hist_rows * width,
            moved=4 * hist_rows * width,
        )(hide_rows, hide_cols, hist_keys.reshape(hist_rows, width), hist_values.reshape(hist_rows, width), *slots)
    )
    keep, send = kernel_call(
        functools.partial(mix_kernel, owners, req_count),
        [bf16((rows, width))] * 2,
        [smem] + [vmem] * (2 + owners),
        [table],
    )(sessions, own_term, gates, *backs)
    got = lax.ppermute(send, "serve", swap)
    return kernel_call(
        output_kernel,
        bf16((req_count, half_cands, model_width)),
        [vmem] * 5,
        flops=8 * rows * model_width * width,
        moved=4 * model_width * width,
    )(candidates, keep, got, w_out, w_other)


def solution(mesh):
    placed = (
        P(("groups", "cache"), "serve", None),
        P(),
        P(None, None, "serve"),
        P("serve", None),
        P(("groups", "cache"), None, "serve"),
        P(("groups", "cache"), None, "serve"),
        P("groups", None),
        P("groups"),
        P("groups", None),
    )
    return jax.shard_map(
        body,
        mesh=mesh,
        in_specs=placed,
        out_specs=P(("groups", "cache"), "serve", None),
        check_vma=False,
    )
```

time: 57.8 us -> 42.6 us (0.74); the launches traced: 57 us -> 42.4 us
  local copies, waits for them, and re-layouts: 22.4 us -> 3.07 us
  starting transfers between devices: 14.1 us -> 22.6 us
  Pallas kernels: 10.9 us -> 7.74 us
  waiting for transfers between devices: 9.57 us -> 8.93 us
    ppermute x0 -> x14, starting transfers between devices: none -> 21.9 us  [exchange(): lax.ppermute(pieces[distance], 'cache', [(place, place ^ distance) for pl...]
    all_to_all x2 -> x0, starting transfers between devices: 12.9 us -> none  [the longest x1 6.85 us: body(): lax.all_to_all(slots.reshape(owners, CAP * cand_count, width), 'cache', s...]
    unnamed x41 -> x17, local copies, waits for them, and re-layouts: 14.2 us -> 3.06 us
    all_to_all x2 -> x0, waiting for transfers between devices: 8.58 us -> none  [the longest x1 8.58 us: body(): lax.all_to_all(attended.reshape(owners * 2, CAP * half_cands, width), ('c...]
    slice x2 -> x0, local copies, waits for them, and re-layouts: 8.15 us -> none  [the longest x1 4.53 us: body(): w_in[:, 1:, :]]
    ppermute x0 -> x14, waiting for transfers between devices: none -> 7.69 us  [exchange(): lax.ppermute(pieces[distance], 'cache', [(place, place ^ distance) for pl...]
    pallas_call x4 -> x5, Pallas kernels: 10.9 us -> 7.74 us  [the longest x1 3.2 us: body(): kernel_call(functools.partial(history_kernel, owners), [piece] * owners,...]
  transfers between devices with their start and end apart: 5 -> 17, of which waited for: 2 -> 5; matrix products, arithmetic and copies ran while one was open for 19% -> 7% of each run, Pallas kernels for 11% -> 16%
where the time goes in v2:
time: 42.6 us; the launch traced here: 42.4 us
  starting transfers between devices  22.6 us (53%)
  waiting for transfers between devices  8.93 us (21%)
  Pallas kernels  7.74 us (18%)
  local copies, waits for them, and re-layouts  3.07 us (7%)
    ppermute x14, starting transfers between devices, exchange(): lax.ppermute(pieces[distance], 'cache', [(place, place ^ distance) for pl...  21.9 us
    ppermute x14, waiting for transfers between devices, exchange(): lax.ppermute(pieces[distance], 'cache', [(place, place ^ distance) for pl...  7.69 us
    pallas_call x1, Pallas kernels, body(): kernel_call(functools.partial(history_kernel, owners), [piece] * owners,...  3.2 us
    unnamed x17, local copies, waits for them, and re-layouts  3.06 us
    pallas_call x1, Pallas kernels, body(): kernel_call(self_kernel, [jax.ShapeDtypeStruct((2 * rows, width), jnp.flo...  1.69 us
    ppermute x1, waiting for transfers between devices, body(): got = lax.ppermute(send, 'serve', swap)  1.24 us
    pallas_call x1, Pallas kernels, body(): kernel_call(output_kernel, bf16((req_count, half_cands, model_width)), [v...  1.14 us
    pallas_call x1, Pallas kernels, body(): kernel_call(query_kernel, [piece] * owners + [bf16((2 * rows, width)), bf...  0.98 us
  transfers between devices with their start and end apart: 17, of which 5 were waited for; matrix products, arithmetic and copies ran while one was open for 7% of the time, Pallas kernels for 16%

profile of v2, /device:TPU:0, one launch (start us, length us, event | category | flops | bytes accessed | tf_op | source)
XLA Modules:
  0.0 42.4 jit_solution(4291757490769100416)
XLA Ops:
  0.0 0.0 copy-start.1
  0.0 0.0 copy-start.7
  0.0 0.0 copy-start.3
  0.0 0.5 %collective-permute-start.16 = (bf16[512,1024]{1,0:T(8,128)(2,1)}, bf16[512,1024]{1,0:T(8,128)(2,1)S(1)}, u32[]{:S(2)}, u32[]{:S(2)}) collective-permute-start(bf16[512,1024]{1,0:T(8,128)(2,1)} %w_own_ref.1), channel_id=1, source_target_pairs={{0,1},{1,0},{2,3},{3,2},{4,5},{5,4},{6,7},{7,6},{8,9},{9,8},{10,11... | collective-permute-start | bytes 3145736 | tf_op jit(solution)/shard_map/ppermute | solution.py:220
  0.5 0.1 collective-permute-start
  0.6 3.0 %copy.12 = bf16[1024,4,512]{2,0,1:T(8,128)(2,1)S(1)} copy(bf16[1024,4,512]{2,1,0:T(4,128)(2,1)} %param.11) | data formatting | bytes 8388608 | tf_op args[2]
  3.6 0.0 copy-done.7
  3.6 0.0 copy-start.2
  3.7 0.0 copy-start.4
  3.7 0.0 collective-permute-done.other_ref
  3.7 0.0 copy-done.1
  3.7 0.0 copy-done.3
  3.7 0.0 copy-start.5
  3.7 0.0 copy-start.6
  3.7 1.0 %shard_map.91 = (bf16[32,512]{1,0:T(8,128)(2,1)S(1)}, bf16[32,512]{1,0:T(8,128)(2,1)S(1)}, bf16[32,512]{1,0:T(8,128)(2,1)S(1)}, bf16[32,512]{1,0:T(8,128)(2,1)S(...) custom-call(s32[64]{0:T(128)S(1)} %bitcast.11, ...), custom_call_target="tpu_custom_call" | custom-call | flops 134217728 | bytes 1048576 | tf_op jit(solution)/shard_map/pallas_call | solution.py:197
  4.7 3.0 %collective-permute-start.1 = (bf16[32,512]{1,0:T(8,128)(2,1)S(1)}, bf16[32,512]{1,0:T(8,128)(2,1)S(1)}, u32[]{:S(2)}, u32[]{:S(2)}) collective-permute-start(bf16[32,512]{1,0:T(8,128)(2,1)S(1)} %get-tuple-element.36), channel_id=1, source_target_pairs={{0,2},{2,0},{4,6},{6,4},{8,10},{10,8},{12,14},{14,12},{1,3},{3,1},... | collective-permute-start | bytes 98312 | tf_op jit(solution)/shard_map/ppermute | solution.py:176
  7.7 1.6 %collective-permute-start.2 = (bf16[32,512]{1,0:T(8,128)(2,1)S(1)}, bf16[32,512]{1,0:T(8,128)(2,1)S(1)}, u32[]{:S(2)}, u32[]{:S(2)}) collective-permute-start(bf16[32,512]{1,0:T(8,128)(2,1)S(1)} %get-tuple-element.37), channel_id=1, source_target_pairs={{0,4},{2,6},{4,0},{6,2},{8,12},{10,14},{12,8},{14,10},{1,5},{3,7},... | collective-permute-start | bytes 98312 | tf_op jit(solution)/shard_map/ppermute | solution.py:176
  9.3 0.0 collective-permute-start.3
  9.3 3.0 %collective-permute-start.4 = (bf16[32,512]{1,0:T(8,128)(2,1)S(1)}, bf16[32,512]{1,0:T(8,128)(2,1)S(1)}, u32[]{:S(2)}, u32[]{:S(2)}) collective-permute-start(bf16[32,512]{1,0:T(8,128)(2,1)S(1)} %get-tuple-element.39), channel_id=1, source_target_pairs={{0,8},{2,10},{4,12},{6,14},{8,0},{10,2},{12,4},{14,6},{1,9},{3,11}... | collective-permute-start | bytes 98312 | tf_op jit(solution)/shard_map/ppermute | solution.py:176
  12.3 0.0 collective-permute-done.1.refs_1_
  12.3 1.4 %collective-permute-start.5 = (bf16[32,512]{1,0:T(8,128)(2,1)S(1)}, bf16[32,512]{1,0:T(8,128)(2,1)S(1)}, u32[]{:S(2)}, u32[]{:S(2)}) collective-permute-start(bf16[32,512]{1,0:T(8,128)(2,1)S(1)} %get-tuple-element.40), channel_id=1, source_target_pairs={{0,10},{2,8},{4,14},{6,12},{8,2},{10,0},{12,6},{14,4},{1,11},{3,9}... | collective-permute-start | bytes 98312 | tf_op jit(solution)/shard_map/ppermute | solution.py:176
  13.7 0.0 collective-permute-done.2.refs_2_
  13.7 3.5 %collective-permute-start.6 = (bf16[32,512]{1,0:T(8,128)(2,1)S(1)}, bf16[32,512]{1,0:T(8,128)(2,1)S(1)}, u32[]{:S(2)}, u32[]{:S(2)}) collective-permute-start(bf16[32,512]{1,0:T(8,128)(2,1)S(1)} %get-tuple-element.41), channel_id=1, source_target_pairs={{0,12},{2,14},{4,8},{6,10},{8,4},{10,6},{12,0},{14,2},{1,13},{3,15... | collective-permute-start | bytes 98312 | tf_op jit(solution)/shard_map/ppermute | solution.py:176
  17.2 0.0 collective-permute-done.3.refs_3_
  17.2 0.3 collective-permute-start.7
  17.4 0.0 copy-done.2
  17.4 0.0 copy-done.4
  17.4 1.7 %shard_map.92 = (f32[128,512]{1,0:T(8,128)S(1)}, bf16[128,512]{1,0:T(8,128)(2,1)S(1)}, bf16[256,128]{1,0:T(8,128)(2,1)S(1)}, bf16[2048,128]{1,0:T(8,128)(2,1)S(1)}) custom-call(s32[1,64]{1,0:T(1,128)S(1)} %bitcast.12, s32[8]{0:T(128)S(1)} %copy-done.4, s32[32,64]{1,0:T(8,128)S(1)} %bitcast.10, bf16[128,1024]{1,0:T(8,128)(2,1)S(1)} %get-tuple-element.29.normed_ref, ...), custom_call_target="tpu_custom_call" | custom-call | flops 402653184 | bytes 3145728 | tf_op jit(solution)/shard_map/pallas_call | solution.py:207
  19.1 0.0 collective-permute-done.4.refs_4_
  19.2 0.0 collective-permute-done.5.refs_5_
  19.2 0.3 collective-permute-done.6.refs_6_
  19.4 4.4 %collective-permute-done.7.refs_7_ = bf16[32,512]{1,0:T(8,128)(2,1)S(1)} collective-permute-done((bf16[32,512]{1,0:T(8,128)(2,1)S(1)}, bf16[32,512]{1,0:T(8,128)(2,1)S(1)}, u32[]{:S(2)}, u32[]{:S(2)}) %collective-permute-start.7) | collective-permute-done | bytes 32800 | tf_op jit(solution)/shard_map/ppermute | solution.py:176
  23.8 0.0 copy-done.5
  23.8 0.0 copy-done.6
  23.8 0.0 copy-start
  23.8 3.2 %shard_map.93 = (bf16[32,512]{1,0:T(8,128)(2,1)S(1)}, bf16[32,512]{1,0:T(8,128)(2,1)S(1)}, bf16[32,512]{1,0:T(8,128)(2,1)S(1)}, bf16[32,512]{1,0:T(8,128)(2,1)S(...) custom-call(bf16[256,128]{1,0:T(8,128)(2,1)S(1)} %get-tuple-element., ...), custom_call_target="tpu_custom_call" | custom-call | flops 2147483648 | bytes 4194304 | tf_op jit(solution)/shard_map/pallas_call | solution.py:222
  27.0 0.1 collective-permute-start.10
  27.1 0.9 %collective-permute-start.11 = (bf16[32,512]{1,0:T(8,128)(2,1)S(1)}, bf16[32,512]{1,0:T(8,128)(2,1)S(1)}, u32[]{:S(2)}, u32[]{:S(2)}) collective-permute-start(bf16[32,512]{1,0:T(8,128)(2,1)S(1)} %get-tuple-element.47), channel_id=1, source_target_pairs={{0,8},{2,10},{4,12},{6,14},{8,0},{10,2},{12,4},{14,6},{1,9},{3,11}... | collective-permute-start | bytes 98312 | tf_op jit(solution)/shard_map/ppermute | solution.py:176
  28.0 2.0 %collective-permute-start.12 = (bf16[32,512]{1,0:T(8,128)(2,1)S(1)}, bf16[32,512]{1,0:T(8,128)(2,1)S(1)}, u32[]{:S(2)}, u32[]{:S(2)}) collective-permute-start(bf16[32,512]{1,0:T(8,128)(2,1)S(1)} %get-tuple-element.48), channel_id=1, source_target_pairs={{0,10},{2,8},{4,14},{6,12},{8,2},{10,0},{12,6},{14,4},{1,11},{3,9}... | collective-permute-start | bytes 98312 | tf_op jit(solution)/shard_map/ppermute | solution.py:176
  30.0 2.3 %collective-permute-start.13 = (bf16[32,512]{1,0:T(8,128)(2,1)S(1)}, bf16[32,512]{1,0:T(8,128)(2,1)S(1)}, u32[]{:S(2)}, u32[]{:S(2)}) collective-permute-start(bf16[32,512]{1,0:T(8,128)(2,1)S(1)} %get-tuple-element.49), channel_id=1, source_target_pairs={{0,12},{2,14},{4,8},{6,10},{8,4},{10,6},{12,0},{14,2},{1,13},{3,15... | collective-permute-start | bytes 98312 | tf_op jit(solution)/shard_map/ppermute | solution.py:176
  32.4 0.2 collective-permute-done.10.refs_3_
  32.6 2.2 %collective-permute-start.14 = (bf16[32,512]{1,0:T(8,128)(2,1)S(1)}, bf16[32,512]{1,0:T(8,128)(2,1)S(1)}, u32[]{:S(2)}, u32[]{:S(2)}) collective-permute-start(bf16[32,512]{1,0:T(8,128)(2,1)S(1)} %get-tuple-element.50), channel_id=1, source_target_pairs={{0,14},{2,12},{4,10},{6,8},{8,6},{10,4},{12,2},{14,0},{1,15},{3,13... | collective-permute-start | bytes 98312 | tf_op jit(solution)/shard_map/ppermute | solution.py:176
  34.8 0.0 collective-permute-done.11.refs_4_
  34.8 0.5 %collective-permute-start.8 = (bf16[32,512]{1,0:T(8,128)(2,1)S(1)}, bf16[32,512]{1,0:T(8,128)(2,1)S(1)}, u32[]{:S(2)}, u32[]{:S(2)}) collective-permute-start(bf16[32,512]{1,0:T(8,128)(2,1)S(1)} %get-tuple-element.44), channel_id=1, source_target_pairs={{0,2},{2,0},{4,6},{6,4},{8,10},{10,8},{12,14},{14,12},{1,3},{3,1},... | collective-permute-start | bytes 98312 | tf_op jit(solution)/shard_map/ppermute | solution.py:176
  35.3 0.0 collective-permute-done.12.refs_5_
  35.3 1.1 %collective-permute-start.9 = (bf16[32,512]{1,0:T(8,128)(2,1)S(1)}, bf16[32,512]{1,0:T(8,128)(2,1)S(1)}, u32[]{:S(2)}, u32[]{:S(2)}) collective-permute-start(bf16[32,512]{1,0:T(8,128)(2,1)S(1)} %get-tuple-element.45), channel_id=1, source_target_pairs={{0,4},{2,6},{4,0},{6,2},{8,12},{10,14},{12,8},{14,10},{1,5},{3,7},... | collective-permute-start | bytes 98312 | tf_op jit(solution)/shard_map/ppermute | solution.py:176
  36.4 0.0 collective-permute-done.13.refs_6_
  36.4 2.8 %collective-permute-done.14.refs_7_ = bf16[32,512]{1,0:T(8,128)(2,1)S(1)} collective-permute-done((bf16[32,512]{1,0:T(8,128)(2,1)S(1)}, bf16[32,512]{1,0:T(8,128)(2,1)S(1)}, u32[]{:S(2)}, u32[]{:S(2)}) %collective-permute-start.14) | collective-permute-done | bytes 32800 | tf_op jit(solution)/shard_map/ppermute | solution.py:176
  39.2 0.0 collective-permute-done.8.refs_1_
  39.2 0.0 collective-permute-done.9.refs_2_
  39.2 0.7 %shard_map.94 = (bf16[64,512]{1,0:T(8,128)(2,1)S(1)}, bf16[64,512]{1,0:T(8,128)(2,1)S(1)}) custom-call(s32[64]{0:T(128)S(1)} %bitcast.13, f32[128,512]{1,0:T(8,128)S(1)} %get-tuple-element.31.own_ref, bf16[128,512]{1,0:T(8,128)(2,1)S(1)} %get-tuple-element.32.gates_ref, bf16[32,512]{1,0:T(8,128)(2,1)S(1)} %get-tuple-element.43.refs_0_, ...), custom_call_target="tpu_custom_call" | custom-call | tf_op jit(solution)/shard_map/pallas_call | solution.py:230
  40.0 0.1 collective-permute-start.15
  40.1 1.2 %collective-permute-done.15.got_ref = bf16[64,512]{1,0:T(8,128)(2,1)S(1)} collective-permute-done((bf16[64,512]{1,0:T(8,128)(2,1)S(1)}, bf16[64,512]{1,0:T(8,128)(2,1)S(1)}, u32[]{:S(2)}, u32[]{:S(2)}) %collective-permute-start.15) | collective-permute-done | bytes 65568 | tf_op jit(solution)/shard_map/ppermute | solution.py:236
  41.3 0.0 collective-permute-done.16.w_other_ref
  41.3 0.0 copy-done
  41.3 1.1 %shard_map.95 = bf16[8,8,1024]{2,1,0:T(8,128)(2,1)} custom-call(bf16[8,8,1024]{2,1,0:T(8,128)(2,1)S(1)} %copy-done.1, bf16[64,512]{1,0:T(8,128)(2,1)S(1)} %get-tuple-element.51.keep_ref, bf16[64,512]{1,0:T(8,128)(2,1)S(1)} %collective-permute-done.15.got_ref, bf16[512,1024]{1,0:T(8,128)(2,1)S(1)} %copy-done, ...), custom_call_target="tpu_custom_call" | custom-call | flops 268435456 | bytes 2097152 | tf_op jit(solution)/shard_map/pallas_call | solution.py:237
  (1 shorter events, 0.0 us)
Async XLA Ops:
  0.0 3.7 %copy-start.1 = (bf16[8,8,1024]{2,1,0:T(8,128)(2,1)S(1)}, bf16[8,8,1024]{2,1,0:T(8,128)(2,1)}, u32[]{:S(2)}) copy-start(bf16[8,8,1024]{2,1,0:T(8,128)(2,1)} %own_ref.3) | copy-start | bytes 393220
  0.0 3.6 %copy-start.7 = (bf16[1024]{0:T(1024)(128)(2,1)S(1)}, bf16[1024]{0:T(1024)(128)(2,1)}, u32[]{:S(2)}) copy-start(bf16[1024]{0:T(1024)(128)(2,1)} %param.10) | copy-start | bytes 6148
  0.0 3.7 %copy-start.3 = (s32[64,1]{0,1:T(1,128)S(1)}, s32[64,1]{0,1:T(1,128)}, u32[]{:S(2)}) copy-start(s32[64,1]{0,1:T(1,128)} %param.15) | copy-start | bytes 772
  0.0 41.3 %collective-permute-start.16 = (bf16[512,1024]{1,0:T(8,128)(2,1)}, bf16[512,1024]{1,0:T(8,128)(2,1)S(1)}, u32[]{:S(2)}, u32[]{:S(2)}) collective-permute-start(bf16[512,1024]{1,0:T(8,128)(2,1)} %w_own_ref.1), channel_id=1, source_target_pairs={{0,1},{1,0},{2,3},{3,2},{4,5},{5,4},{6,7},{7,6},{8,9},{9,8},{10,11... | collective-permute-start | bytes 3145736 | tf_op jit(solution)/shard_map/ppermute | solution.py:220
  0.5 3.2 %collective-permute-start = (bf16[8,8,1024]{2,1,0:T(8,128)(2,1)}, bf16[8,8,1024]{2,1,0:T(8,128)(2,1)S(1)}, u32[]{:S(2)}, u32[]{:S(2)}) collective-permute-start(bf16[8,8,1024]{2,1,0:T(8,128)(2,1)} %own_ref.3), channel_id=1, source_target_pairs={{0,1},{1,0},{2,3},{3,2},{4,5},{5,4},{6,7},{7,6},{8,9},{9,8},{10,11... | collective-permute-start | bytes 393224 | tf_op jit(solution)/shard_map/ppermute | solution.py:195
  3.6 13.8 %copy-start.2 = (s32[64,32]{0,1:T(8,128)S(1)}, s32[64,32]{0,1:T(8,128)}, u32[]{:S(2)}) copy-start(s32[64,32]{0,1:T(8,128)} %param.17) | copy-start | bytes 24580
  3.7 13.8 %copy-start.4 = (s32[8]{0:T(128)S(1)}, s32[8]{0:T(128)}, u32[]{:S(2)}) copy-start(s32[8]{0:T(128)} %len_ref.1) | copy-start | bytes 100
  3.7 20.1 %copy-start.5 = (bf16[1,2048,512]{2,1,0:T(8,128)(2,1)S(1)}, bf16[1,2048,512]{2,1,0:T(8,128)(2,1)}, u32[]{:S(2)}) copy-start(bf16[1,2048,512]{2,1,0:T(8,128)(2,1)} %param.13) | copy-start | bytes 6291460
  3.7 20.1 %copy-start.6 = (bf16[1,2048,512]{2,1,0:T(8,128)(2,1)S(1)}, bf16[1,2048,512]{2,1,0:T(8,128)(2,1)}, u32[]{:S(2)}) copy-start(bf16[1,2048,512]{2,1,0:T(8,128)(2,1)} %param.14) | copy-start | bytes 6291460
  4.7 7.6 %collective-permute-start.1 = (bf16[32,512]{1,0:T(8,128)(2,1)S(1)}, bf16[32,512]{1,0:T(8,128)(2,1)S(1)}, u32[]{:S(2)}, u32[]{:S(2)}) collective-permute-start(bf16[32,512]{1,0:T(8,128)(2,1)S(1)} %get-tuple-element.36), channel_id=1, source_target_pairs={{0,2},{2,0},{4,6},{6,4},{8,10},{10,8},{12,14},{14,12},{1,3},{3,1},... | collective-permute-start | bytes 98312 | tf_op jit(solution)/shard_map/ppermute | solution.py:176
  7.7 5.9 %collective-permute-start.2 = (bf16[32,512]{1,0:T(8,128)(2,1)S(1)}, bf16[32,512]{1,0:T(8,128)(2,1)S(1)}, u32[]{:S(2)}, u32[]{:S(2)}) collective-permute-start(bf16[32,512]{1,0:T(8,128)(2,1)S(1)} %get-tuple-element.37), channel_id=1, source_target_pairs={{0,4},{2,6},{4,0},{6,2},{8,12},{10,14},{12,8},{14,10},{1,5},{3,7},... | collective-permute-start | bytes 98312 | tf_op jit(solution)/shard_map/ppermute | solution.py:176
  9.3 7.9 %collective-permute-start.3 = (bf16[32,512]{1,0:T(8,128)(2,1)S(1)}, bf16[32,512]{1,0:T(8,128)(2,1)S(1)}, u32[]{:S(2)}, u32[]{:S(2)}) collective-permute-start(bf16[32,512]{1,0:T(8,128)(2,1)S(1)} %get-tuple-element.38), channel_id=1, source_target_pairs={{0,6},{2,4},{4,2},{6,0},{8,14},{10,12},{12,10},{14,8},{1,7},{3,5},... | collective-permute-start | bytes 98312 | tf_op jit(solution)/shard_map/ppermute | solution.py:176
  9.3 9.8 %collective-permute-start.4 = (bf16[32,512]{1,0:T(8,128)(2,1)S(1)}, bf16[32,512]{1,0:T(8,128)(2,1)S(1)}, u32[]{:S(2)}, u32[]{:S(2)}) collective-permute-start(bf16[32,512]{1,0:T(8,128)(2,1)S(1)} %get-tuple-element.39), channel_id=1, source_target_pairs={{0,8},{2,10},{4,12},{6,14},{8,0},{10,2},{12,4},{14,6},{1,9},{3,11}... | collective-permute-start | bytes 98312 | tf_op jit(solution)/shard_map/ppermute | solution.py:176
  12.3 6.9 %collective-permute-start.5 = (bf16[32,512]{1,0:T(8,128)(2,1)S(1)}, bf16[32,512]{1,0:T(8,128)(2,1)S(1)}, u32[]{:S(2)}, u32[]{:S(2)}) collective-permute-start(bf16[32,512]{1,0:T(8,128)(2,1)S(1)} %get-tuple-element.40), channel_id=1, source_target_pairs={{0,10},{2,8},{4,14},{6,12},{8,2},{10,0},{12,6},{14,4},{1,11},{3,9}... | collective-permute-start | bytes 98312 | tf_op jit(solution)/shard_map/ppermute | solution.py:176
  13.7 5.7 %collective-permute-start.6 = (bf16[32,512]{1,0:T(8,128)(2,1)S(1)}, bf16[32,512]{1,0:T(8,128)(2,1)S(1)}, u32[]{:S(2)}, u32[]{:S(2)}) collective-permute-start(bf16[32,512]{1,0:T(8,128)(2,1)S(1)} %get-tuple-element.41), channel_id=1, source_target_pairs={{0,12},{2,14},{4,8},{6,10},{8,4},{10,6},{12,0},{14,2},{1,13},{3,15... | collective-permute-start | bytes 98312 | tf_op jit(solution)/shard_map/ppermute | solution.py:176
  17.2 6.6 %collective-permute-start.7 = (bf16[32,512]{1,0:T(8,128)(2,1)S(1)}, bf16[32,512]{1,0:T(8,128)(2,1)S(1)}, u32[]{:S(2)}, u32[]{:S(2)}) collective-permute-start(bf16[32,512]{1,0:T(8,128)(2,1)S(1)} %get-tuple-element.42), channel_id=1, source_target_pairs={{0,14},{2,12},{4,10},{6,8},{8,6},{10,4},{12,2},{14,0},{1,15},{3,13... | collective-permute-start | bytes 98312 | tf_op jit(solution)/shard_map/ppermute | solution.py:176
  23.8 17.5 %copy-start = (bf16[512,1024]{1,0:T(8,128)(2,1)S(1)}, bf16[512,1024]{1,0:T(8,128)(2,1)}, u32[]{:S(2)}) copy-start(bf16[512,1024]{1,0:T(8,128)(2,1)} %w_own_ref.1) | copy-start | bytes 3145732
  27.0 5.6 %collective-permute-start.10 = (bf16[32,512]{1,0:T(8,128)(2,1)S(1)}, bf16[32,512]{1,0:T(8,128)(2,1)S(1)}, u32[]{:S(2)}, u32[]{:S(2)}) collective-permute-start(bf16[32,512]{1,0:T(8,128)(2,1)S(1)} %get-tuple-element.46), channel_id=1, source_target_pairs={{0,6},{2,4},{4,2},{6,0},{8,14},{10,12},{12,10},{14,8},{1,7},{3,5},... | collective-permute-start | bytes 98312 | tf_op jit(solution)/shard_map/ppermute | solution.py:176
  27.1 7.7 %collective-permute-start.11 = (bf16[32,512]{1,0:T(8,128)(2,1)S(1)}, bf16[32,512]{1,0:T(8,128)(2,1)S(1)}, u32[]{:S(2)}, u32[]{:S(2)}) collective-permute-start(bf16[32,512]{1,0:T(8,128)(2,1)S(1)} %get-tuple-element.47), channel_id=1, source_target_pairs={{0,8},{2,10},{4,12},{6,14},{8,0},{10,2},{12,4},{14,6},{1,9},{3,11}... | collective-permute-start | bytes 98312 | tf_op jit(solution)/shard_map/ppermute | solution.py:176
  28.0 7.3 %collective-permute-start.12 = (bf16[32,512]{1,0:T(8,128)(2,1)S(1)}, bf16[32,512]{1,0:T(8,128)(2,1)S(1)}, u32[]{:S(2)}, u32[]{:S(2)}) collective-permute-start(bf16[32,512]{1,0:T(8,128)(2,1)S(1)} %get-tuple-element.48), channel_id=1, source_target_pairs={{0,10},{2,8},{4,14},{6,12},{8,2},{10,0},{12,6},{14,4},{1,11},{3,9}... | collective-permute-start | bytes 98312 | tf_op jit(solution)/shard_map/ppermute | solution.py:176
  30.0 6.4 %collective-permute-start.13 = (bf16[32,512]{1,0:T(8,128)(2,1)S(1)}, bf16[32,512]{1,0:T(8,128)(2,1)S(1)}, u32[]{:S(2)}, u32[]{:S(2)}) collective-permute-start(bf16[32,512]{1,0:T(8,128)(2,1)S(1)} %get-tuple-element.49), channel_id=1, source_target_pairs={{0,12},{2,14},{4,8},{6,10},{8,4},{10,6},{12,0},{14,2},{1,13},{3,15... | collective-permute-start | bytes 98312 | tf_op jit(solution)/shard_map/ppermute | solution.py:176
  32.6 6.6 %collective-permute-start.14 = (bf16[32,512]{1,0:T(8,128)(2,1)S(1)}, bf16[32,512]{1,0:T(8,128)(2,1)S(1)}, u32[]{:S(2)}, u32[]{:S(2)}) collective-permute-start(bf16[32,512]{1,0:T(8,128)(2,1)S(1)} %get-tuple-element.50), channel_id=1, source_target_pairs={{0,14},{2,12},{4,10},{6,8},{8,6},{10,4},{12,2},{14,0},{1,15},{3,13... | collective-permute-start | bytes 98312 | tf_op jit(solution)/shard_map/ppermute | solution.py:176
  34.8 4.4 %collective-permute-start.8 = (bf16[32,512]{1,0:T(8,128)(2,1)S(1)}, bf16[32,512]{1,0:T(8,128)(2,1)S(1)}, u32[]{:S(2)}, u32[]{:S(2)}) collective-permute-start(bf16[32,512]{1,0:T(8,128)(2,1)S(1)} %get-tuple-element.44), channel_id=1, source_target_pairs={{0,2},{2,0},{4,6},{6,4},{8,10},{10,8},{12,14},{14,12},{1,3},{3,1},... | collective-permute-start | bytes 98312 | tf_op jit(solution)/shard_map/ppermute | solution.py:176
  35.3 3.9 %collective-permute-start.9 = (bf16[32,512]{1,0:T(8,128)(2,1)S(1)}, bf16[32,512]{1,0:T(8,128)(2,1)S(1)}, u32[]{:S(2)}, u32[]{:S(2)}) collective-permute-start(bf16[32,512]{1,0:T(8,128)(2,1)S(1)} %get-tuple-element.45), channel_id=1, source_target_pairs={{0,4},{2,6},{4,0},{6,2},{8,12},{10,14},{12,8},{14,10},{1,5},{3,7},... | collective-permute-start | bytes 98312 | tf_op jit(solution)/shard_map/ppermute | solution.py:176
  40.0 1.3 %collective-permute-start.15 = (bf16[64,512]{1,0:T(8,128)(2,1)S(1)}, bf16[64,512]{1,0:T(8,128)(2,1)S(1)}, u32[]{:S(2)}, u32[]{:S(2)}) collective-permute-start(bf16[64,512]{1,0:T(8,128)(2,1)S(1)} %get-tuple-element.52), channel_id=1, source_target_pairs={{0,1},{1,0},{2,3},{3,2},{4,5},{5,4},{6,7},{7,6},{8,9},{9,8},{10,11... | collective-permute-start | bytes 196616 | tf_op jit(solution)/shard_map/ppermute | solution.py:236

commit v3 on v2

--- a/solution.py
+++ b/solution.py
@@ -45,44 +45,40 @@
 
 
 def own_slots(sess_ref, req_count):
-    me = lax.axis_index("cache")
-    base = me * req_count
+    base = lax.axis_index("cache") * req_count
     sessions = [sess_ref[base + request] for request in range(req_count)]
     slots = []
     for request in range(req_count):
         place = 0
         for earlier in range(request):
             place = place + (sessions[earlier] == sessions[request]).astype(jnp.int32)
-        slots.append((sessions[request] ^ me) * CAP + place)
+        slots.append(sessions[request] * CAP + place)
     return slots
 
 
-def query_kernel(sess_ref, own_ref, other_ref, gain_ref, w_ref, *refs):
-    *slot_refs, queries_ref, normed_ref, table_ref = refs
+def query_kernel(sess_ref, own_ref, other_ref, gain_ref, w_ref, table_ref, queries_ref, normed_ref):
     req_count, half_cands, _ = own_ref.shape
     rows = req_count * half_cands
     gain = gain_ref[...].astype(jnp.float32)
     normed_ref[:rows, :] = normed_rows(own_ref, gain)
     normed_ref[rows:, :] = normed_rows(other_ref, gain)
     table_ref[...] = jnp.zeros_like(table_ref)
-    queries = silu(jnp.dot(normed_ref[...], w_ref[0], preferred_element_type=jnp.float32))
+    queries = silu(jnp.dot(normed_ref[...], w_ref[:, 0, :], preferred_element_type=jnp.float32))
     queries_ref[...] = queries.astype(jnp.bfloat16)
     for request, slot in enumerate(own_slots(sess_ref, req_count)):
         low = request * half_cands
         both = jnp.concatenate([queries[low : low + half_cands], queries[rows + low : rows + low + half_cands]], axis=0)
         table_ref[slot] = both.astype(jnp.bfloat16)
-    for distance, slot_ref in enumerate(slot_refs):
-        slot_ref[...] = table_ref[distance * CAP : (distance + 1) * CAP].reshape(slot_ref.shape)
 
 
 def self_kernel(sess_ref, len_ref, mask_ref, normed_ref, queries_ref, w_ref, own_ref, gates_ref, hide_rows_ref, hide_cols_ref, marks_ref):
     width = queries_ref.shape[1]
     normed = normed_ref[...]
     me = lax.axis_index("cache")
-    keys = silu(jnp.dot(normed, w_ref[1], preferred_element_type=jnp.float32)).astype(jnp.bfloat16)
+    keys = silu(jnp.dot(normed, w_ref[:, 1, :], preferred_element_type=jnp.float32)).astype(jnp.bfloat16)
     products = queries_ref[...].astype(jnp.float32) * keys.astype(jnp.float32)
-    values = silu(jnp.dot(normed, w_ref[2], preferred_element_type=jnp.float32)).astype(jnp.bfloat16)
-    gates_ref[...] = silu(jnp.dot(normed, w_ref[3], preferred_element_type=jnp.float32)).astype(jnp.bfloat16)
+    values = silu(jnp.dot(normed, w_ref[:, 2, :], preferred_element_type=jnp.float32)).astype(jnp.bfloat16)
+    gates_ref[...] = silu(jnp.dot(normed, w_ref[:, 3, :], preferred_element_type=jnp.float32)).astype(jnp.bfloat16)
     for low in range(0, width, HD):
         score = jnp.sum(products[:, low : low + HD], axis=-1, keepdims=True) * SCALE
         own_ref[:, low : low + HD] = silu(score) * values[:, low : low + HD].astype(jnp.float32)
@@ -96,7 +92,7 @@
     for back in range(1, per_owner):
         same = (pltpu.roll(sessions, back, 1) == sessions) & (lane % per_owner >= back)
         place = place + same.astype(jnp.int32)
-    slot_of = jnp.where(sessions == me, ((lane // per_owner) ^ me) * CAP + place, -1)
+    slot_of = jnp.where(sessions == me, (lane // per_owner) * CAP + place, -1)
     slots = owners * CAP
     at_slot = lax.broadcasted_iota(jnp.int32, (slots, requests), 0)
     chosen = (at_slot == slot_of).astype(jnp.float32).astype(jnp.bfloat16)
@@ -117,16 +113,14 @@
     ).astype(jnp.bfloat16)
 
 
-def history_kernel(owners, hide_rows_ref, hide_cols_ref, keys_ref, values_ref, *refs):
-    slot_refs, out_refs = refs[:owners], refs[owners:]
-    per_owner, width = slot_refs[0].shape
+def history_kernel(slots_ref, hide_rows_ref, hide_cols_ref, keys_ref, values_ref, out_ref):
+    slot_rows, width = slots_ref.shape
     hist_rows = keys_ref.shape[0]
     span = min(256, hist_rows)
-    per_step = max(1, min(owners, 256 // per_owner))
-    for first in range(0, owners, per_step):
-        group = range(first, min(first + per_step, owners))
-        queries = jnp.concatenate([slot_refs[at][...] for at in group], axis=0)
-        hide_rows = hide_rows_ref[first * per_owner : first * per_owner + queries.shape[0], :]
+    per_step = min(slot_rows, 256)
+    for first in range(0, slot_rows, per_step):
+        queries = slots_ref[first : first + per_step, :]
+        hide_rows = hide_rows_ref[first : first + per_step, :]
         for low in range(0, width, HD):
             lhs = jnp.concatenate([queries[:, low : low + HD], hide_rows], axis=1)
             total = None
@@ -140,17 +134,12 @@
                     weights, values_ref[start : start + span, low : low + HD], preferred_element_type=jnp.float32
                 )
                 total = term if total is None else total + term
-            total = total.astype(jnp.bfloat16)
-            for place, at in enumerate(group):
-                out_refs[at][:, low : low + HD] = total[place * per_owner : (place + 1) * per_owner]
-
-
-def mix_kernel(owners, req_count, sess_ref, own_ref, gates_ref, *refs):
-    back_refs, (keep_ref, send_ref, table_ref) = refs[:owners], refs[owners:]
+            out_ref[first : first + per_step, low : low + HD] = total.astype(jnp.bfloat16)
+
+
+def mix_kernel(req_count, sess_ref, own_ref, gates_ref, table_ref, keep_ref, send_ref):
     rows, width = keep_ref.shape
     half_cands = rows // req_count
-    for distance, back_ref in enumerate(back_refs):
-        table_ref[distance * CAP : (distance + 1) * CAP] = back_ref[...].reshape((CAP,) + table_ref.shape[1:])
     picked = [table_ref[slot].astype(jnp.float32) for slot in own_slots(sess_ref, req_count)]
     for side, out_ref in enumerate((keep_ref, send_ref)):
         history = jnp.concatenate([both[side * half_cands : (side + 1) * half_cands] for both in picked], axis=0)
@@ -170,12 +159,10 @@
     out_ref[...] = total.reshape(req_count, half_cands, model_width).astype(jnp.bfloat16)
 
 
-def exchange(pieces):
-    count = len(pieces)
-    return [pieces[0]] + [
-        lax.ppermute(pieces[distance], "cache", [(place, place ^ distance) for place in range(count)])
-        for distance in range(1, count)
-    ]
+def exchange(table, owners):
+    rows, width = table.shape
+    blocks = table.reshape(owners, rows // owners, width)
+    return lax.all_to_all(blocks, "cache", split_axis=0, concat_axis=0, tiled=True).reshape(rows, width)
 
 
 def body(candidates, input_gain, w_in, w_out, hist_keys, hist_values, request_session, hist_len, block_mask):
@@ -189,21 +176,17 @@
     swap = [(0, 1), (1, 0)]
     bf16 = functools.partial(jax.ShapeDtypeStruct, dtype=jnp.bfloat16)
     sessions = request_session.reshape(-1)
-    piece = bf16((CAP * cand_count, width))
-    table = pltpu.VMEM((owners * CAP, cand_count, width), jnp.bfloat16)
+    slot_rows = owners * CAP * cand_count
 
     other = lax.ppermute(candidates, "serve", swap)
-    weights = jnp.transpose(w_in, (1, 0, 2))
-    *pieces, queries, normed = kernel_call(
+    table, queries, normed = kernel_call(
         query_kernel,
-        [piece] * owners + [bf16((2 * rows, width)), bf16((2 * rows, model_width))],
+        [bf16((owners * CAP, cand_count, width)), bf16((2 * rows, width)), bf16((2 * rows, model_width))],
         [smem, vmem, vmem, vmem, vmem],
-        [table],
         flops=4 * rows * model_width * width,
         moved=2 * model_width * width,
-    )(sessions, candidates, other, input_gain.reshape(1, -1), weights)
-    slots = exchange(pieces)
-    slot_rows = owners * CAP * cand_count
+    )(sessions, candidates, other, input_gain.reshape(1, -1), w_in)
+    slots = exchange(table.reshape(slot_rows, width), owners)
     own_term, gates, hide_rows, hide_cols = kernel_call(
         self_kernel,
         [
@@ -216,23 +199,21 @@
         [pltpu.VMEM((HD, owners * req_count), jnp.bfloat16)],
         flops=12 * rows * model_width * width,
         moved=6 * model_width * width,
-    )(request_session.reshape(1, -1), hist_len, block_mask.T, normed, queries, weights)
+    )(request_session.reshape(1, -1), hist_len, block_mask.T, normed, queries, w_in)
     w_other = lax.ppermute(w_out, "serve", swap)
-    backs = exchange(
-        kernel_call(
-            functools.partial(history_kernel, owners),
-            [piece] * owners,
-            [vmem] * (4 + owners),
-            flops=8 * slot_rows * hist_rows * width,
-            moved=4 * hist_rows * width,
-        )(hide_rows, hide_cols, hist_keys.reshape(hist_rows, width), hist_values.reshape(hist_rows, width), *slots)
-    )
+    attended = kernel_call(
+        history_kernel,
+        bf16((slot_rows, width)),
+        [vmem] * 5,
+        flops=8 * slot_rows * hist_rows * width,
+        moved=4 * hist_rows * width,
+    )(slots, hide_rows, hide_cols, hist_keys.reshape(hist_rows, width), hist_values.reshape(hist_rows, width))
+    returned = exchange(attended, owners).reshape(owners * CAP, cand_count, width)
     keep, send = kernel_call(
-        functools.partial(mix_kernel, owners, req_count),
+        functools.partial(mix_kernel, req_count),
         [bf16((rows, width))] * 2,
-        [smem] + [vmem] * (2 + owners),
-        [table],
-    )(sessions, own_term, gates, *backs)
+        [smem] + [vmem] * 3,
+    )(sessions, own_term, gates, returned)
     got = lax.ppermute(send, "serve", swap)
     return kernel_call(
         output_kernel,

time: 42.6 us -> 53.4 us (1.25)
  blocking collectives: 0 us -> 15.3 us
  starting transfers between devices: 22.6 us -> 7.79 us
  Pallas kernels: 7.74 us -> 16.3 us
  local copies, waits for them, and re-layouts: 3.07 us -> 11.6 us
  waiting for transfers between devices: 8.93 us -> 1.75 us
    ppermute x14 -> x0, starting transfers between devices: 21.9 us -> none  [exchange(): lax.ppermute(pieces[distance], 'cache', [(place, place ^ distance) for pl...]
    all_to_all x0 -> x1, blocking collectives: none -> 15.3 us  [exchange(): lax.all_to_all(blocks, 'cache', split_axis=0, concat_axis=0, tiled=True)]
    unnamed x17 -> x26, local copies, waits for them, and re-layouts: 3.06 us -> 11 us
    ppermute x14 -> x0, waiting for transfers between devices: 7.69 us -> none  [exchange(): lax.ppermute(pieces[distance], 'cache', [(place, place ^ distance) for pl...]
    all_to_all x0 -> x1, starting transfers between devices: none -> 7.19 us  [exchange(): lax.all_to_all(blocks, 'cache', split_axis=0, concat_axis=0, tiled=True)]
    pallas_call x1, Pallas kernels: 1.69 us -> 7.69 us  [body(): kernel_call(self_kernel, [jax.ShapeDtypeStruct((2 * rows, width), jnp.flo...]
    pallas_call x3, Pallas kernels: 4.91 us -> 7.49 us  [the longest x1 3.57 us: body(): kernel_call(query_kernel, [bf16((owners * CAP, cand_count, width)), bf16(...]
    reshape x1, local copies, waits for them, and re-layouts: 0.01 us -> 0.69 us  [body(): input_gain.reshape(1, -1)]
  transfers between devices with their start and end apart: 17 -> 4, of which waited for: 5 -> 2; matrix products, arithmetic and copies ran while one was open for 7% -> 1% of each run, Pallas kernels for 16% -> 22%
where the time goes in v3:
time: 53.4 us; the launch traced here: 52.9 us
  Pallas kernels  16.3 us (31%)
  blocking collectives  15.3 us (29%)
  local copies, waits for them, and re-layouts  11.6 us (22%)
  starting transfers between devices  7.79 us (15%)
  waiting for transfers between devices  1.75 us (3%)
    all_to_all x1, blocking collectives, exchange(): lax.all_to_all(blocks, 'cache', split_axis=0, concat_axis=0, tiled=True)  15.3 us
    unnamed x26, local copies, waits for them, and re-layouts  11 us
    pallas_call x1, Pallas kernels, body(): kernel_call(self_kernel, [jax.ShapeDtypeStruct((2 * rows, width), jnp.flo...  7.69 us
    all_to_all x1, starting transfers between devices, exchange(): lax.all_to_all(blocks, 'cache', split_axis=0, concat_axis=0, tiled=True)  7.19 us
    pallas_call x1, Pallas kernels, body(): kernel_call(query_kernel, [bf16((owners * CAP, cand_count, width)), bf16(...  3.57 us
    pallas_call x1, Pallas kernels, body(): kernel_call(history_kernel, bf16((slot_rows, width)), [vmem] * 5, flops=8...  3.2 us
    ppermute x1, waiting for transfers between devices, body(): got = lax.ppermute(send, 'serve', swap)  1.23 us
    pallas_call x1, Pallas kernels, body(): kernel_call(output_kernel, bf16((req_count, half_cands, model_width)), [v...  1.14 us
  transfers between devices with their start and end apart: 4, of which 2 were waited for; matrix products, arithmetic and copies ran while one was open for 1% of the time, Pallas kernels for 22%

profile of v3, /device:TPU:0, one launch (start us, length us, event | category | flops | bytes accessed | tf_op | source)
XLA Modules:
  0.0 52.9 jit_solution(534200292706213382)
XLA Ops:
  0.0 0.5 collective-permute-start
  0.5 0.7 %reshape.23.gain_ref = bf16[1,1024]{1,0:T(2,128)(2,1)S(1)} reshape(bf16[1024]{0:T(1024)(128)(2,1)} %param.10) | data formatting | bytes 4096 | tf_op jit(solution)/shard_map/reshape | solution.py:188
  1.1 0.5 collective-permute-done.other_ref
  1.7 0.0 copy-start
  1.7 2.2 %copy-done = bf16[1024,4,512]{2,1,0:T(4,128)(2,1)S(1)} copy-done((bf16[1024,4,512]{2,1,0:T(4,128)(2,1)S(1)}, bf16[1024,4,512]{2,1,0:T(4,128)(2,1)}, u32[]{:S(2)}) %copy-start) | copy-done | bytes 4194328
  3.8 0.0 copy-start.3
  3.8 0.9 %copy-done.3 = bf16[8,8,1024]{2,1,0:T(8,128)(2,1)S(1)} copy-done((bf16[8,8,1024]{2,1,0:T(8,128)(2,1)S(1)}, bf16[8,8,1024]{2,1,0:T(8,128)(2,1)}, u32[]{:S(2)}) %copy-start.3) | copy-done | bytes 131096
  4.7 0.0 copy-start.6
  4.7 0.7 %copy-done.6 = s32[64,1]{0,1:T(1,128)S(1)} copy-done((s32[64,1]{0,1:T(1,128)S(1)}, s32[64,1]{0,1:T(1,128)}, u32[]{:S(2)}) %copy-start.6) | copy-done | bytes 280
  5.4 0.0 copy-start.2
  5.4 0.0 copy-start.5
  5.4 0.0 copy-start.7
  5.4 0.0 copy-start.8
  5.4 3.6 %shard_map.91 = (bf16[16,16,512]{2,1,0:T(8,128)(2,1)}, bf16[128,512]{1,0:T(8,128)(2,1)S(1)}, bf16[128,1024]{1,0:T(8,128)(2,1)S(1)}) custom-call(s32[64]{0:T(128)S(1)} %bitcast.13, bf16[8,8,1024]{2,1,0:T(8,128)(2,1)S(1)} %copy-done.3, bf16[8,8,1024]{2,1,0:T(8,128)(2,1)S(1)} %collective-permute-done.other_ref, bf16[1,1024]{1,0:T(2,128)(2,1)S(1)} %reshape.23.gain_ref, ...), custom_call_target="tpu_custom_call" | custom-call | flops 134217728 | bytes 1048576 | tf_op jit(solution)/shard_map/pallas_call | solution.py:182
  9.0 7.2 %all-to-all-start = ((bf16[8,32,512]{2,1,0:T(8,128)(2,1)}), bf16[8,32,512]{2,1,0:T(8,128)(2,1)S(1)}, u32[]{:S(2)}, u32[]{:S(2)}) async-start(bf16[8,32,512]{2,1,0:T(8,128)(2,1)} %bitcast.3), calls=%async_computation | async-start | bytes 524288 | tf_op jit(solution)/shard_map/all_to_all | solution.py:165
  16.2 0.0 copy-done.2
  16.2 0.1 collective-permute-start.2
  16.3 0.0 copy-done.5
  16.3 0.0 copy-done.7
  16.3 0.0 copy-done.8
  16.3 0.0 copy-start.1
  16.3 2.2 %copy-done.1 = bf16[1024,4,512]{2,1,0:T(4,128)(2,1)S(1)} copy-done((bf16[1024,4,512]{2,1,0:T(4,128)(2,1)S(1)}, bf16[1024,4,512]{2,1,0:T(4,128)(2,1)}, u32[]{:S(2)}) %copy-start.1) | copy-done | bytes 4194328
  18.5 7.7 %shard_map.92 = (f32[128,512]{1,0:T(8,128)S(1)}, bf16[128,512]{1,0:T(8,128)(2,1)S(1)}, bf16[256,128]{1,0:T(8,128)(2,1)S(1)}, bf16[2048,128]{1,0:T(8,128)(2,1)S(1)}) custom-call(s32[1,64]{1,0:T(1,128)S(1)} %bitcast.14, s32[8]{0:T(128)S(1)} %copy-done.8, s32[32,64]{1,0:T(8,128)S(1)} %bitcast.12, bf16[128,1024]{1,0:T(8,128)(2,1)S(1)} %get-tuple-element.14.normed_ref, ...), custom_call_target="tpu_custom_call" | custom-call | flops 402653184 | bytes 3145728 | tf_op jit(solution)/shard_map/pallas_call | solution.py:190
  26.2 0.0 copy-start.11
  26.2 0.8 %copy-done.11 = bf16[2048,128]{1,0:T(8,128)(2,1)} copy-done((bf16[2048,128]{1,0:T(8,128)(2,1)}, bf16[2048,128]{1,0:T(8,128)(2,1)S(1)}, u32[]{:S(2)}) %copy-start.11) | copy-done | bytes 524312
  27.0 0.0 all-to-all-done
  27.0 0.0 copy-start.9
  27.0 1.6 %copy-done.9 = bf16[1,2048,512]{2,1,0:T(8,128)(2,1)S(1)} copy-done((bf16[1,2048,512]{2,1,0:T(8,128)(2,1)S(1)}, bf16[1,2048,512]{2,1,0:T(8,128)(2,1)}, u32[]{:S(2)}) %copy-start.9) | copy-done | bytes 2097176
  28.6 0.0 copy-start.10
  28.6 1.6 %copy-done.10 = bf16[1,2048,512]{2,1,0:T(8,128)(2,1)S(1)} copy-done((bf16[1,2048,512]{2,1,0:T(8,128)(2,1)S(1)}, bf16[1,2048,512]{2,1,0:T(8,128)(2,1)}, u32[]{:S(2)}) %copy-start.10) | copy-done | bytes 2097176
  30.2 0.0 copy-start.12
  30.2 1.0 %copy-done.12 = bf16[2048,128]{1,0:T(8,128)(2,1)S(1)} copy-done((bf16[2048,128]{1,0:T(8,128)(2,1)S(1)}, bf16[2048,128]{1,0:T(8,128)(2,1)}, u32[]{:S(2)}) %copy-start.12) | copy-done | bytes 524312
  31.2 0.0 copy-start.4
  31.2 3.2 %shard_map.93 = bf16[256,512]{1,0:T(8,128)(2,1)S(1)} custom-call(bf16[256,512]{1,0:T(8,128)(2,1)S(1)} %bitcast.10, bf16[256,128]{1,0:T(8,128)(2,1)S(1)} %get-tuple-element.19.hide_rows_ref, bf16[2048,128]{1,0:T(8,128)(2,1)S(1)} %copy-done.12, bf16[2048,512]{1,0:T(8,128)(2,1)S(1)} %bitcast.16, bf16[2048,512]{1,0:T(8,128)(2,1)S(1)} %bitcast.17), custom_call_target="tpu_custom_call" | custom-call | flops 2147483648 | bytes 4194304 | tf_op jit(solution)/shard_map/pallas_call | solution.py:204
  34.4 15.3 %all_to_all.10 = bf16[8,32,512]{2,1,0:T(8,128)(2,1)S(1)} all-to-all(bf16[8,32,512]{2,1,0:T(8,128)(2,1)S(1)} %bitcast.11), channel_id=1, replica_groups=mesh['groups'=2,'cache'=8,'serve'=2] {'cache'}, dimensions={0} | all-to-all | bytes 524288 | tf_op jit(solution)/shard_map/all_to_all | solution.py:165
  49.7 0.7 %shard_map.94 = (bf16[64,512]{1,0:T(8,128)(2,1)S(1)}, bf16[64,512]{1,0:T(8,128)(2,1)S(1)}) custom-call(s32[64]{0:T(128)S(1)} %bitcast.15, f32[128,512]{1,0:T(8,128)S(1)} %get-tuple-element.16.own_ref, bf16[128,512]{1,0:T(8,128)(2,1)S(1)} %get-tuple-element.17.gates_ref, bf16[16,16,512]{2,1,0:T(8,128)(2,1)S(1)} %bitcast.9), custom_call_target="tpu_custom_call" | custom-call | tf_op jit(solution)/shard_map/pallas_call | solution.py:212
  50.4 0.1 collective-permute-start.1
  50.5 0.0 collective-permute-done.2.w_other_ref
  50.5 1.2 %collective-permute-done.1.got_ref = bf16[64,512]{1,0:T(8,128)(2,1)S(1)} collective-permute-done((bf16[64,512]{1,0:T(8,128)(2,1)S(1)}, bf16[64,512]{1,0:T(8,128)(2,1)S(1)}, u32[]{:S(2)}, u32[]{:S(2)}) %collective-permute-start.1) | collective-permute-done | bytes 65568 | tf_op jit(solution)/shard_map/ppermute | solution.py:217
  51.7 0.0 copy-done.4
  51.7 1.1 %shard_map.95 = bf16[8,8,1024]{2,1,0:T(8,128)(2,1)} custom-call(bf16[8,8,1024]{2,1,0:T(8,128)(2,1)S(1)} %copy-done.4, bf16[64,512]{1,0:T(8,128)(2,1)S(1)} %get-tuple-element.21.keep_ref, bf16[64,512]{1,0:T(8,128)(2,1)S(1)} %collective-permute-done.1.got_ref, bf16[512,1024]{1,0:T(8,128)(2,1)S(1)} %copy-done.2, ...), custom_call_target="tpu_custom_call" | custom-call | flops 268435456 | bytes 2097152 | tf_op jit(solution)/shard_map/pallas_call | solution.py:218
Async XLA Ops:
  0.0 1.6 %collective-permute-start = (bf16[8,8,1024]{2,1,0:T(8,128)(2,1)}, bf16[8,8,1024]{2,1,0:T(8,128)(2,1)S(1)}, u32[]{:S(2)}, u32[]{:S(2)}) collective-permute-start(bf16[8,8,1024]{2,1,0:T(8,128)(2,1)} %own_ref.3), channel_id=1, source_target_pairs={{0,1},{1,0},{2,3},{3,2},{4,5},{5,4},{6,7},{7,6},{8,9},{9,8},{10,11... | collective-permute-start | bytes 393224 | tf_op jit(solution)/shard_map/ppermute | solution.py:181
  1.7 2.2 %copy-start = (bf16[1024,4,512]{2,1,0:T(4,128)(2,1)S(1)}, bf16[1024,4,512]{2,1,0:T(4,128)(2,1)}, u32[]{:S(2)}) copy-start(bf16[1024,4,512]{2,1,0:T(4,128)(2,1)} %w_ref.3) | copy-start | bytes 12582916
  3.8 0.9 %copy-start.3 = (bf16[8,8,1024]{2,1,0:T(8,128)(2,1)S(1)}, bf16[8,8,1024]{2,1,0:T(8,128)(2,1)}, u32[]{:S(2)}) copy-start(bf16[8,8,1024]{2,1,0:T(8,128)(2,1)} %own_ref.3) | copy-start | bytes 393220
  4.7 0.7 %copy-start.6 = (s32[64,1]{0,1:T(1,128)S(1)}, s32[64,1]{0,1:T(1,128)}, u32[]{:S(2)}) copy-start(s32[64,1]{0,1:T(1,128)} %param.15) | copy-start | bytes 772
  5.4 10.8 %copy-start.2 = (bf16[512,1024]{1,0:T(8,128)(2,1)S(1)}, bf16[512,1024]{1,0:T(8,128)(2,1)}, u32[]{:S(2)}) copy-start(bf16[512,1024]{1,0:T(8,128)(2,1)} %w_own_ref.1) | copy-start | bytes 3145732
  5.4 10.9 %copy-start.5 = (s32[64,32]{0,1:T(8,128)S(1)}, s32[64,32]{0,1:T(8,128)}, u32[]{:S(2)}) copy-start(s32[64,32]{0,1:T(8,128)} %param.17) | copy-start | bytes 24580
  5.4 10.9 %copy-start.7 = (s32[64,1]{0,1:T(1,128)S(1)}, s32[64,1]{0,1:T(1,128)}, u32[]{:S(2)}) copy-start(s32[64,1]{0,1:T(1,128)} %param.15) | copy-start | bytes 772
  5.4 10.9 %copy-start.8 = (s32[8]{0:T(128)S(1)}, s32[8]{0:T(128)}, u32[]{:S(2)}) copy-start(s32[8]{0:T(128)} %len_ref.1) | copy-start | bytes 100
  9.0 18.0 %all-to-all-start = ((bf16[8,32,512]{2,1,0:T(8,128)(2,1)}), bf16[8,32,512]{2,1,0:T(8,128)(2,1)S(1)}, u32[]{:S(2)}, u32[]{:S(2)}) async-start(bf16[8,32,512]{2,1,0:T(8,128)(2,1)} %bitcast.3), calls=%async_computation | async-start | bytes 524288 | tf_op jit(solution)/shard_map/all_to_all | solution.py:165
  16.2 34.3 %collective-permute-start.2 = (bf16[512,1024]{1,0:T(8,128)(2,1)S(1)}, bf16[512,1024]{1,0:T(8,128)(2,1)S(1)}, u32[]{:S(2)}, u32[]{:S(2)}) collective-permute-start(bf16[512,1024]{1,0:T(8,128)(2,1)S(1)} %copy-done.2), channel_id=1, source_target_pairs={{0,1},{1,0},{2,3},{3,2},{4,5},{5,4},{6,7},{7,6},{8,9},{9,8},{10,11... | collective-permute-start | bytes 3145736 | tf_op jit(solution)/shard_map/ppermute | solution.py:203
  16.3 2.2 %copy-start.1 = (bf16[1024,4,512]{2,1,0:T(4,128)(2,1)S(1)}, bf16[1024,4,512]{2,1,0:T(4,128)(2,1)}, u32[]{:S(2)}) copy-start(bf16[1024,4,512]{2,1,0:T(4,128)(2,1)} %w_ref.3) | copy-start | bytes 12582916
  26.2 0.8 %copy-start.11 = (bf16[2048,128]{1,0:T(8,128)(2,1)}, bf16[2048,128]{1,0:T(8,128)(2,1)S(1)}, u32[]{:S(2)}) copy-start(bf16[2048,128]{1,0:T(8,128)(2,1)S(1)} %get-tuple-element.20.hide_cols_ref) | copy-start | bytes 1572868
  27.0 1.6 %copy-start.9 = (bf16[1,2048,512]{2,1,0:T(8,128)(2,1)S(1)}, bf16[1,2048,512]{2,1,0:T(8,128)(2,1)}, u32[]{:S(2)}) copy-start(bf16[1,2048,512]{2,1,0:T(8,128)(2,1)} %param.13) | copy-start | bytes 6291460
  28.6 1.6 %copy-start.10 = (bf16[1,2048,512]{2,1,0:T(8,128)(2,1)S(1)}, bf16[1,2048,512]{2,1,0:T(8,128)(2,1)}, u32[]{:S(2)}) copy-start(bf16[1,2048,512]{2,1,0:T(8,128)(2,1)} %param.14) | copy-start | bytes 6291460
  30.2 1.0 %copy-start.12 = (bf16[2048,128]{1,0:T(8,128)(2,1)S(1)}, bf16[2048,128]{1,0:T(8,128)(2,1)}, u32[]{:S(2)}) copy-start(bf16[2048,128]{1,0:T(8,128)(2,1)} %copy-done.11) | copy-start | bytes 1572868
  31.2 20.5 %copy-start.4 = (bf16[8,8,1024]{2,1,0:T(8,128)(2,1)S(1)}, bf16[8,8,1024]{2,1,0:T(8,128)(2,1)}, u32[]{:S(2)}) copy-start(bf16[8,8,1024]{2,1,0:T(8,128)(2,1)} %own_ref.3) | copy-start | bytes 393220
  50.4 1.3 %collective-permute-start.1 = (bf16[64,512]{1,0:T(8,128)(2,1)S(1)}, bf16[64,512]{1,0:T(8,128)(2,1)S(1)}, u32[]{:S(2)}, u32[]{:S(2)}) collective-permute-start(bf16[64,512]{1,0:T(8,128)(2,1)S(1)} %get-tuple-element.22), channel_id=1, source_target_pairs={{0,1},{1,0},{2,3},{3,2},{4,5},{5,4},{6,7},{7,6},{8,9},{9,8},{10,11... | collective-permute-start | bytes 196616 | tf_op jit(solution)/shard_map/ppermute | solution.py:217

commit v4 on v2

--- a/solution.py
+++ b/solution.py
@@ -71,8 +71,11 @@
         low = request * half_cands
         both = jnp.concatenate([queries[low : low + half_cands], queries[rows + low : rows + low + half_cands]], axis=0)
         table_ref[slot] = both.astype(jnp.bfloat16)
-    for distance, slot_ref in enumerate(slot_refs):
-        slot_ref[...] = table_ref[distance * CAP : (distance + 1) * CAP].reshape(slot_ref.shape)
+    at = 0
+    for slot_ref in slot_refs:
+        slots = slot_ref.shape[0] // table_ref.shape[1]
+        slot_ref[...] = table_ref[at : at + slots].reshape(slot_ref.shape)
+        at += slots
 
 
 def self_kernel(sess_ref, len_ref, mask_ref, normed_ref, queries_ref, w_ref, own_ref, gates_ref, hide_rows_ref, hide_cols_ref, marks_ref):
@@ -123,9 +126,12 @@
     hist_rows = keys_ref.shape[0]
     span = min(256, hist_rows)
     per_step = max(1, min(owners, 256 // per_owner))
+    places = []
+    for out_ref in out_refs:
+        places += [(out_ref, low) for low in range(0, out_ref.shape[0], per_owner)]
     for first in range(0, owners, per_step):
         group = range(first, min(first + per_step, owners))
-        queries = jnp.concatenate([slot_refs[at][...] for at in group], axis=0)
+        queries = jnp.concatenate([slot_refs[at][:per_owner, :] for at in group], axis=0)
         hide_rows = hide_rows_ref[first * per_owner : first * per_owner + queries.shape[0], :]
         for low in range(0, width, HD):
             lhs = jnp.concatenate([queries[:, low : low + HD], hide_rows], axis=1)
@@ -142,7 +148,8 @@
                 total = term if total is None else total + term
             total = total.astype(jnp.bfloat16)
             for place, at in enumerate(group):
-                out_refs[at][:, low : low + HD] = total[place * per_owner : (place + 1) * per_owner]
+                out_ref, row = places[at]
+                out_ref[row : row + per_owner, low : low + HD] = total[place * per_owner : (place + 1) * per_owner]
 
 
 def mix_kernel(owners, req_count, sess_ref, own_ref, gates_ref, *refs):
@@ -150,7 +157,8 @@
     rows, width = keep_ref.shape
     half_cands = rows // req_count
     for distance, back_ref in enumerate(back_refs):
-        table_ref[distance * CAP : (distance + 1) * CAP] = back_ref[...].reshape((CAP,) + table_ref.shape[1:])
+        rows_here = back_ref[: back_refs[0].shape[0], :]
+        table_ref[distance * CAP : (distance + 1) * CAP] = rows_here.reshape((CAP,) + table_ref.shape[1:])
     picked = [table_ref[slot].astype(jnp.float32) for slot in own_slots(sess_ref, req_count)]
     for side, out_ref in enumerate((keep_ref, send_ref)):
         history = jnp.concatenate([both[side * half_cands : (side + 1) * half_cands] for both in picked], axis=0)
@@ -170,12 +178,17 @@
     out_ref[...] = total.reshape(req_count, half_cands, model_width).astype(jnp.bfloat16)
 
 
-def exchange(pieces):
-    count = len(pieces)
-    return [pieces[0]] + [
-        lax.ppermute(pieces[distance], "cache", [(place, place ^ distance) for place in range(count)])
-        for distance in range(1, count)
-    ]
+def exchange(owners, local, near, *far):
+    half = local.shape[0]
+
+    def send(rows, distance):
+        return lax.ppermute(rows, "cache", [(place, place ^ distance) for place in range(owners)])
+
+    came = [send(pair, 2 * (at + 1)) for at, pair in enumerate(far)]
+    out = [local, send(near, 1)]
+    for pair in came:
+        out += [pair, send(pair[half:], 1)]
+    return out
 
 
 def body(candidates, input_gain, w_in, w_out, hist_keys, hist_values, request_session, hist_len, block_mask):
@@ -189,20 +202,21 @@
     swap = [(0, 1), (1, 0)]
     bf16 = functools.partial(jax.ShapeDtypeStruct, dtype=jnp.bfloat16)
     sessions = request_session.reshape(-1)
-    piece = bf16((CAP * cand_count, width))
+    piece, pair = bf16((CAP * cand_count, width)), bf16((2 * CAP * cand_count, width))
+    layout = [piece, piece] + [pair] * (owners // 2 - 1)
     table = pltpu.VMEM((owners * CAP, cand_count, width), jnp.bfloat16)
 
     other = lax.ppermute(candidates, "serve", swap)
     weights = jnp.transpose(w_in, (1, 0, 2))
     *pieces, queries, normed = kernel_call(
         query_kernel,
-        [piece] * owners + [bf16((2 * rows, width)), bf16((2 * rows, model_width))],
+        layout + [bf16((2 * rows, width)), bf16((2 * rows, model_width))],
         [smem, vmem, vmem, vmem, vmem],
         [table],
         flops=4 * rows * model_width * width,
         moved=2 * model_width * width,
     )(sessions, candidates, other, input_gain.reshape(1, -1), weights)
-    slots = exchange(pieces)
+    slots = exchange(owners, *pieces)
     slot_rows = owners * CAP * cand_count
     own_term, gates, hide_rows, hide_cols = kernel_call(
         self_kernel,
@@ -219,9 +233,10 @@
     )(request_session.reshape(1, -1), hist_len, block_mask.T, normed, queries, weights)
     w_other = lax.ppermute(w_out, "serve", swap)
     backs = exchange(
-        kernel_call(
+        owners,
+        *kernel_call(
             functools.partial(history_kernel, owners),
-            [piece] * owners,
+            layout,
             [vmem] * (4 + owners),
             flops=8 * slot_rows * hist_rows * width,
             moved=4 * hist_rows * width,

time: 42.6 us -> 41.1 us (0.965)
  starting transfers between devices: 22.6 us -> 19.3 us
  waiting for transfers between devices: 8.93 us -> 10.6 us
    ppermute x14, starting transfers between devices: 21.9 us -> 18.7 us  [send(): lax.ppermute(rows, 'cache', [(place, place ^ distance) for place in range...]
    ppermute x14, waiting for transfers between devices: 7.69 us -> 9.38 us  [send(): lax.ppermute(rows, 'cache', [(place, place ^ distance) for place in range...]
where the time goes in v4:
time: 41.1 us; the launch traced here: 40.9 us
  starting transfers between devices  19.3 us (47%)
  waiting for transfers between devices  10.6 us (26%)
  Pallas kernels  7.74 us (19%)
  local copies, waits for them, and re-layouts  3.09 us (8%)
    ppermute x14, starting transfers between devices, send(): lax.ppermute(rows, 'cache', [(place, place ^ distance) for place in range...  18.7 us
    ppermute x14, waiting for transfers between devices, send(): lax.ppermute(rows, 'cache', [(place, place ^ distance) for place in range...  9.38 us
    pallas_call x1, Pallas kernels, body(): kernel_call(functools.partial(history_kernel, owners), layout, [vmem] * (...  3.2 us
    unnamed x17, local copies, waits for them, and re-layouts  3.06 us
    pallas_call x1, Pallas kernels, body(): kernel_call(self_kernel, [jax.ShapeDtypeStruct((2 * rows, width), jnp.flo...  1.69 us
    ppermute x1, waiting for transfers between devices, body(): got = lax.ppermute(send, 'serve', swap)  1.24 us
    pallas_call x1, Pallas kernels, body(): kernel_call(output_kernel, bf16((req_count, half_cands, model_width)), [v...  1.14 us
    pallas_call x1, Pallas kernels, body(): kernel_call(query_kernel, layout + [bf16((2 * rows, width)), bf16((2 * ro...  0.98 us
  transfers between devices with their start and end apart: 17, of which 5 were waited for; matrix products, arithmetic and copies ran while one was open for 7% of the time, Pallas kernels for 16%

profile of v4, /device:TPU:0, one launch (start us, length us, event | category | flops | bytes accessed | tf_op | source)
XLA Modules:
  0.0 40.9 jit_solution(15576844770951422386)
XLA Ops:
  0.0 0.0 copy-start.1
  0.0 0.0 copy-start.7
  0.0 0.0 copy-start.3
  0.0 0.5 %collective-permute-start.16 = (bf16[512,1024]{1,0:T(8,128)(2,1)}, bf16[512,1024]{1,0:T(8,128)(2,1)S(1)}, u32[]{:S(2)}, u32[]{:S(2)}) collective-permute-start(bf16[512,1024]{1,0:T(8,128)(2,1)} %w_own_ref.1), channel_id=1, source_target_pairs={{0,1},{1,0},{2,3},{3,2},{4,5},{5,4},{6,7},{7,6},{8,9},{9,8},{10,11... | collective-permute-start | bytes 3145736 | tf_op jit(solution)/shard_map/ppermute | solution.py:234
  0.5 0.1 collective-permute-start
  0.6 3.0 %copy.12 = bf16[1024,4,512]{2,0,1:T(8,128)(2,1)S(1)} copy(bf16[1024,4,512]{2,1,0:T(4,128)(2,1)} %param.11) | data formatting | bytes 8388608 | tf_op args[2]
  3.6 0.0 copy-done.7
  3.6 0.0 copy-start.2
  3.7 0.0 copy-start.4
  3.7 0.0 collective-permute-done.other_ref
  3.7 0.0 copy-done.1
  3.7 0.0 copy-done.3
  3.7 0.0 copy-start.5
  3.7 0.0 copy-start.6
  3.7 1.0 %shard_map.91 = (bf16[32,512]{1,0:T(8,128)(2,1)S(1)}, bf16[32,512]{1,0:T(8,128)(2,1)S(1)}, bf16[64,512]{1,0:T(8,128)(2,1)S(1)}, bf16[64,512]{1,0:T(8,128)(2,1)S(...) custom-call(s32[64]{0:T(128)S(1)} %bitcast.11, ...), custom_call_target="tpu_custom_call" | custom-call | flops 134217728 | bytes 1048576 | tf_op jit(solution)/shard_map/pallas_call | solution.py:211
  4.7 3.1 %collective-permute-start.2 = (bf16[64,512]{1,0:T(8,128)(2,1)S(1)}, bf16[64,512]{1,0:T(8,128)(2,1)S(1)}, u32[]{:S(2)}, u32[]{:S(2)}) collective-permute-start(bf16[64,512]{1,0:T(8,128)(2,1)S(1)} %get-tuple-element.31), channel_id=1, source_target_pairs={{0,4},{2,6},{4,0},{6,2},{8,12},{10,14},{12,8},{14,10},{1,5},{3,7},... | collective-permute-start | bytes 196616 | tf_op jit(solution)/shard_map/ppermute | solution.py:185
  7.8 2.6 %collective-permute-start.4 = (bf16[64,512]{1,0:T(8,128)(2,1)S(1)}, bf16[64,512]{1,0:T(8,128)(2,1)S(1)}, u32[]{:S(2)}, u32[]{:S(2)}) collective-permute-start(bf16[64,512]{1,0:T(8,128)(2,1)S(1)} %get-tuple-element.32), channel_id=1, source_target_pairs={{0,8},{2,10},{4,12},{6,14},{8,0},{10,2},{12,4},{14,6},{1,9},{3,11}... | collective-permute-start | bytes 196616 | tf_op jit(solution)/shard_map/ppermute | solution.py:185
  10.4 0.0 collective-permute-start.6
  10.4 1.7 %collective-permute-start.1 = (bf16[32,512]{1,0:T(8,128)(2,1)S(1)}, bf16[32,512]{1,0:T(8,128)(2,1)S(1)}, u32[]{:S(2)}, u32[]{:S(2)}) collective-permute-start(bf16[32,512]{1,0:T(8,128)(2,1)S(1)} %get-tuple-element.30), channel_id=1, source_target_pairs={{0,2},{2,0},{4,6},{6,4},{8,10},{10,8},{12,14},{14,12},{1,3},{3,1},... | collective-permute-start | bytes 98312 | tf_op jit(solution)/shard_map/ppermute | solution.py:185
  12.1 0.0 collective-permute-done.2.refs_2_
  12.1 0.3 collective-permute-start.3
  12.4 2.9 %collective-permute-done.4.refs_4_ = bf16[64,512]{1,0:T(8,128)(2,1)S(1)} collective-permute-done((bf16[64,512]{1,0:T(8,128)(2,1)S(1)}, bf16[64,512]{1,0:T(8,128)(2,1)S(1)}, u32[]{:S(2)}, u32[]{:S(2)}) %collective-permute-start.4) | collective-permute-done | bytes 65568 | tf_op jit(solution)/shard_map/ppermute | solution.py:185
  15.3 1.5 %collective-permute-start.5 = (bf16[32,512]{1,0:T(8,128)(2,1)S(1)}, bf16[32,512]{1,0:T(8,128)(2,1)S(1)}, u32[]{:S(2)}, u32[]{:S(2)}) collective-permute-start(bf16[32,512]{1,0:T(8,128)(2,1)S(1)} %slice.25), channel_id=1, source_target_pairs={{0,2},{2,0},{4,6},{6,4},{8,10},{10,8},{12,14},{14,12},{1,3},{3,1},... | collective-permute-start | bytes 98312 | tf_op jit(solution)/shard_map/ppermute | solution.py:185
  16.8 0.0 collective-permute-done.6.refs_6_
  16.8 1.2 %collective-permute-start.7 = (bf16[32,512]{1,0:T(8,128)(2,1)S(1)}, bf16[32,512]{1,0:T(8,128)(2,1)S(1)}, u32[]{:S(2)}, u32[]{:S(2)}) collective-permute-start(bf16[32,512]{1,0:T(8,128)(2,1)S(1)} %slice.26), channel_id=1, source_target_pairs={{0,2},{2,0},{4,6},{6,4},{8,10},{10,8},{12,14},{14,12},{1,3},{3,1},... | collective-permute-start | bytes 98312 | tf_op jit(solution)/shard_map/ppermute | solution.py:185
  18.1 0.0 copy-done.2
  18.1 0.0 copy-done.4
  18.1 1.7 %shard_map.92 = (f32[128,512]{1,0:T(8,128)S(1)}, bf16[128,512]{1,0:T(8,128)(2,1)S(1)}, bf16[256,128]{1,0:T(8,128)(2,1)S(1)}, bf16[2048,128]{1,0:T(8,128)(2,1)S(1)}) custom-call(s32[1,64]{1,0:T(1,128)S(1)} %bitcast.12, s32[8]{0:T(128)S(1)} %copy-done.4, s32[32,64]{1,0:T(8,128)S(1)} %bitcast.10, bf16[128,1024]{1,0:T(8,128)(2,1)S(1)} %get-tuple-element.23.normed_ref, ...), custom_call_target="tpu_custom_call" | custom-call | flops 402653184 | bytes 3145728 | tf_op jit(solution)/shard_map/pallas_call | solution.py:221
  19.8 0.0 collective-permute-done.1.refs_1_
  19.8 0.0 collective-permute-done.3.refs_3_
  19.8 0.0 collective-permute-done.5.refs_5_
  19.8 0.9 %collective-permute-done.7.refs_7_ = bf16[32,512]{1,0:T(8,128)(2,1)S(1)} collective-permute-done((bf16[32,512]{1,0:T(8,128)(2,1)S(1)}, bf16[32,512]{1,0:T(8,128)(2,1)S(1)}, u32[]{:S(2)}, u32[]{:S(2)}) %collective-permute-start.7) | collective-permute-done | bytes 32800 | tf_op jit(solution)/shard_map/ppermute | solution.py:185
  20.7 0.0 copy-done.5
  20.7 0.0 copy-done.6
  20.7 0.0 copy-start
  20.8 3.2 %shard_map.93 = (bf16[32,512]{1,0:T(8,128)(2,1)S(1)}, bf16[32,512]{1,0:T(8,128)(2,1)S(1)}, bf16[64,512]{1,0:T(8,128)(2,1)S(1)}, bf16[64,512]{1,0:T(8,128)(2,1)S(1)}, bf16[64,512]{1,0:T(8,128)(2,1)S(1)}) custom-call(bf16[256,128]{1,0:T(8,128)(2,1)S(1)} %get-tuple-element.27.hide_rows_ref, bf16[2048,128]{1,0:T(8,128)(2,1)S(1)} %get-tuple-element.28.hide_cols_ref, ...), custom_call_target="tpu_custom_call" | custom-call | flops 2147483648 | bytes 4194304 | tf_op jit(solution)/shard_map/pallas_call | solution.py:237
  24.0 0.6 %collective-permute-start.9 = (bf16[64,512]{1,0:T(8,128)(2,1)S(1)}, bf16[64,512]{1,0:T(8,128)(2,1)S(1)}, u32[]{:S(2)}, u32[]{:S(2)}) collective-permute-start(bf16[64,512]{1,0:T(8,128)(2,1)S(1)} %get-tuple-element.36), channel_id=1, source_target_pairs={{0,4},{2,6},{4,0},{6,2},{8,12},{10,14},{12,8},{14,10},{1,5},{3,7},... | collective-permute-start | bytes 196616 | tf_op jit(solution)/shard_map/ppermute | solution.py:185
  24.5 3.2 %collective-permute-start.11 = (bf16[64,512]{1,0:T(8,128)(2,1)S(1)}, bf16[64,512]{1,0:T(8,128)(2,1)S(1)}, u32[]{:S(2)}, u32[]{:S(2)}) collective-permute-start(bf16[64,512]{1,0:T(8,128)(2,1)S(1)} %get-tuple-element.37), channel_id=1, source_target_pairs={{0,8},{2,10},{4,12},{6,14},{8,0},{10,2},{12,4},{14,6},{1,9},{3,11}... | collective-permute-start | bytes 196616 | tf_op jit(solution)/shard_map/ppermute | solution.py:185
  27.8 0.7 %collective-permute-start.13 = (bf16[64,512]{1,0:T(8,128)(2,1)S(1)}, bf16[64,512]{1,0:T(8,128)(2,1)S(1)}, u32[]{:S(2)}, u32[]{:S(2)}) collective-permute-start(bf16[64,512]{1,0:T(8,128)(2,1)S(1)} %get-tuple-element.38), channel_id=1, source_target_pairs={{0,12},{2,14},{4,8},{6,10},{8,4},{10,6},{12,0},{14,2},{1,13},{3,15... | collective-permute-start | bytes 196616 | tf_op jit(solution)/shard_map/ppermute | solution.py:185
  28.4 1.2 %collective-permute-start.8 = (bf16[32,512]{1,0:T(8,128)(2,1)S(1)}, bf16[32,512]{1,0:T(8,128)(2,1)S(1)}, u32[]{:S(2)}, u32[]{:S(2)}) collective-permute-start(bf16[32,512]{1,0:T(8,128)(2,1)S(1)} %get-tuple-element.35), channel_id=1, source_target_pairs={{0,2},{2,0},{4,6},{6,4},{8,10},{10,8},{12,14},{14,12},{1,3},{3,1},... | collective-permute-start | bytes 98312 | tf_op jit(solution)/shard_map/ppermute | solution.py:185
  29.6 0.0 collective-permute-done.9.refs_2_
  29.7 0.8 %collective-permute-start.10 = (bf16[32,512]{1,0:T(8,128)(2,1)S(1)}, bf16[32,512]{1,0:T(8,128)(2,1)S(1)}, u32[]{:S(2)}, u32[]{:S(2)}) collective-permute-start(bf16[32,512]{1,0:T(8,128)(2,1)S(1)} %slice.27), channel_id=1, source_target_pairs={{0,2},{2,0},{4,6},{6,4},{8,10},{10,8},{12,14},{14,12},{1,3},{3,1},... | collective-permute-start | bytes 98312 | tf_op jit(solution)/shard_map/ppermute | solution.py:185
  30.4 0.0 collective-permute-done.11.refs_4_
  30.5 1.2 %collective-permute-start.12 = (bf16[32,512]{1,0:T(8,128)(2,1)S(1)}, bf16[32,512]{1,0:T(8,128)(2,1)S(1)}, u32[]{:S(2)}, u32[]{:S(2)}) collective-permute-start(bf16[32,512]{1,0:T(8,128)(2,1)S(1)} %slice.28), channel_id=1, source_target_pairs={{0,2},{2,0},{4,6},{6,4},{8,10},{10,8},{12,14},{14,12},{1,3},{3,1},... | collective-permute-start | bytes 98312 | tf_op jit(solution)/shard_map/ppermute | solution.py:185
  31.7 2.1 %collective-permute-done.13.refs_6_ = bf16[64,512]{1,0:T(8,128)(2,1)S(1)} collective-permute-done((bf16[64,512]{1,0:T(8,128)(2,1)S(1)}, bf16[64,512]{1,0:T(8,128)(2,1)S(1)}, u32[]{:S(2)}, u32[]{:S(2)}) %collective-permute-start.13) | collective-permute-done | bytes 65568 | tf_op jit(solution)/shard_map/ppermute | solution.py:185
  33.8 0.5 %collective-permute-start.14 = (bf16[32,512]{1,0:T(8,128)(2,1)S(1)}, bf16[32,512]{1,0:T(8,128)(2,1)S(1)}, u32[]{:S(2)}, u32[]{:S(2)}) collective-permute-start(bf16[32,512]{1,0:T(8,128)(2,1)S(1)} %slice.29), channel_id=1, source_target_pairs={{0,2},{2,0},{4,6},{6,4},{8,10},{10,8},{12,14},{14,12},{1,3},{3,1},... | collective-permute-start | bytes 98312 | tf_op jit(solution)/shard_map/ppermute | solution.py:185
  34.3 0.0 collective-permute-done.8.refs_1_
  34.3 0.0 collective-permute-done.10.refs_3_
  34.3 0.0 collective-permute-done.12.refs_5_
  34.4 3.4 %collective-permute-done.14.refs_7_ = bf16[32,512]{1,0:T(8,128)(2,1)S(1)} collective-permute-done((bf16[32,512]{1,0:T(8,128)(2,1)S(1)}, bf16[32,512]{1,0:T(8,128)(2,1)S(1)}, u32[]{:S(2)}, u32[]{:S(2)}) %collective-permute-start.14) | collective-permute-done | bytes 32800 | tf_op jit(solution)/shard_map/ppermute | solution.py:185
  37.7 0.7 %shard_map.94 = (bf16[64,512]{1,0:T(8,128)(2,1)S(1)}, bf16[64,512]{1,0:T(8,128)(2,1)S(1)}) custom-call(s32[64]{0:T(128)S(1)} %bitcast.13, f32[128,512]{1,0:T(8,128)S(1)} %get-tuple-element.25.own_ref, bf16[128,512]{1,0:T(8,128)(2,1)S(1)} %get-tuple-element.26.gates_ref, bf16[32,512]{1,0:T(8,128)(2,1)S(1)} %get-tuple-element.34.refs_0_, ...), custom_call_target="tpu_custom_call" | custom-call | tf_op jit(solution)/shard_map/pallas_call | solution.py:245
  38.5 0.1 collective-permute-start.15
  38.6 1.2 %collective-permute-done.15.got_ref = bf16[64,512]{1,0:T(8,128)(2,1)S(1)} collective-permute-done((bf16[64,512]{1,0:T(8,128)(2,1)S(1)}, bf16[64,512]{1,0:T(8,128)(2,1)S(1)}, u32[]{:S(2)}, u32[]{:S(2)}) %collective-permute-start.15) | collective-permute-done | bytes 65568 | tf_op jit(solution)/shard_map/ppermute | solution.py:251
  39.8 0.0 collective-permute-done.16.w_other_ref
  39.8 0.0 copy-done
  39.8 1.1 %shard_map.95 = bf16[8,8,1024]{2,1,0:T(8,128)(2,1)} custom-call(bf16[8,8,1024]{2,1,0:T(8,128)(2,1)S(1)} %copy-done.1, bf16[64,512]{1,0:T(8,128)(2,1)S(1)} %get-tuple-element.39.keep_ref, bf16[64,512]{1,0:T(8,128)(2,1)S(1)} %collective-permute-done.15.got_ref, bf16[512,1024]{1,0:T(8,128)(2,1)S(1)} %copy-done, ...), custom_call_target="tpu_custom_call" | custom-call | flops 268435456 | bytes 2097152 | tf_op jit(solution)/shard_map/pallas_call | solution.py:252
  (7 shorter events, 0.0 us)
Async XLA Ops:
  0.0 3.7 %copy-start.1 = (bf16[8,8,1024]{2,1,0:T(8,128)(2,1)S(1)}, bf16[8,8,1024]{2,1,0:T(8,128)(2,1)}, u32[]{:S(2)}) copy-start(bf16[8,8,1024]{2,1,0:T(8,128)(2,1)} %own_ref.3) | copy-start | bytes 393220
  0.0 3.6 %copy-start.7 = (bf16[1024]{0:T(1024)(128)(2,1)S(1)}, bf16[1024]{0:T(1024)(128)(2,1)}, u32[]{:S(2)}) copy-start(bf16[1024]{0:T(1024)(128)(2,1)} %param.10) | copy-start | bytes 6148
  0.0 3.7 %copy-start.3 = (s32[64,1]{0,1:T(1,128)S(1)}, s32[64,1]{0,1:T(1,128)}, u32[]{:S(2)}) copy-start(s32[64,1]{0,1:T(1,128)} %param.15) | copy-start | bytes 772
  0.0 39.8 %collective-permute-start.16 = (bf16[512,1024]{1,0:T(8,128)(2,1)}, bf16[512,1024]{1,0:T(8,128)(2,1)S(1)}, u32[]{:S(2)}, u32[]{:S(2)}) collective-permute-start(bf16[512,1024]{1,0:T(8,128)(2,1)} %w_own_ref.1), channel_id=1, source_target_pairs={{0,1},{1,0},{2,3},{3,2},{4,5},{5,4},{6,7},{7,6},{8,9},{9,8},{10,11... | collective-permute-start | bytes 3145736 | tf_op jit(solution)/shard_map/ppermute | solution.py:234
  0.5 3.2 %collective-permute-start = (bf16[8,8,1024]{2,1,0:T(8,128)(2,1)}, bf16[8,8,1024]{2,1,0:T(8,128)(2,1)S(1)}, u32[]{:S(2)}, u32[]{:S(2)}) collective-permute-start(bf16[8,8,1024]{2,1,0:T(8,128)(2,1)} %own_ref.3), channel_id=1, source_target_pairs={{0,1},{1,0},{2,3},{3,2},{4,5},{5,4},{6,7},{7,6},{8,9},{9,8},{10,11... | collective-permute-start | bytes 393224 | tf_op jit(solution)/shard_map/ppermute | solution.py:209
  3.6 14.4 %copy-start.2 = (s32[64,32]{0,1:T(8,128)S(1)}, s32[64,32]{0,1:T(8,128)}, u32[]{:S(2)}) copy-start(s32[64,32]{0,1:T(8,128)} %param.17) | copy-start | bytes 24580
  3.7 14.4 %copy-start.4 = (s32[8]{0:T(128)S(1)}, s32[8]{0:T(128)}, u32[]{:S(2)}) copy-start(s32[8]{0:T(128)} %len_ref.1) | copy-start | bytes 100
  3.7 17.0 %copy-start.5 = (bf16[1,2048,512]{2,1,0:T(8,128)(2,1)S(1)}, bf16[1,2048,512]{2,1,0:T(8,128)(2,1)}, u32[]{:S(2)}) copy-start(bf16[1,2048,512]{2,1,0:T(8,128)(2,1)} %param.13) | copy-start | bytes 6291460
  3.7 17.0 %copy-start.6 = (bf16[1,2048,512]{2,1,0:T(8,128)(2,1)S(1)}, bf16[1,2048,512]{2,1,0:T(8,128)(2,1)}, u32[]{:S(2)}) copy-start(bf16[1,2048,512]{2,1,0:T(8,128)(2,1)} %param.14) | copy-start | bytes 6291460
  4.7 7.4 %collective-permute-start.2 = (bf16[64,512]{1,0:T(8,128)(2,1)S(1)}, bf16[64,512]{1,0:T(8,128)(2,1)S(1)}, u32[]{:S(2)}, u32[]{:S(2)}) collective-permute-start(bf16[64,512]{1,0:T(8,128)(2,1)S(1)} %get-tuple-element.31), channel_id=1, source_target_pairs={{0,4},{2,6},{4,0},{6,2},{8,12},{10,14},{12,8},{14,10},{1,5},{3,7},... | collective-permute-start | bytes 196616 | tf_op jit(solution)/shard_map/ppermute | solution.py:185
  7.8 7.5 %collective-permute-start.4 = (bf16[64,512]{1,0:T(8,128)(2,1)S(1)}, bf16[64,512]{1,0:T(8,128)(2,1)S(1)}, u32[]{:S(2)}, u32[]{:S(2)}) collective-permute-start(bf16[64,512]{1,0:T(8,128)(2,1)S(1)} %get-tuple-element.32), channel_id=1, source_target_pairs={{0,8},{2,10},{4,12},{6,14},{8,0},{10,2},{12,4},{14,6},{1,9},{3,11}... | collective-permute-start | bytes 196616 | tf_op jit(solution)/shard_map/ppermute | solution.py:185
  10.4 6.5 %collective-permute-start.6 = (bf16[64,512]{1,0:T(8,128)(2,1)S(1)}, bf16[64,512]{1,0:T(8,128)(2,1)S(1)}, u32[]{:S(2)}, u32[]{:S(2)}) collective-permute-start(bf16[64,512]{1,0:T(8,128)(2,1)S(1)} %get-tuple-element.33), channel_id=1, source_target_pairs={{0,12},{2,14},{4,8},{6,10},{8,4},{10,6},{12,0},{14,2},{1,13},{3,15... | collective-permute-start | bytes 196616 | tf_op jit(solution)/shard_map/ppermute | solution.py:185
  10.4 9.4 %collective-permute-start.1 = (bf16[32,512]{1,0:T(8,128)(2,1)S(1)}, bf16[32,512]{1,0:T(8,128)(2,1)S(1)}, u32[]{:S(2)}, u32[]{:S(2)}) collective-permute-start(bf16[32,512]{1,0:T(8,128)(2,1)S(1)} %get-tuple-element.30), channel_id=1, source_target_pairs={{0,2},{2,0},{4,6},{6,4},{8,10},{10,8},{12,14},{14,12},{1,3},{3,1},... | collective-permute-start | bytes 98312 | tf_op jit(solution)/shard_map/ppermute | solution.py:185
  12.1 7.7 %collective-permute-start.3 = (bf16[32,512]{1,0:T(8,128)(2,1)S(1)}, bf16[32,512]{1,0:T(8,128)(2,1)S(1)}, u32[]{:S(2)}, u32[]{:S(2)}) collective-permute-start(bf16[32,512]{1,0:T(8,128)(2,1)S(1)} %slice.24), channel_id=1, source_target_pairs={{0,2},{2,0},{4,6},{6,4},{8,10},{10,8},{12,14},{14,12},{1,3},{3,1},... | collective-permute-start | bytes 98312 | tf_op jit(solution)/shard_map/ppermute | solution.py:185
  15.3 4.5 %collective-permute-start.5 = (bf16[32,512]{1,0:T(8,128)(2,1)S(1)}, bf16[32,512]{1,0:T(8,128)(2,1)S(1)}, u32[]{:S(2)}, u32[]{:S(2)}) collective-permute-start(bf16[32,512]{1,0:T(8,128)(2,1)S(1)} %slice.25), channel_id=1, source_target_pairs={{0,2},{2,0},{4,6},{6,4},{8,10},{10,8},{12,14},{14,12},{1,3},{3,1},... | collective-permute-start | bytes 98312 | tf_op jit(solution)/shard_map/ppermute | solution.py:185
  16.8 3.9 %collective-permute-start.7 = (bf16[32,512]{1,0:T(8,128)(2,1)S(1)}, bf16[32,512]{1,0:T(8,128)(2,1)S(1)}, u32[]{:S(2)}, u32[]{:S(2)}) collective-permute-start(bf16[32,512]{1,0:T(8,128)(2,1)S(1)} %slice.26), channel_id=1, source_target_pairs={{0,2},{2,0},{4,6},{6,4},{8,10},{10,8},{12,14},{14,12},{1,3},{3,1},... | collective-permute-start | bytes 98312 | tf_op jit(solution)/shard_map/ppermute | solution.py:185
  20.7 19.1 %copy-start = (bf16[512,1024]{1,0:T(8,128)(2,1)S(1)}, bf16[512,1024]{1,0:T(8,128)(2,1)}, u32[]{:S(2)}) copy-start(bf16[512,1024]{1,0:T(8,128)(2,1)} %w_own_ref.1) | copy-start | bytes 3145732
  24.0 5.7 %collective-permute-start.9 = (bf16[64,512]{1,0:T(8,128)(2,1)S(1)}, bf16[64,512]{1,0:T(8,128)(2,1)S(1)}, u32[]{:S(2)}, u32[]{:S(2)}) collective-permute-start(bf16[64,512]{1,0:T(8,128)(2,1)S(1)} %get-tuple-element.36), channel_id=1, source_target_pairs={{0,4},{2,6},{4,0},{6,2},{8,12},{10,14},{12,8},{14,10},{1,5},{3,7},... | collective-permute-start | bytes 196616 | tf_op jit(solution)/shard_map/ppermute | solution.py:185
  24.5 5.9 %collective-permute-start.11 = (bf16[64,512]{1,0:T(8,128)(2,1)S(1)}, bf16[64,512]{1,0:T(8,128)(2,1)S(1)}, u32[]{:S(2)}, u32[]{:S(2)}) collective-permute-start(bf16[64,512]{1,0:T(8,128)(2,1)S(1)} %get-tuple-element.37), channel_id=1, source_target_pairs={{0,8},{2,10},{4,12},{6,14},{8,0},{10,2},{12,4},{14,6},{1,9},{3,11}... | collective-permute-start | bytes 196616 | tf_op jit(solution)/shard_map/ppermute | solution.py:185
  27.8 6.1 %collective-permute-start.13 = (bf16[64,512]{1,0:T(8,128)(2,1)S(1)}, bf16[64,512]{1,0:T(8,128)(2,1)S(1)}, u32[]{:S(2)}, u32[]{:S(2)}) collective-permute-start(bf16[64,512]{1,0:T(8,128)(2,1)S(1)} %get-tuple-element.38), channel_id=1, source_target_pairs={{0,12},{2,14},{4,8},{6,10},{8,4},{10,6},{12,0},{14,2},{1,13},{3,15... | collective-permute-start | bytes 196616 | tf_op jit(solution)/shard_map/ppermute | solution.py:185
  28.4 5.9 %collective-permute-start.8 = (bf16[32,512]{1,0:T(8,128)(2,1)S(1)}, bf16[32,512]{1,0:T(8,128)(2,1)S(1)}, u32[]{:S(2)}, u32[]{:S(2)}) collective-permute-start(bf16[32,512]{1,0:T(8,128)(2,1)S(1)} %get-tuple-element.35), channel_id=1, source_target_pairs={{0,2},{2,0},{4,6},{6,4},{8,10},{10,8},{12,14},{14,12},{1,3},{3,1},... | collective-permute-start | bytes 98312 | tf_op jit(solution)/shard_map/ppermute | solution.py:185
  29.7 4.7 %collective-permute-start.10 = (bf16[32,512]{1,0:T(8,128)(2,1)S(1)}, bf16[32,512]{1,0:T(8,128)(2,1)S(1)}, u32[]{:S(2)}, u32[]{:S(2)}) collective-permute-start(bf16[32,512]{1,0:T(8,128)(2,1)S(1)} %slice.27), channel_id=1, source_target_pairs={{0,2},{2,0},{4,6},{6,4},{8,10},{10,8},{12,14},{14,12},{1,3},{3,1},... | collective-permute-start | bytes 98312 | tf_op jit(solution)/shard_map/ppermute | solution.py:185
  30.5 3.9 %collective-permute-start.12 = (bf16[32,512]{1,0:T(8,128)(2,1)S(1)}, bf16[32,512]{1,0:T(8,128)(2,1)S(1)}, u32[]{:S(2)}, u32[]{:S(2)}) collective-permute-start(bf16[32,512]{1,0:T(8,128)(2,1)S(1)} %slice.28), channel_id=1, source_target_pairs={{0,2},{2,0},{4,6},{6,4},{8,10},{10,8},{12,14},{14,12},{1,3},{3,1},... | collective-permute-start | bytes 98312 | tf_op jit(solution)/shard_map/ppermute | solution.py:185
  33.8 3.9 %collective-permute-start.14 = (bf16[32,512]{1,0:T(8,128)(2,1)S(1)}, bf16[32,512]{1,0:T(8,128)(2,1)S(1)}, u32[]{:S(2)}, u32[]{:S(2)}) collective-permute-start(bf16[32,512]{1,0:T(8,128)(2,1)S(1)} %slice.29), channel_id=1, source_target_pairs={{0,2},{2,0},{4,6},{6,4},{8,10},{10,8},{12,14},{14,12},{1,3},{3,1},... | collective-permute-start | bytes 98312 | tf_op jit(solution)/shard_map/ppermute | solution.py:185
  38.5 1.3 %collective-permute-start.15 = (bf16[64,512]{1,0:T(8,128)(2,1)S(1)}, bf16[64,512]{1,0:T(8,128)(2,1)S(1)}, u32[]{:S(2)}, u32[]{:S(2)}) collective-permute-start(bf16[64,512]{1,0:T(8,128)(2,1)S(1)} %get-tuple-element.40), channel_id=1, source_target_pairs={{0,1},{1,0},{2,3},{3,2},{4,5},{5,4},{6,7},{7,6},{8,9},{9,8},{10,11... | collective-permute-start | bytes 196616 | tf_op jit(solution)/shard_map/ppermute | solution.py:251

commit v5 on v4

--- a/solution.py
+++ b/solution.py
@@ -19,9 +19,12 @@
 smem = pl.BlockSpec(memory_space=pltpu.SMEM)
 
 
+def silu_of_half(half):
+    return half + half * jnp.tanh(half)
+
+
 def silu(x):
-    half = x * 0.5
-    return half + half * jnp.tanh(half)
+    return silu_of_half(x * 0.5)
 
 
 def kernel_call(body, out_shape, in_specs, scratch_shapes=(), flops=0, moved=0):
@@ -120,9 +123,9 @@
     ).astype(jnp.bfloat16)
 
 
-def history_kernel(owners, hide_rows_ref, hide_cols_ref, keys_ref, values_ref, *refs):
+def history_kernel(begin, owners, per_owner, hide_rows_ref, hide_cols_ref, keys_ref, values_ref, *refs):
     slot_refs, out_refs = refs[:owners], refs[owners:]
-    per_owner, width = slot_refs[0].shape
+    width = slot_refs[0].shape[1]
     hist_rows = keys_ref.shape[0]
     span = min(256, hist_rows)
     per_step = max(1, min(owners, 256 // per_owner))
@@ -132,7 +135,8 @@
     for first in range(0, owners, per_step):
         group = range(first, min(first + per_step, owners))
         queries = jnp.concatenate([slot_refs[at][:per_owner, :] for at in group], axis=0)
-        hide_rows = hide_rows_ref[first * per_owner : first * per_owner + queries.shape[0], :]
+        start_row = (begin + first) * per_owner
+        hide_rows = hide_rows_ref[start_row : start_row + queries.shape[0], :]
         for low in range(0, width, HD):
             lhs = jnp.concatenate([queries[:, low : low + HD], hide_rows], axis=1)
             total = None
@@ -141,7 +145,7 @@
                     [keys_ref[start : start + span, low : low + HD], hide_cols_ref[start : start + span, :]], axis=1
                 )
                 scores = lax.dot_general(lhs, rhs, (((1,), (1,)), ((), ())), preferred_element_type=jnp.float32)
-                weights = silu(scores * SCALE).astype(jnp.bfloat16)
+                weights = silu_of_half(scores * (0.5 * SCALE)).astype(jnp.bfloat16)
                 term = jnp.dot(
                     weights, values_ref[start : start + span, low : low + HD], preferred_element_type=jnp.float32
                 )
@@ -170,25 +174,28 @@
             out_ref[:, low : low + HD] = (head * level * gates[:, low : low + HD]).astype(jnp.bfloat16)
 
 
-def output_kernel(own_ref, keep_ref, got_ref, w_own_ref, w_other_ref, out_ref):
-    req_count, half_cands, model_width = own_ref.shape
-    total = own_ref[...].astype(jnp.float32).reshape(req_count * half_cands, model_width)
-    total = total + jnp.dot(keep_ref[...], w_own_ref[...], preferred_element_type=jnp.float32)
-    total = total + jnp.dot(got_ref[...], w_other_ref[...], preferred_element_type=jnp.float32)
-    out_ref[...] = total.reshape(req_count, half_cands, model_width).astype(jnp.bfloat16)
-
-
-def exchange(owners, local, near, *far):
-    half = local.shape[0]
-
-    def send(rows, distance):
-        return lax.ppermute(rows, "cache", [(place, place ^ distance) for place in range(owners)])
-
-    came = [send(pair, 2 * (at + 1)) for at, pair in enumerate(far)]
-    out = [local, send(near, 1)]
-    for pair in came:
-        out += [pair, send(pair[half:], 1)]
-    return out
+def kept_kernel(own_ref, keep_ref, w_own_ref, out_ref):
+    rows, model_width = out_ref.shape
+    total = own_ref[...].astype(jnp.float32).reshape(rows, model_width)
+    out_ref[...] = total + jnp.dot(keep_ref[...], w_own_ref[...], preferred_element_type=jnp.float32)
+
+
+def output_kernel(kept_ref, got_ref, w_other_ref, out_ref):
+    total = kept_ref[...] + jnp.dot(got_ref[...], w_other_ref[...], preferred_element_type=jnp.float32)
+    out_ref[...] = total.reshape(out_ref.shape).astype(jnp.bfloat16)
+
+
+def send(rows, owners, distance):
+    return lax.ppermute(rows, "cache", [(place, place ^ distance) for place in range(owners)])
+
+
+def send_far(owners, pairs):
+    came = {e: send(pairs[e], owners, 2 * e) for e in sorted(pairs, reverse=True)}
+    return dict(sorted(came.items()))
+
+
+def forward(owners, pairs):
+    return {e: send(pair[pair.shape[0] // 2 :], owners, 1) for e, pair in pairs.items()}
 
 
 def body(candidates, input_gain, w_in, w_out, hist_keys, hist_values, request_session, hist_len, block_mask):
@@ -208,7 +215,7 @@
 
     other = lax.ppermute(candidates, "serve", swap)
     weights = jnp.transpose(w_in, (1, 0, 2))
-    *pieces, queries, normed = kernel_call(
+    local, near, *far, queries, normed = kernel_call(
         query_kernel,
         layout + [bf16((2 * rows, width)), bf16((2 * rows, model_width))],
         [smem, vmem, vmem, vmem, vmem],
@@ -216,9 +223,10 @@
         flops=4 * rows * model_width * width,
         moved=2 * model_width * width,
     )(sessions, candidates, other, input_gain.reshape(1, -1), weights)
-    slots = exchange(owners, *pieces)
+    came = send_far(owners, dict(enumerate(far, 1)))
+    near = send(near, owners, 1)
     slot_rows = owners * CAP * cand_count
-    own_term, gates, hide_rows, hide_cols = kernel_call(
+    own = kernel_call(
         self_kernel,
         [
             jax.ShapeDtypeStruct((2 * rows, width), jnp.float32),
@@ -231,31 +239,51 @@
         flops=12 * rows * model_width * width,
         moved=6 * model_width * width,
     )(request_session.reshape(1, -1), hist_len, block_mask.T, normed, queries, weights)
+    came, (own_term, gates, hide_rows, hide_cols) = lax.optimization_barrier((came, own))
+    passed = forward(owners, came)
+    slots = [local, near]
+    for e in came:
+        slots += [came[e], passed[e]]
     w_other = lax.ppermute(w_out, "serve", swap)
-    backs = exchange(
-        owners,
-        *kernel_call(
-            functools.partial(history_kernel, owners),
-            layout,
-            [vmem] * (4 + owners),
-            flops=8 * slot_rows * hist_rows * width,
+    keys, values = hist_keys.reshape(hist_rows, width), hist_values.reshape(hist_rows, width)
+    back = []
+    middle = owners // 2
+    for begin, end, outs in ((0, middle, layout[: 1 + middle // 2]), (middle, owners, layout[1 + middle // 2 :])):
+        back += kernel_call(
+            functools.partial(history_kernel, begin, end - begin, CAP * cand_count),
+            outs,
+            [vmem] * (4 + end - begin),
+            flops=8 * (slot_rows // 2) * hist_rows * width,
             moved=4 * hist_rows * width,
-        )(hide_rows, hide_cols, hist_keys.reshape(hist_rows, width), hist_values.reshape(hist_rows, width), *slots)
-    )
-    keep, send = kernel_call(
+        )(hide_rows, hide_cols, keys, values, *slots[begin:end])
+    local, near, *far = back
+    came = send_far(owners, dict(enumerate(far, 1)))
+    near = send(near, owners, 1)
+    passed = forward(owners, came)
+    backs = [local, near]
+    for e in came:
+        backs += [came[e], passed[e]]
+    keep, send_mixed = kernel_call(
         functools.partial(mix_kernel, owners, req_count),
         [bf16((rows, width))] * 2,
         [smem] + [vmem] * (2 + owners),
         [table],
     )(sessions, own_term, gates, *backs)
-    got = lax.ppermute(send, "serve", swap)
+    got = lax.ppermute(send_mixed, "serve", swap)
+    kept = kernel_call(
+        kept_kernel,
+        jax.ShapeDtypeStruct((rows, model_width), jnp.float32),
+        [vmem] * 3,
+        flops=4 * rows * model_width * width,
+        moved=2 * model_width * width,
+    )(candidates, keep, w_out)
     return kernel_call(
         output_kernel,
         bf16((req_count, half_cands, model_width)),
-        [vmem] * 5,
-        flops=8 * rows * model_width * width,
-        moved=4 * model_width * width,
-    )(candidates, keep, got, w_out, w_other)
+        [vmem] * 3,
+        flops=4 * rows * model_width * width,
+        moved=2 * model_width * width,
+    )(kept, got, w_other)
 
 
 def solution(mesh):

time: 41.1 us -> 47.5 us (1.16)
  Pallas kernels: 7.74 us -> 15.5 us
  starting transfers between devices: 19.3 us -> 17 us
  waiting for transfers between devices: 10.6 us -> 11.5 us
    pallas_call x1 -> x3, Pallas kernels: 3.2 us -> 11.1 us  [the longest x2 10.8 us: body(): kernel_call(functools.partial(history_kernel, begin, end - begin, CAP * c...]
    ppermute x14, starting transfers between devices: 18.7 us -> 16.4 us  [send(): lax.ppermute(rows, 'cache', [(place, place ^ distance) for place in range...]
    ppermute x14, waiting for transfers between devices: 9.38 us -> 10.6 us  [send(): lax.ppermute(rows, 'cache', [(place, place ^ distance) for place in range...]
  transfers between devices with their start and end apart: 17 -> 17, of which waited for: 5 -> 8; matrix products, arithmetic and copies ran while one was open for 7% -> 6% of each run, Pallas kernels for 16% -> 31%
where the time goes in v5:
time: 47.5 us; the launch traced here: 47.3 us
  starting transfers between devices  17 us (36%)
  Pallas kernels  15.5 us (33%)
  waiting for transfers between devices  11.5 us (24%)
  local copies, waits for them, and re-layouts  3.09 us (7%)
    ppermute x14, starting transfers between devices, send(): lax.ppermute(rows, 'cache', [(place, place ^ distance) for place in range...  16.4 us
    pallas_call x2, Pallas kernels, body(): kernel_call(functools.partial(history_kernel, begin, end - begin, CAP * c...  10.8 us
    ppermute x14, waiting for transfers between devices, send(): lax.ppermute(rows, 'cache', [(place, place ^ distance) for place in range...  10.6 us
    unnamed x17, local copies, waits for them, and re-layouts  3.06 us
    pallas_call x1, Pallas kernels, body(): kernel_call(self_kernel, [jax.ShapeDtypeStruct((2 * rows, width), jnp.flo...  1.69 us
    pallas_call x1, Pallas kernels, body(): kernel_call(query_kernel, layout + [bf16((2 * rows, width)), bf16((2 * ro...  0.98 us
    pallas_call x1, Pallas kernels, body(): kernel_call(output_kernel, bf16((req_count, half_cands, model_width)), [v...  0.96 us
  transfers between devices with their start and end apart: 17, of which 8 were waited for; matrix products, arithmetic and copies ran while one was open for 6% of the time, Pallas kernels for 31%

profile of v5, /device:TPU:0, one launch (start us, length us, event | category | flops | bytes accessed | tf_op | source)
XLA Modules:
  0.0 47.3 jit_solution(4653749264533884090)
XLA Ops:
  0.0 0.0 copy-start.3
  0.0 0.0 copy-start.7
  0.0 0.0 copy-start.5
  0.0 0.5 %collective-permute-start.16 = (bf16[512,1024]{1,0:T(8,128)(2,1)}, bf16[512,1024]{1,0:T(8,128)(2,1)S(1)}, u32[]{:S(2)}, u32[]{:S(2)}) collective-permute-start(bf16[512,1024]{1,0:T(8,128)(2,1)} %w_own_ref.1), channel_id=1, source_target_pairs={{0,1},{1,0},{2,3},{3,2},{4,5},{5,4},{6,7},{7,6},{8,9},{9,8},{10,11... | collective-permute-start | bytes 3145736 | tf_op jit(solution)/shard_map/ppermute | solution.py:247
  0.5 0.1 collective-permute-start
  0.6 3.0 %copy.12 = bf16[1024,4,512]{2,0,1:T(8,128)(2,1)S(1)} copy(bf16[1024,4,512]{2,1,0:T(4,128)(2,1)} %param.11) | data formatting | bytes 8388608 | tf_op args[2]
  3.6 0.0 copy-done.7
  3.6 0.0 copy-start.4
  3.7 0.0 copy-start.6
  3.7 0.0 collective-permute-done.other_ref
  3.7 0.0 copy-done.3
  3.7 0.0 copy-done.5
  3.7 0.0 copy-start
  3.7 0.0 copy-start.1
  3.7 1.0 %shard_map.91 = (bf16[32,512]{1,0:T(8,128)(2,1)S(1)}, bf16[32,512]{1,0:T(8,128)(2,1)S(1)}, bf16[64,512]{1,0:T(8,128)(2,1)S(1)}, bf16[64,512]{1,0:T(8,128)(2,1)S(...) custom-call(s32[64]{0:T(128)S(1)} %bitcast.15, ...), custom_call_target="tpu_custom_call" | custom-call | flops 134217728 | bytes 1048576 | tf_op jit(solution)/shard_map/pallas_call | solution.py:218
  4.7 3.1 %collective-permute-start.1 = (bf16[64,512]{1,0:T(8,128)(2,1)S(1)}, bf16[64,512]{1,0:T(8,128)(2,1)S(1)}, u32[]{:S(2)}, u32[]{:S(2)}) collective-permute-start(bf16[64,512]{1,0:T(8,128)(2,1)S(1)} %get-tuple-element.30), channel_id=1, source_target_pairs={{0,4},{2,6},{4,0},{6,2},{8,12},{10,14},{12,8},{14,10},{1,5},{3,7},... | collective-permute-start | bytes 196616 | tf_op jit(solution)/shard_map/ppermute | solution.py:189
  7.8 2.6 %collective-permute-start.2 = (bf16[64,512]{1,0:T(8,128)(2,1)S(1)}, bf16[64,512]{1,0:T(8,128)(2,1)S(1)}, u32[]{:S(2)}, u32[]{:S(2)}) collective-permute-start(bf16[64,512]{1,0:T(8,128)(2,1)S(1)} %get-tuple-element.31), channel_id=1, source_target_pairs={{0,8},{2,10},{4,12},{6,14},{8,0},{10,2},{12,4},{14,6},{1,9},{3,11}... | collective-permute-start | bytes 196616 | tf_op jit(solution)/shard_map/ppermute | solution.py:189
  10.4 0.0 collective-permute-start.3
  10.4 0.0 copy-done.4
  10.4 0.0 copy-done.6
  10.4 1.7 %shard_map.92 = (f32[128,512]{1,0:T(8,128)S(1)}, bf16[128,512]{1,0:T(8,128)(2,1)S(1)}, bf16[256,128]{1,0:T(8,128)(2,1)S(1)}, bf16[2048,128]{1,0:T(8,128)(2,1)S(1)}) custom-call(s32[1,64]{1,0:T(1,128)S(1)} %bitcast.16, s32[8]{0:T(128)S(1)} %copy-done.6, s32[32,64]{1,0:T(8,128)S(1)} %bitcast.14, bf16[128,1024]{1,0:T(8,128)(2,1)S(1)} %get-tuple-element.33.normed_ref, ...), custom_call_target="tpu_custom_call" | custom-call | flops 402653184 | bytes 3145728 | tf_op jit(solution)/shard_map/pallas_call | solution.py:229
  12.1 0.0 collective-permute-done.1.refs_2_
  12.1 3.2 %collective-permute-done.2.refs_0_ = bf16[64,512]{1,0:T(8,128)(2,1)S(1)} collective-permute-done((bf16[64,512]{1,0:T(8,128)(2,1)S(1)}, bf16[64,512]{1,0:T(8,128)(2,1)S(1)}, u32[]{:S(2)}, u32[]{:S(2)}) %collective-permute-start.2) | collective-permute-done | bytes 65568 | tf_op jit(solution)/shard_map/ppermute | solution.py:189
  15.3 1.2 %collective-permute-done.3.refs_2_ = bf16[64,512]{1,0:T(8,128)(2,1)S(1)} collective-permute-done((bf16[64,512]{1,0:T(8,128)(2,1)S(1)}, bf16[64,512]{1,0:T(8,128)(2,1)S(1)}, u32[]{:S(2)}, u32[]{:S(2)}) %collective-permute-start.3) | collective-permute-done | bytes 65568 | tf_op jit(solution)/shard_map/ppermute | solution.py:189
  16.5 1.5 %collective-permute-start.10 = (bf16[32,512]{1,0:T(8,128)(2,1)S(1)}, bf16[32,512]{1,0:T(8,128)(2,1)S(1)}, u32[]{:S(2)}, u32[]{:S(2)}) collective-permute-start(bf16[32,512]{1,0:T(8,128)(2,1)S(1)} %slice.21), channel_id=1, source_target_pairs={{0,2},{2,0},{4,6},{6,4},{8,10},{10,8},{12,14},{14,12},{1,3},{3,1},... | collective-permute-start | bytes 98312 | tf_op jit(solution)/shard_map/ppermute | solution.py:189
  18.1 0.5 %collective-permute-start.9 = (bf16[32,512]{1,0:T(8,128)(2,1)S(1)}, bf16[32,512]{1,0:T(8,128)(2,1)S(1)}, u32[]{:S(2)}, u32[]{:S(2)}) collective-permute-start(bf16[32,512]{1,0:T(8,128)(2,1)S(1)} %slice.20), channel_id=1, source_target_pairs={{0,2},{2,0},{4,6},{6,4},{8,10},{10,8},{12,14},{14,12},{1,3},{3,1},... | collective-permute-start | bytes 98312 | tf_op jit(solution)/shard_map/ppermute | solution.py:189
  18.6 1.5 %collective-permute-start.4 = (bf16[32,512]{1,0:T(8,128)(2,1)S(1)}, bf16[32,512]{1,0:T(8,128)(2,1)S(1)}, u32[]{:S(2)}, u32[]{:S(2)}) collective-permute-start(bf16[32,512]{1,0:T(8,128)(2,1)S(1)} %get-tuple-element.44), channel_id=1, source_target_pairs={{0,2},{2,0},{4,6},{6,4},{8,10},{10,8},{12,14},{14,12},{1,3},{3,1},... | collective-permute-start | bytes 98312 | tf_op jit(solution)/shard_map/ppermute | solution.py:189
  20.1 0.5 %collective-permute-start.5 = (bf16[32,512]{1,0:T(8,128)(2,1)S(1)}, bf16[32,512]{1,0:T(8,128)(2,1)S(1)}, u32[]{:S(2)}, u32[]{:S(2)}) collective-permute-start(bf16[32,512]{1,0:T(8,128)(2,1)S(1)} %slice.18), channel_id=1, source_target_pairs={{0,2},{2,0},{4,6},{6,4},{8,10},{10,8},{12,14},{14,12},{1,3},{3,1},... | collective-permute-start | bytes 98312 | tf_op jit(solution)/shard_map/ppermute | solution.py:189
  20.6 0.1 collective-permute-done.10.refs_3_
  20.7 1.3 %collective-permute-done.9.refs_1_ = bf16[32,512]{1,0:T(8,128)(2,1)S(1)} collective-permute-done((bf16[32,512]{1,0:T(8,128)(2,1)S(1)}, bf16[32,512]{1,0:T(8,128)(2,1)S(1)}, u32[]{:S(2)}, u32[]{:S(2)}) %collective-permute-start.9) | collective-permute-done | bytes 32800 | tf_op jit(solution)/shard_map/ppermute | solution.py:189
  22.0 0.0 copy-done
  22.0 0.0 copy-done.1
  22.0 5.4 %shard_map.94 = (bf16[64,512]{1,0:T(8,128)(2,1)S(1)}, bf16[64,512]{1,0:T(8,128)(2,1)S(1)}) custom-call(bf16[256,128]{1,0:T(8,128)(2,1)S(1)} %get-tuple-element.41.hide_rows_ref, bf16[2048,128]{1,0:T(8,128)(2,1)S(1)} %get-tuple-element.42.hide_cols_ref, bf16[2048,512]{1,0:T(8,128)(2,1)S(1)} %bitcast.10, bf16[2048,512]{1,0:T(8,128)(2,1)S(1)} %bitcast.12, ...), custom_call_target="tpu_custom_call" | custom-call | flops 1073741824 | bytes 4194304 | tf_op jit(solution)/shard_map/pallas_call | solution.py:252
  27.4 0.0 copy-start.2
  27.4 1.8 %collective-permute-start.11 = (bf16[64,512]{1,0:T(8,128)(2,1)S(1)}, bf16[64,512]{1,0:T(8,128)(2,1)S(1)}, u32[]{:S(2)}, u32[]{:S(2)}) collective-permute-start(bf16[64,512]{1,0:T(8,128)(2,1)S(1)} %get-tuple-element.51), channel_id=1, source_target_pairs={{0,8},{2,10},{4,12},{6,14},{8,0},{10,2},{12,4},{14,6},{1,9},{3,11}... | collective-permute-start | bytes 196616 | tf_op jit(solution)/shard_map/ppermute | solution.py:189
  29.2 1.4 %collective-permute-start.13 = (bf16[64,512]{1,0:T(8,128)(2,1)S(1)}, bf16[64,512]{1,0:T(8,128)(2,1)S(1)}, u32[]{:S(2)}, u32[]{:S(2)}) collective-permute-start(bf16[64,512]{1,0:T(8,128)(2,1)S(1)} %get-tuple-element.52), channel_id=1, source_target_pairs={{0,12},{2,14},{4,8},{6,10},{8,4},{10,6},{12,0},{14,2},{1,13},{3,15... | collective-permute-start | bytes 196616 | tf_op jit(solution)/shard_map/ppermute | solution.py:189
  30.6 0.0 collective-permute-done.4.refs_1_
  30.6 0.0 collective-permute-done.5.refs_3_
  30.6 5.4 %shard_map.93 = (bf16[32,512]{1,0:T(8,128)(2,1)S(1)}, bf16[32,512]{1,0:T(8,128)(2,1)S(1)}, bf16[64,512]{1,0:T(8,128)(2,1)S(1)}) custom-call(bf16[256,128]{1,0:T(8,128)(2,1)S(1)} %get-tuple-element.41.hide_rows_ref, bf16[2048,128]{1,0:T(8,128)(2,1)S(1)} %get-tuple-element.42.hide_cols_ref, bf16[2048,512]{1,0:T(8,128)(2,1)S(1)} %bitcast.11, ...), custom_call_target="tpu_custom_call" | custom-call | flops 1073741824 | bytes 4194304 | tf_op jit(solution)/shard_map/pallas_call | solution.py:252
  36.1 0.4 collective-permute-start.7
  36.5 0.5 %collective-permute-start.6 = (bf16[32,512]{1,0:T(8,128)(2,1)S(1)}, bf16[32,512]{1,0:T(8,128)(2,1)S(1)}, u32[]{:S(2)}, u32[]{:S(2)}) collective-permute-start(bf16[32,512]{1,0:T(8,128)(2,1)S(1)} %get-tuple-element.47), channel_id=1, source_target_pairs={{0,2},{2,0},{4,6},{6,4},{8,10},{10,8},{12,14},{14,12},{1,3},{3,1},... | collective-permute-start | bytes 98312 | tf_op jit(solution)/shard_map/ppermute | solution.py:189
  37.0 0.0 collective-permute-done.11.refs_4_
  37.0 1.5 %collective-permute-start.12 = (bf16[32,512]{1,0:T(8,128)(2,1)S(1)}, bf16[32,512]{1,0:T(8,128)(2,1)S(1)}, u32[]{:S(2)}, u32[]{:S(2)}) collective-permute-start(bf16[32,512]{1,0:T(8,128)(2,1)S(1)} %slice.25), channel_id=1, source_target_pairs={{0,2},{2,0},{4,6},{6,4},{8,10},{10,8},{12,14},{14,12},{1,3},{3,1},... | collective-permute-start | bytes 98312 | tf_op jit(solution)/shard_map/ppermute | solution.py:189
  38.5 0.0 collective-permute-done.13.refs_6_
  38.5 0.5 %collective-permute-start.14 = (bf16[32,512]{1,0:T(8,128)(2,1)S(1)}, bf16[32,512]{1,0:T(8,128)(2,1)S(1)}, u32[]{:S(2)}, u32[]{:S(2)}) collective-permute-start(bf16[32,512]{1,0:T(8,128)(2,1)S(1)} %slice.26), channel_id=1, source_target_pairs={{0,2},{2,0},{4,6},{6,4},{8,10},{10,8},{12,14},{14,12},{1,3},{3,1},... | collective-permute-start | bytes 98312 | tf_op jit(solution)/shard_map/ppermute | solution.py:189
  39.0 1.4 %collective-permute-done.7.refs_2_ = bf16[64,512]{1,0:T(8,128)(2,1)S(1)} collective-permute-done((bf16[64,512]{1,0:T(8,128)(2,1)S(1)}, bf16[64,512]{1,0:T(8,128)(2,1)S(1)}, u32[]{:S(2)}, u32[]{:S(2)}) %collective-permute-start.7) | collective-permute-done | bytes 65568 | tf_op jit(solution)/shard_map/ppermute | solution.py:189
  40.4 0.5 %collective-permute-start.8 = (bf16[32,512]{1,0:T(8,128)(2,1)S(1)}, bf16[32,512]{1,0:T(8,128)(2,1)S(1)}, u32[]{:S(2)}, u32[]{:S(2)}) collective-permute-start(bf16[32,512]{1,0:T(8,128)(2,1)S(1)} %slice.24), channel_id=1, source_target_pairs={{0,2},{2,0},{4,6},{6,4},{8,10},{10,8},{12,14},{14,12},{1,3},{3,1},... | collective-permute-start | bytes 98312 | tf_op jit(solution)/shard_map/ppermute | solution.py:189
  40.9 0.0 collective-permute-done.6.refs_1_
  40.9 0.0 collective-permute-done.12.refs_5_
  40.9 1.5 %collective-permute-done.14.refs_7_ = bf16[32,512]{1,0:T(8,128)(2,1)S(1)} collective-permute-done((bf16[32,512]{1,0:T(8,128)(2,1)S(1)}, bf16[32,512]{1,0:T(8,128)(2,1)S(1)}, u32[]{:S(2)}, u32[]{:S(2)}) %collective-permute-start.14) | collective-permute-done | bytes 32800 | tf_op jit(solution)/shard_map/ppermute | solution.py:189
  42.4 1.9 %collective-permute-done.8.refs_3_ = bf16[32,512]{1,0:T(8,128)(2,1)S(1)} collective-permute-done((bf16[32,512]{1,0:T(8,128)(2,1)S(1)}, bf16[32,512]{1,0:T(8,128)(2,1)S(1)}, u32[]{:S(2)}, u32[]{:S(2)}) %collective-permute-start.8) | collective-permute-done | bytes 32800 | tf_op jit(solution)/shard_map/ppermute | solution.py:189
  44.3 0.7 %shard_map.95 = (bf16[64,512]{1,0:T(8,128)(2,1)S(1)}, bf16[64,512]{1,0:T(8,128)(2,1)S(1)}) custom-call(s32[64]{0:T(128)S(1)} %bitcast.17, f32[128,512]{1,0:T(8,128)S(1)} %get-tuple-element.39.own_ref, bf16[128,512]{1,0:T(8,128)(2,1)S(1)} %get-tuple-element.40.gates_ref, bf16[32,512]{1,0:T(8,128)(2,1)S(1)} %get-tuple-element.46.refs_0_, ...), custom_call_target="tpu_custom_call" | custom-call | tf_op jit(solution)/shard_map/pallas_call | solution.py:266
  45.0 0.1 collective-permute-start.15
  45.1 0.0 copy-done.2
  45.1 0.3 shard_map.96.kept_ref
  45.4 0.9 %collective-permute-done.15.got_ref = bf16[64,512]{1,0:T(8,128)(2,1)S(1)} collective-permute-done((bf16[64,512]{1,0:T(8,128)(2,1)S(1)}, bf16[64,512]{1,0:T(8,128)(2,1)S(1)}, u32[]{:S(2)}, u32[]{:S(2)}) %collective-permute-start.15) | collective-permute-done | bytes 65568 | tf_op jit(solution)/shard_map/ppermute | solution.py:272
  46.4 0.0 collective-permute-done.16.w_other_ref
  46.4 1.0 %shard_map.97 = bf16[8,8,1024]{2,1,0:T(8,128)(2,1)} custom-call(f32[64,1024]{1,0:T(8,128)S(1)} %shard_map.96.kept_ref, bf16[64,512]{1,0:T(8,128)(2,1)S(1)} %collective-permute-done.15.got_ref, bf16[512,1024]{1,0:T(8,128)(2,1)S(1)} %collective-permute-done.16.w_other_ref), custom_call_target="tpu_custom_call" | custom-call | flops 134217728 | bytes 1048576 | tf_op jit(solution)/shard_map/pallas_call | solution.py:280
  (7 shorter events, 0.0 us)
Async XLA Ops:
  0.0 3.7 %copy-start.3 = (bf16[8,8,1024]{2,1,0:T(8,128)(2,1)S(1)}, bf16[8,8,1024]{2,1,0:T(8,128)(2,1)}, u32[]{:S(2)}) copy-start(bf16[8,8,1024]{2,1,0:T(8,128)(2,1)} %own_ref.3) | copy-start | bytes 393220
  0.0 3.6 %copy-start.7 = (bf16[1024]{0:T(1024)(128)(2,1)S(1)}, bf16[1024]{0:T(1024)(128)(2,1)}, u32[]{:S(2)}) copy-start(bf16[1024]{0:T(1024)(128)(2,1)} %param.10) | copy-start | bytes 6148
  0.0 3.7 %copy-start.5 = (s32[64,1]{0,1:T(1,128)S(1)}, s32[64,1]{0,1:T(1,128)}, u32[]{:S(2)}) copy-start(s32[64,1]{0,1:T(1,128)} %param.15) | copy-start | bytes 772
  0.0 46.4 %collective-permute-start.16 = (bf16[512,1024]{1,0:T(8,128)(2,1)}, bf16[512,1024]{1,0:T(8,128)(2,1)S(1)}, u32[]{:S(2)}, u32[]{:S(2)}) collective-permute-start(bf16[512,1024]{1,0:T(8,128)(2,1)} %w_own_ref.1), channel_id=1, source_target_pairs={{0,1},{1,0},{2,3},{3,2},{4,5},{5,4},{6,7},{7,6},{8,9},{9,8},{10,11... | collective-permute-start | bytes 3145736 | tf_op jit(solution)/shard_map/ppermute | solution.py:247
  0.5 3.2 %collective-permute-start = (bf16[8,8,1024]{2,1,0:T(8,128)(2,1)}, bf16[8,8,1024]{2,1,0:T(8,128)(2,1)S(1)}, u32[]{:S(2)}, u32[]{:S(2)}) collective-permute-start(bf16[8,8,1024]{2,1,0:T(8,128)(2,1)} %own_ref.3), channel_id=1, source_target_pairs={{0,1},{1,0},{2,3},{3,2},{4,5},{5,4},{6,7},{7,6},{8,9},{9,8},{10,11... | collective-permute-start | bytes 393224 | tf_op jit(solution)/shard_map/ppermute | solution.py:216
  3.6 6.7 %copy-start.4 = (s32[64,32]{0,1:T(8,128)S(1)}, s32[64,32]{0,1:T(8,128)}, u32[]{:S(2)}) copy-start(s32[64,32]{0,1:T(8,128)} %param.17) | copy-start | bytes 24580
  3.7 6.7 %copy-start.6 = (s32[8]{0:T(128)S(1)}, s32[8]{0:T(128)}, u32[]{:S(2)}) copy-start(s32[8]{0:T(128)} %len_ref.1) | copy-start | bytes 100
  3.7 18.3 %copy-start = (bf16[1,2048,512]{2,1,0:T(8,128)(2,1)S(1)}, bf16[1,2048,512]{2,1,0:T(8,128)(2,1)}, u32[]{:S(2)}) copy-start(bf16[1,2048,512]{2,1,0:T(8,128)(2,1)} %param.13) | copy-start | bytes 6291460
  3.7 18.3 %copy-start.1 = (bf16[1,2048,512]{2,1,0:T(8,128)(2,1)S(1)}, bf16[1,2048,512]{2,1,0:T(8,128)(2,1)}, u32[]{:S(2)}) copy-start(bf16[1,2048,512]{2,1,0:T(8,128)(2,1)} %param.14) | copy-start | bytes 6291460
  4.7 7.4 %collective-permute-start.1 = (bf16[64,512]{1,0:T(8,128)(2,1)S(1)}, bf16[64,512]{1,0:T(8,128)(2,1)S(1)}, u32[]{:S(2)}, u32[]{:S(2)}) collective-permute-start(bf16[64,512]{1,0:T(8,128)(2,1)S(1)} %get-tuple-element.30), channel_id=1, source_target_pairs={{0,4},{2,6},{4,0},{6,2},{8,12},{10,14},{12,8},{14,10},{1,5},{3,7},... | collective-permute-start | bytes 196616 | tf_op jit(solution)/shard_map/ppermute | solution.py:189
  7.8 7.5 %collective-permute-start.2 = (bf16[64,512]{1,0:T(8,128)(2,1)S(1)}, bf16[64,512]{1,0:T(8,128)(2,1)S(1)}, u32[]{:S(2)}, u32[]{:S(2)}) collective-permute-start(bf16[64,512]{1,0:T(8,128)(2,1)S(1)} %get-tuple-element.31), channel_id=1, source_target_pairs={{0,8},{2,10},{4,12},{6,14},{8,0},{10,2},{12,4},{14,6},{1,9},{3,11}... | collective-permute-start | bytes 196616 | tf_op jit(solution)/shard_map/ppermute | solution.py:189
  10.4 6.2 %collective-permute-start.3 = (bf16[64,512]{1,0:T(8,128)(2,1)S(1)}, bf16[64,512]{1,0:T(8,128)(2,1)S(1)}, u32[]{:S(2)}, u32[]{:S(2)}) collective-permute-start(bf16[64,512]{1,0:T(8,128)(2,1)S(1)} %get-tuple-element.32), channel_id=1, source_target_pairs={{0,12},{2,14},{4,8},{6,10},{8,4},{10,6},{12,0},{14,2},{1,13},{3,15... | collective-permute-start | bytes 196616 | tf_op jit(solution)/shard_map/ppermute | solution.py:189
  16.5 4.2 %collective-permute-start.10 = (bf16[32,512]{1,0:T(8,128)(2,1)S(1)}, bf16[32,512]{1,0:T(8,128)(2,1)S(1)}, u32[]{:S(2)}, u32[]{:S(2)}) collective-permute-start(bf16[32,512]{1,0:T(8,128)(2,1)S(1)} %slice.21), channel_id=1, source_target_pairs={{0,2},{2,0},{4,6},{6,4},{8,10},{10,8},{12,14},{14,12},{1,3},{3,1},... | collective-permute-start | bytes 98312 | tf_op jit(solution)/shard_map/ppermute | solution.py:189
  18.1 3.9 %collective-permute-start.9 = (bf16[32,512]{1,0:T(8,128)(2,1)S(1)}, bf16[32,512]{1,0:T(8,128)(2,1)S(1)}, u32[]{:S(2)}, u32[]{:S(2)}) collective-permute-start(bf16[32,512]{1,0:T(8,128)(2,1)S(1)} %slice.20), channel_id=1, source_target_pairs={{0,2},{2,0},{4,6},{6,4},{8,10},{10,8},{12,14},{14,12},{1,3},{3,1},... | collective-permute-start | bytes 98312 | tf_op jit(solution)/shard_map/ppermute | solution.py:189
  18.6 12.1 %collective-permute-start.4 = (bf16[32,512]{1,0:T(8,128)(2,1)S(1)}, bf16[32,512]{1,0:T(8,128)(2,1)S(1)}, u32[]{:S(2)}, u32[]{:S(2)}) collective-permute-start(bf16[32,512]{1,0:T(8,128)(2,1)S(1)} %get-tuple-element.44), channel_id=1, source_target_pairs={{0,2},{2,0},{4,6},{6,4},{8,10},{10,8},{12,14},{14,12},{1,3},{3,1},... | collective-permute-start | bytes 98312 | tf_op jit(solution)/shard_map/ppermute | solution.py:189
  20.1 10.5 %collective-permute-start.5 = (bf16[32,512]{1,0:T(8,128)(2,1)S(1)}, bf16[32,512]{1,0:T(8,128)(2,1)S(1)}, u32[]{:S(2)}, u32[]{:S(2)}) collective-permute-start(bf16[32,512]{1,0:T(8,128)(2,1)S(1)} %slice.18), channel_id=1, source_target_pairs={{0,2},{2,0},{4,6},{6,4},{8,10},{10,8},{12,14},{14,12},{1,3},{3,1},... | collective-permute-start | bytes 98312 | tf_op jit(solution)/shard_map/ppermute | solution.py:189
  27.4 17.7 %copy-start.2 = (bf16[512,1024]{1,0:T(8,128)(2,1)S(1)}, bf16[512,1024]{1,0:T(8,128)(2,1)}, u32[]{:S(2)}) copy-start(bf16[512,1024]{1,0:T(8,128)(2,1)} %w_own_ref.1) | copy-start | bytes 3145732
  27.4 9.6 %collective-permute-start.11 = (bf16[64,512]{1,0:T(8,128)(2,1)S(1)}, bf16[64,512]{1,0:T(8,128)(2,1)S(1)}, u32[]{:S(2)}, u32[]{:S(2)}) collective-permute-start(bf16[64,512]{1,0:T(8,128)(2,1)S(1)} %get-tuple-element.51), channel_id=1, source_target_pairs={{0,8},{2,10},{4,12},{6,14},{8,0},{10,2},{12,4},{14,6},{1,9},{3,11}... | collective-permute-start | bytes 196616 | tf_op jit(solution)/shard_map/ppermute | solution.py:189
  29.2 9.3 %collective-permute-start.13 = (bf16[64,512]{1,0:T(8,128)(2,1)S(1)}, bf16[64,512]{1,0:T(8,128)(2,1)S(1)}, u32[]{:S(2)}, u32[]{:S(2)}) collective-permute-start(bf16[64,512]{1,0:T(8,128)(2,1)S(1)} %get-tuple-element.52), channel_id=1, source_target_pairs={{0,12},{2,14},{4,8},{6,10},{8,4},{10,6},{12,0},{14,2},{1,13},{3,15... | collective-permute-start | bytes 196616 | tf_op jit(solution)/shard_map/ppermute | solution.py:189
  36.1 4.3 %collective-permute-start.7 = (bf16[64,512]{1,0:T(8,128)(2,1)S(1)}, bf16[64,512]{1,0:T(8,128)(2,1)S(1)}, u32[]{:S(2)}, u32[]{:S(2)}) collective-permute-start(bf16[64,512]{1,0:T(8,128)(2,1)S(1)} %get-tuple-element.48), channel_id=1, source_target_pairs={{0,4},{2,6},{4,0},{6,2},{8,12},{10,14},{12,8},{14,10},{1,5},{3,7},... | collective-permute-start | bytes 196616 | tf_op jit(solution)/shard_map/ppermute | solution.py:189
  36.5 4.4 %collective-permute-start.6 = (bf16[32,512]{1,0:T(8,128)(2,1)S(1)}, bf16[32,512]{1,0:T(8,128)(2,1)S(1)}, u32[]{:S(2)}, u32[]{:S(2)}) collective-permute-start(bf16[32,512]{1,0:T(8,128)(2,1)S(1)} %get-tuple-element.47), channel_id=1, source_target_pairs={{0,2},{2,0},{4,6},{6,4},{8,10},{10,8},{12,14},{14,12},{1,3},{3,1},... | collective-permute-start | bytes 98312 | tf_op jit(solution)/shard_map/ppermute | solution.py:189
  37.0 3.9 %collective-permute-start.12 = (bf16[32,512]{1,0:T(8,128)(2,1)S(1)}, bf16[32,512]{1,0:T(8,128)(2,1)S(1)}, u32[]{:S(2)}, u32[]{:S(2)}) collective-permute-start(bf16[32,512]{1,0:T(8,128)(2,1)S(1)} %slice.25), channel_id=1, source_target_pairs={{0,2},{2,0},{4,6},{6,4},{8,10},{10,8},{12,14},{14,12},{1,3},{3,1},... | collective-permute-start | bytes 98312 | tf_op jit(solution)/shard_map/ppermute | solution.py:189
  38.5 3.9 %collective-permute-start.14 = (bf16[32,512]{1,0:T(8,128)(2,1)S(1)}, bf16[32,512]{1,0:T(8,128)(2,1)S(1)}, u32[]{:S(2)}, u32[]{:S(2)}) collective-permute-start(bf16[32,512]{1,0:T(8,128)(2,1)S(1)} %slice.26), channel_id=1, source_target_pairs={{0,2},{2,0},{4,6},{6,4},{8,10},{10,8},{12,14},{14,12},{1,3},{3,1},... | collective-permute-start | bytes 98312 | tf_op jit(solution)/shard_map/ppermute | solution.py:189
  40.4 3.9 %collective-permute-start.8 = (bf16[32,512]{1,0:T(8,128)(2,1)S(1)}, bf16[32,512]{1,0:T(8,128)(2,1)S(1)}, u32[]{:S(2)}, u32[]{:S(2)}) collective-permute-start(bf16[32,512]{1,0:T(8,128)(2,1)S(1)} %slice.24), channel_id=1, source_target_pairs={{0,2},{2,0},{4,6},{6,4},{8,10},{10,8},{12,14},{14,12},{1,3},{3,1},... | collective-permute-start | bytes 98312 | tf_op jit(solution)/shard_map/ppermute | solution.py:189
  45.0 1.3 %collective-permute-start.15 = (bf16[64,512]{1,0:T(8,128)(2,1)S(1)}, bf16[64,512]{1,0:T(8,128)(2,1)S(1)}, u32[]{:S(2)}, u32[]{:S(2)}) collective-permute-start(bf16[64,512]{1,0:T(8,128)(2,1)S(1)} %get-tuple-element.54), channel_id=1, source_target_pairs={{0,1},{1,0},{2,3},{3,2},{4,5},{5,4},{6,7},{7,6},{8,9},{9,8},{10,11... | collective-permute-start | bytes 196616 | tf_op jit(solution)/shard_map/ppermute | solution.py:272

commit v6 on v2

v6 whole, which is shorter than its diff:
```python
import functools

import jax
import jax.numpy as jnp
from jax import lax
from jax.experimental import pallas as pl
from jax.experimental.pallas import tpu as pltpu
from jax.sharding import PartitionSpec as P

HD = 128
BLK = 64
CAP = 2
EPS = 1e-06
SCALE = HD ** (-0.5)
HIDE = -1e30
VMEM_LIMIT = 16 * 1024 * 1024

vmem = pl.BlockSpec(memory_space=pltpu.VMEM)
smem = pl.BlockSpec(memory_space=pltpu.SMEM)


def silu_of_half(half):
    return half + half * jnp.tanh(half)


def silu(x):
    return silu_of_half(x * 0.5)


def kernel_call(body, out_shape, in_specs, scratch_shapes=(), flops=0, moved=0):
    return pl.pallas_call(
        body,
        out_shape=out_shape,
        in_specs=in_specs,
        out_specs=jax.tree.map(lambda _: vmem, out_shape),
        scratch_shapes=scratch_shapes,
        cost_estimate=pl.CostEstimate(flops=flops, bytes_accessed=moved, transcendentals=0),
        compiler_params=pltpu.CompilerParams(vmem_limit_bytes=VMEM_LIMIT),
    )


def normed_rows(rows_ref, gain):
    rows = rows_ref[...].astype(jnp.float32)
    count, cands, width = rows.shape
    rows = rows.reshape(count * cands, width)
    mean_square = jnp.mean(rows * rows, axis=-1, keepdims=True)
    return (rows * lax.rsqrt(mean_square + EPS) * gain).astype(jnp.bfloat16)


def position(distance, serve, owners):
    return jnp.where(distance % 2 == serve, 0, owners // 2) + distance // 2


def own_slots(sess_ref, req_count):
    me = lax.axis_index("cache")
    base = me * req_count
    sessions = [sess_ref[base + request] for request in range(req_count)]
    slots = []
    for request in range(req_count):
        place = 0
        for earlier in range(request):
            place = place + (sessions[earlier] == sessions[request]).astype(jnp.int32)
        slots.append((sessions[request] ^ me, place))
    return slots


def query_kernel(sess_ref, own_ref, other_ref, gain_ref, w_ref, keep_ref, give_ref, queries_ref, normed_ref, table_ref):
    req_count, half_cands, _ = own_ref.shape
    rows = req_count * half_cands
    serve = lax.axis_index("serve")
    slots = table_ref.shape[0]
    gain = gain_ref[...].astype(jnp.float32)
    normed_ref[:rows, :] = normed_rows(own_ref, gain)
    normed_ref[rows:, :] = normed_rows(other_ref, gain)
    table_ref[...] = jnp.zeros_like(table_ref)
    queries = silu(jnp.dot(normed_ref[...], w_ref[0], preferred_element_type=jnp.float32))
    queries_ref[...] = queries.astype(jnp.bfloat16)
    for request, (distance, place) in enumerate(own_slots(sess_ref, req_count)):
        low = request * half_cands
        both = jnp.concatenate([queries[low : low + half_cands], queries[rows + low : rows + low + half_cands]], axis=0)
        table_ref[position(distance, serve, slots // CAP) * CAP + place] = both.astype(jnp.bfloat16)
    keep_ref[...] = table_ref[: slots // 2].reshape(keep_ref.shape)
    give_ref[...] = table_ref[slots // 2 :].reshape(give_ref.shape)


def self_kernel(sess_ref, len_ref, mask_ref, normed_ref, queries_ref, w_ref, terms_ref, hide_rows_ref, hide_cols_ref, marks_ref):
    width = queries_ref.shape[1]
    normed = normed_ref[...]
    me = lax.axis_index("cache")
    keys = silu(jnp.dot(normed, w_ref[1], preferred_element_type=jnp.float32)).astype(jnp.bfloat16)
    products = queries_ref[...].astype(jnp.float32) * keys.astype(jnp.float32)
    values = silu(jnp.dot(normed, w_ref[2], preferred_element_type=jnp.float32)).astype(jnp.bfloat16)
    terms_ref[1] = silu(jnp.dot(normed, w_ref[3], preferred_element_type=jnp.float32)).astype(jnp.bfloat16)
    for low in range(0, width, HD):
        score = jnp.sum(products[:, low : low + HD], axis=-1, keepdims=True) * SCALE
        own_term = silu(score) * values[:, low : low + HD].astype(jnp.float32)
        terms_ref[0, :, low : low + HD] = own_term.astype(jnp.bfloat16)

    blocks, requests = mask_ref.shape
    owners = len_ref.shape[0]
    per_owner = requests // owners
    sessions = sess_ref[...]
    lane = lax.broadcasted_iota(jnp.int32, (1, requests), 1)
    place = jnp.zeros((1, requests), jnp.int32)
    for back in range(1, per_owner):
        same = (pltpu.roll(sessions, back, 1) == sessions) & (lane % per_owner >= back)
        place = place + same.astype(jnp.int32)
    at = position((lane // per_owner) ^ me, lax.axis_index("serve"), owners)
    slot_of = jnp.where(sessions == me, at * CAP + place, -1)
    slots = owners * CAP
    at_slot = lax.broadcasted_iota(jnp.int32, (slots, requests), 0)
    chosen = (at_slot == slot_of).astype(jnp.float32).astype(jnp.bfloat16)
    marks_ref[...] = jnp.zeros_like(marks_ref)
    marks_ref[:blocks, :] = mask_ref[...].astype(jnp.float32).astype(jnp.bfloat16)
    seen = lax.dot_general(chosen, marks_ref[...], (((1,), (1,)), ((), ())), preferred_element_type=jnp.float32)
    at_lane = lax.broadcasted_iota(jnp.int32, (slots, HD), 1)
    hidden = jnp.where(at_lane < blocks, (1.0 - seen) * HIDE, jnp.where(at_lane == blocks, HIDE, 0.0))
    per_slot = hide_rows_ref.shape[0] // slots
    hide_rows_ref[...] = (
        jnp.broadcast_to(hidden[:, None, :], (slots, per_slot, HD)).reshape(slots * per_slot, HD).astype(jnp.bfloat16)
    )
    hist_rows = hide_cols_ref.shape[0]
    at_row = lax.broadcasted_iota(jnp.int32, (hist_rows, HD), 0)
    at_lane = lax.broadcasted_iota(jnp.int32, (hist_rows, HD), 1)
    hide_cols_ref[...] = jnp.where(
        (at_lane == at_row // BLK) | ((at_lane == blocks) & (at_row >= len_ref[me])), 1.0, 0.0
    ).astype(jnp.bfloat16)


def pack_kernel(keep_ref, got_ref, *out_refs):
    half = out_refs[0].shape[0] // 2
    for at, out_ref in enumerate(out_refs):
        out_ref[:half, :] = keep_ref[at * half : (at + 1) * half, :]
        out_ref[half:, :] = got_ref[at * half : (at + 1) * half, :]


def history_kernel(owners, hide_rows_ref, hide_cols_ref, keys_ref, values_ref, *refs):
    slot_refs, (keep_ref, give_ref) = refs[:owners], refs[owners:]
    rows, width = keep_ref.shape
    per_owner = rows // (owners // 2)
    hist_rows = keys_ref.shape[0]
    span = min(256, hist_rows)
    per_step = max(1, min(owners, 256 // per_owner))
    for first in range(0, owners, per_step):
        group = range(first, min(first + per_step, owners))
        queries = jnp.concatenate([slot_refs[at][:per_owner, :] for at in group], axis=0)
        hide_rows = hide_rows_ref[first * per_owner : first * per_owner + queries.shape[0], :]
        for low in range(0, width, HD):
            lhs = jnp.concatenate([queries[:, low : low + HD], hide_rows], axis=1)
            total = None
            for start in range(0, hist_rows, span):
                rhs = jnp.concatenate(
                    [keys_ref[start : start + span, low : low + HD], hide_cols_ref[start : start + span, :]], axis=1
                )
                scores = lax.dot_general(lhs, rhs, (((1,), (1,)), ((), ())), preferred_element_type=jnp.float32)
                weights = silu_of_half(scores * (0.5 * SCALE)).astype(jnp.bfloat16)
                term = jnp.dot(
                    weights, values_ref[start : start + span, low : low + HD], preferred_element_type=jnp.float32
                )
                total = term if total is None else total + term
            total = total.astype(jnp.bfloat16)
            for place, at in enumerate(group):
                out_ref, row = (keep_ref, at * per_owner) if at < owners // 2 else (give_ref, at * per_owner - rows)
                out_ref[row : row + per_owner, low : low + HD] = total[place * per_owner : (place + 1) * per_owner]


def mix_kernel(messages, req_count, sess_ref, terms_ref, their_terms_ref, *refs):
    back_refs, (keep_ref, give_ref, table_ref) = refs[:messages], refs[messages:]
    rows, model_width = keep_ref.shape
    width = model_width // 2
    half_cands = rows // req_count
    slots = messages * CAP
    for at, back_ref in enumerate(back_refs):
        half = back_ref.shape[0] // 2
        for side in range(2):
            part = back_ref[side * half : (side + 1) * half, :].reshape((CAP,) + table_ref.shape[1:])
            table_ref[side * slots + at * CAP : side * slots + (at + 1) * CAP] = part
    picks = [distance // 2 * CAP + place for distance, place in own_slots(sess_ref, req_count)]
    for side, source_ref in enumerate((terms_ref, their_terms_ref)):
        picked = [table_ref[side * slots + pick].astype(jnp.float32) for pick in picks]
        for part in range(2):
            history = jnp.concatenate([both[part * half_cands : (part + 1) * half_cands] for both in picked], axis=0)
            attended = history + source_ref[0, part * rows : (part + 1) * rows, :].astype(jnp.float32)
            gates = source_ref[1, part * rows : (part + 1) * rows, :].astype(jnp.float32)
            ours = part == side
            out_ref, offset = (keep_ref, side * width) if ours else (give_ref, (1 - side) * width)
            for low in range(0, width, HD):
                head = attended[:, low : low + HD]
                level = lax.rsqrt(jnp.mean(head * head, axis=-1, keepdims=True) + EPS)
                mixed = head * level * gates[:, low : low + HD]
                out_ref[:, offset + low : offset + low + HD] = mixed.astype(jnp.bfloat16)


def output_kernel(sess_ref, own_ref, keep_ref, got_ref, w_own_ref, w_other_ref, out_ref):
    req_count, half_cands, model_width = own_ref.shape
    width = model_width // 2
    serve = lax.axis_index("serve")
    keep, got = keep_ref[...].astype(jnp.float32), got_ref[...].astype(jnp.float32)
    picked = []
    for request, (distance, _) in enumerate(own_slots(sess_ref, req_count)):
        low = request * half_cands
        picked.append(jnp.where(distance % 2 == serve, keep[low : low + half_cands], got[low : low + half_cands]))
    mixed = jnp.concatenate(picked, axis=0).astype(jnp.bfloat16)
    total = own_ref[...].astype(jnp.float32).reshape(req_count * half_cands, model_width)
    total = total + jnp.dot(mixed[:, :width], w_own_ref[...], preferred_element_type=jnp.float32)
    total = total + jnp.dot(mixed[:, width:], w_other_ref[...], preferred_element_type=jnp.float32)
    out_ref[...] = total.reshape(req_count, half_cands, model_width).astype(jnp.bfloat16)


def swap(rows):
    return lax.ppermute(rows, "serve", [(0, 1), (1, 0)])


def cross(owners, messages):
    came = {}
    for at in reversed(range(len(messages))):
        pairs = [
            (place * 2 + core, (place ^ (2 * at + core)) * 2 + core) for place in range(owners) for core in range(2)
        ]
        came[at] = lax.ppermute(messages[at], ("cache", "serve"), pairs)
    return [came[at] for at in range(len(messages))]


def body(candidates, input_gain, w_in, w_out, hist_keys, hist_values, request_session, hist_len, block_mask):
    owners = lax.axis_size("cache")
    req_count, half_cands, model_width = candidates.shape
    width = w_in.shape[2]
    cand_count = 2 * half_cands
    rows = req_count * half_cands
    hist_rows = hist_keys.shape[1]
    bf16 = functools.partial(jax.ShapeDtypeStruct, dtype=jnp.bfloat16)
    sessions = request_session.reshape(-1)
    messages = owners // 2
    piece = CAP * cand_count
    half_table = bf16((messages * piece, width))
    table = pltpu.VMEM((owners * CAP, cand_count, width), jnp.bfloat16)

    def pack(keep, got):
        return kernel_call(pack_kernel, [bf16((2 * piece, width))] * messages, [vmem] * 2)(keep, got)

    other = swap(candidates)
    weights = jnp.transpose(w_in, (1, 0, 2))
    keep, give, queries, normed = kernel_call(
        query_kernel,
        [half_table, half_table, bf16((2 * rows, width)), bf16((2 * rows, model_width))],
        [smem, vmem, vmem, vmem, vmem],
        [table],
        flops=4 * rows * model_width * width,
        moved=2 * model_width * width,
    )(sessions, candidates, other, input_gain.reshape(1, -1), weights)
    got = swap(give)
    own = kernel_call(
        self_kernel,
        [bf16((2, 2 * rows, width)), bf16((owners * piece, HD)), bf16((hist_rows, HD))],
        [vmem, smem, vmem, vmem, vmem, vmem],
        [pltpu.VMEM((HD, owners * req_count), jnp.bfloat16)],
        flops=12 * rows * model_width * width,
        moved=6 * model_width * width,
    )(request_session.reshape(1, -1), hist_len, block_mask.T, normed, queries, weights)
    got, (terms, hide_rows, hide_cols) = lax.optimization_barrier((got, own))
    came = cross(owners, pack(keep, got))
    slots = came + [swap(rows_of[piece:]) for rows_of in came]
    their_terms = swap(terms)
    w_other = swap(w_out)
    keep, give = kernel_call(
        functools.partial(history_kernel, owners),
        [half_table] * 2,
        [vmem] * (4 + owners),
        flops=8 * owners * piece * hist_rows * width,
        moved=4 * hist_rows * width,
    )(hide_rows, hide_cols, hist_keys.reshape(hist_rows, width), hist_values.reshape(hist_rows, width), *slots)
    backs = cross(owners, pack(keep, swap(give)))
    keep, give = kernel_call(
        functools.partial(mix_kernel, messages, req_count),
        [bf16((rows, model_width))] * 2,
        [smem] + [vmem] * (2 + messages),
        [table],
    )(sessions, terms, their_terms, *backs)
    return kernel_call(
        output_kernel,
        bf16((req_count, half_cands, model_width)),
        [smem] + [vmem] * 5,
        flops=8 * rows * model_width * width,
        moved=4 * model_width * width,
    )(sessions, candidates, keep, swap(give), w_out, w_other)


def solution(mesh):
    placed = (
        P(("groups", "cache"), "serve", None),
        P(),
        P(None, None, "serve"),
        P("serve", None),
        P(("groups", "cache"), None, "serve"),
        P(("groups", "cache"), None, "serve"),
        P("groups", None),
        P("groups"),
        P("groups", None),
    )
    return jax.shard_map(
        body,
        mesh=mesh,
        in_specs=placed,
        out_specs=P(("groups", "cache"), "serve", None),
        check_vma=False,
    )
```

time: 42.6 us -> 41.7 us (0.979)
  starting transfers between devices: 22.6 us -> 21.3 us
  Pallas kernels: 7.74 us -> 8.42 us
    ppermute x17 -> x18, starting transfers between devices: 22.6 us -> 21.3 us  [the longest x8 11.3 us: cross(): came[at] = lax.ppermute(messages[at], ('cache', 'serve'), pairs)]
    pallas_call x5 -> x7, Pallas kernels: 7.74 us -> 8.42 us  [the longest x1 3.18 us: body(): kernel_call(functools.partial(history_kernel, owners), [half_table] * 2,...]
    ppermute x17 -> x18, waiting for transfers between devices: 8.93 us -> 8.63 us  [the longest x8 5.84 us: cross(): came[at] = lax.ppermute(messages[at], ('cache', 'serve'), pairs)]
  transfers between devices with their start and end apart: 17 -> 18, of which waited for: 5 -> 5; matrix products, arithmetic and copies ran while one was open for 7% -> 7% of each run, Pallas kernels for 16% -> 16%
where the time goes in v6:
time: 41.7 us; the launch traced here: 41.6 us
  starting transfers between devices  21.3 us (51%)
  waiting for transfers between devices  8.63 us (21%)
  Pallas kernels  8.42 us (20%)
  local copies, waits for them, and re-layouts  3.08 us (7%)
    ppermute x8, starting transfers between devices, cross(): came[at] = lax.ppermute(messages[at], ('cache', 'serve'), pairs)  11.3 us
    ppermute x10, starting transfers between devices, swap(): return lax.ppermute(rows, 'serve', [(0, 1), (1, 0)])  9.97 us
    ppermute x8, waiting for transfers between devices, cross(): came[at] = lax.ppermute(messages[at], ('cache', 'serve'), pairs)  5.84 us
    pallas_call x1, Pallas kernels, body(): kernel_call(functools.partial(history_kernel, owners), [half_table] * 2,...  3.18 us
    unnamed x17, local copies, waits for them, and re-layouts  3.06 us
    ppermute x10, waiting for transfers between devices, swap(): return lax.ppermute(rows, 'serve', [(0, 1), (1, 0)])  2.79 us
    pallas_call x1, Pallas kernels, body(): kernel_call(output_kernel, bf16((req_count, half_cands, model_width)), [s...  1.69 us
    pallas_call x1, Pallas kernels, body(): kernel_call(self_kernel, [bf16((2, 2 * rows, width)), bf16((owners * piec...  1.69 us
  transfers between devices with their start and end apart: 18, of which 5 were waited for; matrix products, arithmetic and copies ran while one was open for 7% of the time, Pallas kernels for 16%

profile of v6, /device:TPU:0, one launch (start us, length us, event | category | flops | bytes accessed | tf_op | source)
XLA Modules:
  0.0 41.6 jit_solution(3436387376963058498)
XLA Ops:
  0.0 0.0 copy-start.1
  0.0 0.0 copy-start.7
  0.0 0.0 copy-start.3
  0.0 0.5 %collective-permute-start.17 = (bf16[512,1024]{1,0:T(8,128)(2,1)}, bf16[512,1024]{1,0:T(8,128)(2,1)S(1)}, u32[]{:S(2)}, u32[]{:S(2)}) collective-permute-start(bf16[512,1024]{1,0:T(8,128)(2,1)} %w_own_ref.1), channel_id=1, source_target_pairs={{0,1},{1,0},{2,3},{3,2},{4,5},{5,4},{6,7},{7,6},{8,9},{9,8},{10,11... | collective-permute-start | bytes 3145736 | tf_op jit(solution)/shard_map/ppermute | solution.py:211
  0.5 0.1 collective-permute-start
  0.6 3.0 %copy.12 = bf16[1024,4,512]{2,0,1:T(8,128)(2,1)S(1)} copy(bf16[1024,4,512]{2,1,0:T(4,128)(2,1)} %param.11) | data formatting | bytes 8388608 | tf_op args[2]
  3.6 0.0 copy-done.7
  3.6 0.0 copy-start.2
  3.7 0.0 copy-start.4
  3.7 0.0 collective-permute-done.other_ref
  3.7 0.0 copy-done.1
  3.7 0.0 copy-done.3
  3.7 0.0 copy-start.5
  3.7 0.0 copy-start.6
  3.7 1.0 %shard_map.91 = (bf16[128,512]{1,0:T(8,128)(2,1)S(1)}, bf16[128,512]{1,0:T(8,128)(2,1)S(1)}, bf16[128,512]{1,0:T(8,128)(2,1)S(1)}, bf16[128,1024]{1,0:T(8,128)(2,1)S(1)}) custom-call(s32[64]{0:T(128)S(1)} %bitcast.11, bf16[8,8,1024]{2,1,0:T(8,128)(2,1)S(1)} %copy-done.1, bf16[8,8,1024]{2,1,0:T(8,128)(2,1)S(1)} %collective-permute-done.other_ref, ...), custom_call_target="tpu_custom_call" | custom-call | flops 134217728 | bytes 1048576 | tf_op jit(solution)/shard_map/pallas_call | solution.py:243
  4.7 0.5 %collective-permute-start.1 = (bf16[128,512]{1,0:T(8,128)(2,1)S(1)}, bf16[128,512]{1,0:T(8,128)(2,1)S(1)}, u32[]{:S(2)}, u32[]{:S(2)}) collective-permute-start(bf16[128,512]{1,0:T(8,128)(2,1)S(1)} %get-tuple-element.28), channel_id=1, source_target_pairs={{0,1},{1,0},{2,3},{3,2},{4,5},{5,4},{6,7},{7,6},{8,9},{9,8},{10,11... | collective-permute-start | bytes 393224 | tf_op jit(solution)/shard_map/ppermute | solution.py:211
  5.2 0.0 copy-done.2
  5.2 0.0 copy-done.4
  5.2 1.7 %shard_map.92 = (bf16[2,128,512]{2,1,0:T(8,128)(2,1)S(1)}, bf16[256,128]{1,0:T(8,128)(2,1)S(1)}, bf16[2048,128]{1,0:T(8,128)(2,1)S(1)}) custom-call(s32[1,64]{1,0:T(1,128)S(1)} %bitcast.12, s32[8]{0:T(128)S(1)} %copy-done.4, s32[32,64]{1,0:T(8,128)S(1)} %bitcast.10, bf16[128,1024]{1,0:T(8,128)(2,1)S(1)} %get-tuple-element.29.normed_ref, ...), custom_call_target="tpu_custom_call" | custom-call | flops 402653184 | bytes 3145728 | tf_op jit(solution)/shard_map/pallas_call | solution.py:252
  6.9 0.0 collective-permute-done.1.got_ref
  7.0 4.7 %collective-permute-start.6 = (bf16[64,512]{1,0:T(8,128)(2,1)S(1)}, bf16[64,512]{1,0:T(8,128)(2,1)S(1)}, u32[]{:S(2)}, u32[]{:S(2)}) collective-permute-start(bf16[64,512]{1,0:T(8,128)(2,1)S(1)} %get-tuple-element.42), channel_id=1, source_target_pairs={{0,12},{1,15},{2,14},{3,13},{4,8},{5,11},{6,10},{7,9},{8,4},{9,7},... | collective-permute-start | bytes 196616 | tf_op jit(solution)/shard_map/ppermute | solution.py:220
  11.7 0.7 %collective-permute-start.3 = (bf16[64,512]{1,0:T(8,128)(2,1)S(1)}, bf16[64,512]{1,0:T(8,128)(2,1)S(1)}, u32[]{:S(2)}, u32[]{:S(2)}) collective-permute-start(bf16[64,512]{1,0:T(8,128)(2,1)S(1)} %get-tuple-element.39), channel_id=1, source_target_pairs={{0,0},{1,3},{2,2},{3,1},{4,4},{5,7},{6,6},{7,5},{8,8},{9,11},{10,1... | collective-permute-start | bytes 196616 | tf_op jit(solution)/shard_map/ppermute | solution.py:220
  12.4 0.1 collective-permute-start.4
  12.4 0.6 %collective-permute-start.5 = (bf16[64,512]{1,0:T(8,128)(2,1)S(1)}, bf16[64,512]{1,0:T(8,128)(2,1)S(1)}, u32[]{:S(2)}, u32[]{:S(2)}) collective-permute-start(bf16[64,512]{1,0:T(8,128)(2,1)S(1)} %get-tuple-element.41), channel_id=1, source_target_pairs={{0,8},{1,11},{2,10},{3,9},{4,12},{5,15},{6,14},{7,13},{8,0},{9,3},... | collective-permute-start | bytes 196616 | tf_op jit(solution)/shard_map/ppermute | solution.py:220
  13.0 1.1 %collective-permute-done.6.refs_3_ = bf16[64,512]{1,0:T(8,128)(2,1)S(1)} collective-permute-done((bf16[64,512]{1,0:T(8,128)(2,1)S(1)}, bf16[64,512]{1,0:T(8,128)(2,1)S(1)}, u32[]{:S(2)}, u32[]{:S(2)}) %collective-permute-start.6) | collective-permute-done | bytes 65568 | tf_op jit(solution)/shard_map/ppermute | solution.py:220
  14.2 2.1 %collective-permute-start.10 = (bf16[32,512]{1,0:T(8,128)(2,1)S(1)}, bf16[32,512]{1,0:T(8,128)(2,1)S(1)}, u32[]{:S(2)}, u32[]{:S(2)}) collective-permute-start(bf16[32,512]{1,0:T(8,128)(2,1)S(1)} %slice.19), channel_id=1, source_target_pairs={{0,1},{1,0},{2,3},{3,2},{4,5},{5,4},{6,7},{7,6},{8,9},{9,8},{10,11... | collective-permute-start | bytes 98312 | tf_op jit(solution)/shard_map/ppermute | solution.py:211
  16.3 0.0 collective-permute-done.3.refs_0_
  16.3 1.5 %collective-permute-start.7 = (bf16[32,512]{1,0:T(8,128)(2,1)S(1)}, bf16[32,512]{1,0:T(8,128)(2,1)S(1)}, u32[]{:S(2)}, u32[]{:S(2)}) collective-permute-start(bf16[32,512]{1,0:T(8,128)(2,1)S(1)} %slice.16), channel_id=1, source_target_pairs={{0,1},{1,0},{2,3},{3,2},{4,5},{5,4},{6,7},{7,6},{8,9},{9,8},{10,11... | collective-permute-start | bytes 98312 | tf_op jit(solution)/shard_map/ppermute | solution.py:211
  17.8 0.0 collective-permute-done.4.refs_1_
  17.8 1.3 %collective-permute-start.8 = (bf16[32,512]{1,0:T(8,128)(2,1)S(1)}, bf16[32,512]{1,0:T(8,128)(2,1)S(1)}, u32[]{:S(2)}, u32[]{:S(2)}) collective-permute-start(bf16[32,512]{1,0:T(8,128)(2,1)S(1)} %slice.17), channel_id=1, source_target_pairs={{0,1},{1,0},{2,3},{3,2},{4,5},{5,4},{6,7},{7,6},{8,9},{9,8},{10,11... | collective-permute-start | bytes 98312 | tf_op jit(solution)/shard_map/ppermute | solution.py:211
  19.1 0.0 collective-permute-done.5.refs_2_
  19.1 1.4 %collective-permute-start.9 = (bf16[32,512]{1,0:T(8,128)(2,1)S(1)}, bf16[32,512]{1,0:T(8,128)(2,1)S(1)}, u32[]{:S(2)}, u32[]{:S(2)}) collective-permute-start(bf16[32,512]{1,0:T(8,128)(2,1)S(1)} %slice.18), channel_id=1, source_target_pairs={{0,1},{1,0},{2,3},{3,2},{4,5},{5,4},{6,7},{7,6},{8,9},{9,8},{10,11... | collective-permute-start | bytes 98312 | tf_op jit(solution)/shard_map/ppermute | solution.py:211
  20.5 0.0 collective-permute-done.10.refs_7_
  20.5 0.1 collective-permute-start.2
  20.6 0.0 collective-permute-done.7.refs_4_
  20.6 0.0 collective-permute-done.8.refs_5_
  20.6 0.8 %collective-permute-done.9.refs_6_ = bf16[32,512]{1,0:T(8,128)(2,1)S(1)} collective-permute-done((bf16[32,512]{1,0:T(8,128)(2,1)S(1)}, bf16[32,512]{1,0:T(8,128)(2,1)S(1)}, u32[]{:S(2)}, u32[]{:S(2)}) %collective-permute-start.9) | collective-permute-done | bytes 32800 | tf_op jit(solution)/shard_map/ppermute | solution.py:211
  21.4 0.0 copy-done.5
  21.4 0.0 copy-done.6
  21.4 0.0 copy-start
  21.4 3.2 %shard_map.94 = (bf16[128,512]{1,0:T(8,128)(2,1)S(1)}, bf16[128,512]{1,0:T(8,128)(2,1)S(1)}) custom-call(bf16[256,128]{1,0:T(8,128)(2,1)S(1)} %get-tuple-element.35.hide_rows_ref, bf16[2048,128]{1,0:T(8,128)(2,1)S(1)} %get-tuple-element.36.hide_cols_ref, bf16[2048,512]{1,0:T(8,128)(2,1)S(1)} %bitcast.15, bf16[2048,512]{1,0:T(8,128)(2,1)S(1)} %bitcast.16, ...), custom_call_target="tpu_custom_call" | custom-call | flops 2147483648 | bytes 4194304 | tf_op jit(solution)/shard_map/pallas_call | solution.py:265
  24.6 0.4 collective-permute-start.11
  25.0 1.0 %collective-permute-done.11.got_ref = bf16[128,512]{1,0:T(8,128)(2,1)S(1)} collective-permute-done((bf16[128,512]{1,0:T(8,128)(2,1)S(1)}, bf16[128,512]{1,0:T(8,128)(2,1)S(1)}, u32[]{:S(2)}, u32[]{:S(2)}) %collective-permute-start.11) | collective-permute-done | bytes 131104 | tf_op jit(solution)/shard_map/ppermute | solution.py:211
  26.0 0.7 %collective-permute-start.12 = (bf16[64,512]{1,0:T(8,128)(2,1)S(1)}, bf16[64,512]{1,0:T(8,128)(2,1)S(1)}, u32[]{:S(2)}, u32[]{:S(2)}) collective-permute-start(bf16[64,512]{1,0:T(8,128)(2,1)S(1)} %get-tuple-element.45), channel_id=1, source_target_pairs={{0,0},{1,3},{2,2},{3,1},{4,4},{5,7},{6,6},{7,5},{8,8},{9,11},{10,1... | collective-permute-start | bytes 196616 | tf_op jit(solution)/shard_map/ppermute | solution.py:220
  26.7 2.2 %collective-permute-start.13 = (bf16[64,512]{1,0:T(8,128)(2,1)S(1)}, bf16[64,512]{1,0:T(8,128)(2,1)S(1)}, u32[]{:S(2)}, u32[]{:S(2)}) collective-permute-start(bf16[64,512]{1,0:T(8,128)(2,1)S(1)} %get-tuple-element.46), channel_id=1, source_target_pairs={{0,4},{1,7},{2,6},{3,5},{4,0},{5,3},{6,2},{7,1},{8,12},{9,15},{10,... | collective-permute-start | bytes 196616 | tf_op jit(solution)/shard_map/ppermute | solution.py:220
  28.8 0.0 collective-permute-start.14
  28.8 0.0 collective-permute-done.2.their_terms_ref
  28.8 2.4 %collective-permute-start.15 = (bf16[64,512]{1,0:T(8,128)(2,1)S(1)}, bf16[64,512]{1,0:T(8,128)(2,1)S(1)}, u32[]{:S(2)}, u32[]{:S(2)}) collective-permute-start(bf16[64,512]{1,0:T(8,128)(2,1)S(1)} %get-tuple-element.48), channel_id=1, source_target_pairs={{0,12},{1,15},{2,14},{3,13},{4,8},{5,11},{6,10},{7,9},{8,4},{9,7},... | collective-permute-start | bytes 196616 | tf_op jit(solution)/shard_map/ppermute | solution.py:220
  31.3 0.0 collective-permute-done.12.refs_0_
  31.3 0.0 collective-permute-done.13.refs_1_
  31.3 4.7 %collective-permute-done.14.refs_2_ = bf16[64,512]{1,0:T(8,128)(2,1)S(1)} collective-permute-done((bf16[64,512]{1,0:T(8,128)(2,1)S(1)}, bf16[64,512]{1,0:T(8,128)(2,1)S(1)}, u32[]{:S(2)}, u32[]{:S(2)}) %collective-permute-start.14) | collective-permute-done | bytes 65568 | tf_op jit(solution)/shard_map/ppermute | solution.py:220
  36.0 0.0 collective-permute-done.15.refs_3_
  36.0 0.8 %shard_map.96 = (bf16[64,1024]{1,0:T(8,128)(2,1)S(1)}, bf16[64,1024]{1,0:T(8,128)(2,1)S(1)}) custom-call(s32[64]{0:T(128)S(1)} %bitcast.13, bf16[2,128,512]{2,1,0:T(8,128)(2,1)S(1)} %get-tuple-element.34.terms_ref, bf16[2,128,512]{2,1,0:T(8,128)(2,1)S(1)} %collective-permute-done.2.their_terms_ref, bf16[64,512]{1,0:T(8,128)(2,1)S(1)} %collective-permute-done.12.refs_0_, ...), custom_call_target="tpu_custom_call" | custom-call | tf_op jit(solution)/shard_map/pallas_call | solution.py:273
  36.8 2.0 %collective-permute-start.16 = (bf16[64,1024]{1,0:T(8,128)(2,1)S(1)}, bf16[64,1024]{1,0:T(8,128)(2,1)S(1)}, u32[]{:S(2)}, u32[]{:S(2)}) collective-permute-start(bf16[64,1024]{1,0:T(8,128)(2,1)S(1)} %get-tuple-element.50), channel_id=1, source_target_pairs={{0,1},{1,0},{2,3},{3,2},{4,5},{5,4},{6,7},{7,6},{8,9},{9,8},{10,11... | collective-permute-start | bytes 393224 | tf_op jit(solution)/shard_map/ppermute | solution.py:211
  38.9 1.0 %collective-permute-done.16.got_ref = bf16[64,1024]{1,0:T(8,128)(2,1)S(1)} collective-permute-done((bf16[64,1024]{1,0:T(8,128)(2,1)S(1)}, bf16[64,1024]{1,0:T(8,128)(2,1)S(1)}, u32[]{:S(2)}, u32[]{:S(2)}) %collective-permute-start.16) | collective-permute-done | bytes 131104 | tf_op jit(solution)/shard_map/ppermute | solution.py:211
  39.9 0.0 collective-permute-done.17.w_other_ref
  39.9 0.0 copy-done
  39.9 1.7 %shard_map.97 = bf16[8,8,1024]{2,1,0:T(8,128)(2,1)} custom-call(s32[64]{0:T(128)S(1)} %bitcast.14, bf16[8,8,1024]{2,1,0:T(8,128)(2,1)S(1)} %copy-done.1, bf16[64,1024]{1,0:T(8,128)(2,1)S(1)} %get-tuple-element.49.keep_ref, bf16[64,1024]{1,0:T(8,128)(2,1)S(1)} %collective-permute-done.16.got_ref, bf16[512,1024]{1,0:T(8,128)(2,1)S(1)} %copy-done, ...), custom_call_target="tpu_custom_call" | custom-call | flops 268435456 | bytes 2097152 | tf_op jit(solution)/shard_map/pallas_call | solution.py:279
  (7 shorter events, 0.1 us)
Async XLA Ops:
  0.0 3.7 %copy-start.1 = (bf16[8,8,1024]{2,1,0:T(8,128)(2,1)S(1)}, bf16[8,8,1024]{2,1,0:T(8,128)(2,1)}, u32[]{:S(2)}) copy-start(bf16[8,8,1024]{2,1,0:T(8,128)(2,1)} %own_ref.3) | copy-start | bytes 393220
  0.0 3.6 %copy-start.7 = (bf16[1024]{0:T(1024)(128)(2,1)S(1)}, bf16[1024]{0:T(1024)(128)(2,1)}, u32[]{:S(2)}) copy-start(bf16[1024]{0:T(1024)(128)(2,1)} %param.10) | copy-start | bytes 6148
  0.0 3.7 %copy-start.3 = (s32[64,1]{0,1:T(1,128)S(1)}, s32[64,1]{0,1:T(1,128)}, u32[]{:S(2)}) copy-start(s32[64,1]{0,1:T(1,128)} %param.15) | copy-start | bytes 772
  0.0 39.9 %collective-permute-start.17 = (bf16[512,1024]{1,0:T(8,128)(2,1)}, bf16[512,1024]{1,0:T(8,128)(2,1)S(1)}, u32[]{:S(2)}, u32[]{:S(2)}) collective-permute-start(bf16[512,1024]{1,0:T(8,128)(2,1)} %w_own_ref.1), channel_id=1, source_target_pairs={{0,1},{1,0},{2,3},{3,2},{4,5},{5,4},{6,7},{7,6},{8,9},{9,8},{10,11... | collective-permute-start | bytes 3145736 | tf_op jit(solution)/shard_map/ppermute | solution.py:211
  0.5 3.2 %collective-permute-start = (bf16[8,8,1024]{2,1,0:T(8,128)(2,1)}, bf16[8,8,1024]{2,1,0:T(8,128)(2,1)S(1)}, u32[]{:S(2)}, u32[]{:S(2)}) collective-permute-start(bf16[8,8,1024]{2,1,0:T(8,128)(2,1)} %own_ref.3), channel_id=1, source_target_pairs={{0,1},{1,0},{2,3},{3,2},{4,5},{5,4},{6,7},{7,6},{8,9},{9,8},{10,11... | collective-permute-start | bytes 393224 | tf_op jit(solution)/shard_map/ppermute | solution.py:211
  3.6 1.6 %copy-start.2 = (s32[64,32]{0,1:T(8,128)S(1)}, s32[64,32]{0,1:T(8,128)}, u32[]{:S(2)}) copy-start(s32[64,32]{0,1:T(8,128)} %param.17) | copy-start | bytes 24580
  3.7 1.6 %copy-start.4 = (s32[8]{0:T(128)S(1)}, s32[8]{0:T(128)}, u32[]{:S(2)}) copy-start(s32[8]{0:T(128)} %len_ref.1) | copy-start | bytes 100
  3.7 17.7 %copy-start.5 = (bf16[1,2048,512]{2,1,0:T(8,128)(2,1)S(1)}, bf16[1,2048,512]{2,1,0:T(8,128)(2,1)}, u32[]{:S(2)}) copy-start(bf16[1,2048,512]{2,1,0:T(8,128)(2,1)} %param.13) | copy-start | bytes 6291460
  3.7 17.7 %copy-start.6 = (bf16[1,2048,512]{2,1,0:T(8,128)(2,1)S(1)}, bf16[1,2048,512]{2,1,0:T(8,128)(2,1)}, u32[]{:S(2)}) copy-start(bf16[1,2048,512]{2,1,0:T(8,128)(2,1)} %param.14) | copy-start | bytes 6291460
  4.7 2.2 %collective-permute-start.1 = (bf16[128,512]{1,0:T(8,128)(2,1)S(1)}, bf16[128,512]{1,0:T(8,128)(2,1)S(1)}, u32[]{:S(2)}, u32[]{:S(2)}) collective-permute-start(bf16[128,512]{1,0:T(8,128)(2,1)S(1)} %get-tuple-element.28), channel_id=1, source_target_pairs={{0,1},{1,0},{2,3},{3,2},{4,5},{5,4},{6,7},{7,6},{8,9},{9,8},{10,11... | collective-permute-start | bytes 393224 | tf_op jit(solution)/shard_map/ppermute | solution.py:211
  7.0 7.2 %collective-permute-start.6 = (bf16[64,512]{1,0:T(8,128)(2,1)S(1)}, bf16[64,512]{1,0:T(8,128)(2,1)S(1)}, u32[]{:S(2)}, u32[]{:S(2)}) collective-permute-start(bf16[64,512]{1,0:T(8,128)(2,1)S(1)} %get-tuple-element.42), channel_id=1, source_target_pairs={{0,12},{1,15},{2,14},{3,13},{4,8},{5,11},{6,10},{7,9},{8,4},{9,7},... | collective-permute-start | bytes 196616 | tf_op jit(solution)/shard_map/ppermute | solution.py:220
  11.7 4.6 %collective-permute-start.3 = (bf16[64,512]{1,0:T(8,128)(2,1)S(1)}, bf16[64,512]{1,0:T(8,128)(2,1)S(1)}, u32[]{:S(2)}, u32[]{:S(2)}) collective-permute-start(bf16[64,512]{1,0:T(8,128)(2,1)S(1)} %get-tuple-element.39), channel_id=1, source_target_pairs={{0,0},{1,3},{2,2},{3,1},{4,4},{5,7},{6,6},{7,5},{8,8},{9,11},{10,1... | collective-permute-start | bytes 196616 | tf_op jit(solution)/shard_map/ppermute | solution.py:220
  12.4 5.4 %collective-permute-start.4 = (bf16[64,512]{1,0:T(8,128)(2,1)S(1)}, bf16[64,512]{1,0:T(8,128)(2,1)S(1)}, u32[]{:S(2)}, u32[]{:S(2)}) collective-permute-start(bf16[64,512]{1,0:T(8,128)(2,1)S(1)} %get-tuple-element.40), channel_id=1, source_target_pairs={{0,4},{1,7},{2,6},{3,5},{4,0},{5,3},{6,2},{7,1},{8,12},{9,15},{10,... | collective-permute-start | bytes 196616 | tf_op jit(solution)/shard_map/ppermute | solution.py:220
  12.4 6.7 %collective-permute-start.5 = (bf16[64,512]{1,0:T(8,128)(2,1)S(1)}, bf16[64,512]{1,0:T(8,128)(2,1)S(1)}, u32[]{:S(2)}, u32[]{:S(2)}) collective-permute-start(bf16[64,512]{1,0:T(8,128)(2,1)S(1)} %get-tuple-element.41), channel_id=1, source_target_pairs={{0,8},{1,11},{2,10},{3,9},{4,12},{5,15},{6,14},{7,13},{8,0},{9,3},... | collective-permute-start | bytes 196616 | tf_op jit(solution)/shard_map/ppermute | solution.py:220
  14.2 6.4 %collective-permute-start.10 = (bf16[32,512]{1,0:T(8,128)(2,1)S(1)}, bf16[32,512]{1,0:T(8,128)(2,1)S(1)}, u32[]{:S(2)}, u32[]{:S(2)}) collective-permute-start(bf16[32,512]{1,0:T(8,128)(2,1)S(1)} %slice.19), channel_id=1, source_target_pairs={{0,1},{1,0},{2,3},{3,2},{4,5},{5,4},{6,7},{7,6},{8,9},{9,8},{10,11... | collective-permute-start | bytes 98312 | tf_op jit(solution)/shard_map/ppermute | solution.py:211
  16.3 4.3 %collective-permute-start.7 = (bf16[32,512]{1,0:T(8,128)(2,1)S(1)}, bf16[32,512]{1,0:T(8,128)(2,1)S(1)}, u32[]{:S(2)}, u32[]{:S(2)}) collective-permute-start(bf16[32,512]{1,0:T(8,128)(2,1)S(1)} %slice.16), channel_id=1, source_target_pairs={{0,1},{1,0},{2,3},{3,2},{4,5},{5,4},{6,7},{7,6},{8,9},{9,8},{10,11... | collective-permute-start | bytes 98312 | tf_op jit(solution)/shard_map/ppermute | solution.py:211
  17.8 2.8 %collective-permute-start.8 = (bf16[32,512]{1,0:T(8,128)(2,1)S(1)}, bf16[32,512]{1,0:T(8,128)(2,1)S(1)}, u32[]{:S(2)}, u32[]{:S(2)}) collective-permute-start(bf16[32,512]{1,0:T(8,128)(2,1)S(1)} %slice.17), channel_id=1, source_target_pairs={{0,1},{1,0},{2,3},{3,2},{4,5},{5,4},{6,7},{7,6},{8,9},{9,8},{10,11... | collective-permute-start | bytes 98312 | tf_op jit(solution)/shard_map/ppermute | solution.py:211
  19.1 2.2 %collective-permute-start.9 = (bf16[32,512]{1,0:T(8,128)(2,1)S(1)}, bf16[32,512]{1,0:T(8,128)(2,1)S(1)}, u32[]{:S(2)}, u32[]{:S(2)}) collective-permute-start(bf16[32,512]{1,0:T(8,128)(2,1)S(1)} %slice.18), channel_id=1, source_target_pairs={{0,1},{1,0},{2,3},{3,2},{4,5},{5,4},{6,7},{7,6},{8,9},{9,8},{10,11... | collective-permute-start | bytes 98312 | tf_op jit(solution)/shard_map/ppermute | solution.py:211
  20.5 8.3 %collective-permute-start.2 = (bf16[2,128,512]{2,1,0:T(8,128)(2,1)S(1)}, bf16[2,128,512]{2,1,0:T(8,128)(2,1)S(1)}, u32[]{:S(2)}, u32[]{:S(2)}) collective-permute-start(bf16[2,128,512]{2,1,0:T(8,128)(2,1)S(1)} %get-tuple-element.34.terms_ref), channel_id=1, source_target_pairs={{0,1},{1,0},{2,3},{3,2},{4,5},{5,4},{6,7},{7,6},{8,9},{9,8},{10,11... | collective-permute-start | bytes 786440 | tf_op jit(solution)/shard_map/ppermute | solution.py:211
  21.4 18.5 %copy-start = (bf16[512,1024]{1,0:T(8,128)(2,1)S(1)}, bf16[512,1024]{1,0:T(8,128)(2,1)}, u32[]{:S(2)}) copy-start(bf16[512,1024]{1,0:T(8,128)(2,1)} %w_own_ref.1) | copy-start | bytes 3145732
  24.6 1.4 %collective-permute-start.11 = (bf16[128,512]{1,0:T(8,128)(2,1)S(1)}, bf16[128,512]{1,0:T(8,128)(2,1)S(1)}, u32[]{:S(2)}, u32[]{:S(2)}) collective-permute-start(bf16[128,512]{1,0:T(8,128)(2,1)S(1)} %get-tuple-element.44), channel_id=1, source_target_pairs={{0,1},{1,0},{2,3},{3,2},{4,5},{5,4},{6,7},{7,6},{8,9},{9,8},{10,11... | collective-permute-start | bytes 393224 | tf_op jit(solution)/shard_map/ppermute | solution.py:211
  26.0 5.3 %collective-permute-start.12 = (bf16[64,512]{1,0:T(8,128)(2,1)S(1)}, bf16[64,512]{1,0:T(8,128)(2,1)S(1)}, u32[]{:S(2)}, u32[]{:S(2)}) collective-permute-start(bf16[64,512]{1,0:T(8,128)(2,1)S(1)} %get-tuple-element.45), channel_id=1, source_target_pairs={{0,0},{1,3},{2,2},{3,1},{4,4},{5,7},{6,6},{7,5},{8,8},{9,11},{10,1... | collective-permute-start | bytes 196616 | tf_op jit(solution)/shard_map/ppermute | solution.py:220
  26.7 4.6 %collective-permute-start.13 = (bf16[64,512]{1,0:T(8,128)(2,1)S(1)}, bf16[64,512]{1,0:T(8,128)(2,1)S(1)}, u32[]{:S(2)}, u32[]{:S(2)}) collective-permute-start(bf16[64,512]{1,0:T(8,128)(2,1)S(1)} %get-tuple-element.46), channel_id=1, source_target_pairs={{0,4},{1,7},{2,6},{3,5},{4,0},{5,3},{6,2},{7,1},{8,12},{9,15},{10,... | collective-permute-start | bytes 196616 | tf_op jit(solution)/shard_map/ppermute | solution.py:220
  28.8 7.1 %collective-permute-start.14 = (bf16[64,512]{1,0:T(8,128)(2,1)S(1)}, bf16[64,512]{1,0:T(8,128)(2,1)S(1)}, u32[]{:S(2)}, u32[]{:S(2)}) collective-permute-start(bf16[64,512]{1,0:T(8,128)(2,1)S(1)} %get-tuple-element.47), channel_id=1, source_target_pairs={{0,8},{1,11},{2,10},{3,9},{4,12},{5,15},{6,14},{7,13},{8,0},{9,3},... | collective-permute-start | bytes 196616 | tf_op jit(solution)/shard_map/ppermute | solution.py:220
  28.8 7.1 %collective-permute-start.15 = (bf16[64,512]{1,0:T(8,128)(2,1)S(1)}, bf16[64,512]{1,0:T(8,128)(2,1)S(1)}, u32[]{:S(2)}, u32[]{:S(2)}) collective-permute-start(bf16[64,512]{1,0:T(8,128)(2,1)S(1)} %get-tuple-element.48), channel_id=1, source_target_pairs={{0,12},{1,15},{2,14},{3,13},{4,8},{5,11},{6,10},{7,9},{8,4},{9,7},... | collective-permute-start | bytes 196616 | tf_op jit(solution)/shard_map/ppermute | solution.py:220
  36.8 3.0 %collective-permute-start.16 = (bf16[64,1024]{1,0:T(8,128)(2,1)S(1)}, bf16[64,1024]{1,0:T(8,128)(2,1)S(1)}, u32[]{:S(2)}, u32[]{:S(2)}) collective-permute-start(bf16[64,1024]{1,0:T(8,128)(2,1)S(1)} %get-tuple-element.50), channel_id=1, source_target_pairs={{0,1},{1,0},{2,3},{3,2},{4,5},{5,4},{6,7},{7,6},{8,9},{9,8},{10,11... | collective-permute-start | bytes 393224 | tf_op jit(solution)/shard_map/ppermute | solution.py:211

commit v7 on v6

--- a/solution.py
+++ b/solution.py
@@ -135,7 +135,10 @@
 
 
 def history_kernel(owners, hide_rows_ref, hide_cols_ref, keys_ref, values_ref, *refs):
-    slot_refs, (keep_ref, give_ref) = refs[:owners], refs[owners:]
+    keep_ref, give_ref = refs[owners:]
+    slot_refs = [None] * owners
+    for at, order in enumerate(far_first(owners // 2)):
+        slot_refs[order], slot_refs[owners // 2 + order] = refs[2 * at : 2 * at + 2]
     rows, width = keep_ref.shape
     per_owner = rows // (owners // 2)
     hist_rows = keys_ref.shape[0]
@@ -170,12 +173,17 @@
     width = model_width // 2
     half_cands = rows // req_count
     slots = messages * CAP
-    for at, back_ref in enumerate(back_refs):
+    for at, back_ref in zip(far_first(messages), back_refs):
         half = back_ref.shape[0] // 2
         for side in range(2):
             part = back_ref[side * half : (side + 1) * half, :].reshape((CAP,) + table_ref.shape[1:])
             table_ref[side * slots + at * CAP : side * slots + (at + 1) * CAP] = part
-    picks = [distance // 2 * CAP + place for distance, place in own_slots(sess_ref, req_count)]
+    serve = lax.axis_index("serve")
+    own = own_slots(sess_ref, req_count)
+    picks = [distance // 2 * CAP + place for distance, place in own]
+    live = jnp.concatenate(
+        [jnp.full((half_cands, HD), distance % 2 == serve, jnp.int32) for distance, _ in own], axis=0
+    ) == 1
     for side, source_ref in enumerate((terms_ref, their_terms_ref)):
         picked = [table_ref[side * slots + pick].astype(jnp.float32) for pick in picks]
         for part in range(2):
@@ -188,23 +196,28 @@
                 head = attended[:, low : low + HD]
                 level = lax.rsqrt(jnp.mean(head * head, axis=-1, keepdims=True) + EPS)
                 mixed = head * level * gates[:, low : low + HD]
-                out_ref[:, offset + low : offset + low + HD] = mixed.astype(jnp.bfloat16)
-
-
-def output_kernel(sess_ref, own_ref, keep_ref, got_ref, w_own_ref, w_other_ref, out_ref):
-    req_count, half_cands, model_width = own_ref.shape
-    width = model_width // 2
-    serve = lax.axis_index("serve")
-    keep, got = keep_ref[...].astype(jnp.float32), got_ref[...].astype(jnp.float32)
-    picked = []
-    for request, (distance, _) in enumerate(own_slots(sess_ref, req_count)):
-        low = request * half_cands
-        picked.append(jnp.where(distance % 2 == serve, keep[low : low + half_cands], got[low : low + half_cands]))
-    mixed = jnp.concatenate(picked, axis=0).astype(jnp.bfloat16)
-    total = own_ref[...].astype(jnp.float32).reshape(req_count * half_cands, model_width)
-    total = total + jnp.dot(mixed[:, :width], w_own_ref[...], preferred_element_type=jnp.float32)
-    total = total + jnp.dot(mixed[:, width:], w_other_ref[...], preferred_element_type=jnp.float32)
-    out_ref[...] = total.reshape(req_count, half_cands, model_width).astype(jnp.bfloat16)
+                out_ref[:, offset + low : offset + low + HD] = jnp.where(live, mixed, 0.0).astype(jnp.bfloat16)
+
+
+def project(mixed_ref, w_own_ref, w_other_ref):
+    width = w_own_ref.shape[0]
+    return jnp.dot(mixed_ref[:, :width], w_own_ref[...], preferred_element_type=jnp.float32) + jnp.dot(
+        mixed_ref[:, width:], w_other_ref[...], preferred_element_type=jnp.float32
+    )
+
+
+def kept_kernel(own_ref, keep_ref, w_own_ref, w_other_ref, out_ref):
+    own = own_ref[...].astype(jnp.float32).reshape(out_ref.shape)
+    out_ref[...] = own + project(keep_ref, w_own_ref, w_other_ref)
+
+
+def output_kernel(kept_ref, got_ref, w_own_ref, w_other_ref, out_ref):
+    total = kept_ref[...] + project(got_ref, w_own_ref, w_other_ref)
+    out_ref[...] = total.reshape(out_ref.shape).astype(jnp.bfloat16)
+
+
+def far_first(count):
+    return list(reversed(range(count)))
 
 
 def swap(rows):
@@ -212,13 +225,13 @@
 
 
 def cross(owners, messages):
-    came = {}
-    for at in reversed(range(len(messages))):
+    came = []
+    for at in far_first(len(messages)):
         pairs = [
             (place * 2 + core, (place ^ (2 * at + core)) * 2 + core) for place in range(owners) for core in range(2)
         ]
-        came[at] = lax.ppermute(messages[at], ("cache", "serve"), pairs)
-    return [came[at] for at in range(len(messages))]
+        came.append(lax.ppermute(messages[at], ("cache", "serve"), pairs))
+    return came
 
 
 def body(candidates, input_gain, w_in, w_out, hist_keys, hist_values, request_session, hist_len, block_mask):
@@ -259,7 +272,8 @@
     )(request_session.reshape(1, -1), hist_len, block_mask.T, normed, queries, weights)
     got, (terms, hide_rows, hide_cols) = lax.optimization_barrier((got, own))
     came = cross(owners, pack(keep, got))
-    slots = came + [swap(rows_of[piece:]) for rows_of in came]
+    swapped = [swap(rows_of[piece:]) for rows_of in came]
+    slots = [rows_of for both in zip(came, swapped) for rows_of in both]
     their_terms = swap(terms)
     w_other = swap(w_out)
     keep, give = kernel_call(
@@ -276,13 +290,21 @@
         [smem] + [vmem] * (2 + messages),
         [table],
     )(sessions, terms, their_terms, *backs)
+    got = swap(give)
+    kept = kernel_call(
+        kept_kernel,
+        jax.ShapeDtypeStruct((rows, model_width), jnp.float32),
+        [vmem] * 4,
+        flops=8 * rows * model_width * width,
+        moved=4 * model_width * width,
+    )(candidates, keep, w_out, w_other)
     return kernel_call(
         output_kernel,
         bf16((req_count, half_cands, model_width)),
-        [smem] + [vmem] * 5,
+        [vmem] * 4,
         flops=8 * rows * model_width * width,
         moved=4 * model_width * width,
-    )(sessions, candidates, keep, swap(give), w_out, w_other)
+    )(kept, got, w_out, w_other)
 
 
 def solution(mesh):

time: 41.7 us -> 39.7 us (0.952)
  waiting for transfers between devices: 8.63 us -> 6.8 us
    ppermute x8, waiting for transfers between devices: 5.84 us -> 4.42 us  [cross(): came.append(lax.ppermute(messages[at], ('cache', 'serve'), pairs))]
    pallas_call x1 -> x2, Pallas kernels: 1.69 us -> 1.63 us  [the longest x1 1.15 us: body(): kernel_call(output_kernel, bf16((req_count, half_cands, model_width)), [v...]
  transfers between devices with their start and end apart: 18 -> 18, of which waited for: 5 -> 6; matrix products, arithmetic and copies ran while one was open for 7% -> 8% of each run, Pallas kernels for 16% -> 18%
where the time goes in v7:
time: 39.7 us; the launch traced here: 39.6 us
  starting transfers between devices  21.2 us (53%)
  Pallas kernels  8.37 us (21%)
  waiting for transfers between devices  6.8 us (17%)
  local copies, waits for them, and re-layouts  3.08 us (8%)
    ppermute x8, starting transfers between devices, cross(): came.append(lax.ppermute(messages[at], ('cache', 'serve'), pairs))  11.2 us
    ppermute x10, starting transfers between devices, swap(): return lax.ppermute(rows, 'serve', [(0, 1), (1, 0)])  10 us
    ppermute x8, waiting for transfers between devices, cross(): came.append(lax.ppermute(messages[at], ('cache', 'serve'), pairs))  4.42 us
    pallas_call x1, Pallas kernels, body(): kernel_call(functools.partial(history_kernel, owners), [half_table] * 2,...  3.18 us
    unnamed x17, local copies, waits for them, and re-layouts  3.06 us
    ppermute x10, waiting for transfers between devices, swap(): return lax.ppermute(rows, 'serve', [(0, 1), (1, 0)])  2.38 us
    pallas_call x1, Pallas kernels, body(): kernel_call(self_kernel, [bf16((2, 2 * rows, width)), bf16((owners * piec...  1.69 us
    pallas_call x1, Pallas kernels, body(): kernel_call(output_kernel, bf16((req_count, half_cands, model_width)), [v...  1.15 us
  transfers between devices with their start and end apart: 18, of which 6 were waited for; matrix products, arithmetic and copies ran while one was open for 8% of the time, Pallas kernels for 18%

profile of v7, /device:TPU:0, one launch (start us, length us, event | category | flops | bytes accessed | tf_op | source)
XLA Modules:
  0.0 39.6 jit_solution(5539954177641427393)
XLA Ops:
  0.0 0.0 copy-start.1
  0.0 0.0 copy-start.7
  0.0 0.0 copy-start.3
  0.0 0.5 %collective-permute-start.16 = (bf16[512,1024]{1,0:T(8,128)(2,1)}, bf16[512,1024]{1,0:T(8,128)(2,1)S(1)}, u32[]{:S(2)}, u32[]{:S(2)}) collective-permute-start(bf16[512,1024]{1,0:T(8,128)(2,1)} %w_own_ref.3), channel_id=1, source_target_pairs={{0,1},{1,0},{2,3},{3,2},{4,5},{5,4},{6,7},{7,6},{8,9},{9,8},{10,11... | collective-permute-start | bytes 3145736 | tf_op jit(solution)/shard_map/ppermute | solution.py:224
  0.5 0.1 collective-permute-start
  0.6 3.0 %copy.12 = bf16[1024,4,512]{2,0,1:T(8,128)(2,1)S(1)} copy(bf16[1024,4,512]{2,1,0:T(4,128)(2,1)} %param.11) | data formatting | bytes 8388608 | tf_op args[2]
  3.6 0.0 copy-done.7
  3.6 0.0 copy-start.2
  3.7 0.0 copy-start.4
  3.7 0.0 collective-permute-done.other_ref
  3.7 0.0 copy-done.1
  3.7 0.0 copy-done.3
  3.7 0.0 copy-start.5
  3.7 0.0 copy-start.6
  3.7 1.0 %shard_map.91 = (bf16[128,512]{1,0:T(8,128)(2,1)S(1)}, bf16[128,512]{1,0:T(8,128)(2,1)S(1)}, bf16[128,512]{1,0:T(8,128)(2,1)S(1)}, bf16[128,1024]{1,0:T(8,128)(2,1)S(1)}) custom-call(s32[64]{0:T(128)S(1)} %bitcast.11, bf16[8,8,1024]{2,1,0:T(8,128)(2,1)S(1)} %copy-done.1, bf16[8,8,1024]{2,1,0:T(8,128)(2,1)S(1)} %collective-permute-done.other_ref, ...), custom_call_target="tpu_custom_call" | custom-call | flops 134217728 | bytes 1048576 | tf_op jit(solution)/shard_map/pallas_call | solution.py:256
  4.7 0.5 %collective-permute-start.1 = (bf16[128,512]{1,0:T(8,128)(2,1)S(1)}, bf16[128,512]{1,0:T(8,128)(2,1)S(1)}, u32[]{:S(2)}, u32[]{:S(2)}) collective-permute-start(bf16[128,512]{1,0:T(8,128)(2,1)S(1)} %get-tuple-element.28), channel_id=1, source_target_pairs={{0,1},{1,0},{2,3},{3,2},{4,5},{5,4},{6,7},{7,6},{8,9},{9,8},{10,11... | collective-permute-start | bytes 393224 | tf_op jit(solution)/shard_map/ppermute | solution.py:224
  5.2 0.0 copy-done.2
  5.2 0.0 copy-done.4
  5.2 1.7 %shard_map.92 = (bf16[2,128,512]{2,1,0:T(8,128)(2,1)S(1)}, bf16[256,128]{1,0:T(8,128)(2,1)S(1)}, bf16[2048,128]{1,0:T(8,128)(2,1)S(1)}) custom-call(s32[1,64]{1,0:T(1,128)S(1)} %bitcast.12, s32[8]{0:T(128)S(1)} %copy-done.4, s32[32,64]{1,0:T(8,128)S(1)} %bitcast.10, bf16[128,1024]{1,0:T(8,128)(2,1)S(1)} %get-tuple-element.29.normed_ref, ...), custom_call_target="tpu_custom_call" | custom-call | flops 402653184 | bytes 3145728 | tf_op jit(solution)/shard_map/pallas_call | solution.py:265
  6.9 0.0 collective-permute-done.1.got_ref
  7.0 0.7 %collective-permute-start.9 = (bf16[64,512]{1,0:T(8,128)(2,1)S(1)}, bf16[64,512]{1,0:T(8,128)(2,1)S(1)}, u32[]{:S(2)}, u32[]{:S(2)}) collective-permute-start(bf16[64,512]{1,0:T(8,128)(2,1)S(1)} %get-tuple-element.42), channel_id=1, source_target_pairs={{0,0},{1,3},{2,2},{3,1},{4,4},{5,7},{6,6},{7,5},{8,8},{9,11},{10,1... | collective-permute-start | bytes 196616 | tf_op jit(solution)/shard_map/ppermute | solution.py:233
  7.6 4.7 %collective-permute-start.3 = (bf16[64,512]{1,0:T(8,128)(2,1)S(1)}, bf16[64,512]{1,0:T(8,128)(2,1)S(1)}, u32[]{:S(2)}, u32[]{:S(2)}) collective-permute-start(bf16[64,512]{1,0:T(8,128)(2,1)S(1)} %get-tuple-element.39), channel_id=1, source_target_pairs={{0,12},{1,15},{2,14},{3,13},{4,8},{5,11},{6,10},{7,9},{8,4},{9,7},... | collective-permute-start | bytes 196616 | tf_op jit(solution)/shard_map/ppermute | solution.py:233
  12.4 0.0 collective-permute-start.5
  12.4 0.6 %collective-permute-start.7 = (bf16[64,512]{1,0:T(8,128)(2,1)S(1)}, bf16[64,512]{1,0:T(8,128)(2,1)S(1)}, u32[]{:S(2)}, u32[]{:S(2)}) collective-permute-start(bf16[64,512]{1,0:T(8,128)(2,1)S(1)} %get-tuple-element.41), channel_id=1, source_target_pairs={{0,4},{1,7},{2,6},{3,5},{4,0},{5,3},{6,2},{7,1},{8,12},{9,15},{10,... | collective-permute-start | bytes 196616 | tf_op jit(solution)/shard_map/ppermute | solution.py:233
  13.0 0.0 collective-permute-done.9.refs_6_
  13.0 3.2 %collective-permute-start.10 = (bf16[32,512]{1,0:T(8,128)(2,1)S(1)}, bf16[32,512]{1,0:T(8,128)(2,1)S(1)}, u32[]{:S(2)}, u32[]{:S(2)}) collective-permute-start(bf16[32,512]{1,0:T(8,128)(2,1)S(1)} %slice.19), channel_id=1, source_target_pairs={{0,1},{1,0},{2,3},{3,2},{4,5},{5,4},{6,7},{7,6},{8,9},{9,8},{10,11... | collective-permute-start | bytes 98312 | tf_op jit(solution)/shard_map/ppermute | solution.py:224
  16.3 0.0 collective-permute-done.3.refs_0_
  16.3 1.8 %collective-permute-start.4 = (bf16[32,512]{1,0:T(8,128)(2,1)S(1)}, bf16[32,512]{1,0:T(8,128)(2,1)S(1)}, u32[]{:S(2)}, u32[]{:S(2)}) collective-permute-start(bf16[32,512]{1,0:T(8,128)(2,1)S(1)} %slice.16), channel_id=1, source_target_pairs={{0,1},{1,0},{2,3},{3,2},{4,5},{5,4},{6,7},{7,6},{8,9},{9,8},{10,11... | collective-permute-start | bytes 98312 | tf_op jit(solution)/shard_map/ppermute | solution.py:224
  18.1 0.0 collective-permute-done.5.refs_2_
  18.1 2.2 %collective-permute-start.6 = (bf16[32,512]{1,0:T(8,128)(2,1)S(1)}, bf16[32,512]{1,0:T(8,128)(2,1)S(1)}, u32[]{:S(2)}, u32[]{:S(2)}) collective-permute-start(bf16[32,512]{1,0:T(8,128)(2,1)S(1)} %slice.17), channel_id=1, source_target_pairs={{0,1},{1,0},{2,3},{3,2},{4,5},{5,4},{6,7},{7,6},{8,9},{9,8},{10,11... | collective-permute-start | bytes 98312 | tf_op jit(solution)/shard_map/ppermute | solution.py:224
  20.3 0.0 collective-permute-done.7.refs_4_
  20.3 0.1 collective-permute-start.8
  20.4 0.0 collective-permute-done.10.refs_7_
  20.5 0.4 collective-permute-start.2
  20.8 0.0 collective-permute-done.4.refs_1_
  20.8 0.3 collective-permute-done.6.refs_3_
  21.2 0.4 collective-permute-done.8.refs_5_
  21.5 0.0 copy-done.5
  21.5 0.0 copy-done.6
  21.5 0.0 copy-start
  21.5 3.2 %shard_map.94 = (bf16[128,512]{1,0:T(8,128)(2,1)S(1)}, bf16[128,512]{1,0:T(8,128)(2,1)S(1)}) custom-call(bf16[256,128]{1,0:T(8,128)(2,1)S(1)} %get-tuple-element.35.hide_rows_ref, bf16[2048,128]{1,0:T(8,128)(2,1)S(1)} %get-tuple-element.36.hide_cols_ref, bf16[2048,512]{1,0:T(8,128)(2,1)S(1)} %bitcast.14, bf16[2048,512]{1,0:T(8,128)(2,1)S(1)} %bitcast.15, ...), custom_call_target="tpu_custom_call" | custom-call | flops 2147483648 | bytes 4194304 | tf_op jit(solution)/shard_map/pallas_call | solution.py:279
  24.7 0.2 collective-permute-start.11
  25.0 1.2 %collective-permute-done.11.got_ref = bf16[128,512]{1,0:T(8,128)(2,1)S(1)} collective-permute-done((bf16[128,512]{1,0:T(8,128)(2,1)S(1)}, bf16[128,512]{1,0:T(8,128)(2,1)S(1)}, u32[]{:S(2)}, u32[]{:S(2)}) %collective-permute-start.11) | collective-permute-done | bytes 131104 | tf_op jit(solution)/shard_map/ppermute | solution.py:224
  26.2 2.5 %collective-permute-start.12 = (bf16[64,512]{1,0:T(8,128)(2,1)S(1)}, bf16[64,512]{1,0:T(8,128)(2,1)S(1)}, u32[]{:S(2)}, u32[]{:S(2)}) collective-permute-start(bf16[64,512]{1,0:T(8,128)(2,1)S(1)} %get-tuple-element.45), channel_id=1, source_target_pairs={{0,12},{1,15},{2,14},{3,13},{4,8},{5,11},{6,10},{7,9},{8,4},{9,7},... | collective-permute-start | bytes 196616 | tf_op jit(solution)/shard_map/ppermute | solution.py:233
  28.7 0.0 collective-permute-start.13
  28.7 2.0 %collective-permute-start.14 = (bf16[64,512]{1,0:T(8,128)(2,1)S(1)}, bf16[64,512]{1,0:T(8,128)(2,1)S(1)}, u32[]{:S(2)}, u32[]{:S(2)}) collective-permute-start(bf16[64,512]{1,0:T(8,128)(2,1)S(1)} %get-tuple-element.47), channel_id=1, source_target_pairs={{0,4},{1,7},{2,6},{3,5},{4,0},{5,3},{6,2},{7,1},{8,12},{9,15},{10,... | collective-permute-start | bytes 196616 | tf_op jit(solution)/shard_map/ppermute | solution.py:233
  30.6 0.0 collective-permute-done.2.their_terms_ref
  30.6 0.7 %collective-permute-start.15 = (bf16[64,512]{1,0:T(8,128)(2,1)S(1)}, bf16[64,512]{1,0:T(8,128)(2,1)S(1)}, u32[]{:S(2)}, u32[]{:S(2)}) collective-permute-start(bf16[64,512]{1,0:T(8,128)(2,1)S(1)} %get-tuple-element.48), channel_id=1, source_target_pairs={{0,0},{1,3},{2,2},{3,1},{4,4},{5,7},{6,6},{7,5},{8,8},{9,11},{10,1... | collective-permute-start | bytes 196616 | tf_op jit(solution)/shard_map/ppermute | solution.py:233
  31.3 1.7 %collective-permute-done.12.refs_0_ = bf16[64,512]{1,0:T(8,128)(2,1)S(1)} collective-permute-done((bf16[64,512]{1,0:T(8,128)(2,1)S(1)}, bf16[64,512]{1,0:T(8,128)(2,1)S(1)}, u32[]{:S(2)}, u32[]{:S(2)}) %collective-permute-start.12) | collective-permute-done | bytes 65568 | tf_op jit(solution)/shard_map/ppermute | solution.py:233
  33.0 2.7 %collective-permute-done.13.refs_1_ = bf16[64,512]{1,0:T(8,128)(2,1)S(1)} collective-permute-done((bf16[64,512]{1,0:T(8,128)(2,1)S(1)}, bf16[64,512]{1,0:T(8,128)(2,1)S(1)}, u32[]{:S(2)}, u32[]{:S(2)}) %collective-permute-start.13) | collective-permute-done | bytes 65568 | tf_op jit(solution)/shard_map/ppermute | solution.py:233
  35.7 0.0 collective-permute-done.14.refs_2_
  35.7 0.0 collective-permute-done.15.refs_3_
  35.7 0.9 %shard_map.96 = (bf16[64,1024]{1,0:T(8,128)(2,1)S(1)}, bf16[64,1024]{1,0:T(8,128)(2,1)S(1)}) custom-call(s32[64]{0:T(128)S(1)} %bitcast.13, bf16[2,128,512]{2,1,0:T(8,128)(2,1)S(1)} %get-tuple-element.34.terms_ref, bf16[2,128,512]{2,1,0:T(8,128)(2,1)S(1)} %collective-permute-done.2.their_terms_ref, bf16[64,512]{1,0:T(8,128)(2,1)S(1)} %collective-permute-done.12.refs_0_, ...), custom_call_target="tpu_custom_call" | custom-call | tf_op jit(solution)/shard_map/pallas_call | solution.py:287
  36.6 0.9 %collective-permute-start.17 = (bf16[64,1024]{1,0:T(8,128)(2,1)S(1)}, bf16[64,1024]{1,0:T(8,128)(2,1)S(1)}, u32[]{:S(2)}, u32[]{:S(2)}) collective-permute-start(bf16[64,1024]{1,0:T(8,128)(2,1)S(1)} %get-tuple-element.50), channel_id=1, source_target_pairs={{0,1},{1,0},{2,3},{3,2},{4,5},{5,4},{6,7},{7,6},{8,9},{9,8},{10,11... | collective-permute-start | bytes 393224 | tf_op jit(solution)/shard_map/ppermute | solution.py:224
  37.5 0.0 collective-permute-done.16.w_other_ref
  37.5 0.0 copy-done
  37.5 0.5 %shard_map.97.kept_ref = f32[64,1024]{1,0:T(8,128)S(1)} custom-call(bf16[8,8,1024]{2,1,0:T(8,128)(2,1)S(1)} %copy-done.1, bf16[64,1024]{1,0:T(8,128)(2,1)S(1)} %get-tuple-element.49.keep_ref, bf16[512,1024]{1,0:T(8,128)(2,1)S(1)} %copy-done, bf16[512,1024]{1,0:T(8,128)(2,1)S(1)} %collective-permute-done.16.w_other_ref), custom_call_target="tpu_custom_call" | custom-call | flops 268435456 | bytes 2097152 | tf_op jit(solution)/shard_map/pallas_call | solution.py:294
  38.0 0.5 %collective-permute-done.17.got_ref = bf16[64,1024]{1,0:T(8,128)(2,1)S(1)} collective-permute-done((bf16[64,1024]{1,0:T(8,128)(2,1)S(1)}, bf16[64,1024]{1,0:T(8,128)(2,1)S(1)}, u32[]{:S(2)}, u32[]{:S(2)}) %collective-permute-start.17) | collective-permute-done | bytes 131104 | tf_op jit(solution)/shard_map/ppermute | solution.py:224
  38.4 1.1 %shard_map.98 = bf16[8,8,1024]{2,1,0:T(8,128)(2,1)} custom-call(f32[64,1024]{1,0:T(8,128)S(1)} %shard_map.97.kept_ref, bf16[64,1024]{1,0:T(8,128)(2,1)S(1)} %collective-permute-done.17.got_ref, bf16[512,1024]{1,0:T(8,128)(2,1)S(1)} %copy-done, bf16[512,1024]{1,0:T(8,128)(2,1)S(1)} %collective-permute-done.16.w_other_ref), custom_call_target="tpu_custom_call" | custom-call | flops 268435456 | bytes 2097152 | tf_op jit(solution)/shard_map/pallas_call | solution.py:301
  (7 shorter events, 0.1 us)
Async XLA Ops:
  0.0 3.7 %copy-start.1 = (bf16[8,8,1024]{2,1,0:T(8,128)(2,1)S(1)}, bf16[8,8,1024]{2,1,0:T(8,128)(2,1)}, u32[]{:S(2)}) copy-start(bf16[8,8,1024]{2,1,0:T(8,128)(2,1)} %own_ref.3) | copy-start | bytes 393220
  0.0 3.6 %copy-start.7 = (bf16[1024]{0:T(1024)(128)(2,1)S(1)}, bf16[1024]{0:T(1024)(128)(2,1)}, u32[]{:S(2)}) copy-start(bf16[1024]{0:T(1024)(128)(2,1)} %param.10) | copy-start | bytes 6148
  0.0 3.7 %copy-start.3 = (s32[64,1]{0,1:T(1,128)S(1)}, s32[64,1]{0,1:T(1,128)}, u32[]{:S(2)}) copy-start(s32[64,1]{0,1:T(1,128)} %param.15) | copy-start | bytes 772
  0.0 37.5 %collective-permute-start.16 = (bf16[512,1024]{1,0:T(8,128)(2,1)}, bf16[512,1024]{1,0:T(8,128)(2,1)S(1)}, u32[]{:S(2)}, u32[]{:S(2)}) collective-permute-start(bf16[512,1024]{1,0:T(8,128)(2,1)} %w_own_ref.3), channel_id=1, source_target_pairs={{0,1},{1,0},{2,3},{3,2},{4,5},{5,4},{6,7},{7,6},{8,9},{9,8},{10,11... | collective-permute-start | bytes 3145736 | tf_op jit(solution)/shard_map/ppermute | solution.py:224
  0.5 3.2 %collective-permute-start = (bf16[8,8,1024]{2,1,0:T(8,128)(2,1)}, bf16[8,8,1024]{2,1,0:T(8,128)(2,1)S(1)}, u32[]{:S(2)}, u32[]{:S(2)}) collective-permute-start(bf16[8,8,1024]{2,1,0:T(8,128)(2,1)} %own_ref.3), channel_id=1, source_target_pairs={{0,1},{1,0},{2,3},{3,2},{4,5},{5,4},{6,7},{7,6},{8,9},{9,8},{10,11... | collective-permute-start | bytes 393224 | tf_op jit(solution)/shard_map/ppermute | solution.py:224
  3.6 1.6 %copy-start.2 = (s32[64,32]{0,1:T(8,128)S(1)}, s32[64,32]{0,1:T(8,128)}, u32[]{:S(2)}) copy-start(s32[64,32]{0,1:T(8,128)} %param.17) | copy-start | bytes 24580
  3.7 1.6 %copy-start.4 = (s32[8]{0:T(128)S(1)}, s32[8]{0:T(128)}, u32[]{:S(2)}) copy-start(s32[8]{0:T(128)} %len_ref.1) | copy-start | bytes 100
  3.7 17.8 %copy-start.5 = (bf16[1,2048,512]{2,1,0:T(8,128)(2,1)S(1)}, bf16[1,2048,512]{2,1,0:T(8,128)(2,1)}, u32[]{:S(2)}) copy-start(bf16[1,2048,512]{2,1,0:T(8,128)(2,1)} %param.13) | copy-start | bytes 6291460
  3.7 17.8 %copy-start.6 = (bf16[1,2048,512]{2,1,0:T(8,128)(2,1)S(1)}, bf16[1,2048,512]{2,1,0:T(8,128)(2,1)}, u32[]{:S(2)}) copy-start(bf16[1,2048,512]{2,1,0:T(8,128)(2,1)} %param.14) | copy-start | bytes 6291460
  4.7 2.2 %collective-permute-start.1 = (bf16[128,512]{1,0:T(8,128)(2,1)S(1)}, bf16[128,512]{1,0:T(8,128)(2,1)S(1)}, u32[]{:S(2)}, u32[]{:S(2)}) collective-permute-start(bf16[128,512]{1,0:T(8,128)(2,1)S(1)} %get-tuple-element.28), channel_id=1, source_target_pairs={{0,1},{1,0},{2,3},{3,2},{4,5},{5,4},{6,7},{7,6},{8,9},{9,8},{10,11... | collective-permute-start | bytes 393224 | tf_op jit(solution)/shard_map/ppermute | solution.py:224
  7.0 6.1 %collective-permute-start.9 = (bf16[64,512]{1,0:T(8,128)(2,1)S(1)}, bf16[64,512]{1,0:T(8,128)(2,1)S(1)}, u32[]{:S(2)}, u32[]{:S(2)}) collective-permute-start(bf16[64,512]{1,0:T(8,128)(2,1)S(1)} %get-tuple-element.42), channel_id=1, source_target_pairs={{0,0},{1,3},{2,2},{3,1},{4,4},{5,7},{6,6},{7,5},{8,8},{9,11},{10,1... | collective-permute-start | bytes 196616 | tf_op jit(solution)/shard_map/ppermute | solution.py:233
  7.6 8.6 %collective-permute-start.3 = (bf16[64,512]{1,0:T(8,128)(2,1)S(1)}, bf16[64,512]{1,0:T(8,128)(2,1)S(1)}, u32[]{:S(2)}, u32[]{:S(2)}) collective-permute-start(bf16[64,512]{1,0:T(8,128)(2,1)S(1)} %get-tuple-element.39), channel_id=1, source_target_pairs={{0,12},{1,15},{2,14},{3,13},{4,8},{5,11},{6,10},{7,9},{8,4},{9,7},... | collective-permute-start | bytes 196616 | tf_op jit(solution)/shard_map/ppermute | solution.py:233
  12.4 5.7 %collective-permute-start.5 = (bf16[64,512]{1,0:T(8,128)(2,1)S(1)}, bf16[64,512]{1,0:T(8,128)(2,1)S(1)}, u32[]{:S(2)}, u32[]{:S(2)}) collective-permute-start(bf16[64,512]{1,0:T(8,128)(2,1)S(1)} %get-tuple-element.40), channel_id=1, source_target_pairs={{0,8},{1,11},{2,10},{3,9},{4,12},{5,15},{6,14},{7,13},{8,0},{9,3},... | collective-permute-start | bytes 196616 | tf_op jit(solution)/shard_map/ppermute | solution.py:233
  12.4 7.9 %collective-permute-start.7 = (bf16[64,512]{1,0:T(8,128)(2,1)S(1)}, bf16[64,512]{1,0:T(8,128)(2,1)S(1)}, u32[]{:S(2)}, u32[]{:S(2)}) collective-permute-start(bf16[64,512]{1,0:T(8,128)(2,1)S(1)} %get-tuple-element.41), channel_id=1, source_target_pairs={{0,4},{1,7},{2,6},{3,5},{4,0},{5,3},{6,2},{7,1},{8,12},{9,15},{10,... | collective-permute-start | bytes 196616 | tf_op jit(solution)/shard_map/ppermute | solution.py:233
  13.0 7.4 %collective-permute-start.10 = (bf16[32,512]{1,0:T(8,128)(2,1)S(1)}, bf16[32,512]{1,0:T(8,128)(2,1)S(1)}, u32[]{:S(2)}, u32[]{:S(2)}) collective-permute-start(bf16[32,512]{1,0:T(8,128)(2,1)S(1)} %slice.19), channel_id=1, source_target_pairs={{0,1},{1,0},{2,3},{3,2},{4,5},{5,4},{6,7},{7,6},{8,9},{9,8},{10,11... | collective-permute-start | bytes 98312 | tf_op jit(solution)/shard_map/ppermute | solution.py:224
  16.3 4.6 %collective-permute-start.4 = (bf16[32,512]{1,0:T(8,128)(2,1)S(1)}, bf16[32,512]{1,0:T(8,128)(2,1)S(1)}, u32[]{:S(2)}, u32[]{:S(2)}) collective-permute-start(bf16[32,512]{1,0:T(8,128)(2,1)S(1)} %slice.16), channel_id=1, source_target_pairs={{0,1},{1,0},{2,3},{3,2},{4,5},{5,4},{6,7},{7,6},{8,9},{9,8},{10,11... | collective-permute-start | bytes 98312 | tf_op jit(solution)/shard_map/ppermute | solution.py:224
  18.1 3.1 %collective-permute-start.6 = (bf16[32,512]{1,0:T(8,128)(2,1)S(1)}, bf16[32,512]{1,0:T(8,128)(2,1)S(1)}, u32[]{:S(2)}, u32[]{:S(2)}) collective-permute-start(bf16[32,512]{1,0:T(8,128)(2,1)S(1)} %slice.17), channel_id=1, source_target_pairs={{0,1},{1,0},{2,3},{3,2},{4,5},{5,4},{6,7},{7,6},{8,9},{9,8},{10,11... | collective-permute-start | bytes 98312 | tf_op jit(solution)/shard_map/ppermute | solution.py:224
  20.3 1.2 %collective-permute-start.8 = (bf16[32,512]{1,0:T(8,128)(2,1)S(1)}, bf16[32,512]{1,0:T(8,128)(2,1)S(1)}, u32[]{:S(2)}, u32[]{:S(2)}) collective-permute-start(bf16[32,512]{1,0:T(8,128)(2,1)S(1)} %slice.18), channel_id=1, source_target_pairs={{0,1},{1,0},{2,3},{3,2},{4,5},{5,4},{6,7},{7,6},{8,9},{9,8},{10,11... | collective-permute-start | bytes 98312 | tf_op jit(solution)/shard_map/ppermute | solution.py:224
  20.5 10.2 %collective-permute-start.2 = (bf16[2,128,512]{2,1,0:T(8,128)(2,1)S(1)}, bf16[2,128,512]{2,1,0:T(8,128)(2,1)S(1)}, u32[]{:S(2)}, u32[]{:S(2)}) collective-permute-start(bf16[2,128,512]{2,1,0:T(8,128)(2,1)S(1)} %get-tuple-element.34.terms_ref), channel_id=1, source_target_pairs={{0,1},{1,0},{2,3},{3,2},{4,5},{5,4},{6,7},{7,6},{8,9},{9,8},{10,11... | collective-permute-start | bytes 786440 | tf_op jit(solution)/shard_map/ppermute | solution.py:224
  21.5 15.9 %copy-start = (bf16[512,1024]{1,0:T(8,128)(2,1)S(1)}, bf16[512,1024]{1,0:T(8,128)(2,1)}, u32[]{:S(2)}) copy-start(bf16[512,1024]{1,0:T(8,128)(2,1)} %w_own_ref.3) | copy-start | bytes 3145732
  24.7 1.4 %collective-permute-start.11 = (bf16[128,512]{1,0:T(8,128)(2,1)S(1)}, bf16[128,512]{1,0:T(8,128)(2,1)S(1)}, u32[]{:S(2)}, u32[]{:S(2)}) collective-permute-start(bf16[128,512]{1,0:T(8,128)(2,1)S(1)} %get-tuple-element.44), channel_id=1, source_target_pairs={{0,1},{1,0},{2,3},{3,2},{4,5},{5,4},{6,7},{7,6},{8,9},{9,8},{10,11... | collective-permute-start | bytes 393224 | tf_op jit(solution)/shard_map/ppermute | solution.py:224
  26.2 6.8 %collective-permute-start.12 = (bf16[64,512]{1,0:T(8,128)(2,1)S(1)}, bf16[64,512]{1,0:T(8,128)(2,1)S(1)}, u32[]{:S(2)}, u32[]{:S(2)}) collective-permute-start(bf16[64,512]{1,0:T(8,128)(2,1)S(1)} %get-tuple-element.45), channel_id=1, source_target_pairs={{0,12},{1,15},{2,14},{3,13},{4,8},{5,11},{6,10},{7,9},{8,4},{9,7},... | collective-permute-start | bytes 196616 | tf_op jit(solution)/shard_map/ppermute | solution.py:233
  28.7 7.0 %collective-permute-start.13 = (bf16[64,512]{1,0:T(8,128)(2,1)S(1)}, bf16[64,512]{1,0:T(8,128)(2,1)S(1)}, u32[]{:S(2)}, u32[]{:S(2)}) collective-permute-start(bf16[64,512]{1,0:T(8,128)(2,1)S(1)} %get-tuple-element.46), channel_id=1, source_target_pairs={{0,8},{1,11},{2,10},{3,9},{4,12},{5,15},{6,14},{7,13},{8,0},{9,3},... | collective-permute-start | bytes 196616 | tf_op jit(solution)/shard_map/ppermute | solution.py:233
  28.7 7.0 %collective-permute-start.14 = (bf16[64,512]{1,0:T(8,128)(2,1)S(1)}, bf16[64,512]{1,0:T(8,128)(2,1)S(1)}, u32[]{:S(2)}, u32[]{:S(2)}) collective-permute-start(bf16[64,512]{1,0:T(8,128)(2,1)S(1)} %get-tuple-element.47), channel_id=1, source_target_pairs={{0,4},{1,7},{2,6},{3,5},{4,0},{5,3},{6,2},{7,1},{8,12},{9,15},{10,... | collective-permute-start | bytes 196616 | tf_op jit(solution)/shard_map/ppermute | solution.py:233
  30.6 5.1 %collective-permute-start.15 = (bf16[64,512]{1,0:T(8,128)(2,1)S(1)}, bf16[64,512]{1,0:T(8,128)(2,1)S(1)}, u32[]{:S(2)}, u32[]{:S(2)}) collective-permute-start(bf16[64,512]{1,0:T(8,128)(2,1)S(1)} %get-tuple-element.48), channel_id=1, source_target_pairs={{0,0},{1,3},{2,2},{3,1},{4,4},{5,7},{6,6},{7,5},{8,8},{9,11},{10,1... | collective-permute-start | bytes 196616 | tf_op jit(solution)/shard_map/ppermute | solution.py:233
  36.6 1.9 %collective-permute-start.17 = (bf16[64,1024]{1,0:T(8,128)(2,1)S(1)}, bf16[64,1024]{1,0:T(8,128)(2,1)S(1)}, u32[]{:S(2)}, u32[]{:S(2)}) collective-permute-start(bf16[64,1024]{1,0:T(8,128)(2,1)S(1)} %get-tuple-element.50), channel_id=1, source_target_pairs={{0,1},{1,0},{2,3},{3,2},{4,5},{5,4},{6,7},{7,6},{8,9},{9,8},{10,11... | collective-permute-start | bytes 393224 | tf_op jit(solution)/shard_map/ppermute | solution.py:224

commit v8 on v7

v8 whole, which is shorter than its diff:
```python
import functools

import jax
import jax.numpy as jnp
from jax import lax
from jax.experimental import pallas as pl
from jax.experimental.pallas import tpu as pltpu
from jax.sharding import PartitionSpec as P

HD = 128
BLK = 64
CAP = 2
EPS = 1e-06
SCALE = HD ** (-0.5)
HIDE = -1e30
VMEM_LIMIT = 16 * 1024 * 1024

vmem = pl.BlockSpec(memory_space=pltpu.VMEM)
smem = pl.BlockSpec(memory_space=pltpu.SMEM)


def silu_of_half(half):
    return half + half * jnp.tanh(half)


def silu(x):
    return silu_of_half(x * 0.5)


def kernel_call(body, out_shape, in_specs, scratch_shapes=(), flops=0, moved=0):
    return pl.pallas_call(
        body,
        out_shape=out_shape,
        in_specs=in_specs,
        out_specs=jax.tree.map(lambda _: vmem, out_shape),
        scratch_shapes=scratch_shapes,
        cost_estimate=pl.CostEstimate(flops=flops, bytes_accessed=moved, transcendentals=0),
        compiler_params=pltpu.CompilerParams(vmem_limit_bytes=VMEM_LIMIT),
    )


def normed_rows(rows_ref, gain):
    rows = rows_ref[...].astype(jnp.float32)
    rows = rows.reshape(-1, rows.shape[-1])
    mean_square = jnp.mean(rows * rows, axis=-1, keepdims=True)
    return (rows * lax.rsqrt(mean_square + EPS) * gain).astype(jnp.bfloat16)


def position(distance, serve, owners):
    return jnp.where(distance % 2 == serve, 0, owners // 2) + distance // 2


def own_slots(sess_ref, req_count):
    me = lax.axis_index("cache")
    base = me * req_count
    sessions = [sess_ref[base + request] for request in range(req_count)]
    slots = []
    for request in range(req_count):
        place = 0
        for earlier in range(request):
            place = place + (sessions[earlier] == sessions[request]).astype(jnp.int32)
        slots.append((sessions[request] ^ me, place))
    return slots


def message_kernel(sess_ref, own_ref, other_ref, *refs):
    *out_refs, table_ref = refs
    req_count, half_cands, _ = own_ref.shape
    serve = lax.axis_index("serve")
    messages = len(out_refs)
    unused = 2 * messages * CAP
    for at in range(2 * messages * CAP):
        table_ref[at] = jnp.zeros_like(table_ref[at])
    for request, (distance, place) in enumerate(own_slots(sess_ref, req_count)):
        ours = distance % 2 == serve
        for side, rows_ref in enumerate((own_ref, other_ref)):
            at = (distance // 2 * 2 + side) * CAP + place
            table_ref[jnp.where(ours, at, unused + side)] = rows_ref[request].astype(jnp.float32)
    for at, out_ref in enumerate(out_refs):
        rows = table_ref[2 * CAP * at : 2 * CAP * (at + 1)]
        out_ref[...] = rows.reshape(out_ref.shape).astype(jnp.bfloat16)


def visible_kernel(sess_ref, len_ref, mask_ref, hide_rows_ref, hide_cols_ref, marks_ref):
    me = lax.axis_index("cache")
    blocks, requests = mask_ref.shape
    owners = len_ref.shape[0]
    per_owner = requests // owners
    sessions = sess_ref[...]
    lane = lax.broadcasted_iota(jnp.int32, (1, requests), 1)
    place = jnp.zeros((1, requests), jnp.int32)
    for back in range(1, per_owner):
        same = (pltpu.roll(sessions, back, 1) == sessions) & (lane % per_owner >= back)
        place = place + same.astype(jnp.int32)
    at = position((lane // per_owner) ^ me, lax.axis_index("serve"), owners)
    slot_of = jnp.where(sessions == me, at * CAP + place, -1)
    slots = owners * CAP
    at_slot = lax.broadcasted_iota(jnp.int32, (slots, requests), 0)
    chosen = (at_slot == slot_of).astype(jnp.float32).astype(jnp.bfloat16)
    marks_ref[...] = jnp.zeros_like(marks_ref)
    marks_ref[:blocks, :] = mask_ref[...].astype(jnp.float32).astype(jnp.bfloat16)
    seen = lax.dot_general(chosen, marks_ref[...], (((1,), (1,)), ((), ())), preferred_element_type=jnp.float32)
    at_lane = lax.broadcasted_iota(jnp.int32, (slots, HD), 1)
    hidden = jnp.where(at_lane < blocks, (1.0 - seen) * HIDE, jnp.where(at_lane == blocks, HIDE, 0.0))
    half = hide_rows_ref.shape[0] // slots // 2
    spread = jnp.broadcast_to(hidden.reshape(owners, 1, CAP, 1, HD), (owners, 2, CAP, half, HD))
    hide_rows_ref[...] = spread.reshape(hide_rows_ref.shape).astype(jnp.bfloat16)
    hist_rows = hide_cols_ref.shape[0]
    at_row = lax.broadcasted_iota(jnp.int32, (hist_rows, HD), 0)
    at_lane = lax.broadcasted_iota(jnp.int32, (hist_rows, HD), 1)
    hide_cols_ref[...] = jnp.where(
        (at_lane == at_row // BLK) | ((at_lane == blocks) & (at_row >= len_ref[me])), 1.0, 0.0
    ).astype(jnp.bfloat16)


def self_kernel(own_ref, other_ref, gain_ref, w_ref, keep_ref, give_ref, normed_ref):
    rows, width = keep_ref.shape[1:]
    gain = gain_ref[...].astype(jnp.float32)
    normed_ref[:rows, :] = normed_rows(own_ref, gain)
    normed_ref[rows:, :] = normed_rows(other_ref, gain)
    normed = normed_ref[...]

    def activated(part):
        return silu(jnp.dot(normed, w_ref[part], preferred_element_type=jnp.float32)).astype(jnp.bfloat16)

    products = activated(0).astype(jnp.float32) * activated(1).astype(jnp.float32)
    values, gates = activated(2), activated(3)
    for low in range(0, width, HD):
        score = jnp.sum(products[:, low : low + HD], axis=-1, keepdims=True) * SCALE
        term = (silu(score) * values[:, low : low + HD].astype(jnp.float32)).astype(jnp.bfloat16)
        keep_ref[0, :, low : low + HD] = term[:rows]
        give_ref[0, :, low : low + HD] = term[rows:]
    keep_ref[1] = gates[:rows]
    give_ref[1] = gates[rows:]


def pack_kernel(keep_ref, got_ref, *out_refs):
    part = out_refs[0].shape[0] // 4
    for at, out_ref in enumerate(out_refs):
        for side in range(2):
            low = (2 * at + side) * part
            out_ref[2 * side * part : (2 * side + 1) * part, :] = keep_ref[low : low + part, :]
            out_ref[(2 * side + 1) * part : (2 * side + 2) * part, :] = got_ref[low : low + part, :]


def history_kernel(owners, gain_ref, w_ref, hide_rows_ref, hide_cols_ref, keys_ref, values_ref, *refs):
    keep_ref, give_ref = refs[owners:]
    slot_refs = [None] * owners
    for at, order in enumerate(far_first(owners // 2)):
        slot_refs[order], slot_refs[owners // 2 + order] = refs[2 * at : 2 * at + 2]
    rows, width = keep_ref.shape
    per_owner = rows // (owners // 2)
    hist_rows = keys_ref.shape[0]
    span = min(256, hist_rows)
    per_step = max(1, min(owners, 256 // per_owner))
    gain = gain_ref[...].astype(jnp.float32)
    for first in range(0, owners, per_step):
        group = range(first, min(first + per_step, owners))
        normed = jnp.concatenate([normed_rows(slot_refs[at], gain) for at in group], axis=0)
        queries = silu(jnp.dot(normed, w_ref[0], preferred_element_type=jnp.float32)).astype(jnp.bfloat16)
        hide_rows = hide_rows_ref[first * per_owner : first * per_owner + queries.shape[0], :]
        for low in range(0, width, HD):
            lhs = jnp.concatenate([queries[:, low : low + HD], hide_rows], axis=1)
            total = None
            for start in range(0, hist_rows, span):
                rhs = jnp.concatenate(
                    [keys_ref[start : start + span, low : low + HD], hide_cols_ref[start : start + span, :]], axis=1
                )
                scores = lax.dot_general(lhs, rhs, (((1,), (1,)), ((), ())), preferred_element_type=jnp.float32)
                weights = silu_of_half(scores * (0.5 * SCALE)).astype(jnp.bfloat16)
                term = jnp.dot(
                    weights, values_ref[start : start + span, low : low + HD], preferred_element_type=jnp.float32
                )
                total = term if total is None else total + term
            total = total.astype(jnp.bfloat16)
            for place, at in enumerate(group):
                out_ref, row = (keep_ref, at * per_owner) if at < owners // 2 else (give_ref, at * per_owner - rows)
                out_ref[row : row + per_owner, low : low + HD] = total[place * per_owner : (place + 1) * per_owner]


def output_kernel(messages, sess_ref, own_ref, keep_ref, got_ref, w_own_ref, w_other_ref, *refs):
    back_refs, (out_ref, table_ref) = refs[: 2 * messages], refs[2 * messages :]
    req_count, half_cands, model_width = own_ref.shape
    rows = req_count * half_cands
    width = model_width // 2
    serve = lax.axis_index("serve")
    part = CAP * half_cands
    for order, at in enumerate(far_first(messages)):
        for side in range(2):
            block = back_refs[2 * order + side][: 2 * part, :].astype(jnp.float32).reshape(2, CAP, half_cands, width)
            for heads in range(2):
                low = ((side * messages + at) * 2 + heads) * CAP
                table_ref[low : low + CAP] = block[heads if side == 0 else 1 - heads]
    own = own_slots(sess_ref, req_count)
    total = own_ref[...].astype(jnp.float32).reshape(rows, model_width)
    for heads, (terms_ref, w_ref) in enumerate(((keep_ref, w_own_ref), (got_ref, w_other_ref))):
        history = []
        for distance, place in own:
            side = jnp.where(distance % 2 == serve, 0, messages)
            history.append(table_ref[((side + distance // 2) * 2 + heads) * CAP + place])
        attended = jnp.concatenate(history, axis=0) + terms_ref[0].astype(jnp.float32)
        gates = terms_ref[1].astype(jnp.float32)
        mixed = []
        for low in range(0, width, HD):
            head = attended[:, low : low + HD]
            level = lax.rsqrt(jnp.mean(head * head, axis=-1, keepdims=True) + EPS)
            mixed.append((head * level * gates[:, low : low + HD]).astype(jnp.bfloat16))
        total = total + jnp.dot(jnp.concatenate(mixed, axis=1), w_ref[...], preferred_element_type=jnp.float32)
    out_ref[...] = total.reshape(out_ref.shape).astype(jnp.bfloat16)


def far_first(count):
    return list(reversed(range(count)))


def swap(rows):
    return lax.ppermute(rows, "serve", [(0, 1), (1, 0)])


def cross(owners, messages):
    came = []
    for at in far_first(len(messages)):
        pairs = [
            (place * 2 + core, (place ^ (2 * at + core)) * 2 + core) for place in range(owners) for core in range(2)
        ]
        came.append(lax.ppermute(messages[at], ("cache", "serve"), pairs))
    return came


def body(candidates, input_gain, w_in, w_out, hist_keys, hist_values, request_session, hist_len, block_mask):
    owners = lax.axis_size("cache")
    req_count, half_cands, model_width = candidates.shape
    width = w_in.shape[2]
    rows = req_count * half_cands
    hist_rows = hist_keys.shape[1]
    bf16 = functools.partial(jax.ShapeDtypeStruct, dtype=jnp.bfloat16)
    sessions = request_session.reshape(-1)
    gain = input_gain.reshape(1, -1)
    messages = owners // 2
    piece = 2 * CAP * half_cands
    half_table = bf16((messages * piece, width))

    other, w_out = lax.optimization_barrier((swap(candidates), w_out))
    w_other = swap(w_out)
    out = kernel_call(
        message_kernel,
        [bf16((piece, model_width))] * messages,
        [smem, vmem, vmem],
        [pltpu.VMEM((2 * messages * CAP + 2, half_cands, model_width), jnp.float32)],
    )(sessions, candidates, other)
    out, w_in = lax.optimization_barrier((out, w_in))
    weights = jnp.transpose(w_in, (1, 0, 2))
    came = cross(owners, out)
    visible = kernel_call(
        visible_kernel,
        [bf16((owners * piece, HD)), bf16((hist_rows, HD))],
        [vmem, smem, vmem],
        [pltpu.VMEM((HD, owners * req_count), jnp.bfloat16)],
    )(request_session.reshape(1, -1), hist_len, block_mask.T)
    came, weights, (hide_rows, hide_cols) = lax.optimization_barrier((came, weights, visible))
    swapped = [swap(message) for message in came]
    keep, give = kernel_call(
        functools.partial(history_kernel, owners),
        [half_table] * 2,
        [vmem] * (6 + owners),
        flops=8 * owners * piece * hist_rows * width,
        moved=4 * hist_rows * width,
    )(
        gain,
        weights,
        hide_rows,
        hide_cols,
        hist_keys.reshape(hist_rows, width),
        hist_values.reshape(hist_rows, width),
        *[rows_of for both in zip(came, swapped) for rows_of in both],
    )
    out = kernel_call(pack_kernel, [bf16((2 * piece, width))] * messages, [vmem] * 2)(keep, swap(give))
    out, other = lax.optimization_barrier((out, other))
    backs = cross(owners, out)
    keep, give = kernel_call(
        self_kernel,
        [bf16((2, rows, width))] * 2,
        [vmem] * 4,
        [pltpu.VMEM((2 * rows, model_width), jnp.bfloat16)],
        flops=16 * rows * model_width * width,
        moved=8 * model_width * width,
    )(candidates, other, gain, weights)
    backs, keep, give = lax.optimization_barrier((backs, keep, give))
    got = swap(give)
    returned = [(back, swap(back[piece:])) for back in backs]
    return kernel_call(
        functools.partial(output_kernel, messages),
        bf16((req_count, half_cands, model_width)),
        [smem] + [vmem] * (5 + 2 * messages),
        [pltpu.VMEM((4 * messages * CAP, half_cands, width), jnp.float32)],
        flops=8 * rows * model_width * width,
        moved=4 * model_width * width,
    )(sessions, candidates, keep, got, w_out, w_other, *[rows_of for both in returned for rows_of in both])


def solution(mesh):
    placed = (
        P(("groups", "cache"), "serve", None),
        P(),
        P(None, None, "serve"),
        P("serve", None),
        P(("groups", "cache"), None, "serve"),
        P(("groups", "cache"), None, "serve"),
        P("groups", None),
        P("groups"),
        P("groups", None),
    )
    return jax.shard_map(
        body,
        mesh=mesh,
        in_specs=placed,
        out_specs=P(("groups", "cache"), "serve", None),
        check_vma=False,
    )
```

time: 39.7 us -> 41.6 us (1.048)
  starting transfers between devices: 21.2 us -> 17.7 us
  local copies, waits for them, and re-layouts: 3.08 us -> 6.16 us
  waiting for transfers between devices: 6.8 us -> 8.87 us
    ppermute x10 -> x12, starting transfers between devices: 10 us -> 6.54 us  [swap(): return lax.ppermute(rows, 'serve', [(0, 1), (1, 0)])]
    optimization_barrier x0 -> x1, local copies, waits for them, and re-layouts: none -> 3.18 us  [body(): out, w_in = lax.optimization_barrier((out, w_in))]
    ppermute x10 -> x12, waiting for transfers between devices: 2.38 us -> 5.2 us  [swap(): return lax.ppermute(rows, 'serve', [(0, 1), (1, 0)])]
    ppermute x8, waiting for transfers between devices: 4.42 us -> 3.67 us  [cross(): came.append(lax.ppermute(messages[at], ('cache', 'serve'), pairs))]
    pallas_call x7 -> x5, Pallas kernels: 5.19 us -> 4.74 us  [the longest x1 1.83 us: body(): kernel_call(functools.partial(output_kernel, messages), bf16((req_count,...]
    pallas_call x1, Pallas kernels: 3.18 us -> 3.62 us  [body(): kernel_call(functools.partial(history_kernel, owners), [half_table] * 2,...]
    unnamed x17 -> x20, local copies, waits for them, and re-layouts: 3.06 us -> 2.96 us
  transfers between devices with their start and end apart: 18 -> 20, of which waited for: 6 -> 11; matrix products, arithmetic and copies ran while one was open for 8% -> 8% of each run, Pallas kernels for 18% -> 16%
where the time goes in v8:
time: 41.6 us; the launch traced here: 41.3 us
  starting transfers between devices  17.7 us (43%)
  waiting for transfers between devices  8.87 us (21%)
  Pallas kernels  8.36 us (20%)
  local copies, waits for them, and re-layouts  6.16 us (15%)
    ppermute x8, starting transfers between devices, cross(): came.append(lax.ppermute(messages[at], ('cache', 'serve'), pairs))  11.2 us
    ppermute x12, starting transfers between devices, swap(): return lax.ppermute(rows, 'serve', [(0, 1), (1, 0)])  6.54 us
    ppermute x12, waiting for transfers between devices, swap(): return lax.ppermute(rows, 'serve', [(0, 1), (1, 0)])  5.2 us
    ppermute x8, waiting for transfers between devices, cross(): came.append(lax.ppermute(messages[at], ('cache', 'serve'), pairs))  3.67 us
    pallas_call x1, Pallas kernels, body(): kernel_call(functools.partial(history_kernel, owners), [half_table] * 2,...  3.62 us
    optimization_barrier x1, local copies, waits for them, and re-layouts, body(): out, w_in = lax.optimization_barrier((out, w_in))  3.18 us
    unnamed x20, local copies, waits for them, and re-layouts  2.96 us
    pallas_call x1, Pallas kernels, body(): kernel_call(functools.partial(output_kernel, messages), bf16((req_count,...  1.83 us
  transfers between devices with their start and end apart: 20, of which 11 were waited for; matrix products, arithmetic and copies ran while one was open for 8% of the time, Pallas kernels for 16%

profile of v8, /device:TPU:0, one launch (start us, length us, event | category | flops | bytes accessed | tf_op | source)
XLA Modules:
  0.0 41.3 jit_solution(15459577129422903811)
XLA Ops:
  0.0 0.5 %collective-permute-start = (bf16[8,8,1024]{2,1,0:T(8,128)(2,1)}, bf16[8,8,1024]{2,1,0:T(8,128)(2,1)S(1)}, u32[]{:S(2)}, u32[]{:S(2)}) collective-permute-start(bf16[8,8,1024]{2,1,0:T(8,128)(2,1)} %own_ref.5), channel_id=1, source_target_pairs={{0,1},{1,0},{2,3},{3,2},{4,5},{5,4},{6,7},{7,6},{8,9},{9,8},{10,11... | collective-permute-start | bytes 393224 | tf_op jit(solution)/shard_map/ppermute | solution.py:217
  0.5 1.2 %collective-permute-done.other_ref = bf16[8,8,1024]{2,1,0:T(8,128)(2,1)S(1)} collective-permute-done((bf16[8,8,1024]{2,1,0:T(8,128)(2,1)}, bf16[8,8,1024]{2,1,0:T(8,128)(2,1)S(1)}, u32[]{:S(2)}, u32[]{:S(2)}) %collective-permute-start) | collective-permute-done | bytes 131104 | tf_op jit(solution)/shard_map/ppermute | solution.py:217
  1.7 0.4 collective-permute-start.15
  2.0 0.0 copy-start.2
  2.0 0.9 %copy-done.2 = bf16[8,8,1024]{2,1,0:T(8,128)(2,1)S(1)} copy-done((bf16[8,8,1024]{2,1,0:T(8,128)(2,1)S(1)}, bf16[8,8,1024]{2,1,0:T(8,128)(2,1)}, u32[]{:S(2)}) %copy-start.2) | copy-done | bytes 131096
  2.9 0.0 copy-start.6
  2.9 0.7 %copy-done.6 = s32[64,1]{0,1:T(1,128)S(1)} copy-done((s32[64,1]{0,1:T(1,128)S(1)}, s32[64,1]{0,1:T(1,128)}, u32[]{:S(2)}) %copy-start.6) | copy-done | bytes 280
  3.6 0.7 %shard_map.91 = (bf16[32,1024]{1,0:T(8,128)(2,1)S(1)}, bf16[32,1024]{1,0:T(8,128)(2,1)S(1)}, bf16[32,1024]{1,0:T(8,128)(2,1)S(1)}, bf16[32,1024]{1,0:T(8,128)(2,1)S(1)}) custom-call(s32[64]{0:T(128)S(1)} %bitcast.13, bf16[8,8,1024]{2,1,0:T(8,128)(2,1)S(1)} %copy-done.2, bf16[8,8,1024]{2,1,0:T(8,128)(2,1)S(1)} %collective-permute-done.other_ref), custom_call_target="tpu_custom_call" | custom-call | tf_op jit(solution)/shard_map/pallas_call | solution.py:245
  4.3 4.8 %collective-permute-start.1 = (bf16[32,1024]{1,0:T(8,128)(2,1)S(1)}, bf16[32,1024]{1,0:T(8,128)(2,1)S(1)}, u32[]{:S(2)}, u32[]{:S(2)}) collective-permute-start(bf16[32,1024]{1,0:T(8,128)(2,1)S(1)} %get-tuple-element.49), channel_id=1, source_target_pairs={{0,12},{1,15},{2,14},{3,13},{4,8},{5,11},{6,10},{7,9},{8,4},{9,7},... | collective-permute-start | bytes 196616 | tf_op jit(solution)/shard_map/ppermute | solution.py:226
  9.1 0.0 collective-permute-start.2
  9.1 0.6 %collective-permute-start.3 = (bf16[32,1024]{1,0:T(8,128)(2,1)S(1)}, bf16[32,1024]{1,0:T(8,128)(2,1)S(1)}, u32[]{:S(2)}, u32[]{:S(2)}) collective-permute-start(bf16[32,1024]{1,0:T(8,128)(2,1)S(1)} %get-tuple-element.51), channel_id=1, source_target_pairs={{0,4},{1,7},{2,6},{3,5},{4,0},{5,3},{6,2},{7,1},{8,12},{9,15},{10,... | collective-permute-start | bytes 196616 | tf_op jit(solution)/shard_map/ppermute | solution.py:226
  9.7 0.7 %collective-permute-start.4 = (bf16[32,1024]{1,0:T(8,128)(2,1)S(1)}, bf16[32,1024]{1,0:T(8,128)(2,1)S(1)}, u32[]{:S(2)}, u32[]{:S(2)}) collective-permute-start(bf16[32,1024]{1,0:T(8,128)(2,1)S(1)} %get-tuple-element.52), channel_id=1, source_target_pairs={{0,0},{1,3},{2,2},{3,1},{4,4},{5,7},{6,6},{7,5},{8,8},{9,11},{10,1... | collective-permute-start | bytes 196616 | tf_op jit(solution)/shard_map/ppermute | solution.py:226
  10.4 0.0 copy-start.5
  10.4 0.7 %copy-done.5 = s32[64,32]{0,1:T(8,128)S(1)} copy-done((s32[64,32]{0,1:T(8,128)S(1)}, s32[64,32]{0,1:T(8,128)}, u32[]{:S(2)}) %copy-start.5) | copy-done | bytes 8216
  11.1 0.7 %copy-done.8 = s32[8]{0:T(128)S(1)} copy-done((s32[8]{0:T(128)S(1)}, s32[8]{0:T(128)}, u32[]{:S(2)}) %copy-start.8) | copy-done | bytes 56
  11.8 1.3 %shard_map.92 = (bf16[256,128]{1,0:T(8,128)(2,1)S(1)}, bf16[2048,128]{1,0:T(8,128)(2,1)S(1)}) custom-call(s32[1,64]{1,0:T(1,128)S(1)} %bitcast.14, s32[8]{0:T(128)S(1)} %copy-done.8, s32[32,64]{1,0:T(8,128)S(1)} %bitcast.12), custom_call_target="tpu_custom_call" | custom-call | tf_op jit(solution)/shard_map/pallas_call | solution.py:254
  13.1 0.0 copy-start.9
  13.1 0.0 copy-start
  13.1 0.0 copy-start.1
  13.1 3.2 %copy.12 = bf16[1024,4,512]{2,0,1:T(8,128)(2,1)S(1)} copy(bf16[1024,4,512]{2,1,0:T(4,128)(2,1)} %param.11) | data formatting | bytes 8388608 | tf_op jit(solution)/shard_map/optimization_barrier | solution.py:251
  16.3 0.0 collective-permute-done.1.refs_0_
  16.3 0.0 collective-permute-done.2.refs_2_
  16.3 0.0 collective-permute-done.3.refs_4_
  16.4 0.0 collective-permute-done.4.refs_6_
  16.4 3.2 %collective-permute-start.5 = (bf16[32,1024]{1,0:T(8,128)(2,1)S(1)}, bf16[32,1024]{1,0:T(8,128)(2,1)S(1)}, u32[]{:S(2)}, u32[]{:S(2)}) collective-permute-start(bf16[32,1024]{1,0:T(8,128)(2,1)S(1)} %collective-permute-done.1.refs_0_), channel_id=1, source_target_pairs={{0,1},{1,0},{2,3},{3,2},{4,5},{5,4},{6,7},{7,6},{8,9},{9,8},{10,11... | collective-permute-start | bytes 196616 | tf_op jit(solution)/shard_map/ppermute | solution.py:217
  19.6 0.1 collective-permute-start.6
  19.7 0.4 %collective-permute-start.7 = (bf16[32,1024]{1,0:T(8,128)(2,1)S(1)}, bf16[32,1024]{1,0:T(8,128)(2,1)S(1)}, u32[]{:S(2)}, u32[]{:S(2)}) collective-permute-start(bf16[32,1024]{1,0:T(8,128)(2,1)S(1)} %collective-permute-done.3.refs_4_), channel_id=1, source_target_pairs={{0,1},{1,0},{2,3},{3,2},{4,5},{5,4},{6,7},{7,6},{8,9},{9,8},{10,11... | collective-permute-start | bytes 196616 | tf_op jit(solution)/shard_map/ppermute | solution.py:217
  20.1 0.1 collective-permute-start.8
  20.2 0.0 copy-done.9
  20.2 0.3 collective-permute-done.5.refs_1_
  20.5 0.4 collective-permute-done.6.refs_3_
  20.9 0.2 collective-permute-done.7.refs_5_
  21.0 0.4 collective-permute-done.8.refs_7_
  21.4 0.0 copy-done
  21.4 0.0 copy-done.1
  21.4 3.6 %shard_map.93 = (bf16[128,512]{1,0:T(8,128)(2,1)S(1)}, bf16[128,512]{1,0:T(8,128)(2,1)S(1)}) custom-call(bf16[1,1024]{1,0:T(2,128)(2,1)S(1)} %reshape.16.gain_ref, bf16[4,1024,512]{2,1,0:T(8,128)(2,1)S(1)} %bitcast.8, bf16[256,128]{1,0:T(8,128)(2,1)S(1)} %get-tuple-element.57.hide_rows_ref, bf16[2048,128]{1,0:T(8,128)(2,1)S(1)} %get-tuple-element.58.hide_cols_ref, ...), custom_call_target="tpu_custom_call" | custom-call | flops 2147483648 | bytes 4194304 | tf_op jit(solution)/shard_map/pallas_call | solution.py:262
  25.0 0.0 copy-start.4
  25.0 0.0 copy-start.7
  25.0 0.2 collective-permute-start.9
  25.3 1.2 %collective-permute-done.9.got_ref = bf16[128,512]{1,0:T(8,128)(2,1)S(1)} collective-permute-done((bf16[128,512]{1,0:T(8,128)(2,1)S(1)}, bf16[128,512]{1,0:T(8,128)(2,1)S(1)}, u32[]{:S(2)}, u32[]{:S(2)}) %collective-permute-start.9) | collective-permute-done | bytes 131104 | tf_op jit(solution)/shard_map/ppermute | solution.py:217
  26.5 3.5 %collective-permute-start.10 = (bf16[64,512]{1,0:T(8,128)(2,1)S(1)}, bf16[64,512]{1,0:T(8,128)(2,1)S(1)}, u32[]{:S(2)}, u32[]{:S(2)}) collective-permute-start(bf16[64,512]{1,0:T(8,128)(2,1)S(1)} %get-tuple-element.69), channel_id=1, source_target_pairs={{0,12},{1,15},{2,14},{3,13},{4,8},{5,11},{6,10},{7,9},{8,4},{9,7},... | collective-permute-start | bytes 196616 | tf_op jit(solution)/shard_map/ppermute | solution.py:226
  30.0 0.0 collective-permute-start.11
  30.0 1.0 %collective-permute-start.12 = (bf16[64,512]{1,0:T(8,128)(2,1)S(1)}, bf16[64,512]{1,0:T(8,128)(2,1)S(1)}, u32[]{:S(2)}, u32[]{:S(2)}) collective-permute-start(bf16[64,512]{1,0:T(8,128)(2,1)S(1)} %get-tuple-element.71), channel_id=1, source_target_pairs={{0,4},{1,7},{2,6},{3,5},{4,0},{5,3},{6,2},{7,1},{8,12},{9,15},{10,... | collective-permute-start | bytes 196616 | tf_op jit(solution)/shard_map/ppermute | solution.py:226
  30.9 0.7 %collective-permute-start.13 = (bf16[64,512]{1,0:T(8,128)(2,1)S(1)}, bf16[64,512]{1,0:T(8,128)(2,1)S(1)}, u32[]{:S(2)}, u32[]{:S(2)}) collective-permute-start(bf16[64,512]{1,0:T(8,128)(2,1)S(1)} %get-tuple-element.72), channel_id=1, source_target_pairs={{0,0},{1,3},{2,2},{3,1},{4,4},{5,7},{6,6},{7,5},{8,8},{9,11},{10,1... | collective-permute-start | bytes 196616 | tf_op jit(solution)/shard_map/ppermute | solution.py:226
  31.6 0.0 copy-done.3
  31.6 0.9 %shard_map.95 = (bf16[2,64,512]{2,1,0:T(8,128)(2,1)S(1)}, bf16[2,64,512]{2,1,0:T(8,128)(2,1)S(1)}) custom-call(bf16[8,8,1024]{2,1,0:T(8,128)(2,1)S(1)} %copy-done.3, bf16[8,8,1024]{2,1,0:T(8,128)(2,1)S(1)} %collective-permute-done.other_ref, bf16[1,1024]{1,0:T(2,128)(2,1)S(1)} %reshape.16.gain_ref, bf16[4,1024,512]{2,1,0:T(8,128)(2,1)S(1)} %bitcast.9), custom_call_target="tpu_custom_call" | custom-call | flops 536870912 | bytes 4194304 | tf_op jit(solution)/shard_map/pallas_call | solution.py:280
  32.5 0.8 %collective-permute-done.10.refs_0_ = bf16[64,512]{1,0:T(8,128)(2,1)S(1)} collective-permute-done((bf16[64,512]{1,0:T(8,128)(2,1)S(1)}, bf16[64,512]{1,0:T(8,128)(2,1)S(1)}, u32[]{:S(2)}, u32[]{:S(2)}) %collective-permute-start.10) | collective-permute-done | bytes 65568 | tf_op jit(solution)/shard_map/ppermute | solution.py:226
  33.3 2.8 %collective-permute-done.11.refs_2_ = bf16[64,512]{1,0:T(8,128)(2,1)S(1)} collective-permute-done((bf16[64,512]{1,0:T(8,128)(2,1)S(1)}, bf16[64,512]{1,0:T(8,128)(2,1)S(1)}, u32[]{:S(2)}, u32[]{:S(2)}) %collective-permute-start.11) | collective-permute-done | bytes 65568 | tf_op jit(solution)/shard_map/ppermute | solution.py:226
  36.1 0.0 collective-permute-done.12.refs_4_
  36.1 0.0 collective-permute-done.13.refs_6_
  36.1 0.9 %collective-permute-start.14 = (bf16[2,64,512]{2,1,0:T(8,128)(2,1)S(1)}, bf16[2,64,512]{2,1,0:T(8,128)(2,1)S(1)}, u32[]{:S(2)}, u32[]{:S(2)}) collective-permute-start(bf16[2,64,512]{2,1,0:T(8,128)(2,1)S(1)} %get-tuple-element.77), channel_id=1, source_target_pairs={{0,1},{1,0},{2,3},{3,2},{4,5},{5,4},{6,7},{7,6},{8,9},{9,8},{10,11... | collective-permute-start | bytes 393224 | tf_op jit(solution)/shard_map/ppermute | solution.py:217
  37.0 0.0 collective-permute-start.16
  37.1 0.5 %collective-permute-start.17 = (bf16[32,512]{1,0:T(8,128)(2,1)S(1)}, bf16[32,512]{1,0:T(8,128)(2,1)S(1)}, u32[]{:S(2)}, u32[]{:S(2)}) collective-permute-start(bf16[32,512]{1,0:T(8,128)(2,1)S(1)} %slice.13), channel_id=1, source_target_pairs={{0,1},{1,0},{2,3},{3,2},{4,5},{5,4},{6,7},{7,6},{8,9},{9,8},{10,11... | collective-permute-start | bytes 98312 | tf_op jit(solution)/shard_map/ppermute | solution.py:217
  37.6 0.1 collective-permute-start.18
  37.6 0.6 %collective-permute-done.16.refs_1_ = bf16[32,512]{1,0:T(8,128)(2,1)S(1)} collective-permute-done((bf16[32,512]{1,0:T(8,128)(2,1)S(1)}, bf16[32,512]{1,0:T(8,128)(2,1)S(1)}, u32[]{:S(2)}, u32[]{:S(2)}) %collective-permute-start.16) | collective-permute-done | bytes 32800 | tf_op jit(solution)/shard_map/ppermute | solution.py:217
  38.3 0.2 collective-permute-start.19
  38.4 0.0 collective-permute-done.17.refs_3_
  38.4 0.3 collective-permute-done.18.refs_5_
  38.8 0.7 %collective-permute-done.19.refs_7_ = bf16[32,512]{1,0:T(8,128)(2,1)S(1)} collective-permute-done((bf16[32,512]{1,0:T(8,128)(2,1)S(1)}, bf16[32,512]{1,0:T(8,128)(2,1)S(1)}, u32[]{:S(2)}, u32[]{:S(2)}) %collective-permute-start.19) | collective-permute-done | bytes 32800 | tf_op jit(solution)/shard_map/ppermute | solution.py:217
  39.5 0.0 collective-permute-done.14.got_ref
  39.5 0.0 collective-permute-done.15.w_other_ref
  39.5 0.0 copy-done.4
  39.5 0.0 copy-done.7
  39.5 1.8 %shard_map.96 = bf16[8,8,1024]{2,1,0:T(8,128)(2,1)} custom-call(s32[64]{0:T(128)S(1)} %bitcast.15, bf16[8,8,1024]{2,1,0:T(8,128)(2,1)S(1)} %copy-done.3, bf16[2,64,512]{2,1,0:T(8,128)(2,1)S(1)} %get-tuple-element.76.keep_ref, bf16[2,64,512]{2,1,0:T(8,128)(2,1)S(1)} %collective-permute-done.14.got_ref, bf16[512,1024]{1,0:T(8,128)(2,1)S(1)} %copy-done.4, ...), custom_call_target="tpu_custom_call" | custom-call | flops 268435456 | bytes 2097152 | tf_op jit(solution)/shard_map/pallas_call | solution.py:291
  (8 shorter events, 0.0 us)
Async XLA Ops:
  0.0 1.6 %collective-permute-start = (bf16[8,8,1024]{2,1,0:T(8,128)(2,1)}, bf16[8,8,1024]{2,1,0:T(8,128)(2,1)S(1)}, u32[]{:S(2)}, u32[]{:S(2)}) collective-permute-start(bf16[8,8,1024]{2,1,0:T(8,128)(2,1)} %own_ref.5), channel_id=1, source_target_pairs={{0,1},{1,0},{2,3},{3,2},{4,5},{5,4},{6,7},{7,6},{8,9},{9,8},{10,11... | collective-permute-start | bytes 393224 | tf_op jit(solution)/shard_map/ppermute | solution.py:217
  1.7 37.8 %collective-permute-start.15 = (bf16[512,1024]{1,0:T(8,128)(2,1)}, bf16[512,1024]{1,0:T(8,128)(2,1)S(1)}, u32[]{:S(2)}, u32[]{:S(2)}) collective-permute-start(bf16[512,1024]{1,0:T(8,128)(2,1)} %w_own_ref), channel_id=1, source_target_pairs={{0,1},{1,0},{2,3},{3,2},{4,5},{5,4},{6,7},{7,6},{8,9},{9,8},{10,11... | collective-permute-start | bytes 3145736 | tf_op jit(solution)/shard_map/ppermute | solution.py:217
  2.0 0.9 %copy-start.2 = (bf16[8,8,1024]{2,1,0:T(8,128)(2,1)S(1)}, bf16[8,8,1024]{2,1,0:T(8,128)(2,1)}, u32[]{:S(2)}) copy-start(bf16[8,8,1024]{2,1,0:T(8,128)(2,1)} %own_ref.5) | copy-start | bytes 393220
  2.9 0.7 %copy-start.6 = (s32[64,1]{0,1:T(1,128)S(1)}, s32[64,1]{0,1:T(1,128)}, u32[]{:S(2)}) copy-start(s32[64,1]{0,1:T(1,128)} %param.15) | copy-start | bytes 772
  4.3 12.1 %collective-permute-start.1 = (bf16[32,1024]{1,0:T(8,128)(2,1)S(1)}, bf16[32,1024]{1,0:T(8,128)(2,1)S(1)}, u32[]{:S(2)}, u32[]{:S(2)}) collective-permute-start(bf16[32,1024]{1,0:T(8,128)(2,1)S(1)} %get-tuple-element.49), channel_id=1, source_target_pairs={{0,12},{1,15},{2,14},{3,13},{4,8},{5,11},{6,10},{7,9},{8,4},{9,7},... | collective-permute-start | bytes 196616 | tf_op jit(solution)/shard_map/ppermute | solution.py:226
  9.1 7.3 %collective-permute-start.2 = (bf16[32,1024]{1,0:T(8,128)(2,1)S(1)}, bf16[32,1024]{1,0:T(8,128)(2,1)S(1)}, u32[]{:S(2)}, u32[]{:S(2)}) collective-permute-start(bf16[32,1024]{1,0:T(8,128)(2,1)S(1)} %get-tuple-element.50), channel_id=1, source_target_pairs={{0,8},{1,11},{2,10},{3,9},{4,12},{5,15},{6,14},{7,13},{8,0},{9,3},... | collective-permute-start | bytes 196616 | tf_op jit(solution)/shard_map/ppermute | solution.py:226
  9.1 7.3 %collective-permute-start.3 = (bf16[32,1024]{1,0:T(8,128)(2,1)S(1)}, bf16[32,1024]{1,0:T(8,128)(2,1)S(1)}, u32[]{:S(2)}, u32[]{:S(2)}) collective-permute-start(bf16[32,1024]{1,0:T(8,128)(2,1)S(1)} %get-tuple-element.51), channel_id=1, source_target_pairs={{0,4},{1,7},{2,6},{3,5},{4,0},{5,3},{6,2},{7,1},{8,12},{9,15},{10,... | collective-permute-start | bytes 196616 | tf_op jit(solution)/shard_map/ppermute | solution.py:226
  9.7 6.6 %collective-permute-start.4 = (bf16[32,1024]{1,0:T(8,128)(2,1)S(1)}, bf16[32,1024]{1,0:T(8,128)(2,1)S(1)}, u32[]{:S(2)}, u32[]{:S(2)}) collective-permute-start(bf16[32,1024]{1,0:T(8,128)(2,1)S(1)} %get-tuple-element.52), channel_id=1, source_target_pairs={{0,0},{1,3},{2,2},{3,1},{4,4},{5,7},{6,6},{7,5},{8,8},{9,11},{10,1... | collective-permute-start | bytes 196616 | tf_op jit(solution)/shard_map/ppermute | solution.py:226
  10.4 0.7 %copy-start.5 = (s32[64,32]{0,1:T(8,128)S(1)}, s32[64,32]{0,1:T(8,128)}, u32[]{:S(2)}) copy-start(s32[64,32]{0,1:T(8,128)} %param.17) | copy-start | bytes 24580
  11.1 0.7 %copy-start.8 = (s32[8]{0:T(128)S(1)}, s32[8]{0:T(128)}, u32[]{:S(2)}) copy-start(s32[8]{0:T(128)} %len_ref.1) | copy-start | bytes 100
  13.1 7.1 %copy-start.9 = (bf16[1024]{0:T(1024)(128)(2,1)S(1)}, bf16[1024]{0:T(1024)(128)(2,1)}, u32[]{:S(2)}) copy-start(bf16[1024]{0:T(1024)(128)(2,1)} %param.10) | copy-start | bytes 6148
  13.1 8.3 %copy-start = (bf16[1,2048,512]{2,1,0:T(8,128)(2,1)S(1)}, bf16[1,2048,512]{2,1,0:T(8,128)(2,1)}, u32[]{:S(2)}) copy-start(bf16[1,2048,512]{2,1,0:T(8,128)(2,1)} %param.13) | copy-start | bytes 6291460
  13.1 8.3 %copy-start.1 = (bf16[1,2048,512]{2,1,0:T(8,128)(2,1)S(1)}, bf16[1,2048,512]{2,1,0:T(8,128)(2,1)}, u32[]{:S(2)}) copy-start(bf16[1,2048,512]{2,1,0:T(8,128)(2,1)} %param.14) | copy-start | bytes 6291460
  16.4 4.2 %collective-permute-start.5 = (bf16[32,1024]{1,0:T(8,128)(2,1)S(1)}, bf16[32,1024]{1,0:T(8,128)(2,1)S(1)}, u32[]{:S(2)}, u32[]{:S(2)}) collective-permute-start(bf16[32,1024]{1,0:T(8,128)(2,1)S(1)} %collective-permute-done.1.refs_0_), channel_id=1, source_target_pairs={{0,1},{1,0},{2,3},{3,2},{4,5},{5,4},{6,7},{7,6},{8,9},{9,8},{10,11... | collective-permute-start | bytes 196616 | tf_op jit(solution)/shard_map/ppermute | solution.py:217
  19.6 1.3 %collective-permute-start.6 = (bf16[32,1024]{1,0:T(8,128)(2,1)S(1)}, bf16[32,1024]{1,0:T(8,128)(2,1)S(1)}, u32[]{:S(2)}, u32[]{:S(2)}) collective-permute-start(bf16[32,1024]{1,0:T(8,128)(2,1)S(1)} %collective-permute-done.2.refs_2_), channel_id=1, source_target_pairs={{0,1},{1,0},{2,3},{3,2},{4,5},{5,4},{6,7},{7,6},{8,9},{9,8},{10,11... | collective-permute-start | bytes 196616 | tf_op jit(solution)/shard_map/ppermute | solution.py:217
  19.7 1.3 %collective-permute-start.7 = (bf16[32,1024]{1,0:T(8,128)(2,1)S(1)}, bf16[32,1024]{1,0:T(8,128)(2,1)S(1)}, u32[]{:S(2)}, u32[]{:S(2)}) collective-permute-start(bf16[32,1024]{1,0:T(8,128)(2,1)S(1)} %collective-permute-done.3.refs_4_), channel_id=1, source_target_pairs={{0,1},{1,0},{2,3},{3,2},{4,5},{5,4},{6,7},{7,6},{8,9},{9,8},{10,11... | collective-permute-start | bytes 196616 | tf_op jit(solution)/shard_map/ppermute | solution.py:217
  20.1 1.3 %collective-permute-start.8 = (bf16[32,1024]{1,0:T(8,128)(2,1)S(1)}, bf16[32,1024]{1,0:T(8,128)(2,1)S(1)}, u32[]{:S(2)}, u32[]{:S(2)}) collective-permute-start(bf16[32,1024]{1,0:T(8,128)(2,1)S(1)} %collective-permute-done.4.refs_6_), channel_id=1, source_target_pairs={{0,1},{1,0},{2,3},{3,2},{4,5},{5,4},{6,7},{7,6},{8,9},{9,8},{10,11... | collective-permute-start | bytes 196616 | tf_op jit(solution)/shard_map/ppermute | solution.py:217
  21.4 10.2 %copy-start.3 = (bf16[8,8,1024]{2,1,0:T(8,128)(2,1)S(1)}, bf16[8,8,1024]{2,1,0:T(8,128)(2,1)}, u32[]{:S(2)}) copy-start(bf16[8,8,1024]{2,1,0:T(8,128)(2,1)} %own_ref.5) | copy-start | bytes 393220
  25.0 14.5 %copy-start.4 = (bf16[512,1024]{1,0:T(8,128)(2,1)S(1)}, bf16[512,1024]{1,0:T(8,128)(2,1)}, u32[]{:S(2)}) copy-start(bf16[512,1024]{1,0:T(8,128)(2,1)} %w_own_ref) | copy-start | bytes 3145732
  25.0 14.4 %copy-start.7 = (s32[64,1]{0,1:T(1,128)S(1)}, s32[64,1]{0,1:T(1,128)}, u32[]{:S(2)}) copy-start(s32[64,1]{0,1:T(1,128)} %param.15) | copy-start | bytes 772
  25.0 1.4 %collective-permute-start.9 = (bf16[128,512]{1,0:T(8,128)(2,1)S(1)}, bf16[128,512]{1,0:T(8,128)(2,1)S(1)}, u32[]{:S(2)}, u32[]{:S(2)}) collective-permute-start(bf16[128,512]{1,0:T(8,128)(2,1)S(1)} %get-tuple-element.64), channel_id=1, source_target_pairs={{0,1},{1,0},{2,3},{3,2},{4,5},{5,4},{6,7},{7,6},{8,9},{9,8},{10,11... | collective-permute-start | bytes 393224 | tf_op jit(solution)/shard_map/ppermute | solution.py:217
  26.5 6.8 %collective-permute-start.10 = (bf16[64,512]{1,0:T(8,128)(2,1)S(1)}, bf16[64,512]{1,0:T(8,128)(2,1)S(1)}, u32[]{:S(2)}, u32[]{:S(2)}) collective-permute-start(bf16[64,512]{1,0:T(8,128)(2,1)S(1)} %get-tuple-element.69), channel_id=1, source_target_pairs={{0,12},{1,15},{2,14},{3,13},{4,8},{5,11},{6,10},{7,9},{8,4},{9,7},... | collective-permute-start | bytes 196616 | tf_op jit(solution)/shard_map/ppermute | solution.py:226
  30.0 6.2 %collective-permute-start.11 = (bf16[64,512]{1,0:T(8,128)(2,1)S(1)}, bf16[64,512]{1,0:T(8,128)(2,1)S(1)}, u32[]{:S(2)}, u32[]{:S(2)}) collective-permute-start(bf16[64,512]{1,0:T(8,128)(2,1)S(1)} %get-tuple-element.70), channel_id=1, source_target_pairs={{0,8},{1,11},{2,10},{3,9},{4,12},{5,15},{6,14},{7,13},{8,0},{9,3},... | collective-permute-start | bytes 196616 | tf_op jit(solution)/shard_map/ppermute | solution.py:226
  30.0 6.2 %collective-permute-start.12 = (bf16[64,512]{1,0:T(8,128)(2,1)S(1)}, bf16[64,512]{1,0:T(8,128)(2,1)S(1)}, u32[]{:S(2)}, u32[]{:S(2)}) collective-permute-start(bf16[64,512]{1,0:T(8,128)(2,1)S(1)} %get-tuple-element.71), channel_id=1, source_target_pairs={{0,4},{1,7},{2,6},{3,5},{4,0},{5,3},{6,2},{7,1},{8,12},{9,15},{10,... | collective-permute-start | bytes 196616 | tf_op jit(solution)/shard_map/ppermute | solution.py:226
  30.9 5.2 %collective-permute-start.13 = (bf16[64,512]{1,0:T(8,128)(2,1)S(1)}, bf16[64,512]{1,0:T(8,128)(2,1)S(1)}, u32[]{:S(2)}, u32[]{:S(2)}) collective-permute-start(bf16[64,512]{1,0:T(8,128)(2,1)S(1)} %get-tuple-element.72), channel_id=1, source_target_pairs={{0,0},{1,3},{2,2},{3,1},{4,4},{5,7},{6,6},{7,5},{8,8},{9,11},{10,1... | collective-permute-start | bytes 196616 | tf_op jit(solution)/shard_map/ppermute | solution.py:226
  36.1 3.3 %collective-permute-start.14 = (bf16[2,64,512]{2,1,0:T(8,128)(2,1)S(1)}, bf16[2,64,512]{2,1,0:T(8,128)(2,1)S(1)}, u32[]{:S(2)}, u32[]{:S(2)}) collective-permute-start(bf16[2,64,512]{2,1,0:T(8,128)(2,1)S(1)} %get-tuple-element.77), channel_id=1, source_target_pairs={{0,1},{1,0},{2,3},{3,2},{4,5},{5,4},{6,7},{7,6},{8,9},{9,8},{10,11... | collective-permute-start | bytes 393224 | tf_op jit(solution)/shard_map/ppermute | solution.py:217
  37.0 1.2 %collective-permute-start.16 = (bf16[32,512]{1,0:T(8,128)(2,1)S(1)}, bf16[32,512]{1,0:T(8,128)(2,1)S(1)}, u32[]{:S(2)}, u32[]{:S(2)}) collective-permute-start(bf16[32,512]{1,0:T(8,128)(2,1)S(1)} %slice.12), channel_id=1, source_target_pairs={{0,1},{1,0},{2,3},{3,2},{4,5},{5,4},{6,7},{7,6},{8,9},{9,8},{10,11... | collective-permute-start | bytes 98312 | tf_op jit(solution)/shard_map/ppermute | solution.py:217
  37.1 1.4 %collective-permute-start.17 = (bf16[32,512]{1,0:T(8,128)(2,1)S(1)}, bf16[32,512]{1,0:T(8,128)(2,1)S(1)}, u32[]{:S(2)}, u32[]{:S(2)}) collective-permute-start(bf16[32,512]{1,0:T(8,128)(2,1)S(1)} %slice.13), channel_id=1, source_target_pairs={{0,1},{1,0},{2,3},{3,2},{4,5},{5,4},{6,7},{7,6},{8,9},{9,8},{10,11... | collective-permute-start | bytes 98312 | tf_op jit(solution)/shard_map/ppermute | solution.py:217
  37.6 1.2 %collective-permute-start.18 = (bf16[32,512]{1,0:T(8,128)(2,1)S(1)}, bf16[32,512]{1,0:T(8,128)(2,1)S(1)}, u32[]{:S(2)}, u32[]{:S(2)}) collective-permute-start(bf16[32,512]{1,0:T(8,128)(2,1)S(1)} %slice.14), channel_id=1, source_target_pairs={{0,1},{1,0},{2,3},{3,2},{4,5},{5,4},{6,7},{7,6},{8,9},{9,8},{10,11... | collective-permute-start | bytes 98312 | tf_op jit(solution)/shard_map/ppermute | solution.py:217
  38.3 1.2 %collective-permute-start.19 = (bf16[32,512]{1,0:T(8,128)(2,1)S(1)}, bf16[32,512]{1,0:T(8,128)(2,1)S(1)}, u32[]{:S(2)}, u32[]{:S(2)}) collective-permute-start(bf16[32,512]{1,0:T(8,128)(2,1)S(1)} %slice.15), channel_id=1, source_target_pairs={{0,1},{1,0},{2,3},{3,2},{4,5},{5,4},{6,7},{7,6},{8,9},{9,8},{10,11... | collective-permute-start | bytes 98312 | tf_op jit(solution)/shard_map/ppermute | solution.py:217

commit v9 on v8

--- a/solution.py
+++ b/solution.py
@@ -217,14 +217,20 @@
     return lax.ppermute(rows, "serve", [(0, 1), (1, 0)])
 
 
-def cross(owners, messages):
-    came = []
-    for at in far_first(len(messages)):
-        pairs = [
-            (place * 2 + core, (place ^ (2 * at + core)) * 2 + core) for place in range(owners) for core in range(2)
-        ]
-        came.append(lax.ppermute(messages[at], ("cache", "serve"), pairs))
-    return came
+def cross(owners, at, message):
+    pairs = [(place * 2 + core, (place ^ (2 * at + core)) * 2 + core) for place in range(owners) for core in range(2)]
+    return lax.ppermute(message, ("cache", "serve"), pairs)
+
+
+def cross_beside(owners, messages, work, take):
+    order = far_first(len(messages))
+    first, (second, *rest) = messages[order[0]], [messages[at] for at in order[1:]]
+    came = [cross(owners, order[0], first)]
+    second, done = lax.optimization_barrier((second, work(first)))
+    came.append(cross(owners, order[1], second))
+    came[0], rest = lax.optimization_barrier((came[0], rest))
+    came += [cross(owners, at, message) for at, message in zip(order[2:], rest)]
+    return [rows_of for message in came for rows_of in (message, swap(message[take:]))], done
 
 
 def body(candidates, input_gain, w_in, w_out, hist_keys, hist_values, request_session, hist_len, block_mask):
@@ -240,7 +246,13 @@
     piece = 2 * CAP * half_cands
     half_table = bf16((messages * piece, width))
 
-    other, w_out = lax.optimization_barrier((swap(candidates), w_out))
+    visible = kernel_call(
+        visible_kernel,
+        [bf16((owners * piece, HD)), bf16((hist_rows, HD))],
+        [vmem, smem, vmem],
+        [pltpu.VMEM((HD, owners * req_count), jnp.bfloat16)],
+    )(request_session.reshape(1, -1), hist_len, block_mask.T)
+    other, w_out, (hide_rows, hide_cols) = lax.optimization_barrier((swap(candidates), w_out, visible))
     w_other = swap(w_out)
     out = kernel_call(
         message_kernel,
@@ -248,17 +260,11 @@
         [smem, vmem, vmem],
         [pltpu.VMEM((2 * messages * CAP + 2, half_cands, model_width), jnp.float32)],
     )(sessions, candidates, other)
-    out, w_in = lax.optimization_barrier((out, w_in))
-    weights = jnp.transpose(w_in, (1, 0, 2))
-    came = cross(owners, out)
-    visible = kernel_call(
-        visible_kernel,
-        [bf16((owners * piece, HD)), bf16((hist_rows, HD))],
-        [vmem, smem, vmem],
-        [pltpu.VMEM((HD, owners * req_count), jnp.bfloat16)],
-    )(request_session.reshape(1, -1), hist_len, block_mask.T)
-    came, weights, (hide_rows, hide_cols) = lax.optimization_barrier((came, weights, visible))
-    swapped = [swap(message) for message in came]
+
+    def relayout(after):
+        return jnp.transpose(lax.optimization_barrier((w_in, after))[0], (1, 0, 2))
+
+    came, weights = cross_beside(owners, out, relayout, 0)
     keep, give = kernel_call(
         functools.partial(history_kernel, owners),
         [half_table] * 2,
@@ -272,22 +278,22 @@
         hide_cols,
         hist_keys.reshape(hist_rows, width),
         hist_values.reshape(hist_rows, width),
-        *[rows_of for both in zip(came, swapped) for rows_of in both],
+        *came,
     )
+    keep, give, w_other = lax.optimization_barrier((keep, give, w_other))
     out = kernel_call(pack_kernel, [bf16((2 * piece, width))] * messages, [vmem] * 2)(keep, swap(give))
-    out, other = lax.optimization_barrier((out, other))
-    backs = cross(owners, out)
-    keep, give = kernel_call(
-        self_kernel,
-        [bf16((2, rows, width))] * 2,
-        [vmem] * 4,
-        [pltpu.VMEM((2 * rows, model_width), jnp.bfloat16)],
-        flops=16 * rows * model_width * width,
-        moved=8 * model_width * width,
-    )(candidates, other, gain, weights)
-    backs, keep, give = lax.optimization_barrier((backs, keep, give))
-    got = swap(give)
-    returned = [(back, swap(back[piece:])) for back in backs]
+
+    def own_terms(after):
+        return kernel_call(
+            self_kernel,
+            [bf16((2, rows, width))] * 2,
+            [vmem] * 4,
+            [pltpu.VMEM((2 * rows, model_width), jnp.bfloat16)],
+            flops=16 * rows * model_width * width,
+            moved=8 * model_width * width,
+        )(candidates, lax.optimization_barrier((other, after))[0], gain, weights)
+
+    backs, (keep, give) = cross_beside(owners, out, own_terms, piece)
     return kernel_call(
         functools.partial(output_kernel, messages),
         bf16((req_count, half_cands, model_width)),
@@ -295,7 +301,7 @@
         [pltpu.VMEM((4 * messages * CAP, half_cands, width), jnp.float32)],
         flops=8 * rows * model_width * width,
         moved=4 * model_width * width,
-    )(sessions, candidates, keep, got, w_out, w_other, *[rows_of for both in returned for rows_of in both])
+    )(sessions, candidates, keep, swap(give), w_out, w_other, *backs)
 
 
 def solution(mesh):

time: 41.6 us -> 43.4 us (1.043)
  starting transfers between devices: 17.7 us -> 18.4 us
  waiting for transfers between devices: 8.87 us -> 9.51 us
  local copies, waits for them, and re-layouts: 6.16 us -> 6.66 us
    ppermute x8, waiting for transfers between devices: 3.67 us -> 6.76 us  [cross(): return lax.ppermute(message, ('cache', 'serve'), pairs)]
    ppermute x12, waiting for transfers between devices: 5.2 us -> 2.75 us  [swap(): return lax.ppermute(rows, 'serve', [(0, 1), (1, 0)])]
    ppermute x12, starting transfers between devices: 6.54 us -> 7.44 us  [swap(): return lax.ppermute(rows, 'serve', [(0, 1), (1, 0)])]
    unnamed x20 -> x22, local copies, waits for them, and re-layouts: 2.96 us -> 3.62 us
  transfers between devices with their start and end apart: 20 -> 20, of which waited for: 11 -> 10; matrix products, arithmetic and copies ran while one was open for 8% -> 7% of each run, Pallas kernels for 16% -> 15%
where the time goes in v9:
time: 43.4 us; the launch traced here: 43.1 us
  starting transfers between devices  18.4 us (42%)
  waiting for transfers between devices  9.51 us (22%)
  Pallas kernels  8.35 us (19%)
  local copies, waits for them, and re-layouts  6.66 us (15%)
    ppermute x8, starting transfers between devices, cross(): return lax.ppermute(message, ('cache', 'serve'), pairs)  11 us
    ppermute x12, starting transfers between devices, swap(): return lax.ppermute(rows, 'serve', [(0, 1), (1, 0)])  7.44 us
    ppermute x8, waiting for transfers between devices, cross(): return lax.ppermute(message, ('cache', 'serve'), pairs)  6.76 us
    unnamed x22, local copies, waits for them, and re-layouts  3.62 us
    pallas_call x1, Pallas kernels, body(): kernel_call(functools.partial(history_kernel, owners), [half_table] * 2,...  3.62 us
    optimization_barrier x1, local copies, waits for them, and re-layouts, relayout(): return jnp.transpose(lax.optimization_barrier((w_in, after))[0], (1, 0, 2))  3.02 us
    ppermute x12, waiting for transfers between devices, swap(): return lax.ppermute(rows, 'serve', [(0, 1), (1, 0)])  2.75 us
    pallas_call x1, Pallas kernels, body(): kernel_call(functools.partial(output_kernel, messages), bf16((req_count,...  1.83 us
  transfers between devices with their start and end apart: 20, of which 10 were waited for; matrix products, arithmetic and copies ran while one was open for 7% of the time, Pallas kernels for 15%

profile of v9, /device:TPU:0, one launch (start us, length us, event | category | flops | bytes accessed | tf_op | source)
XLA Modules:
  0.0 43.1 jit_solution(13887065549924088718)
XLA Ops:
  0.0 0.5 %collective-permute-start = (bf16[8,8,1024]{2,1,0:T(8,128)(2,1)}, bf16[8,8,1024]{2,1,0:T(8,128)(2,1)S(1)}, u32[]{:S(2)}, u32[]{:S(2)}) collective-permute-start(bf16[8,8,1024]{2,1,0:T(8,128)(2,1)} %own_ref.5), channel_id=1, source_target_pairs={{0,1},{1,0},{2,3},{3,2},{4,5},{5,4},{6,7},{7,6},{8,9},{9,8},{10,11... | collective-permute-start | bytes 393224 | tf_op jit(solution)/shard_map/ppermute | solution.py:217
  0.5 0.0 copy-start.5
  0.5 0.7 %copy-done.5 = s32[64,32]{0,1:T(8,128)S(1)} copy-done((s32[64,32]{0,1:T(8,128)S(1)}, s32[64,32]{0,1:T(8,128)}, u32[]{:S(2)}) %copy-start.5) | copy-done | bytes 8216
  1.2 0.0 copy-start.6
  1.2 0.7 %copy-done.6 = s32[64,1]{0,1:T(1,128)S(1)} copy-done((s32[64,1]{0,1:T(1,128)S(1)}, s32[64,1]{0,1:T(1,128)}, u32[]{:S(2)}) %copy-start.6) | copy-done | bytes 280
  1.8 0.7 %copy-done.9 = s32[8]{0:T(128)S(1)} copy-done((s32[8]{0:T(128)S(1)}, s32[8]{0:T(128)}, u32[]{:S(2)}) %copy-start.9) | copy-done | bytes 56
  2.5 1.3 %shard_map.91 = (bf16[256,128]{1,0:T(8,128)(2,1)S(1)}, bf16[2048,128]{1,0:T(8,128)(2,1)S(1)}) custom-call(s32[1,64]{1,0:T(1,128)S(1)} %bitcast.13, s32[8]{0:T(128)S(1)} %copy-done.9, s32[32,64]{1,0:T(8,128)S(1)} %bitcast.12), custom_call_target="tpu_custom_call" | custom-call | tf_op jit(solution)/shard_map/pallas_call | solution.py:249
  3.8 0.0 collective-permute-done.other_ref
  3.8 0.1 collective-permute-start.9
  4.0 0.9 %copy-done.2 = bf16[8,8,1024]{2,1,0:T(8,128)(2,1)S(1)} copy-done((bf16[8,8,1024]{2,1,0:T(8,128)(2,1)S(1)}, bf16[8,8,1024]{2,1,0:T(8,128)(2,1)}, u32[]{:S(2)}) %copy-start.2) | copy-done | bytes 131096
  4.9 0.7 %copy-done.7 = s32[64,1]{0,1:T(1,128)S(1)} copy-done((s32[64,1]{0,1:T(1,128)S(1)}, s32[64,1]{0,1:T(1,128)}, u32[]{:S(2)}) %copy-start.7) | copy-done | bytes 280
  5.5 0.7 %shard_map.92 = (bf16[32,1024]{1,0:T(8,128)(2,1)S(1)}, bf16[32,1024]{1,0:T(8,128)(2,1)S(1)}, bf16[32,1024]{1,0:T(8,128)(2,1)S(1)}, bf16[32,1024]{1,0:T(8,128)(2,1)S(1)}) custom-call(s32[64]{0:T(128)S(1)} %bitcast.14, bf16[8,8,1024]{2,1,0:T(8,128)(2,1)S(1)} %copy-done.2, bf16[8,8,1024]{2,1,0:T(8,128)(2,1)S(1)} %collective-permute-done.other_ref), custom_call_target="tpu_custom_call" | custom-call | tf_op jit(solution)/shard_map/pallas_call | solution.py:257
  6.2 0.0 copy-start.10
  6.2 0.0 copy-start
  6.2 0.0 copy-start.1
  6.3 5.1 %collective-permute-start.1 = (bf16[32,1024]{1,0:T(8,128)(2,1)S(1)}, bf16[32,1024]{1,0:T(8,128)(2,1)S(1)}, u32[]{:S(2)}, u32[]{:S(2)}) collective-permute-start(bf16[32,1024]{1,0:T(8,128)(2,1)S(1)} %get-tuple-element.43), channel_id=1, source_target_pairs={{0,12},{1,15},{2,14},{3,13},{4,8},{5,11},{6,10},{7,9},{8,4},{9,7},... | collective-permute-start | bytes 196616 | tf_op jit(solution)/shard_map/ppermute | solution.py:222
  11.4 3.0 %copy.12 = bf16[1024,4,512]{2,0,1:T(8,128)(2,1)S(1)} copy(bf16[1024,4,512]{2,1,0:T(4,128)(2,1)} %param.11) | data formatting | bytes 8388608 | tf_op jit(solution)/shard_map/optimization_barrier | solution.py:265
  14.4 0.1 collective-permute-start.3
  14.5 0.0 collective-permute-done.1.refs_0_
  14.5 1.2 %collective-permute-start.5 = (bf16[32,1024]{1,0:T(8,128)(2,1)S(1)}, bf16[32,1024]{1,0:T(8,128)(2,1)S(1)}, u32[]{:S(2)}, u32[]{:S(2)}) collective-permute-start(bf16[32,1024]{1,0:T(8,128)(2,1)S(1)} %get-tuple-element.52), channel_id=1, source_target_pairs={{0,4},{1,7},{2,6},{3,5},{4,0},{5,3},{6,2},{7,1},{8,12},{9,15},{10,... | collective-permute-start | bytes 196616 | tf_op jit(solution)/shard_map/ppermute | solution.py:222
  15.7 0.7 %collective-permute-start.7 = (bf16[32,1024]{1,0:T(8,128)(2,1)S(1)}, bf16[32,1024]{1,0:T(8,128)(2,1)S(1)}, u32[]{:S(2)}, u32[]{:S(2)}) collective-permute-start(bf16[32,1024]{1,0:T(8,128)(2,1)S(1)} %get-tuple-element.53), channel_id=1, source_target_pairs={{0,0},{1,3},{2,2},{3,1},{4,4},{5,7},{6,6},{7,5},{8,8},{9,11},{10,1... | collective-permute-start | bytes 196616 | tf_op jit(solution)/shard_map/ppermute | solution.py:222
  16.4 2.4 %collective-permute-start.2 = (bf16[32,1024]{1,0:T(8,128)(2,1)S(1)}, bf16[32,1024]{1,0:T(8,128)(2,1)S(1)}, u32[]{:S(2)}, u32[]{:S(2)}) collective-permute-start(bf16[32,1024]{1,0:T(8,128)(2,1)S(1)} %collective-permute-done.1.refs_0_), channel_id=1, source_target_pairs={{0,1},{1,0},{2,3},{3,2},{4,5},{5,4},{6,7},{7,6},{8,9},{9,8},{10,11... | collective-permute-start | bytes 196616 | tf_op jit(solution)/shard_map/ppermute | solution.py:217
  18.8 1.7 %collective-permute-done.3.refs_2_ = bf16[32,1024]{1,0:T(8,128)(2,1)S(1)} collective-permute-done((bf16[32,1024]{1,0:T(8,128)(2,1)S(1)}, bf16[32,1024]{1,0:T(8,128)(2,1)S(1)}, u32[]{:S(2)}, u32[]{:S(2)}) %collective-permute-start.3) | collective-permute-done | bytes 65568 | tf_op jit(solution)/shard_map/ppermute | solution.py:222
  20.5 0.7 %collective-permute-start.4 = (bf16[32,1024]{1,0:T(8,128)(2,1)S(1)}, bf16[32,1024]{1,0:T(8,128)(2,1)S(1)}, u32[]{:S(2)}, u32[]{:S(2)}) collective-permute-start(bf16[32,1024]{1,0:T(8,128)(2,1)S(1)} %collective-permute-done.3.refs_2_), channel_id=1, source_target_pairs={{0,1},{1,0},{2,3},{3,2},{4,5},{5,4},{6,7},{7,6},{8,9},{9,8},{10,11... | collective-permute-start | bytes 196616 | tf_op jit(solution)/shard_map/ppermute | solution.py:217
  21.2 0.0 collective-permute-done.5.refs_4_
  21.2 0.0 collective-permute-start.6
  21.2 0.0 collective-permute-done.7.refs_6_
  21.2 0.5 %collective-permute-start.8 = (bf16[32,1024]{1,0:T(8,128)(2,1)S(1)}, bf16[32,1024]{1,0:T(8,128)(2,1)S(1)}, u32[]{:S(2)}, u32[]{:S(2)}) collective-permute-start(bf16[32,1024]{1,0:T(8,128)(2,1)S(1)} %collective-permute-done.7.refs_6_), channel_id=1, source_target_pairs={{0,1},{1,0},{2,3},{3,2},{4,5},{5,4},{6,7},{7,6},{8,9},{9,8},{10,11... | collective-permute-start | bytes 196616 | tf_op jit(solution)/shard_map/ppermute | solution.py:217
  21.8 0.0 copy-done.10
  21.8 0.0 collective-permute-done.2.refs_1_
  21.8 0.4 collective-permute-done.4.refs_3_
  22.1 0.4 collective-permute-done.6.refs_5_
  22.5 0.2 collective-permute-done.8.refs_7_
  22.7 0.0 copy-done
  22.7 0.0 copy-done.1
  22.7 3.6 %shard_map.93 = (bf16[128,512]{1,0:T(8,128)(2,1)S(1)}, bf16[128,512]{1,0:T(8,128)(2,1)S(1)}) custom-call(bf16[1,1024]{1,0:T(2,128)(2,1)S(1)} %reshape.16.gain_ref, bf16[4,1024,512]{2,1,0:T(8,128)(2,1)S(1)} %bitcast.8, bf16[256,128]{1,0:T(8,128)(2,1)S(1)} %get-tuple-element.46.hide_rows_ref, bf16[2048,128]{1,0:T(8,128)(2,1)S(1)} %get-tuple-element.47.hide_cols_ref, ...), custom_call_target="tpu_custom_call" | custom-call | flops 2147483648 | bytes 4194304 | tf_op jit(solution)/shard_map/pallas_call | solution.py:268
  26.3 0.0 copy-start.4
  26.3 0.0 copy-start.8
  26.3 0.0 collective-permute-done.9.w_other_ref
  26.3 0.4 collective-permute-start.10
  26.7 1.0 %collective-permute-done.10.got_ref = bf16[128,512]{1,0:T(8,128)(2,1)S(1)} collective-permute-done((bf16[128,512]{1,0:T(8,128)(2,1)S(1)}, bf16[128,512]{1,0:T(8,128)(2,1)S(1)}, u32[]{:S(2)}, u32[]{:S(2)}) %collective-permute-start.10) | collective-permute-done | bytes 131104 | tf_op jit(solution)/shard_map/ppermute | solution.py:217
  27.8 3.2 %collective-permute-start.12 = (bf16[64,512]{1,0:T(8,128)(2,1)S(1)}, bf16[64,512]{1,0:T(8,128)(2,1)S(1)}, u32[]{:S(2)}, u32[]{:S(2)}) collective-permute-start(bf16[64,512]{1,0:T(8,128)(2,1)S(1)} %get-tuple-element.60), channel_id=1, source_target_pairs={{0,12},{1,15},{2,14},{3,13},{4,8},{5,11},{6,10},{7,9},{8,4},{9,7},... | collective-permute-start | bytes 196616 | tf_op jit(solution)/shard_map/ppermute | solution.py:222
  31.0 0.0 copy-done.3
  31.0 0.9 %shard_map.95 = (bf16[2,64,512]{2,1,0:T(8,128)(2,1)S(1)}, bf16[2,64,512]{2,1,0:T(8,128)(2,1)S(1)}) custom-call(bf16[8,8,1024]{2,1,0:T(8,128)(2,1)S(1)} %copy-done.3, bf16[8,8,1024]{2,1,0:T(8,128)(2,1)S(1)} %collective-permute-done.other_ref, bf16[1,1024]{1,0:T(2,128)(2,1)S(1)} %reshape.16.gain_ref, bf16[4,1024,512]{2,1,0:T(8,128)(2,1)S(1)} %bitcast.9), custom_call_target="tpu_custom_call" | custom-call | flops 536870912 | bytes 4194304 | tf_op jit(solution)/shard_map/pallas_call | solution.py:287
  31.8 0.1 collective-permute-start.11
  31.9 0.1 collective-permute-start.14
  32.0 2.4 %collective-permute-done.12.refs_0_ = bf16[64,512]{1,0:T(8,128)(2,1)S(1)} collective-permute-done((bf16[64,512]{1,0:T(8,128)(2,1)S(1)}, bf16[64,512]{1,0:T(8,128)(2,1)S(1)}, u32[]{:S(2)}, u32[]{:S(2)}) %collective-permute-start.12) | collective-permute-done | bytes 65568 | tf_op jit(solution)/shard_map/ppermute | solution.py:222
  34.3 0.0 collective-permute-start.16
  34.3 0.7 %collective-permute-start.18 = (bf16[64,512]{1,0:T(8,128)(2,1)S(1)}, bf16[64,512]{1,0:T(8,128)(2,1)S(1)}, u32[]{:S(2)}, u32[]{:S(2)}) collective-permute-start(bf16[64,512]{1,0:T(8,128)(2,1)S(1)} %get-tuple-element.72), channel_id=1, source_target_pairs={{0,0},{1,3},{2,2},{3,1},{4,4},{5,7},{6,6},{7,5},{8,8},{9,11},{10,1... | collective-permute-start | bytes 196616 | tf_op jit(solution)/shard_map/ppermute | solution.py:222
  35.0 2.1 %collective-permute-start.13 = (bf16[32,512]{1,0:T(8,128)(2,1)S(1)}, bf16[32,512]{1,0:T(8,128)(2,1)S(1)}, u32[]{:S(2)}, u32[]{:S(2)}) collective-permute-start(bf16[32,512]{1,0:T(8,128)(2,1)S(1)} %slice.12), channel_id=1, source_target_pairs={{0,1},{1,0},{2,3},{3,2},{4,5},{5,4},{6,7},{7,6},{8,9},{9,8},{10,11... | collective-permute-start | bytes 98312 | tf_op jit(solution)/shard_map/ppermute | solution.py:217
  37.1 1.5 %collective-permute-done.14.refs_2_ = bf16[64,512]{1,0:T(8,128)(2,1)S(1)} collective-permute-done((bf16[64,512]{1,0:T(8,128)(2,1)S(1)}, bf16[64,512]{1,0:T(8,128)(2,1)S(1)}, u32[]{:S(2)}, u32[]{:S(2)}) %collective-permute-start.14) | collective-permute-done | bytes 65568 | tf_op jit(solution)/shard_map/ppermute | solution.py:222
  38.6 0.1 collective-permute-start.15
  38.7 1.2 %collective-permute-done.16.refs_4_ = bf16[64,512]{1,0:T(8,128)(2,1)S(1)} collective-permute-done((bf16[64,512]{1,0:T(8,128)(2,1)S(1)}, bf16[64,512]{1,0:T(8,128)(2,1)S(1)}, u32[]{:S(2)}, u32[]{:S(2)}) %collective-permute-start.16) | collective-permute-done | bytes 65568 | tf_op jit(solution)/shard_map/ppermute | solution.py:222
  39.9 0.1 collective-permute-start.17
  40.0 0.0 collective-permute-done.18.refs_6_
  40.0 0.4 collective-permute-start.19
  40.4 0.0 collective-permute-done.13.refs_1_
  40.4 0.0 collective-permute-done.15.refs_3_
  40.4 0.0 collective-permute-done.11.got_ref
  40.4 0.7 %collective-permute-done.17.refs_5_ = bf16[32,512]{1,0:T(8,128)(2,1)S(1)} collective-permute-done((bf16[32,512]{1,0:T(8,128)(2,1)S(1)}, bf16[32,512]{1,0:T(8,128)(2,1)S(1)}, u32[]{:S(2)}, u32[]{:S(2)}) %collective-permute-start.17) | collective-permute-done | bytes 32800 | tf_op jit(solution)/shard_map/ppermute | solution.py:217
  41.1 0.2 collective-permute-done.19.refs_7_
  41.3 0.0 copy-done.4
  41.3 0.0 copy-done.8
  41.3 1.8 %shard_map.96 = bf16[8,8,1024]{2,1,0:T(8,128)(2,1)} custom-call(s32[64]{0:T(128)S(1)} %bitcast.15, bf16[8,8,1024]{2,1,0:T(8,128)(2,1)S(1)} %copy-done.3, bf16[2,64,512]{2,1,0:T(8,128)(2,1)S(1)} %get-tuple-element.64.keep_ref, bf16[2,64,512]{2,1,0:T(8,128)(2,1)S(1)} %collective-permute-done.11.got_ref, bf16[512,1024]{1,0:T(8,128)(2,1)S(1)} %copy-done.4, ...), custom_call_target="tpu_custom_call" | custom-call | flops 268435456 | bytes 2097152 | tf_op jit(solution)/shard_map/pallas_call | solution.py:297
  (10 shorter events, 0.0 us)
Async XLA Ops:
  0.0 3.8 %collective-permute-start = (bf16[8,8,1024]{2,1,0:T(8,128)(2,1)}, bf16[8,8,1024]{2,1,0:T(8,128)(2,1)S(1)}, u32[]{:S(2)}, u32[]{:S(2)}) collective-permute-start(bf16[8,8,1024]{2,1,0:T(8,128)(2,1)} %own_ref.5), channel_id=1, source_target_pairs={{0,1},{1,0},{2,3},{3,2},{4,5},{5,4},{6,7},{7,6},{8,9},{9,8},{10,11... | collective-permute-start | bytes 393224 | tf_op jit(solution)/shard_map/ppermute | solution.py:217
  0.5 0.7 %copy-start.5 = (s32[64,32]{0,1:T(8,128)S(1)}, s32[64,32]{0,1:T(8,128)}, u32[]{:S(2)}) copy-start(s32[64,32]{0,1:T(8,128)} %param.17) | copy-start | bytes 24580
  1.2 0.7 %copy-start.6 = (s32[64,1]{0,1:T(1,128)S(1)}, s32[64,1]{0,1:T(1,128)}, u32[]{:S(2)}) copy-start(s32[64,1]{0,1:T(1,128)} %param.15) | copy-start | bytes 772
  1.8 0.7 %copy-start.9 = (s32[8]{0:T(128)S(1)}, s32[8]{0:T(128)}, u32[]{:S(2)}) copy-start(s32[8]{0:T(128)} %len_ref.1) | copy-start | bytes 100
  3.8 22.5 %collective-permute-start.9 = (bf16[512,1024]{1,0:T(8,128)(2,1)}, bf16[512,1024]{1,0:T(8,128)(2,1)S(1)}, u32[]{:S(2)}, u32[]{:S(2)}) collective-permute-start(bf16[512,1024]{1,0:T(8,128)(2,1)} %w_own_ref), channel_id=1, source_target_pairs={{0,1},{1,0},{2,3},{3,2},{4,5},{5,4},{6,7},{7,6},{8,9},{9,8},{10,11... | collective-permute-start | bytes 3145736 | tf_op jit(solution)/shard_map/ppermute | solution.py:217
  4.0 0.9 %copy-start.2 = (bf16[8,8,1024]{2,1,0:T(8,128)(2,1)S(1)}, bf16[8,8,1024]{2,1,0:T(8,128)(2,1)}, u32[]{:S(2)}) copy-start(bf16[8,8,1024]{2,1,0:T(8,128)(2,1)} %own_ref.5) | copy-start | bytes 393220
  4.9 0.7 %copy-start.7 = (s32[64,1]{0,1:T(1,128)S(1)}, s32[64,1]{0,1:T(1,128)}, u32[]{:S(2)}) copy-start(s32[64,1]{0,1:T(1,128)} %param.15) | copy-start | bytes 772
  6.2 15.5 %copy-start.10 = (bf16[1024]{0:T(1024)(128)(2,1)S(1)}, bf16[1024]{0:T(1024)(128)(2,1)}, u32[]{:S(2)}) copy-start(bf16[1024]{0:T(1024)(128)(2,1)} %param.10) | copy-start | bytes 6148
  6.2 16.4 %copy-start = (bf16[1,2048,512]{2,1,0:T(8,128)(2,1)S(1)}, bf16[1,2048,512]{2,1,0:T(8,128)(2,1)}, u32[]{:S(2)}) copy-start(bf16[1,2048,512]{2,1,0:T(8,128)(2,1)} %param.13) | copy-start | bytes 6291460
  6.2 16.4 %copy-start.1 = (bf16[1,2048,512]{2,1,0:T(8,128)(2,1)S(1)}, bf16[1,2048,512]{2,1,0:T(8,128)(2,1)}, u32[]{:S(2)}) copy-start(bf16[1,2048,512]{2,1,0:T(8,128)(2,1)} %param.14) | copy-start | bytes 6291460
  6.3 8.2 %collective-permute-start.1 = (bf16[32,1024]{1,0:T(8,128)(2,1)S(1)}, bf16[32,1024]{1,0:T(8,128)(2,1)S(1)}, u32[]{:S(2)}, u32[]{:S(2)}) collective-permute-start(bf16[32,1024]{1,0:T(8,128)(2,1)S(1)} %get-tuple-element.43), channel_id=1, source_target_pairs={{0,12},{1,15},{2,14},{3,13},{4,8},{5,11},{6,10},{7,9},{8,4},{9,7},... | collective-permute-start | bytes 196616 | tf_op jit(solution)/shard_map/ppermute | solution.py:222
  14.4 6.1 %collective-permute-start.3 = (bf16[32,1024]{1,0:T(8,128)(2,1)S(1)}, bf16[32,1024]{1,0:T(8,128)(2,1)S(1)}, u32[]{:S(2)}, u32[]{:S(2)}) collective-permute-start(bf16[32,1024]{1,0:T(8,128)(2,1)S(1)} %get-tuple-element.51), channel_id=1, source_target_pairs={{0,8},{1,11},{2,10},{3,9},{4,12},{5,15},{6,14},{7,13},{8,0},{9,3},... | collective-permute-start | bytes 196616 | tf_op jit(solution)/shard_map/ppermute | solution.py:222
  14.5 6.8 %collective-permute-start.5 = (bf16[32,1024]{1,0:T(8,128)(2,1)S(1)}, bf16[32,1024]{1,0:T(8,128)(2,1)S(1)}, u32[]{:S(2)}, u32[]{:S(2)}) collective-permute-start(bf16[32,1024]{1,0:T(8,128)(2,1)S(1)} %get-tuple-element.52), channel_id=1, source_target_pairs={{0,4},{1,7},{2,6},{3,5},{4,0},{5,3},{6,2},{7,1},{8,12},{9,15},{10,... | collective-permute-start | bytes 196616 | tf_op jit(solution)/shard_map/ppermute | solution.py:222
  15.7 5.5 %collective-permute-start.7 = (bf16[32,1024]{1,0:T(8,128)(2,1)S(1)}, bf16[32,1024]{1,0:T(8,128)(2,1)S(1)}, u32[]{:S(2)}, u32[]{:S(2)}) collective-permute-start(bf16[32,1024]{1,0:T(8,128)(2,1)S(1)} %get-tuple-element.53), channel_id=1, source_target_pairs={{0,0},{1,3},{2,2},{3,1},{4,4},{5,7},{6,6},{7,5},{8,8},{9,11},{10,1... | collective-permute-start | bytes 196616 | tf_op jit(solution)/shard_map/ppermute | solution.py:222
  16.4 5.4 %collective-permute-start.2 = (bf16[32,1024]{1,0:T(8,128)(2,1)S(1)}, bf16[32,1024]{1,0:T(8,128)(2,1)S(1)}, u32[]{:S(2)}, u32[]{:S(2)}) collective-permute-start(bf16[32,1024]{1,0:T(8,128)(2,1)S(1)} %collective-permute-done.1.refs_0_), channel_id=1, source_target_pairs={{0,1},{1,0},{2,3},{3,2},{4,5},{5,4},{6,7},{7,6},{8,9},{9,8},{10,11... | collective-permute-start | bytes 196616 | tf_op jit(solution)/shard_map/ppermute | solution.py:217
  20.5 1.6 %collective-permute-start.4 = (bf16[32,1024]{1,0:T(8,128)(2,1)S(1)}, bf16[32,1024]{1,0:T(8,128)(2,1)S(1)}, u32[]{:S(2)}, u32[]{:S(2)}) collective-permute-start(bf16[32,1024]{1,0:T(8,128)(2,1)S(1)} %collective-permute-done.3.refs_2_), channel_id=1, source_target_pairs={{0,1},{1,0},{2,3},{3,2},{4,5},{5,4},{6,7},{7,6},{8,9},{9,8},{10,11... | collective-permute-start | bytes 196616 | tf_op jit(solution)/shard_map/ppermute | solution.py:217
  21.2 1.3 %collective-permute-start.6 = (bf16[32,1024]{1,0:T(8,128)(2,1)S(1)}, bf16[32,1024]{1,0:T(8,128)(2,1)S(1)}, u32[]{:S(2)}, u32[]{:S(2)}) collective-permute-start(bf16[32,1024]{1,0:T(8,128)(2,1)S(1)} %collective-permute-done.5.refs_4_), channel_id=1, source_target_pairs={{0,1},{1,0},{2,3},{3,2},{4,5},{5,4},{6,7},{7,6},{8,9},{9,8},{10,11... | collective-permute-start | bytes 196616 | tf_op jit(solution)/shard_map/ppermute | solution.py:217
  21.2 1.4 %collective-permute-start.8 = (bf16[32,1024]{1,0:T(8,128)(2,1)S(1)}, bf16[32,1024]{1,0:T(8,128)(2,1)S(1)}, u32[]{:S(2)}, u32[]{:S(2)}) collective-permute-start(bf16[32,1024]{1,0:T(8,128)(2,1)S(1)} %collective-permute-done.7.refs_6_), channel_id=1, source_target_pairs={{0,1},{1,0},{2,3},{3,2},{4,5},{5,4},{6,7},{7,6},{8,9},{9,8},{10,11... | collective-permute-start | bytes 196616 | tf_op jit(solution)/shard_map/ppermute | solution.py:217
  22.7 8.3 %copy-start.3 = (bf16[8,8,1024]{2,1,0:T(8,128)(2,1)S(1)}, bf16[8,8,1024]{2,1,0:T(8,128)(2,1)}, u32[]{:S(2)}) copy-start(bf16[8,8,1024]{2,1,0:T(8,128)(2,1)} %own_ref.5) | copy-start | bytes 393220
  26.3 15.0 %copy-start.4 = (bf16[512,1024]{1,0:T(8,128)(2,1)S(1)}, bf16[512,1024]{1,0:T(8,128)(2,1)}, u32[]{:S(2)}) copy-start(bf16[512,1024]{1,0:T(8,128)(2,1)} %w_own_ref) | copy-start | bytes 3145732
  26.3 15.0 %copy-start.8 = (s32[64,1]{0,1:T(1,128)S(1)}, s32[64,1]{0,1:T(1,128)}, u32[]{:S(2)}) copy-start(s32[64,1]{0,1:T(1,128)} %param.15) | copy-start | bytes 772
  26.3 1.4 %collective-permute-start.10 = (bf16[128,512]{1,0:T(8,128)(2,1)S(1)}, bf16[128,512]{1,0:T(8,128)(2,1)S(1)}, u32[]{:S(2)}, u32[]{:S(2)}) collective-permute-start(bf16[128,512]{1,0:T(8,128)(2,1)S(1)} %get-tuple-element.58), channel_id=1, source_target_pairs={{0,1},{1,0},{2,3},{3,2},{4,5},{5,4},{6,7},{7,6},{8,9},{9,8},{10,11... | collective-permute-start | bytes 393224 | tf_op jit(solution)/shard_map/ppermute | solution.py:217
  27.8 6.6 %collective-permute-start.12 = (bf16[64,512]{1,0:T(8,128)(2,1)S(1)}, bf16[64,512]{1,0:T(8,128)(2,1)S(1)}, u32[]{:S(2)}, u32[]{:S(2)}) collective-permute-start(bf16[64,512]{1,0:T(8,128)(2,1)S(1)} %get-tuple-element.60), channel_id=1, source_target_pairs={{0,12},{1,15},{2,14},{3,13},{4,8},{5,11},{6,10},{7,9},{8,4},{9,7},... | collective-permute-start | bytes 196616 | tf_op jit(solution)/shard_map/ppermute | solution.py:222
  31.8 8.6 %collective-permute-start.11 = (bf16[2,64,512]{2,1,0:T(8,128)(2,1)S(1)}, bf16[2,64,512]{2,1,0:T(8,128)(2,1)S(1)}, u32[]{:S(2)}, u32[]{:S(2)}) collective-permute-start(bf16[2,64,512]{2,1,0:T(8,128)(2,1)S(1)} %get-tuple-element.65), channel_id=1, source_target_pairs={{0,1},{1,0},{2,3},{3,2},{4,5},{5,4},{6,7},{7,6},{8,9},{9,8},{10,11... | collective-permute-start | bytes 393224 | tf_op jit(solution)/shard_map/ppermute | solution.py:217
  31.9 6.7 %collective-permute-start.14 = (bf16[64,512]{1,0:T(8,128)(2,1)S(1)}, bf16[64,512]{1,0:T(8,128)(2,1)S(1)}, u32[]{:S(2)}, u32[]{:S(2)}) collective-permute-start(bf16[64,512]{1,0:T(8,128)(2,1)S(1)} %get-tuple-element.70), channel_id=1, source_target_pairs={{0,8},{1,11},{2,10},{3,9},{4,12},{5,15},{6,14},{7,13},{8,0},{9,3},... | collective-permute-start | bytes 196616 | tf_op jit(solution)/shard_map/ppermute | solution.py:222
  34.3 5.6 %collective-permute-start.16 = (bf16[64,512]{1,0:T(8,128)(2,1)S(1)}, bf16[64,512]{1,0:T(8,128)(2,1)S(1)}, u32[]{:S(2)}, u32[]{:S(2)}) collective-permute-start(bf16[64,512]{1,0:T(8,128)(2,1)S(1)} %get-tuple-element.71), channel_id=1, source_target_pairs={{0,4},{1,7},{2,6},{3,5},{4,0},{5,3},{6,2},{7,1},{8,12},{9,15},{10,... | collective-permute-start | bytes 196616 | tf_op jit(solution)/shard_map/ppermute | solution.py:222
  34.3 5.7 %collective-permute-start.18 = (bf16[64,512]{1,0:T(8,128)(2,1)S(1)}, bf16[64,512]{1,0:T(8,128)(2,1)S(1)}, u32[]{:S(2)}, u32[]{:S(2)}) collective-permute-start(bf16[64,512]{1,0:T(8,128)(2,1)S(1)} %get-tuple-element.72), channel_id=1, source_target_pairs={{0,0},{1,3},{2,2},{3,1},{4,4},{5,7},{6,6},{7,5},{8,8},{9,11},{10,1... | collective-permute-start | bytes 196616 | tf_op jit(solution)/shard_map/ppermute | solution.py:222
  35.0 5.4 %collective-permute-start.13 = (bf16[32,512]{1,0:T(8,128)(2,1)S(1)}, bf16[32,512]{1,0:T(8,128)(2,1)S(1)}, u32[]{:S(2)}, u32[]{:S(2)}) collective-permute-start(bf16[32,512]{1,0:T(8,128)(2,1)S(1)} %slice.12), channel_id=1, source_target_pairs={{0,1},{1,0},{2,3},{3,2},{4,5},{5,4},{6,7},{7,6},{8,9},{9,8},{10,11... | collective-permute-start | bytes 98312 | tf_op jit(solution)/shard_map/ppermute | solution.py:217
  38.6 1.8 %collective-permute-start.15 = (bf16[32,512]{1,0:T(8,128)(2,1)S(1)}, bf16[32,512]{1,0:T(8,128)(2,1)S(1)}, u32[]{:S(2)}, u32[]{:S(2)}) collective-permute-start(bf16[32,512]{1,0:T(8,128)(2,1)S(1)} %slice.16), channel_id=1, source_target_pairs={{0,1},{1,0},{2,3},{3,2},{4,5},{5,4},{6,7},{7,6},{8,9},{9,8},{10,11... | collective-permute-start | bytes 98312 | tf_op jit(solution)/shard_map/ppermute | solution.py:217
  39.9 1.2 %collective-permute-start.17 = (bf16[32,512]{1,0:T(8,128)(2,1)S(1)}, bf16[32,512]{1,0:T(8,128)(2,1)S(1)}, u32[]{:S(2)}, u32[]{:S(2)}) collective-permute-start(bf16[32,512]{1,0:T(8,128)(2,1)S(1)} %slice.17), channel_id=1, source_target_pairs={{0,1},{1,0},{2,3},{3,2},{4,5},{5,4},{6,7},{7,6},{8,9},{9,8},{10,11... | collective-permute-start | bytes 98312 | tf_op jit(solution)/shard_map/ppermute | solution.py:217
  40.0 1.2 %collective-permute-start.19 = (bf16[32,512]{1,0:T(8,128)(2,1)S(1)}, bf16[32,512]{1,0:T(8,128)(2,1)S(1)}, u32[]{:S(2)}, u32[]{:S(2)}) collective-permute-start(bf16[32,512]{1,0:T(8,128)(2,1)S(1)} %slice.18), channel_id=1, source_target_pairs={{0,1},{1,0},{2,3},{3,2},{4,5},{5,4},{6,7},{7,6},{8,9},{9,8},{10,11... | collective-permute-start | bytes 98312 | tf_op jit(solution)/shard_map/ppermute | solution.py:217

commit v10 on v8

--- a/solution.py
+++ b/solution.py
@@ -46,8 +46,15 @@
     return (rows * lax.rsqrt(mean_square + EPS) * gain).astype(jnp.bfloat16)
 
 
+def core_of(distance):
+    parity = distance
+    for shift in (16, 8, 4, 2, 1):
+        parity = parity ^ (parity >> shift)
+    return parity & 1
+
+
 def position(distance, serve, owners):
-    return jnp.where(distance % 2 == serve, 0, owners // 2) + distance // 2
+    return jnp.where(core_of(distance) == serve, 0, owners // 2) + distance // 2
 
 
 def own_slots(sess_ref, req_count):
@@ -63,54 +70,78 @@
     return slots
 
 
-def message_kernel(sess_ref, own_ref, other_ref, *refs):
-    *out_refs, table_ref = refs
-    req_count, half_cands, _ = own_ref.shape
-    serve = lax.axis_index("serve")
-    messages = len(out_refs)
-    unused = 2 * messages * CAP
-    for at in range(2 * messages * CAP):
-        table_ref[at] = jnp.zeros_like(table_ref[at])
-    for request, (distance, place) in enumerate(own_slots(sess_ref, req_count)):
-        ours = distance % 2 == serve
-        for side, rows_ref in enumerate((own_ref, other_ref)):
-            at = (distance // 2 * 2 + side) * CAP + place
-            table_ref[jnp.where(ours, at, unused + side)] = rows_ref[request].astype(jnp.float32)
-    for at, out_ref in enumerate(out_refs):
-        rows = table_ref[2 * CAP * at : 2 * CAP * (at + 1)]
-        out_ref[...] = rows.reshape(out_ref.shape).astype(jnp.bfloat16)
-
-
-def visible_kernel(sess_ref, len_ref, mask_ref, hide_rows_ref, hide_cols_ref, marks_ref):
-    me = lax.axis_index("cache")
+def front_kernel(
+    sess_hbm, len_hbm, mask_hbm, cand_hbm,
+    hide_rows_ref, hide_cols_ref, chosen_ref, own_ref,
+    sess_ref, len_ref, mask_ref, marks_ref, sems,
+):
+    copies = [
+        pltpu.make_async_copy(source, target, sems.at[at])
+        for at, (source, target) in enumerate(
+            ((sess_hbm, sess_ref), (len_hbm, len_ref), (mask_hbm, mask_ref), (cand_hbm, own_ref))
+        )
+    ]
+    for copy in copies:
+        copy.start()
+    me, serve = lax.axis_index("cache"), lax.axis_index("serve")
     blocks, requests = mask_ref.shape
-    owners = len_ref.shape[0]
+    owners = len_ref.shape[1]
     per_owner = requests // owners
+    half_cands = own_ref.shape[1]
+    rows = per_owner * half_cands
+    hist_rows = hide_cols_ref.shape[0]
+    at_row = lax.broadcasted_iota(jnp.int32, (hist_rows, HD), 0)
+    at_lane = lax.broadcasted_iota(jnp.int32, (hist_rows, HD), 1)
+    in_block = at_lane == at_row // BLK
+    marks_ref[...] = jnp.zeros_like(marks_ref)
+    for copy in copies[:3]:
+        copy.wait()
+
     sessions = sess_ref[...]
     lane = lax.broadcasted_iota(jnp.int32, (1, requests), 1)
     place = jnp.zeros((1, requests), jnp.int32)
     for back in range(1, per_owner):
         same = (pltpu.roll(sessions, back, 1) == sessions) & (lane % per_owner >= back)
         place = place + same.astype(jnp.int32)
-    at = position((lane // per_owner) ^ me, lax.axis_index("serve"), owners)
+
+    distance = sessions ^ me
+    code = jnp.where(core_of(distance) == serve, (distance // 2) * (2 * CAP) + place, owners * CAP)
+    request = lax.broadcasted_iota(jnp.int32, (requests, 2 * rows), 0)
+    column = lax.broadcasted_iota(jnp.int32, (requests, 2 * rows), 1)
+    spread = (request == me * per_owner + (column % rows) // half_cands).astype(jnp.float32).astype(jnp.bfloat16)
+    codes = jnp.broadcast_to(code, (8, requests)).astype(jnp.float32).astype(jnp.bfloat16)
+    target = jnp.dot(codes, spread, preferred_element_type=jnp.float32)[:1].astype(jnp.int32)
+    at = lax.broadcasted_iota(jnp.int32, chosen_ref.shape, 0)
+    column = lax.broadcasted_iota(jnp.int32, chosen_ref.shape, 1)
+    hit = (at // half_cands == target + (column // rows) * CAP) & (at % half_cands == column % half_cands)
+    chosen_ref[...] = hit.astype(jnp.float32).astype(jnp.bfloat16)
+
+    at = position((lane // per_owner) ^ me, serve, owners)
     slot_of = jnp.where(sessions == me, at * CAP + place, -1)
     slots = owners * CAP
     at_slot = lax.broadcasted_iota(jnp.int32, (slots, requests), 0)
-    chosen = (at_slot == slot_of).astype(jnp.float32).astype(jnp.bfloat16)
-    marks_ref[...] = jnp.zeros_like(marks_ref)
+    taken = (at_slot == slot_of).astype(jnp.float32).astype(jnp.bfloat16)
     marks_ref[:blocks, :] = mask_ref[...].astype(jnp.float32).astype(jnp.bfloat16)
-    seen = lax.dot_general(chosen, marks_ref[...], (((1,), (1,)), ((), ())), preferred_element_type=jnp.float32)
-    at_lane = lax.broadcasted_iota(jnp.int32, (slots, HD), 1)
-    hidden = jnp.where(at_lane < blocks, (1.0 - seen) * HIDE, jnp.where(at_lane == blocks, HIDE, 0.0))
-    half = hide_rows_ref.shape[0] // slots // 2
-    spread = jnp.broadcast_to(hidden.reshape(owners, 1, CAP, 1, HD), (owners, 2, CAP, half, HD))
-    hide_rows_ref[...] = spread.reshape(hide_rows_ref.shape).astype(jnp.bfloat16)
-    hist_rows = hide_cols_ref.shape[0]
-    at_row = lax.broadcasted_iota(jnp.int32, (hist_rows, HD), 0)
-    at_lane = lax.broadcasted_iota(jnp.int32, (hist_rows, HD), 1)
-    hide_cols_ref[...] = jnp.where(
-        (at_lane == at_row // BLK) | ((at_lane == blocks) & (at_row >= len_ref[me])), 1.0, 0.0
+    seen = lax.dot_general(taken, marks_ref[...], (((1,), (1,)), ((), ())), preferred_element_type=jnp.float32)
+    slot_lane = lax.broadcasted_iota(jnp.int32, (slots, HD), 1)
+    hidden = jnp.where(slot_lane < blocks, (1.0 - seen) * HIDE, jnp.where(slot_lane == blocks, HIDE, 0.0))
+    wide = jnp.broadcast_to(hidden.reshape(owners, 1, CAP, 1, HD), (owners, 2, CAP, half_cands, HD))
+    hide_rows_ref[...] = wide.reshape(hide_rows_ref.shape).astype(jnp.bfloat16)
+    owner_lane = lax.broadcasted_iota(jnp.int32, (1, owners), 1)
+    length = jnp.sum(jnp.where(owner_lane == me, len_ref[...], 0), axis=1, keepdims=True)
+    hide_cols_ref[...] = jnp.where(in_block | ((at_lane == blocks) & (at_row >= length)), 1.0, 0.0).astype(jnp.bfloat16)
+    copies[3].wait()
+
+
+def message_kernel(chosen_ref, own_ref, other_ref, *out_refs):
+    model_width = own_ref.shape[2]
+    source = jnp.concatenate(
+        [ref[...].astype(jnp.float32).reshape(-1, model_width) for ref in (own_ref, other_ref)], axis=0
     ).astype(jnp.bfloat16)
+    rows = jnp.dot(chosen_ref[...], source, preferred_element_type=jnp.float32)
+    piece = out_refs[0].shape[0]
+    for at, out_ref in enumerate(out_refs):
+        out_ref[...] = rows[at * piece : (at + 1) * piece].astype(jnp.bfloat16)
 
 
 def self_kernel(own_ref, other_ref, gain_ref, w_ref, keep_ref, give_ref, normed_ref):
@@ -196,7 +227,7 @@
     for heads, (terms_ref, w_ref) in enumerate(((keep_ref, w_own_ref), (got_ref, w_other_ref))):
         history = []
         for distance, place in own:
-            side = jnp.where(distance % 2 == serve, 0, messages)
+            side = jnp.where(core_of(distance) == serve, 0, messages)
             history.append(table_ref[((side + distance // 2) * 2 + heads) * CAP + place])
         attended = jnp.concatenate(history, axis=0) + terms_ref[0].astype(jnp.float32)
         gates = terms_ref[1].astype(jnp.float32)
@@ -220,9 +251,8 @@
 def cross(owners, messages):
     came = []
     for at in far_first(len(messages)):
-        pairs = [
-            (place * 2 + core, (place ^ (2 * at + core)) * 2 + core) for place in range(owners) for core in range(2)
-        ]
+        steps = [2 * at + side for side in range(2)]
+        pairs = [(place * 2 + core_of(step), (place ^ step) * 2 + core_of(step)) for place in range(owners) for step in steps]
         came.append(lax.ppermute(messages[at], ("cache", "serve"), pairs))
     return came
 
@@ -240,25 +270,41 @@
     piece = 2 * CAP * half_cands
     half_table = bf16((messages * piece, width))
 
-    other, w_out = lax.optimization_barrier((swap(candidates), w_out))
+    hbm = pl.BlockSpec(memory_space=pltpu.HBM)
+    hide_rows, hide_cols, chosen, own = kernel_call(
+        front_kernel,
+        [
+            bf16((owners * piece, HD)),
+            bf16((hist_rows, HD)),
+            bf16((messages * piece, 2 * rows)),
+            bf16(candidates.shape),
+        ],
+        [hbm] * 4,
+        [
+            pltpu.VMEM((1, owners * req_count), jnp.int32),
+            pltpu.VMEM((1, owners), jnp.int32),
+            pltpu.VMEM(block_mask.shape[::-1], jnp.int32),
+            pltpu.VMEM((HD, owners * req_count), jnp.bfloat16),
+            pltpu.SemaphoreType.DMA((4,)),
+        ],
+    )(request_session.reshape(1, -1), hist_len.reshape(1, -1), block_mask.T, candidates)
+    other, w_out, own = lax.optimization_barrier((swap(candidates), w_out, own))
     w_other = swap(w_out)
-    out = kernel_call(
-        message_kernel,
-        [bf16((piece, model_width))] * messages,
-        [smem, vmem, vmem],
-        [pltpu.VMEM((2 * messages * CAP + 2, half_cands, model_width), jnp.float32)],
-    )(sessions, candidates, other)
+    out = kernel_call(message_kernel, [bf16((piece, model_width))] * messages, [vmem] * 3)(chosen, own, other)
     out, w_in = lax.optimization_barrier((out, w_in))
     weights = jnp.transpose(w_in, (1, 0, 2))
     came = cross(owners, out)
-    visible = kernel_call(
-        visible_kernel,
-        [bf16((owners * piece, HD)), bf16((hist_rows, HD))],
-        [vmem, smem, vmem],
-        [pltpu.VMEM((HD, owners * req_count), jnp.bfloat16)],
-    )(request_session.reshape(1, -1), hist_len, block_mask.T)
-    came, weights, (hide_rows, hide_cols) = lax.optimization_barrier((came, weights, visible))
+    terms = kernel_call(
+        self_kernel,
+        [bf16((2, rows, width))] * 2,
+        [vmem] * 4,
+        [pltpu.VMEM((2 * rows, model_width), jnp.bfloat16)],
+        flops=16 * rows * model_width * width,
+        moved=8 * model_width * width,
+    )(own, other, gain, weights)
+    came, weights, (keep_terms, give_terms) = lax.optimization_barrier((came, weights, terms))
     swapped = [swap(message) for message in came]
+    got_terms = swap(give_terms)
     keep, give = kernel_call(
         functools.partial(history_kernel, owners),
         [half_table] * 2,
@@ -274,20 +320,9 @@
         hist_values.reshape(hist_rows, width),
         *[rows_of for both in zip(came, swapped) for rows_of in both],
     )
-    out = kernel_call(pack_kernel, [bf16((2 * piece, width))] * messages, [vmem] * 2)(keep, swap(give))
-    out, other = lax.optimization_barrier((out, other))
-    backs = cross(owners, out)
-    keep, give = kernel_call(
-        self_kernel,
-        [bf16((2, rows, width))] * 2,
-        [vmem] * 4,
-        [pltpu.VMEM((2 * rows, model_width), jnp.bfloat16)],
-        flops=16 * rows * model_width * width,
-        moved=8 * model_width * width,
-    )(candidates, other, gain, weights)
-    backs, keep, give = lax.optimization_barrier((backs, keep, give))
-    got = swap(give)
-    returned = [(back, swap(back[piece:])) for back in backs]
+    keep, give, got_terms, w_other = lax.optimization_barrier((keep, give, got_terms, w_other))
+    backs = cross(owners, kernel_call(pack_kernel, [bf16((2 * piece, width))] * messages, [vmem] * 2)(keep, swap(give)))
+    returned = [rows_of for back in backs for rows_of in (back, swap(back[piece:]))]
     return kernel_call(
         functools.partial(output_kernel, messages),
         bf16((req_count, half_cands, model_width)),
@@ -295,7 +330,7 @@
         [pltpu.VMEM((4 * messages * CAP, half_cands, width), jnp.float32)],
         flops=8 * rows * model_width * width,
         moved=4 * model_width * width,
-    )(sessions, candidates, keep, got, w_out, w_other, *[rows_of for both in returned for rows_of in both])
+    )(sessions, own, keep_terms, got_terms, w_out, w_other, *returned)
 
 
 def solution(mesh):

time: 41.6 us -> 39.2 us (0.942)
  waiting for transfers between devices: 8.87 us -> 7.62 us
  starting transfers between devices: 17.7 us -> 16.7 us
  Pallas kernels: 8.36 us -> 7.76 us
  local copies, waits for them, and re-layouts: 6.16 us -> 6.67 us
    ppermute x12, starting transfers between devices: 6.54 us -> 3.4 us  [swap(): return lax.ppermute(rows, 'serve', [(0, 1), (1, 0)])]
    ppermute x8, starting transfers between devices: 11.2 us -> 13.3 us  [cross(): came.append(lax.ppermute(messages[at], ('cache', 'serve'), pairs))]
    ppermute x12, waiting for transfers between devices: 5.2 us -> 3.11 us  [swap(): return lax.ppermute(rows, 'serve', [(0, 1), (1, 0)])]
    ppermute x8, waiting for transfers between devices: 3.67 us -> 4.5 us  [cross(): came.append(lax.ppermute(messages[at], ('cache', 'serve'), pairs))]
    reshape x1, local copies, waits for them, and re-layouts: 0.01 us -> 0.69 us  [body(): gain = input_gain.reshape(1, -1)]
    pallas_call x2, Pallas kernels: 2.02 us -> 1.39 us  [the longest x1 1.18 us: body(): kernel_call(front_kernel, [bf16((owners * piece, HD)), bf16((hist_rows, H...]
    unnamed x20 -> x16, local copies, waits for them, and re-layouts: 2.96 us -> 2.95 us
  transfers between devices with their start and end apart: 20 -> 20, of which waited for: 11 -> 10; matrix products, arithmetic and copies ran while one was open for 8% -> 10% of each run, Pallas kernels for 16% -> 15%
where the time goes in v10:
time: 39.2 us; the launch traced here: 38.9 us
  starting transfers between devices  16.7 us (43%)
  Pallas kernels  7.76 us (20%)
  waiting for transfers between devices  7.62 us (19%)
  local copies, waits for them, and re-layouts  6.67 us (17%)
    ppermute x8, starting transfers between devices, cross(): came.append(lax.ppermute(messages[at], ('cache', 'serve'), pairs))  13.3 us
    ppermute x8, waiting for transfers between devices, cross(): came.append(lax.ppermute(messages[at], ('cache', 'serve'), pairs))  4.5 us
    pallas_call x1, Pallas kernels, body(): kernel_call(functools.partial(history_kernel, owners), [half_table] * 2,...  3.65 us
    ppermute x12, starting transfers between devices, swap(): return lax.ppermute(rows, 'serve', [(0, 1), (1, 0)])  3.4 us
    ppermute x12, waiting for transfers between devices, swap(): return lax.ppermute(rows, 'serve', [(0, 1), (1, 0)])  3.11 us
    optimization_barrier x1, local copies, waits for them, and re-layouts, body(): out, w_in = lax.optimization_barrier((out, w_in))  3.02 us
    unnamed x16, local copies, waits for them, and re-layouts  2.95 us
    pallas_call x1, Pallas kernels, body(): kernel_call(functools.partial(output_kernel, messages), bf16((req_count,...  1.84 us
  transfers between devices with their start and end apart: 20, of which 10 were waited for; matrix products, arithmetic and copies ran while one was open for 10% of the time, Pallas kernels for 15%

profile of v10, /device:TPU:0, one launch (start us, length us, event | category | flops | bytes accessed | tf_op | source)
XLA Modules:
  0.0 38.9 jit_solution(4991011964245562611)
XLA Ops:
  0.0 0.5 %collective-permute-start = (bf16[8,8,1024]{2,1,0:T(8,128)(2,1)}, bf16[8,8,1024]{2,1,0:T(8,128)(2,1)S(1)}, u32[]{:S(2)}, u32[]{:S(2)}) collective-permute-start(bf16[8,8,1024]{2,1,0:T(8,128)(2,1)} %cand_hbm.1), channel_id=1, source_target_pairs={{0,1},{1,0},{2,3},{3,2},{4,5},{5,4},{6,7},{7,6},{8,9},{9,8},{10,11... | collective-permute-start | bytes 393224 | tf_op jit(solution)/shard_map/ppermute | solution.py:248
  0.5 0.0 copy-start.3
  0.5 0.9 %copy-done.3 = bf16[8,8,1024]{2,1,0:T(8,128)(2,1)S(1)} copy-done((bf16[8,8,1024]{2,1,0:T(8,128)(2,1)S(1)}, bf16[8,8,1024]{2,1,0:T(8,128)(2,1)}, u32[]{:S(2)}) %copy-start.3) | copy-done | bytes 131096
  1.4 0.0 copy-start.4
  1.4 0.7 %copy-done.4 = s32[64,32]{0,1:T(8,128)S(1)} copy-done((s32[64,32]{0,1:T(8,128)S(1)}, s32[64,32]{0,1:T(8,128)}, u32[]{:S(2)}) %copy-start.4) | copy-done | bytes 8216
  2.1 0.0 copy-start.5
  2.1 0.7 %copy-done.5 = s32[64,1]{0,1:T(1,128)S(1)} copy-done((s32[64,1]{0,1:T(1,128)S(1)}, s32[64,1]{0,1:T(1,128)}, u32[]{:S(2)}) %copy-start.5) | copy-done | bytes 280
  2.7 0.0 copy-start.7
  2.7 0.7 %copy-done.7 = s32[8]{0:T(128)S(1)} copy-done((s32[8]{0:T(128)S(1)}, s32[8]{0:T(128)}, u32[]{:S(2)}) %copy-start.7) | copy-done | bytes 56
  3.4 1.2 %shard_map.91 = (bf16[256,128]{1,0:T(8,128)(2,1)S(1)}, bf16[2048,128]{1,0:T(8,128)(2,1)S(1)}, bf16[128,128]{1,0:T(8,128)(2,1)S(1)}, bf16[8,8,1024]{2,1,0:T(8,128)(2,1)S(1)}) custom-call(s32[1,64]{1,0:T(1,128)S(1)} %bitcast.14, s32[1,8]{1,0:T(1,128)S(1)} %bitcast.16, s32[32,64]{1,0:T(8,128)S(1)} %bitcast.13, bf16[8,8,1024]{2,1,0:T(8,128)(2,1)S(1)} %copy-done.3), custom_call_target="tpu_custom_call" | custom-call | tf_op jit(solution)/shard_map/pallas_call | solution.py:274
  4.6 0.0 collective-permute-done.other_ref
  4.6 0.1 collective-permute-start.10
  4.7 0.2 shard_map.92
  4.9 5.1 %collective-permute-start.1 = (bf16[32,1024]{1,0:T(8,128)(2,1)S(1)}, bf16[32,1024]{1,0:T(8,128)(2,1)S(1)}, u32[]{:S(2)}, u32[]{:S(2)}) collective-permute-start(bf16[32,1024]{1,0:T(8,128)(2,1)S(1)} %get-tuple-element.48), channel_id=1, source_target_pairs={{0,12},{1,15},{2,14},{3,13},{4,8},{5,11},{6,10},{7,9},{8,4},{9,7},... | collective-permute-start | bytes 196616 | tf_op jit(solution)/shard_map/ppermute | solution.py:256
  10.0 0.4 %collective-permute-start.2 = (bf16[32,1024]{1,0:T(8,128)(2,1)S(1)}, bf16[32,1024]{1,0:T(8,128)(2,1)S(1)}, u32[]{:S(2)}, u32[]{:S(2)}) collective-permute-start(bf16[32,1024]{1,0:T(8,128)(2,1)S(1)} %get-tuple-element.49), channel_id=1, source_target_pairs={{1,9},{0,10},{3,11},{2,8},{5,13},{4,14},{7,15},{6,12},{9,1},{8,2},... | collective-permute-start | bytes 196616 | tf_op jit(solution)/shard_map/ppermute | solution.py:256
  10.4 1.2 %collective-permute-start.3 = (bf16[32,1024]{1,0:T(8,128)(2,1)S(1)}, bf16[32,1024]{1,0:T(8,128)(2,1)S(1)}, u32[]{:S(2)}, u32[]{:S(2)}) collective-permute-start(bf16[32,1024]{1,0:T(8,128)(2,1)S(1)} %get-tuple-element.50), channel_id=1, source_target_pairs={{1,5},{0,6},{3,7},{2,4},{5,1},{4,2},{7,3},{6,0},{9,13},{8,14},{11,... | collective-permute-start | bytes 196616 | tf_op jit(solution)/shard_map/ppermute | solution.py:256
  11.6 0.7 %collective-permute-start.4 = (bf16[32,1024]{1,0:T(8,128)(2,1)S(1)}, bf16[32,1024]{1,0:T(8,128)(2,1)S(1)}, u32[]{:S(2)}, u32[]{:S(2)}) collective-permute-start(bf16[32,1024]{1,0:T(8,128)(2,1)S(1)} %get-tuple-element.51), channel_id=1, source_target_pairs={{0,0},{1,3},{2,2},{3,1},{4,4},{5,7},{6,6},{7,5},{8,8},{9,11},{10,1... | collective-permute-start | bytes 196616 | tf_op jit(solution)/shard_map/ppermute | solution.py:256
  12.2 0.7 %reshape.21.gain_ref = bf16[1,1024]{1,0:T(2,128)(2,1)S(1)} reshape(bf16[1024]{0:T(1024)(128)(2,1)} %param.10) | data formatting | bytes 4096 | tf_op jit(solution)/shard_map/reshape | solution.py:268
  12.9 3.0 %copy.12 = bf16[1024,4,512]{2,0,1:T(8,128)(2,1)S(1)} copy(bf16[1024,4,512]{2,1,0:T(4,128)(2,1)} %param.11) | data formatting | bytes 8388608 | tf_op jit(solution)/shard_map/optimization_barrier | solution.py:294
  16.0 0.0 copy-start
  16.0 0.0 copy-start.1
  16.0 0.9 %shard_map.93 = (bf16[2,64,512]{2,1,0:T(8,128)(2,1)S(1)}, bf16[2,64,512]{2,1,0:T(8,128)(2,1)S(1)}) custom-call(bf16[8,8,1024]{2,1,0:T(8,128)(2,1)S(1)} %get-tuple-element.41.own_ref, bf16[8,8,1024]{2,1,0:T(8,128)(2,1)S(1)} %collective-permute-done.other_ref, bf16[1,1024]{1,0:T(2,128)(2,1)S(1)} %reshape.21.gain_ref, bf16[4,1024,512]{2,1,0:T(8,128)(2,1)S(1)} %bitcast.9), custom_call_target="tpu_custom_call" | custom-call | flops 536870912 | bytes 4194304 | tf_op jit(solution)/shard_map/pallas_call | solution.py:297
  16.9 0.0 collective-permute-done.1.refs_0_
  16.9 0.1 collective-permute-done.2.refs_2_
  16.9 0.0 collective-permute-done.3.refs_4_
  17.0 0.0 collective-permute-done.4.refs_6_
  17.0 1.0 %collective-permute-start.5 = (bf16[32,1024]{1,0:T(8,128)(2,1)S(1)}, bf16[32,1024]{1,0:T(8,128)(2,1)S(1)}, u32[]{:S(2)}, u32[]{:S(2)}) collective-permute-start(bf16[32,1024]{1,0:T(8,128)(2,1)S(1)} %collective-permute-done.1.refs_0_), channel_id=1, source_target_pairs={{0,1},{1,0},{2,3},{3,2},{4,5},{5,4},{6,7},{7,6},{8,9},{9,8},{10,11... | collective-permute-start | bytes 196616 | tf_op jit(solution)/shard_map/ppermute | solution.py:248
  18.0 0.1 collective-permute-start.6
  18.1 0.4 %collective-permute-start.7 = (bf16[32,1024]{1,0:T(8,128)(2,1)S(1)}, bf16[32,1024]{1,0:T(8,128)(2,1)S(1)}, u32[]{:S(2)}, u32[]{:S(2)}) collective-permute-start(bf16[32,1024]{1,0:T(8,128)(2,1)S(1)} %collective-permute-done.3.refs_4_), channel_id=1, source_target_pairs={{0,1},{1,0},{2,3},{3,2},{4,5},{5,4},{6,7},{7,6},{8,9},{9,8},{10,11... | collective-permute-start | bytes 196616 | tf_op jit(solution)/shard_map/ppermute | solution.py:248
  18.5 0.1 collective-permute-start.8
  18.6 0.3 collective-permute-done.5.refs_1_
  18.9 0.4 collective-permute-start.9
  19.3 0.0 collective-permute-done.6.refs_3_
  19.3 0.2 collective-permute-done.7.refs_5_
  19.4 0.4 collective-permute-done.8.refs_7_
  19.8 0.0 copy-done
  19.8 0.0 copy-done.1
  19.8 0.0 copy-start.2
  19.8 0.0 copy-start.6
  19.8 3.7 %shard_map.94 = (bf16[128,512]{1,0:T(8,128)(2,1)S(1)}, bf16[128,512]{1,0:T(8,128)(2,1)S(1)}) custom-call(bf16[1,1024]{1,0:T(2,128)(2,1)S(1)} %reshape.21.gain_ref, bf16[4,1024,512]{2,1,0:T(8,128)(2,1)S(1)} %bitcast.10, bf16[256,128]{1,0:T(8,128)(2,1)S(1)} %get-tuple-element.57.hide_rows_ref, bf16[2048,128]{1,0:T(8,128)(2,1)S(1)} %get-tuple-element.58.hide_cols_ref, ...), custom_call_target="tpu_custom_call" | custom-call | flops 2147483648 | bytes 4194304 | tf_op jit(solution)/shard_map/pallas_call | solution.py:308
  23.4 0.0 collective-permute-done.9.got_ref
  23.5 0.0 collective-permute-done.10.w_other_ref
  23.5 0.2 collective-permute-start.11
  23.7 1.2 %collective-permute-done.11.got_ref = bf16[128,512]{1,0:T(8,128)(2,1)S(1)} collective-permute-done((bf16[128,512]{1,0:T(8,128)(2,1)S(1)}, bf16[128,512]{1,0:T(8,128)(2,1)S(1)}, u32[]{:S(2)}, u32[]{:S(2)}) %collective-permute-start.11) | collective-permute-done | bytes 131104 | tf_op jit(solution)/shard_map/ppermute | solution.py:248
  24.9 3.5 %collective-permute-start.12 = (bf16[64,512]{1,0:T(8,128)(2,1)S(1)}, bf16[64,512]{1,0:T(8,128)(2,1)S(1)}, u32[]{:S(2)}, u32[]{:S(2)}) collective-permute-start(bf16[64,512]{1,0:T(8,128)(2,1)S(1)} %get-tuple-element.71), channel_id=1, source_target_pairs={{0,12},{1,15},{2,14},{3,13},{4,8},{5,11},{6,10},{7,9},{8,4},{9,7},... | collective-permute-start | bytes 196616 | tf_op jit(solution)/shard_map/ppermute | solution.py:256
  28.4 0.3 collective-permute-start.14
  28.7 1.5 %collective-permute-start.16 = (bf16[64,512]{1,0:T(8,128)(2,1)S(1)}, bf16[64,512]{1,0:T(8,128)(2,1)S(1)}, u32[]{:S(2)}, u32[]{:S(2)}) collective-permute-start(bf16[64,512]{1,0:T(8,128)(2,1)S(1)} %get-tuple-element.73), channel_id=1, source_target_pairs={{1,5},{0,6},{3,7},{2,4},{5,1},{4,2},{7,3},{6,0},{9,13},{8,14},{11,... | collective-permute-start | bytes 196616 | tf_op jit(solution)/shard_map/ppermute | solution.py:256
  30.3 0.7 %collective-permute-start.18 = (bf16[64,512]{1,0:T(8,128)(2,1)S(1)}, bf16[64,512]{1,0:T(8,128)(2,1)S(1)}, u32[]{:S(2)}, u32[]{:S(2)}) collective-permute-start(bf16[64,512]{1,0:T(8,128)(2,1)S(1)} %get-tuple-element.74), channel_id=1, source_target_pairs={{0,0},{1,3},{2,2},{3,1},{4,4},{5,7},{6,6},{7,5},{8,8},{9,11},{10,1... | collective-permute-start | bytes 196616 | tf_op jit(solution)/shard_map/ppermute | solution.py:256
  30.9 0.9 %collective-permute-done.12.refs_0_ = bf16[64,512]{1,0:T(8,128)(2,1)S(1)} collective-permute-done((bf16[64,512]{1,0:T(8,128)(2,1)S(1)}, bf16[64,512]{1,0:T(8,128)(2,1)S(1)}, u32[]{:S(2)}, u32[]{:S(2)}) %collective-permute-start.12) | collective-permute-done | bytes 65568 | tf_op jit(solution)/shard_map/ppermute | solution.py:256
  31.8 0.0 collective-permute-start.13
  31.9 3.5 %collective-permute-done.14.refs_2_ = bf16[64,512]{1,0:T(8,128)(2,1)S(1)} collective-permute-done((bf16[64,512]{1,0:T(8,128)(2,1)S(1)}, bf16[64,512]{1,0:T(8,128)(2,1)S(1)}, u32[]{:S(2)}, u32[]{:S(2)}) %collective-permute-start.14) | collective-permute-done | bytes 65568 | tf_op jit(solution)/shard_map/ppermute | solution.py:256
  35.3 0.0 collective-permute-start.15
  35.3 0.0 collective-permute-done.16.refs_4_
  35.3 0.5 %collective-permute-start.17 = (bf16[32,512]{1,0:T(8,128)(2,1)S(1)}, bf16[32,512]{1,0:T(8,128)(2,1)S(1)}, u32[]{:S(2)}, u32[]{:S(2)}) collective-permute-start(bf16[32,512]{1,0:T(8,128)(2,1)S(1)} %slice.18), channel_id=1, source_target_pairs={{0,1},{1,0},{2,3},{3,2},{4,5},{5,4},{6,7},{7,6},{8,9},{9,8},{10,11... | collective-permute-start | bytes 98312 | tf_op jit(solution)/shard_map/ppermute | solution.py:248
  35.8 0.0 collective-permute-done.18.refs_6_
  35.9 0.1 collective-permute-start.19
  36.0 0.0 collective-permute-done.13.refs_1_
  36.0 0.6 %collective-permute-done.15.refs_3_ = bf16[32,512]{1,0:T(8,128)(2,1)S(1)} collective-permute-done((bf16[32,512]{1,0:T(8,128)(2,1)S(1)}, bf16[32,512]{1,0:T(8,128)(2,1)S(1)}, u32[]{:S(2)}, u32[]{:S(2)}) %collective-permute-start.15) | collective-permute-done | bytes 32800 | tf_op jit(solution)/shard_map/ppermute | solution.py:248
  36.5 0.2 collective-permute-done.17.refs_5_
  36.7 0.4 collective-permute-done.19.refs_7_
  37.1 0.0 copy-done.2
  37.1 0.0 copy-done.6
  37.1 1.8 %shard_map.96 = bf16[8,8,1024]{2,1,0:T(8,128)(2,1)} custom-call(s32[64]{0:T(128)S(1)} %bitcast.15, bf16[8,8,1024]{2,1,0:T(8,128)(2,1)S(1)} %get-tuple-element.41.own_ref, bf16[2,64,512]{2,1,0:T(8,128)(2,1)S(1)} %get-tuple-element.55.keep_ref, bf16[2,64,512]{2,1,0:T(8,128)(2,1)S(1)} %collective-permute-done.9.got_ref, bf16[512,1024]{1,0:T(8,128)(2,1)S(1)} %copy-done.2, ...), custom_call_target="tpu_custom_call" | custom-call | flops 268435456 | bytes 2097152 | tf_op jit(solution)/shard_map/pallas_call | solution.py:326
  (5 shorter events, 0.0 us)
Async XLA Ops:
  0.0 4.6 %collective-permute-start = (bf16[8,8,1024]{2,1,0:T(8,128)(2,1)}, bf16[8,8,1024]{2,1,0:T(8,128)(2,1)S(1)}, u32[]{:S(2)}, u32[]{:S(2)}) collective-permute-start(bf16[8,8,1024]{2,1,0:T(8,128)(2,1)} %cand_hbm.1), channel_id=1, source_target_pairs={{0,1},{1,0},{2,3},{3,2},{4,5},{5,4},{6,7},{7,6},{8,9},{9,8},{10,11... | collective-permute-start | bytes 393224 | tf_op jit(solution)/shard_map/ppermute | solution.py:248
  0.5 0.9 %copy-start.3 = (bf16[8,8,1024]{2,1,0:T(8,128)(2,1)S(1)}, bf16[8,8,1024]{2,1,0:T(8,128)(2,1)}, u32[]{:S(2)}) copy-start(bf16[8,8,1024]{2,1,0:T(8,128)(2,1)} %cand_hbm.1) | copy-start | bytes 393220
  1.4 0.7 %copy-start.4 = (s32[64,32]{0,1:T(8,128)S(1)}, s32[64,32]{0,1:T(8,128)}, u32[]{:S(2)}) copy-start(s32[64,32]{0,1:T(8,128)} %param.17) | copy-start | bytes 24580
  2.1 0.7 %copy-start.5 = (s32[64,1]{0,1:T(1,128)S(1)}, s32[64,1]{0,1:T(1,128)}, u32[]{:S(2)}) copy-start(s32[64,1]{0,1:T(1,128)} %param.15) | copy-start | bytes 772
  2.7 0.7 %copy-start.7 = (s32[8]{0:T(128)S(1)}, s32[8]{0:T(128)}, u32[]{:S(2)}) copy-start(s32[8]{0:T(128)} %param.16) | copy-start | bytes 100
  4.6 18.9 %collective-permute-start.10 = (bf16[512,1024]{1,0:T(8,128)(2,1)}, bf16[512,1024]{1,0:T(8,128)(2,1)S(1)}, u32[]{:S(2)}, u32[]{:S(2)}) collective-permute-start(bf16[512,1024]{1,0:T(8,128)(2,1)} %w_own_ref), channel_id=1, source_target_pairs={{0,1},{1,0},{2,3},{3,2},{4,5},{5,4},{6,7},{7,6},{8,9},{9,8},{10,11... | collective-permute-start | bytes 3145736 | tf_op jit(solution)/shard_map/ppermute | solution.py:248
  4.9 11.9 %collective-permute-start.1 = (bf16[32,1024]{1,0:T(8,128)(2,1)S(1)}, bf16[32,1024]{1,0:T(8,128)(2,1)S(1)}, u32[]{:S(2)}, u32[]{:S(2)}) collective-permute-start(bf16[32,1024]{1,0:T(8,128)(2,1)S(1)} %get-tuple-element.48), channel_id=1, source_target_pairs={{0,12},{1,15},{2,14},{3,13},{4,8},{5,11},{6,10},{7,9},{8,4},{9,7},... | collective-permute-start | bytes 196616 | tf_op jit(solution)/shard_map/ppermute | solution.py:256
  10.0 6.9 %collective-permute-start.2 = (bf16[32,1024]{1,0:T(8,128)(2,1)S(1)}, bf16[32,1024]{1,0:T(8,128)(2,1)S(1)}, u32[]{:S(2)}, u32[]{:S(2)}) collective-permute-start(bf16[32,1024]{1,0:T(8,128)(2,1)S(1)} %get-tuple-element.49), channel_id=1, source_target_pairs={{1,9},{0,10},{3,11},{2,8},{5,13},{4,14},{7,15},{6,12},{9,1},{8,2},... | collective-permute-start | bytes 196616 | tf_op jit(solution)/shard_map/ppermute | solution.py:256
  10.4 6.5 %collective-permute-start.3 = (bf16[32,1024]{1,0:T(8,128)(2,1)S(1)}, bf16[32,1024]{1,0:T(8,128)(2,1)S(1)}, u32[]{:S(2)}, u32[]{:S(2)}) collective-permute-start(bf16[32,1024]{1,0:T(8,128)(2,1)S(1)} %get-tuple-element.50), channel_id=1, source_target_pairs={{1,5},{0,6},{3,7},{2,4},{5,1},{4,2},{7,3},{6,0},{9,13},{8,14},{11,... | collective-permute-start | bytes 196616 | tf_op jit(solution)/shard_map/ppermute | solution.py:256
  11.6 5.4 %collective-permute-start.4 = (bf16[32,1024]{1,0:T(8,128)(2,1)S(1)}, bf16[32,1024]{1,0:T(8,128)(2,1)S(1)}, u32[]{:S(2)}, u32[]{:S(2)}) collective-permute-start(bf16[32,1024]{1,0:T(8,128)(2,1)S(1)} %get-tuple-element.51), channel_id=1, source_target_pairs={{0,0},{1,3},{2,2},{3,1},{4,4},{5,7},{6,6},{7,5},{8,8},{9,11},{10,1... | collective-permute-start | bytes 196616 | tf_op jit(solution)/shard_map/ppermute | solution.py:256
  16.0 3.8 %copy-start = (bf16[1,2048,512]{2,1,0:T(8,128)(2,1)S(1)}, bf16[1,2048,512]{2,1,0:T(8,128)(2,1)}, u32[]{:S(2)}) copy-start(bf16[1,2048,512]{2,1,0:T(8,128)(2,1)} %param.13) | copy-start | bytes 6291460
  16.0 3.8 %copy-start.1 = (bf16[1,2048,512]{2,1,0:T(8,128)(2,1)S(1)}, bf16[1,2048,512]{2,1,0:T(8,128)(2,1)}, u32[]{:S(2)}) copy-start(bf16[1,2048,512]{2,1,0:T(8,128)(2,1)} %param.14) | copy-start | bytes 6291460
  17.0 1.9 %collective-permute-start.5 = (bf16[32,1024]{1,0:T(8,128)(2,1)S(1)}, bf16[32,1024]{1,0:T(8,128)(2,1)S(1)}, u32[]{:S(2)}, u32[]{:S(2)}) collective-permute-start(bf16[32,1024]{1,0:T(8,128)(2,1)S(1)} %collective-permute-done.1.refs_0_), channel_id=1, source_target_pairs={{0,1},{1,0},{2,3},{3,2},{4,5},{5,4},{6,7},{7,6},{8,9},{9,8},{10,11... | collective-permute-start | bytes 196616 | tf_op jit(solution)/shard_map/ppermute | solution.py:248
  18.0 1.3 %collective-permute-start.6 = (bf16[32,1024]{1,0:T(8,128)(2,1)S(1)}, bf16[32,1024]{1,0:T(8,128)(2,1)S(1)}, u32[]{:S(2)}, u32[]{:S(2)}) collective-permute-start(bf16[32,1024]{1,0:T(8,128)(2,1)S(1)} %collective-permute-done.2.refs_2_), channel_id=1, source_target_pairs={{0,1},{1,0},{2,3},{3,2},{4,5},{5,4},{6,7},{7,6},{8,9},{9,8},{10,11... | collective-permute-start | bytes 196616 | tf_op jit(solution)/shard_map/ppermute | solution.py:248
  18.1 1.3 %collective-permute-start.7 = (bf16[32,1024]{1,0:T(8,128)(2,1)S(1)}, bf16[32,1024]{1,0:T(8,128)(2,1)S(1)}, u32[]{:S(2)}, u32[]{:S(2)}) collective-permute-start(bf16[32,1024]{1,0:T(8,128)(2,1)S(1)} %collective-permute-done.3.refs_4_), channel_id=1, source_target_pairs={{0,1},{1,0},{2,3},{3,2},{4,5},{5,4},{6,7},{7,6},{8,9},{9,8},{10,11... | collective-permute-start | bytes 196616 | tf_op jit(solution)/shard_map/ppermute | solution.py:248
  18.5 1.3 %collective-permute-start.8 = (bf16[32,1024]{1,0:T(8,128)(2,1)S(1)}, bf16[32,1024]{1,0:T(8,128)(2,1)S(1)}, u32[]{:S(2)}, u32[]{:S(2)}) collective-permute-start(bf16[32,1024]{1,0:T(8,128)(2,1)S(1)} %collective-permute-done.4.refs_6_), channel_id=1, source_target_pairs={{0,1},{1,0},{2,3},{3,2},{4,5},{5,4},{6,7},{7,6},{8,9},{9,8},{10,11... | collective-permute-start | bytes 196616 | tf_op jit(solution)/shard_map/ppermute | solution.py:248
  18.9 4.5 %collective-permute-start.9 = (bf16[2,64,512]{2,1,0:T(8,128)(2,1)S(1)}, bf16[2,64,512]{2,1,0:T(8,128)(2,1)S(1)}, u32[]{:S(2)}, u32[]{:S(2)}) collective-permute-start(bf16[2,64,512]{2,1,0:T(8,128)(2,1)S(1)} %get-tuple-element.65), channel_id=1, source_target_pairs={{0,1},{1,0},{2,3},{3,2},{4,5},{5,4},{6,7},{7,6},{8,9},{9,8},{10,11... | collective-permute-start | bytes 393224 | tf_op jit(solution)/shard_map/ppermute | solution.py:248
  19.8 17.3 %copy-start.2 = (bf16[512,1024]{1,0:T(8,128)(2,1)S(1)}, bf16[512,1024]{1,0:T(8,128)(2,1)}, u32[]{:S(2)}) copy-start(bf16[512,1024]{1,0:T(8,128)(2,1)} %w_own_ref) | copy-start | bytes 3145732
  19.8 17.3 %copy-start.6 = (s32[64,1]{0,1:T(1,128)S(1)}, s32[64,1]{0,1:T(1,128)}, u32[]{:S(2)}) copy-start(s32[64,1]{0,1:T(1,128)} %param.15) | copy-start | bytes 772
  23.5 1.4 %collective-permute-start.11 = (bf16[128,512]{1,0:T(8,128)(2,1)S(1)}, bf16[128,512]{1,0:T(8,128)(2,1)S(1)}, u32[]{:S(2)}, u32[]{:S(2)}) collective-permute-start(bf16[128,512]{1,0:T(8,128)(2,1)S(1)} %get-tuple-element.70), channel_id=1, source_target_pairs={{0,1},{1,0},{2,3},{3,2},{4,5},{5,4},{6,7},{7,6},{8,9},{9,8},{10,11... | collective-permute-start | bytes 393224 | tf_op jit(solution)/shard_map/ppermute | solution.py:248
  24.9 6.9 %collective-permute-start.12 = (bf16[64,512]{1,0:T(8,128)(2,1)S(1)}, bf16[64,512]{1,0:T(8,128)(2,1)S(1)}, u32[]{:S(2)}, u32[]{:S(2)}) collective-permute-start(bf16[64,512]{1,0:T(8,128)(2,1)S(1)} %get-tuple-element.71), channel_id=1, source_target_pairs={{0,12},{1,15},{2,14},{3,13},{4,8},{5,11},{6,10},{7,9},{8,4},{9,7},... | collective-permute-start | bytes 196616 | tf_op jit(solution)/shard_map/ppermute | solution.py:256
  28.4 6.9 %collective-permute-start.14 = (bf16[64,512]{1,0:T(8,128)(2,1)S(1)}, bf16[64,512]{1,0:T(8,128)(2,1)S(1)}, u32[]{:S(2)}, u32[]{:S(2)}) collective-permute-start(bf16[64,512]{1,0:T(8,128)(2,1)S(1)} %get-tuple-element.72), channel_id=1, source_target_pairs={{1,9},{0,10},{3,11},{2,8},{5,13},{4,14},{7,15},{6,12},{9,1},{8,2},... | collective-permute-start | bytes 196616 | tf_op jit(solution)/shard_map/ppermute | solution.py:256
  28.7 6.6 %collective-permute-start.16 = (bf16[64,512]{1,0:T(8,128)(2,1)S(1)}, bf16[64,512]{1,0:T(8,128)(2,1)S(1)}, u32[]{:S(2)}, u32[]{:S(2)}) collective-permute-start(bf16[64,512]{1,0:T(8,128)(2,1)S(1)} %get-tuple-element.73), channel_id=1, source_target_pairs={{1,5},{0,6},{3,7},{2,4},{5,1},{4,2},{7,3},{6,0},{9,13},{8,14},{11,... | collective-permute-start | bytes 196616 | tf_op jit(solution)/shard_map/ppermute | solution.py:256
  30.3 5.6 %collective-permute-start.18 = (bf16[64,512]{1,0:T(8,128)(2,1)S(1)}, bf16[64,512]{1,0:T(8,128)(2,1)S(1)}, u32[]{:S(2)}, u32[]{:S(2)}) collective-permute-start(bf16[64,512]{1,0:T(8,128)(2,1)S(1)} %get-tuple-element.74), channel_id=1, source_target_pairs={{0,0},{1,3},{2,2},{3,1},{4,4},{5,7},{6,6},{7,5},{8,8},{9,11},{10,1... | collective-permute-start | bytes 196616 | tf_op jit(solution)/shard_map/ppermute | solution.py:256
  31.8 4.1 %collective-permute-start.13 = (bf16[32,512]{1,0:T(8,128)(2,1)S(1)}, bf16[32,512]{1,0:T(8,128)(2,1)S(1)}, u32[]{:S(2)}, u32[]{:S(2)}) collective-permute-start(bf16[32,512]{1,0:T(8,128)(2,1)S(1)} %slice.16), channel_id=1, source_target_pairs={{0,1},{1,0},{2,3},{3,2},{4,5},{5,4},{6,7},{7,6},{8,9},{9,8},{10,11... | collective-permute-start | bytes 98312 | tf_op jit(solution)/shard_map/ppermute | solution.py:248
  35.3 1.2 %collective-permute-start.15 = (bf16[32,512]{1,0:T(8,128)(2,1)S(1)}, bf16[32,512]{1,0:T(8,128)(2,1)S(1)}, u32[]{:S(2)}, u32[]{:S(2)}) collective-permute-start(bf16[32,512]{1,0:T(8,128)(2,1)S(1)} %slice.17), channel_id=1, source_target_pairs={{0,1},{1,0},{2,3},{3,2},{4,5},{5,4},{6,7},{7,6},{8,9},{9,8},{10,11... | collective-permute-start | bytes 98312 | tf_op jit(solution)/shard_map/ppermute | solution.py:248
  35.3 1.4 %collective-permute-start.17 = (bf16[32,512]{1,0:T(8,128)(2,1)S(1)}, bf16[32,512]{1,0:T(8,128)(2,1)S(1)}, u32[]{:S(2)}, u32[]{:S(2)}) collective-permute-start(bf16[32,512]{1,0:T(8,128)(2,1)S(1)} %slice.18), channel_id=1, source_target_pairs={{0,1},{1,0},{2,3},{3,2},{4,5},{5,4},{6,7},{7,6},{8,9},{9,8},{10,11... | collective-permute-start | bytes 98312 | tf_op jit(solution)/shard_map/ppermute | solution.py:248
  35.9 1.2 %collective-permute-start.19 = (bf16[32,512]{1,0:T(8,128)(2,1)S(1)}, bf16[32,512]{1,0:T(8,128)(2,1)S(1)}, u32[]{:S(2)}, u32[]{:S(2)}) collective-permute-start(bf16[32,512]{1,0:T(8,128)(2,1)S(1)} %slice.19), channel_id=1, source_target_pairs={{0,1},{1,0},{2,3},{3,2},{4,5},{5,4},{6,7},{7,6},{8,9},{9,8},{10,11... | collective-permute-start | bytes 98312 | tf_op jit(solution)/shard_map/ppermute | solution.py:248

commit v11 on v10

--- a/solution.py
+++ b/solution.py
@@ -37,6 +37,11 @@
         cost_estimate=pl.CostEstimate(flops=flops, bytes_accessed=moved, transcendentals=0),
         compiler_params=pltpu.CompilerParams(vmem_limit_bytes=VMEM_LIMIT),
     )
+
+
+def gain_row(gain_ref):
+    gain = gain_ref[...].astype(jnp.float32)
+    return jnp.concatenate([gain[at : at + 1] for at in range(gain.shape[0])], axis=1)
 
 
 def normed_rows(rows_ref, gain):
@@ -70,34 +75,18 @@
     return slots
 
 
-def front_kernel(
-    sess_hbm, len_hbm, mask_hbm, cand_hbm,
-    hide_rows_ref, hide_cols_ref, chosen_ref, own_ref,
-    sess_ref, len_ref, mask_ref, marks_ref, sems,
-):
-    copies = [
-        pltpu.make_async_copy(source, target, sems.at[at])
-        for at, (source, target) in enumerate(
-            ((sess_hbm, sess_ref), (len_hbm, len_ref), (mask_hbm, mask_ref), (cand_hbm, own_ref))
-        )
-    ]
-    for copy in copies:
-        copy.start()
+def front_kernel(owners, half_cands, facts_ref, hide_rows_ref, hide_cols_ref, chosen_ref, marks_ref):
     me, serve = lax.axis_index("cache"), lax.axis_index("serve")
-    blocks, requests = mask_ref.shape
-    owners = len_ref.shape[1]
+    blocks, requests = facts_ref.shape[0] - 2, facts_ref.shape[1]
     per_owner = requests // owners
-    half_cands = own_ref.shape[1]
     rows = per_owner * half_cands
     hist_rows = hide_cols_ref.shape[0]
     at_row = lax.broadcasted_iota(jnp.int32, (hist_rows, HD), 0)
     at_lane = lax.broadcasted_iota(jnp.int32, (hist_rows, HD), 1)
     in_block = at_lane == at_row // BLK
     marks_ref[...] = jnp.zeros_like(marks_ref)
-    for copy in copies[:3]:
-        copy.wait()
-
-    sessions = sess_ref[...]
+
+    sessions = facts_ref[blocks : blocks + 1, :]
     lane = lax.broadcasted_iota(jnp.int32, (1, requests), 1)
     place = jnp.zeros((1, requests), jnp.int32)
     for back in range(1, per_owner):
@@ -121,16 +110,15 @@
     slots = owners * CAP
     at_slot = lax.broadcasted_iota(jnp.int32, (slots, requests), 0)
     taken = (at_slot == slot_of).astype(jnp.float32).astype(jnp.bfloat16)
-    marks_ref[:blocks, :] = mask_ref[...].astype(jnp.float32).astype(jnp.bfloat16)
+    marks_ref[:blocks, :] = facts_ref[:blocks, :].astype(jnp.float32).astype(jnp.bfloat16)
     seen = lax.dot_general(taken, marks_ref[...], (((1,), (1,)), ((), ())), preferred_element_type=jnp.float32)
     slot_lane = lax.broadcasted_iota(jnp.int32, (slots, HD), 1)
     hidden = jnp.where(slot_lane < blocks, (1.0 - seen) * HIDE, jnp.where(slot_lane == blocks, HIDE, 0.0))
     wide = jnp.broadcast_to(hidden.reshape(owners, 1, CAP, 1, HD), (owners, 2, CAP, half_cands, HD))
     hide_rows_ref[...] = wide.reshape(hide_rows_ref.shape).astype(jnp.bfloat16)
-    owner_lane = lax.broadcasted_iota(jnp.int32, (1, owners), 1)
-    length = jnp.sum(jnp.where(owner_lane == me, len_ref[...], 0), axis=1, keepdims=True)
+    lengths = facts_ref[blocks + 1 : blocks + 2, :]
+    length = jnp.sum(jnp.where(lane == me, lengths, 0), axis=1, keepdims=True)
     hide_cols_ref[...] = jnp.where(in_block | ((at_lane == blocks) & (at_row >= length)), 1.0, 0.0).astype(jnp.bfloat16)
-    copies[3].wait()
 
 
 def message_kernel(chosen_ref, own_ref, other_ref, *out_refs):
@@ -146,7 +134,7 @@
 
 def self_kernel(own_ref, other_ref, gain_ref, w_ref, keep_ref, give_ref, normed_ref):
     rows, width = keep_ref.shape[1:]
-    gain = gain_ref[...].astype(jnp.float32)
+    gain = gain_row(gain_ref)
     normed_ref[:rows, :] = normed_rows(own_ref, gain)
     normed_ref[rows:, :] = normed_rows(other_ref, gain)
     normed = normed_ref[...]
@@ -184,7 +172,7 @@
     hist_rows = keys_ref.shape[0]
     span = min(256, hist_rows)
     per_step = max(1, min(owners, 256 // per_owner))
-    gain = gain_ref[...].astype(jnp.float32)
+    gain = gain_row(gain_ref)
     for first in range(0, owners, per_step):
         group = range(first, min(first + per_step, owners))
         normed = jnp.concatenate([normed_rows(slot_refs[at], gain) for at in group], axis=0)
@@ -265,46 +253,35 @@
     hist_rows = hist_keys.shape[1]
     bf16 = functools.partial(jax.ShapeDtypeStruct, dtype=jnp.bfloat16)
     sessions = request_session.reshape(-1)
-    gain = input_gain.reshape(1, -1)
+    gain = input_gain.reshape(-1, HD)
     messages = owners // 2
     piece = 2 * CAP * half_cands
     half_table = bf16((messages * piece, width))
 
-    hbm = pl.BlockSpec(memory_space=pltpu.HBM)
-    hide_rows, hide_cols, chosen, own = kernel_call(
-        front_kernel,
+    facts = jnp.concatenate(
         [
-            bf16((owners * piece, HD)),
-            bf16((hist_rows, HD)),
-            bf16((messages * piece, 2 * rows)),
-            bf16(candidates.shape),
+            block_mask.T,
+            request_session.reshape(1, -1),
+            jnp.pad(hist_len, (0, owners * (req_count - 1))).reshape(1, -1),
         ],
-        [hbm] * 4,
-        [
-            pltpu.VMEM((1, owners * req_count), jnp.int32),
-            pltpu.VMEM((1, owners), jnp.int32),
-            pltpu.VMEM(block_mask.shape[::-1], jnp.int32),
-            pltpu.VMEM((HD, owners * req_count), jnp.bfloat16),
-            pltpu.SemaphoreType.DMA((4,)),
-        ],
-    )(request_session.reshape(1, -1), hist_len.reshape(1, -1), block_mask.T, candidates)
-    other, w_out, own = lax.optimization_barrier((swap(candidates), w_out, own))
+        axis=0,
+    )
+    hide_rows, hide_cols, chosen = kernel_call(
+        functools.partial(front_kernel, owners, half_cands),
+        [bf16((owners * piece, HD)), bf16((hist_rows, HD)), bf16((messages * piece, 2 * rows))],
+        [vmem],
+        [pltpu.VMEM((HD, owners * req_count), jnp.bfloat16)],
+        flops=8 * messages * piece * model_width * width,
+        moved=2 * hist_rows * HD,
+    )(facts)
+    other, w_out, chosen = lax.optimization_barrier((swap(candidates), w_out, chosen))
     w_other = swap(w_out)
-    out = kernel_call(message_kernel, [bf16((piece, model_width))] * messages, [vmem] * 3)(chosen, own, other)
+    out = kernel_call(message_kernel, [bf16((piece, model_width))] * messages, [vmem] * 3)(chosen, candidates, other)
     out, w_in = lax.optimization_barrier((out, w_in))
     weights = jnp.transpose(w_in, (1, 0, 2))
     came = cross(owners, out)
-    terms = kernel_call(
-        self_kernel,
-        [bf16((2, rows, width))] * 2,
-        [vmem] * 4,
-        [pltpu.VMEM((2 * rows, model_width), jnp.bfloat16)],
-        flops=16 * rows * model_width * width,
-        moved=8 * model_width * width,
-    )(own, other, gain, weights)
-    came, weights, (keep_terms, give_terms) = lax.optimization_barrier((came, weights, terms))
+    came, weights = lax.optimization_barrier((came, weights))
     swapped = [swap(message) for message in came]
-    got_terms = swap(give_terms)
     keep, give = kernel_call(
         functools.partial(history_kernel, owners),
         [half_table] * 2,
@@ -320,8 +297,19 @@
         hist_values.reshape(hist_rows, width),
         *[rows_of for both in zip(came, swapped) for rows_of in both],
     )
-    keep, give, got_terms, w_other = lax.optimization_barrier((keep, give, got_terms, w_other))
-    backs = cross(owners, kernel_call(pack_kernel, [bf16((2 * piece, width))] * messages, [vmem] * 2)(keep, swap(give)))
+    keep, give, w_other = lax.optimization_barrier((keep, give, w_other))
+    out = kernel_call(pack_kernel, [bf16((2 * piece, width))] * messages, [vmem] * 2)(keep, swap(give))
+    out, other = lax.optimization_barrier((out, other))
+    backs = cross(owners, out)
+    terms = kernel_call(
+        self_kernel,
+        [bf16((2, rows, width))] * 2,
+        [vmem] * 4,
+        [pltpu.VMEM((2 * rows, model_width), jnp.bfloat16)],
+        flops=16 * rows * model_width * width,
+        moved=8 * model_width * width,
+    )(candidates, other, gain, weights)
+    backs[0], (keep_terms, give_terms) = lax.optimization_barrier((backs[0], terms))
     returned = [rows_of for back in backs for rows_of in (back, swap(back[piece:]))]
     return kernel_call(
         functools.partial(output_kernel, messages),
@@ -330,7 +318,7 @@
         [pltpu.VMEM((4 * messages * CAP, half_cands, width), jnp.float32)],
         flops=8 * rows * model_width * width,
         moved=4 * model_width * width,
-    )(sessions, own, keep_terms, got_terms, w_out, w_other, *returned)
+    )(sessions, candidates, keep_terms, swap(give_terms), w_out, w_other, *returned)
 
 
 def solution(mesh):

time: 39.2 us -> 41.2 us (1.051)
  local copies, waits for them, and re-layouts: 6.67 us -> 4.64 us
  waiting for transfers between devices: 7.62 us -> 9.6 us
  starting transfers between devices: 16.7 us -> 18.3 us
  other arithmetic: 0 us -> 0.74 us
    ppermute x8, waiting for transfers between devices: 4.5 us -> 6.84 us  [cross(): came.append(lax.ppermute(messages[at], ('cache', 'serve'), pairs))]
    unnamed x16 -> x14, local copies, waits for them, and re-layouts: 2.95 us -> 0.94 us
    ppermute x8, starting transfers between devices: 13.3 us -> 14.9 us  [cross(): came.append(lax.ppermute(messages[at], ('cache', 'serve'), pairs))]
    concatenate x0 -> x1, other arithmetic: none -> 0.74 us  [body(): jnp.concatenate([block_mask.T, request_session.reshape(1, -1), jnp.pad(hi...]
  transfers between devices with their start and end apart: 20 -> 20, of which waited for: 10 -> 12; matrix products, arithmetic and copies ran while one was open for 10% -> 11% of each run, Pallas kernels for 15% -> 14%
where the time goes in v11:
time: 41.2 us; the launch traced here: 41 us
  starting transfers between devices  18.3 us (44%)
  waiting for transfers between devices  9.6 us (23%)
  Pallas kernels  7.51 us (18%)
  local copies, waits for them, and re-layouts  4.64 us (11%)
  other arithmetic  0.74 us (2%)
    ppermute x8, starting transfers between devices, cross(): came.append(lax.ppermute(messages[at], ('cache', 'serve'), pairs))  14.9 us
    ppermute x8, waiting for transfers between devices, cross(): came.append(lax.ppermute(messages[at], ('cache', 'serve'), pairs))  6.84 us
    pallas_call x1, Pallas kernels, body(): kernel_call(functools.partial(history_kernel, owners), [half_table] * 2,...  3.62 us
    ppermute x12, starting transfers between devices, swap(): return lax.ppermute(rows, 'serve', [(0, 1), (1, 0)])  3.48 us
    optimization_barrier x1, local copies, waits for them, and re-layouts, body(): out, w_in = lax.optimization_barrier((out, w_in))  3.03 us
    ppermute x12, waiting for transfers between devices, swap(): return lax.ppermute(rows, 'serve', [(0, 1), (1, 0)])  2.75 us
    pallas_call x1, Pallas kernels, body(): kernel_call(functools.partial(output_kernel, messages), bf16((req_count,...  1.84 us
    pallas_call x1, Pallas kernels, body(): kernel_call(functools.partial(front_kernel, owners, half_cands), [bf16((o...  0.95 us
  transfers between devices with their start and end apart: 20, of which 12 were waited for; matrix products, arithmetic and copies ran while one was open for 11% of the time, Pallas kernels for 14%

profile of v11, /device:TPU:0, one launch (start us, length us, event | category | flops | bytes accessed | tf_op | source)
XLA Modules:
  0.0 41.0 jit_solution(9972476423758447474)
XLA Ops:
  0.0 0.5 %collective-permute-start = (bf16[8,8,1024]{2,1,0:T(8,128)(2,1)}, bf16[8,8,1024]{2,1,0:T(8,128)(2,1)S(1)}, u32[]{:S(2)}, u32[]{:S(2)}) collective-permute-start(bf16[8,8,1024]{2,1,0:T(8,128)(2,1)} %own_ref.5), channel_id=1, source_target_pairs={{0,1},{1,0},{2,3},{3,2},{4,5},{5,4},{6,7},{7,6},{8,9},{9,8},{10,11... | collective-permute-start | bytes 393224 | tf_op jit(solution)/shard_map/ppermute | solution.py:236
  0.5 0.7 %pad_bitcast_fusion = s32[1,64]{1,0:T(1,128)S(1)} fusion(s32[8]{0:T(128)} %param.16), kind=kLoop, calls=%fused_computation.2 | loop fusion | bytes 288 | tf_op jit(solution)/shard_map/reshape | solution.py:265
  1.1 0.7 %pad_add_fusion.facts_ref = s32[34,64]{1,0:T(8,128)S(1)} fusion(s32[1,64]{1,0:T(1,128)S(1)} %pad_bitcast_fusion, s32[1,64]{1,0:T(1,128)} %bitcast.17, s32[32,64]{1,0:T(8,128)} %bitcast.19), kind=kLoop, calls=%fused_computation.1 | loop fusion | flops 4352 | bytes 17408 | tf_op jit(solution)/shard_map/concatenate | solution.py:261
  1.9 1.0 %shard_map.91 = (bf16[256,128]{1,0:T(8,128)(2,1)S(1)}, bf16[2048,128]{1,0:T(8,128)(2,1)S(1)}, bf16[128,128]{1,0:T(8,128)(2,1)S(1)}) custom-call(s32[34,64]{1,0:T(8,128)S(1)} %pad_add_fusion.facts_ref), custom_call_target="tpu_custom_call" | custom-call | flops 536870912 | bytes 524288 | tf_op jit(solution)/shard_map/pallas_call | solution.py:269
  2.8 0.0 collective-permute-done.other_ref
  2.8 0.1 collective-permute-start.9
  2.9 0.0 copy-start.2
  3.0 0.9 %copy-done.2 = bf16[8,8,1024]{2,1,0:T(8,128)(2,1)S(1)} copy-done((bf16[8,8,1024]{2,1,0:T(8,128)(2,1)S(1)}, bf16[8,8,1024]{2,1,0:T(8,128)(2,1)}, u32[]{:S(2)}) %copy-start.2) | copy-done | bytes 131096
  3.9 0.2 shard_map.92
  4.1 0.0 copy-start
  4.1 0.0 copy-start.1
  4.1 0.0 copy-start.5
  4.1 5.1 %collective-permute-start.1 = (bf16[32,1024]{1,0:T(8,128)(2,1)S(1)}, bf16[32,1024]{1,0:T(8,128)(2,1)S(1)}, u32[]{:S(2)}, u32[]{:S(2)}) collective-permute-start(bf16[32,1024]{1,0:T(8,128)(2,1)S(1)} %get-tuple-element.51), channel_id=1, source_target_pairs={{0,12},{1,15},{2,14},{3,13},{4,8},{5,11},{6,10},{7,9},{8,4},{9,7},... | collective-permute-start | bytes 196616 | tf_op jit(solution)/shard_map/ppermute | solution.py:244
  9.2 0.4 collective-permute-start.2
  9.6 1.2 %collective-permute-start.3 = (bf16[32,1024]{1,0:T(8,128)(2,1)S(1)}, bf16[32,1024]{1,0:T(8,128)(2,1)S(1)}, u32[]{:S(2)}, u32[]{:S(2)}) collective-permute-start(bf16[32,1024]{1,0:T(8,128)(2,1)S(1)} %get-tuple-element.53), channel_id=1, source_target_pairs={{1,5},{0,6},{3,7},{2,4},{5,1},{4,2},{7,3},{6,0},{9,13},{8,14},{11,... | collective-permute-start | bytes 196616 | tf_op jit(solution)/shard_map/ppermute | solution.py:244
  10.8 0.7 %collective-permute-start.4 = (bf16[32,1024]{1,0:T(8,128)(2,1)S(1)}, bf16[32,1024]{1,0:T(8,128)(2,1)S(1)}, u32[]{:S(2)}, u32[]{:S(2)}) collective-permute-start(bf16[32,1024]{1,0:T(8,128)(2,1)S(1)} %get-tuple-element.54), channel_id=1, source_target_pairs={{0,0},{1,3},{2,2},{3,1},{4,4},{5,7},{6,6},{7,5},{8,8},{9,11},{10,1... | collective-permute-start | bytes 196616 | tf_op jit(solution)/shard_map/ppermute | solution.py:244
  11.4 3.0 %copy.12 = bf16[1024,4,512]{2,0,1:T(8,128)(2,1)S(1)} copy(bf16[1024,4,512]{2,1,0:T(4,128)(2,1)} %param.11) | data formatting | bytes 8388608 | tf_op jit(solution)/shard_map/optimization_barrier | solution.py:280
  14.5 0.0 collective-permute-done.1.refs_0_
  14.5 1.7 %collective-permute-done.2.refs_2_ = bf16[32,1024]{1,0:T(8,128)(2,1)S(1)} collective-permute-done((bf16[32,1024]{1,0:T(8,128)(2,1)S(1)}, bf16[32,1024]{1,0:T(8,128)(2,1)S(1)}, u32[]{:S(2)}, u32[]{:S(2)}) %collective-permute-start.2) | collective-permute-done | bytes 65568 | tf_op jit(solution)/shard_map/ppermute | solution.py:244
  16.1 0.0 collective-permute-done.3.refs_4_
  16.1 0.0 collective-permute-done.4.refs_6_
  16.2 0.1 collective-permute-start.5
  16.2 0.5 %collective-permute-start.6 = (bf16[32,1024]{1,0:T(8,128)(2,1)S(1)}, bf16[32,1024]{1,0:T(8,128)(2,1)S(1)}, u32[]{:S(2)}, u32[]{:S(2)}) collective-permute-start(bf16[32,1024]{1,0:T(8,128)(2,1)S(1)} %collective-permute-done.2.refs_2_), channel_id=1, source_target_pairs={{0,1},{1,0},{2,3},{3,2},{4,5},{5,4},{6,7},{7,6},{8,9},{9,8},{10,11... | collective-permute-start | bytes 196616 | tf_op jit(solution)/shard_map/ppermute | solution.py:236
  16.7 0.1 collective-permute-start.7
  16.7 0.5 %collective-permute-start.8 = (bf16[32,1024]{1,0:T(8,128)(2,1)S(1)}, bf16[32,1024]{1,0:T(8,128)(2,1)S(1)}, u32[]{:S(2)}, u32[]{:S(2)}) collective-permute-start(bf16[32,1024]{1,0:T(8,128)(2,1)S(1)} %collective-permute-done.4.refs_6_), channel_id=1, source_target_pairs={{0,1},{1,0},{2,3},{3,2},{4,5},{5,4},{6,7},{7,6},{8,9},{9,8},{10,11... | collective-permute-start | bytes 196616 | tf_op jit(solution)/shard_map/ppermute | solution.py:236
  17.2 0.2 collective-permute-done.5.refs_1_
  17.4 0.2 collective-permute-done.6.refs_3_
  17.6 0.4 collective-permute-done.7.refs_5_
  17.9 0.2 collective-permute-done.8.refs_7_
  18.1 0.0 copy-done
  18.1 0.0 copy-done.1
  18.1 0.0 copy-done.5
  18.1 0.0 copy-start.3
  18.1 3.6 %shard_map.93 = (bf16[128,512]{1,0:T(8,128)(2,1)S(1)}, bf16[128,512]{1,0:T(8,128)(2,1)S(1)}) custom-call(bf16[8,128]{1,0:T(8,128)(2,1)S(1)} %bitcast.15, bf16[4,1024,512]{2,1,0:T(8,128)(2,1)S(1)} %bitcast.11, bf16[256,128]{1,0:T(8,128)(2,1)S(1)} %get-tuple-element.57.hide_rows_ref, bf16[2048,128]{1,0:T(8,128)(2,1)S(1)} %get-tuple-element.58.hide_cols_ref, ...), custom_call_target="tpu_custom_call" | custom-call | flops 2147483648 | bytes 4194304 | tf_op jit(solution)/shard_map/pallas_call | solution.py:285
  21.7 0.0 copy-start.4
  21.7 0.0 copy-start.6
  21.7 0.0 collective-permute-done.9.w_other_ref
  21.7 0.4 %collective-permute-start.10 = (bf16[128,512]{1,0:T(8,128)(2,1)S(1)}, bf16[128,512]{1,0:T(8,128)(2,1)S(1)}, u32[]{:S(2)}, u32[]{:S(2)}) collective-permute-start(bf16[128,512]{1,0:T(8,128)(2,1)S(1)} %get-tuple-element.67), channel_id=1, source_target_pairs={{0,1},{1,0},{2,3},{3,2},{4,5},{5,4},{6,7},{7,6},{8,9},{9,8},{10,11... | collective-permute-start | bytes 393224 | tf_op jit(solution)/shard_map/ppermute | solution.py:236
  22.2 1.0 %collective-permute-done.10.got_ref = bf16[128,512]{1,0:T(8,128)(2,1)S(1)} collective-permute-done((bf16[128,512]{1,0:T(8,128)(2,1)S(1)}, bf16[128,512]{1,0:T(8,128)(2,1)S(1)}, u32[]{:S(2)}, u32[]{:S(2)}) %collective-permute-start.10) | collective-permute-done | bytes 131104 | tf_op jit(solution)/shard_map/ppermute | solution.py:236
  23.2 2.8 %collective-permute-start.11 = (bf16[64,512]{1,0:T(8,128)(2,1)S(1)}, bf16[64,512]{1,0:T(8,128)(2,1)S(1)}, u32[]{:S(2)}, u32[]{:S(2)}) collective-permute-start(bf16[64,512]{1,0:T(8,128)(2,1)S(1)} %get-tuple-element.72), channel_id=1, source_target_pairs={{0,12},{1,15},{2,14},{3,13},{4,8},{5,11},{6,10},{7,9},{8,4},{9,7},... | collective-permute-start | bytes 196616 | tf_op jit(solution)/shard_map/ppermute | solution.py:244
  26.0 0.0 copy-done.3
  26.0 0.9 %shard_map.95 = (bf16[2,64,512]{2,1,0:T(8,128)(2,1)S(1)}, bf16[2,64,512]{2,1,0:T(8,128)(2,1)S(1)}) custom-call(bf16[8,8,1024]{2,1,0:T(8,128)(2,1)S(1)} %copy-done.3, bf16[8,8,1024]{2,1,0:T(8,128)(2,1)S(1)} %collective-permute-done.other_ref, bf16[8,128]{1,0:T(8,128)(2,1)S(1)} %bitcast.16, bf16[4,1024,512]{2,1,0:T(8,128)(2,1)S(1)} %bitcast.12), custom_call_target="tpu_custom_call" | custom-call | flops 536870912 | bytes 4194304 | tf_op jit(solution)/shard_map/pallas_call | solution.py:304
  26.9 3.2 %collective-permute-done.11.refs_0_ = bf16[64,512]{1,0:T(8,128)(2,1)S(1)} collective-permute-done((bf16[64,512]{1,0:T(8,128)(2,1)S(1)}, bf16[64,512]{1,0:T(8,128)(2,1)S(1)}, u32[]{:S(2)}, u32[]{:S(2)}) %collective-permute-start.11) | collective-permute-done | bytes 65568 | tf_op jit(solution)/shard_map/ppermute | solution.py:244
  30.1 0.0 collective-permute-start.12
  30.1 1.4 %collective-permute-start.14 = (bf16[64,512]{1,0:T(8,128)(2,1)S(1)}, bf16[64,512]{1,0:T(8,128)(2,1)S(1)}, u32[]{:S(2)}, u32[]{:S(2)}) collective-permute-start(bf16[64,512]{1,0:T(8,128)(2,1)S(1)} %get-tuple-element.80), channel_id=1, source_target_pairs={{1,9},{0,10},{3,11},{2,8},{5,13},{4,14},{7,15},{6,12},{9,1},{8,2},... | collective-permute-start | bytes 196616 | tf_op jit(solution)/shard_map/ppermute | solution.py:244
  31.5 2.7 %collective-permute-start.16 = (bf16[64,512]{1,0:T(8,128)(2,1)S(1)}, bf16[64,512]{1,0:T(8,128)(2,1)S(1)}, u32[]{:S(2)}, u32[]{:S(2)}) collective-permute-start(bf16[64,512]{1,0:T(8,128)(2,1)S(1)} %get-tuple-element.81), channel_id=1, source_target_pairs={{1,5},{0,6},{3,7},{2,4},{5,1},{4,2},{7,3},{6,0},{9,13},{8,14},{11,... | collective-permute-start | bytes 196616 | tf_op jit(solution)/shard_map/ppermute | solution.py:244
  34.2 0.7 %collective-permute-start.18 = (bf16[64,512]{1,0:T(8,128)(2,1)S(1)}, bf16[64,512]{1,0:T(8,128)(2,1)S(1)}, u32[]{:S(2)}, u32[]{:S(2)}) collective-permute-start(bf16[64,512]{1,0:T(8,128)(2,1)S(1)} %get-tuple-element.82), channel_id=1, source_target_pairs={{0,0},{1,3},{2,2},{3,1},{4,4},{5,7},{6,6},{7,5},{8,8},{9,11},{10,1... | collective-permute-start | bytes 196616 | tf_op jit(solution)/shard_map/ppermute | solution.py:244
  34.8 0.9 %collective-permute-start.13 = (bf16[32,512]{1,0:T(8,128)(2,1)S(1)}, bf16[32,512]{1,0:T(8,128)(2,1)S(1)}, u32[]{:S(2)}, u32[]{:S(2)}) collective-permute-start(bf16[32,512]{1,0:T(8,128)(2,1)S(1)} %slice.12), channel_id=1, source_target_pairs={{0,1},{1,0},{2,3},{3,2},{4,5},{5,4},{6,7},{7,6},{8,9},{9,8},{10,11... | collective-permute-start | bytes 98312 | tf_op jit(solution)/shard_map/ppermute | solution.py:236
  35.8 1.5 %collective-permute-done.14.refs_2_ = bf16[64,512]{1,0:T(8,128)(2,1)S(1)} collective-permute-done((bf16[64,512]{1,0:T(8,128)(2,1)S(1)}, bf16[64,512]{1,0:T(8,128)(2,1)S(1)}, u32[]{:S(2)}, u32[]{:S(2)}) %collective-permute-start.14) | collective-permute-done | bytes 65568 | tf_op jit(solution)/shard_map/ppermute | solution.py:244
  37.2 0.0 collective-permute-start.15
  37.3 0.5 %collective-permute-done.16.refs_4_ = bf16[64,512]{1,0:T(8,128)(2,1)S(1)} collective-permute-done((bf16[64,512]{1,0:T(8,128)(2,1)S(1)}, bf16[64,512]{1,0:T(8,128)(2,1)S(1)}, u32[]{:S(2)}, u32[]{:S(2)}) %collective-permute-start.16) | collective-permute-done | bytes 65568 | tf_op jit(solution)/shard_map/ppermute | solution.py:244
  37.7 0.0 collective-permute-start.17
  37.8 0.0 collective-permute-done.18.refs_6_
  37.8 0.5 %collective-permute-start.19 = (bf16[32,512]{1,0:T(8,128)(2,1)S(1)}, bf16[32,512]{1,0:T(8,128)(2,1)S(1)}, u32[]{:S(2)}, u32[]{:S(2)}) collective-permute-start(bf16[32,512]{1,0:T(8,128)(2,1)S(1)} %slice.18), channel_id=1, source_target_pairs={{0,1},{1,0},{2,3},{3,2},{4,5},{5,4},{6,7},{7,6},{8,9},{9,8},{10,11... | collective-permute-start | bytes 98312 | tf_op jit(solution)/shard_map/ppermute | solution.py:236
  38.3 0.0 collective-permute-done.13.refs_1_
  38.3 0.2 collective-permute-done.15.refs_3_
  38.5 0.5 %collective-permute-done.17.refs_5_ = bf16[32,512]{1,0:T(8,128)(2,1)S(1)} collective-permute-done((bf16[32,512]{1,0:T(8,128)(2,1)S(1)}, bf16[32,512]{1,0:T(8,128)(2,1)S(1)}, u32[]{:S(2)}, u32[]{:S(2)}) %collective-permute-start.17) | collective-permute-done | bytes 32800 | tf_op jit(solution)/shard_map/ppermute | solution.py:236
  38.9 0.2 collective-permute-done.19.refs_7_
  39.1 0.0 collective-permute-done.12.got_ref
  39.1 0.0 copy-done.4
  39.1 0.0 copy-done.6
  39.1 1.8 %shard_map.96 = bf16[8,8,1024]{2,1,0:T(8,128)(2,1)} custom-call(s32[64]{0:T(128)S(1)} %bitcast.18, bf16[8,8,1024]{2,1,0:T(8,128)(2,1)S(1)} %copy-done.3, bf16[2,64,512]{2,1,0:T(8,128)(2,1)S(1)} %get-tuple-element.76.keep_ref, bf16[2,64,512]{2,1,0:T(8,128)(2,1)S(1)} %collective-permute-done.12.got_ref, bf16[512,1024]{1,0:T(8,128)(2,1)S(1)} %copy-done.4, ...), custom_call_target="tpu_custom_call" | custom-call | flops 268435456 | bytes 2097152 | tf_op jit(solution)/shard_map/pallas_call | solution.py:314
  (5 shorter events, 0.0 us)
Async XLA Ops:
  0.0 2.8 %collective-permute-start = (bf16[8,8,1024]{2,1,0:T(8,128)(2,1)}, bf16[8,8,1024]{2,1,0:T(8,128)(2,1)S(1)}, u32[]{:S(2)}, u32[]{:S(2)}) collective-permute-start(bf16[8,8,1024]{2,1,0:T(8,128)(2,1)} %own_ref.5), channel_id=1, source_target_pairs={{0,1},{1,0},{2,3},{3,2},{4,5},{5,4},{6,7},{7,6},{8,9},{9,8},{10,11... | collective-permute-start | bytes 393224 | tf_op jit(solution)/shard_map/ppermute | solution.py:236
  2.8 18.9 %collective-permute-start.9 = (bf16[512,1024]{1,0:T(8,128)(2,1)}, bf16[512,1024]{1,0:T(8,128)(2,1)S(1)}, u32[]{:S(2)}, u32[]{:S(2)}) collective-permute-start(bf16[512,1024]{1,0:T(8,128)(2,1)} %w_own_ref), channel_id=1, source_target_pairs={{0,1},{1,0},{2,3},{3,2},{4,5},{5,4},{6,7},{7,6},{8,9},{9,8},{10,11... | collective-permute-start | bytes 3145736 | tf_op jit(solution)/shard_map/ppermute | solution.py:236
  2.9 0.9 %copy-start.2 = (bf16[8,8,1024]{2,1,0:T(8,128)(2,1)S(1)}, bf16[8,8,1024]{2,1,0:T(8,128)(2,1)}, u32[]{:S(2)}) copy-start(bf16[8,8,1024]{2,1,0:T(8,128)(2,1)} %own_ref.5) | copy-start | bytes 393220
  4.1 14.0 %copy-start = (bf16[1,2048,512]{2,1,0:T(8,128)(2,1)S(1)}, bf16[1,2048,512]{2,1,0:T(8,128)(2,1)}, u32[]{:S(2)}) copy-start(bf16[1,2048,512]{2,1,0:T(8,128)(2,1)} %param.13) | copy-start | bytes 6291460
  4.1 14.0 %copy-start.1 = (bf16[1,2048,512]{2,1,0:T(8,128)(2,1)S(1)}, bf16[1,2048,512]{2,1,0:T(8,128)(2,1)}, u32[]{:S(2)}) copy-start(bf16[1,2048,512]{2,1,0:T(8,128)(2,1)} %param.14) | copy-start | bytes 6291460
  4.1 14.0 %copy-start.5 = (bf16[1024]{0:T(1024)(128)(2,1)S(1)}, bf16[1024]{0:T(1024)(128)(2,1)}, u32[]{:S(2)}) copy-start(bf16[1024]{0:T(1024)(128)(2,1)} %param.10) | copy-start | bytes 6148
  4.1 10.4 %collective-permute-start.1 = (bf16[32,1024]{1,0:T(8,128)(2,1)S(1)}, bf16[32,1024]{1,0:T(8,128)(2,1)S(1)}, u32[]{:S(2)}, u32[]{:S(2)}) collective-permute-start(bf16[32,1024]{1,0:T(8,128)(2,1)S(1)} %get-tuple-element.51), channel_id=1, source_target_pairs={{0,12},{1,15},{2,14},{3,13},{4,8},{5,11},{6,10},{7,9},{8,4},{9,7},... | collective-permute-start | bytes 196616 | tf_op jit(solution)/shard_map/ppermute | solution.py:244
  9.2 6.9 %collective-permute-start.2 = (bf16[32,1024]{1,0:T(8,128)(2,1)S(1)}, bf16[32,1024]{1,0:T(8,128)(2,1)S(1)}, u32[]{:S(2)}, u32[]{:S(2)}) collective-permute-start(bf16[32,1024]{1,0:T(8,128)(2,1)S(1)} %get-tuple-element.52), channel_id=1, source_target_pairs={{1,9},{0,10},{3,11},{2,8},{5,13},{4,14},{7,15},{6,12},{9,1},{8,2},... | collective-permute-start | bytes 196616 | tf_op jit(solution)/shard_map/ppermute | solution.py:244
  9.6 6.5 %collective-permute-start.3 = (bf16[32,1024]{1,0:T(8,128)(2,1)S(1)}, bf16[32,1024]{1,0:T(8,128)(2,1)S(1)}, u32[]{:S(2)}, u32[]{:S(2)}) collective-permute-start(bf16[32,1024]{1,0:T(8,128)(2,1)S(1)} %get-tuple-element.53), channel_id=1, source_target_pairs={{1,5},{0,6},{3,7},{2,4},{5,1},{4,2},{7,3},{6,0},{9,13},{8,14},{11,... | collective-permute-start | bytes 196616 | tf_op jit(solution)/shard_map/ppermute | solution.py:244
  10.8 5.4 %collective-permute-start.4 = (bf16[32,1024]{1,0:T(8,128)(2,1)S(1)}, bf16[32,1024]{1,0:T(8,128)(2,1)S(1)}, u32[]{:S(2)}, u32[]{:S(2)}) collective-permute-start(bf16[32,1024]{1,0:T(8,128)(2,1)S(1)} %get-tuple-element.54), channel_id=1, source_target_pairs={{0,0},{1,3},{2,2},{3,1},{4,4},{5,7},{6,6},{7,5},{8,8},{9,11},{10,1... | collective-permute-start | bytes 196616 | tf_op jit(solution)/shard_map/ppermute | solution.py:244
  16.2 1.3 %collective-permute-start.5 = (bf16[32,1024]{1,0:T(8,128)(2,1)S(1)}, bf16[32,1024]{1,0:T(8,128)(2,1)S(1)}, u32[]{:S(2)}, u32[]{:S(2)}) collective-permute-start(bf16[32,1024]{1,0:T(8,128)(2,1)S(1)} %collective-permute-done.1.refs_0_), channel_id=1, source_target_pairs={{0,1},{1,0},{2,3},{3,2},{4,5},{5,4},{6,7},{7,6},{8,9},{9,8},{10,11... | collective-permute-start | bytes 196616 | tf_op jit(solution)/shard_map/ppermute | solution.py:236
  16.2 1.4 %collective-permute-start.6 = (bf16[32,1024]{1,0:T(8,128)(2,1)S(1)}, bf16[32,1024]{1,0:T(8,128)(2,1)S(1)}, u32[]{:S(2)}, u32[]{:S(2)}) collective-permute-start(bf16[32,1024]{1,0:T(8,128)(2,1)S(1)} %collective-permute-done.2.refs_2_), channel_id=1, source_target_pairs={{0,1},{1,0},{2,3},{3,2},{4,5},{5,4},{6,7},{7,6},{8,9},{9,8},{10,11... | collective-permute-start | bytes 196616 | tf_op jit(solution)/shard_map/ppermute | solution.py:236
  16.7 1.3 %collective-permute-start.7 = (bf16[32,1024]{1,0:T(8,128)(2,1)S(1)}, bf16[32,1024]{1,0:T(8,128)(2,1)S(1)}, u32[]{:S(2)}, u32[]{:S(2)}) collective-permute-start(bf16[32,1024]{1,0:T(8,128)(2,1)S(1)} %collective-permute-done.3.refs_4_), channel_id=1, source_target_pairs={{0,1},{1,0},{2,3},{3,2},{4,5},{5,4},{6,7},{7,6},{8,9},{9,8},{10,11... | collective-permute-start | bytes 196616 | tf_op jit(solution)/shard_map/ppermute | solution.py:236
  16.7 1.4 %collective-permute-start.8 = (bf16[32,1024]{1,0:T(8,128)(2,1)S(1)}, bf16[32,1024]{1,0:T(8,128)(2,1)S(1)}, u32[]{:S(2)}, u32[]{:S(2)}) collective-permute-start(bf16[32,1024]{1,0:T(8,128)(2,1)S(1)} %collective-permute-done.4.refs_6_), channel_id=1, source_target_pairs={{0,1},{1,0},{2,3},{3,2},{4,5},{5,4},{6,7},{7,6},{8,9},{9,8},{10,11... | collective-permute-start | bytes 196616 | tf_op jit(solution)/shard_map/ppermute | solution.py:236
  18.1 7.9 %copy-start.3 = (bf16[8,8,1024]{2,1,0:T(8,128)(2,1)S(1)}, bf16[8,8,1024]{2,1,0:T(8,128)(2,1)}, u32[]{:S(2)}) copy-start(bf16[8,8,1024]{2,1,0:T(8,128)(2,1)} %own_ref.5) | copy-start | bytes 393220
  21.7 17.4 %copy-start.4 = (bf16[512,1024]{1,0:T(8,128)(2,1)S(1)}, bf16[512,1024]{1,0:T(8,128)(2,1)}, u32[]{:S(2)}) copy-start(bf16[512,1024]{1,0:T(8,128)(2,1)} %w_own_ref) | copy-start | bytes 3145732
  21.7 17.4 %copy-start.6 = (s32[64,1]{0,1:T(1,128)S(1)}, s32[64,1]{0,1:T(1,128)}, u32[]{:S(2)}) copy-start(s32[64,1]{0,1:T(1,128)} %param.15) | copy-start | bytes 772
  21.7 1.4 %collective-permute-start.10 = (bf16[128,512]{1,0:T(8,128)(2,1)S(1)}, bf16[128,512]{1,0:T(8,128)(2,1)S(1)}, u32[]{:S(2)}, u32[]{:S(2)}) collective-permute-start(bf16[128,512]{1,0:T(8,128)(2,1)S(1)} %get-tuple-element.67), channel_id=1, source_target_pairs={{0,1},{1,0},{2,3},{3,2},{4,5},{5,4},{6,7},{7,6},{8,9},{9,8},{10,11... | collective-permute-start | bytes 393224 | tf_op jit(solution)/shard_map/ppermute | solution.py:236
  23.2 6.9 %collective-permute-start.11 = (bf16[64,512]{1,0:T(8,128)(2,1)S(1)}, bf16[64,512]{1,0:T(8,128)(2,1)S(1)}, u32[]{:S(2)}, u32[]{:S(2)}) collective-permute-start(bf16[64,512]{1,0:T(8,128)(2,1)S(1)} %get-tuple-element.72), channel_id=1, source_target_pairs={{0,12},{1,15},{2,14},{3,13},{4,8},{5,11},{6,10},{7,9},{8,4},{9,7},... | collective-permute-start | bytes 196616 | tf_op jit(solution)/shard_map/ppermute | solution.py:244
  30.1 9.0 %collective-permute-start.12 = (bf16[2,64,512]{2,1,0:T(8,128)(2,1)S(1)}, bf16[2,64,512]{2,1,0:T(8,128)(2,1)S(1)}, u32[]{:S(2)}, u32[]{:S(2)}) collective-permute-start(bf16[2,64,512]{2,1,0:T(8,128)(2,1)S(1)} %get-tuple-element.77), channel_id=1, source_target_pairs={{0,1},{1,0},{2,3},{3,2},{4,5},{5,4},{6,7},{7,6},{8,9},{9,8},{10,11... | collective-permute-start | bytes 393224 | tf_op jit(solution)/shard_map/ppermute | solution.py:236
  30.1 7.1 %collective-permute-start.14 = (bf16[64,512]{1,0:T(8,128)(2,1)S(1)}, bf16[64,512]{1,0:T(8,128)(2,1)S(1)}, u32[]{:S(2)}, u32[]{:S(2)}) collective-permute-start(bf16[64,512]{1,0:T(8,128)(2,1)S(1)} %get-tuple-element.80), channel_id=1, source_target_pairs={{1,9},{0,10},{3,11},{2,8},{5,13},{4,14},{7,15},{6,12},{9,1},{8,2},... | collective-permute-start | bytes 196616 | tf_op jit(solution)/shard_map/ppermute | solution.py:244
  31.5 6.2 %collective-permute-start.16 = (bf16[64,512]{1,0:T(8,128)(2,1)S(1)}, bf16[64,512]{1,0:T(8,128)(2,1)S(1)}, u32[]{:S(2)}, u32[]{:S(2)}) collective-permute-start(bf16[64,512]{1,0:T(8,128)(2,1)S(1)} %get-tuple-element.81), channel_id=1, source_target_pairs={{1,5},{0,6},{3,7},{2,4},{5,1},{4,2},{7,3},{6,0},{9,13},{8,14},{11,... | collective-permute-start | bytes 196616 | tf_op jit(solution)/shard_map/ppermute | solution.py:244
  34.2 3.6 %collective-permute-start.18 = (bf16[64,512]{1,0:T(8,128)(2,1)S(1)}, bf16[64,512]{1,0:T(8,128)(2,1)S(1)}, u32[]{:S(2)}, u32[]{:S(2)}) collective-permute-start(bf16[64,512]{1,0:T(8,128)(2,1)S(1)} %get-tuple-element.82), channel_id=1, source_target_pairs={{0,0},{1,3},{2,2},{3,1},{4,4},{5,7},{6,6},{7,5},{8,8},{9,11},{10,1... | collective-permute-start | bytes 196616 | tf_op jit(solution)/shard_map/ppermute | solution.py:244
  34.8 3.4 %collective-permute-start.13 = (bf16[32,512]{1,0:T(8,128)(2,1)S(1)}, bf16[32,512]{1,0:T(8,128)(2,1)S(1)}, u32[]{:S(2)}, u32[]{:S(2)}) collective-permute-start(bf16[32,512]{1,0:T(8,128)(2,1)S(1)} %slice.12), channel_id=1, source_target_pairs={{0,1},{1,0},{2,3},{3,2},{4,5},{5,4},{6,7},{7,6},{8,9},{9,8},{10,11... | collective-permute-start | bytes 98312 | tf_op jit(solution)/shard_map/ppermute | solution.py:236
  37.2 1.2 %collective-permute-start.15 = (bf16[32,512]{1,0:T(8,128)(2,1)S(1)}, bf16[32,512]{1,0:T(8,128)(2,1)S(1)}, u32[]{:S(2)}, u32[]{:S(2)}) collective-permute-start(bf16[32,512]{1,0:T(8,128)(2,1)S(1)} %slice.16), channel_id=1, source_target_pairs={{0,1},{1,0},{2,3},{3,2},{4,5},{5,4},{6,7},{7,6},{8,9},{9,8},{10,11... | collective-permute-start | bytes 98312 | tf_op jit(solution)/shard_map/ppermute | solution.py:236
  37.7 1.2 %collective-permute-start.17 = (bf16[32,512]{1,0:T(8,128)(2,1)S(1)}, bf16[32,512]{1,0:T(8,128)(2,1)S(1)}, u32[]{:S(2)}, u32[]{:S(2)}) collective-permute-start(bf16[32,512]{1,0:T(8,128)(2,1)S(1)} %slice.17), channel_id=1, source_target_pairs={{0,1},{1,0},{2,3},{3,2},{4,5},{5,4},{6,7},{7,6},{8,9},{9,8},{10,11... | collective-permute-start | bytes 98312 | tf_op jit(solution)/shard_map/ppermute | solution.py:236
  37.8 1.4 %collective-permute-start.19 = (bf16[32,512]{1,0:T(8,128)(2,1)S(1)}, bf16[32,512]{1,0:T(8,128)(2,1)S(1)}, u32[]{:S(2)}, u32[]{:S(2)}) collective-permute-start(bf16[32,512]{1,0:T(8,128)(2,1)S(1)} %slice.18), channel_id=1, source_target_pairs={{0,1},{1,0},{2,3},{3,2},{4,5},{5,4},{6,7},{7,6},{8,9},{9,8},{10,11... | collective-permute-start | bytes 98312 | tf_op jit(solution)/shard_map/ppermute | solution.py:236

commit v12 on v11

--- a/solution.py
+++ b/solution.py
@@ -298,9 +298,7 @@
         *[rows_of for both in zip(came, swapped) for rows_of in both],
     )
     keep, give, w_other = lax.optimization_barrier((keep, give, w_other))
-    out = kernel_call(pack_kernel, [bf16((2 * piece, width))] * messages, [vmem] * 2)(keep, swap(give))
-    out, other = lax.optimization_barrier((out, other))
-    backs = cross(owners, out)
+    got = swap(give)
     terms = kernel_call(
         self_kernel,
         [bf16((2, rows, width))] * 2,
@@ -308,8 +306,9 @@
         [pltpu.VMEM((2 * rows, model_width), jnp.bfloat16)],
         flops=16 * rows * model_width * width,
         moved=8 * model_width * width,
-    )(candidates, other, gain, weights)
-    backs[0], (keep_terms, give_terms) = lax.optimization_barrier((backs[0], terms))
+    )(candidates, lax.optimization_barrier((other, give))[0], gain, weights)
+    got, (keep_terms, give_terms) = lax.optimization_barrier((got, terms))
+    backs = cross(owners, kernel_call(pack_kernel, [bf16((2 * piece, width))] * messages, [vmem] * 2)(keep, got))
     returned = [rows_of for back in backs for rows_of in (back, swap(back[piece:]))]
     return kernel_call(
         functools.partial(output_kernel, messages),

time: 41.2 us -> 37.2 us (0.903)
  starting transfers between devices: 18.3 us -> 16.3 us
  waiting for transfers between devices: 9.6 us -> 7.61 us
    ppermute x8, starting transfers between devices: 14.9 us -> 13.3 us  [cross(): came.append(lax.ppermute(messages[at], ('cache', 'serve'), pairs))]
    ppermute x8, waiting for transfers between devices: 6.84 us -> 5.5 us  [cross(): came.append(lax.ppermute(messages[at], ('cache', 'serve'), pairs))]
    ppermute x12, waiting for transfers between devices: 2.75 us -> 2.11 us  [swap(): return lax.ppermute(rows, 'serve', [(0, 1), (1, 0)])]
    ppermute x12, starting transfers between devices: 3.48 us -> 3 us  [swap(): return lax.ppermute(rows, 'serve', [(0, 1), (1, 0)])]
  transfers between devices with their start and end apart: 20 -> 20, of which waited for: 12 -> 11; matrix products, arithmetic and copies ran while one was open for 11% -> 12% of each run, Pallas kernels for 14% -> 15%
where the time goes in v12:
time: 37.2 us; the launch traced here: 37 us
  starting transfers between devices  16.3 us (44%)
  waiting for transfers between devices  7.61 us (20%)
  Pallas kernels  7.51 us (20%)
  local copies, waits for them, and re-layouts  4.64 us (12%)
  other arithmetic  0.74 us (2%)
    ppermute x8, starting transfers between devices, cross(): came.append(lax.ppermute(messages[at], ('cache', 'serve'), pairs))  13.3 us
    ppermute x8, waiting for transfers between devices, cross(): came.append(lax.ppermute(messages[at], ('cache', 'serve'), pairs))  5.5 us
    pallas_call x1, Pallas kernels, body(): kernel_call(functools.partial(history_kernel, owners), [half_table] * 2,...  3.62 us
    optimization_barrier x1, local copies, waits for them, and re-layouts, body(): out, w_in = lax.optimization_barrier((out, w_in))  3.03 us
    ppermute x12, starting transfers between devices, swap(): return lax.ppermute(rows, 'serve', [(0, 1), (1, 0)])  3 us
    ppermute x12, waiting for transfers between devices, swap(): return lax.ppermute(rows, 'serve', [(0, 1), (1, 0)])  2.11 us
    pallas_call x1, Pallas kernels, body(): kernel_call(functools.partial(output_kernel, messages), bf16((req_count,...  1.84 us
    pallas_call x1, Pallas kernels, body(): kernel_call(functools.partial(front_kernel, owners, half_cands), [bf16((o...  0.95 us
  transfers between devices with their start and end apart: 20, of which 11 were waited for; matrix products, arithmetic and copies ran while one was open for 12% of the time, Pallas kernels for 15%

profile of v12, /device:TPU:0, one launch (start us, length us, event | category | flops | bytes accessed | tf_op | source)
XLA Modules:
  0.0 37.0 jit_solution(985585388413754999)
XLA Ops:
  0.0 0.5 %collective-permute-start = (bf16[8,8,1024]{2,1,0:T(8,128)(2,1)}, bf16[8,8,1024]{2,1,0:T(8,128)(2,1)S(1)}, u32[]{:S(2)}, u32[]{:S(2)}) collective-permute-start(bf16[8,8,1024]{2,1,0:T(8,128)(2,1)} %own_ref.5), channel_id=1, source_target_pairs={{0,1},{1,0},{2,3},{3,2},{4,5},{5,4},{6,7},{7,6},{8,9},{9,8},{10,11... | collective-permute-start | bytes 393224 | tf_op jit(solution)/shard_map/ppermute | solution.py:236
  0.5 0.7 %pad_bitcast_fusion = s32[1,64]{1,0:T(1,128)S(1)} fusion(s32[8]{0:T(128)} %param.16), kind=kLoop, calls=%fused_computation.2 | loop fusion | bytes 288 | tf_op jit(solution)/shard_map/reshape | solution.py:265
  1.1 0.7 %pad_add_fusion.facts_ref = s32[34,64]{1,0:T(8,128)S(1)} fusion(s32[1,64]{1,0:T(1,128)S(1)} %pad_bitcast_fusion, s32[1,64]{1,0:T(1,128)} %bitcast.17, s32[32,64]{1,0:T(8,128)} %bitcast.19), kind=kLoop, calls=%fused_computation.1 | loop fusion | flops 4352 | bytes 17408 | tf_op jit(solution)/shard_map/concatenate | solution.py:261
  1.9 1.0 %shard_map.91 = (bf16[256,128]{1,0:T(8,128)(2,1)S(1)}, bf16[2048,128]{1,0:T(8,128)(2,1)S(1)}, bf16[128,128]{1,0:T(8,128)(2,1)S(1)}) custom-call(s32[34,64]{1,0:T(8,128)S(1)} %pad_add_fusion.facts_ref), custom_call_target="tpu_custom_call" | custom-call | flops 536870912 | bytes 524288 | tf_op jit(solution)/shard_map/pallas_call | solution.py:269
  2.8 0.0 collective-permute-done.other_ref
  2.8 0.1 collective-permute-start.9
  2.9 0.0 copy-start.2
  3.0 0.9 %copy-done.2 = bf16[8,8,1024]{2,1,0:T(8,128)(2,1)S(1)} copy-done((bf16[8,8,1024]{2,1,0:T(8,128)(2,1)S(1)}, bf16[8,8,1024]{2,1,0:T(8,128)(2,1)}, u32[]{:S(2)}) %copy-start.2) | copy-done | bytes 131096
  3.9 0.2 shard_map.92
  4.1 0.0 copy-start
  4.1 0.0 copy-start.1
  4.1 0.0 copy-start.5
  4.1 5.1 %collective-permute-start.1 = (bf16[32,1024]{1,0:T(8,128)(2,1)S(1)}, bf16[32,1024]{1,0:T(8,128)(2,1)S(1)}, u32[]{:S(2)}, u32[]{:S(2)}) collective-permute-start(bf16[32,1024]{1,0:T(8,128)(2,1)S(1)} %get-tuple-element.47), channel_id=1, source_target_pairs={{0,12},{1,15},{2,14},{3,13},{4,8},{5,11},{6,10},{7,9},{8,4},{9,7},... | collective-permute-start | bytes 196616 | tf_op jit(solution)/shard_map/ppermute | solution.py:244
  9.2 0.4 %collective-permute-start.2 = (bf16[32,1024]{1,0:T(8,128)(2,1)S(1)}, bf16[32,1024]{1,0:T(8,128)(2,1)S(1)}, u32[]{:S(2)}, u32[]{:S(2)}) collective-permute-start(bf16[32,1024]{1,0:T(8,128)(2,1)S(1)} %get-tuple-element.48), channel_id=1, source_target_pairs={{1,9},{0,10},{3,11},{2,8},{5,13},{4,14},{7,15},{6,12},{9,1},{8,2},... | collective-permute-start | bytes 196616 | tf_op jit(solution)/shard_map/ppermute | solution.py:244
  9.6 1.2 %collective-permute-start.3 = (bf16[32,1024]{1,0:T(8,128)(2,1)S(1)}, bf16[32,1024]{1,0:T(8,128)(2,1)S(1)}, u32[]{:S(2)}, u32[]{:S(2)}) collective-permute-start(bf16[32,1024]{1,0:T(8,128)(2,1)S(1)} %get-tuple-element.49), channel_id=1, source_target_pairs={{1,5},{0,6},{3,7},{2,4},{5,1},{4,2},{7,3},{6,0},{9,13},{8,14},{11,... | collective-permute-start | bytes 196616 | tf_op jit(solution)/shard_map/ppermute | solution.py:244
  10.8 0.7 %collective-permute-start.4 = (bf16[32,1024]{1,0:T(8,128)(2,1)S(1)}, bf16[32,1024]{1,0:T(8,128)(2,1)S(1)}, u32[]{:S(2)}, u32[]{:S(2)}) collective-permute-start(bf16[32,1024]{1,0:T(8,128)(2,1)S(1)} %get-tuple-element.50), channel_id=1, source_target_pairs={{0,0},{1,3},{2,2},{3,1},{4,4},{5,7},{6,6},{7,5},{8,8},{9,11},{10,1... | collective-permute-start | bytes 196616 | tf_op jit(solution)/shard_map/ppermute | solution.py:244
  11.4 3.0 %copy.12 = bf16[1024,4,512]{2,0,1:T(8,128)(2,1)S(1)} copy(bf16[1024,4,512]{2,1,0:T(4,128)(2,1)} %param.11) | data formatting | bytes 8388608 | tf_op jit(solution)/shard_map/optimization_barrier | solution.py:280
  14.5 0.0 collective-permute-done.1.refs_0_
  14.5 1.7 %collective-permute-done.2.refs_2_ = bf16[32,1024]{1,0:T(8,128)(2,1)S(1)} collective-permute-done((bf16[32,1024]{1,0:T(8,128)(2,1)S(1)}, bf16[32,1024]{1,0:T(8,128)(2,1)S(1)}, u32[]{:S(2)}, u32[]{:S(2)}) %collective-permute-start.2) | collective-permute-done | bytes 65568 | tf_op jit(solution)/shard_map/ppermute | solution.py:244
  16.1 0.0 collective-permute-done.3.refs_4_
  16.1 0.0 collective-permute-done.4.refs_6_
  16.2 0.1 collective-permute-start.5
  16.2 0.5 %collective-permute-start.6 = (bf16[32,1024]{1,0:T(8,128)(2,1)S(1)}, bf16[32,1024]{1,0:T(8,128)(2,1)S(1)}, u32[]{:S(2)}, u32[]{:S(2)}) collective-permute-start(bf16[32,1024]{1,0:T(8,128)(2,1)S(1)} %collective-permute-done.2.refs_2_), channel_id=1, source_target_pairs={{0,1},{1,0},{2,3},{3,2},{4,5},{5,4},{6,7},{7,6},{8,9},{9,8},{10,11... | collective-permute-start | bytes 196616 | tf_op jit(solution)/shard_map/ppermute | solution.py:236
  16.7 0.1 collective-permute-start.7
  16.7 0.5 %collective-permute-start.8 = (bf16[32,1024]{1,0:T(8,128)(2,1)S(1)}, bf16[32,1024]{1,0:T(8,128)(2,1)S(1)}, u32[]{:S(2)}, u32[]{:S(2)}) collective-permute-start(bf16[32,1024]{1,0:T(8,128)(2,1)S(1)} %collective-permute-done.4.refs_6_), channel_id=1, source_target_pairs={{0,1},{1,0},{2,3},{3,2},{4,5},{5,4},{6,7},{7,6},{8,9},{9,8},{10,11... | collective-permute-start | bytes 196616 | tf_op jit(solution)/shard_map/ppermute | solution.py:236
  17.2 0.2 collective-permute-done.5.refs_1_
  17.4 0.2 collective-permute-done.6.refs_3_
  17.6 0.4 collective-permute-done.7.refs_5_
  17.9 0.2 collective-permute-done.8.refs_7_
  18.1 0.0 copy-done
  18.1 0.0 copy-done.1
  18.1 0.0 copy-done.5
  18.1 0.0 copy-start.3
  18.1 3.6 %shard_map.93 = (bf16[128,512]{1,0:T(8,128)(2,1)S(1)}, bf16[128,512]{1,0:T(8,128)(2,1)S(1)}) custom-call(bf16[8,128]{1,0:T(8,128)(2,1)S(1)} %bitcast.15, bf16[4,1024,512]{2,1,0:T(8,128)(2,1)S(1)} %bitcast.11, bf16[256,128]{1,0:T(8,128)(2,1)S(1)} %get-tuple-element.53.hide_rows_ref, bf16[2048,128]{1,0:T(8,128)(2,1)S(1)} %get-tuple-element.54.hide_cols_ref, ...), custom_call_target="tpu_custom_call" | custom-call | flops 2147483648 | bytes 4194304 | tf_op jit(solution)/shard_map/pallas_call | solution.py:285
  21.7 0.0 copy-start.4
  21.7 0.0 copy-start.6
  21.7 0.0 collective-permute-done.9.w_other_ref
  21.7 0.4 %collective-permute-start.10 = (bf16[128,512]{1,0:T(8,128)(2,1)S(1)}, bf16[128,512]{1,0:T(8,128)(2,1)S(1)}, u32[]{:S(2)}, u32[]{:S(2)}) collective-permute-start(bf16[128,512]{1,0:T(8,128)(2,1)S(1)} %get-tuple-element.62), channel_id=1, source_target_pairs={{0,1},{1,0},{2,3},{3,2},{4,5},{5,4},{6,7},{7,6},{8,9},{9,8},{10,11... | collective-permute-start | bytes 393224 | tf_op jit(solution)/shard_map/ppermute | solution.py:236
  22.2 0.0 copy-done.3
  22.2 0.9 %shard_map.94 = (bf16[2,64,512]{2,1,0:T(8,128)(2,1)S(1)}, bf16[2,64,512]{2,1,0:T(8,128)(2,1)S(1)}) custom-call(bf16[8,8,1024]{2,1,0:T(8,128)(2,1)S(1)} %copy-done.3, bf16[8,8,1024]{2,1,0:T(8,128)(2,1)S(1)} %collective-permute-done.other_ref, bf16[8,128]{1,0:T(8,128)(2,1)S(1)} %bitcast.16, bf16[4,1024,512]{2,1,0:T(8,128)(2,1)S(1)} %bitcast.12), custom_call_target="tpu_custom_call" | custom-call | flops 536870912 | bytes 4194304 | tf_op jit(solution)/shard_map/pallas_call | solution.py:302
  23.1 0.1 collective-permute-done.10.got_ref
  23.2 0.4 collective-permute-start.11
  23.6 2.6 %collective-permute-start.12 = (bf16[64,512]{1,0:T(8,128)(2,1)S(1)}, bf16[64,512]{1,0:T(8,128)(2,1)S(1)}, u32[]{:S(2)}, u32[]{:S(2)}) collective-permute-start(bf16[64,512]{1,0:T(8,128)(2,1)S(1)} %get-tuple-element.71), channel_id=1, source_target_pairs={{0,12},{1,15},{2,14},{3,13},{4,8},{5,11},{6,10},{7,9},{8,4},{9,7},... | collective-permute-start | bytes 196616 | tf_op jit(solution)/shard_map/ppermute | solution.py:244
  26.2 0.7 %collective-permute-start.14 = (bf16[64,512]{1,0:T(8,128)(2,1)S(1)}, bf16[64,512]{1,0:T(8,128)(2,1)S(1)}, u32[]{:S(2)}, u32[]{:S(2)}) collective-permute-start(bf16[64,512]{1,0:T(8,128)(2,1)S(1)} %get-tuple-element.72), channel_id=1, source_target_pairs={{1,9},{0,10},{3,11},{2,8},{5,13},{4,14},{7,15},{6,12},{9,1},{8,2},... | collective-permute-start | bytes 196616 | tf_op jit(solution)/shard_map/ppermute | solution.py:244
  26.9 2.0 %collective-permute-start.16 = (bf16[64,512]{1,0:T(8,128)(2,1)S(1)}, bf16[64,512]{1,0:T(8,128)(2,1)S(1)}, u32[]{:S(2)}, u32[]{:S(2)}) collective-permute-start(bf16[64,512]{1,0:T(8,128)(2,1)S(1)} %get-tuple-element.73), channel_id=1, source_target_pairs={{1,5},{0,6},{3,7},{2,4},{5,1},{4,2},{7,3},{6,0},{9,13},{8,14},{11,... | collective-permute-start | bytes 196616 | tf_op jit(solution)/shard_map/ppermute | solution.py:244
  28.9 0.7 %collective-permute-start.18 = (bf16[64,512]{1,0:T(8,128)(2,1)S(1)}, bf16[64,512]{1,0:T(8,128)(2,1)S(1)}, u32[]{:S(2)}, u32[]{:S(2)}) collective-permute-start(bf16[64,512]{1,0:T(8,128)(2,1)S(1)} %get-tuple-element.74), channel_id=1, source_target_pairs={{0,0},{1,3},{2,2},{3,1},{4,4},{5,7},{6,6},{7,5},{8,8},{9,11},{10,1... | collective-permute-start | bytes 196616 | tf_op jit(solution)/shard_map/ppermute | solution.py:244
  29.6 0.9 %collective-permute-done.12.refs_0_ = bf16[64,512]{1,0:T(8,128)(2,1)S(1)} collective-permute-done((bf16[64,512]{1,0:T(8,128)(2,1)S(1)}, bf16[64,512]{1,0:T(8,128)(2,1)S(1)}, u32[]{:S(2)}, u32[]{:S(2)}) %collective-permute-start.12) | collective-permute-done | bytes 65568 | tf_op jit(solution)/shard_map/ppermute | solution.py:244
  30.5 0.0 collective-permute-start.13
  30.5 2.9 %collective-permute-done.14.refs_2_ = bf16[64,512]{1,0:T(8,128)(2,1)S(1)} collective-permute-done((bf16[64,512]{1,0:T(8,128)(2,1)S(1)}, bf16[64,512]{1,0:T(8,128)(2,1)S(1)}, u32[]{:S(2)}, u32[]{:S(2)}) %collective-permute-start.14) | collective-permute-done | bytes 65568 | tf_op jit(solution)/shard_map/ppermute | solution.py:244
  33.4 0.0 collective-permute-start.15
  33.4 0.0 collective-permute-done.16.refs_4_
  33.4 0.5 %collective-permute-start.17 = (bf16[32,512]{1,0:T(8,128)(2,1)S(1)}, bf16[32,512]{1,0:T(8,128)(2,1)S(1)}, u32[]{:S(2)}, u32[]{:S(2)}) collective-permute-start(bf16[32,512]{1,0:T(8,128)(2,1)S(1)} %slice.18), channel_id=1, source_target_pairs={{0,1},{1,0},{2,3},{3,2},{4,5},{5,4},{6,7},{7,6},{8,9},{9,8},{10,11... | collective-permute-start | bytes 98312 | tf_op jit(solution)/shard_map/ppermute | solution.py:236
  33.9 0.0 collective-permute-done.18.refs_6_
  33.9 0.1 collective-permute-start.19
  34.0 0.0 collective-permute-done.13.refs_1_
  34.0 0.6 %collective-permute-done.15.refs_3_ = bf16[32,512]{1,0:T(8,128)(2,1)S(1)} collective-permute-done((bf16[32,512]{1,0:T(8,128)(2,1)S(1)}, bf16[32,512]{1,0:T(8,128)(2,1)S(1)}, u32[]{:S(2)}, u32[]{:S(2)}) %collective-permute-start.15) | collective-permute-done | bytes 32800 | tf_op jit(solution)/shard_map/ppermute | solution.py:236
  34.6 0.2 collective-permute-done.17.refs_5_
  34.8 0.4 collective-permute-done.19.refs_7_
  35.1 0.0 collective-permute-done.11.got_ref
  35.1 0.0 copy-done.4
  35.1 0.0 copy-done.6
  35.1 1.8 %shard_map.96 = bf16[8,8,1024]{2,1,0:T(8,128)(2,1)} custom-call(s32[64]{0:T(128)S(1)} %bitcast.18, bf16[8,8,1024]{2,1,0:T(8,128)(2,1)S(1)} %copy-done.3, bf16[2,64,512]{2,1,0:T(8,128)(2,1)S(1)} %get-tuple-element.66.keep_ref, bf16[2,64,512]{2,1,0:T(8,128)(2,1)S(1)} %collective-permute-done.11.got_ref, bf16[512,1024]{1,0:T(8,128)(2,1)S(1)} %copy-done.4, ...), custom_call_target="tpu_custom_call" | custom-call | flops 268435456 | bytes 2097152 | tf_op jit(solution)/shard_map/pallas_call | solution.py:313
  (5 shorter events, 0.0 us)
Async XLA Ops:
  0.0 2.8 %collective-permute-start = (bf16[8,8,1024]{2,1,0:T(8,128)(2,1)}, bf16[8,8,1024]{2,1,0:T(8,128)(2,1)S(1)}, u32[]{:S(2)}, u32[]{:S(2)}) collective-permute-start(bf16[8,8,1024]{2,1,0:T(8,128)(2,1)} %own_ref.5), channel_id=1, source_target_pairs={{0,1},{1,0},{2,3},{3,2},{4,5},{5,4},{6,7},{7,6},{8,9},{9,8},{10,11... | collective-permute-start | bytes 393224 | tf_op jit(solution)/shard_map/ppermute | solution.py:236
  2.8 18.9 %collective-permute-start.9 = (bf16[512,1024]{1,0:T(8,128)(2,1)}, bf16[512,1024]{1,0:T(8,128)(2,1)S(1)}, u32[]{:S(2)}, u32[]{:S(2)}) collective-permute-start(bf16[512,1024]{1,0:T(8,128)(2,1)} %w_own_ref), channel_id=1, source_target_pairs={{0,1},{1,0},{2,3},{3,2},{4,5},{5,4},{6,7},{7,6},{8,9},{9,8},{10,11... | collective-permute-start | bytes 3145736 | tf_op jit(solution)/shard_map/ppermute | solution.py:236
  2.9 0.9 %copy-start.2 = (bf16[8,8,1024]{2,1,0:T(8,128)(2,1)S(1)}, bf16[8,8,1024]{2,1,0:T(8,128)(2,1)}, u32[]{:S(2)}) copy-start(bf16[8,8,1024]{2,1,0:T(8,128)(2,1)} %own_ref.5) | copy-start | bytes 393220
  4.1 14.0 %copy-start = (bf16[1,2048,512]{2,1,0:T(8,128)(2,1)S(1)}, bf16[1,2048,512]{2,1,0:T(8,128)(2,1)}, u32[]{:S(2)}) copy-start(bf16[1,2048,512]{2,1,0:T(8,128)(2,1)} %param.13) | copy-start | bytes 6291460
  4.1 14.0 %copy-start.1 = (bf16[1,2048,512]{2,1,0:T(8,128)(2,1)S(1)}, bf16[1,2048,512]{2,1,0:T(8,128)(2,1)}, u32[]{:S(2)}) copy-start(bf16[1,2048,512]{2,1,0:T(8,128)(2,1)} %param.14) | copy-start | bytes 6291460
  4.1 14.0 %copy-start.5 = (bf16[1024]{0:T(1024)(128)(2,1)S(1)}, bf16[1024]{0:T(1024)(128)(2,1)}, u32[]{:S(2)}) copy-start(bf16[1024]{0:T(1024)(128)(2,1)} %param.10) | copy-start | bytes 6148
  4.1 10.4 %collective-permute-start.1 = (bf16[32,1024]{1,0:T(8,128)(2,1)S(1)}, bf16[32,1024]{1,0:T(8,128)(2,1)S(1)}, u32[]{:S(2)}, u32[]{:S(2)}) collective-permute-start(bf16[32,1024]{1,0:T(8,128)(2,1)S(1)} %get-tuple-element.47), channel_id=1, source_target_pairs={{0,12},{1,15},{2,14},{3,13},{4,8},{5,11},{6,10},{7,9},{8,4},{9,7},... | collective-permute-start | bytes 196616 | tf_op jit(solution)/shard_map/ppermute | solution.py:244
  9.2 6.9 %collective-permute-start.2 = (bf16[32,1024]{1,0:T(8,128)(2,1)S(1)}, bf16[32,1024]{1,0:T(8,128)(2,1)S(1)}, u32[]{:S(2)}, u32[]{:S(2)}) collective-permute-start(bf16[32,1024]{1,0:T(8,128)(2,1)S(1)} %get-tuple-element.48), channel_id=1, source_target_pairs={{1,9},{0,10},{3,11},{2,8},{5,13},{4,14},{7,15},{6,12},{9,1},{8,2},... | collective-permute-start | bytes 196616 | tf_op jit(solution)/shard_map/ppermute | solution.py:244
  9.6 6.5 %collective-permute-start.3 = (bf16[32,1024]{1,0:T(8,128)(2,1)S(1)}, bf16[32,1024]{1,0:T(8,128)(2,1)S(1)}, u32[]{:S(2)}, u32[]{:S(2)}) collective-permute-start(bf16[32,1024]{1,0:T(8,128)(2,1)S(1)} %get-tuple-element.49), channel_id=1, source_target_pairs={{1,5},{0,6},{3,7},{2,4},{5,1},{4,2},{7,3},{6,0},{9,13},{8,14},{11,... | collective-permute-start | bytes 196616 | tf_op jit(solution)/shard_map/ppermute | solution.py:244
  10.8 5.4 %collective-permute-start.4 = (bf16[32,1024]{1,0:T(8,128)(2,1)S(1)}, bf16[32,1024]{1,0:T(8,128)(2,1)S(1)}, u32[]{:S(2)}, u32[]{:S(2)}) collective-permute-start(bf16[32,1024]{1,0:T(8,128)(2,1)S(1)} %get-tuple-element.50), channel_id=1, source_target_pairs={{0,0},{1,3},{2,2},{3,1},{4,4},{5,7},{6,6},{7,5},{8,8},{9,11},{10,1... | collective-permute-start | bytes 196616 | tf_op jit(solution)/shard_map/ppermute | solution.py:244
  16.2 1.3 %collective-permute-start.5 = (bf16[32,1024]{1,0:T(8,128)(2,1)S(1)}, bf16[32,1024]{1,0:T(8,128)(2,1)S(1)}, u32[]{:S(2)}, u32[]{:S(2)}) collective-permute-start(bf16[32,1024]{1,0:T(8,128)(2,1)S(1)} %collective-permute-done.1.refs_0_), channel_id=1, source_target_pairs={{0,1},{1,0},{2,3},{3,2},{4,5},{5,4},{6,7},{7,6},{8,9},{9,8},{10,11... | collective-permute-start | bytes 196616 | tf_op jit(solution)/shard_map/ppermute | solution.py:236
  16.2 1.4 %collective-permute-start.6 = (bf16[32,1024]{1,0:T(8,128)(2,1)S(1)}, bf16[32,1024]{1,0:T(8,128)(2,1)S(1)}, u32[]{:S(2)}, u32[]{:S(2)}) collective-permute-start(bf16[32,1024]{1,0:T(8,128)(2,1)S(1)} %collective-permute-done.2.refs_2_), channel_id=1, source_target_pairs={{0,1},{1,0},{2,3},{3,2},{4,5},{5,4},{6,7},{7,6},{8,9},{9,8},{10,11... | collective-permute-start | bytes 196616 | tf_op jit(solution)/shard_map/ppermute | solution.py:236
  16.7 1.3 %collective-permute-start.7 = (bf16[32,1024]{1,0:T(8,128)(2,1)S(1)}, bf16[32,1024]{1,0:T(8,128)(2,1)S(1)}, u32[]{:S(2)}, u32[]{:S(2)}) collective-permute-start(bf16[32,1024]{1,0:T(8,128)(2,1)S(1)} %collective-permute-done.3.refs_4_), channel_id=1, source_target_pairs={{0,1},{1,0},{2,3},{3,2},{4,5},{5,4},{6,7},{7,6},{8,9},{9,8},{10,11... | collective-permute-start | bytes 196616 | tf_op jit(solution)/shard_map/ppermute | solution.py:236
  16.7 1.4 %collective-permute-start.8 = (bf16[32,1024]{1,0:T(8,128)(2,1)S(1)}, bf16[32,1024]{1,0:T(8,128)(2,1)S(1)}, u32[]{:S(2)}, u32[]{:S(2)}) collective-permute-start(bf16[32,1024]{1,0:T(8,128)(2,1)S(1)} %collective-permute-done.4.refs_6_), channel_id=1, source_target_pairs={{0,1},{1,0},{2,3},{3,2},{4,5},{5,4},{6,7},{7,6},{8,9},{9,8},{10,11... | collective-permute-start | bytes 196616 | tf_op jit(solution)/shard_map/ppermute | solution.py:236
  18.1 4.1 %copy-start.3 = (bf16[8,8,1024]{2,1,0:T(8,128)(2,1)S(1)}, bf16[8,8,1024]{2,1,0:T(8,128)(2,1)}, u32[]{:S(2)}) copy-start(bf16[8,8,1024]{2,1,0:T(8,128)(2,1)} %own_ref.5) | copy-start | bytes 393220
  21.7 13.4 %copy-start.4 = (bf16[512,1024]{1,0:T(8,128)(2,1)S(1)}, bf16[512,1024]{1,0:T(8,128)(2,1)}, u32[]{:S(2)}) copy-start(bf16[512,1024]{1,0:T(8,128)(2,1)} %w_own_ref) | copy-start | bytes 3145732
  21.7 13.4 %copy-start.6 = (s32[64,1]{0,1:T(1,128)S(1)}, s32[64,1]{0,1:T(1,128)}, u32[]{:S(2)}) copy-start(s32[64,1]{0,1:T(1,128)} %param.15) | copy-start | bytes 772
  21.7 1.4 %collective-permute-start.10 = (bf16[128,512]{1,0:T(8,128)(2,1)S(1)}, bf16[128,512]{1,0:T(8,128)(2,1)S(1)}, u32[]{:S(2)}, u32[]{:S(2)}) collective-permute-start(bf16[128,512]{1,0:T(8,128)(2,1)S(1)} %get-tuple-element.62), channel_id=1, source_target_pairs={{0,1},{1,0},{2,3},{3,2},{4,5},{5,4},{6,7},{7,6},{8,9},{9,8},{10,11... | collective-permute-start | bytes 393224 | tf_op jit(solution)/shard_map/ppermute | solution.py:236
  23.2 12.0 %collective-permute-start.11 = (bf16[2,64,512]{2,1,0:T(8,128)(2,1)S(1)}, bf16[2,64,512]{2,1,0:T(8,128)(2,1)S(1)}, u32[]{:S(2)}, u32[]{:S(2)}) collective-permute-start(bf16[2,64,512]{2,1,0:T(8,128)(2,1)S(1)} %get-tuple-element.67), channel_id=1, source_target_pairs={{0,1},{1,0},{2,3},{3,2},{4,5},{5,4},{6,7},{7,6},{8,9},{9,8},{10,11... | collective-permute-start | bytes 393224 | tf_op jit(solution)/shard_map/ppermute | solution.py:236
  23.6 6.9 %collective-permute-start.12 = (bf16[64,512]{1,0:T(8,128)(2,1)S(1)}, bf16[64,512]{1,0:T(8,128)(2,1)S(1)}, u32[]{:S(2)}, u32[]{:S(2)}) collective-permute-start(bf16[64,512]{1,0:T(8,128)(2,1)S(1)} %get-tuple-element.71), channel_id=1, source_target_pairs={{0,12},{1,15},{2,14},{3,13},{4,8},{5,11},{6,10},{7,9},{8,4},{9,7},... | collective-permute-start | bytes 196616 | tf_op jit(solution)/shard_map/ppermute | solution.py:244
  26.2 7.2 %collective-permute-start.14 = (bf16[64,512]{1,0:T(8,128)(2,1)S(1)}, bf16[64,512]{1,0:T(8,128)(2,1)S(1)}, u32[]{:S(2)}, u32[]{:S(2)}) collective-permute-start(bf16[64,512]{1,0:T(8,128)(2,1)S(1)} %get-tuple-element.72), channel_id=1, source_target_pairs={{1,9},{0,10},{3,11},{2,8},{5,13},{4,14},{7,15},{6,12},{9,1},{8,2},... | collective-permute-start | bytes 196616 | tf_op jit(solution)/shard_map/ppermute | solution.py:244
  26.9 6.5 %collective-permute-start.16 = (bf16[64,512]{1,0:T(8,128)(2,1)S(1)}, bf16[64,512]{1,0:T(8,128)(2,1)S(1)}, u32[]{:S(2)}, u32[]{:S(2)}) collective-permute-start(bf16[64,512]{1,0:T(8,128)(2,1)S(1)} %get-tuple-element.73), channel_id=1, source_target_pairs={{1,5},{0,6},{3,7},{2,4},{5,1},{4,2},{7,3},{6,0},{9,13},{8,14},{11,... | collective-permute-start | bytes 196616 | tf_op jit(solution)/shard_map/ppermute | solution.py:244
  28.9 5.0 %collective-permute-start.18 = (bf16[64,512]{1,0:T(8,128)(2,1)S(1)}, bf16[64,512]{1,0:T(8,128)(2,1)S(1)}, u32[]{:S(2)}, u32[]{:S(2)}) collective-permute-start(bf16[64,512]{1,0:T(8,128)(2,1)S(1)} %get-tuple-element.74), channel_id=1, source_target_pairs={{0,0},{1,3},{2,2},{3,1},{4,4},{5,7},{6,6},{7,5},{8,8},{9,11},{10,1... | collective-permute-start | bytes 196616 | tf_op jit(solution)/shard_map/ppermute | solution.py:244
  30.5 3.5 %collective-permute-start.13 = (bf16[32,512]{1,0:T(8,128)(2,1)S(1)}, bf16[32,512]{1,0:T(8,128)(2,1)S(1)}, u32[]{:S(2)}, u32[]{:S(2)}) collective-permute-start(bf16[32,512]{1,0:T(8,128)(2,1)S(1)} %slice.16), channel_id=1, source_target_pairs={{0,1},{1,0},{2,3},{3,2},{4,5},{5,4},{6,7},{7,6},{8,9},{9,8},{10,11... | collective-permute-start | bytes 98312 | tf_op jit(solution)/shard_map/ppermute | solution.py:236
  33.4 1.2 %collective-permute-start.15 = (bf16[32,512]{1,0:T(8,128)(2,1)S(1)}, bf16[32,512]{1,0:T(8,128)(2,1)S(1)}, u32[]{:S(2)}, u32[]{:S(2)}) collective-permute-start(bf16[32,512]{1,0:T(8,128)(2,1)S(1)} %slice.17), channel_id=1, source_target_pairs={{0,1},{1,0},{2,3},{3,2},{4,5},{5,4},{6,7},{7,6},{8,9},{9,8},{10,11... | collective-permute-start | bytes 98312 | tf_op jit(solution)/shard_map/ppermute | solution.py:236
  33.4 1.4 %collective-permute-start.17 = (bf16[32,512]{1,0:T(8,128)(2,1)S(1)}, bf16[32,512]{1,0:T(8,128)(2,1)S(1)}, u32[]{:S(2)}, u32[]{:S(2)}) collective-permute-start(bf16[32,512]{1,0:T(8,128)(2,1)S(1)} %slice.18), channel_id=1, source_target_pairs={{0,1},{1,0},{2,3},{3,2},{4,5},{5,4},{6,7},{7,6},{8,9},{9,8},{10,11... | collective-permute-start | bytes 98312 | tf_op jit(solution)/shard_map/ppermute | solution.py:236
  33.9 1.2 %collective-permute-start.19 = (bf16[32,512]{1,0:T(8,128)(2,1)S(1)}, bf16[32,512]{1,0:T(8,128)(2,1)S(1)}, u32[]{:S(2)}, u32[]{:S(2)}) collective-permute-start(bf16[32,512]{1,0:T(8,128)(2,1)S(1)} %slice.19), channel_id=1, source_target_pairs={{0,1},{1,0},{2,3},{3,2},{4,5},{5,4},{6,7},{7,6},{8,9},{9,8},{10,11... | collective-permute-start | bytes 98312 | tf_op jit(solution)/shard_map/ppermute | solution.py:236

commit v13 on v12

--- a/solution.py
+++ b/solution.py
@@ -75,26 +75,24 @@
     return slots
 
 
-def front_kernel(owners, half_cands, facts_ref, hide_rows_ref, hide_cols_ref, chosen_ref, marks_ref):
-    me, serve = lax.axis_index("cache"), lax.axis_index("serve")
-    blocks, requests = facts_ref.shape[0] - 2, facts_ref.shape[1]
-    per_owner = requests // owners
-    rows = per_owner * half_cands
-    hist_rows = hide_cols_ref.shape[0]
-    at_row = lax.broadcasted_iota(jnp.int32, (hist_rows, HD), 0)
-    at_lane = lax.broadcasted_iota(jnp.int32, (hist_rows, HD), 1)
-    in_block = at_lane == at_row // BLK
-    marks_ref[...] = jnp.zeros_like(marks_ref)
-
-    sessions = facts_ref[blocks : blocks + 1, :]
-    lane = lax.broadcasted_iota(jnp.int32, (1, requests), 1)
-    place = jnp.zeros((1, requests), jnp.int32)
+def places(sessions, per_owner):
+    lane = lax.broadcasted_iota(jnp.int32, sessions.shape, 1)
+    place = jnp.zeros_like(sessions)
     for back in range(1, per_owner):
         same = (pltpu.roll(sessions, back, 1) == sessions) & (lane % per_owner >= back)
         place = place + same.astype(jnp.int32)
-
+    return place
+
+
+def front_kernel(owners, half_cands, sess_ref, chosen_ref):
+    me, serve = lax.axis_index("cache"), lax.axis_index("serve")
+    sessions = sess_ref[...]
+    requests = sessions.shape[1]
+    per_owner = requests // owners
+    rows = per_owner * half_cands
     distance = sessions ^ me
-    code = jnp.where(core_of(distance) == serve, (distance // 2) * (2 * CAP) + place, owners * CAP)
+    first = distance // 2 * (2 * CAP)
+    code = jnp.where(core_of(distance) == serve, first + places(sessions, per_owner), owners * CAP)
     request = lax.broadcasted_iota(jnp.int32, (requests, 2 * rows), 0)
     column = lax.broadcasted_iota(jnp.int32, (requests, 2 * rows), 1)
     spread = (request == me * per_owner + (column % rows) // half_cands).astype(jnp.float32).astype(jnp.bfloat16)
@@ -105,20 +103,35 @@
     hit = (at // half_cands == target + (column // rows) * CAP) & (at % half_cands == column % half_cands)
     chosen_ref[...] = hit.astype(jnp.float32).astype(jnp.bfloat16)
 
+
+def visible_kernel(sess_ref, len_ref, mask_ref, hide_rows_ref, hide_cols_ref, marks_ref):
+    me, serve = lax.axis_index("cache"), lax.axis_index("serve")
+    blocks, requests = mask_ref.shape
+    owners = len_ref.shape[1]
+    per_owner = requests // owners
+    sessions = sess_ref[...]
+    lane = lax.broadcasted_iota(jnp.int32, (1, requests), 1)
     at = position((lane // per_owner) ^ me, serve, owners)
-    slot_of = jnp.where(sessions == me, at * CAP + place, -1)
+    slot_of = jnp.where(sessions == me, at * CAP + places(sessions, per_owner), -1)
     slots = owners * CAP
     at_slot = lax.broadcasted_iota(jnp.int32, (slots, requests), 0)
     taken = (at_slot == slot_of).astype(jnp.float32).astype(jnp.bfloat16)
-    marks_ref[:blocks, :] = facts_ref[:blocks, :].astype(jnp.float32).astype(jnp.bfloat16)
+    marks_ref[...] = jnp.zeros_like(marks_ref)
+    marks_ref[:blocks, :] = mask_ref[...].astype(jnp.float32).astype(jnp.bfloat16)
     seen = lax.dot_general(taken, marks_ref[...], (((1,), (1,)), ((), ())), preferred_element_type=jnp.float32)
     slot_lane = lax.broadcasted_iota(jnp.int32, (slots, HD), 1)
     hidden = jnp.where(slot_lane < blocks, (1.0 - seen) * HIDE, jnp.where(slot_lane == blocks, HIDE, 0.0))
-    wide = jnp.broadcast_to(hidden.reshape(owners, 1, CAP, 1, HD), (owners, 2, CAP, half_cands, HD))
+    half = hide_rows_ref.shape[0] // slots // 2
+    wide = jnp.broadcast_to(hidden.reshape(owners, 1, CAP, 1, HD), (owners, 2, CAP, half, HD))
     hide_rows_ref[...] = wide.reshape(hide_rows_ref.shape).astype(jnp.bfloat16)
-    lengths = facts_ref[blocks + 1 : blocks + 2, :]
-    length = jnp.sum(jnp.where(lane == me, lengths, 0), axis=1, keepdims=True)
-    hide_cols_ref[...] = jnp.where(in_block | ((at_lane == blocks) & (at_row >= length)), 1.0, 0.0).astype(jnp.bfloat16)
+    hist_rows = hide_cols_ref.shape[0]
+    owner_lane = lax.broadcasted_iota(jnp.int32, (1, owners), 1)
+    length = jnp.sum(jnp.where(owner_lane == me, len_ref[...], 0), axis=1, keepdims=True)
+    at_row = lax.broadcasted_iota(jnp.int32, (hist_rows, HD), 0)
+    at_lane = lax.broadcasted_iota(jnp.int32, (hist_rows, HD), 1)
+    hide_cols_ref[...] = jnp.where(
+        (at_lane == at_row // BLK) | ((at_lane == blocks) & (at_row >= length)), 1.0, 0.0
+    ).astype(jnp.bfloat16)
 
 
 def message_kernel(chosen_ref, own_ref, other_ref, *out_refs):
@@ -258,29 +271,25 @@
     piece = 2 * CAP * half_cands
     half_table = bf16((messages * piece, width))
 
-    facts = jnp.concatenate(
-        [
-            block_mask.T,
-            request_session.reshape(1, -1),
-            jnp.pad(hist_len, (0, owners * (req_count - 1))).reshape(1, -1),
-        ],
-        axis=0,
-    )
-    hide_rows, hide_cols, chosen = kernel_call(
+    session_row = request_session.reshape(1, -1)
+    chosen = kernel_call(
         functools.partial(front_kernel, owners, half_cands),
-        [bf16((owners * piece, HD)), bf16((hist_rows, HD)), bf16((messages * piece, 2 * rows))],
+        bf16((messages * piece, 2 * rows)),
         [vmem],
-        [pltpu.VMEM((HD, owners * req_count), jnp.bfloat16)],
-        flops=8 * messages * piece * model_width * width,
-        moved=2 * hist_rows * HD,
-    )(facts)
+    )(session_row)
     other, w_out, chosen = lax.optimization_barrier((swap(candidates), w_out, chosen))
     w_other = swap(w_out)
     out = kernel_call(message_kernel, [bf16((piece, model_width))] * messages, [vmem] * 3)(chosen, candidates, other)
     out, w_in = lax.optimization_barrier((out, w_in))
     weights = jnp.transpose(w_in, (1, 0, 2))
     came = cross(owners, out)
-    came, weights = lax.optimization_barrier((came, weights))
+    visible = kernel_call(
+        visible_kernel,
+        [bf16((owners * piece, HD)), bf16((hist_rows, HD))],
+        [vmem] * 3,
+        [pltpu.VMEM((HD, owners * req_count), jnp.bfloat16)],
+    )(session_row, hist_len.reshape(1, -1), lax.optimization_barrier((block_mask.T, out))[0])
+    came, weights, (hide_rows, hide_cols) = lax.optimization_barrier((came, weights, visible))
     swapped = [swap(message) for message in came]
     keep, give = kernel_call(
         functools.partial(history_kernel, owners),

time: 37.2 us -> 37.2 us (level)
  other arithmetic: 0.74 us -> 0 us
  Pallas kernels: 7.51 us -> 7.95 us
  starting transfers between devices: 16.3 us -> 16.7 us
    ppermute x8, waiting for transfers between devices: 5.5 us -> 4.66 us  [cross(): came.append(lax.ppermute(messages[at], ('cache', 'serve'), pairs))]
    concatenate x1 -> x0, other arithmetic: 0.74 us -> none  [body(): jnp.concatenate([block_mask.T, request_session.reshape(1, -1), jnp.pad(hi...]
    ppermute x12, starting transfers between devices: 3 us -> 3.68 us  [swap(): return lax.ppermute(rows, 'serve', [(0, 1), (1, 0)])]
    unnamed x14 -> x20, local copies, waits for them, and re-layouts: 0.94 us -> 1.61 us
    reshape x1 -> x0, local copies, waits for them, and re-layouts: 0.66 us -> none  [body(): jnp.pad(hist_len, (0, owners * (req_count - 1))).reshape(1, -1)]
    ppermute x12, waiting for transfers between devices: 2.11 us -> 2.73 us  [swap(): return lax.ppermute(rows, 'serve', [(0, 1), (1, 0)])]
    pallas_call x1 -> x2, Pallas kernels: 0.95 us -> 1.36 us  [the longest x1 0.95 us: body(): kernel_call(visible_kernel, [bf16((owners * piece, HD)), bf16((hist_rows,...]
  transfers between devices with their start and end apart: 20 -> 20, of which waited for: 11 -> 12; matrix products, arithmetic and copies ran while one was open for 12% -> 9% of each run, Pallas kernels for 15% -> 17%
where the time goes in v13:
time: 37.2 us; the launch traced here: 37 us
  starting transfers between devices  16.7 us (45%)
  Pallas kernels  7.95 us (21%)
  waiting for transfers between devices  7.39 us (20%)
  local copies, waits for them, and re-layouts  4.8 us (13%)
    ppermute x8, starting transfers between devices, cross(): came.append(lax.ppermute(messages[at], ('cache', 'serve'), pairs))  13 us
    ppermute x8, waiting for transfers between devices, cross(): came.append(lax.ppermute(messages[at], ('cache', 'serve'), pairs))  4.66 us
    ppermute x12, starting transfers between devices, swap(): return lax.ppermute(rows, 'serve', [(0, 1), (1, 0)])  3.68 us
    pallas_call x1, Pallas kernels, body(): kernel_call(functools.partial(history_kernel, owners), [half_table] * 2,...  3.65 us
    optimization_barrier x1, local copies, waits for them, and re-layouts, body(): out, w_in = lax.optimization_barrier((out, w_in))  3.18 us
    ppermute x12, waiting for transfers between devices, swap(): return lax.ppermute(rows, 'serve', [(0, 1), (1, 0)])  2.73 us
    pallas_call x1, Pallas kernels, body(): kernel_call(functools.partial(output_kernel, messages), bf16((req_count,...  1.84 us
    unnamed x20, local copies, waits for them, and re-layouts  1.61 us
  transfers between devices with their start and end apart: 20, of which 12 were waited for; matrix products, arithmetic and copies ran while one was open for 9% of the time, Pallas kernels for 17%

profile of v13, /device:TPU:0, one launch (start us, length us, event | category | flops | bytes accessed | tf_op | source)
XLA Modules:
  0.0 37.0 jit_solution(6784166836217241166)
XLA Ops:
  0.0 0.5 %collective-permute-start = (bf16[8,8,1024]{2,1,0:T(8,128)(2,1)}, bf16[8,8,1024]{2,1,0:T(8,128)(2,1)S(1)}, u32[]{:S(2)}, u32[]{:S(2)}) collective-permute-start(bf16[8,8,1024]{2,1,0:T(8,128)(2,1)} %own_ref.5), channel_id=1, source_target_pairs={{0,1},{1,0},{2,3},{3,2},{4,5},{5,4},{6,7},{7,6},{8,9},{9,8},{10,11... | collective-permute-start | bytes 393224 | tf_op jit(solution)/shard_map/ppermute | solution.py:249
  0.5 0.7 %copy-done.7 = s32[64,1]{0,1:T(1,128)S(1)} copy-done((s32[64,1]{0,1:T(1,128)S(1)}, s32[64,1]{0,1:T(1,128)}, u32[]{:S(2)}) %copy-start.7) | copy-done | bytes 280
  1.1 0.4 %shard_map.91.chosen_ref = bf16[128,128]{1,0:T(8,128)(2,1)S(1)} custom-call(s32[1,64]{1,0:T(1,128)S(1)} %bitcast.17), custom_call_target="tpu_custom_call" | custom-call | tf_op jit(solution)/shard_map/pallas_call | solution.py:275
  1.5 0.1 collective-permute-done.other_ref
  1.7 0.4 collective-permute-start.9
  2.0 0.9 %copy-done.2 = bf16[8,8,1024]{2,1,0:T(8,128)(2,1)S(1)} copy-done((bf16[8,8,1024]{2,1,0:T(8,128)(2,1)S(1)}, bf16[8,8,1024]{2,1,0:T(8,128)(2,1)}, u32[]{:S(2)}) %copy-start.2) | copy-done | bytes 131096
  2.9 0.2 shard_map.92
  3.1 4.8 %collective-permute-start.1 = (bf16[32,1024]{1,0:T(8,128)(2,1)S(1)}, bf16[32,1024]{1,0:T(8,128)(2,1)S(1)}, u32[]{:S(2)}, u32[]{:S(2)}) collective-permute-start(bf16[32,1024]{1,0:T(8,128)(2,1)S(1)} %get-tuple-element.48), channel_id=1, source_target_pairs={{0,12},{1,15},{2,14},{3,13},{4,8},{5,11},{6,10},{7,9},{8,4},{9,7},... | collective-permute-start | bytes 196616 | tf_op jit(solution)/shard_map/ppermute | solution.py:257
  7.9 0.4 %collective-permute-start.2 = (bf16[32,1024]{1,0:T(8,128)(2,1)S(1)}, bf16[32,1024]{1,0:T(8,128)(2,1)S(1)}, u32[]{:S(2)}, u32[]{:S(2)}) collective-permute-start(bf16[32,1024]{1,0:T(8,128)(2,1)S(1)} %get-tuple-element.49), channel_id=1, source_target_pairs={{1,9},{0,10},{3,11},{2,8},{5,13},{4,14},{7,15},{6,12},{9,1},{8,2},... | collective-permute-start | bytes 196616 | tf_op jit(solution)/shard_map/ppermute | solution.py:257
  8.3 1.1 %collective-permute-start.3 = (bf16[32,1024]{1,0:T(8,128)(2,1)S(1)}, bf16[32,1024]{1,0:T(8,128)(2,1)S(1)}, u32[]{:S(2)}, u32[]{:S(2)}) collective-permute-start(bf16[32,1024]{1,0:T(8,128)(2,1)S(1)} %get-tuple-element.50), channel_id=1, source_target_pairs={{1,5},{0,6},{3,7},{2,4},{5,1},{4,2},{7,3},{6,0},{9,13},{8,14},{11,... | collective-permute-start | bytes 196616 | tf_op jit(solution)/shard_map/ppermute | solution.py:257
  9.5 0.7 %collective-permute-start.4 = (bf16[32,1024]{1,0:T(8,128)(2,1)S(1)}, bf16[32,1024]{1,0:T(8,128)(2,1)S(1)}, u32[]{:S(2)}, u32[]{:S(2)}) collective-permute-start(bf16[32,1024]{1,0:T(8,128)(2,1)S(1)} %get-tuple-element.51), channel_id=1, source_target_pairs={{0,0},{1,3},{2,2},{3,1},{4,4},{5,7},{6,6},{7,5},{8,8},{9,11},{10,1... | collective-permute-start | bytes 196616 | tf_op jit(solution)/shard_map/ppermute | solution.py:257
  10.1 0.0 copy-start.5
  10.2 0.0 copy-start.8
  10.2 0.0 copy-start.9
  10.2 0.0 copy-start
  10.2 0.0 copy-start.1
  10.2 0.0 copy-start.6
  10.2 3.2 %copy.12 = bf16[1024,4,512]{2,0,1:T(8,128)(2,1)S(1)} copy(bf16[1024,4,512]{2,1,0:T(4,128)(2,1)} %param.11) | data formatting | bytes 8388608 | tf_op jit(solution)/shard_map/optimization_barrier | solution.py:283
  13.4 0.0 copy-done.5
  13.4 0.0 copy-done.8
  13.4 0.0 copy-done.9
  13.4 1.0 %shard_map.93 = (bf16[256,128]{1,0:T(8,128)(2,1)S(1)}, bf16[2048,128]{1,0:T(8,128)(2,1)S(1)}) custom-call(s32[1,64]{1,0:T(1,128)S(1)} %bitcast.18, s32[1,8]{1,0:T(1,128)S(1)} %bitcast.20, s32[32,64]{1,0:T(8,128)S(1)} %bitcast.14), custom_call_target="tpu_custom_call" | custom-call | tf_op jit(solution)/shard_map/pallas_call | solution.py:286
  14.4 0.0 collective-permute-done.1.refs_0_
  14.4 0.5 %collective-permute-done.2.refs_2_ = bf16[32,1024]{1,0:T(8,128)(2,1)S(1)} collective-permute-done((bf16[32,1024]{1,0:T(8,128)(2,1)S(1)}, bf16[32,1024]{1,0:T(8,128)(2,1)S(1)}, u32[]{:S(2)}, u32[]{:S(2)}) %collective-permute-start.2) | collective-permute-done | bytes 65568 | tf_op jit(solution)/shard_map/ppermute | solution.py:257
  15.0 0.0 collective-permute-done.3.refs_4_
  15.0 0.0 collective-permute-done.4.refs_6_
  15.0 0.9 %collective-permute-start.5 = (bf16[32,1024]{1,0:T(8,128)(2,1)S(1)}, bf16[32,1024]{1,0:T(8,128)(2,1)S(1)}, u32[]{:S(2)}, u32[]{:S(2)}) collective-permute-start(bf16[32,1024]{1,0:T(8,128)(2,1)S(1)} %collective-permute-done.1.refs_0_), channel_id=1, source_target_pairs={{0,1},{1,0},{2,3},{3,2},{4,5},{5,4},{6,7},{7,6},{8,9},{9,8},{10,11... | collective-permute-start | bytes 196616 | tf_op jit(solution)/shard_map/ppermute | solution.py:249
  15.9 0.1 collective-permute-start.6
  16.0 0.4 %collective-permute-start.7 = (bf16[32,1024]{1,0:T(8,128)(2,1)S(1)}, bf16[32,1024]{1,0:T(8,128)(2,1)S(1)}, u32[]{:S(2)}, u32[]{:S(2)}) collective-permute-start(bf16[32,1024]{1,0:T(8,128)(2,1)S(1)} %collective-permute-done.3.refs_4_), channel_id=1, source_target_pairs={{0,1},{1,0},{2,3},{3,2},{4,5},{5,4},{6,7},{7,6},{8,9},{9,8},{10,11... | collective-permute-start | bytes 196616 | tf_op jit(solution)/shard_map/ppermute | solution.py:249
  16.4 0.1 collective-permute-start.8
  16.5 0.3 collective-permute-done.5.refs_1_
  16.8 0.4 collective-permute-done.6.refs_3_
  17.1 0.2 collective-permute-done.7.refs_5_
  17.3 0.4 collective-permute-done.8.refs_7_
  17.7 0.0 copy-done
  17.7 0.0 copy-done.1
  17.7 0.0 copy-done.6
  17.7 0.0 copy-start.3
  17.7 3.7 %shard_map.94 = (bf16[128,512]{1,0:T(8,128)(2,1)S(1)}, bf16[128,512]{1,0:T(8,128)(2,1)S(1)}) custom-call(bf16[8,128]{1,0:T(8,128)(2,1)S(1)} %bitcast.15, bf16[4,1024,512]{2,1,0:T(8,128)(2,1)S(1)} %bitcast.10, bf16[256,128]{1,0:T(8,128)(2,1)S(1)} %get-tuple-element.57.hide_rows_ref, bf16[2048,128]{1,0:T(8,128)(2,1)S(1)} %get-tuple-element.58.hide_cols_ref, ...), custom_call_target="tpu_custom_call" | custom-call | flops 2147483648 | bytes 4194304 | tf_op jit(solution)/shard_map/pallas_call | solution.py:294
  21.3 0.0 copy-start.4
  21.4 0.0 collective-permute-done.9.w_other_ref
  21.4 0.2 collective-permute-start.10
  21.6 0.0 copy-done.3
  21.6 0.9 %shard_map.95 = (bf16[2,64,512]{2,1,0:T(8,128)(2,1)S(1)}, bf16[2,64,512]{2,1,0:T(8,128)(2,1)S(1)}) custom-call(bf16[8,8,1024]{2,1,0:T(8,128)(2,1)S(1)} %copy-done.3, bf16[8,8,1024]{2,1,0:T(8,128)(2,1)S(1)} %collective-permute-done.other_ref, bf16[8,128]{1,0:T(8,128)(2,1)S(1)} %bitcast.16, bf16[4,1024,512]{2,1,0:T(8,128)(2,1)S(1)} %bitcast.11), custom_call_target="tpu_custom_call" | custom-call | flops 536870912 | bytes 4194304 | tf_op jit(solution)/shard_map/pallas_call | solution.py:311
  22.5 0.3 collective-permute-done.10.got_ref
  22.8 0.1 collective-permute-start.11
  23.0 3.5 %collective-permute-start.12 = (bf16[64,512]{1,0:T(8,128)(2,1)S(1)}, bf16[64,512]{1,0:T(8,128)(2,1)S(1)}, u32[]{:S(2)}, u32[]{:S(2)}) collective-permute-start(bf16[64,512]{1,0:T(8,128)(2,1)S(1)} %get-tuple-element.75), channel_id=1, source_target_pairs={{0,12},{1,15},{2,14},{3,13},{4,8},{5,11},{6,10},{7,9},{8,4},{9,7},... | collective-permute-start | bytes 196616 | tf_op jit(solution)/shard_map/ppermute | solution.py:257
  26.4 0.3 collective-permute-start.14
  26.8 1.5 %collective-permute-start.16 = (bf16[64,512]{1,0:T(8,128)(2,1)S(1)}, bf16[64,512]{1,0:T(8,128)(2,1)S(1)}, u32[]{:S(2)}, u32[]{:S(2)}) collective-permute-start(bf16[64,512]{1,0:T(8,128)(2,1)S(1)} %get-tuple-element.77), channel_id=1, source_target_pairs={{1,5},{0,6},{3,7},{2,4},{5,1},{4,2},{7,3},{6,0},{9,13},{8,14},{11,... | collective-permute-start | bytes 196616 | tf_op jit(solution)/shard_map/ppermute | solution.py:257
  28.3 0.7 %collective-permute-start.18 = (bf16[64,512]{1,0:T(8,128)(2,1)S(1)}, bf16[64,512]{1,0:T(8,128)(2,1)S(1)}, u32[]{:S(2)}, u32[]{:S(2)}) collective-permute-start(bf16[64,512]{1,0:T(8,128)(2,1)S(1)} %get-tuple-element.78), channel_id=1, source_target_pairs={{0,0},{1,3},{2,2},{3,1},{4,4},{5,7},{6,6},{7,5},{8,8},{9,11},{10,1... | collective-permute-start | bytes 196616 | tf_op jit(solution)/shard_map/ppermute | solution.py:257
  29.0 0.8 %collective-permute-done.12.refs_0_ = bf16[64,512]{1,0:T(8,128)(2,1)S(1)} collective-permute-done((bf16[64,512]{1,0:T(8,128)(2,1)S(1)}, bf16[64,512]{1,0:T(8,128)(2,1)S(1)}, u32[]{:S(2)}, u32[]{:S(2)}) %collective-permute-start.12) | collective-permute-done | bytes 65568 | tf_op jit(solution)/shard_map/ppermute | solution.py:257
  29.7 0.4 collective-permute-start.13
  30.1 3.3 %collective-permute-done.14.refs_2_ = bf16[64,512]{1,0:T(8,128)(2,1)S(1)} collective-permute-done((bf16[64,512]{1,0:T(8,128)(2,1)S(1)}, bf16[64,512]{1,0:T(8,128)(2,1)S(1)}, u32[]{:S(2)}, u32[]{:S(2)}) %collective-permute-start.14) | collective-permute-done | bytes 65568 | tf_op jit(solution)/shard_map/ppermute | solution.py:257
  33.4 0.0 collective-permute-start.15
  33.4 0.0 collective-permute-done.16.refs_4_
  33.5 0.5 %collective-permute-start.17 = (bf16[32,512]{1,0:T(8,128)(2,1)S(1)}, bf16[32,512]{1,0:T(8,128)(2,1)S(1)}, u32[]{:S(2)}, u32[]{:S(2)}) collective-permute-start(bf16[32,512]{1,0:T(8,128)(2,1)S(1)} %slice.18), channel_id=1, source_target_pairs={{0,1},{1,0},{2,3},{3,2},{4,5},{5,4},{6,7},{7,6},{8,9},{9,8},{10,11... | collective-permute-start | bytes 98312 | tf_op jit(solution)/shard_map/ppermute | solution.py:249
  34.0 0.0 collective-permute-done.18.refs_6_
  34.0 0.1 collective-permute-start.19
  34.1 0.0 collective-permute-done.13.refs_1_
  34.1 0.6 %collective-permute-done.15.refs_3_ = bf16[32,512]{1,0:T(8,128)(2,1)S(1)} collective-permute-done((bf16[32,512]{1,0:T(8,128)(2,1)S(1)}, bf16[32,512]{1,0:T(8,128)(2,1)S(1)}, u32[]{:S(2)}, u32[]{:S(2)}) %collective-permute-start.15) | collective-permute-done | bytes 32800 | tf_op jit(solution)/shard_map/ppermute | solution.py:249
  34.7 0.2 collective-permute-done.17.refs_5_
  34.8 0.4 collective-permute-done.19.refs_7_
  35.2 0.0 collective-permute-done.11.got_ref
  35.2 1.8 %shard_map.97 = bf16[8,8,1024]{2,1,0:T(8,128)(2,1)} custom-call(s32[64]{0:T(128)S(1)} %bitcast.19, bf16[8,8,1024]{2,1,0:T(8,128)(2,1)S(1)} %copy-done.3, bf16[2,64,512]{2,1,0:T(8,128)(2,1)S(1)} %get-tuple-element.70.keep_ref, bf16[2,64,512]{2,1,0:T(8,128)(2,1)S(1)} %collective-permute-done.11.got_ref, bf16[512,1024]{1,0:T(8,128)(2,1)S(1)} %copy-done.4, ...), custom_call_target="tpu_custom_call" | custom-call | flops 268435456 | bytes 2097152 | tf_op jit(solution)/shard_map/pallas_call | solution.py:322
  (8 shorter events, 0.0 us)
Async XLA Ops:
  0.0 1.6 %collective-permute-start = (bf16[8,8,1024]{2,1,0:T(8,128)(2,1)}, bf16[8,8,1024]{2,1,0:T(8,128)(2,1)S(1)}, u32[]{:S(2)}, u32[]{:S(2)}) collective-permute-start(bf16[8,8,1024]{2,1,0:T(8,128)(2,1)} %own_ref.5), channel_id=1, source_target_pairs={{0,1},{1,0},{2,3},{3,2},{4,5},{5,4},{6,7},{7,6},{8,9},{9,8},{10,11... | collective-permute-start | bytes 393224 | tf_op jit(solution)/shard_map/ppermute | solution.py:249
  0.5 0.7 %copy-start.7 = (s32[64,1]{0,1:T(1,128)S(1)}, s32[64,1]{0,1:T(1,128)}, u32[]{:S(2)}) copy-start(s32[64,1]{0,1:T(1,128)} %param.15) | copy-start | bytes 772
  1.7 19.7 %collective-permute-start.9 = (bf16[512,1024]{1,0:T(8,128)(2,1)}, bf16[512,1024]{1,0:T(8,128)(2,1)S(1)}, u32[]{:S(2)}, u32[]{:S(2)}) collective-permute-start(bf16[512,1024]{1,0:T(8,128)(2,1)} %w_own_ref), channel_id=1, source_target_pairs={{0,1},{1,0},{2,3},{3,2},{4,5},{5,4},{6,7},{7,6},{8,9},{9,8},{10,11... | collective-permute-start | bytes 3145736 | tf_op jit(solution)/shard_map/ppermute | solution.py:249
  2.0 0.9 %copy-start.2 = (bf16[8,8,1024]{2,1,0:T(8,128)(2,1)S(1)}, bf16[8,8,1024]{2,1,0:T(8,128)(2,1)}, u32[]{:S(2)}) copy-start(bf16[8,8,1024]{2,1,0:T(8,128)(2,1)} %own_ref.5) | copy-start | bytes 393220
  3.1 11.3 %collective-permute-start.1 = (bf16[32,1024]{1,0:T(8,128)(2,1)S(1)}, bf16[32,1024]{1,0:T(8,128)(2,1)S(1)}, u32[]{:S(2)}, u32[]{:S(2)}) collective-permute-start(bf16[32,1024]{1,0:T(8,128)(2,1)S(1)} %get-tuple-element.48), channel_id=1, source_target_pairs={{0,12},{1,15},{2,14},{3,13},{4,8},{5,11},{6,10},{7,9},{8,4},{9,7},... | collective-permute-start | bytes 196616 | tf_op jit(solution)/shard_map/ppermute | solution.py:257
  7.9 7.0 %collective-permute-start.2 = (bf16[32,1024]{1,0:T(8,128)(2,1)S(1)}, bf16[32,1024]{1,0:T(8,128)(2,1)S(1)}, u32[]{:S(2)}, u32[]{:S(2)}) collective-permute-start(bf16[32,1024]{1,0:T(8,128)(2,1)S(1)} %get-tuple-element.49), channel_id=1, source_target_pairs={{1,9},{0,10},{3,11},{2,8},{5,13},{4,14},{7,15},{6,12},{9,1},{8,2},... | collective-permute-start | bytes 196616 | tf_op jit(solution)/shard_map/ppermute | solution.py:257
  8.3 6.6 %collective-permute-start.3 = (bf16[32,1024]{1,0:T(8,128)(2,1)S(1)}, bf16[32,1024]{1,0:T(8,128)(2,1)S(1)}, u32[]{:S(2)}, u32[]{:S(2)}) collective-permute-start(bf16[32,1024]{1,0:T(8,128)(2,1)S(1)} %get-tuple-element.50), channel_id=1, source_target_pairs={{1,5},{0,6},{3,7},{2,4},{5,1},{4,2},{7,3},{6,0},{9,13},{8,14},{11,... | collective-permute-start | bytes 196616 | tf_op jit(solution)/shard_map/ppermute | solution.py:257
  9.5 5.5 %collective-permute-start.4 = (bf16[32,1024]{1,0:T(8,128)(2,1)S(1)}, bf16[32,1024]{1,0:T(8,128)(2,1)S(1)}, u32[]{:S(2)}, u32[]{:S(2)}) collective-permute-start(bf16[32,1024]{1,0:T(8,128)(2,1)S(1)} %get-tuple-element.51), channel_id=1, source_target_pairs={{0,0},{1,3},{2,2},{3,1},{4,4},{5,7},{6,6},{7,5},{8,8},{9,11},{10,1... | collective-permute-start | bytes 196616 | tf_op jit(solution)/shard_map/ppermute | solution.py:257
  10.1 3.3 %copy-start.5 = (s32[64,32]{0,1:T(8,128)S(1)}, s32[64,32]{0,1:T(8,128)}, u32[]{:S(2)}) copy-start(s32[64,32]{0,1:T(8,128)} %param.17) | copy-start | bytes 24580
  10.2 3.3 %copy-start.8 = (s32[64,1]{0,1:T(1,128)S(1)}, s32[64,1]{0,1:T(1,128)}, u32[]{:S(2)}) copy-start(s32[64,1]{0,1:T(1,128)} %param.15) | copy-start | bytes 772
  10.2 3.3 %copy-start.9 = (s32[8]{0:T(128)S(1)}, s32[8]{0:T(128)}, u32[]{:S(2)}) copy-start(s32[8]{0:T(128)} %param.16) | copy-start | bytes 100
  10.2 7.5 %copy-start = (bf16[1,2048,512]{2,1,0:T(8,128)(2,1)S(1)}, bf16[1,2048,512]{2,1,0:T(8,128)(2,1)}, u32[]{:S(2)}) copy-start(bf16[1,2048,512]{2,1,0:T(8,128)(2,1)} %param.13) | copy-start | bytes 6291460
  10.2 7.5 %copy-start.1 = (bf16[1,2048,512]{2,1,0:T(8,128)(2,1)S(1)}, bf16[1,2048,512]{2,1,0:T(8,128)(2,1)}, u32[]{:S(2)}) copy-start(bf16[1,2048,512]{2,1,0:T(8,128)(2,1)} %param.14) | copy-start | bytes 6291460
  10.2 7.5 %copy-start.6 = (bf16[1024]{0:T(1024)(128)(2,1)S(1)}, bf16[1024]{0:T(1024)(128)(2,1)}, u32[]{:S(2)}) copy-start(bf16[1024]{0:T(1024)(128)(2,1)} %param.10) | copy-start | bytes 6148
  15.0 1.8 %collective-permute-start.5 = (bf16[32,1024]{1,0:T(8,128)(2,1)S(1)}, bf16[32,1024]{1,0:T(8,128)(2,1)S(1)}, u32[]{:S(2)}, u32[]{:S(2)}) collective-permute-start(bf16[32,1024]{1,0:T(8,128)(2,1)S(1)} %collective-permute-done.1.refs_0_), channel_id=1, source_target_pairs={{0,1},{1,0},{2,3},{3,2},{4,5},{5,4},{6,7},{7,6},{8,9},{9,8},{10,11... | collective-permute-start | bytes 196616 | tf_op jit(solution)/shard_map/ppermute | solution.py:249
  15.9 1.3 %collective-permute-start.6 = (bf16[32,1024]{1,0:T(8,128)(2,1)S(1)}, bf16[32,1024]{1,0:T(8,128)(2,1)S(1)}, u32[]{:S(2)}, u32[]{:S(2)}) collective-permute-start(bf16[32,1024]{1,0:T(8,128)(2,1)S(1)} %collective-permute-done.2.refs_2_), channel_id=1, source_target_pairs={{0,1},{1,0},{2,3},{3,2},{4,5},{5,4},{6,7},{7,6},{8,9},{9,8},{10,11... | collective-permute-start | bytes 196616 | tf_op jit(solution)/shard_map/ppermute | solution.py:249
  16.0 1.3 %collective-permute-start.7 = (bf16[32,1024]{1,0:T(8,128)(2,1)S(1)}, bf16[32,1024]{1,0:T(8,128)(2,1)S(1)}, u32[]{:S(2)}, u32[]{:S(2)}) collective-permute-start(bf16[32,1024]{1,0:T(8,128)(2,1)S(1)} %collective-permute-done.3.refs_4_), channel_id=1, source_target_pairs={{0,1},{1,0},{2,3},{3,2},{4,5},{5,4},{6,7},{7,6},{8,9},{9,8},{10,11... | collective-permute-start | bytes 196616 | tf_op jit(solution)/shard_map/ppermute | solution.py:249
  16.4 1.3 %collective-permute-start.8 = (bf16[32,1024]{1,0:T(8,128)(2,1)S(1)}, bf16[32,1024]{1,0:T(8,128)(2,1)S(1)}, u32[]{:S(2)}, u32[]{:S(2)}) collective-permute-start(bf16[32,1024]{1,0:T(8,128)(2,1)S(1)} %collective-permute-done.4.refs_6_), channel_id=1, source_target_pairs={{0,1},{1,0},{2,3},{3,2},{4,5},{5,4},{6,7},{7,6},{8,9},{9,8},{10,11... | collective-permute-start | bytes 196616 | tf_op jit(solution)/shard_map/ppermute | solution.py:249
  17.7 3.9 %copy-start.3 = (bf16[8,8,1024]{2,1,0:T(8,128)(2,1)S(1)}, bf16[8,8,1024]{2,1,0:T(8,128)(2,1)}, u32[]{:S(2)}) copy-start(bf16[8,8,1024]{2,1,0:T(8,128)(2,1)} %own_ref.5) | copy-start | bytes 393220
  21.3 13.8 %copy-start.4 = (bf16[512,1024]{1,0:T(8,128)(2,1)S(1)}, bf16[512,1024]{1,0:T(8,128)(2,1)}, u32[]{:S(2)}) copy-start(bf16[512,1024]{1,0:T(8,128)(2,1)} %w_own_ref) | copy-start | bytes 3145732
  21.4 1.4 %collective-permute-start.10 = (bf16[128,512]{1,0:T(8,128)(2,1)S(1)}, bf16[128,512]{1,0:T(8,128)(2,1)S(1)}, u32[]{:S(2)}, u32[]{:S(2)}) collective-permute-start(bf16[128,512]{1,0:T(8,128)(2,1)S(1)} %get-tuple-element.66), channel_id=1, source_target_pairs={{0,1},{1,0},{2,3},{3,2},{4,5},{5,4},{6,7},{7,6},{8,9},{9,8},{10,11... | collective-permute-start | bytes 393224 | tf_op jit(solution)/shard_map/ppermute | solution.py:249
  22.8 12.4 %collective-permute-start.11 = (bf16[2,64,512]{2,1,0:T(8,128)(2,1)S(1)}, bf16[2,64,512]{2,1,0:T(8,128)(2,1)S(1)}, u32[]{:S(2)}, u32[]{:S(2)}) collective-permute-start(bf16[2,64,512]{2,1,0:T(8,128)(2,1)S(1)} %get-tuple-element.71), channel_id=1, source_target_pairs={{0,1},{1,0},{2,3},{3,2},{4,5},{5,4},{6,7},{7,6},{8,9},{9,8},{10,11... | collective-permute-start | bytes 393224 | tf_op jit(solution)/shard_map/ppermute | solution.py:249
  23.0 6.8 %collective-permute-start.12 = (bf16[64,512]{1,0:T(8,128)(2,1)S(1)}, bf16[64,512]{1,0:T(8,128)(2,1)S(1)}, u32[]{:S(2)}, u32[]{:S(2)}) collective-permute-start(bf16[64,512]{1,0:T(8,128)(2,1)S(1)} %get-tuple-element.75), channel_id=1, source_target_pairs={{0,12},{1,15},{2,14},{3,13},{4,8},{5,11},{6,10},{7,9},{8,4},{9,7},... | collective-permute-start | bytes 196616 | tf_op jit(solution)/shard_map/ppermute | solution.py:257
  26.4 7.0 %collective-permute-start.14 = (bf16[64,512]{1,0:T(8,128)(2,1)S(1)}, bf16[64,512]{1,0:T(8,128)(2,1)S(1)}, u32[]{:S(2)}, u32[]{:S(2)}) collective-permute-start(bf16[64,512]{1,0:T(8,128)(2,1)S(1)} %get-tuple-element.76), channel_id=1, source_target_pairs={{1,9},{0,10},{3,11},{2,8},{5,13},{4,14},{7,15},{6,12},{9,1},{8,2},... | collective-permute-start | bytes 196616 | tf_op jit(solution)/shard_map/ppermute | solution.py:257
  26.8 6.7 %collective-permute-start.16 = (bf16[64,512]{1,0:T(8,128)(2,1)S(1)}, bf16[64,512]{1,0:T(8,128)(2,1)S(1)}, u32[]{:S(2)}, u32[]{:S(2)}) collective-permute-start(bf16[64,512]{1,0:T(8,128)(2,1)S(1)} %get-tuple-element.77), channel_id=1, source_target_pairs={{1,5},{0,6},{3,7},{2,4},{5,1},{4,2},{7,3},{6,0},{9,13},{8,14},{11,... | collective-permute-start | bytes 196616 | tf_op jit(solution)/shard_map/ppermute | solution.py:257
  28.3 5.7 %collective-permute-start.18 = (bf16[64,512]{1,0:T(8,128)(2,1)S(1)}, bf16[64,512]{1,0:T(8,128)(2,1)S(1)}, u32[]{:S(2)}, u32[]{:S(2)}) collective-permute-start(bf16[64,512]{1,0:T(8,128)(2,1)S(1)} %get-tuple-element.78), channel_id=1, source_target_pairs={{0,0},{1,3},{2,2},{3,1},{4,4},{5,7},{6,6},{7,5},{8,8},{9,11},{10,1... | collective-permute-start | bytes 196616 | tf_op jit(solution)/shard_map/ppermute | solution.py:257
  29.7 4.4 %collective-permute-start.13 = (bf16[32,512]{1,0:T(8,128)(2,1)S(1)}, bf16[32,512]{1,0:T(8,128)(2,1)S(1)}, u32[]{:S(2)}, u32[]{:S(2)}) collective-permute-start(bf16[32,512]{1,0:T(8,128)(2,1)S(1)} %slice.16), channel_id=1, source_target_pairs={{0,1},{1,0},{2,3},{3,2},{4,5},{5,4},{6,7},{7,6},{8,9},{9,8},{10,11... | collective-permute-start | bytes 98312 | tf_op jit(solution)/shard_map/ppermute | solution.py:249
  33.4 1.2 %collective-permute-start.15 = (bf16[32,512]{1,0:T(8,128)(2,1)S(1)}, bf16[32,512]{1,0:T(8,128)(2,1)S(1)}, u32[]{:S(2)}, u32[]{:S(2)}) collective-permute-start(bf16[32,512]{1,0:T(8,128)(2,1)S(1)} %slice.17), channel_id=1, source_target_pairs={{0,1},{1,0},{2,3},{3,2},{4,5},{5,4},{6,7},{7,6},{8,9},{9,8},{10,11... | collective-permute-start | bytes 98312 | tf_op jit(solution)/shard_map/ppermute | solution.py:249
  33.5 1.4 %collective-permute-start.17 = (bf16[32,512]{1,0:T(8,128)(2,1)S(1)}, bf16[32,512]{1,0:T(8,128)(2,1)S(1)}, u32[]{:S(2)}, u32[]{:S(2)}) collective-permute-start(bf16[32,512]{1,0:T(8,128)(2,1)S(1)} %slice.18), channel_id=1, source_target_pairs={{0,1},{1,0},{2,3},{3,2},{4,5},{5,4},{6,7},{7,6},{8,9},{9,8},{10,11... | collective-permute-start | bytes 98312 | tf_op jit(solution)/shard_map/ppermute | solution.py:249
  34.0 1.2 %collective-permute-start.19 = (bf16[32,512]{1,0:T(8,128)(2,1)S(1)}, bf16[32,512]{1,0:T(8,128)(2,1)S(1)}, u32[]{:S(2)}, u32[]{:S(2)}) collective-permute-start(bf16[32,512]{1,0:T(8,128)(2,1)S(1)} %slice.19), channel_id=1, source_target_pairs={{0,1},{1,0},{2,3},{3,2},{4,5},{5,4},{6,7},{7,6},{8,9},{9,8},{10,11... | collective-permute-start | bytes 98312 | tf_op jit(solution)/shard_map/ppermute | solution.py:249

commit v14 on v13

--- a/solution.py
+++ b/solution.py
@@ -59,7 +59,8 @@
 
 
 def position(distance, serve, owners):
-    return jnp.where(core_of(distance) == serve, 0, owners // 2) + distance // 2
+    far = jnp.where(core_of(distance) == serve, 0, owners // 2 - 1) + distance // 2 + 1
+    return jnp.where(distance < 2, distance, far)
 
 
 def own_slots(sess_ref, req_count):
@@ -91,8 +92,9 @@
     per_owner = requests // owners
     rows = per_owner * half_cands
     distance = sessions ^ me
-    first = distance // 2 * (2 * CAP)
-    code = jnp.where(core_of(distance) == serve, first + places(sessions, per_owner), owners * CAP)
+    at = position(distance, serve, owners)
+    sent = at <= owners // 2
+    code = jnp.where(sent, at * (2 * CAP) + places(sessions, per_owner), owners * (2 * CAP))
     request = lax.broadcasted_iota(jnp.int32, (requests, 2 * rows), 0)
     column = lax.broadcasted_iota(jnp.int32, (requests, 2 * rows), 1)
     spread = (request == me * per_owner + (column % rows) // half_cands).astype(jnp.float32).astype(jnp.bfloat16)
@@ -176,12 +178,13 @@
 
 
 def history_kernel(owners, gain_ref, w_ref, hide_rows_ref, hide_cols_ref, keys_ref, values_ref, *refs):
-    keep_ref, give_ref = refs[owners:]
-    slot_refs = [None] * owners
-    for at, order in enumerate(far_first(owners // 2)):
-        slot_refs[order], slot_refs[owners // 2 + order] = refs[2 * at : 2 * at + 2]
-    rows, width = keep_ref.shape
-    per_owner = rows // (owners // 2)
+    slot_refs, (local_ref, near_ref, keep_ref, give_ref) = refs[:owners], refs[owners:]
+    width = near_ref.shape[1]
+    per_owner = near_ref.shape[0]
+    half = per_owner // 2
+    far = [(ref, at * per_owner, 0, per_owner) for ref in (keep_ref, give_ref) for at in range(owners // 2 - 1)]
+    local = [(local_ref, 0, 0, half), (give_ref, (owners // 2 - 1) * per_owner, half, half)]
+    targets = [local, [(near_ref, 0, 0, per_owner)]] + [[target] for target in far]
     hist_rows = keys_ref.shape[0]
     span = min(256, hist_rows)
     per_step = max(1, min(owners, 256 // per_owner))
@@ -206,30 +209,40 @@
                 total = term if total is None else total + term
             total = total.astype(jnp.bfloat16)
             for place, at in enumerate(group):
-                out_ref, row = (keep_ref, at * per_owner) if at < owners // 2 else (give_ref, at * per_owner - rows)
-                out_ref[row : row + per_owner, low : low + HD] = total[place * per_owner : (place + 1) * per_owner]
-
-
-def output_kernel(messages, sess_ref, own_ref, keep_ref, got_ref, w_own_ref, w_other_ref, *refs):
-    back_refs, (out_ref, table_ref) = refs[: 2 * messages], refs[2 * messages :]
+                for out_ref, row, start, count in targets[at]:
+                    low_row = place * per_owner + start
+                    out_ref[row : row + count, low : low + HD] = total[low_row : low_row + count]
+
+
+def output_kernel(owners, sess_ref, own_ref, keep_ref, got_ref, w_own_ref, w_other_ref, *refs):
+    local_ref, given_ref, near_ref, their_near_ref, *back_refs = refs[:-2]
+    out_ref, table_ref = refs[-2:]
     req_count, half_cands, model_width = own_ref.shape
     rows = req_count * half_cands
     width = model_width // 2
     serve = lax.axis_index("serve")
     part = CAP * half_cands
+    messages = owners // 2 - 1
+
+    def store(at, heads, block):
+        table_ref[(at * 2 + heads) * CAP : (at * 2 + heads + 1) * CAP] = block.reshape(CAP, half_cands, width)
+
+    store(0, 0, local_ref[...].astype(jnp.float32))
+    store(0, 1, given_ref[given_ref.shape[0] - part :, :].astype(jnp.float32))
+    store(1, 0, near_ref[:part, :].astype(jnp.float32))
+    store(1, 1, their_near_ref[...].astype(jnp.float32))
     for order, at in enumerate(far_first(messages)):
         for side in range(2):
-            block = back_refs[2 * order + side][: 2 * part, :].astype(jnp.float32).reshape(2, CAP, half_cands, width)
+            block = back_refs[2 * order + side][: 2 * part, :].astype(jnp.float32)
             for heads in range(2):
-                low = ((side * messages + at) * 2 + heads) * CAP
-                table_ref[low : low + CAP] = block[heads if side == 0 else 1 - heads]
+                source = heads if side == 0 else 1 - heads
+                store(2 + side * messages + at, heads, block[source * part : (source + 1) * part])
     own = own_slots(sess_ref, req_count)
     total = own_ref[...].astype(jnp.float32).reshape(rows, model_width)
     for heads, (terms_ref, w_ref) in enumerate(((keep_ref, w_own_ref), (got_ref, w_other_ref))):
         history = []
         for distance, place in own:
-            side = jnp.where(core_of(distance) == serve, 0, messages)
-            history.append(table_ref[((side + distance // 2) * 2 + heads) * CAP + place])
+            history.append(table_ref[(position(distance, serve, owners) * 2 + heads) * CAP + place])
         attended = jnp.concatenate(history, axis=0) + terms_ref[0].astype(jnp.float32)
         gates = terms_ref[1].astype(jnp.float32)
         mixed = []
@@ -252,10 +265,14 @@
 def cross(owners, messages):
     came = []
     for at in far_first(len(messages)):
-        steps = [2 * at + side for side in range(2)]
+        steps = [2 * (at + 1) + side for side in range(2)]
         pairs = [(place * 2 + core_of(step), (place ^ step) * 2 + core_of(step)) for place in range(owners) for step in steps]
         came.append(lax.ppermute(messages[at], ("cache", "serve"), pairs))
     return came
+
+
+def to_neighbour(owners, rows):
+    return lax.ppermute(rows, "cache", [(place, place ^ 1) for place in range(owners)])
 
 
 def body(candidates, input_gain, w_in, w_out, hist_keys, hist_values, request_session, hist_len, block_mask):
@@ -267,22 +284,22 @@
     bf16 = functools.partial(jax.ShapeDtypeStruct, dtype=jnp.bfloat16)
     sessions = request_session.reshape(-1)
     gain = input_gain.reshape(-1, HD)
-    messages = owners // 2
+    messages = owners // 2 - 1
     piece = 2 * CAP * half_cands
-    half_table = bf16((messages * piece, width))
 
     session_row = request_session.reshape(1, -1)
     chosen = kernel_call(
         functools.partial(front_kernel, owners, half_cands),
-        bf16((messages * piece, 2 * rows)),
+        bf16(((messages + 2) * piece, 2 * rows)),
         [vmem],
     )(session_row)
     other, w_out, chosen = lax.optimization_barrier((swap(candidates), w_out, chosen))
     w_other = swap(w_out)
-    out = kernel_call(message_kernel, [bf16((piece, model_width))] * messages, [vmem] * 3)(chosen, candidates, other)
-    out, w_in = lax.optimization_barrier((out, w_in))
+    out = kernel_call(message_kernel, [bf16((piece, model_width))] * (messages + 2), [vmem] * 3)(chosen, candidates, other)
+    (local, near, *out), w_in = lax.optimization_barrier((out, w_in))
     weights = jnp.transpose(w_in, (1, 0, 2))
     came = cross(owners, out)
+    near = to_neighbour(owners, near)
     visible = kernel_call(
         visible_kernel,
         [bf16((owners * piece, HD)), bf16((hist_rows, HD))],
@@ -291,9 +308,9 @@
     )(session_row, hist_len.reshape(1, -1), lax.optimization_barrier((block_mask.T, out))[0])
     came, weights, (hide_rows, hide_cols) = lax.optimization_barrier((came, weights, visible))
     swapped = [swap(message) for message in came]
-    keep, give = kernel_call(
+    local, near, keep, give = kernel_call(
         functools.partial(history_kernel, owners),
-        [half_table] * 2,
+        [bf16((rows_out, width)) for rows_out in (piece // 2, piece, messages * piece, messages * piece + piece // 2)],
         [vmem] * (6 + owners),
         flops=8 * owners * piece * hist_rows * width,
         moved=4 * hist_rows * width,
@@ -304,8 +321,12 @@
         hide_cols,
         hist_keys.reshape(hist_rows, width),
         hist_values.reshape(hist_rows, width),
-        *[rows_of for both in zip(came, swapped) for rows_of in both],
+        local,
+        near,
+        *reversed(came),
+        *reversed(swapped),
     )
+    near = to_neighbour(owners, near)
     keep, give, w_other = lax.optimization_barrier((keep, give, w_other))
     got = swap(give)
     terms = kernel_call(
@@ -318,15 +339,16 @@
     )(candidates, lax.optimization_barrier((other, give))[0], gain, weights)
     got, (keep_terms, give_terms) = lax.optimization_barrier((got, terms))
     backs = cross(owners, kernel_call(pack_kernel, [bf16((2 * piece, width))] * messages, [vmem] * 2)(keep, got))
+    their_near = swap(near[piece // 2 :])
     returned = [rows_of for back in backs for rows_of in (back, swap(back[piece:]))]
     return kernel_call(
-        functools.partial(output_kernel, messages),
+        functools.partial(output_kernel, owners),
         bf16((req_count, half_cands, model_width)),
-        [smem] + [vmem] * (5 + 2 * messages),
-        [pltpu.VMEM((4 * messages * CAP, half_cands, width), jnp.float32)],
+        [smem] + [vmem] * (9 + 2 * messages),
+        [pltpu.VMEM((2 * owners * CAP, half_cands, width), jnp.float32)],
         flops=8 * rows * model_width * width,
         moved=4 * model_width * width,
-    )(sessions, candidates, keep_terms, swap(give_terms), w_out, w_other, *returned)
+    )(sessions, candidates, keep_terms, swap(give_terms), w_out, w_other, local, got, near, their_near, *returned)
 
 
 def solution(mesh):

time: 37.2 us -> 36.6 us (0.984)
  waiting for transfers between devices: 7.39 us -> 6.21 us
  starting transfers between devices: 16.7 us -> 17.3 us
    ppermute x0 -> x2, starting transfers between devices: none -> 3.2 us  [to_neighbour(): lax.ppermute(rows, 'cache', [(place, place ^ 1) for place in range(owners)])]
    ppermute x8 -> x6, starting transfers between devices: 13 us -> 11.7 us  [cross(): came.append(lax.ppermute(messages[at], ('cache', 'serve'), pairs))]
    ppermute x12 -> x11, starting transfers between devices: 3.68 us -> 2.42 us  [swap(): return lax.ppermute(rows, 'serve', [(0, 1), (1, 0)])]
    ppermute x8 -> x6, waiting for transfers between devices: 4.66 us -> 3.49 us  [cross(): came.append(lax.ppermute(messages[at], ('cache', 'serve'), pairs))]
    ppermute x12 -> x11, waiting for transfers between devices: 2.73 us -> 1.76 us  [swap(): return lax.ppermute(rows, 'serve', [(0, 1), (1, 0)])]
    ppermute x0 -> x2, waiting for transfers between devices: none -> 0.95 us  [to_neighbour(): lax.ppermute(rows, 'cache', [(place, place ^ 1) for place in range(owners)])]
  transfers between devices with their start and end apart: 20 -> 19, of which waited for: 12 -> 6; matrix products, arithmetic and copies ran while one was open for 9% -> 9% of each run, Pallas kernels for 17% -> 17%
where the time goes in v14:
time: 36.6 us; the launch traced here: 36.5 us
  starting transfers between devices  17.3 us (47%)
  Pallas kernels  7.97 us (22%)
  waiting for transfers between devices  6.21 us (17%)
  local copies, waits for them, and re-layouts  4.79 us (13%)
    ppermute x6, starting transfers between devices, cross(): came.append(lax.ppermute(messages[at], ('cache', 'serve'), pairs))  11.7 us
    pallas_call x1, Pallas kernels, body(): kernel_call(functools.partial(history_kernel, owners), [bf16((rows_out, w...  3.65 us
    ppermute x6, waiting for transfers between devices, cross(): came.append(lax.ppermute(messages[at], ('cache', 'serve'), pairs))  3.49 us
    ppermute x2, starting transfers between devices, to_neighbour(): lax.ppermute(rows, 'cache', [(place, place ^ 1) for place in range(owners)])  3.2 us
    optimization_barrier x1, local copies, waits for them, and re-layouts, body(): (local, near, *out), w_in = lax.optimization_barrier((out, w_in))  3.18 us
    ppermute x11, starting transfers between devices, swap(): return lax.ppermute(rows, 'serve', [(0, 1), (1, 0)])  2.42 us
    pallas_call x1, Pallas kernels, body(): kernel_call(functools.partial(output_kernel, owners), bf16((req_count, ha...  1.85 us
    ppermute x11, waiting for transfers between devices, swap(): return lax.ppermute(rows, 'serve', [(0, 1), (1, 0)])  1.76 us
  transfers between devices with their start and end apart: 19, of which 6 were waited for; matrix products, arithmetic and copies ran while one was open for 9% of the time, Pallas kernels for 17%

profile of v14, /device:TPU:0, one launch (start us, length us, event | category | flops | bytes accessed | tf_op | source)
XLA Modules:
  0.0 36.5 jit_solution(12494139584906111449)
XLA Ops:
  0.0 0.5 %collective-permute-start = (bf16[8,8,1024]{2,1,0:T(8,128)(2,1)}, bf16[8,8,1024]{2,1,0:T(8,128)(2,1)S(1)}, u32[]{:S(2)}, u32[]{:S(2)}) collective-permute-start(bf16[8,8,1024]{2,1,0:T(8,128)(2,1)} %own_ref.5), channel_id=1, source_target_pairs={{0,1},{1,0},{2,3},{3,2},{4,5},{5,4},{6,7},{7,6},{8,9},{9,8},{10,11... | collective-permute-start | bytes 393224 | tf_op jit(solution)/shard_map/ppermute | solution.py:262
  0.5 0.0 copy-start.7
  0.5 0.7 %copy-done.7 = s32[64,1]{0,1:T(1,128)S(1)} copy-done((s32[64,1]{0,1:T(1,128)S(1)}, s32[64,1]{0,1:T(1,128)}, u32[]{:S(2)}) %copy-start.7) | copy-done | bytes 280
  1.1 0.4 %shard_map.91.chosen_ref = bf16[160,128]{1,0:T(8,128)(2,1)S(1)} custom-call(s32[1,64]{1,0:T(1,128)S(1)} %bitcast.17), custom_call_target="tpu_custom_call" | custom-call | tf_op jit(solution)/shard_map/pallas_call | solution.py:291
  1.5 0.1 collective-permute-done.other_ref
  1.7 0.4 collective-permute-start.8
  2.0 0.0 copy-start.2
  2.0 0.9 %copy-done.2 = bf16[8,8,1024]{2,1,0:T(8,128)(2,1)S(1)} copy-done((bf16[8,8,1024]{2,1,0:T(8,128)(2,1)S(1)}, bf16[8,8,1024]{2,1,0:T(8,128)(2,1)}, u32[]{:S(2)}) %copy-start.2) | copy-done | bytes 131096
  2.9 0.2 shard_map.92
  3.2 4.8 %collective-permute-start.1 = (bf16[32,1024]{1,0:T(8,128)(2,1)S(1)}, bf16[32,1024]{1,0:T(8,128)(2,1)S(1)}, u32[]{:S(2)}, u32[]{:S(2)}) collective-permute-start(bf16[32,1024]{1,0:T(8,128)(2,1)S(1)} %get-tuple-element.51), channel_id=1, source_target_pairs={{0,12},{1,15},{2,14},{3,13},{4,8},{5,11},{6,10},{7,9},{8,4},{9,7},... | collective-permute-start | bytes 196616 | tf_op jit(solution)/shard_map/ppermute | solution.py:270
  8.0 0.4 %collective-permute-start.2 = (bf16[32,1024]{1,0:T(8,128)(2,1)S(1)}, bf16[32,1024]{1,0:T(8,128)(2,1)S(1)}, u32[]{:S(2)}, u32[]{:S(2)}) collective-permute-start(bf16[32,1024]{1,0:T(8,128)(2,1)S(1)} %get-tuple-element.52), channel_id=1, source_target_pairs={{1,9},{0,10},{3,11},{2,8},{5,13},{4,14},{7,15},{6,12},{9,1},{8,2},... | collective-permute-start | bytes 196616 | tf_op jit(solution)/shard_map/ppermute | solution.py:270
  8.4 1.1 %collective-permute-start.3 = (bf16[32,1024]{1,0:T(8,128)(2,1)S(1)}, bf16[32,1024]{1,0:T(8,128)(2,1)S(1)}, u32[]{:S(2)}, u32[]{:S(2)}) collective-permute-start(bf16[32,1024]{1,0:T(8,128)(2,1)S(1)} %get-tuple-element.53), channel_id=1, source_target_pairs={{1,5},{0,6},{3,7},{2,4},{5,1},{4,2},{7,3},{6,0},{9,13},{8,14},{11,... | collective-permute-start | bytes 196616 | tf_op jit(solution)/shard_map/ppermute | solution.py:270
  9.5 0.0 copy-start.5
  9.5 0.0 copy-start.8
  9.5 0.0 copy-start.9
  9.5 0.0 copy-start.1
  9.5 0.0 copy-start.6
  9.5 3.2 %copy.12 = bf16[1024,4,512]{2,0,1:T(8,128)(2,1)S(1)} copy(bf16[1024,4,512]{2,1,0:T(4,128)(2,1)} %param.11) | data formatting | bytes 8388608 | tf_op jit(solution)/shard_map/optimization_barrier | solution.py:299
  12.7 1.7 %collective-permute-start.4 = (bf16[32,1024]{1,0:T(8,128)(2,1)S(1)}, bf16[32,1024]{1,0:T(8,128)(2,1)S(1)}, u32[]{:S(2)}, u32[]{:S(2)}) collective-permute-start(bf16[32,1024]{1,0:T(8,128)(2,1)S(1)} %get-tuple-element.62), channel_id=1, source_target_pairs={{0,2},{2,0},{4,6},{6,4},{8,10},{10,8},{12,14},{14,12},{1,3},{3,1},... | collective-permute-start | bytes 196616 | tf_op jit(solution)/shard_map/ppermute | solution.py:275
  14.5 0.0 copy-done.5
  14.5 0.0 copy-done.8
  14.5 0.0 copy-done.9
  14.5 1.0 %shard_map.93 = (bf16[256,128]{1,0:T(8,128)(2,1)S(1)}, bf16[2048,128]{1,0:T(8,128)(2,1)S(1)}) custom-call(s32[1,64]{1,0:T(1,128)S(1)} %bitcast.18, s32[1,8]{1,0:T(1,128)S(1)} %bitcast.20, s32[32,64]{1,0:T(8,128)S(1)} %bitcast.14), custom_call_target="tpu_custom_call" | custom-call | tf_op jit(solution)/shard_map/pallas_call | solution.py:303
  15.4 0.0 collective-permute-done.1.refs_4_
  15.4 0.0 collective-permute-done.2.refs_3_
  15.4 0.0 collective-permute-done.3.refs_2_
  15.5 0.1 collective-permute-start.5
  15.5 0.5 %collective-permute-start.6 = (bf16[32,1024]{1,0:T(8,128)(2,1)S(1)}, bf16[32,1024]{1,0:T(8,128)(2,1)S(1)}, u32[]{:S(2)}, u32[]{:S(2)}) collective-permute-start(bf16[32,1024]{1,0:T(8,128)(2,1)S(1)} %collective-permute-done.2.refs_3_), channel_id=1, source_target_pairs={{0,1},{1,0},{2,3},{3,2},{4,5},{5,4},{6,7},{7,6},{8,9},{9,8},{10,11... | collective-permute-start | bytes 196616 | tf_op jit(solution)/shard_map/ppermute | solution.py:262
  16.0 0.1 collective-permute-start.7
  16.1 0.9 %collective-permute-done.4.refs_1_ = bf16[32,1024]{1,0:T(8,128)(2,1)S(1)} collective-permute-done((bf16[32,1024]{1,0:T(8,128)(2,1)S(1)}, bf16[32,1024]{1,0:T(8,128)(2,1)S(1)}, u32[]{:S(2)}, u32[]{:S(2)}) %collective-permute-start.4) | collective-permute-done | bytes 65568 | tf_op jit(solution)/shard_map/ppermute | solution.py:275
  17.1 0.0 collective-permute-done.5.refs_5_
  17.1 0.0 collective-permute-done.6.refs_6_
  17.1 0.2 collective-permute-done.7.refs_7_
  17.3 0.0 copy-done
  17.3 0.0 copy-done.1
  17.3 0.0 copy-done.6
  17.3 0.0 copy-start.3
  17.3 3.7 %shard_map.94 = (bf16[16,512]{1,0:T(8,128)(2,1)S(1)}, bf16[32,512]{1,0:T(8,128)(2,1)S(1)}, bf16[96,512]{1,0:T(8,128)(2,1)S(1)}, bf16[112,512]{1,0:T(8,128)(2,1)S(1)}) custom-call(bf16[8,128]{1,0:T(8,128)(2,1)S(1)} %bitcast.15, bf16[4,1024,512]{2,1,0:T(8,128)(2,1)S(1)} %bitcast.10, bf16[256,128]{1,0:T(8,128)(2,1)S(1)} %get-tuple-element.59.hide_rows_ref, ...), custom_call_target="tpu_custom_call" | custom-call | flops 2147483648 | bytes 4194304 | tf_op jit(solution)/shard_map/pallas_call | solution.py:311
  21.0 0.0 copy-start.4
  21.0 0.0 collective-permute-done.8.w_other_ref
  21.0 0.2 collective-permute-start.9
  21.2 0.0 copy-done.3
  21.2 0.9 %shard_map.95 = (bf16[2,64,512]{2,1,0:T(8,128)(2,1)S(1)}, bf16[2,64,512]{2,1,0:T(8,128)(2,1)S(1)}) custom-call(bf16[8,8,1024]{2,1,0:T(8,128)(2,1)S(1)} %copy-done.3, bf16[8,8,1024]{2,1,0:T(8,128)(2,1)S(1)} %collective-permute-done.other_ref, bf16[8,128]{1,0:T(8,128)(2,1)S(1)} %bitcast.16, bf16[4,1024,512]{2,1,0:T(8,128)(2,1)S(1)} %bitcast.11), custom_call_target="tpu_custom_call" | custom-call | flops 536870912 | bytes 4194304 | tf_op jit(solution)/shard_map/pallas_call | solution.py:332
  22.1 0.3 collective-permute-done.9.got_ref.refs_1_
  22.4 0.2 collective-permute-start.10
  22.6 3.7 %collective-permute-start.13 = (bf16[64,512]{1,0:T(8,128)(2,1)S(1)}, bf16[64,512]{1,0:T(8,128)(2,1)S(1)}, u32[]{:S(2)}, u32[]{:S(2)}) collective-permute-start(bf16[64,512]{1,0:T(8,128)(2,1)S(1)} %get-tuple-element.80), channel_id=1, source_target_pairs={{0,12},{1,15},{2,14},{3,13},{4,8},{5,11},{6,10},{7,9},{8,4},{9,7},... | collective-permute-start | bytes 196616 | tf_op jit(solution)/shard_map/ppermute | solution.py:270
  26.2 0.0 collective-permute-start.15
  26.2 1.7 %collective-permute-start.17 = (bf16[64,512]{1,0:T(8,128)(2,1)S(1)}, bf16[64,512]{1,0:T(8,128)(2,1)S(1)}, u32[]{:S(2)}, u32[]{:S(2)}) collective-permute-start(bf16[64,512]{1,0:T(8,128)(2,1)S(1)} %get-tuple-element.82), channel_id=1, source_target_pairs={{1,5},{0,6},{3,7},{2,4},{5,1},{4,2},{7,3},{6,0},{9,13},{8,14},{11,... | collective-permute-start | bytes 196616 | tf_op jit(solution)/shard_map/ppermute | solution.py:270
  27.9 1.5 %collective-permute-start.11 = (bf16[32,512]{1,0:T(8,128)(2,1)S(1)}, bf16[32,512]{1,0:T(8,128)(2,1)S(1)}, u32[]{:S(2)}, u32[]{:S(2)}) collective-permute-start(bf16[32,512]{1,0:T(8,128)(2,1)S(1)} %get-tuple-element.78), channel_id=1, source_target_pairs={{0,2},{2,0},{4,6},{6,4},{8,10},{10,8},{12,14},{14,12},{1,3},{3,1},... | collective-permute-start | bytes 98312 | tf_op jit(solution)/shard_map/ppermute | solution.py:275
  29.4 0.0 collective-permute-done.13.refs_4_
  29.4 0.0 collective-permute-start.14
  29.4 3.5 %collective-permute-done.15.refs_6_ = bf16[64,512]{1,0:T(8,128)(2,1)S(1)} collective-permute-done((bf16[64,512]{1,0:T(8,128)(2,1)S(1)}, bf16[64,512]{1,0:T(8,128)(2,1)S(1)}, u32[]{:S(2)}, u32[]{:S(2)}) %collective-permute-start.15) | collective-permute-done | bytes 65568 | tf_op jit(solution)/shard_map/ppermute | solution.py:270
  32.9 0.0 collective-permute-start.16
  32.9 0.0 collective-permute-done.17.refs_8_
  32.9 0.5 %collective-permute-start.18 = (bf16[32,512]{1,0:T(8,128)(2,1)S(1)}, bf16[32,512]{1,0:T(8,128)(2,1)S(1)}, u32[]{:S(2)}, u32[]{:S(2)}) collective-permute-start(bf16[32,512]{1,0:T(8,128)(2,1)S(1)} %slice.19), channel_id=1, source_target_pairs={{0,1},{1,0},{2,3},{3,2},{4,5},{5,4},{6,7},{7,6},{8,9},{9,8},{10,11... | collective-permute-start | bytes 98312 | tf_op jit(solution)/shard_map/ppermute | solution.py:262
  33.4 0.0 collective-permute-done.11.refs_2_
  33.4 0.1 collective-permute-start.12
  33.5 1.1 %collective-permute-done.12.refs_3_ = bf16[16,512]{1,0:T(8,128)(2,1)S(1)} collective-permute-done((bf16[16,512]{1,0:T(8,128)(2,1)S(1)}, bf16[16,512]{1,0:T(8,128)(2,1)S(1)}, u32[]{:S(2)}, u32[]{:S(2)}) %collective-permute-start.12) | collective-permute-done | bytes 16416 | tf_op jit(solution)/shard_map/ppermute | solution.py:262
  34.6 0.0 collective-permute-done.14.refs_5_
  34.6 0.0 collective-permute-done.16.refs_7_
  34.6 0.0 collective-permute-done.18.refs_9_
  34.6 0.0 collective-permute-done.10.got_ref
  34.6 0.0 copy-done.4
  34.6 1.9 %shard_map.97 = bf16[8,8,1024]{2,1,0:T(8,128)(2,1)} custom-call(s32[64]{0:T(128)S(1)} %bitcast.19, bf16[8,8,1024]{2,1,0:T(8,128)(2,1)S(1)} %copy-done.3, bf16[2,64,512]{2,1,0:T(8,128)(2,1)S(1)} %get-tuple-element.73.keep_ref, bf16[2,64,512]{2,1,0:T(8,128)(2,1)S(1)} %collective-permute-done.10.got_ref, bf16[512,1024]{1,0:T(8,128)(2,1)S(1)} %copy-done.4, ...), custom_call_target="tpu_custom_call" | custom-call | flops 268435456 | bytes 2097152 | tf_op jit(solution)/shard_map/pallas_call | solution.py:344
  (6 shorter events, 0.0 us)
Async XLA Ops:
  0.0 1.6 %collective-permute-start = (bf16[8,8,1024]{2,1,0:T(8,128)(2,1)}, bf16[8,8,1024]{2,1,0:T(8,128)(2,1)S(1)}, u32[]{:S(2)}, u32[]{:S(2)}) collective-permute-start(bf16[8,8,1024]{2,1,0:T(8,128)(2,1)} %own_ref.5), channel_id=1, source_target_pairs={{0,1},{1,0},{2,3},{3,2},{4,5},{5,4},{6,7},{7,6},{8,9},{9,8},{10,11... | collective-permute-start | bytes 393224 | tf_op jit(solution)/shard_map/ppermute | solution.py:262
  0.5 0.7 %copy-start.7 = (s32[64,1]{0,1:T(1,128)S(1)}, s32[64,1]{0,1:T(1,128)}, u32[]{:S(2)}) copy-start(s32[64,1]{0,1:T(1,128)} %param.15) | copy-start | bytes 772
  1.7 19.3 %collective-permute-start.8 = (bf16[512,1024]{1,0:T(8,128)(2,1)}, bf16[512,1024]{1,0:T(8,128)(2,1)S(1)}, u32[]{:S(2)}, u32[]{:S(2)}) collective-permute-start(bf16[512,1024]{1,0:T(8,128)(2,1)} %w_own_ref), channel_id=1, source_target_pairs={{0,1},{1,0},{2,3},{3,2},{4,5},{5,4},{6,7},{7,6},{8,9},{9,8},{10,11... | collective-permute-start | bytes 3145736 | tf_op jit(solution)/shard_map/ppermute | solution.py:262
  2.0 0.9 %copy-start.2 = (bf16[8,8,1024]{2,1,0:T(8,128)(2,1)S(1)}, bf16[8,8,1024]{2,1,0:T(8,128)(2,1)}, u32[]{:S(2)}) copy-start(bf16[8,8,1024]{2,1,0:T(8,128)(2,1)} %own_ref.5) | copy-start | bytes 393220
  3.2 12.3 %collective-permute-start.1 = (bf16[32,1024]{1,0:T(8,128)(2,1)S(1)}, bf16[32,1024]{1,0:T(8,128)(2,1)S(1)}, u32[]{:S(2)}, u32[]{:S(2)}) collective-permute-start(bf16[32,1024]{1,0:T(8,128)(2,1)S(1)} %get-tuple-element.51), channel_id=1, source_target_pairs={{0,12},{1,15},{2,14},{3,13},{4,8},{5,11},{6,10},{7,9},{8,4},{9,7},... | collective-permute-start | bytes 196616 | tf_op jit(solution)/shard_map/ppermute | solution.py:270
  8.0 7.5 %collective-permute-start.2 = (bf16[32,1024]{1,0:T(8,128)(2,1)S(1)}, bf16[32,1024]{1,0:T(8,128)(2,1)S(1)}, u32[]{:S(2)}, u32[]{:S(2)}) collective-permute-start(bf16[32,1024]{1,0:T(8,128)(2,1)S(1)} %get-tuple-element.52), channel_id=1, source_target_pairs={{1,9},{0,10},{3,11},{2,8},{5,13},{4,14},{7,15},{6,12},{9,1},{8,2},... | collective-permute-start | bytes 196616 | tf_op jit(solution)/shard_map/ppermute | solution.py:270
  8.4 7.1 %collective-permute-start.3 = (bf16[32,1024]{1,0:T(8,128)(2,1)S(1)}, bf16[32,1024]{1,0:T(8,128)(2,1)S(1)}, u32[]{:S(2)}, u32[]{:S(2)}) collective-permute-start(bf16[32,1024]{1,0:T(8,128)(2,1)S(1)} %get-tuple-element.53), channel_id=1, source_target_pairs={{1,5},{0,6},{3,7},{2,4},{5,1},{4,2},{7,3},{6,0},{9,13},{8,14},{11,... | collective-permute-start | bytes 196616 | tf_op jit(solution)/shard_map/ppermute | solution.py:270
  9.5 5.0 %copy-start.5 = (s32[64,32]{0,1:T(8,128)S(1)}, s32[64,32]{0,1:T(8,128)}, u32[]{:S(2)}) copy-start(s32[64,32]{0,1:T(8,128)} %param.17) | copy-start | bytes 24580
  9.5 5.0 %copy-start.8 = (s32[64,1]{0,1:T(1,128)S(1)}, s32[64,1]{0,1:T(1,128)}, u32[]{:S(2)}) copy-start(s32[64,1]{0,1:T(1,128)} %param.15) | copy-start | bytes 772
  9.5 5.0 %copy-start.9 = (s32[8]{0:T(128)S(1)}, s32[8]{0:T(128)}, u32[]{:S(2)}) copy-start(s32[8]{0:T(128)} %param.16) | copy-start | bytes 100
  9.5 7.8 %copy-start = (bf16[1,2048,512]{2,1,0:T(8,128)(2,1)S(1)}, bf16[1,2048,512]{2,1,0:T(8,128)(2,1)}, u32[]{:S(2)}) copy-start(bf16[1,2048,512]{2,1,0:T(8,128)(2,1)} %param.13) | copy-start | bytes 6291460
  9.5 7.8 %copy-start.1 = (bf16[1,2048,512]{2,1,0:T(8,128)(2,1)S(1)}, bf16[1,2048,512]{2,1,0:T(8,128)(2,1)}, u32[]{:S(2)}) copy-start(bf16[1,2048,512]{2,1,0:T(8,128)(2,1)} %param.14) | copy-start | bytes 6291460
  9.5 7.8 %copy-start.6 = (bf16[1024]{0:T(1024)(128)(2,1)S(1)}, bf16[1024]{0:T(1024)(128)(2,1)}, u32[]{:S(2)}) copy-start(bf16[1024]{0:T(1024)(128)(2,1)} %param.10) | copy-start | bytes 6148
  12.7 4.3 %collective-permute-start.4 = (bf16[32,1024]{1,0:T(8,128)(2,1)S(1)}, bf16[32,1024]{1,0:T(8,128)(2,1)S(1)}, u32[]{:S(2)}, u32[]{:S(2)}) collective-permute-start(bf16[32,1024]{1,0:T(8,128)(2,1)S(1)} %get-tuple-element.62), channel_id=1, source_target_pairs={{0,2},{2,0},{4,6},{6,4},{8,10},{10,8},{12,14},{14,12},{1,3},{3,1},... | collective-permute-start | bytes 196616 | tf_op jit(solution)/shard_map/ppermute | solution.py:275
  15.5 1.6 %collective-permute-start.5 = (bf16[32,1024]{1,0:T(8,128)(2,1)S(1)}, bf16[32,1024]{1,0:T(8,128)(2,1)S(1)}, u32[]{:S(2)}, u32[]{:S(2)}) collective-permute-start(bf16[32,1024]{1,0:T(8,128)(2,1)S(1)} %collective-permute-done.3.refs_2_), channel_id=1, source_target_pairs={{0,1},{1,0},{2,3},{3,2},{4,5},{5,4},{6,7},{7,6},{8,9},{9,8},{10,11... | collective-permute-start | bytes 196616 | tf_op jit(solution)/shard_map/ppermute | solution.py:262
  15.5 1.5 %collective-permute-start.6 = (bf16[32,1024]{1,0:T(8,128)(2,1)S(1)}, bf16[32,1024]{1,0:T(8,128)(2,1)S(1)}, u32[]{:S(2)}, u32[]{:S(2)}) collective-permute-start(bf16[32,1024]{1,0:T(8,128)(2,1)S(1)} %collective-permute-done.2.refs_3_), channel_id=1, source_target_pairs={{0,1},{1,0},{2,3},{3,2},{4,5},{5,4},{6,7},{7,6},{8,9},{9,8},{10,11... | collective-permute-start | bytes 196616 | tf_op jit(solution)/shard_map/ppermute | solution.py:262
  16.0 1.3 %collective-permute-start.7 = (bf16[32,1024]{1,0:T(8,128)(2,1)S(1)}, bf16[32,1024]{1,0:T(8,128)(2,1)S(1)}, u32[]{:S(2)}, u32[]{:S(2)}) collective-permute-start(bf16[32,1024]{1,0:T(8,128)(2,1)S(1)} %collective-permute-done.1.refs_4_), channel_id=1, source_target_pairs={{0,1},{1,0},{2,3},{3,2},{4,5},{5,4},{6,7},{7,6},{8,9},{9,8},{10,11... | collective-permute-start | bytes 196616 | tf_op jit(solution)/shard_map/ppermute | solution.py:262
  17.3 3.9 %copy-start.3 = (bf16[8,8,1024]{2,1,0:T(8,128)(2,1)S(1)}, bf16[8,8,1024]{2,1,0:T(8,128)(2,1)}, u32[]{:S(2)}) copy-start(bf16[8,8,1024]{2,1,0:T(8,128)(2,1)} %own_ref.5) | copy-start | bytes 393220
  21.0 13.6 %copy-start.4 = (bf16[512,1024]{1,0:T(8,128)(2,1)S(1)}, bf16[512,1024]{1,0:T(8,128)(2,1)}, u32[]{:S(2)}) copy-start(bf16[512,1024]{1,0:T(8,128)(2,1)} %w_own_ref) | copy-start | bytes 3145732
  21.0 1.4 %collective-permute-start.9 = (bf16[112,512]{1,0:T(8,128)(2,1)S(1)}, bf16[112,512]{1,0:T(8,128)(2,1)S(1)}, u32[]{:S(2)}, u32[]{:S(2)}) collective-permute-start(bf16[112,512]{1,0:T(8,128)(2,1)S(1)} %get-tuple-element.69), channel_id=1, source_target_pairs={{0,1},{1,0},{2,3},{3,2},{4,5},{5,4},{6,7},{7,6},{8,9},{9,8},{10,11... | collective-permute-start | bytes 344072 | tf_op jit(solution)/shard_map/ppermute | solution.py:262
  22.4 12.2 %collective-permute-start.10 = (bf16[2,64,512]{2,1,0:T(8,128)(2,1)S(1)}, bf16[2,64,512]{2,1,0:T(8,128)(2,1)S(1)}, u32[]{:S(2)}, u32[]{:S(2)}) collective-permute-start(bf16[2,64,512]{2,1,0:T(8,128)(2,1)S(1)} %get-tuple-element.74), channel_id=1, source_target_pairs={{0,1},{1,0},{2,3},{3,2},{4,5},{5,4},{6,7},{7,6},{8,9},{9,8},{10,11... | collective-permute-start | bytes 393224 | tf_op jit(solution)/shard_map/ppermute | solution.py:262
  22.6 6.8 %collective-permute-start.13 = (bf16[64,512]{1,0:T(8,128)(2,1)S(1)}, bf16[64,512]{1,0:T(8,128)(2,1)S(1)}, u32[]{:S(2)}, u32[]{:S(2)}) collective-permute-start(bf16[64,512]{1,0:T(8,128)(2,1)S(1)} %get-tuple-element.80), channel_id=1, source_target_pairs={{0,12},{1,15},{2,14},{3,13},{4,8},{5,11},{6,10},{7,9},{8,4},{9,7},... | collective-permute-start | bytes 196616 | tf_op jit(solution)/shard_map/ppermute | solution.py:270
  26.2 6.6 %collective-permute-start.15 = (bf16[64,512]{1,0:T(8,128)(2,1)S(1)}, bf16[64,512]{1,0:T(8,128)(2,1)S(1)}, u32[]{:S(2)}, u32[]{:S(2)}) collective-permute-start(bf16[64,512]{1,0:T(8,128)(2,1)S(1)} %get-tuple-element.81), channel_id=1, source_target_pairs={{1,9},{0,10},{3,11},{2,8},{5,13},{4,14},{7,15},{6,12},{9,1},{8,2},... | collective-permute-start | bytes 196616 | tf_op jit(solution)/shard_map/ppermute | solution.py:270
  26.2 6.7 %collective-permute-start.17 = (bf16[64,512]{1,0:T(8,128)(2,1)S(1)}, bf16[64,512]{1,0:T(8,128)(2,1)S(1)}, u32[]{:S(2)}, u32[]{:S(2)}) collective-permute-start(bf16[64,512]{1,0:T(8,128)(2,1)S(1)} %get-tuple-element.82), channel_id=1, source_target_pairs={{1,5},{0,6},{3,7},{2,4},{5,1},{4,2},{7,3},{6,0},{9,13},{8,14},{11,... | collective-permute-start | bytes 196616 | tf_op jit(solution)/shard_map/ppermute | solution.py:270
  27.9 5.5 %collective-permute-start.11 = (bf16[32,512]{1,0:T(8,128)(2,1)S(1)}, bf16[32,512]{1,0:T(8,128)(2,1)S(1)}, u32[]{:S(2)}, u32[]{:S(2)}) collective-permute-start(bf16[32,512]{1,0:T(8,128)(2,1)S(1)} %get-tuple-element.78), channel_id=1, source_target_pairs={{0,2},{2,0},{4,6},{6,4},{8,10},{10,8},{12,14},{14,12},{1,3},{3,1},... | collective-permute-start | bytes 98312 | tf_op jit(solution)/shard_map/ppermute | solution.py:275
  29.4 5.2 %collective-permute-start.14 = (bf16[32,512]{1,0:T(8,128)(2,1)S(1)}, bf16[32,512]{1,0:T(8,128)(2,1)S(1)}, u32[]{:S(2)}, u32[]{:S(2)}) collective-permute-start(bf16[32,512]{1,0:T(8,128)(2,1)S(1)} %slice.17), channel_id=1, source_target_pairs={{0,1},{1,0},{2,3},{3,2},{4,5},{5,4},{6,7},{7,6},{8,9},{9,8},{10,11... | collective-permute-start | bytes 98312 | tf_op jit(solution)/shard_map/ppermute | solution.py:262
  32.9 1.7 %collective-permute-start.16 = (bf16[32,512]{1,0:T(8,128)(2,1)S(1)}, bf16[32,512]{1,0:T(8,128)(2,1)S(1)}, u32[]{:S(2)}, u32[]{:S(2)}) collective-permute-start(bf16[32,512]{1,0:T(8,128)(2,1)S(1)} %slice.18), channel_id=1, source_target_pairs={{0,1},{1,0},{2,3},{3,2},{4,5},{5,4},{6,7},{7,6},{8,9},{9,8},{10,11... | collective-permute-start | bytes 98312 | tf_op jit(solution)/shard_map/ppermute | solution.py:262
  32.9 1.7 %collective-permute-start.18 = (bf16[32,512]{1,0:T(8,128)(2,1)S(1)}, bf16[32,512]{1,0:T(8,128)(2,1)S(1)}, u32[]{:S(2)}, u32[]{:S(2)}) collective-permute-start(bf16[32,512]{1,0:T(8,128)(2,1)S(1)} %slice.19), channel_id=1, source_target_pairs={{0,1},{1,0},{2,3},{3,2},{4,5},{5,4},{6,7},{7,6},{8,9},{9,8},{10,11... | collective-permute-start | bytes 98312 | tf_op jit(solution)/shard_map/ppermute | solution.py:262
  33.4 1.2 %collective-permute-start.12 = (bf16[16,512]{1,0:T(8,128)(2,1)S(1)}, bf16[16,512]{1,0:T(8,128)(2,1)S(1)}, u32[]{:S(2)}, u32[]{:S(2)}) collective-permute-start(bf16[16,512]{1,0:T(8,128)(2,1)S(1)} %slice.16), channel_id=1, source_target_pairs={{0,1},{1,0},{2,3},{3,2},{4,5},{5,4},{6,7},{7,6},{8,9},{9,8},{10,11... | collective-permute-start | bytes 49160 | tf_op jit(solution)/shard_map/ppermute | solution.py:262

commit v15 on v14

--- a/solution.py
+++ b/solution.py
@@ -298,15 +298,15 @@
     out = kernel_call(message_kernel, [bf16((piece, model_width))] * (messages + 2), [vmem] * 3)(chosen, candidates, other)
     (local, near, *out), w_in = lax.optimization_barrier((out, w_in))
     weights = jnp.transpose(w_in, (1, 0, 2))
+    near = to_neighbour(owners, near)
     came = cross(owners, out)
-    near = to_neighbour(owners, near)
     visible = kernel_call(
         visible_kernel,
         [bf16((owners * piece, HD)), bf16((hist_rows, HD))],
         [vmem] * 3,
         [pltpu.VMEM((HD, owners * req_count), jnp.bfloat16)],
     )(session_row, hist_len.reshape(1, -1), lax.optimization_barrier((block_mask.T, out))[0])
-    came, weights, (hide_rows, hide_cols) = lax.optimization_barrier((came, weights, visible))
+    near, came, weights, (hide_rows, hide_cols) = lax.optimization_barrier((near, came, weights, visible))
     swapped = [swap(message) for message in came]
     local, near, keep, give = kernel_call(
         functools.partial(history_kernel, owners),

time: 36.6 us -> 36.3 us (level)
  starting transfers between devices: 17.3 us -> 16.4 us
  waiting for transfers between devices: 6.21 us -> 6.79 us
    ppermute x2, waiting for transfers between devices: 0.95 us -> 0.01 us  [to_neighbour(): lax.ppermute(rows, 'cache', [(place, place ^ 1) for place in range(owners)])]
    ppermute x2, starting transfers between devices: 3.2 us -> 2.32 us  [to_neighbour(): lax.ppermute(rows, 'cache', [(place, place ^ 1) for place in range(owners)])]
    ppermute x6, waiting for transfers between devices: 3.49 us -> 4.33 us  [cross(): came.append(lax.ppermute(messages[at], ('cache', 'serve'), pairs))]
    ppermute x11, waiting for transfers between devices: 1.76 us -> 2.45 us  [swap(): return lax.ppermute(rows, 'serve', [(0, 1), (1, 0)])]
  transfers between devices with their start and end apart: 19 -> 19, of which waited for: 6 -> 9; matrix products, arithmetic and copies ran while one was open for 9% -> 9% of each run, Pallas kernels for 17% -> 17%
where the time goes in v15:
time: 36.3 us; the launch traced here: 36.1 us
  starting transfers between devices  16.4 us (45%)
  Pallas kernels  7.97 us (22%)
  waiting for transfers between devices  6.79 us (19%)
  local copies, waits for them, and re-layouts  4.79 us (13%)
    ppermute x6, starting transfers between devices, cross(): came.append(lax.ppermute(messages[at], ('cache', 'serve'), pairs))  11.7 us
    ppermute x6, waiting for transfers between devices, cross(): came.append(lax.ppermute(messages[at], ('cache', 'serve'), pairs))  4.33 us
    pallas_call x1, Pallas kernels, body(): kernel_call(functools.partial(history_kernel, owners), [bf16((rows_out, w...  3.65 us
    optimization_barrier x1, local copies, waits for them, and re-layouts, body(): (local, near, *out), w_in = lax.optimization_barrier((out, w_in))  3.18 us
    ppermute x11, waiting for transfers between devices, swap(): return lax.ppermute(rows, 'serve', [(0, 1), (1, 0)])  2.45 us
    ppermute x11, starting transfers between devices, swap(): return lax.ppermute(rows, 'serve', [(0, 1), (1, 0)])  2.34 us
    ppermute x2, starting transfers between devices, to_neighbour(): lax.ppermute(rows, 'cache', [(place, place ^ 1) for place in range(owners)])  2.32 us
    pallas_call x1, Pallas kernels, body(): kernel_call(functools.partial(output_kernel, owners), bf16((req_count, ha...  1.85 us
  transfers between devices with their start and end apart: 19, of which 9 were waited for; matrix products, arithmetic and copies ran while one was open for 9% of the time, Pallas kernels for 17%

profile of v15, /device:TPU:0, one launch (start us, length us, event | category | flops | bytes accessed | tf_op | source)
XLA Modules:
  0.0 36.1 jit_solution(16923344535040546812)
XLA Ops:
  0.0 0.5 %collective-permute-start = (bf16[8,8,1024]{2,1,0:T(8,128)(2,1)}, bf16[8,8,1024]{2,1,0:T(8,128)(2,1)S(1)}, u32[]{:S(2)}, u32[]{:S(2)}) collective-permute-start(bf16[8,8,1024]{2,1,0:T(8,128)(2,1)} %own_ref.5), channel_id=1, source_target_pairs={{0,1},{1,0},{2,3},{3,2},{4,5},{5,4},{6,7},{7,6},{8,9},{9,8},{10,11... | collective-permute-start | bytes 393224 | tf_op jit(solution)/shard_map/ppermute | solution.py:262
  0.5 0.0 copy-start.7
  0.5 0.7 %copy-done.7 = s32[64,1]{0,1:T(1,128)S(1)} copy-done((s32[64,1]{0,1:T(1,128)S(1)}, s32[64,1]{0,1:T(1,128)}, u32[]{:S(2)}) %copy-start.7) | copy-done | bytes 280
  1.1 0.4 %shard_map.91.chosen_ref = bf16[160,128]{1,0:T(8,128)(2,1)S(1)} custom-call(s32[1,64]{1,0:T(1,128)S(1)} %bitcast.17), custom_call_target="tpu_custom_call" | custom-call | tf_op jit(solution)/shard_map/pallas_call | solution.py:291
  1.5 0.1 collective-permute-done.other_ref
  1.7 0.4 %collective-permute-start.8 = (bf16[512,1024]{1,0:T(8,128)(2,1)}, bf16[512,1024]{1,0:T(8,128)(2,1)S(1)}, u32[]{:S(2)}, u32[]{:S(2)}) collective-permute-start(bf16[512,1024]{1,0:T(8,128)(2,1)} %w_own_ref), channel_id=1, source_target_pairs={{0,1},{1,0},{2,3},{3,2},{4,5},{5,4},{6,7},{7,6},{8,9},{9,8},{10,11... | collective-permute-start | bytes 3145736 | tf_op jit(solution)/shard_map/ppermute | solution.py:262
  2.0 0.0 copy-start.2
  2.0 0.9 %copy-done.2 = bf16[8,8,1024]{2,1,0:T(8,128)(2,1)S(1)} copy-done((bf16[8,8,1024]{2,1,0:T(8,128)(2,1)S(1)}, bf16[8,8,1024]{2,1,0:T(8,128)(2,1)}, u32[]{:S(2)}) %copy-start.2) | copy-done | bytes 131096
  2.9 0.2 shard_map.92
  3.2 4.8 %collective-permute-start.2 = (bf16[32,1024]{1,0:T(8,128)(2,1)S(1)}, bf16[32,1024]{1,0:T(8,128)(2,1)S(1)}, u32[]{:S(2)}, u32[]{:S(2)}) collective-permute-start(bf16[32,1024]{1,0:T(8,128)(2,1)S(1)} %get-tuple-element.53), channel_id=1, source_target_pairs={{0,12},{1,15},{2,14},{3,13},{4,8},{5,11},{6,10},{7,9},{8,4},{9,7},... | collective-permute-start | bytes 196616 | tf_op jit(solution)/shard_map/ppermute | solution.py:270
  8.0 0.4 %collective-permute-start.3 = (bf16[32,1024]{1,0:T(8,128)(2,1)S(1)}, bf16[32,1024]{1,0:T(8,128)(2,1)S(1)}, u32[]{:S(2)}, u32[]{:S(2)}) collective-permute-start(bf16[32,1024]{1,0:T(8,128)(2,1)S(1)} %get-tuple-element.54), channel_id=1, source_target_pairs={{1,9},{0,10},{3,11},{2,8},{5,13},{4,14},{7,15},{6,12},{9,1},{8,2},... | collective-permute-start | bytes 196616 | tf_op jit(solution)/shard_map/ppermute | solution.py:270
  8.4 1.1 %collective-permute-start.4 = (bf16[32,1024]{1,0:T(8,128)(2,1)S(1)}, bf16[32,1024]{1,0:T(8,128)(2,1)S(1)}, u32[]{:S(2)}, u32[]{:S(2)}) collective-permute-start(bf16[32,1024]{1,0:T(8,128)(2,1)S(1)} %get-tuple-element.55), channel_id=1, source_target_pairs={{1,5},{0,6},{3,7},{2,4},{5,1},{4,2},{7,3},{6,0},{9,13},{8,14},{11,... | collective-permute-start | bytes 196616 | tf_op jit(solution)/shard_map/ppermute | solution.py:270
  9.5 1.7 %collective-permute-start.1 = (bf16[32,1024]{1,0:T(8,128)(2,1)S(1)}, bf16[32,1024]{1,0:T(8,128)(2,1)S(1)}, u32[]{:S(2)}, u32[]{:S(2)}) collective-permute-start(bf16[32,1024]{1,0:T(8,128)(2,1)S(1)} %get-tuple-element.52), channel_id=1, source_target_pairs={{0,2},{2,0},{4,6},{6,4},{8,10},{10,8},{12,14},{14,12},{1,3},{3,1},... | collective-permute-start | bytes 196616 | tf_op jit(solution)/shard_map/ppermute | solution.py:275
  11.2 0.0 copy-start.5
  11.2 0.0 copy-start.9
  11.2 0.0 copy-start
  11.2 0.0 copy-start.1
  11.2 0.0 copy-start.6
  11.2 3.2 %copy.12 = bf16[1024,4,512]{2,0,1:T(8,128)(2,1)S(1)} copy(bf16[1024,4,512]{2,1,0:T(4,128)(2,1)} %param.11) | data formatting | bytes 8388608 | tf_op jit(solution)/shard_map/optimization_barrier | solution.py:299
  14.4 0.0 copy-done.5
  14.4 0.0 copy-done.8
  14.4 0.0 copy-done.9
  14.4 1.0 %shard_map.93 = (bf16[256,128]{1,0:T(8,128)(2,1)S(1)}, bf16[2048,128]{1,0:T(8,128)(2,1)S(1)}) custom-call(s32[1,64]{1,0:T(1,128)S(1)} %bitcast.18, s32[1,8]{1,0:T(1,128)S(1)} %bitcast.20, s32[32,64]{1,0:T(8,128)S(1)} %bitcast.14), custom_call_target="tpu_custom_call" | custom-call | tf_op jit(solution)/shard_map/pallas_call | solution.py:303
  15.4 0.0 collective-permute-done.2.refs_4_
  15.4 0.0 collective-permute-done.3.refs_3_
  15.4 0.0 collective-permute-done.4.refs_2_
  15.4 0.0 collective-permute-done.1.refs_1_
  15.4 0.1 collective-permute-start.5
  15.5 0.5 %collective-permute-start.6 = (bf16[32,1024]{1,0:T(8,128)(2,1)S(1)}, bf16[32,1024]{1,0:T(8,128)(2,1)S(1)}, u32[]{:S(2)}, u32[]{:S(2)}) collective-permute-start(bf16[32,1024]{1,0:T(8,128)(2,1)S(1)} %collective-permute-done.3.refs_3_), channel_id=1, source_target_pairs={{0,1},{1,0},{2,3},{3,2},{4,5},{5,4},{6,7},{7,6},{8,9},{9,8},{10,11... | collective-permute-start | bytes 196616 | tf_op jit(solution)/shard_map/ppermute | solution.py:262
  16.0 0.1 collective-permute-start.7
  16.1 0.7 %collective-permute-done.5.refs_5_ = bf16[32,1024]{1,0:T(8,128)(2,1)S(1)} collective-permute-done((bf16[32,1024]{1,0:T(8,128)(2,1)S(1)}, bf16[32,1024]{1,0:T(8,128)(2,1)S(1)}, u32[]{:S(2)}, u32[]{:S(2)}) %collective-permute-start.5) | collective-permute-done | bytes 65568 | tf_op jit(solution)/shard_map/ppermute | solution.py:262
  16.7 0.2 collective-permute-done.6.refs_6_
  16.9 0.4 collective-permute-done.7.refs_7_
  17.3 0.0 copy-done
  17.3 0.0 copy-done.1
  17.3 0.0 copy-done.6
  17.3 0.0 copy-start.3
  17.3 3.7 %shard_map.94 = (bf16[16,512]{1,0:T(8,128)(2,1)S(1)}, bf16[32,512]{1,0:T(8,128)(2,1)S(1)}, bf16[96,512]{1,0:T(8,128)(2,1)S(1)}, bf16[112,512]{1,0:T(8,128)(2,1)S(1)}) custom-call(bf16[8,128]{1,0:T(8,128)(2,1)S(1)} %bitcast.15, bf16[4,1024,512]{2,1,0:T(8,128)(2,1)S(1)} %bitcast.10, bf16[256,128]{1,0:T(8,128)(2,1)S(1)} %get-tuple-element.61.hide_rows_ref, ...), custom_call_target="tpu_custom_call" | custom-call | flops 2147483648 | bytes 4194304 | tf_op jit(solution)/shard_map/pallas_call | solution.py:311
  20.9 0.0 copy-start.4
  21.0 0.0 collective-permute-done.8.w_other_ref
  21.0 0.2 collective-permute-start.9
  21.2 0.0 copy-done.3
  21.2 0.9 %shard_map.95 = (bf16[2,64,512]{2,1,0:T(8,128)(2,1)S(1)}, bf16[2,64,512]{2,1,0:T(8,128)(2,1)S(1)}) custom-call(bf16[8,8,1024]{2,1,0:T(8,128)(2,1)S(1)} %copy-done.3, bf16[8,8,1024]{2,1,0:T(8,128)(2,1)S(1)} %collective-permute-done.other_ref, bf16[8,128]{1,0:T(8,128)(2,1)S(1)} %bitcast.16, bf16[4,1024,512]{2,1,0:T(8,128)(2,1)S(1)} %bitcast.11), custom_call_target="tpu_custom_call" | custom-call | flops 536870912 | bytes 4194304 | tf_op jit(solution)/shard_map/pallas_call | solution.py:332
  22.1 0.3 collective-permute-done.9.got_ref.refs_1_
  22.4 0.2 collective-permute-start.10
  22.5 3.7 %collective-permute-start.13 = (bf16[64,512]{1,0:T(8,128)(2,1)S(1)}, bf16[64,512]{1,0:T(8,128)(2,1)S(1)}, u32[]{:S(2)}, u32[]{:S(2)}) collective-permute-start(bf16[64,512]{1,0:T(8,128)(2,1)S(1)} %get-tuple-element.82), channel_id=1, source_target_pairs={{0,12},{1,15},{2,14},{3,13},{4,8},{5,11},{6,10},{7,9},{8,4},{9,7},... | collective-permute-start | bytes 196616 | tf_op jit(solution)/shard_map/ppermute | solution.py:270
  26.2 0.0 collective-permute-start.15
  26.2 1.7 %collective-permute-start.17 = (bf16[64,512]{1,0:T(8,128)(2,1)S(1)}, bf16[64,512]{1,0:T(8,128)(2,1)S(1)}, u32[]{:S(2)}, u32[]{:S(2)}) collective-permute-start(bf16[64,512]{1,0:T(8,128)(2,1)S(1)} %get-tuple-element.84), channel_id=1, source_target_pairs={{1,5},{0,6},{3,7},{2,4},{5,1},{4,2},{7,3},{6,0},{9,13},{8,14},{11,... | collective-permute-start | bytes 196616 | tf_op jit(solution)/shard_map/ppermute | solution.py:270
  27.9 0.7 %collective-permute-start.11 = (bf16[32,512]{1,0:T(8,128)(2,1)S(1)}, bf16[32,512]{1,0:T(8,128)(2,1)S(1)}, u32[]{:S(2)}, u32[]{:S(2)}) collective-permute-start(bf16[32,512]{1,0:T(8,128)(2,1)S(1)} %get-tuple-element.80), channel_id=1, source_target_pairs={{0,2},{2,0},{4,6},{6,4},{8,10},{10,8},{12,14},{14,12},{1,3},{3,1},... | collective-permute-start | bytes 98312 | tf_op jit(solution)/shard_map/ppermute | solution.py:275
  28.5 0.8 %collective-permute-done.13.refs_4_ = bf16[64,512]{1,0:T(8,128)(2,1)S(1)} collective-permute-done((bf16[64,512]{1,0:T(8,128)(2,1)S(1)}, bf16[64,512]{1,0:T(8,128)(2,1)S(1)}, u32[]{:S(2)}, u32[]{:S(2)}) %collective-permute-start.13) | collective-permute-done | bytes 65568 | tf_op jit(solution)/shard_map/ppermute | solution.py:270
  29.4 0.0 collective-permute-start.14
  29.4 3.1 %collective-permute-done.15.refs_6_ = bf16[64,512]{1,0:T(8,128)(2,1)S(1)} collective-permute-done((bf16[64,512]{1,0:T(8,128)(2,1)S(1)}, bf16[64,512]{1,0:T(8,128)(2,1)S(1)}, u32[]{:S(2)}, u32[]{:S(2)}) %collective-permute-start.15) | collective-permute-done | bytes 65568 | tf_op jit(solution)/shard_map/ppermute | solution.py:270
  32.5 0.0 collective-permute-start.16
  32.5 0.4 %collective-permute-done.17.refs_8_ = bf16[64,512]{1,0:T(8,128)(2,1)S(1)} collective-permute-done((bf16[64,512]{1,0:T(8,128)(2,1)S(1)}, bf16[64,512]{1,0:T(8,128)(2,1)S(1)}, u32[]{:S(2)}, u32[]{:S(2)}) %collective-permute-start.17) | collective-permute-done | bytes 65568 | tf_op jit(solution)/shard_map/ppermute | solution.py:270
  32.9 0.1 collective-permute-start.18
  33.0 0.0 collective-permute-done.11.refs_2_
  33.0 0.4 %collective-permute-start.12 = (bf16[16,512]{1,0:T(8,128)(2,1)S(1)}, bf16[16,512]{1,0:T(8,128)(2,1)S(1)}, u32[]{:S(2)}, u32[]{:S(2)}) collective-permute-start(bf16[16,512]{1,0:T(8,128)(2,1)S(1)} %slice.16), channel_id=1, source_target_pairs={{0,1},{1,0},{2,3},{3,2},{4,5},{5,4},{6,7},{7,6},{8,9},{9,8},{10,11... | collective-permute-start | bytes 49160 | tf_op jit(solution)/shard_map/ppermute | solution.py:262
  33.4 0.8 %collective-permute-done.12.refs_3_ = bf16[16,512]{1,0:T(8,128)(2,1)S(1)} collective-permute-done((bf16[16,512]{1,0:T(8,128)(2,1)S(1)}, bf16[16,512]{1,0:T(8,128)(2,1)S(1)}, u32[]{:S(2)}, u32[]{:S(2)}) %collective-permute-start.12) | collective-permute-done | bytes 16416 | tf_op jit(solution)/shard_map/ppermute | solution.py:262
  34.2 0.0 collective-permute-done.14.refs_5_
  34.2 0.0 collective-permute-done.16.refs_7_
  34.2 0.0 collective-permute-done.18.refs_9_
  34.2 0.0 collective-permute-done.10.got_ref
  34.3 0.0 copy-done.4
  34.3 1.9 %shard_map.97 = bf16[8,8,1024]{2,1,0:T(8,128)(2,1)} custom-call(s32[64]{0:T(128)S(1)} %bitcast.19, bf16[8,8,1024]{2,1,0:T(8,128)(2,1)S(1)} %copy-done.3, bf16[2,64,512]{2,1,0:T(8,128)(2,1)S(1)} %get-tuple-element.75.keep_ref, bf16[2,64,512]{2,1,0:T(8,128)(2,1)S(1)} %collective-permute-done.10.got_ref, bf16[512,1024]{1,0:T(8,128)(2,1)S(1)} %copy-done.4, ...), custom_call_target="tpu_custom_call" | custom-call | flops 268435456 | bytes 2097152 | tf_op jit(solution)/shard_map/pallas_call | solution.py:344
  (6 shorter events, 0.0 us)
Async XLA Ops:
  0.0 1.6 %collective-permute-start = (bf16[8,8,1024]{2,1,0:T(8,128)(2,1)}, bf16[8,8,1024]{2,1,0:T(8,128)(2,1)S(1)}, u32[]{:S(2)}, u32[]{:S(2)}) collective-permute-start(bf16[8,8,1024]{2,1,0:T(8,128)(2,1)} %own_ref.5), channel_id=1, source_target_pairs={{0,1},{1,0},{2,3},{3,2},{4,5},{5,4},{6,7},{7,6},{8,9},{9,8},{10,11... | collective-permute-start | bytes 393224 | tf_op jit(solution)/shard_map/ppermute | solution.py:262
  0.5 0.7 %copy-start.7 = (s32[64,1]{0,1:T(1,128)S(1)}, s32[64,1]{0,1:T(1,128)}, u32[]{:S(2)}) copy-start(s32[64,1]{0,1:T(1,128)} %param.15) | copy-start | bytes 772
  1.7 19.3 %collective-permute-start.8 = (bf16[512,1024]{1,0:T(8,128)(2,1)}, bf16[512,1024]{1,0:T(8,128)(2,1)S(1)}, u32[]{:S(2)}, u32[]{:S(2)}) collective-permute-start(bf16[512,1024]{1,0:T(8,128)(2,1)} %w_own_ref), channel_id=1, source_target_pairs={{0,1},{1,0},{2,3},{3,2},{4,5},{5,4},{6,7},{7,6},{8,9},{9,8},{10,11... | collective-permute-start | bytes 3145736 | tf_op jit(solution)/shard_map/ppermute | solution.py:262
  2.0 0.9 %copy-start.2 = (bf16[8,8,1024]{2,1,0:T(8,128)(2,1)S(1)}, bf16[8,8,1024]{2,1,0:T(8,128)(2,1)}, u32[]{:S(2)}) copy-start(bf16[8,8,1024]{2,1,0:T(8,128)(2,1)} %own_ref.5) | copy-start | bytes 393220
  3.2 12.2 %collective-permute-start.2 = (bf16[32,1024]{1,0:T(8,128)(2,1)S(1)}, bf16[32,1024]{1,0:T(8,128)(2,1)S(1)}, u32[]{:S(2)}, u32[]{:S(2)}) collective-permute-start(bf16[32,1024]{1,0:T(8,128)(2,1)S(1)} %get-tuple-element.53), channel_id=1, source_target_pairs={{0,12},{1,15},{2,14},{3,13},{4,8},{5,11},{6,10},{7,9},{8,4},{9,7},... | collective-permute-start | bytes 196616 | tf_op jit(solution)/shard_map/ppermute | solution.py:270
  8.0 7.4 %collective-permute-start.3 = (bf16[32,1024]{1,0:T(8,128)(2,1)S(1)}, bf16[32,1024]{1,0:T(8,128)(2,1)S(1)}, u32[]{:S(2)}, u32[]{:S(2)}) collective-permute-start(bf16[32,1024]{1,0:T(8,128)(2,1)S(1)} %get-tuple-element.54), channel_id=1, source_target_pairs={{1,9},{0,10},{3,11},{2,8},{5,13},{4,14},{7,15},{6,12},{9,1},{8,2},... | collective-permute-start | bytes 196616 | tf_op jit(solution)/shard_map/ppermute | solution.py:270
  8.4 7.0 %collective-permute-start.4 = (bf16[32,1024]{1,0:T(8,128)(2,1)S(1)}, bf16[32,1024]{1,0:T(8,128)(2,1)S(1)}, u32[]{:S(2)}, u32[]{:S(2)}) collective-permute-start(bf16[32,1024]{1,0:T(8,128)(2,1)S(1)} %get-tuple-element.55), channel_id=1, source_target_pairs={{1,5},{0,6},{3,7},{2,4},{5,1},{4,2},{7,3},{6,0},{9,13},{8,14},{11,... | collective-permute-start | bytes 196616 | tf_op jit(solution)/shard_map/ppermute | solution.py:270
  9.5 5.9 %collective-permute-start.1 = (bf16[32,1024]{1,0:T(8,128)(2,1)S(1)}, bf16[32,1024]{1,0:T(8,128)(2,1)S(1)}, u32[]{:S(2)}, u32[]{:S(2)}) collective-permute-start(bf16[32,1024]{1,0:T(8,128)(2,1)S(1)} %get-tuple-element.52), channel_id=1, source_target_pairs={{0,2},{2,0},{4,6},{6,4},{8,10},{10,8},{12,14},{14,12},{1,3},{3,1},... | collective-permute-start | bytes 196616 | tf_op jit(solution)/shard_map/ppermute | solution.py:275
  11.2 3.2 %copy-start.5 = (s32[64,32]{0,1:T(8,128)S(1)}, s32[64,32]{0,1:T(8,128)}, u32[]{:S(2)}) copy-start(s32[64,32]{0,1:T(8,128)} %param.17) | copy-start | bytes 24580
  11.2 3.2 %copy-start.8 = (s32[64,1]{0,1:T(1,128)S(1)}, s32[64,1]{0,1:T(1,128)}, u32[]{:S(2)}) copy-start(s32[64,1]{0,1:T(1,128)} %param.15) | copy-start | bytes 772
  11.2 3.2 %copy-start.9 = (s32[8]{0:T(128)S(1)}, s32[8]{0:T(128)}, u32[]{:S(2)}) copy-start(s32[8]{0:T(128)} %param.16) | copy-start | bytes 100
  11.2 6.1 %copy-start = (bf16[1,2048,512]{2,1,0:T(8,128)(2,1)S(1)}, bf16[1,2048,512]{2,1,0:T(8,128)(2,1)}, u32[]{:S(2)}) copy-start(bf16[1,2048,512]{2,1,0:T(8,128)(2,1)} %param.13) | copy-start | bytes 6291460
  11.2 6.1 %copy-start.1 = (bf16[1,2048,512]{2,1,0:T(8,128)(2,1)S(1)}, bf16[1,2048,512]{2,1,0:T(8,128)(2,1)}, u32[]{:S(2)}) copy-start(bf16[1,2048,512]{2,1,0:T(8,128)(2,1)} %param.14) | copy-start | bytes 6291460
  11.2 6.1 %copy-start.6 = (bf16[1024]{0:T(1024)(128)(2,1)S(1)}, bf16[1024]{0:T(1024)(128)(2,1)}, u32[]{:S(2)}) copy-start(bf16[1024]{0:T(1024)(128)(2,1)} %param.10) | copy-start | bytes 6148
  15.4 1.3 %collective-permute-start.5 = (bf16[32,1024]{1,0:T(8,128)(2,1)S(1)}, bf16[32,1024]{1,0:T(8,128)(2,1)S(1)}, u32[]{:S(2)}, u32[]{:S(2)}) collective-permute-start(bf16[32,1024]{1,0:T(8,128)(2,1)S(1)} %collective-permute-done.4.refs_2_), channel_id=1, source_target_pairs={{0,1},{1,0},{2,3},{3,2},{4,5},{5,4},{6,7},{7,6},{8,9},{9,8},{10,11... | collective-permute-start | bytes 196616 | tf_op jit(solution)/shard_map/ppermute | solution.py:262
  15.5 1.4 %collective-permute-start.6 = (bf16[32,1024]{1,0:T(8,128)(2,1)S(1)}, bf16[32,1024]{1,0:T(8,128)(2,1)S(1)}, u32[]{:S(2)}, u32[]{:S(2)}) collective-permute-start(bf16[32,1024]{1,0:T(8,128)(2,1)S(1)} %collective-permute-done.3.refs_3_), channel_id=1, source_target_pairs={{0,1},{1,0},{2,3},{3,2},{4,5},{5,4},{6,7},{7,6},{8,9},{9,8},{10,11... | collective-permute-start | bytes 196616 | tf_op jit(solution)/shard_map/ppermute | solution.py:262
  16.0 1.3 %collective-permute-start.7 = (bf16[32,1024]{1,0:T(8,128)(2,1)S(1)}, bf16[32,1024]{1,0:T(8,128)(2,1)S(1)}, u32[]{:S(2)}, u32[]{:S(2)}) collective-permute-start(bf16[32,1024]{1,0:T(8,128)(2,1)S(1)} %collective-permute-done.2.refs_4_), channel_id=1, source_target_pairs={{0,1},{1,0},{2,3},{3,2},{4,5},{5,4},{6,7},{7,6},{8,9},{9,8},{10,11... | collective-permute-start | bytes 196616 | tf_op jit(solution)/shard_map/ppermute | solution.py:262
  17.3 3.9 %copy-start.3 = (bf16[8,8,1024]{2,1,0:T(8,128)(2,1)S(1)}, bf16[8,8,1024]{2,1,0:T(8,128)(2,1)}, u32[]{:S(2)}) copy-start(bf16[8,8,1024]{2,1,0:T(8,128)(2,1)} %own_ref.5) | copy-start | bytes 393220
  20.9 13.3 %copy-start.4 = (bf16[512,1024]{1,0:T(8,128)(2,1)S(1)}, bf16[512,1024]{1,0:T(8,128)(2,1)}, u32[]{:S(2)}) copy-start(bf16[512,1024]{1,0:T(8,128)(2,1)} %w_own_ref) | copy-start | bytes 3145732
  21.0 1.4 %collective-permute-start.9 = (bf16[112,512]{1,0:T(8,128)(2,1)S(1)}, bf16[112,512]{1,0:T(8,128)(2,1)S(1)}, u32[]{:S(2)}, u32[]{:S(2)}) collective-permute-start(bf16[112,512]{1,0:T(8,128)(2,1)S(1)} %get-tuple-element.71), channel_id=1, source_target_pairs={{0,1},{1,0},{2,3},{3,2},{4,5},{5,4},{6,7},{7,6},{8,9},{9,8},{10,11... | collective-permute-start | bytes 344072 | tf_op jit(solution)/shard_map/ppermute | solution.py:262
  22.4 11.9 %collective-permute-start.10 = (bf16[2,64,512]{2,1,0:T(8,128)(2,1)S(1)}, bf16[2,64,512]{2,1,0:T(8,128)(2,1)S(1)}, u32[]{:S(2)}, u32[]{:S(2)}) collective-permute-start(bf16[2,64,512]{2,1,0:T(8,128)(2,1)S(1)} %get-tuple-element.76), channel_id=1, source_target_pairs={{0,1},{1,0},{2,3},{3,2},{4,5},{5,4},{6,7},{7,6},{8,9},{9,8},{10,11... | collective-permute-start | bytes 393224 | tf_op jit(solution)/shard_map/ppermute | solution.py:262
  22.5 6.9 %collective-permute-start.13 = (bf16[64,512]{1,0:T(8,128)(2,1)S(1)}, bf16[64,512]{1,0:T(8,128)(2,1)S(1)}, u32[]{:S(2)}, u32[]{:S(2)}) collective-permute-start(bf16[64,512]{1,0:T(8,128)(2,1)S(1)} %get-tuple-element.82), channel_id=1, source_target_pairs={{0,12},{1,15},{2,14},{3,13},{4,8},{5,11},{6,10},{7,9},{8,4},{9,7},... | collective-permute-start | bytes 196616 | tf_op jit(solution)/shard_map/ppermute | solution.py:270
  26.2 6.3 %collective-permute-start.15 = (bf16[64,512]{1,0:T(8,128)(2,1)S(1)}, bf16[64,512]{1,0:T(8,128)(2,1)S(1)}, u32[]{:S(2)}, u32[]{:S(2)}) collective-permute-start(bf16[64,512]{1,0:T(8,128)(2,1)S(1)} %get-tuple-element.83), channel_id=1, source_target_pairs={{1,9},{0,10},{3,11},{2,8},{5,13},{4,14},{7,15},{6,12},{9,1},{8,2},... | collective-permute-start | bytes 196616 | tf_op jit(solution)/shard_map/ppermute | solution.py:270
  26.2 6.7 %collective-permute-start.17 = (bf16[64,512]{1,0:T(8,128)(2,1)S(1)}, bf16[64,512]{1,0:T(8,128)(2,1)S(1)}, u32[]{:S(2)}, u32[]{:S(2)}) collective-permute-start(bf16[64,512]{1,0:T(8,128)(2,1)S(1)} %get-tuple-element.84), channel_id=1, source_target_pairs={{1,5},{0,6},{3,7},{2,4},{5,1},{4,2},{7,3},{6,0},{9,13},{8,14},{11,... | collective-permute-start | bytes 196616 | tf_op jit(solution)/shard_map/ppermute | solution.py:270
  27.9 5.1 %collective-permute-start.11 = (bf16[32,512]{1,0:T(8,128)(2,1)S(1)}, bf16[32,512]{1,0:T(8,128)(2,1)S(1)}, u32[]{:S(2)}, u32[]{:S(2)}) collective-permute-start(bf16[32,512]{1,0:T(8,128)(2,1)S(1)} %get-tuple-element.80), channel_id=1, source_target_pairs={{0,2},{2,0},{4,6},{6,4},{8,10},{10,8},{12,14},{14,12},{1,3},{3,1},... | collective-permute-start | bytes 98312 | tf_op jit(solution)/shard_map/ppermute | solution.py:275
  29.4 4.9 %collective-permute-start.14 = (bf16[32,512]{1,0:T(8,128)(2,1)S(1)}, bf16[32,512]{1,0:T(8,128)(2,1)S(1)}, u32[]{:S(2)}, u32[]{:S(2)}) collective-permute-start(bf16[32,512]{1,0:T(8,128)(2,1)S(1)} %slice.17), channel_id=1, source_target_pairs={{0,1},{1,0},{2,3},{3,2},{4,5},{5,4},{6,7},{7,6},{8,9},{9,8},{10,11... | collective-permute-start | bytes 98312 | tf_op jit(solution)/shard_map/ppermute | solution.py:262
  32.5 1.8 %collective-permute-start.16 = (bf16[32,512]{1,0:T(8,128)(2,1)S(1)}, bf16[32,512]{1,0:T(8,128)(2,1)S(1)}, u32[]{:S(2)}, u32[]{:S(2)}) collective-permute-start(bf16[32,512]{1,0:T(8,128)(2,1)S(1)} %slice.18), channel_id=1, source_target_pairs={{0,1},{1,0},{2,3},{3,2},{4,5},{5,4},{6,7},{7,6},{8,9},{9,8},{10,11... | collective-permute-start | bytes 98312 | tf_op jit(solution)/shard_map/ppermute | solution.py:262
  32.9 1.4 %collective-permute-start.18 = (bf16[32,512]{1,0:T(8,128)(2,1)S(1)}, bf16[32,512]{1,0:T(8,128)(2,1)S(1)}, u32[]{:S(2)}, u32[]{:S(2)}) collective-permute-start(bf16[32,512]{1,0:T(8,128)(2,1)S(1)} %slice.19), channel_id=1, source_target_pairs={{0,1},{1,0},{2,3},{3,2},{4,5},{5,4},{6,7},{7,6},{8,9},{9,8},{10,11... | collective-permute-start | bytes 98312 | tf_op jit(solution)/shard_map/ppermute | solution.py:262
  33.0 1.2 %collective-permute-start.12 = (bf16[16,512]{1,0:T(8,128)(2,1)S(1)}, bf16[16,512]{1,0:T(8,128)(2,1)S(1)}, u32[]{:S(2)}, u32[]{:S(2)}) collective-permute-start(bf16[16,512]{1,0:T(8,128)(2,1)S(1)} %slice.16), channel_id=1, source_target_pairs={{0,1},{1,0},{2,3},{3,2},{4,5},{5,4},{6,7},{7,6},{8,9},{9,8},{10,11... | collective-permute-start | bytes 49160 | tf_op jit(solution)/shard_map/ppermute | solution.py:262

commit v16 on v15

--- a/solution.py
+++ b/solution.py
@@ -44,8 +44,8 @@
     return jnp.concatenate([gain[at : at + 1] for at in range(gain.shape[0])], axis=1)
 
 
-def normed_rows(rows_ref, gain):
-    rows = rows_ref[...].astype(jnp.float32)
+def normed_rows(rows_ref, start, count, gain):
+    rows = rows_ref[start : start + count].astype(jnp.float32)
     rows = rows.reshape(-1, rows.shape[-1])
     mean_square = jnp.mean(rows * rows, axis=-1, keepdims=True)
     return (rows * lax.rsqrt(mean_square + EPS) * gain).astype(jnp.bfloat16)
@@ -150,8 +150,8 @@
 def self_kernel(own_ref, other_ref, gain_ref, w_ref, keep_ref, give_ref, normed_ref):
     rows, width = keep_ref.shape[1:]
     gain = gain_row(gain_ref)
-    normed_ref[:rows, :] = normed_rows(own_ref, gain)
-    normed_ref[rows:, :] = normed_rows(other_ref, gain)
+    normed_ref[:rows, :] = normed_rows(own_ref, 0, own_ref.shape[0], gain)
+    normed_ref[rows:, :] = normed_rows(other_ref, 0, other_ref.shape[0], gain)
     normed = normed_ref[...]
 
     def activated(part):
@@ -177,13 +177,21 @@
             out_ref[(2 * side + 1) * part : (2 * side + 2) * part, :] = got_ref[low : low + part, :]
 
 
+def stack_kernel(*refs):
+    *in_refs, out_ref = refs
+    rows = in_refs[0].shape[0]
+    for at, in_ref in enumerate(in_refs):
+        out_ref[at * rows : (at + 1) * rows, :] = in_ref[...]
+
+
 def history_kernel(owners, gain_ref, w_ref, hide_rows_ref, hide_cols_ref, keys_ref, values_ref, *refs):
-    slot_refs, (local_ref, near_ref, keep_ref, give_ref) = refs[:owners], refs[owners:]
+    *slot_refs, swapped_ref, local_ref, near_ref, keep_ref, give_ref = refs
     width = near_ref.shape[1]
     per_owner = near_ref.shape[0]
     half = per_owner // 2
     far = [(ref, at * per_owner, 0, per_owner) for ref in (keep_ref, give_ref) for at in range(owners // 2 - 1)]
     local = [(local_ref, 0, 0, half), (give_ref, (owners // 2 - 1) * per_owner, half, half)]
+    sources = [(ref, 0) for ref in slot_refs] + [(swapped_ref, at * per_owner) for at in range(owners // 2 - 1)]
     targets = [local, [(near_ref, 0, 0, per_owner)]] + [[target] for target in far]
     hist_rows = keys_ref.shape[0]
     span = min(256, hist_rows)
@@ -191,7 +199,7 @@
     gain = gain_row(gain_ref)
     for first in range(0, owners, per_step):
         group = range(first, min(first + per_step, owners))
-        normed = jnp.concatenate([normed_rows(slot_refs[at], gain) for at in group], axis=0)
+        normed = jnp.concatenate([normed_rows(*sources[at], per_owner, gain) for at in group], axis=0)
         queries = silu(jnp.dot(normed, w_ref[0], preferred_element_type=jnp.float32)).astype(jnp.bfloat16)
         hide_rows = hide_rows_ref[first * per_owner : first * per_owner + queries.shape[0], :]
         for low in range(0, width, HD):
@@ -300,18 +308,20 @@
     weights = jnp.transpose(w_in, (1, 0, 2))
     near = to_neighbour(owners, near)
     came = cross(owners, out)
+    near, came, weights = lax.optimization_barrier((near, came, weights))
+    stacked = kernel_call(stack_kernel, bf16((messages * piece, model_width)), [vmem] * messages)(*reversed(came))
     visible = kernel_call(
         visible_kernel,
         [bf16((owners * piece, HD)), bf16((hist_rows, HD))],
         [vmem] * 3,
         [pltpu.VMEM((HD, owners * req_count), jnp.bfloat16)],
-    )(session_row, hist_len.reshape(1, -1), lax.optimization_barrier((block_mask.T, out))[0])
-    near, came, weights, (hide_rows, hide_cols) = lax.optimization_barrier((near, came, weights, visible))
-    swapped = [swap(message) for message in came]
+        flops=2 * messages * piece * model_width * width,
+    )(session_row, hist_len.reshape(1, -1), lax.optimization_barrier((block_mask.T, stacked))[0])
+    swapped, (hide_rows, hide_cols) = lax.optimization_barrier((swap(stacked), visible))
     local, near, keep, give = kernel_call(
         functools.partial(history_kernel, owners),
         [bf16((rows_out, width)) for rows_out in (piece // 2, piece, messages * piece, messages * piece + piece // 2)],
-        [vmem] * (6 + owners),
+        [vmem] * (6 + owners // 2 + 2),
         flops=8 * owners * piece * hist_rows * width,
         moved=4 * hist_rows * width,
     )(
@@ -324,7 +334,7 @@
         local,
         near,
         *reversed(came),
-        *reversed(swapped),
+        swapped,
     )
     near = to_neighbour(owners, near)
     keep, give, w_other = lax.optimization_barrier((keep, give, w_other))

time: 36.3 us -> 36.6 us (level)
  waiting for transfers between devices: 6.79 us -> 7.19 us
    ppermute x2, starting transfers between devices: 2.32 us -> 3.57 us  [to_neighbour(): lax.ppermute(rows, 'cache', [(place, place ^ 1) for place in range(owners)])]
    ppermute x6, starting transfers between devices: 11.7 us -> 10.6 us  [cross(): came.append(lax.ppermute(messages[at], ('cache', 'serve'), pairs))]
    ppermute x6, waiting for transfers between devices: 4.33 us -> 5.2 us  [cross(): came.append(lax.ppermute(messages[at], ('cache', 'serve'), pairs))]
    ppermute x11 -> x9, waiting for transfers between devices: 2.45 us -> 1.99 us  [swap(): return lax.ppermute(rows, 'serve', [(0, 1), (1, 0)])]
    ppermute x11 -> x9, starting transfers between devices: 2.34 us -> 2.17 us  [swap(): return lax.ppermute(rows, 'serve', [(0, 1), (1, 0)])]
  transfers between devices with their start and end apart: 19 -> 17, of which waited for: 9 -> 7; matrix products, arithmetic and copies ran while one was open for 9% -> 8% of each run, Pallas kernels for 17% -> 17%
where the time goes in v16:
time: 36.6 us; the launch traced here: 36.4 us
  starting transfers between devices  16.4 us (45%)
  Pallas kernels  7.98 us (22%)
  waiting for transfers between devices  7.19 us (20%)
  local copies, waits for them, and re-layouts  4.64 us (13%)
    ppermute x6, starting transfers between devices, cross(): came.append(lax.ppermute(messages[at], ('cache', 'serve'), pairs))  10.6 us
    ppermute x6, waiting for transfers between devices, cross(): came.append(lax.ppermute(messages[at], ('cache', 'serve'), pairs))  5.2 us
    pallas_call x1, Pallas kernels, body(): kernel_call(functools.partial(history_kernel, owners), [bf16((rows_out, w...  3.64 us
    ppermute x2, starting transfers between devices, to_neighbour(): lax.ppermute(rows, 'cache', [(place, place ^ 1) for place in range(owners)])  3.57 us
    optimization_barrier x1, local copies, waits for them, and re-layouts, body(): (local, near, *out), w_in = lax.optimization_barrier((out, w_in))  3.02 us
    ppermute x9, starting transfers between devices, swap(): return lax.ppermute(rows, 'serve', [(0, 1), (1, 0)])  2.17 us
    ppermute x9, waiting for transfers between devices, swap(): return lax.ppermute(rows, 'serve', [(0, 1), (1, 0)])  1.99 us
    pallas_call x1, Pallas kernels, body(): kernel_call(functools.partial(output_kernel, owners), bf16((req_count, ha...  1.85 us
  transfers between devices with their start and end apart: 17, of which 7 were waited for; matrix products, arithmetic and copies ran while one was open for 8% of the time, Pallas kernels for 17%

profile of v16, /device:TPU:0, one launch (start us, length us, event | category | flops | bytes accessed | tf_op | source)
XLA Modules:
  0.0 36.4 jit_solution(14733545521482879012)
XLA Ops:
  0.0 0.5 %collective-permute-start = (bf16[8,8,1024]{2,1,0:T(8,128)(2,1)}, bf16[8,8,1024]{2,1,0:T(8,128)(2,1)S(1)}, u32[]{:S(2)}, u32[]{:S(2)}) collective-permute-start(bf16[8,8,1024]{2,1,0:T(8,128)(2,1)} %own_ref.5), channel_id=1, source_target_pairs={{0,1},{1,0},{2,3},{3,2},{4,5},{5,4},{6,7},{7,6},{8,9},{9,8},{10,11... | collective-permute-start | bytes 393224 | tf_op jit(solution)/shard_map/ppermute | solution.py:270
  0.5 0.0 copy-start.6
  0.5 0.7 %copy-done.6 = s32[64,1]{0,1:T(1,128)S(1)} copy-done((s32[64,1]{0,1:T(1,128)S(1)}, s32[64,1]{0,1:T(1,128)}, u32[]{:S(2)}) %copy-start.6) | copy-done | bytes 280
  1.1 0.4 %shard_map.91.chosen_ref = bf16[160,128]{1,0:T(8,128)(2,1)S(1)} custom-call(s32[1,64]{1,0:T(1,128)S(1)} %bitcast.16), custom_call_target="tpu_custom_call" | custom-call | tf_op jit(solution)/shard_map/pallas_call | solution.py:299
  1.5 0.1 collective-permute-done.other_ref
  1.7 0.4 collective-permute-start.6
  2.0 0.0 copy-start.2
  2.0 0.9 %copy-done.2 = bf16[8,8,1024]{2,1,0:T(8,128)(2,1)S(1)} copy-done((bf16[8,8,1024]{2,1,0:T(8,128)(2,1)S(1)}, bf16[8,8,1024]{2,1,0:T(8,128)(2,1)}, u32[]{:S(2)}) %copy-start.2) | copy-done | bytes 131096
  2.9 0.2 shard_map.92
  3.2 0.0 copy-start.7
  3.2 0.0 copy-start.8
  3.2 0.0 copy-start.9
  3.2 0.0 copy-start
  3.2 0.0 copy-start.1
  3.2 0.0 copy-start.5
  3.2 2.7 %collective-permute-start.1 = (bf16[32,1024]{1,0:T(8,128)(2,1)S(1)}, bf16[32,1024]{1,0:T(8,128)(2,1)S(1)}, u32[]{:S(2)}, u32[]{:S(2)}) collective-permute-start(bf16[32,1024]{1,0:T(8,128)(2,1)S(1)} %get-tuple-element.53), channel_id=1, source_target_pairs={{0,2},{2,0},{4,6},{6,4},{8,10},{10,8},{12,14},{14,12},{1,3},{3,1},... | collective-permute-start | bytes 196616 | tf_op jit(solution)/shard_map/ppermute | solution.py:283
  6.0 3.6 %collective-permute-start.2 = (bf16[32,1024]{1,0:T(8,128)(2,1)S(1)}, bf16[32,1024]{1,0:T(8,128)(2,1)S(1)}, u32[]{:S(2)}, u32[]{:S(2)}) collective-permute-start(bf16[32,1024]{1,0:T(8,128)(2,1)S(1)} %get-tuple-element.54), channel_id=1, source_target_pairs={{0,12},{1,15},{2,14},{3,13},{4,8},{5,11},{6,10},{7,9},{8,4},{9,7},... | collective-permute-start | bytes 196616 | tf_op jit(solution)/shard_map/ppermute | solution.py:278
  9.6 0.0 collective-permute-start.3
  9.6 1.7 %collective-permute-start.4 = (bf16[32,1024]{1,0:T(8,128)(2,1)S(1)}, bf16[32,1024]{1,0:T(8,128)(2,1)S(1)}, u32[]{:S(2)}, u32[]{:S(2)}) collective-permute-start(bf16[32,1024]{1,0:T(8,128)(2,1)S(1)} %get-tuple-element.56), channel_id=1, source_target_pairs={{1,5},{0,6},{3,7},{2,4},{5,1},{4,2},{7,3},{6,0},{9,13},{8,14},{11,... | collective-permute-start | bytes 196616 | tf_op jit(solution)/shard_map/ppermute | solution.py:278
  11.3 3.0 %copy.12 = bf16[1024,4,512]{2,0,1:T(8,128)(2,1)S(1)} copy(bf16[1024,4,512]{2,1,0:T(4,128)(2,1)} %param.11) | data formatting | bytes 8388608 | tf_op jit(solution)/shard_map/optimization_barrier | solution.py:307
  14.3 0.0 collective-permute-done.1.refs_1_
  14.3 0.0 collective-permute-done.2.refs_2_.refs_4_
  14.3 1.8 %collective-permute-done.3.refs_1_.refs_3_ = bf16[32,1024]{1,0:T(8,128)(2,1)S(1)} collective-permute-done((bf16[32,1024]{1,0:T(8,128)(2,1)S(1)}, bf16[32,1024]{1,0:T(8,128)(2,1)S(1)}, u32[]{:S(2)}, u32[]{:S(2)}) %collective-permute-start.3) | collective-permute-done | bytes 65568 | tf_op jit(solution)/shard_map/ppermute | solution.py:278
  16.1 0.0 collective-permute-done.4.refs_0_.refs_2_
  16.2 0.1 collective-permute-start.5
  16.2 0.0 copy-done.7
  16.2 0.0 copy-done.8
  16.2 0.0 copy-done.9
  16.3 1.0 %shard_map.94 = (bf16[256,128]{1,0:T(8,128)(2,1)S(1)}, bf16[2048,128]{1,0:T(8,128)(2,1)S(1)}) custom-call(s32[1,64]{1,0:T(1,128)S(1)} %bitcast.17, s32[1,8]{1,0:T(1,128)S(1)} %bitcast.20, s32[32,64]{1,0:T(8,128)S(1)} %bitcast.19), custom_call_target="tpu_custom_call" | custom-call | flops 100663296 | tf_op jit(solution)/shard_map/pallas_call | solution.py:313
  17.2 0.4 %collective-permute-done.5.refs_5_ = bf16[96,1024]{1,0:T(8,128)(2,1)S(1)} collective-permute-done((bf16[96,1024]{1,0:T(8,128)(2,1)S(1)}, bf16[96,1024]{1,0:T(8,128)(2,1)S(1)}, u32[]{:S(2)}, u32[]{:S(2)}) %collective-permute-start.5) | collective-permute-done | bytes 196640 | tf_op jit(solution)/shard_map/ppermute | solution.py:270
  17.7 0.0 copy-done
  17.7 0.0 copy-done.1
  17.7 0.0 copy-done.5
  17.7 0.0 copy-start.3
  17.7 3.6 %shard_map.95 = (bf16[16,512]{1,0:T(8,128)(2,1)S(1)}, bf16[32,512]{1,0:T(8,128)(2,1)S(1)}, bf16[96,512]{1,0:T(8,128)(2,1)S(1)}, bf16[112,512]{1,0:T(8,128)(2,1)S(1)}) custom-call(bf16[8,128]{1,0:T(8,128)(2,1)S(1)} %bitcast.14, bf16[4,1024,512]{2,1,0:T(8,128)(2,1)S(1)} %bitcast.10, bf16[256,128]{1,0:T(8,128)(2,1)S(1)} %get-tuple-element.65.hide_rows_ref, ...), custom_call_target="tpu_custom_call" | custom-call | flops 2147483648 | bytes 4194304 | tf_op jit(solution)/shard_map/pallas_call | solution.py:321
  21.3 0.0 copy-start.4
  21.3 0.0 collective-permute-done.6.w_other_ref
  21.3 0.2 collective-permute-start.7
  21.5 0.0 copy-done.3
  21.5 0.9 %shard_map.96 = (bf16[2,64,512]{2,1,0:T(8,128)(2,1)S(1)}, bf16[2,64,512]{2,1,0:T(8,128)(2,1)S(1)}) custom-call(bf16[8,8,1024]{2,1,0:T(8,128)(2,1)S(1)} %copy-done.3, bf16[8,8,1024]{2,1,0:T(8,128)(2,1)S(1)} %collective-permute-done.other_ref, bf16[8,128]{1,0:T(8,128)(2,1)S(1)} %bitcast.15, bf16[4,1024,512]{2,1,0:T(8,128)(2,1)S(1)} %bitcast.11), custom_call_target="tpu_custom_call" | custom-call | flops 536870912 | bytes 4194304 | tf_op jit(solution)/shard_map/pallas_call | solution.py:342
  22.4 0.3 collective-permute-done.7.got_ref.refs_1_
  22.7 0.2 collective-permute-start.8
  22.9 2.5 %collective-permute-start.11 = (bf16[64,512]{1,0:T(8,128)(2,1)S(1)}, bf16[64,512]{1,0:T(8,128)(2,1)S(1)}, u32[]{:S(2)}, u32[]{:S(2)}) collective-permute-start(bf16[64,512]{1,0:T(8,128)(2,1)S(1)} %get-tuple-element.84), channel_id=1, source_target_pairs={{0,12},{1,15},{2,14},{3,13},{4,8},{5,11},{6,10},{7,9},{8,4},{9,7},... | collective-permute-start | bytes 196616 | tf_op jit(solution)/shard_map/ppermute | solution.py:278
  25.4 0.2 collective-permute-start.13
  25.6 2.6 %collective-permute-start.15 = (bf16[64,512]{1,0:T(8,128)(2,1)S(1)}, bf16[64,512]{1,0:T(8,128)(2,1)S(1)}, u32[]{:S(2)}, u32[]{:S(2)}) collective-permute-start(bf16[64,512]{1,0:T(8,128)(2,1)S(1)} %get-tuple-element.86), channel_id=1, source_target_pairs={{1,5},{0,6},{3,7},{2,4},{5,1},{4,2},{7,3},{6,0},{9,13},{8,14},{11,... | collective-permute-start | bytes 196616 | tf_op jit(solution)/shard_map/ppermute | solution.py:278
  28.3 0.8 %collective-permute-start.9 = (bf16[32,512]{1,0:T(8,128)(2,1)S(1)}, bf16[32,512]{1,0:T(8,128)(2,1)S(1)}, u32[]{:S(2)}, u32[]{:S(2)}) collective-permute-start(bf16[32,512]{1,0:T(8,128)(2,1)S(1)} %get-tuple-element.82), channel_id=1, source_target_pairs={{0,2},{2,0},{4,6},{6,4},{8,10},{10,8},{12,14},{14,12},{1,3},{3,1},... | collective-permute-start | bytes 98312 | tf_op jit(solution)/shard_map/ppermute | solution.py:283
  29.1 0.6 %collective-permute-done.11.refs_4_ = bf16[64,512]{1,0:T(8,128)(2,1)S(1)} collective-permute-done((bf16[64,512]{1,0:T(8,128)(2,1)S(1)}, bf16[64,512]{1,0:T(8,128)(2,1)S(1)}, u32[]{:S(2)}, u32[]{:S(2)}) %collective-permute-start.11) | collective-permute-done | bytes 65568 | tf_op jit(solution)/shard_map/ppermute | solution.py:278
  29.7 0.3 collective-permute-start.12
  30.0 2.8 %collective-permute-done.13.refs_6_ = bf16[64,512]{1,0:T(8,128)(2,1)S(1)} collective-permute-done((bf16[64,512]{1,0:T(8,128)(2,1)S(1)}, bf16[64,512]{1,0:T(8,128)(2,1)S(1)}, u32[]{:S(2)}, u32[]{:S(2)}) %collective-permute-start.13) | collective-permute-done | bytes 65568 | tf_op jit(solution)/shard_map/ppermute | solution.py:278
  32.8 0.0 collective-permute-start.14
  32.8 0.0 collective-permute-done.15.refs_8_
  32.8 0.5 %collective-permute-start.16 = (bf16[32,512]{1,0:T(8,128)(2,1)S(1)}, bf16[32,512]{1,0:T(8,128)(2,1)S(1)}, u32[]{:S(2)}, u32[]{:S(2)}) collective-permute-start(bf16[32,512]{1,0:T(8,128)(2,1)S(1)} %slice.19), channel_id=1, source_target_pairs={{0,1},{1,0},{2,3},{3,2},{4,5},{5,4},{6,7},{7,6},{8,9},{9,8},{10,11... | collective-permute-start | bytes 98312 | tf_op jit(solution)/shard_map/ppermute | solution.py:270
  33.3 0.0 collective-permute-done.9.refs_2_
  33.3 0.1 collective-permute-start.10
  33.4 1.1 %collective-permute-done.10.refs_3_ = bf16[16,512]{1,0:T(8,128)(2,1)S(1)} collective-permute-done((bf16[16,512]{1,0:T(8,128)(2,1)S(1)}, bf16[16,512]{1,0:T(8,128)(2,1)S(1)}, u32[]{:S(2)}, u32[]{:S(2)}) %collective-permute-start.10) | collective-permute-done | bytes 16416 | tf_op jit(solution)/shard_map/ppermute | solution.py:270
  34.5 0.0 collective-permute-done.12.refs_5_
  34.5 0.0 collective-permute-done.14.refs_7_
  34.5 0.0 collective-permute-done.16.refs_9_
  34.5 0.0 collective-permute-done.8.got_ref
  34.5 0.0 copy-done.4
  34.6 1.9 %shard_map.98 = bf16[8,8,1024]{2,1,0:T(8,128)(2,1)} custom-call(s32[64]{0:T(128)S(1)} %bitcast.18, bf16[8,8,1024]{2,1,0:T(8,128)(2,1)S(1)} %copy-done.3, bf16[2,64,512]{2,1,0:T(8,128)(2,1)S(1)} %get-tuple-element.77.keep_ref, bf16[2,64,512]{2,1,0:T(8,128)(2,1)S(1)} %collective-permute-done.8.got_ref, bf16[512,1024]{1,0:T(8,128)(2,1)S(1)} %copy-done.4, ...), custom_call_target="tpu_custom_call" | custom-call | flops 268435456 | bytes 2097152 | tf_op jit(solution)/shard_map/pallas_call | solution.py:354
  (6 shorter events, 0.0 us)
Async XLA Ops:
  0.0 1.6 %collective-permute-start = (bf16[8,8,1024]{2,1,0:T(8,128)(2,1)}, bf16[8,8,1024]{2,1,0:T(8,128)(2,1)S(1)}, u32[]{:S(2)}, u32[]{:S(2)}) collective-permute-start(bf16[8,8,1024]{2,1,0:T(8,128)(2,1)} %own_ref.5), channel_id=1, source_target_pairs={{0,1},{1,0},{2,3},{3,2},{4,5},{5,4},{6,7},{7,6},{8,9},{9,8},{10,11... | collective-permute-start | bytes 393224 | tf_op jit(solution)/shard_map/ppermute | solution.py:270
  0.5 0.7 %copy-start.6 = (s32[64,1]{0,1:T(1,128)S(1)}, s32[64,1]{0,1:T(1,128)}, u32[]{:S(2)}) copy-start(s32[64,1]{0,1:T(1,128)} %param.15) | copy-start | bytes 772
  1.7 19.7 %collective-permute-start.6 = (bf16[512,1024]{1,0:T(8,128)(2,1)}, bf16[512,1024]{1,0:T(8,128)(2,1)S(1)}, u32[]{:S(2)}, u32[]{:S(2)}) collective-permute-start(bf16[512,1024]{1,0:T(8,128)(2,1)} %w_own_ref), channel_id=1, source_target_pairs={{0,1},{1,0},{2,3},{3,2},{4,5},{5,4},{6,7},{7,6},{8,9},{9,8},{10,11... | collective-permute-start | bytes 3145736 | tf_op jit(solution)/shard_map/ppermute | solution.py:270
  2.0 0.9 %copy-start.2 = (bf16[8,8,1024]{2,1,0:T(8,128)(2,1)S(1)}, bf16[8,8,1024]{2,1,0:T(8,128)(2,1)}, u32[]{:S(2)}) copy-start(bf16[8,8,1024]{2,1,0:T(8,128)(2,1)} %own_ref.5) | copy-start | bytes 393220
  3.2 13.1 %copy-start.7 = (s32[64,1]{0,1:T(1,128)S(1)}, s32[64,1]{0,1:T(1,128)}, u32[]{:S(2)}) copy-start(s32[64,1]{0,1:T(1,128)} %param.15) | copy-start | bytes 772
  3.2 13.1 %copy-start.8 = (s32[64,32]{0,1:T(8,128)S(1)}, s32[64,32]{0,1:T(8,128)}, u32[]{:S(2)}) copy-start(s32[64,32]{0,1:T(8,128)} %param.17) | copy-start | bytes 24580
  3.2 13.1 %copy-start.9 = (s32[8]{0:T(128)S(1)}, s32[8]{0:T(128)}, u32[]{:S(2)}) copy-start(s32[8]{0:T(128)} %param.16) | copy-start | bytes 100
  3.2 14.5 %copy-start = (bf16[1,2048,512]{2,1,0:T(8,128)(2,1)S(1)}, bf16[1,2048,512]{2,1,0:T(8,128)(2,1)}, u32[]{:S(2)}) copy-start(bf16[1,2048,512]{2,1,0:T(8,128)(2,1)} %param.13) | copy-start | bytes 6291460
  3.2 14.5 %copy-start.1 = (bf16[1,2048,512]{2,1,0:T(8,128)(2,1)S(1)}, bf16[1,2048,512]{2,1,0:T(8,128)(2,1)}, u32[]{:S(2)}) copy-start(bf16[1,2048,512]{2,1,0:T(8,128)(2,1)} %param.14) | copy-start | bytes 6291460
  3.2 14.5 %copy-start.5 = (bf16[1024]{0:T(1024)(128)(2,1)S(1)}, bf16[1024]{0:T(1024)(128)(2,1)}, u32[]{:S(2)}) copy-start(bf16[1024]{0:T(1024)(128)(2,1)} %param.10) | copy-start | bytes 6148
  3.2 11.1 %collective-permute-start.1 = (bf16[32,1024]{1,0:T(8,128)(2,1)S(1)}, bf16[32,1024]{1,0:T(8,128)(2,1)S(1)}, u32[]{:S(2)}, u32[]{:S(2)}) collective-permute-start(bf16[32,1024]{1,0:T(8,128)(2,1)S(1)} %get-tuple-element.53), channel_id=1, source_target_pairs={{0,2},{2,0},{4,6},{6,4},{8,10},{10,8},{12,14},{14,12},{1,3},{3,1},... | collective-permute-start | bytes 196616 | tf_op jit(solution)/shard_map/ppermute | solution.py:283
  6.0 8.3 %collective-permute-start.2 = (bf16[32,1024]{1,0:T(8,128)(2,1)S(1)}, bf16[32,1024]{1,0:T(8,128)(2,1)S(1)}, u32[]{:S(2)}, u32[]{:S(2)}) collective-permute-start(bf16[32,1024]{1,0:T(8,128)(2,1)S(1)} %get-tuple-element.54), channel_id=1, source_target_pairs={{0,12},{1,15},{2,14},{3,13},{4,8},{5,11},{6,10},{7,9},{8,4},{9,7},... | collective-permute-start | bytes 196616 | tf_op jit(solution)/shard_map/ppermute | solution.py:278
  9.6 6.5 %collective-permute-start.3 = (bf16[32,1024]{1,0:T(8,128)(2,1)S(1)}, bf16[32,1024]{1,0:T(8,128)(2,1)S(1)}, u32[]{:S(2)}, u32[]{:S(2)}) collective-permute-start(bf16[32,1024]{1,0:T(8,128)(2,1)S(1)} %get-tuple-element.55), channel_id=1, source_target_pairs={{1,9},{0,10},{3,11},{2,8},{5,13},{4,14},{7,15},{6,12},{9,1},{8,2},... | collective-permute-start | bytes 196616 | tf_op jit(solution)/shard_map/ppermute | solution.py:278
  9.6 6.5 %collective-permute-start.4 = (bf16[32,1024]{1,0:T(8,128)(2,1)S(1)}, bf16[32,1024]{1,0:T(8,128)(2,1)S(1)}, u32[]{:S(2)}, u32[]{:S(2)}) collective-permute-start(bf16[32,1024]{1,0:T(8,128)(2,1)S(1)} %get-tuple-element.56), channel_id=1, source_target_pairs={{1,5},{0,6},{3,7},{2,4},{5,1},{4,2},{7,3},{6,0},{9,13},{8,14},{11,... | collective-permute-start | bytes 196616 | tf_op jit(solution)/shard_map/ppermute | solution.py:278
  16.2 1.5 %collective-permute-start.5 = (bf16[96,1024]{1,0:T(8,128)(2,1)S(1)}, bf16[96,1024]{1,0:T(8,128)(2,1)S(1)}, u32[]{:S(2)}, u32[]{:S(2)}) collective-permute-start(bf16[96,1024]{1,0:T(8,128)(2,1)S(1)} %shard_map.93), channel_id=1, source_target_pairs={{0,1},{1,0},{2,3},{3,2},{4,5},{5,4},{6,7},{7,6},{8,9},{9,8},{10,11... | collective-permute-start | bytes 589832 | tf_op jit(solution)/shard_map/ppermute | solution.py:270
  17.7 3.9 %copy-start.3 = (bf16[8,8,1024]{2,1,0:T(8,128)(2,1)S(1)}, bf16[8,8,1024]{2,1,0:T(8,128)(2,1)}, u32[]{:S(2)}) copy-start(bf16[8,8,1024]{2,1,0:T(8,128)(2,1)} %own_ref.5) | copy-start | bytes 393220
  21.3 13.2 %copy-start.4 = (bf16[512,1024]{1,0:T(8,128)(2,1)S(1)}, bf16[512,1024]{1,0:T(8,128)(2,1)}, u32[]{:S(2)}) copy-start(bf16[512,1024]{1,0:T(8,128)(2,1)} %w_own_ref) | copy-start | bytes 3145732
  21.3 1.4 %collective-permute-start.7 = (bf16[112,512]{1,0:T(8,128)(2,1)S(1)}, bf16[112,512]{1,0:T(8,128)(2,1)S(1)}, u32[]{:S(2)}, u32[]{:S(2)}) collective-permute-start(bf16[112,512]{1,0:T(8,128)(2,1)S(1)} %get-tuple-element.73), channel_id=1, source_target_pairs={{0,1},{1,0},{2,3},{3,2},{4,5},{5,4},{6,7},{7,6},{8,9},{9,8},{10,11... | collective-permute-start | bytes 344072 | tf_op jit(solution)/shard_map/ppermute | solution.py:270
  22.7 11.8 %collective-permute-start.8 = (bf16[2,64,512]{2,1,0:T(8,128)(2,1)S(1)}, bf16[2,64,512]{2,1,0:T(8,128)(2,1)S(1)}, u32[]{:S(2)}, u32[]{:S(2)}) collective-permute-start(bf16[2,64,512]{2,1,0:T(8,128)(2,1)S(1)} %get-tuple-element.78), channel_id=1, source_target_pairs={{0,1},{1,0},{2,3},{3,2},{4,5},{5,4},{6,7},{7,6},{8,9},{9,8},{10,11... | collective-permute-start | bytes 393224 | tf_op jit(solution)/shard_map/ppermute | solution.py:270
  22.9 6.8 %collective-permute-start.11 = (bf16[64,512]{1,0:T(8,128)(2,1)S(1)}, bf16[64,512]{1,0:T(8,128)(2,1)S(1)}, u32[]{:S(2)}, u32[]{:S(2)}) collective-permute-start(bf16[64,512]{1,0:T(8,128)(2,1)S(1)} %get-tuple-element.84), channel_id=1, source_target_pairs={{0,12},{1,15},{2,14},{3,13},{4,8},{5,11},{6,10},{7,9},{8,4},{9,7},... | collective-permute-start | bytes 196616 | tf_op jit(solution)/shard_map/ppermute | solution.py:278
  25.4 7.4 %collective-permute-start.13 = (bf16[64,512]{1,0:T(8,128)(2,1)S(1)}, bf16[64,512]{1,0:T(8,128)(2,1)S(1)}, u32[]{:S(2)}, u32[]{:S(2)}) collective-permute-start(bf16[64,512]{1,0:T(8,128)(2,1)S(1)} %get-tuple-element.85), channel_id=1, source_target_pairs={{1,9},{0,10},{3,11},{2,8},{5,13},{4,14},{7,15},{6,12},{9,1},{8,2},... | collective-permute-start | bytes 196616 | tf_op jit(solution)/shard_map/ppermute | solution.py:278
  25.6 7.2 %collective-permute-start.15 = (bf16[64,512]{1,0:T(8,128)(2,1)S(1)}, bf16[64,512]{1,0:T(8,128)(2,1)S(1)}, u32[]{:S(2)}, u32[]{:S(2)}) collective-permute-start(bf16[64,512]{1,0:T(8,128)(2,1)S(1)} %get-tuple-element.86), channel_id=1, source_target_pairs={{1,5},{0,6},{3,7},{2,4},{5,1},{4,2},{7,3},{6,0},{9,13},{8,14},{11,... | collective-permute-start | bytes 196616 | tf_op jit(solution)/shard_map/ppermute | solution.py:278
  28.3 5.1 %collective-permute-start.9 = (bf16[32,512]{1,0:T(8,128)(2,1)S(1)}, bf16[32,512]{1,0:T(8,128)(2,1)S(1)}, u32[]{:S(2)}, u32[]{:S(2)}) collective-permute-start(bf16[32,512]{1,0:T(8,128)(2,1)S(1)} %get-tuple-element.82), channel_id=1, source_target_pairs={{0,2},{2,0},{4,6},{6,4},{8,10},{10,8},{12,14},{14,12},{1,3},{3,1},... | collective-permute-start | bytes 98312 | tf_op jit(solution)/shard_map/ppermute | solution.py:283
  29.7 4.8 %collective-permute-start.12 = (bf16[32,512]{1,0:T(8,128)(2,1)S(1)}, bf16[32,512]{1,0:T(8,128)(2,1)S(1)}, u32[]{:S(2)}, u32[]{:S(2)}) collective-permute-start(bf16[32,512]{1,0:T(8,128)(2,1)S(1)} %slice.17), channel_id=1, source_target_pairs={{0,1},{1,0},{2,3},{3,2},{4,5},{5,4},{6,7},{7,6},{8,9},{9,8},{10,11... | collective-permute-start | bytes 98312 | tf_op jit(solution)/shard_map/ppermute | solution.py:270
  32.8 1.7 %collective-permute-start.14 = (bf16[32,512]{1,0:T(8,128)(2,1)S(1)}, bf16[32,512]{1,0:T(8,128)(2,1)S(1)}, u32[]{:S(2)}, u32[]{:S(2)}) collective-permute-start(bf16[32,512]{1,0:T(8,128)(2,1)S(1)} %slice.18), channel_id=1, source_target_pairs={{0,1},{1,0},{2,3},{3,2},{4,5},{5,4},{6,7},{7,6},{8,9},{9,8},{10,11... | collective-permute-start | bytes 98312 | tf_op jit(solution)/shard_map/ppermute | solution.py:270
  32.8 1.7 %collective-permute-start.16 = (bf16[32,512]{1,0:T(8,128)(2,1)S(1)}, bf16[32,512]{1,0:T(8,128)(2,1)S(1)}, u32[]{:S(2)}, u32[]{:S(2)}) collective-permute-start(bf16[32,512]{1,0:T(8,128)(2,1)S(1)} %slice.19), channel_id=1, source_target_pairs={{0,1},{1,0},{2,3},{3,2},{4,5},{5,4},{6,7},{7,6},{8,9},{9,8},{10,11... | collective-permute-start | bytes 98312 | tf_op jit(solution)/shard_map/ppermute | solution.py:270
  33.3 1.2 %collective-permute-start.10 = (bf16[16,512]{1,0:T(8,128)(2,1)S(1)}, bf16[16,512]{1,0:T(8,128)(2,1)S(1)}, u32[]{:S(2)}, u32[]{:S(2)}) collective-permute-start(bf16[16,512]{1,0:T(8,128)(2,1)S(1)} %slice.16), channel_id=1, source_target_pairs={{0,1},{1,0},{2,3},{3,2},{4,5},{5,4},{6,7},{7,6},{8,9},{9,8},{10,11... | collective-permute-start | bytes 49160 | tf_op jit(solution)/shard_map/ppermute | solution.py:270

commit v17 on v16

--- a/solution.py
+++ b/solution.py
@@ -180,7 +180,7 @@
 def stack_kernel(*refs):
     *in_refs, out_ref = refs
     rows = in_refs[0].shape[0]
-    for at, in_ref in enumerate(in_refs):
+    for at, in_ref in zip(far_first(len(in_refs)), in_refs):
         out_ref[at * rows : (at + 1) * rows, :] = in_ref[...]
 
 
@@ -308,8 +308,8 @@
     weights = jnp.transpose(w_in, (1, 0, 2))
     near = to_neighbour(owners, near)
     came = cross(owners, out)
-    near, came, weights = lax.optimization_barrier((near, came, weights))
-    stacked = kernel_call(stack_kernel, bf16((messages * piece, model_width)), [vmem] * messages)(*reversed(came))
+    came, near, weights = lax.optimization_barrier((came, near, weights))
+    stacked = kernel_call(stack_kernel, bf16((messages * piece, model_width)), [vmem] * messages)(*came)
     visible = kernel_call(
         visible_kernel,
         [bf16((owners * piece, HD)), bf16((hist_rows, HD))],

time: 36.6 us -> 35.7 us (0.975)
  waiting for transfers between devices: 7.19 us -> 6.27 us
    ppermute x6, starting transfers between devices: 10.6 us -> 11.7 us  [cross(): came.append(lax.ppermute(messages[at], ('cache', 'serve'), pairs))]
    ppermute x6, waiting for transfers between devices: 5.2 us -> 4.28 us  [cross(): came.append(lax.ppermute(messages[at], ('cache', 'serve'), pairs))]
    ppermute x2, starting transfers between devices: 3.57 us -> 2.87 us  [to_neighbour(): lax.ppermute(rows, 'cache', [(place, place ^ 1) for place in range(owners)])]
  transfers between devices with their start and end apart: 17 -> 17, of which waited for: 7 -> 7; matrix products, arithmetic and copies ran while one was open for 8% -> 9% of each run, Pallas kernels for 17% -> 17%
where the time goes in v17:
time: 35.7 us; the launch traced here: 35.5 us
  starting transfers between devices  16.4 us (46%)
  Pallas kernels  7.98 us (22%)
  waiting for transfers between devices  6.27 us (18%)
  local copies, waits for them, and re-layouts  4.64 us (13%)
    ppermute x6, starting transfers between devices, cross(): came.append(lax.ppermute(messages[at], ('cache', 'serve'), pairs))  11.7 us
    ppermute x6, waiting for transfers between devices, cross(): came.append(lax.ppermute(messages[at], ('cache', 'serve'), pairs))  4.28 us
    pallas_call x1, Pallas kernels, body(): kernel_call(functools.partial(history_kernel, owners), [bf16((rows_out, w...  3.64 us
    optimization_barrier x1, local copies, waits for them, and re-layouts, body(): (local, near, *out), w_in = lax.optimization_barrier((out, w_in))  3.02 us
    ppermute x2, starting transfers between devices, to_neighbour(): lax.ppermute(rows, 'cache', [(place, place ^ 1) for place in range(owners)])  2.87 us
    ppermute x9, waiting for transfers between devices, swap(): return lax.ppermute(rows, 'serve', [(0, 1), (1, 0)])  1.98 us
    pallas_call x1, Pallas kernels, body(): kernel_call(functools.partial(output_kernel, owners), bf16((req_count, ha...  1.85 us
    ppermute x9, starting transfers between devices, swap(): return lax.ppermute(rows, 'serve', [(0, 1), (1, 0)])  1.83 us
  transfers between devices with their start and end apart: 17, of which 7 were waited for; matrix products, arithmetic and copies ran while one was open for 9% of the time, Pallas kernels for 17%

profile of v17, /device:TPU:0, one launch (start us, length us, event | category | flops | bytes accessed | tf_op | source)
XLA Modules:
  0.0 35.5 jit_solution(12831781723845687453)
XLA Ops:
  0.0 0.5 %collective-permute-start = (bf16[8,8,1024]{2,1,0:T(8,128)(2,1)}, bf16[8,8,1024]{2,1,0:T(8,128)(2,1)S(1)}, u32[]{:S(2)}, u32[]{:S(2)}) collective-permute-start(bf16[8,8,1024]{2,1,0:T(8,128)(2,1)} %own_ref.5), channel_id=1, source_target_pairs={{0,1},{1,0},{2,3},{3,2},{4,5},{5,4},{6,7},{7,6},{8,9},{9,8},{10,11... | collective-permute-start | bytes 393224 | tf_op jit(solution)/shard_map/ppermute | solution.py:270
  0.5 0.0 copy-start.6
  0.5 0.7 %copy-done.6 = s32[64,1]{0,1:T(1,128)S(1)} copy-done((s32[64,1]{0,1:T(1,128)S(1)}, s32[64,1]{0,1:T(1,128)}, u32[]{:S(2)}) %copy-start.6) | copy-done | bytes 280
  1.1 0.4 %shard_map.91.chosen_ref = bf16[160,128]{1,0:T(8,128)(2,1)S(1)} custom-call(s32[1,64]{1,0:T(1,128)S(1)} %bitcast.16), custom_call_target="tpu_custom_call" | custom-call | tf_op jit(solution)/shard_map/pallas_call | solution.py:299
  1.5 0.1 collective-permute-done.other_ref
  1.7 0.4 %collective-permute-start.6 = (bf16[512,1024]{1,0:T(8,128)(2,1)}, bf16[512,1024]{1,0:T(8,128)(2,1)S(1)}, u32[]{:S(2)}, u32[]{:S(2)}) collective-permute-start(bf16[512,1024]{1,0:T(8,128)(2,1)} %w_own_ref), channel_id=1, source_target_pairs={{0,1},{1,0},{2,3},{3,2},{4,5},{5,4},{6,7},{7,6},{8,9},{9,8},{10,11... | collective-permute-start | bytes 3145736 | tf_op jit(solution)/shard_map/ppermute | solution.py:270
  2.0 0.0 copy-start.2
  2.0 0.9 %copy-done.2 = bf16[8,8,1024]{2,1,0:T(8,128)(2,1)S(1)} copy-done((bf16[8,8,1024]{2,1,0:T(8,128)(2,1)S(1)}, bf16[8,8,1024]{2,1,0:T(8,128)(2,1)}, u32[]{:S(2)}) %copy-start.2) | copy-done | bytes 131096
  2.9 0.2 shard_map.92
  3.2 0.0 copy-start.7
  3.2 0.0 copy-start.8
  3.2 0.0 copy-start.9
  3.2 0.0 copy-start
  3.2 0.0 copy-start.1
  3.2 0.0 copy-start.5
  3.2 4.8 %collective-permute-start.1 = (bf16[32,1024]{1,0:T(8,128)(2,1)S(1)}, bf16[32,1024]{1,0:T(8,128)(2,1)S(1)}, u32[]{:S(2)}, u32[]{:S(2)}) collective-permute-start(bf16[32,1024]{1,0:T(8,128)(2,1)S(1)} %get-tuple-element.53), channel_id=1, source_target_pairs={{0,12},{1,15},{2,14},{3,13},{4,8},{5,11},{6,10},{7,9},{8,4},{9,7},... | collective-permute-start | bytes 196616 | tf_op jit(solution)/shard_map/ppermute | solution.py:278
  8.0 0.4 %collective-permute-start.2 = (bf16[32,1024]{1,0:T(8,128)(2,1)S(1)}, bf16[32,1024]{1,0:T(8,128)(2,1)S(1)}, u32[]{:S(2)}, u32[]{:S(2)}) collective-permute-start(bf16[32,1024]{1,0:T(8,128)(2,1)S(1)} %get-tuple-element.54), channel_id=1, source_target_pairs={{1,9},{0,10},{3,11},{2,8},{5,13},{4,14},{7,15},{6,12},{9,1},{8,2},... | collective-permute-start | bytes 196616 | tf_op jit(solution)/shard_map/ppermute | solution.py:278
  8.4 1.1 %collective-permute-start.3 = (bf16[32,1024]{1,0:T(8,128)(2,1)S(1)}, bf16[32,1024]{1,0:T(8,128)(2,1)S(1)}, u32[]{:S(2)}, u32[]{:S(2)}) collective-permute-start(bf16[32,1024]{1,0:T(8,128)(2,1)S(1)} %get-tuple-element.55), channel_id=1, source_target_pairs={{1,5},{0,6},{3,7},{2,4},{5,1},{4,2},{7,3},{6,0},{9,13},{8,14},{11,... | collective-permute-start | bytes 196616 | tf_op jit(solution)/shard_map/ppermute | solution.py:278
  9.6 1.7 %collective-permute-start.4 = (bf16[32,1024]{1,0:T(8,128)(2,1)S(1)}, bf16[32,1024]{1,0:T(8,128)(2,1)S(1)}, u32[]{:S(2)}, u32[]{:S(2)}) collective-permute-start(bf16[32,1024]{1,0:T(8,128)(2,1)S(1)} %get-tuple-element.56), channel_id=1, source_target_pairs={{0,2},{2,0},{4,6},{6,4},{8,10},{10,8},{12,14},{14,12},{1,3},{3,1},... | collective-permute-start | bytes 196616 | tf_op jit(solution)/shard_map/ppermute | solution.py:283
  11.2 3.0 %copy.12 = bf16[1024,4,512]{2,0,1:T(8,128)(2,1)S(1)} copy(bf16[1024,4,512]{2,1,0:T(4,128)(2,1)} %param.11) | data formatting | bytes 8388608 | tf_op jit(solution)/shard_map/optimization_barrier | solution.py:307
  14.3 0.0 collective-permute-done.1.refs_0_.refs_4_
  14.3 0.7 %collective-permute-done.2.refs_1_.refs_3_ = bf16[32,1024]{1,0:T(8,128)(2,1)S(1)} collective-permute-done((bf16[32,1024]{1,0:T(8,128)(2,1)S(1)}, bf16[32,1024]{1,0:T(8,128)(2,1)S(1)}, u32[]{:S(2)}, u32[]{:S(2)}) %collective-permute-start.2) | collective-permute-done | bytes 65568 | tf_op jit(solution)/shard_map/ppermute | solution.py:278
  15.0 0.0 collective-permute-done.3.refs_2_
  15.0 0.0 collective-permute-done.4.refs_1_
  15.0 0.1 collective-permute-start.5
  15.1 0.0 copy-done.7
  15.1 0.0 copy-done.8
  15.1 0.0 copy-done.9
  15.1 1.0 %shard_map.94 = (bf16[256,128]{1,0:T(8,128)(2,1)S(1)}, bf16[2048,128]{1,0:T(8,128)(2,1)S(1)}) custom-call(s32[1,64]{1,0:T(1,128)S(1)} %bitcast.17, s32[1,8]{1,0:T(1,128)S(1)} %bitcast.20, s32[32,64]{1,0:T(8,128)S(1)} %bitcast.19), custom_call_target="tpu_custom_call" | custom-call | flops 100663296 | tf_op jit(solution)/shard_map/pallas_call | solution.py:313
  16.1 0.4 %collective-permute-done.5.refs_5_ = bf16[96,1024]{1,0:T(8,128)(2,1)S(1)} collective-permute-done((bf16[96,1024]{1,0:T(8,128)(2,1)S(1)}, bf16[96,1024]{1,0:T(8,128)(2,1)S(1)}, u32[]{:S(2)}, u32[]{:S(2)}) %collective-permute-start.5) | collective-permute-done | bytes 196640 | tf_op jit(solution)/shard_map/ppermute | solution.py:270
  16.5 0.0 copy-done
  16.5 0.0 copy-done.1
  16.5 0.0 copy-done.5
  16.6 0.0 copy-start.3
  16.6 3.6 %shard_map.95 = (bf16[16,512]{1,0:T(8,128)(2,1)S(1)}, bf16[32,512]{1,0:T(8,128)(2,1)S(1)}, bf16[96,512]{1,0:T(8,128)(2,1)S(1)}, bf16[112,512]{1,0:T(8,128)(2,1)S(1)}) custom-call(bf16[8,128]{1,0:T(8,128)(2,1)S(1)} %bitcast.14, bf16[4,1024,512]{2,1,0:T(8,128)(2,1)S(1)} %bitcast.10, bf16[256,128]{1,0:T(8,128)(2,1)S(1)} %get-tuple-element.65.hide_rows_ref, ...), custom_call_target="tpu_custom_call" | custom-call | flops 2147483648 | bytes 4194304 | tf_op jit(solution)/shard_map/pallas_call | solution.py:321
  20.2 0.0 copy-start.4
  20.2 0.0 collective-permute-done.6.w_other_ref
  20.2 0.2 collective-permute-start.7
  20.4 0.0 copy-done.3
  20.4 0.9 %shard_map.96 = (bf16[2,64,512]{2,1,0:T(8,128)(2,1)S(1)}, bf16[2,64,512]{2,1,0:T(8,128)(2,1)S(1)}) custom-call(bf16[8,8,1024]{2,1,0:T(8,128)(2,1)S(1)} %copy-done.3, bf16[8,8,1024]{2,1,0:T(8,128)(2,1)S(1)} %collective-permute-done.other_ref, bf16[8,128]{1,0:T(8,128)(2,1)S(1)} %bitcast.15, bf16[4,1024,512]{2,1,0:T(8,128)(2,1)S(1)} %bitcast.11), custom_call_target="tpu_custom_call" | custom-call | flops 536870912 | bytes 4194304 | tf_op jit(solution)/shard_map/pallas_call | solution.py:342
  21.3 0.3 collective-permute-done.7.got_ref.refs_1_
  21.6 0.2 collective-permute-start.8
  21.8 3.2 %collective-permute-start.11 = (bf16[64,512]{1,0:T(8,128)(2,1)S(1)}, bf16[64,512]{1,0:T(8,128)(2,1)S(1)}, u32[]{:S(2)}, u32[]{:S(2)}) collective-permute-start(bf16[64,512]{1,0:T(8,128)(2,1)S(1)} %get-tuple-element.84), channel_id=1, source_target_pairs={{0,12},{1,15},{2,14},{3,13},{4,8},{5,11},{6,10},{7,9},{8,4},{9,7},... | collective-permute-start | bytes 196616 | tf_op jit(solution)/shard_map/ppermute | solution.py:278
  25.0 0.0 collective-permute-start.13
  25.0 2.1 %collective-permute-start.15 = (bf16[64,512]{1,0:T(8,128)(2,1)S(1)}, bf16[64,512]{1,0:T(8,128)(2,1)S(1)}, u32[]{:S(2)}, u32[]{:S(2)}) collective-permute-start(bf16[64,512]{1,0:T(8,128)(2,1)S(1)} %get-tuple-element.86), channel_id=1, source_target_pairs={{1,5},{0,6},{3,7},{2,4},{5,1},{4,2},{7,3},{6,0},{9,13},{8,14},{11,... | collective-permute-start | bytes 196616 | tf_op jit(solution)/shard_map/ppermute | solution.py:278
  27.1 1.2 %collective-permute-start.9 = (bf16[32,512]{1,0:T(8,128)(2,1)S(1)}, bf16[32,512]{1,0:T(8,128)(2,1)S(1)}, u32[]{:S(2)}, u32[]{:S(2)}) collective-permute-start(bf16[32,512]{1,0:T(8,128)(2,1)S(1)} %get-tuple-element.82), channel_id=1, source_target_pairs={{0,2},{2,0},{4,6},{6,4},{8,10},{10,8},{12,14},{14,12},{1,3},{3,1},... | collective-permute-start | bytes 98312 | tf_op jit(solution)/shard_map/ppermute | solution.py:283
  28.3 0.3 collective-permute-done.11.refs_4_
  28.6 0.0 collective-permute-start.12
  28.6 3.3 %collective-permute-done.13.refs_6_ = bf16[64,512]{1,0:T(8,128)(2,1)S(1)} collective-permute-done((bf16[64,512]{1,0:T(8,128)(2,1)S(1)}, bf16[64,512]{1,0:T(8,128)(2,1)S(1)}, u32[]{:S(2)}, u32[]{:S(2)}) %collective-permute-start.13) | collective-permute-done | bytes 65568 | tf_op jit(solution)/shard_map/ppermute | solution.py:278
  31.9 0.0 collective-permute-start.14
  31.9 0.0 collective-permute-done.15.refs_8_
  31.9 0.5 %collective-permute-start.16 = (bf16[32,512]{1,0:T(8,128)(2,1)S(1)}, bf16[32,512]{1,0:T(8,128)(2,1)S(1)}, u32[]{:S(2)}, u32[]{:S(2)}) collective-permute-start(bf16[32,512]{1,0:T(8,128)(2,1)S(1)} %slice.19), channel_id=1, source_target_pairs={{0,1},{1,0},{2,3},{3,2},{4,5},{5,4},{6,7},{7,6},{8,9},{9,8},{10,11... | collective-permute-start | bytes 98312 | tf_op jit(solution)/shard_map/ppermute | solution.py:270
  32.4 0.0 collective-permute-done.9.refs_2_
  32.4 0.1 collective-permute-start.10
  32.5 1.1 %collective-permute-done.10.refs_3_ = bf16[16,512]{1,0:T(8,128)(2,1)S(1)} collective-permute-done((bf16[16,512]{1,0:T(8,128)(2,1)S(1)}, bf16[16,512]{1,0:T(8,128)(2,1)S(1)}, u32[]{:S(2)}, u32[]{:S(2)}) %collective-permute-start.10) | collective-permute-done | bytes 16416 | tf_op jit(solution)/shard_map/ppermute | solution.py:270
  33.6 0.0 collective-permute-done.12.refs_5_
  33.6 0.0 collective-permute-done.14.refs_7_
  33.6 0.0 collective-permute-done.16.refs_9_
  33.6 0.0 collective-permute-done.8.got_ref
  33.6 0.0 copy-done.4
  33.6 1.9 %shard_map.98 = bf16[8,8,1024]{2,1,0:T(8,128)(2,1)} custom-call(s32[64]{0:T(128)S(1)} %bitcast.18, bf16[8,8,1024]{2,1,0:T(8,128)(2,1)S(1)} %copy-done.3, bf16[2,64,512]{2,1,0:T(8,128)(2,1)S(1)} %get-tuple-element.77.keep_ref, bf16[2,64,512]{2,1,0:T(8,128)(2,1)S(1)} %collective-permute-done.8.got_ref, bf16[512,1024]{1,0:T(8,128)(2,1)S(1)} %copy-done.4, ...), custom_call_target="tpu_custom_call" | custom-call | flops 268435456 | bytes 2097152 | tf_op jit(solution)/shard_map/pallas_call | solution.py:354
  (6 shorter events, 0.0 us)
Async XLA Ops:
  0.0 1.6 %collective-permute-start = (bf16[8,8,1024]{2,1,0:T(8,128)(2,1)}, bf16[8,8,1024]{2,1,0:T(8,128)(2,1)S(1)}, u32[]{:S(2)}, u32[]{:S(2)}) collective-permute-start(bf16[8,8,1024]{2,1,0:T(8,128)(2,1)} %own_ref.5), channel_id=1, source_target_pairs={{0,1},{1,0},{2,3},{3,2},{4,5},{5,4},{6,7},{7,6},{8,9},{9,8},{10,11... | collective-permute-start | bytes 393224 | tf_op jit(solution)/shard_map/ppermute | solution.py:270
  0.5 0.7 %copy-start.6 = (s32[64,1]{0,1:T(1,128)S(1)}, s32[64,1]{0,1:T(1,128)}, u32[]{:S(2)}) copy-start(s32[64,1]{0,1:T(1,128)} %param.15) | copy-start | bytes 772
  1.7 18.6 %collective-permute-start.6 = (bf16[512,1024]{1,0:T(8,128)(2,1)}, bf16[512,1024]{1,0:T(8,128)(2,1)S(1)}, u32[]{:S(2)}, u32[]{:S(2)}) collective-permute-start(bf16[512,1024]{1,0:T(8,128)(2,1)} %w_own_ref), channel_id=1, source_target_pairs={{0,1},{1,0},{2,3},{3,2},{4,5},{5,4},{6,7},{7,6},{8,9},{9,8},{10,11... | collective-permute-start | bytes 3145736 | tf_op jit(solution)/shard_map/ppermute | solution.py:270
  2.0 0.9 %copy-start.2 = (bf16[8,8,1024]{2,1,0:T(8,128)(2,1)S(1)}, bf16[8,8,1024]{2,1,0:T(8,128)(2,1)}, u32[]{:S(2)}) copy-start(bf16[8,8,1024]{2,1,0:T(8,128)(2,1)} %own_ref.5) | copy-start | bytes 393220
  3.2 12.0 %copy-start.7 = (s32[64,1]{0,1:T(1,128)S(1)}, s32[64,1]{0,1:T(1,128)}, u32[]{:S(2)}) copy-start(s32[64,1]{0,1:T(1,128)} %param.15) | copy-start | bytes 772
  3.2 12.0 %copy-start.8 = (s32[64,32]{0,1:T(8,128)S(1)}, s32[64,32]{0,1:T(8,128)}, u32[]{:S(2)}) copy-start(s32[64,32]{0,1:T(8,128)} %param.17) | copy-start | bytes 24580
  3.2 12.0 %copy-start.9 = (s32[8]{0:T(128)S(1)}, s32[8]{0:T(128)}, u32[]{:S(2)}) copy-start(s32[8]{0:T(128)} %param.16) | copy-start | bytes 100
  3.2 13.4 %copy-start = (bf16[1,2048,512]{2,1,0:T(8,128)(2,1)S(1)}, bf16[1,2048,512]{2,1,0:T(8,128)(2,1)}, u32[]{:S(2)}) copy-start(bf16[1,2048,512]{2,1,0:T(8,128)(2,1)} %param.13) | copy-start | bytes 6291460
  3.2 13.3 %copy-start.1 = (bf16[1,2048,512]{2,1,0:T(8,128)(2,1)S(1)}, bf16[1,2048,512]{2,1,0:T(8,128)(2,1)}, u32[]{:S(2)}) copy-start(bf16[1,2048,512]{2,1,0:T(8,128)(2,1)} %param.14) | copy-start | bytes 6291460
  3.2 13.3 %copy-start.5 = (bf16[1024]{0:T(1024)(128)(2,1)S(1)}, bf16[1024]{0:T(1024)(128)(2,1)}, u32[]{:S(2)}) copy-start(bf16[1024]{0:T(1024)(128)(2,1)} %param.10) | copy-start | bytes 6148
  3.2 11.0 %collective-permute-start.1 = (bf16[32,1024]{1,0:T(8,128)(2,1)S(1)}, bf16[32,1024]{1,0:T(8,128)(2,1)S(1)}, u32[]{:S(2)}, u32[]{:S(2)}) collective-permute-start(bf16[32,1024]{1,0:T(8,128)(2,1)S(1)} %get-tuple-element.53), channel_id=1, source_target_pairs={{0,12},{1,15},{2,14},{3,13},{4,8},{5,11},{6,10},{7,9},{8,4},{9,7},... | collective-permute-start | bytes 196616 | tf_op jit(solution)/shard_map/ppermute | solution.py:278
  8.0 7.0 %collective-permute-start.2 = (bf16[32,1024]{1,0:T(8,128)(2,1)S(1)}, bf16[32,1024]{1,0:T(8,128)(2,1)S(1)}, u32[]{:S(2)}, u32[]{:S(2)}) collective-permute-start(bf16[32,1024]{1,0:T(8,128)(2,1)S(1)} %get-tuple-element.54), channel_id=1, source_target_pairs={{1,9},{0,10},{3,11},{2,8},{5,13},{4,14},{7,15},{6,12},{9,1},{8,2},... | collective-permute-start | bytes 196616 | tf_op jit(solution)/shard_map/ppermute | solution.py:278
  8.4 6.6 %collective-permute-start.3 = (bf16[32,1024]{1,0:T(8,128)(2,1)S(1)}, bf16[32,1024]{1,0:T(8,128)(2,1)S(1)}, u32[]{:S(2)}, u32[]{:S(2)}) collective-permute-start(bf16[32,1024]{1,0:T(8,128)(2,1)S(1)} %get-tuple-element.55), channel_id=1, source_target_pairs={{1,5},{0,6},{3,7},{2,4},{5,1},{4,2},{7,3},{6,0},{9,13},{8,14},{11,... | collective-permute-start | bytes 196616 | tf_op jit(solution)/shard_map/ppermute | solution.py:278
  9.6 5.4 %collective-permute-start.4 = (bf16[32,1024]{1,0:T(8,128)(2,1)S(1)}, bf16[32,1024]{1,0:T(8,128)(2,1)S(1)}, u32[]{:S(2)}, u32[]{:S(2)}) collective-permute-start(bf16[32,1024]{1,0:T(8,128)(2,1)S(1)} %get-tuple-element.56), channel_id=1, source_target_pairs={{0,2},{2,0},{4,6},{6,4},{8,10},{10,8},{12,14},{14,12},{1,3},{3,1},... | collective-permute-start | bytes 196616 | tf_op jit(solution)/shard_map/ppermute | solution.py:283
  15.0 1.5 %collective-permute-start.5 = (bf16[96,1024]{1,0:T(8,128)(2,1)S(1)}, bf16[96,1024]{1,0:T(8,128)(2,1)S(1)}, u32[]{:S(2)}, u32[]{:S(2)}) collective-permute-start(bf16[96,1024]{1,0:T(8,128)(2,1)S(1)} %shard_map.93), channel_id=1, source_target_pairs={{0,1},{1,0},{2,3},{3,2},{4,5},{5,4},{6,7},{7,6},{8,9},{9,8},{10,11... | collective-permute-start | bytes 589832 | tf_op jit(solution)/shard_map/ppermute | solution.py:270
  16.6 3.9 %copy-start.3 = (bf16[8,8,1024]{2,1,0:T(8,128)(2,1)S(1)}, bf16[8,8,1024]{2,1,0:T(8,128)(2,1)}, u32[]{:S(2)}) copy-start(bf16[8,8,1024]{2,1,0:T(8,128)(2,1)} %own_ref.5) | copy-start | bytes 393220
  20.2 13.4 %copy-start.4 = (bf16[512,1024]{1,0:T(8,128)(2,1)S(1)}, bf16[512,1024]{1,0:T(8,128)(2,1)}, u32[]{:S(2)}) copy-start(bf16[512,1024]{1,0:T(8,128)(2,1)} %w_own_ref) | copy-start | bytes 3145732
  20.2 1.4 %collective-permute-start.7 = (bf16[112,512]{1,0:T(8,128)(2,1)S(1)}, bf16[112,512]{1,0:T(8,128)(2,1)S(1)}, u32[]{:S(2)}, u32[]{:S(2)}) collective-permute-start(bf16[112,512]{1,0:T(8,128)(2,1)S(1)} %get-tuple-element.73), channel_id=1, source_target_pairs={{0,1},{1,0},{2,3},{3,2},{4,5},{5,4},{6,7},{7,6},{8,9},{9,8},{10,11... | collective-permute-start | bytes 344072 | tf_op jit(solution)/shard_map/ppermute | solution.py:270
  21.6 12.0 %collective-permute-start.8 = (bf16[2,64,512]{2,1,0:T(8,128)(2,1)S(1)}, bf16[2,64,512]{2,1,0:T(8,128)(2,1)S(1)}, u32[]{:S(2)}, u32[]{:S(2)}) collective-permute-start(bf16[2,64,512]{2,1,0:T(8,128)(2,1)S(1)} %get-tuple-element.78), channel_id=1, source_target_pairs={{0,1},{1,0},{2,3},{3,2},{4,5},{5,4},{6,7},{7,6},{8,9},{9,8},{10,11... | collective-permute-start | bytes 393224 | tf_op jit(solution)/shard_map/ppermute | solution.py:270
  21.8 6.8 %collective-permute-start.11 = (bf16[64,512]{1,0:T(8,128)(2,1)S(1)}, bf16[64,512]{1,0:T(8,128)(2,1)S(1)}, u32[]{:S(2)}, u32[]{:S(2)}) collective-permute-start(bf16[64,512]{1,0:T(8,128)(2,1)S(1)} %get-tuple-element.84), channel_id=1, source_target_pairs={{0,12},{1,15},{2,14},{3,13},{4,8},{5,11},{6,10},{7,9},{8,4},{9,7},... | collective-permute-start | bytes 196616 | tf_op jit(solution)/shard_map/ppermute | solution.py:278
  25.0 6.9 %collective-permute-start.13 = (bf16[64,512]{1,0:T(8,128)(2,1)S(1)}, bf16[64,512]{1,0:T(8,128)(2,1)S(1)}, u32[]{:S(2)}, u32[]{:S(2)}) collective-permute-start(bf16[64,512]{1,0:T(8,128)(2,1)S(1)} %get-tuple-element.85), channel_id=1, source_target_pairs={{1,9},{0,10},{3,11},{2,8},{5,13},{4,14},{7,15},{6,12},{9,1},{8,2},... | collective-permute-start | bytes 196616 | tf_op jit(solution)/shard_map/ppermute | solution.py:278
  25.0 6.9 %collective-permute-start.15 = (bf16[64,512]{1,0:T(8,128)(2,1)S(1)}, bf16[64,512]{1,0:T(8,128)(2,1)S(1)}, u32[]{:S(2)}, u32[]{:S(2)}) collective-permute-start(bf16[64,512]{1,0:T(8,128)(2,1)S(1)} %get-tuple-element.86), channel_id=1, source_target_pairs={{1,5},{0,6},{3,7},{2,4},{5,1},{4,2},{7,3},{6,0},{9,13},{8,14},{11,... | collective-permute-start | bytes 196616 | tf_op jit(solution)/shard_map/ppermute | solution.py:278
  27.1 5.3 %collective-permute-start.9 = (bf16[32,512]{1,0:T(8,128)(2,1)S(1)}, bf16[32,512]{1,0:T(8,128)(2,1)S(1)}, u32[]{:S(2)}, u32[]{:S(2)}) collective-permute-start(bf16[32,512]{1,0:T(8,128)(2,1)S(1)} %get-tuple-element.82), channel_id=1, source_target_pairs={{0,2},{2,0},{4,6},{6,4},{8,10},{10,8},{12,14},{14,12},{1,3},{3,1},... | collective-permute-start | bytes 98312 | tf_op jit(solution)/shard_map/ppermute | solution.py:283
  28.6 5.0 %collective-permute-start.12 = (bf16[32,512]{1,0:T(8,128)(2,1)S(1)}, bf16[32,512]{1,0:T(8,128)(2,1)S(1)}, u32[]{:S(2)}, u32[]{:S(2)}) collective-permute-start(bf16[32,512]{1,0:T(8,128)(2,1)S(1)} %slice.17), channel_id=1, source_target_pairs={{0,1},{1,0},{2,3},{3,2},{4,5},{5,4},{6,7},{7,6},{8,9},{9,8},{10,11... | collective-permute-start | bytes 98312 | tf_op jit(solution)/shard_map/ppermute | solution.py:270
  31.9 1.7 %collective-permute-start.14 = (bf16[32,512]{1,0:T(8,128)(2,1)S(1)}, bf16[32,512]{1,0:T(8,128)(2,1)S(1)}, u32[]{:S(2)}, u32[]{:S(2)}) collective-permute-start(bf16[32,512]{1,0:T(8,128)(2,1)S(1)} %slice.18), channel_id=1, source_target_pairs={{0,1},{1,0},{2,3},{3,2},{4,5},{5,4},{6,7},{7,6},{8,9},{9,8},{10,11... | collective-permute-start | bytes 98312 | tf_op jit(solution)/shard_map/ppermute | solution.py:270
  31.9 1.7 %collective-permute-start.16 = (bf16[32,512]{1,0:T(8,128)(2,1)S(1)}, bf16[32,512]{1,0:T(8,128)(2,1)S(1)}, u32[]{:S(2)}, u32[]{:S(2)}) collective-permute-start(bf16[32,512]{1,0:T(8,128)(2,1)S(1)} %slice.19), channel_id=1, source_target_pairs={{0,1},{1,0},{2,3},{3,2},{4,5},{5,4},{6,7},{7,6},{8,9},{9,8},{10,11... | collective-permute-start | bytes 98312 | tf_op jit(solution)/shard_map/ppermute | solution.py:270
  32.4 1.2 %collective-permute-start.10 = (bf16[16,512]{1,0:T(8,128)(2,1)S(1)}, bf16[16,512]{1,0:T(8,128)(2,1)S(1)}, u32[]{:S(2)}, u32[]{:S(2)}) collective-permute-start(bf16[16,512]{1,0:T(8,128)(2,1)S(1)} %slice.16), channel_id=1, source_target_pairs={{0,1},{1,0},{2,3},{3,2},{4,5},{5,4},{6,7},{7,6},{8,9},{9,8},{10,11... | collective-permute-start | bytes 49160 | tf_op jit(solution)/shard_map/ppermute | solution.py:270

commit v18 on v17

--- a/solution.py
+++ b/solution.py
@@ -85,7 +85,8 @@
     return place
 
 
-def front_kernel(owners, half_cands, sess_ref, chosen_ref):
+def front_kernel(owners, sess_ref, own_ref, moved_ref, chosen_ref):
+    half_cands, model_width = own_ref.shape[1:]
     me, serve = lax.axis_index("cache"), lax.axis_index("serve")
     sessions = sess_ref[...]
     requests = sessions.shape[1]
@@ -95,15 +96,18 @@
     at = position(distance, serve, owners)
     sent = at <= owners // 2
     code = jnp.where(sent, at * (2 * CAP) + places(sessions, per_owner), owners * (2 * CAP))
-    request = lax.broadcasted_iota(jnp.int32, (requests, 2 * rows), 0)
-    column = lax.broadcasted_iota(jnp.int32, (requests, 2 * rows), 1)
-    spread = (request == me * per_owner + (column % rows) // half_cands).astype(jnp.float32).astype(jnp.bfloat16)
+    request = lax.broadcasted_iota(jnp.int32, (requests, rows), 0)
+    column = lax.broadcasted_iota(jnp.int32, (requests, rows), 1)
+    spread = (request == me * per_owner + column // half_cands).astype(jnp.float32).astype(jnp.bfloat16)
     codes = jnp.broadcast_to(code, (8, requests)).astype(jnp.float32).astype(jnp.bfloat16)
     target = jnp.dot(codes, spread, preferred_element_type=jnp.float32)[:1].astype(jnp.int32)
     at = lax.broadcasted_iota(jnp.int32, chosen_ref.shape, 0)
     column = lax.broadcasted_iota(jnp.int32, chosen_ref.shape, 1)
-    hit = (at // half_cands == target + (column // rows) * CAP) & (at % half_cands == column % half_cands)
-    chosen_ref[...] = hit.astype(jnp.float32).astype(jnp.bfloat16)
+    same = at % half_cands == column % half_cands
+    own = ((at // half_cands == target) & same).astype(jnp.float32).astype(jnp.bfloat16)
+    chosen_ref[...] = ((at // half_cands == target + CAP) & same).astype(jnp.float32).astype(jnp.bfloat16)
+    source = own_ref[...].astype(jnp.float32).reshape(-1, model_width).astype(jnp.bfloat16)
+    moved_ref[...] = jnp.dot(own, source, preferred_element_type=jnp.float32).astype(jnp.bfloat16)
 
 
 def visible_kernel(sess_ref, len_ref, mask_ref, hide_rows_ref, hide_cols_ref, marks_ref):
@@ -136,12 +140,10 @@
     ).astype(jnp.bfloat16)
 
 
-def message_kernel(chosen_ref, own_ref, other_ref, *out_refs):
-    model_width = own_ref.shape[2]
-    source = jnp.concatenate(
-        [ref[...].astype(jnp.float32).reshape(-1, model_width) for ref in (own_ref, other_ref)], axis=0
-    ).astype(jnp.bfloat16)
-    rows = jnp.dot(chosen_ref[...], source, preferred_element_type=jnp.float32)
+def message_kernel(moved_ref, chosen_ref, other_ref, *out_refs):
+    model_width = other_ref.shape[2]
+    source = other_ref[...].astype(jnp.float32).reshape(-1, model_width).astype(jnp.bfloat16)
+    rows = moved_ref[...].astype(jnp.float32) + jnp.dot(chosen_ref[...], source, preferred_element_type=jnp.float32)
     piece = out_refs[0].shape[0]
     for at, out_ref in enumerate(out_refs):
         out_ref[...] = rows[at * piece : (at + 1) * piece].astype(jnp.bfloat16)
@@ -296,14 +298,13 @@
     piece = 2 * CAP * half_cands
 
     session_row = request_session.reshape(1, -1)
-    chosen = kernel_call(
-        functools.partial(front_kernel, owners, half_cands),
-        bf16(((messages + 2) * piece, 2 * rows)),
-        [vmem],
-    )(session_row)
-    other, w_out, chosen = lax.optimization_barrier((swap(candidates), w_out, chosen))
-    w_other = swap(w_out)
-    out = kernel_call(message_kernel, [bf16((piece, model_width))] * (messages + 2), [vmem] * 3)(chosen, candidates, other)
+    placed = kernel_call(
+        functools.partial(front_kernel, owners),
+        [bf16(((messages + 2) * piece, columns)) for columns in (model_width, rows)],
+        [vmem] * 2,
+    )(session_row, candidates)
+    other, placed = lax.optimization_barrier((swap(candidates), placed))
+    out = kernel_call(message_kernel, [bf16((piece, model_width))] * (messages + 2), [vmem] * 3)(*placed, other)
     (local, near, *out), w_in = lax.optimization_barrier((out, w_in))
     weights = jnp.transpose(w_in, (1, 0, 2))
     near = to_neighbour(owners, near)
@@ -317,7 +318,8 @@
         [pltpu.VMEM((HD, owners * req_count), jnp.bfloat16)],
         flops=2 * messages * piece * model_width * width,
     )(session_row, hist_len.reshape(1, -1), lax.optimization_barrier((block_mask.T, stacked))[0])
-    swapped, (hide_rows, hide_cols) = lax.optimization_barrier((swap(stacked), visible))
+    swapped, (hide_rows, hide_cols), w_out = lax.optimization_barrier((swap(stacked), visible, w_out))
+    w_other = swap(w_out)
     local, near, keep, give = kernel_call(
         functools.partial(history_kernel, owners),
         [bf16((rows_out, width)) for rows_out in (piece // 2, piece, messages * piece, messages * piece + piece // 2)],

time: 35.7 us -> 35.5 us (level)
  waiting for transfers between devices: 6.27 us -> 5.86 us
  transfers between devices with their start and end apart: 17 -> 17, of which waited for: 7 -> 6; matrix products, arithmetic and copies ran while one was open for 9% -> 9% of each run, Pallas kernels for 17% -> 17%
where the time goes in v18:
time: 35.5 us; the launch traced here: 35.3 us
  starting transfers between devices  16.4 us (46%)
  Pallas kernels  8.18 us (23%)
  waiting for transfers between devices  5.86 us (17%)
  local copies, waits for them, and re-layouts  4.64 us (13%)
    ppermute x6, starting transfers between devices, cross(): came.append(lax.ppermute(messages[at], ('cache', 'serve'), pairs))  11.6 us
    ppermute x6, waiting for transfers between devices, cross(): came.append(lax.ppermute(messages[at], ('cache', 'serve'), pairs))  4.22 us
    pallas_call x1, Pallas kernels, body(): kernel_call(functools.partial(history_kernel, owners), [bf16((rows_out, w...  3.64 us
    optimization_barrier x1, local copies, waits for them, and re-layouts, body(): (local, near, *out), w_in = lax.optimization_barrier((out, w_in))  3.02 us
    ppermute x2, starting transfers between devices, to_neighbour(): lax.ppermute(rows, 'cache', [(place, place ^ 1) for place in range(owners)])  2.83 us
    ppermute x9, starting transfers between devices, swap(): return lax.ppermute(rows, 'serve', [(0, 1), (1, 0)])  2.05 us
    pallas_call x1, Pallas kernels, body(): kernel_call(functools.partial(output_kernel, owners), bf16((req_count, ha...  1.86 us
    ppermute x9, waiting for transfers between devices, swap(): return lax.ppermute(rows, 'serve', [(0, 1), (1, 0)])  1.64 us
  transfers between devices with their start and end apart: 17, of which 6 were waited for; matrix products, arithmetic and copies ran while one was open for 9% of the time, Pallas kernels for 17%

profile of v18, /device:TPU:0, one launch (start us, length us, event | category | flops | bytes accessed | tf_op | source)
XLA Modules:
  0.0 35.3 jit_solution(990112804126651859)
XLA Ops:
  0.0 0.5 %collective-permute-start = (bf16[8,8,1024]{2,1,0:T(8,128)(2,1)}, bf16[8,8,1024]{2,1,0:T(8,128)(2,1)S(1)}, u32[]{:S(2)}, u32[]{:S(2)}) collective-permute-start(bf16[8,8,1024]{2,1,0:T(8,128)(2,1)} %own_ref.5), channel_id=1, source_target_pairs={{0,1},{1,0},{2,3},{3,2},{4,5},{5,4},{6,7},{7,6},{8,9},{9,8},{10,11... | collective-permute-start | bytes 393224 | tf_op jit(solution)/shard_map/ppermute | solution.py:272
  0.5 0.0 copy-start.2
  0.5 0.9 %copy-done.2 = bf16[8,8,1024]{2,1,0:T(8,128)(2,1)S(1)} copy-done((bf16[8,8,1024]{2,1,0:T(8,128)(2,1)S(1)}, bf16[8,8,1024]{2,1,0:T(8,128)(2,1)}, u32[]{:S(2)}) %copy-start.2) | copy-done | bytes 131096
  1.4 0.0 copy-start.6
  1.4 0.7 %copy-done.6 = s32[64,1]{0,1:T(1,128)S(1)} copy-done((s32[64,1]{0,1:T(1,128)S(1)}, s32[64,1]{0,1:T(1,128)}, u32[]{:S(2)}) %copy-start.6) | copy-done | bytes 280
  2.0 0.6 %shard_map.91 = (bf16[160,1024]{1,0:T(8,128)(2,1)S(1)}, bf16[160,64]{1,0:T(8,128)(2,1)S(1)}) custom-call(s32[1,64]{1,0:T(1,128)S(1)} %bitcast.16, bf16[8,8,1024]{2,1,0:T(8,128)(2,1)S(1)} %copy-done.2), custom_call_target="tpu_custom_call" | custom-call | tf_op jit(solution)/shard_map/pallas_call | solution.py:301
  2.6 0.0 collective-permute-done.other_ref
  2.6 0.2 shard_map.92
  2.9 0.0 copy-start.7
  2.9 0.0 copy-start.8
  2.9 0.0 copy-start.9
  2.9 0.0 copy-start.4
  2.9 0.0 copy-start
  2.9 0.0 copy-start.1
  2.9 0.0 copy-start.5
  3.0 4.7 %collective-permute-start.1 = (bf16[32,1024]{1,0:T(8,128)(2,1)S(1)}, bf16[32,1024]{1,0:T(8,128)(2,1)S(1)}, u32[]{:S(2)}, u32[]{:S(2)}) collective-permute-start(bf16[32,1024]{1,0:T(8,128)(2,1)S(1)} %get-tuple-element.59), channel_id=1, source_target_pairs={{0,12},{1,15},{2,14},{3,13},{4,8},{5,11},{6,10},{7,9},{8,4},{9,7},... | collective-permute-start | bytes 196616 | tf_op jit(solution)/shard_map/ppermute | solution.py:280
  7.6 0.4 %collective-permute-start.2 = (bf16[32,1024]{1,0:T(8,128)(2,1)S(1)}, bf16[32,1024]{1,0:T(8,128)(2,1)S(1)}, u32[]{:S(2)}, u32[]{:S(2)}) collective-permute-start(bf16[32,1024]{1,0:T(8,128)(2,1)S(1)} %get-tuple-element.60), channel_id=1, source_target_pairs={{1,9},{0,10},{3,11},{2,8},{5,13},{4,14},{7,15},{6,12},{9,1},{8,2},... | collective-permute-start | bytes 196616 | tf_op jit(solution)/shard_map/ppermute | solution.py:280
  8.0 1.1 %collective-permute-start.3 = (bf16[32,1024]{1,0:T(8,128)(2,1)S(1)}, bf16[32,1024]{1,0:T(8,128)(2,1)S(1)}, u32[]{:S(2)}, u32[]{:S(2)}) collective-permute-start(bf16[32,1024]{1,0:T(8,128)(2,1)S(1)} %get-tuple-element.61), channel_id=1, source_target_pairs={{1,5},{0,6},{3,7},{2,4},{5,1},{4,2},{7,3},{6,0},{9,13},{8,14},{11,... | collective-permute-start | bytes 196616 | tf_op jit(solution)/shard_map/ppermute | solution.py:280
  9.2 1.7 %collective-permute-start.4 = (bf16[32,1024]{1,0:T(8,128)(2,1)S(1)}, bf16[32,1024]{1,0:T(8,128)(2,1)S(1)}, u32[]{:S(2)}, u32[]{:S(2)}) collective-permute-start(bf16[32,1024]{1,0:T(8,128)(2,1)S(1)} %get-tuple-element.62), channel_id=1, source_target_pairs={{0,2},{2,0},{4,6},{6,4},{8,10},{10,8},{12,14},{14,12},{1,3},{3,1},... | collective-permute-start | bytes 196616 | tf_op jit(solution)/shard_map/ppermute | solution.py:285
  10.8 3.0 %copy.12 = bf16[1024,4,512]{2,0,1:T(8,128)(2,1)S(1)} copy(bf16[1024,4,512]{2,1,0:T(4,128)(2,1)} %param.11) | data formatting | bytes 8388608 | tf_op jit(solution)/shard_map/optimization_barrier | solution.py:308
  13.9 0.0 collective-permute-done.1.refs_0_.refs_4_
  13.9 0.8 %collective-permute-done.2.refs_1_.refs_3_ = bf16[32,1024]{1,0:T(8,128)(2,1)S(1)} collective-permute-done((bf16[32,1024]{1,0:T(8,128)(2,1)S(1)}, bf16[32,1024]{1,0:T(8,128)(2,1)S(1)}, u32[]{:S(2)}, u32[]{:S(2)}) %collective-permute-start.2) | collective-permute-done | bytes 65568 | tf_op jit(solution)/shard_map/ppermute | solution.py:280
  14.6 0.0 collective-permute-done.3.refs_2_
  14.7 0.0 collective-permute-done.4.refs_1_
  14.7 0.1 collective-permute-start.5
  14.8 0.0 copy-done.7
  14.8 0.0 copy-done.8
  14.8 0.0 copy-done.9
  14.8 1.0 %shard_map.94 = (bf16[256,128]{1,0:T(8,128)(2,1)S(1)}, bf16[2048,128]{1,0:T(8,128)(2,1)S(1)}) custom-call(s32[1,64]{1,0:T(1,128)S(1)} %bitcast.17, s32[1,8]{1,0:T(1,128)S(1)} %bitcast.20, s32[32,64]{1,0:T(8,128)S(1)} %bitcast.19), custom_call_target="tpu_custom_call" | custom-call | flops 100663296 | tf_op jit(solution)/shard_map/pallas_call | solution.py:314
  15.7 0.4 %collective-permute-done.5.refs_5_ = bf16[96,1024]{1,0:T(8,128)(2,1)S(1)} collective-permute-done((bf16[96,1024]{1,0:T(8,128)(2,1)S(1)}, bf16[96,1024]{1,0:T(8,128)(2,1)S(1)}, u32[]{:S(2)}, u32[]{:S(2)}) %collective-permute-start.5) | collective-permute-done | bytes 196640 | tf_op jit(solution)/shard_map/ppermute | solution.py:272
  16.2 0.0 copy-done.4
  16.2 0.1 collective-permute-start.6
  16.3 0.0 copy-done
  16.3 0.0 copy-done.1
  16.3 0.0 copy-done.5
  16.3 0.0 copy-start.3
  16.3 3.6 %shard_map.95 = (bf16[16,512]{1,0:T(8,128)(2,1)S(1)}, bf16[32,512]{1,0:T(8,128)(2,1)S(1)}, bf16[96,512]{1,0:T(8,128)(2,1)S(1)}, bf16[112,512]{1,0:T(8,128)(2,1)S(1)}) custom-call(bf16[8,128]{1,0:T(8,128)(2,1)S(1)} %bitcast.14, bf16[4,1024,512]{2,1,0:T(8,128)(2,1)S(1)} %bitcast.10, bf16[256,128]{1,0:T(8,128)(2,1)S(1)} %get-tuple-element.71.hide_rows_ref, ...), custom_call_target="tpu_custom_call" | custom-call | flops 2147483648 | bytes 4194304 | tf_op jit(solution)/shard_map/pallas_call | solution.py:323
  20.0 0.0 collective-permute-done.6.w_other_ref
  20.0 0.4 %collective-permute-start.7 = (bf16[112,512]{1,0:T(8,128)(2,1)S(1)}, bf16[112,512]{1,0:T(8,128)(2,1)S(1)}, u32[]{:S(2)}, u32[]{:S(2)}) collective-permute-start(bf16[112,512]{1,0:T(8,128)(2,1)S(1)} %get-tuple-element.79), channel_id=1, source_target_pairs={{0,1},{1,0},{2,3},{3,2},{4,5},{5,4},{6,7},{7,6},{8,9},{9,8},{10,11... | collective-permute-start | bytes 344072 | tf_op jit(solution)/shard_map/ppermute | solution.py:272
  20.4 0.0 copy-done.3
  20.4 0.9 %shard_map.96 = (bf16[2,64,512]{2,1,0:T(8,128)(2,1)S(1)}, bf16[2,64,512]{2,1,0:T(8,128)(2,1)S(1)}) custom-call(bf16[8,8,1024]{2,1,0:T(8,128)(2,1)S(1)} %copy-done.3, bf16[8,8,1024]{2,1,0:T(8,128)(2,1)S(1)} %collective-permute-done.other_ref, bf16[8,128]{1,0:T(8,128)(2,1)S(1)} %bitcast.15, bf16[4,1024,512]{2,1,0:T(8,128)(2,1)S(1)} %bitcast.11), custom_call_target="tpu_custom_call" | custom-call | flops 536870912 | bytes 4194304 | tf_op jit(solution)/shard_map/pallas_call | solution.py:344
  21.3 0.1 collective-permute-done.7.got_ref.refs_1_
  21.4 0.4 %collective-permute-start.8 = (bf16[2,64,512]{2,1,0:T(8,128)(2,1)S(1)}, bf16[2,64,512]{2,1,0:T(8,128)(2,1)S(1)}, u32[]{:S(2)}, u32[]{:S(2)}) collective-permute-start(bf16[2,64,512]{2,1,0:T(8,128)(2,1)S(1)} %get-tuple-element.84), channel_id=1, source_target_pairs={{0,1},{1,0},{2,3},{3,2},{4,5},{5,4},{6,7},{7,6},{8,9},{9,8},{10,11... | collective-permute-start | bytes 393224 | tf_op jit(solution)/shard_map/ppermute | solution.py:272
  21.8 3.2 %collective-permute-start.11 = (bf16[64,512]{1,0:T(8,128)(2,1)S(1)}, bf16[64,512]{1,0:T(8,128)(2,1)S(1)}, u32[]{:S(2)}, u32[]{:S(2)}) collective-permute-start(bf16[64,512]{1,0:T(8,128)(2,1)S(1)} %get-tuple-element.90), channel_id=1, source_target_pairs={{0,12},{1,15},{2,14},{3,13},{4,8},{5,11},{6,10},{7,9},{8,4},{9,7},... | collective-permute-start | bytes 196616 | tf_op jit(solution)/shard_map/ppermute | solution.py:280
  25.0 0.0 collective-permute-start.13
  25.0 2.1 %collective-permute-start.15 = (bf16[64,512]{1,0:T(8,128)(2,1)S(1)}, bf16[64,512]{1,0:T(8,128)(2,1)S(1)}, u32[]{:S(2)}, u32[]{:S(2)}) collective-permute-start(bf16[64,512]{1,0:T(8,128)(2,1)S(1)} %get-tuple-element.92), channel_id=1, source_target_pairs={{1,5},{0,6},{3,7},{2,4},{5,1},{4,2},{7,3},{6,0},{9,13},{8,14},{11,... | collective-permute-start | bytes 196616 | tf_op jit(solution)/shard_map/ppermute | solution.py:280
  27.1 1.2 %collective-permute-start.9 = (bf16[32,512]{1,0:T(8,128)(2,1)S(1)}, bf16[32,512]{1,0:T(8,128)(2,1)S(1)}, u32[]{:S(2)}, u32[]{:S(2)}) collective-permute-start(bf16[32,512]{1,0:T(8,128)(2,1)S(1)} %get-tuple-element.88), channel_id=1, source_target_pairs={{0,2},{2,0},{4,6},{6,4},{8,10},{10,8},{12,14},{14,12},{1,3},{3,1},... | collective-permute-start | bytes 98312 | tf_op jit(solution)/shard_map/ppermute | solution.py:285
  28.3 0.3 collective-permute-done.11.refs_4_
  28.6 0.0 collective-permute-start.12
  28.6 3.1 %collective-permute-done.13.refs_6_ = bf16[64,512]{1,0:T(8,128)(2,1)S(1)} collective-permute-done((bf16[64,512]{1,0:T(8,128)(2,1)S(1)}, bf16[64,512]{1,0:T(8,128)(2,1)S(1)}, u32[]{:S(2)}, u32[]{:S(2)}) %collective-permute-start.13) | collective-permute-done | bytes 65568 | tf_op jit(solution)/shard_map/ppermute | solution.py:280
  31.7 0.0 collective-permute-start.14
  31.7 0.0 collective-permute-done.15.refs_8_
  31.7 0.5 %collective-permute-start.16 = (bf16[32,512]{1,0:T(8,128)(2,1)S(1)}, bf16[32,512]{1,0:T(8,128)(2,1)S(1)}, u32[]{:S(2)}, u32[]{:S(2)}) collective-permute-start(bf16[32,512]{1,0:T(8,128)(2,1)S(1)} %slice.19), channel_id=1, source_target_pairs={{0,1},{1,0},{2,3},{3,2},{4,5},{5,4},{6,7},{7,6},{8,9},{9,8},{10,11... | collective-permute-start | bytes 98312 | tf_op jit(solution)/shard_map/ppermute | solution.py:272
  32.2 0.0 collective-permute-done.9.refs_2_
  32.3 0.1 collective-permute-start.10
  32.3 1.1 %collective-permute-done.10.refs_3_ = bf16[16,512]{1,0:T(8,128)(2,1)S(1)} collective-permute-done((bf16[16,512]{1,0:T(8,128)(2,1)S(1)}, bf16[16,512]{1,0:T(8,128)(2,1)S(1)}, u32[]{:S(2)}, u32[]{:S(2)}) %collective-permute-start.10) | collective-permute-done | bytes 16416 | tf_op jit(solution)/shard_map/ppermute | solution.py:272
  33.4 0.0 collective-permute-done.12.refs_5_
  33.4 0.0 collective-permute-done.14.refs_7_
  33.4 0.0 collective-permute-done.16.refs_9_
  33.4 0.0 collective-permute-done.8.got_ref
  33.5 1.9 %shard_map.98 = bf16[8,8,1024]{2,1,0:T(8,128)(2,1)} custom-call(s32[64]{0:T(128)S(1)} %bitcast.18, bf16[8,8,1024]{2,1,0:T(8,128)(2,1)S(1)} %copy-done.3, bf16[2,64,512]{2,1,0:T(8,128)(2,1)S(1)} %get-tuple-element.83.keep_ref, bf16[2,64,512]{2,1,0:T(8,128)(2,1)S(1)} %collective-permute-done.8.got_ref, bf16[512,1024]{1,0:T(8,128)(2,1)S(1)} %copy-done.4, ...), custom_call_target="tpu_custom_call" | custom-call | flops 268435456 | bytes 2097152 | tf_op jit(solution)/shard_map/pallas_call | solution.py:356
  (6 shorter events, 0.0 us)
Async XLA Ops:
  0.0 2.6 %collective-permute-start = (bf16[8,8,1024]{2,1,0:T(8,128)(2,1)}, bf16[8,8,1024]{2,1,0:T(8,128)(2,1)S(1)}, u32[]{:S(2)}, u32[]{:S(2)}) collective-permute-start(bf16[8,8,1024]{2,1,0:T(8,128)(2,1)} %own_ref.5), channel_id=1, source_target_pairs={{0,1},{1,0},{2,3},{3,2},{4,5},{5,4},{6,7},{7,6},{8,9},{9,8},{10,11... | collective-permute-start | bytes 393224 | tf_op jit(solution)/shard_map/ppermute | solution.py:272
  0.5 0.9 %copy-start.2 = (bf16[8,8,1024]{2,1,0:T(8,128)(2,1)S(1)}, bf16[8,8,1024]{2,1,0:T(8,128)(2,1)}, u32[]{:S(2)}) copy-start(bf16[8,8,1024]{2,1,0:T(8,128)(2,1)} %own_ref.5) | copy-start | bytes 393220
  1.4 0.7 %copy-start.6 = (s32[64,1]{0,1:T(1,128)S(1)}, s32[64,1]{0,1:T(1,128)}, u32[]{:S(2)}) copy-start(s32[64,1]{0,1:T(1,128)} %param.15) | copy-start | bytes 772
  2.9 11.9 %copy-start.7 = (s32[64,1]{0,1:T(1,128)S(1)}, s32[64,1]{0,1:T(1,128)}, u32[]{:S(2)}) copy-start(s32[64,1]{0,1:T(1,128)} %param.15) | copy-start | bytes 772
  2.9 11.9 %copy-start.8 = (s32[64,32]{0,1:T(8,128)S(1)}, s32[64,32]{0,1:T(8,128)}, u32[]{:S(2)}) copy-start(s32[64,32]{0,1:T(8,128)} %param.17) | copy-start | bytes 24580
  2.9 11.9 %copy-start.9 = (s32[8]{0:T(128)S(1)}, s32[8]{0:T(128)}, u32[]{:S(2)}) copy-start(s32[8]{0:T(128)} %param.16) | copy-start | bytes 100
  2.9 13.3 %copy-start.4 = (bf16[512,1024]{1,0:T(8,128)(2,1)S(1)}, bf16[512,1024]{1,0:T(8,128)(2,1)}, u32[]{:S(2)}) copy-start(bf16[512,1024]{1,0:T(8,128)(2,1)} %w_own_ref) | copy-start | bytes 3145732
  2.9 13.4 %copy-start = (bf16[1,2048,512]{2,1,0:T(8,128)(2,1)S(1)}, bf16[1,2048,512]{2,1,0:T(8,128)(2,1)}, u32[]{:S(2)}) copy-start(bf16[1,2048,512]{2,1,0:T(8,128)(2,1)} %param.13) | copy-start | bytes 6291460
  2.9 13.4 %copy-start.1 = (bf16[1,2048,512]{2,1,0:T(8,128)(2,1)S(1)}, bf16[1,2048,512]{2,1,0:T(8,128)(2,1)}, u32[]{:S(2)}) copy-start(bf16[1,2048,512]{2,1,0:T(8,128)(2,1)} %param.14) | copy-start | bytes 6291460
  2.9 13.4 %copy-start.5 = (bf16[1024]{0:T(1024)(128)(2,1)S(1)}, bf16[1024]{0:T(1024)(128)(2,1)}, u32[]{:S(2)}) copy-start(bf16[1024]{0:T(1024)(128)(2,1)} %param.10) | copy-start | bytes 6148
  3.0 10.9 %collective-permute-start.1 = (bf16[32,1024]{1,0:T(8,128)(2,1)S(1)}, bf16[32,1024]{1,0:T(8,128)(2,1)S(1)}, u32[]{:S(2)}, u32[]{:S(2)}) collective-permute-start(bf16[32,1024]{1,0:T(8,128)(2,1)S(1)} %get-tuple-element.59), channel_id=1, source_target_pairs={{0,12},{1,15},{2,14},{3,13},{4,8},{5,11},{6,10},{7,9},{8,4},{9,7},... | collective-permute-start | bytes 196616 | tf_op jit(solution)/shard_map/ppermute | solution.py:280
  7.6 7.0 %collective-permute-start.2 = (bf16[32,1024]{1,0:T(8,128)(2,1)S(1)}, bf16[32,1024]{1,0:T(8,128)(2,1)S(1)}, u32[]{:S(2)}, u32[]{:S(2)}) collective-permute-start(bf16[32,1024]{1,0:T(8,128)(2,1)S(1)} %get-tuple-element.60), channel_id=1, source_target_pairs={{1,9},{0,10},{3,11},{2,8},{5,13},{4,14},{7,15},{6,12},{9,1},{8,2},... | collective-permute-start | bytes 196616 | tf_op jit(solution)/shard_map/ppermute | solution.py:280
  8.0 6.6 %collective-permute-start.3 = (bf16[32,1024]{1,0:T(8,128)(2,1)S(1)}, bf16[32,1024]{1,0:T(8,128)(2,1)S(1)}, u32[]{:S(2)}, u32[]{:S(2)}) collective-permute-start(bf16[32,1024]{1,0:T(8,128)(2,1)S(1)} %get-tuple-element.61), channel_id=1, source_target_pairs={{1,5},{0,6},{3,7},{2,4},{5,1},{4,2},{7,3},{6,0},{9,13},{8,14},{11,... | collective-permute-start | bytes 196616 | tf_op jit(solution)/shard_map/ppermute | solution.py:280
  9.2 5.5 %collective-permute-start.4 = (bf16[32,1024]{1,0:T(8,128)(2,1)S(1)}, bf16[32,1024]{1,0:T(8,128)(2,1)S(1)}, u32[]{:S(2)}, u32[]{:S(2)}) collective-permute-start(bf16[32,1024]{1,0:T(8,128)(2,1)S(1)} %get-tuple-element.62), channel_id=1, source_target_pairs={{0,2},{2,0},{4,6},{6,4},{8,10},{10,8},{12,14},{14,12},{1,3},{3,1},... | collective-permute-start | bytes 196616 | tf_op jit(solution)/shard_map/ppermute | solution.py:285
  14.7 1.5 %collective-permute-start.5 = (bf16[96,1024]{1,0:T(8,128)(2,1)S(1)}, bf16[96,1024]{1,0:T(8,128)(2,1)S(1)}, u32[]{:S(2)}, u32[]{:S(2)}) collective-permute-start(bf16[96,1024]{1,0:T(8,128)(2,1)S(1)} %shard_map.93), channel_id=1, source_target_pairs={{0,1},{1,0},{2,3},{3,2},{4,5},{5,4},{6,7},{7,6},{8,9},{9,8},{10,11... | collective-permute-start | bytes 589832 | tf_op jit(solution)/shard_map/ppermute | solution.py:272
  16.2 3.8 %collective-permute-start.6 = (bf16[512,1024]{1,0:T(8,128)(2,1)S(1)}, bf16[512,1024]{1,0:T(8,128)(2,1)S(1)}, u32[]{:S(2)}, u32[]{:S(2)}) collective-permute-start(bf16[512,1024]{1,0:T(8,128)(2,1)S(1)} %copy-done.4), channel_id=1, source_target_pairs={{0,1},{1,0},{2,3},{3,2},{4,5},{5,4},{6,7},{7,6},{8,9},{9,8},{10,11... | collective-permute-start | bytes 3145736 | tf_op jit(solution)/shard_map/ppermute | solution.py:272
  16.3 4.1 %copy-start.3 = (bf16[8,8,1024]{2,1,0:T(8,128)(2,1)S(1)}, bf16[8,8,1024]{2,1,0:T(8,128)(2,1)}, u32[]{:S(2)}) copy-start(bf16[8,8,1024]{2,1,0:T(8,128)(2,1)} %own_ref.5) | copy-start | bytes 393220
  20.0 1.4 %collective-permute-start.7 = (bf16[112,512]{1,0:T(8,128)(2,1)S(1)}, bf16[112,512]{1,0:T(8,128)(2,1)S(1)}, u32[]{:S(2)}, u32[]{:S(2)}) collective-permute-start(bf16[112,512]{1,0:T(8,128)(2,1)S(1)} %get-tuple-element.79), channel_id=1, source_target_pairs={{0,1},{1,0},{2,3},{3,2},{4,5},{5,4},{6,7},{7,6},{8,9},{9,8},{10,11... | collective-permute-start | bytes 344072 | tf_op jit(solution)/shard_map/ppermute | solution.py:272
  21.4 12.1 %collective-permute-start.8 = (bf16[2,64,512]{2,1,0:T(8,128)(2,1)S(1)}, bf16[2,64,512]{2,1,0:T(8,128)(2,1)S(1)}, u32[]{:S(2)}, u32[]{:S(2)}) collective-permute-start(bf16[2,64,512]{2,1,0:T(8,128)(2,1)S(1)} %get-tuple-element.84), channel_id=1, source_target_pairs={{0,1},{1,0},{2,3},{3,2},{4,5},{5,4},{6,7},{7,6},{8,9},{9,8},{10,11... | collective-permute-start | bytes 393224 | tf_op jit(solution)/shard_map/ppermute | solution.py:272
  21.8 6.8 %collective-permute-start.11 = (bf16[64,512]{1,0:T(8,128)(2,1)S(1)}, bf16[64,512]{1,0:T(8,128)(2,1)S(1)}, u32[]{:S(2)}, u32[]{:S(2)}) collective-permute-start(bf16[64,512]{1,0:T(8,128)(2,1)S(1)} %get-tuple-element.90), channel_id=1, source_target_pairs={{0,12},{1,15},{2,14},{3,13},{4,8},{5,11},{6,10},{7,9},{8,4},{9,7},... | collective-permute-start | bytes 196616 | tf_op jit(solution)/shard_map/ppermute | solution.py:280
  25.0 6.7 %collective-permute-start.13 = (bf16[64,512]{1,0:T(8,128)(2,1)S(1)}, bf16[64,512]{1,0:T(8,128)(2,1)S(1)}, u32[]{:S(2)}, u32[]{:S(2)}) collective-permute-start(bf16[64,512]{1,0:T(8,128)(2,1)S(1)} %get-tuple-element.91), channel_id=1, source_target_pairs={{1,9},{0,10},{3,11},{2,8},{5,13},{4,14},{7,15},{6,12},{9,1},{8,2},... | collective-permute-start | bytes 196616 | tf_op jit(solution)/shard_map/ppermute | solution.py:280
  25.0 6.7 %collective-permute-start.15 = (bf16[64,512]{1,0:T(8,128)(2,1)S(1)}, bf16[64,512]{1,0:T(8,128)(2,1)S(1)}, u32[]{:S(2)}, u32[]{:S(2)}) collective-permute-start(bf16[64,512]{1,0:T(8,128)(2,1)S(1)} %get-tuple-element.92), channel_id=1, source_target_pairs={{1,5},{0,6},{3,7},{2,4},{5,1},{4,2},{7,3},{6,0},{9,13},{8,14},{11,... | collective-permute-start | bytes 196616 | tf_op jit(solution)/shard_map/ppermute | solution.py:280
  27.1 5.1 %collective-permute-start.9 = (bf16[32,512]{1,0:T(8,128)(2,1)S(1)}, bf16[32,512]{1,0:T(8,128)(2,1)S(1)}, u32[]{:S(2)}, u32[]{:S(2)}) collective-permute-start(bf16[32,512]{1,0:T(8,128)(2,1)S(1)} %get-tuple-element.88), channel_id=1, source_target_pairs={{0,2},{2,0},{4,6},{6,4},{8,10},{10,8},{12,14},{14,12},{1,3},{3,1},... | collective-permute-start | bytes 98312 | tf_op jit(solution)/shard_map/ppermute | solution.py:285
  28.6 4.8 %collective-permute-start.12 = (bf16[32,512]{1,0:T(8,128)(2,1)S(1)}, bf16[32,512]{1,0:T(8,128)(2,1)S(1)}, u32[]{:S(2)}, u32[]{:S(2)}) collective-permute-start(bf16[32,512]{1,0:T(8,128)(2,1)S(1)} %slice.17), channel_id=1, source_target_pairs={{0,1},{1,0},{2,3},{3,2},{4,5},{5,4},{6,7},{7,6},{8,9},{9,8},{10,11... | collective-permute-start | bytes 98312 | tf_op jit(solution)/shard_map/ppermute | solution.py:272
  31.7 1.7 %collective-permute-start.14 = (bf16[32,512]{1,0:T(8,128)(2,1)S(1)}, bf16[32,512]{1,0:T(8,128)(2,1)S(1)}, u32[]{:S(2)}, u32[]{:S(2)}) collective-permute-start(bf16[32,512]{1,0:T(8,128)(2,1)S(1)} %slice.18), channel_id=1, source_target_pairs={{0,1},{1,0},{2,3},{3,2},{4,5},{5,4},{6,7},{7,6},{8,9},{9,8},{10,11... | collective-permute-start | bytes 98312 | tf_op jit(solution)/shard_map/ppermute | solution.py:272
  31.7 1.7 %collective-permute-start.16 = (bf16[32,512]{1,0:T(8,128)(2,1)S(1)}, bf16[32,512]{1,0:T(8,128)(2,1)S(1)}, u32[]{:S(2)}, u32[]{:S(2)}) collective-permute-start(bf16[32,512]{1,0:T(8,128)(2,1)S(1)} %slice.19), channel_id=1, source_target_pairs={{0,1},{1,0},{2,3},{3,2},{4,5},{5,4},{6,7},{7,6},{8,9},{9,8},{10,11... | collective-permute-start | bytes 98312 | tf_op jit(solution)/shard_map/ppermute | solution.py:272
  32.3 1.2 %collective-permute-start.10 = (bf16[16,512]{1,0:T(8,128)(2,1)S(1)}, bf16[16,512]{1,0:T(8,128)(2,1)S(1)}, u32[]{:S(2)}, u32[]{:S(2)}) collective-permute-start(bf16[16,512]{1,0:T(8,128)(2,1)S(1)} %slice.16), channel_id=1, source_target_pairs={{0,1},{1,0},{2,3},{3,2},{4,5},{5,4},{6,7},{7,6},{8,9},{9,8},{10,11... | collective-permute-start | bytes 49160 | tf_op jit(solution)/shard_map/ppermute | solution.py:272

commit v19 on v18

--- a/solution.py
+++ b/solution.py
@@ -202,7 +202,8 @@
     for first in range(0, owners, per_step):
         group = range(first, min(first + per_step, owners))
         normed = jnp.concatenate([normed_rows(*sources[at], per_owner, gain) for at in group], axis=0)
-        queries = silu(jnp.dot(normed, w_ref[0], preferred_element_type=jnp.float32)).astype(jnp.bfloat16)
+        queries = silu(jnp.dot(normed, w_ref[0], preferred_element_type=jnp.float32))
+        queries = (queries * (0.5 * SCALE)).astype(jnp.bfloat16)
         hide_rows = hide_rows_ref[first * per_owner : first * per_owner + queries.shape[0], :]
         for low in range(0, width, HD):
             lhs = jnp.concatenate([queries[:, low : low + HD], hide_rows], axis=1)
@@ -211,8 +212,8 @@
                 rhs = jnp.concatenate(
                     [keys_ref[start : start + span, low : low + HD], hide_cols_ref[start : start + span, :]], axis=1
                 )
-                scores = lax.dot_general(lhs, rhs, (((1,), (1,)), ((), ())), preferred_element_type=jnp.float32)
-                weights = silu_of_half(scores * (0.5 * SCALE)).astype(jnp.bfloat16)
+                half_scores = lax.dot_general(lhs, rhs, (((1,), (1,)), ((), ())), preferred_element_type=jnp.float32)
+                weights = silu_of_half(half_scores.astype(jnp.bfloat16))
                 term = jnp.dot(
                     weights, values_ref[start : start + span, low : low + HD], preferred_element_type=jnp.float32
                 )

time: 35.5 us -> 35.5 us (level)
  no operation moved by 1% of the time
where the time goes in v19:
time: 35.5 us; the launch traced here: 35.3 us
  starting transfers between devices  16.4 us (46%)
  Pallas kernels  8.15 us (23%)
  waiting for transfers between devices  5.86 us (17%)
  local copies, waits for them, and re-layouts  4.64 us (13%)
    ppermute x6, starting transfers between devices, cross(): came.append(lax.ppermute(messages[at], ('cache', 'serve'), pairs))  11.6 us
    ppermute x6, waiting for transfers between devices, cross(): came.append(lax.ppermute(messages[at], ('cache', 'serve'), pairs))  4.22 us
    pallas_call x1, Pallas kernels, body(): kernel_call(functools.partial(history_kernel, owners), [bf16((rows_out, w...  3.61 us
    optimization_barrier x1, local copies, waits for them, and re-layouts, body(): (local, near, *out), w_in = lax.optimization_barrier((out, w_in))  3.02 us
    ppermute x2, starting transfers between devices, to_neighbour(): lax.ppermute(rows, 'cache', [(place, place ^ 1) for place in range(owners)])  2.83 us
    ppermute x9, starting transfers between devices, swap(): return lax.ppermute(rows, 'serve', [(0, 1), (1, 0)])  2.04 us
    pallas_call x1, Pallas kernels, body(): kernel_call(functools.partial(output_kernel, owners), bf16((req_count, ha...  1.86 us
    ppermute x9, waiting for transfers between devices, swap(): return lax.ppermute(rows, 'serve', [(0, 1), (1, 0)])  1.64 us
  transfers between devices with their start and end apart: 17, of which 6 were waited for; matrix products, arithmetic and copies ran while one was open for 9% of the time, Pallas kernels for 17%

profile of v19, /device:TPU:0, one launch (start us, length us, event | category | flops | bytes accessed | tf_op | source)
XLA Modules:
  0.0 35.3 jit_solution(11503731297719706375)
XLA Ops:
  0.0 0.5 %collective-permute-start = (bf16[8,8,1024]{2,1,0:T(8,128)(2,1)}, bf16[8,8,1024]{2,1,0:T(8,128)(2,1)S(1)}, u32[]{:S(2)}, u32[]{:S(2)}) collective-permute-start(bf16[8,8,1024]{2,1,0:T(8,128)(2,1)} %own_ref.5), channel_id=1, source_target_pairs={{0,1},{1,0},{2,3},{3,2},{4,5},{5,4},{6,7},{7,6},{8,9},{9,8},{10,11... | collective-permute-start | bytes 393224 | tf_op jit(solution)/shard_map/ppermute | solution.py:273
  0.5 0.0 copy-start.2
  0.5 0.9 %copy-done.2 = bf16[8,8,1024]{2,1,0:T(8,128)(2,1)S(1)} copy-done((bf16[8,8,1024]{2,1,0:T(8,128)(2,1)S(1)}, bf16[8,8,1024]{2,1,0:T(8,128)(2,1)}, u32[]{:S(2)}) %copy-start.2) | copy-done | bytes 131096
  1.4 0.0 copy-start.6
  1.4 0.7 %copy-done.6 = s32[64,1]{0,1:T(1,128)S(1)} copy-done((s32[64,1]{0,1:T(1,128)S(1)}, s32[64,1]{0,1:T(1,128)}, u32[]{:S(2)}) %copy-start.6) | copy-done | bytes 280
  2.0 0.6 %shard_map.91 = (bf16[160,1024]{1,0:T(8,128)(2,1)S(1)}, bf16[160,64]{1,0:T(8,128)(2,1)S(1)}) custom-call(s32[1,64]{1,0:T(1,128)S(1)} %bitcast.16, bf16[8,8,1024]{2,1,0:T(8,128)(2,1)S(1)} %copy-done.2), custom_call_target="tpu_custom_call" | custom-call | tf_op jit(solution)/shard_map/pallas_call | solution.py:302
  2.6 0.0 collective-permute-done.other_ref
  2.6 0.2 shard_map.92
  2.9 0.0 copy-start.7
  2.9 0.0 copy-start.8
  2.9 0.0 copy-start.9
  2.9 0.0 copy-start.4
  2.9 0.0 copy-start
  2.9 0.0 copy-start.1
  2.9 0.0 copy-start.5
  3.0 4.7 %collective-permute-start.1 = (bf16[32,1024]{1,0:T(8,128)(2,1)S(1)}, bf16[32,1024]{1,0:T(8,128)(2,1)S(1)}, u32[]{:S(2)}, u32[]{:S(2)}) collective-permute-start(bf16[32,1024]{1,0:T(8,128)(2,1)S(1)} %get-tuple-element.59), channel_id=1, source_target_pairs={{0,12},{1,15},{2,14},{3,13},{4,8},{5,11},{6,10},{7,9},{8,4},{9,7},... | collective-permute-start | bytes 196616 | tf_op jit(solution)/shard_map/ppermute | solution.py:281
  7.6 0.4 %collective-permute-start.2 = (bf16[32,1024]{1,0:T(8,128)(2,1)S(1)}, bf16[32,1024]{1,0:T(8,128)(2,1)S(1)}, u32[]{:S(2)}, u32[]{:S(2)}) collective-permute-start(bf16[32,1024]{1,0:T(8,128)(2,1)S(1)} %get-tuple-element.60), channel_id=1, source_target_pairs={{1,9},{0,10},{3,11},{2,8},{5,13},{4,14},{7,15},{6,12},{9,1},{8,2},... | collective-permute-start | bytes 196616 | tf_op jit(solution)/shard_map/ppermute | solution.py:281
  8.0 1.1 %collective-permute-start.3 = (bf16[32,1024]{1,0:T(8,128)(2,1)S(1)}, bf16[32,1024]{1,0:T(8,128)(2,1)S(1)}, u32[]{:S(2)}, u32[]{:S(2)}) collective-permute-start(bf16[32,1024]{1,0:T(8,128)(2,1)S(1)} %get-tuple-element.61), channel_id=1, source_target_pairs={{1,5},{0,6},{3,7},{2,4},{5,1},{4,2},{7,3},{6,0},{9,13},{8,14},{11,... | collective-permute-start | bytes 196616 | tf_op jit(solution)/shard_map/ppermute | solution.py:281
  9.2 1.7 %collective-permute-start.4 = (bf16[32,1024]{1,0:T(8,128)(2,1)S(1)}, bf16[32,1024]{1,0:T(8,128)(2,1)S(1)}, u32[]{:S(2)}, u32[]{:S(2)}) collective-permute-start(bf16[32,1024]{1,0:T(8,128)(2,1)S(1)} %get-tuple-element.62), channel_id=1, source_target_pairs={{0,2},{2,0},{4,6},{6,4},{8,10},{10,8},{12,14},{14,12},{1,3},{3,1},... | collective-permute-start | bytes 196616 | tf_op jit(solution)/shard_map/ppermute | solution.py:286
  10.8 3.0 %copy.12 = bf16[1024,4,512]{2,0,1:T(8,128)(2,1)S(1)} copy(bf16[1024,4,512]{2,1,0:T(4,128)(2,1)} %param.11) | data formatting | bytes 8388608 | tf_op jit(solution)/shard_map/optimization_barrier | solution.py:309
  13.9 0.0 collective-permute-done.1.refs_0_.refs_4_
  13.9 0.8 %collective-permute-done.2.refs_1_.refs_3_ = bf16[32,1024]{1,0:T(8,128)(2,1)S(1)} collective-permute-done((bf16[32,1024]{1,0:T(8,128)(2,1)S(1)}, bf16[32,1024]{1,0:T(8,128)(2,1)S(1)}, u32[]{:S(2)}, u32[]{:S(2)}) %collective-permute-start.2) | collective-permute-done | bytes 65568 | tf_op jit(solution)/shard_map/ppermute | solution.py:281
  14.6 0.0 collective-permute-done.3.refs_2_
  14.7 0.0 collective-permute-done.4.refs_1_
  14.7 0.1 collective-permute-start.5
  14.8 0.0 copy-done.7
  14.8 0.0 copy-done.8
  14.8 0.0 copy-done.9
  14.8 1.0 %shard_map.94 = (bf16[256,128]{1,0:T(8,128)(2,1)S(1)}, bf16[2048,128]{1,0:T(8,128)(2,1)S(1)}) custom-call(s32[1,64]{1,0:T(1,128)S(1)} %bitcast.17, s32[1,8]{1,0:T(1,128)S(1)} %bitcast.20, s32[32,64]{1,0:T(8,128)S(1)} %bitcast.19), custom_call_target="tpu_custom_call" | custom-call | flops 100663296 | tf_op jit(solution)/shard_map/pallas_call | solution.py:315
  15.7 0.4 %collective-permute-done.5.refs_5_ = bf16[96,1024]{1,0:T(8,128)(2,1)S(1)} collective-permute-done((bf16[96,1024]{1,0:T(8,128)(2,1)S(1)}, bf16[96,1024]{1,0:T(8,128)(2,1)S(1)}, u32[]{:S(2)}, u32[]{:S(2)}) %collective-permute-start.5) | collective-permute-done | bytes 196640 | tf_op jit(solution)/shard_map/ppermute | solution.py:273
  16.2 0.0 copy-done.4
  16.2 0.1 collective-permute-start.6
  16.3 0.0 copy-done
  16.3 0.0 copy-done.1
  16.3 0.0 copy-done.5
  16.3 0.0 copy-start.3
  16.3 3.6 %shard_map.95 = (bf16[16,512]{1,0:T(8,128)(2,1)S(1)}, bf16[32,512]{1,0:T(8,128)(2,1)S(1)}, bf16[96,512]{1,0:T(8,128)(2,1)S(1)}, bf16[112,512]{1,0:T(8,128)(2,1)S(1)}) custom-call(bf16[8,128]{1,0:T(8,128)(2,1)S(1)} %bitcast.14, bf16[4,1024,512]{2,1,0:T(8,128)(2,1)S(1)} %bitcast.10, bf16[256,128]{1,0:T(8,128)(2,1)S(1)} %get-tuple-element.71.hide_rows_ref, ...), custom_call_target="tpu_custom_call" | custom-call | flops 2147483648 | bytes 4194304 | tf_op jit(solution)/shard_map/pallas_call | solution.py:324
  20.0 0.0 collective-permute-done.6.w_other_ref
  20.0 0.4 %collective-permute-start.7 = (bf16[112,512]{1,0:T(8,128)(2,1)S(1)}, bf16[112,512]{1,0:T(8,128)(2,1)S(1)}, u32[]{:S(2)}, u32[]{:S(2)}) collective-permute-start(bf16[112,512]{1,0:T(8,128)(2,1)S(1)} %get-tuple-element.79), channel_id=1, source_target_pairs={{0,1},{1,0},{2,3},{3,2},{4,5},{5,4},{6,7},{7,6},{8,9},{9,8},{10,11... | collective-permute-start | bytes 344072 | tf_op jit(solution)/shard_map/ppermute | solution.py:273
  20.4 0.0 copy-done.3
  20.4 0.9 %shard_map.96 = (bf16[2,64,512]{2,1,0:T(8,128)(2,1)S(1)}, bf16[2,64,512]{2,1,0:T(8,128)(2,1)S(1)}) custom-call(bf16[8,8,1024]{2,1,0:T(8,128)(2,1)S(1)} %copy-done.3, bf16[8,8,1024]{2,1,0:T(8,128)(2,1)S(1)} %collective-permute-done.other_ref, bf16[8,128]{1,0:T(8,128)(2,1)S(1)} %bitcast.15, bf16[4,1024,512]{2,1,0:T(8,128)(2,1)S(1)} %bitcast.11), custom_call_target="tpu_custom_call" | custom-call | flops 536870912 | bytes 4194304 | tf_op jit(solution)/shard_map/pallas_call | solution.py:345
  21.3 0.1 collective-permute-done.7.got_ref.refs_1_
  21.4 0.4 %collective-permute-start.8 = (bf16[2,64,512]{2,1,0:T(8,128)(2,1)S(1)}, bf16[2,64,512]{2,1,0:T(8,128)(2,1)S(1)}, u32[]{:S(2)}, u32[]{:S(2)}) collective-permute-start(bf16[2,64,512]{2,1,0:T(8,128)(2,1)S(1)} %get-tuple-element.84), channel_id=1, source_target_pairs={{0,1},{1,0},{2,3},{3,2},{4,5},{5,4},{6,7},{7,6},{8,9},{9,8},{10,11... | collective-permute-start | bytes 393224 | tf_op jit(solution)/shard_map/ppermute | solution.py:273
  21.7 3.2 %collective-permute-start.11 = (bf16[64,512]{1,0:T(8,128)(2,1)S(1)}, bf16[64,512]{1,0:T(8,128)(2,1)S(1)}, u32[]{:S(2)}, u32[]{:S(2)}) collective-permute-start(bf16[64,512]{1,0:T(8,128)(2,1)S(1)} %get-tuple-element.90), channel_id=1, source_target_pairs={{0,12},{1,15},{2,14},{3,13},{4,8},{5,11},{6,10},{7,9},{8,4},{9,7},... | collective-permute-start | bytes 196616 | tf_op jit(solution)/shard_map/ppermute | solution.py:281
  25.0 0.0 collective-permute-start.13
  25.0 2.1 %collective-permute-start.15 = (bf16[64,512]{1,0:T(8,128)(2,1)S(1)}, bf16[64,512]{1,0:T(8,128)(2,1)S(1)}, u32[]{:S(2)}, u32[]{:S(2)}) collective-permute-start(bf16[64,512]{1,0:T(8,128)(2,1)S(1)} %get-tuple-element.92), channel_id=1, source_target_pairs={{1,5},{0,6},{3,7},{2,4},{5,1},{4,2},{7,3},{6,0},{9,13},{8,14},{11,... | collective-permute-start | bytes 196616 | tf_op jit(solution)/shard_map/ppermute | solution.py:281
  27.1 1.2 %collective-permute-start.9 = (bf16[32,512]{1,0:T(8,128)(2,1)S(1)}, bf16[32,512]{1,0:T(8,128)(2,1)S(1)}, u32[]{:S(2)}, u32[]{:S(2)}) collective-permute-start(bf16[32,512]{1,0:T(8,128)(2,1)S(1)} %get-tuple-element.88), channel_id=1, source_target_pairs={{0,2},{2,0},{4,6},{6,4},{8,10},{10,8},{12,14},{14,12},{1,3},{3,1},... | collective-permute-start | bytes 98312 | tf_op jit(solution)/shard_map/ppermute | solution.py:286
  28.3 0.3 collective-permute-done.11.refs_4_
  28.6 0.0 collective-permute-start.12
  28.6 3.1 %collective-permute-done.13.refs_6_ = bf16[64,512]{1,0:T(8,128)(2,1)S(1)} collective-permute-done((bf16[64,512]{1,0:T(8,128)(2,1)S(1)}, bf16[64,512]{1,0:T(8,128)(2,1)S(1)}, u32[]{:S(2)}, u32[]{:S(2)}) %collective-permute-start.13) | collective-permute-done | bytes 65568 | tf_op jit(solution)/shard_map/ppermute | solution.py:281
  31.7 0.0 collective-permute-start.14
  31.7 0.0 collective-permute-done.15.refs_8_
  31.7 0.5 %collective-permute-start.16 = (bf16[32,512]{1,0:T(8,128)(2,1)S(1)}, bf16[32,512]{1,0:T(8,128)(2,1)S(1)}, u32[]{:S(2)}, u32[]{:S(2)}) collective-permute-start(bf16[32,512]{1,0:T(8,128)(2,1)S(1)} %slice.19), channel_id=1, source_target_pairs={{0,1},{1,0},{2,3},{3,2},{4,5},{5,4},{6,7},{7,6},{8,9},{9,8},{10,11... | collective-permute-start | bytes 98312 | tf_op jit(solution)/shard_map/ppermute | solution.py:273
  32.2 0.0 collective-permute-done.9.refs_2_
  32.2 0.1 collective-permute-start.10
  32.3 1.1 %collective-permute-done.10.refs_3_ = bf16[16,512]{1,0:T(8,128)(2,1)S(1)} collective-permute-done((bf16[16,512]{1,0:T(8,128)(2,1)S(1)}, bf16[16,512]{1,0:T(8,128)(2,1)S(1)}, u32[]{:S(2)}, u32[]{:S(2)}) %collective-permute-start.10) | collective-permute-done | bytes 16416 | tf_op jit(solution)/shard_map/ppermute | solution.py:273
  33.4 0.0 collective-permute-done.12.refs_5_
  33.4 0.0 collective-permute-done.14.refs_7_
  33.4 0.0 collective-permute-done.16.refs_9_
  33.4 0.0 collective-permute-done.8.got_ref
  33.4 1.9 %shard_map.98 = bf16[8,8,1024]{2,1,0:T(8,128)(2,1)} custom-call(s32[64]{0:T(128)S(1)} %bitcast.18, bf16[8,8,1024]{2,1,0:T(8,128)(2,1)S(1)} %copy-done.3, bf16[2,64,512]{2,1,0:T(8,128)(2,1)S(1)} %get-tuple-element.83.keep_ref, bf16[2,64,512]{2,1,0:T(8,128)(2,1)S(1)} %collective-permute-done.8.got_ref, bf16[512,1024]{1,0:T(8,128)(2,1)S(1)} %copy-done.4, ...), custom_call_target="tpu_custom_call" | custom-call | flops 268435456 | bytes 2097152 | tf_op jit(solution)/shard_map/pallas_call | solution.py:357
  (6 shorter events, 0.0 us)
Async XLA Ops:
  0.0 2.6 %collective-permute-start = (bf16[8,8,1024]{2,1,0:T(8,128)(2,1)}, bf16[8,8,1024]{2,1,0:T(8,128)(2,1)S(1)}, u32[]{:S(2)}, u32[]{:S(2)}) collective-permute-start(bf16[8,8,1024]{2,1,0:T(8,128)(2,1)} %own_ref.5), channel_id=1, source_target_pairs={{0,1},{1,0},{2,3},{3,2},{4,5},{5,4},{6,7},{7,6},{8,9},{9,8},{10,11... | collective-permute-start | bytes 393224 | tf_op jit(solution)/shard_map/ppermute | solution.py:273
  0.5 0.9 %copy-start.2 = (bf16[8,8,1024]{2,1,0:T(8,128)(2,1)S(1)}, bf16[8,8,1024]{2,1,0:T(8,128)(2,1)}, u32[]{:S(2)}) copy-start(bf16[8,8,1024]{2,1,0:T(8,128)(2,1)} %own_ref.5) | copy-start | bytes 393220
  1.4 0.7 %copy-start.6 = (s32[64,1]{0,1:T(1,128)S(1)}, s32[64,1]{0,1:T(1,128)}, u32[]{:S(2)}) copy-start(s32[64,1]{0,1:T(1,128)} %param.15) | copy-start | bytes 772
  2.9 11.9 %copy-start.7 = (s32[64,1]{0,1:T(1,128)S(1)}, s32[64,1]{0,1:T(1,128)}, u32[]{:S(2)}) copy-start(s32[64,1]{0,1:T(1,128)} %param.15) | copy-start | bytes 772
  2.9 11.9 %copy-start.8 = (s32[64,32]{0,1:T(8,128)S(1)}, s32[64,32]{0,1:T(8,128)}, u32[]{:S(2)}) copy-start(s32[64,32]{0,1:T(8,128)} %param.17) | copy-start | bytes 24580
  2.9 11.9 %copy-start.9 = (s32[8]{0:T(128)S(1)}, s32[8]{0:T(128)}, u32[]{:S(2)}) copy-start(s32[8]{0:T(128)} %param.16) | copy-start | bytes 100
  2.9 13.3 %copy-start.4 = (bf16[512,1024]{1,0:T(8,128)(2,1)S(1)}, bf16[512,1024]{1,0:T(8,128)(2,1)}, u32[]{:S(2)}) copy-start(bf16[512,1024]{1,0:T(8,128)(2,1)} %w_own_ref) | copy-start | bytes 3145732
  2.9 13.4 %copy-start = (bf16[1,2048,512]{2,1,0:T(8,128)(2,1)S(1)}, bf16[1,2048,512]{2,1,0:T(8,128)(2,1)}, u32[]{:S(2)}) copy-start(bf16[1,2048,512]{2,1,0:T(8,128)(2,1)} %param.13) | copy-start | bytes 6291460
  2.9 13.4 %copy-start.1 = (bf16[1,2048,512]{2,1,0:T(8,128)(2,1)S(1)}, bf16[1,2048,512]{2,1,0:T(8,128)(2,1)}, u32[]{:S(2)}) copy-start(bf16[1,2048,512]{2,1,0:T(8,128)(2,1)} %param.14) | copy-start | bytes 6291460
  2.9 13.4 %copy-start.5 = (bf16[1024]{0:T(1024)(128)(2,1)S(1)}, bf16[1024]{0:T(1024)(128)(2,1)}, u32[]{:S(2)}) copy-start(bf16[1024]{0:T(1024)(128)(2,1)} %param.10) | copy-start | bytes 6148
  3.0 10.9 %collective-permute-start.1 = (bf16[32,1024]{1,0:T(8,128)(2,1)S(1)}, bf16[32,1024]{1,0:T(8,128)(2,1)S(1)}, u32[]{:S(2)}, u32[]{:S(2)}) collective-permute-start(bf16[32,1024]{1,0:T(8,128)(2,1)S(1)} %get-tuple-element.59), channel_id=1, source_target_pairs={{0,12},{1,15},{2,14},{3,13},{4,8},{5,11},{6,10},{7,9},{8,4},{9,7},... | collective-permute-start | bytes 196616 | tf_op jit(solution)/shard_map/ppermute | solution.py:281
  7.6 7.0 %collective-permute-start.2 = (bf16[32,1024]{1,0:T(8,128)(2,1)S(1)}, bf16[32,1024]{1,0:T(8,128)(2,1)S(1)}, u32[]{:S(2)}, u32[]{:S(2)}) collective-permute-start(bf16[32,1024]{1,0:T(8,128)(2,1)S(1)} %get-tuple-element.60), channel_id=1, source_target_pairs={{1,9},{0,10},{3,11},{2,8},{5,13},{4,14},{7,15},{6,12},{9,1},{8,2},... | collective-permute-start | bytes 196616 | tf_op jit(solution)/shard_map/ppermute | solution.py:281
  8.0 6.6 %collective-permute-start.3 = (bf16[32,1024]{1,0:T(8,128)(2,1)S(1)}, bf16[32,1024]{1,0:T(8,128)(2,1)S(1)}, u32[]{:S(2)}, u32[]{:S(2)}) collective-permute-start(bf16[32,1024]{1,0:T(8,128)(2,1)S(1)} %get-tuple-element.61), channel_id=1, source_target_pairs={{1,5},{0,6},{3,7},{2,4},{5,1},{4,2},{7,3},{6,0},{9,13},{8,14},{11,... | collective-permute-start | bytes 196616 | tf_op jit(solution)/shard_map/ppermute | solution.py:281
  9.2 5.5 %collective-permute-start.4 = (bf16[32,1024]{1,0:T(8,128)(2,1)S(1)}, bf16[32,1024]{1,0:T(8,128)(2,1)S(1)}, u32[]{:S(2)}, u32[]{:S(2)}) collective-permute-start(bf16[32,1024]{1,0:T(8,128)(2,1)S(1)} %get-tuple-element.62), channel_id=1, source_target_pairs={{0,2},{2,0},{4,6},{6,4},{8,10},{10,8},{12,14},{14,12},{1,3},{3,1},... | collective-permute-start | bytes 196616 | tf_op jit(solution)/shard_map/ppermute | solution.py:286
  14.7 1.5 %collective-permute-start.5 = (bf16[96,1024]{1,0:T(8,128)(2,1)S(1)}, bf16[96,1024]{1,0:T(8,128)(2,1)S(1)}, u32[]{:S(2)}, u32[]{:S(2)}) collective-permute-start(bf16[96,1024]{1,0:T(8,128)(2,1)S(1)} %shard_map.93), channel_id=1, source_target_pairs={{0,1},{1,0},{2,3},{3,2},{4,5},{5,4},{6,7},{7,6},{8,9},{9,8},{10,11... | collective-permute-start | bytes 589832 | tf_op jit(solution)/shard_map/ppermute | solution.py:273
  16.2 3.8 %collective-permute-start.6 = (bf16[512,1024]{1,0:T(8,128)(2,1)S(1)}, bf16[512,1024]{1,0:T(8,128)(2,1)S(1)}, u32[]{:S(2)}, u32[]{:S(2)}) collective-permute-start(bf16[512,1024]{1,0:T(8,128)(2,1)S(1)} %copy-done.4), channel_id=1, source_target_pairs={{0,1},{1,0},{2,3},{3,2},{4,5},{5,4},{6,7},{7,6},{8,9},{9,8},{10,11... | collective-permute-start | bytes 3145736 | tf_op jit(solution)/shard_map/ppermute | solution.py:273
  16.3 4.1 %copy-start.3 = (bf16[8,8,1024]{2,1,0:T(8,128)(2,1)S(1)}, bf16[8,8,1024]{2,1,0:T(8,128)(2,1)}, u32[]{:S(2)}) copy-start(bf16[8,8,1024]{2,1,0:T(8,128)(2,1)} %own_ref.5) | copy-start | bytes 393220
  20.0 1.4 %collective-permute-start.7 = (bf16[112,512]{1,0:T(8,128)(2,1)S(1)}, bf16[112,512]{1,0:T(8,128)(2,1)S(1)}, u32[]{:S(2)}, u32[]{:S(2)}) collective-permute-start(bf16[112,512]{1,0:T(8,128)(2,1)S(1)} %get-tuple-element.79), channel_id=1, source_target_pairs={{0,1},{1,0},{2,3},{3,2},{4,5},{5,4},{6,7},{7,6},{8,9},{9,8},{10,11... | collective-permute-start | bytes 344072 | tf_op jit(solution)/shard_map/ppermute | solution.py:273
  21.4 12.1 %collective-permute-start.8 = (bf16[2,64,512]{2,1,0:T(8,128)(2,1)S(1)}, bf16[2,64,512]{2,1,0:T(8,128)(2,1)S(1)}, u32[]{:S(2)}, u32[]{:S(2)}) collective-permute-start(bf16[2,64,512]{2,1,0:T(8,128)(2,1)S(1)} %get-tuple-element.84), channel_id=1, source_target_pairs={{0,1},{1,0},{2,3},{3,2},{4,5},{5,4},{6,7},{7,6},{8,9},{9,8},{10,11... | collective-permute-start | bytes 393224 | tf_op jit(solution)/shard_map/ppermute | solution.py:273
  21.7 6.8 %collective-permute-start.11 = (bf16[64,512]{1,0:T(8,128)(2,1)S(1)}, bf16[64,512]{1,0:T(8,128)(2,1)S(1)}, u32[]{:S(2)}, u32[]{:S(2)}) collective-permute-start(bf16[64,512]{1,0:T(8,128)(2,1)S(1)} %get-tuple-element.90), channel_id=1, source_target_pairs={{0,12},{1,15},{2,14},{3,13},{4,8},{5,11},{6,10},{7,9},{8,4},{9,7},... | collective-permute-start | bytes 196616 | tf_op jit(solution)/shard_map/ppermute | solution.py:281
  25.0 6.7 %collective-permute-start.13 = (bf16[64,512]{1,0:T(8,128)(2,1)S(1)}, bf16[64,512]{1,0:T(8,128)(2,1)S(1)}, u32[]{:S(2)}, u32[]{:S(2)}) collective-permute-start(bf16[64,512]{1,0:T(8,128)(2,1)S(1)} %get-tuple-element.91), channel_id=1, source_target_pairs={{1,9},{0,10},{3,11},{2,8},{5,13},{4,14},{7,15},{6,12},{9,1},{8,2},... | collective-permute-start | bytes 196616 | tf_op jit(solution)/shard_map/ppermute | solution.py:281
  25.0 6.7 %collective-permute-start.15 = (bf16[64,512]{1,0:T(8,128)(2,1)S(1)}, bf16[64,512]{1,0:T(8,128)(2,1)S(1)}, u32[]{:S(2)}, u32[]{:S(2)}) collective-permute-start(bf16[64,512]{1,0:T(8,128)(2,1)S(1)} %get-tuple-element.92), channel_id=1, source_target_pairs={{1,5},{0,6},{3,7},{2,4},{5,1},{4,2},{7,3},{6,0},{9,13},{8,14},{11,... | collective-permute-start | bytes 196616 | tf_op jit(solution)/shard_map/ppermute | solution.py:281
  27.1 5.1 %collective-permute-start.9 = (bf16[32,512]{1,0:T(8,128)(2,1)S(1)}, bf16[32,512]{1,0:T(8,128)(2,1)S(1)}, u32[]{:S(2)}, u32[]{:S(2)}) collective-permute-start(bf16[32,512]{1,0:T(8,128)(2,1)S(1)} %get-tuple-element.88), channel_id=1, source_target_pairs={{0,2},{2,0},{4,6},{6,4},{8,10},{10,8},{12,14},{14,12},{1,3},{3,1},... | collective-permute-start | bytes 98312 | tf_op jit(solution)/shard_map/ppermute | solution.py:286
  28.6 4.8 %collective-permute-start.12 = (bf16[32,512]{1,0:T(8,128)(2,1)S(1)}, bf16[32,512]{1,0:T(8,128)(2,1)S(1)}, u32[]{:S(2)}, u32[]{:S(2)}) collective-permute-start(bf16[32,512]{1,0:T(8,128)(2,1)S(1)} %slice.17), channel_id=1, source_target_pairs={{0,1},{1,0},{2,3},{3,2},{4,5},{5,4},{6,7},{7,6},{8,9},{9,8},{10,11... | collective-permute-start | bytes 98312 | tf_op jit(solution)/shard_map/ppermute | solution.py:273
  31.7 1.7 %collective-permute-start.14 = (bf16[32,512]{1,0:T(8,128)(2,1)S(1)}, bf16[32,512]{1,0:T(8,128)(2,1)S(1)}, u32[]{:S(2)}, u32[]{:S(2)}) collective-permute-start(bf16[32,512]{1,0:T(8,128)(2,1)S(1)} %slice.18), channel_id=1, source_target_pairs={{0,1},{1,0},{2,3},{3,2},{4,5},{5,4},{6,7},{7,6},{8,9},{9,8},{10,11... | collective-permute-start | bytes 98312 | tf_op jit(solution)/shard_map/ppermute | solution.py:273
  31.7 1.7 %collective-permute-start.16 = (bf16[32,512]{1,0:T(8,128)(2,1)S(1)}, bf16[32,512]{1,0:T(8,128)(2,1)S(1)}, u32[]{:S(2)}, u32[]{:S(2)}) collective-permute-start(bf16[32,512]{1,0:T(8,128)(2,1)S(1)} %slice.19), channel_id=1, source_target_pairs={{0,1},{1,0},{2,3},{3,2},{4,5},{5,4},{6,7},{7,6},{8,9},{9,8},{10,11... | collective-permute-start | bytes 98312 | tf_op jit(solution)/shard_map/ppermute | solution.py:273
  32.2 1.2 %collective-permute-start.10 = (bf16[16,512]{1,0:T(8,128)(2,1)S(1)}, bf16[16,512]{1,0:T(8,128)(2,1)S(1)}, u32[]{:S(2)}, u32[]{:S(2)}) collective-permute-start(bf16[16,512]{1,0:T(8,128)(2,1)S(1)} %slice.16), channel_id=1, source_target_pairs={{0,1},{1,0},{2,3},{3,2},{4,5},{5,4},{6,7},{7,6},{8,9},{9,8},{10,11... | collective-permute-start | bytes 49160 | tf_op jit(solution)/shard_map/ppermute | solution.py:273

commit v20 on v18

--- a/solution.py
+++ b/solution.py
@@ -205,19 +205,22 @@
         queries = silu(jnp.dot(normed, w_ref[0], preferred_element_type=jnp.float32)).astype(jnp.bfloat16)
         hide_rows = hide_rows_ref[first * per_owner : first * per_owner + queries.shape[0], :]
         for low in range(0, width, HD):
-            lhs = jnp.concatenate([queries[:, low : low + HD], hide_rows], axis=1)
+            asked = jnp.concatenate([queries[:, low : low + HD], hide_rows], axis=1)
             total = None
             for start in range(0, hist_rows, span):
-                rhs = jnp.concatenate(
+                kept = jnp.concatenate(
                     [keys_ref[start : start + span, low : low + HD], hide_cols_ref[start : start + span, :]], axis=1
                 )
-                scores = lax.dot_general(lhs, rhs, (((1,), (1,)), ((), ())), preferred_element_type=jnp.float32)
+                scores = lax.dot_general(kept, asked, (((1,), (1,)), ((), ())), preferred_element_type=jnp.float32)
                 weights = silu_of_half(scores * (0.5 * SCALE)).astype(jnp.bfloat16)
-                term = jnp.dot(
-                    weights, values_ref[start : start + span, low : low + HD], preferred_element_type=jnp.float32
+                term = lax.dot_general(
+                    values_ref[start : start + span, low : low + HD],
+                    weights,
+                    (((0,), (0,)), ((), ())),
+                    preferred_element_type=jnp.float32,
                 )
                 total = term if total is None else total + term
-            total = total.astype(jnp.bfloat16)
+            total = total.T.astype(jnp.bfloat16)
             for place, at in enumerate(group):
                 for out_ref, row, start, count in targets[at]:
                     low_row = place * per_owner + start

time: 35.5 us -> 36.2 us (1.020)
  Pallas kernels: 8.18 us -> 8.86 us
    pallas_call x1, Pallas kernels: 3.64 us -> 4.32 us  [body(): kernel_call(functools.partial(history_kernel, owners), [bf16((rows_out, w...]
  transfers between devices with their start and end apart: 17 -> 17, of which waited for: 6 -> 6; matrix products, arithmetic and copies ran while one was open for 9% -> 8% of each run, Pallas kernels for 17% -> 19%
where the time goes in v20:
time: 36.2 us; the launch traced here: 36 us
  starting transfers between devices  16.4 us (45%)
  Pallas kernels  8.86 us (24%)
  waiting for transfers between devices  5.85 us (16%)
  local copies, waits for them, and re-layouts  4.64 us (13%)
    ppermute x6, starting transfers between devices, cross(): came.append(lax.ppermute(messages[at], ('cache', 'serve'), pairs))  11.6 us
    pallas_call x1, Pallas kernels, body(): kernel_call(functools.partial(history_kernel, owners), [bf16((rows_out, w...  4.32 us
    ppermute x6, waiting for transfers between devices, cross(): came.append(lax.ppermute(messages[at], ('cache', 'serve'), pairs))  4.21 us
    optimization_barrier x1, local copies, waits for them, and re-layouts, body(): (local, near, *out), w_in = lax.optimization_barrier((out, w_in))  3.02 us
    ppermute x2, starting transfers between devices, to_neighbour(): lax.ppermute(rows, 'cache', [(place, place ^ 1) for place in range(owners)])  2.83 us
    ppermute x9, starting transfers between devices, swap(): return lax.ppermute(rows, 'serve', [(0, 1), (1, 0)])  2.06 us
    pallas_call x1, Pallas kernels, body(): kernel_call(functools.partial(output_kernel, owners), bf16((req_count, ha...  1.86 us
    ppermute x9, waiting for transfers between devices, swap(): return lax.ppermute(rows, 'serve', [(0, 1), (1, 0)])  1.64 us
  transfers between devices with their start and end apart: 17, of which 6 were waited for; matrix products, arithmetic and copies ran while one was open for 8% of the time, Pallas kernels for 19%

profile of v20, /device:TPU:0, one launch (start us, length us, event | category | flops | bytes accessed | tf_op | source)
XLA Modules:
  0.0 36.0 jit_solution(6303965172179408679)
XLA Ops:
  0.0 0.5 %collective-permute-start = (bf16[8,8,1024]{2,1,0:T(8,128)(2,1)}, bf16[8,8,1024]{2,1,0:T(8,128)(2,1)S(1)}, u32[]{:S(2)}, u32[]{:S(2)}) collective-permute-start(bf16[8,8,1024]{2,1,0:T(8,128)(2,1)} %own_ref.5), channel_id=1, source_target_pairs={{0,1},{1,0},{2,3},{3,2},{4,5},{5,4},{6,7},{7,6},{8,9},{9,8},{10,11... | collective-permute-start | bytes 393224 | tf_op jit(solution)/shard_map/ppermute | solution.py:275
  0.5 0.0 copy-start.2
  0.5 0.9 %copy-done.2 = bf16[8,8,1024]{2,1,0:T(8,128)(2,1)S(1)} copy-done((bf16[8,8,1024]{2,1,0:T(8,128)(2,1)S(1)}, bf16[8,8,1024]{2,1,0:T(8,128)(2,1)}, u32[]{:S(2)}) %copy-start.2) | copy-done | bytes 131096
  1.4 0.0 copy-start.6
  1.4 0.7 %copy-done.6 = s32[64,1]{0,1:T(1,128)S(1)} copy-done((s32[64,1]{0,1:T(1,128)S(1)}, s32[64,1]{0,1:T(1,128)}, u32[]{:S(2)}) %copy-start.6) | copy-done | bytes 280
  2.0 0.6 %shard_map.91 = (bf16[160,1024]{1,0:T(8,128)(2,1)S(1)}, bf16[160,64]{1,0:T(8,128)(2,1)S(1)}) custom-call(s32[1,64]{1,0:T(1,128)S(1)} %bitcast.16, bf16[8,8,1024]{2,1,0:T(8,128)(2,1)S(1)} %copy-done.2), custom_call_target="tpu_custom_call" | custom-call | tf_op jit(solution)/shard_map/pallas_call | solution.py:304
  2.6 0.0 collective-permute-done.other_ref
  2.6 0.2 shard_map.92
  2.9 0.0 copy-start.7
  2.9 0.0 copy-start.8
  2.9 0.0 copy-start.9
  2.9 0.0 copy-start.4
  2.9 0.0 copy-start
  2.9 0.0 copy-start.1
  2.9 0.0 copy-start.5
  3.0 4.7 %collective-permute-start.1 = (bf16[32,1024]{1,0:T(8,128)(2,1)S(1)}, bf16[32,1024]{1,0:T(8,128)(2,1)S(1)}, u32[]{:S(2)}, u32[]{:S(2)}) collective-permute-start(bf16[32,1024]{1,0:T(8,128)(2,1)S(1)} %get-tuple-element.59), channel_id=1, source_target_pairs={{0,12},{1,15},{2,14},{3,13},{4,8},{5,11},{6,10},{7,9},{8,4},{9,7},... | collective-permute-start | bytes 196616 | tf_op jit(solution)/shard_map/ppermute | solution.py:283
  7.6 0.4 %collective-permute-start.2 = (bf16[32,1024]{1,0:T(8,128)(2,1)S(1)}, bf16[32,1024]{1,0:T(8,128)(2,1)S(1)}, u32[]{:S(2)}, u32[]{:S(2)}) collective-permute-start(bf16[32,1024]{1,0:T(8,128)(2,1)S(1)} %get-tuple-element.60), channel_id=1, source_target_pairs={{1,9},{0,10},{3,11},{2,8},{5,13},{4,14},{7,15},{6,12},{9,1},{8,2},... | collective-permute-start | bytes 196616 | tf_op jit(solution)/shard_map/ppermute | solution.py:283
  8.0 1.1 %collective-permute-start.3 = (bf16[32,1024]{1,0:T(8,128)(2,1)S(1)}, bf16[32,1024]{1,0:T(8,128)(2,1)S(1)}, u32[]{:S(2)}, u32[]{:S(2)}) collective-permute-start(bf16[32,1024]{1,0:T(8,128)(2,1)S(1)} %get-tuple-element.61), channel_id=1, source_target_pairs={{1,5},{0,6},{3,7},{2,4},{5,1},{4,2},{7,3},{6,0},{9,13},{8,14},{11,... | collective-permute-start | bytes 196616 | tf_op jit(solution)/shard_map/ppermute | solution.py:283
  9.2 1.7 %collective-permute-start.4 = (bf16[32,1024]{1,0:T(8,128)(2,1)S(1)}, bf16[32,1024]{1,0:T(8,128)(2,1)S(1)}, u32[]{:S(2)}, u32[]{:S(2)}) collective-permute-start(bf16[32,1024]{1,0:T(8,128)(2,1)S(1)} %get-tuple-element.62), channel_id=1, source_target_pairs={{0,2},{2,0},{4,6},{6,4},{8,10},{10,8},{12,14},{14,12},{1,3},{3,1},... | collective-permute-start | bytes 196616 | tf_op jit(solution)/shard_map/ppermute | solution.py:288
  10.8 3.0 %copy.12 = bf16[1024,4,512]{2,0,1:T(8,128)(2,1)S(1)} copy(bf16[1024,4,512]{2,1,0:T(4,128)(2,1)} %param.11) | data formatting | bytes 8388608 | tf_op jit(solution)/shard_map/optimization_barrier | solution.py:311
  13.9 0.0 collective-permute-done.1.refs_0_.refs_4_
  13.9 0.8 %collective-permute-done.2.refs_1_.refs_3_ = bf16[32,1024]{1,0:T(8,128)(2,1)S(1)} collective-permute-done((bf16[32,1024]{1,0:T(8,128)(2,1)S(1)}, bf16[32,1024]{1,0:T(8,128)(2,1)S(1)}, u32[]{:S(2)}, u32[]{:S(2)}) %collective-permute-start.2) | collective-permute-done | bytes 65568 | tf_op jit(solution)/shard_map/ppermute | solution.py:283
  14.6 0.0 collective-permute-done.3.refs_2_
  14.7 0.0 collective-permute-done.4.refs_1_
  14.7 0.1 collective-permute-start.5
  14.8 0.0 copy-done.7
  14.8 0.0 copy-done.8
  14.8 0.0 copy-done.9
  14.8 1.0 %shard_map.94 = (bf16[256,128]{1,0:T(8,128)(2,1)S(1)}, bf16[2048,128]{1,0:T(8,128)(2,1)S(1)}) custom-call(s32[1,64]{1,0:T(1,128)S(1)} %bitcast.17, s32[1,8]{1,0:T(1,128)S(1)} %bitcast.20, s32[32,64]{1,0:T(8,128)S(1)} %bitcast.19), custom_call_target="tpu_custom_call" | custom-call | flops 100663296 | tf_op jit(solution)/shard_map/pallas_call | solution.py:317
  15.7 0.4 %collective-permute-done.5.refs_5_ = bf16[96,1024]{1,0:T(8,128)(2,1)S(1)} collective-permute-done((bf16[96,1024]{1,0:T(8,128)(2,1)S(1)}, bf16[96,1024]{1,0:T(8,128)(2,1)S(1)}, u32[]{:S(2)}, u32[]{:S(2)}) %collective-permute-start.5) | collective-permute-done | bytes 196640 | tf_op jit(solution)/shard_map/ppermute | solution.py:275
  16.2 0.0 copy-done.4
  16.2 0.1 collective-permute-start.6
  16.3 0.0 copy-done
  16.3 0.0 copy-done.1
  16.3 0.0 copy-done.5
  16.3 0.0 copy-start.3
  16.3 4.3 %shard_map.95 = (bf16[16,512]{1,0:T(8,128)(2,1)S(1)}, bf16[32,512]{1,0:T(8,128)(2,1)S(1)}, bf16[96,512]{1,0:T(8,128)(2,1)S(1)}, bf16[112,512]{1,0:T(8,128)(2,1)S(1)}) custom-call(bf16[8,128]{1,0:T(8,128)(2,1)S(1)} %bitcast.14, bf16[4,1024,512]{2,1,0:T(8,128)(2,1)S(1)} %bitcast.10, bf16[256,128]{1,0:T(8,128)(2,1)S(1)} %get-tuple-element.71.hide_rows_ref, ...), custom_call_target="tpu_custom_call" | custom-call | flops 2147483648 | bytes 4194304 | tf_op jit(solution)/shard_map/pallas_call | solution.py:326
  20.7 0.0 collective-permute-done.6.w_other_ref
  20.7 0.4 %collective-permute-start.7 = (bf16[112,512]{1,0:T(8,128)(2,1)S(1)}, bf16[112,512]{1,0:T(8,128)(2,1)S(1)}, u32[]{:S(2)}, u32[]{:S(2)}) collective-permute-start(bf16[112,512]{1,0:T(8,128)(2,1)S(1)} %get-tuple-element.79), channel_id=1, source_target_pairs={{0,1},{1,0},{2,3},{3,2},{4,5},{5,4},{6,7},{7,6},{8,9},{9,8},{10,11... | collective-permute-start | bytes 344072 | tf_op jit(solution)/shard_map/ppermute | solution.py:275
  21.1 0.0 copy-done.3
  21.1 0.9 %shard_map.96 = (bf16[2,64,512]{2,1,0:T(8,128)(2,1)S(1)}, bf16[2,64,512]{2,1,0:T(8,128)(2,1)S(1)}) custom-call(bf16[8,8,1024]{2,1,0:T(8,128)(2,1)S(1)} %copy-done.3, bf16[8,8,1024]{2,1,0:T(8,128)(2,1)S(1)} %collective-permute-done.other_ref, bf16[8,128]{1,0:T(8,128)(2,1)S(1)} %bitcast.15, bf16[4,1024,512]{2,1,0:T(8,128)(2,1)S(1)} %bitcast.11), custom_call_target="tpu_custom_call" | custom-call | flops 536870912 | bytes 4194304 | tf_op jit(solution)/shard_map/pallas_call | solution.py:347
  22.0 0.1 collective-permute-done.7.got_ref.refs_1_
  22.1 0.4 collective-permute-start.8
  22.5 3.2 %collective-permute-start.11 = (bf16[64,512]{1,0:T(8,128)(2,1)S(1)}, bf16[64,512]{1,0:T(8,128)(2,1)S(1)}, u32[]{:S(2)}, u32[]{:S(2)}) collective-permute-start(bf16[64,512]{1,0:T(8,128)(2,1)S(1)} %get-tuple-element.90), channel_id=1, source_target_pairs={{0,12},{1,15},{2,14},{3,13},{4,8},{5,11},{6,10},{7,9},{8,4},{9,7},... | collective-permute-start | bytes 196616 | tf_op jit(solution)/shard_map/ppermute | solution.py:283
  25.7 0.0 collective-permute-start.13
  25.7 2.1 %collective-permute-start.15 = (bf16[64,512]{1,0:T(8,128)(2,1)S(1)}, bf16[64,512]{1,0:T(8,128)(2,1)S(1)}, u32[]{:S(2)}, u32[]{:S(2)}) collective-permute-start(bf16[64,512]{1,0:T(8,128)(2,1)S(1)} %get-tuple-element.92), channel_id=1, source_target_pairs={{1,5},{0,6},{3,7},{2,4},{5,1},{4,2},{7,3},{6,0},{9,13},{8,14},{11,... | collective-permute-start | bytes 196616 | tf_op jit(solution)/shard_map/ppermute | solution.py:283
  27.8 1.2 %collective-permute-start.9 = (bf16[32,512]{1,0:T(8,128)(2,1)S(1)}, bf16[32,512]{1,0:T(8,128)(2,1)S(1)}, u32[]{:S(2)}, u32[]{:S(2)}) collective-permute-start(bf16[32,512]{1,0:T(8,128)(2,1)S(1)} %get-tuple-element.88), channel_id=1, source_target_pairs={{0,2},{2,0},{4,6},{6,4},{8,10},{10,8},{12,14},{14,12},{1,3},{3,1},... | collective-permute-start | bytes 98312 | tf_op jit(solution)/shard_map/ppermute | solution.py:288
  29.0 0.3 collective-permute-done.11.refs_4_
  29.3 0.0 collective-permute-start.12
  29.3 3.1 %collective-permute-done.13.refs_6_ = bf16[64,512]{1,0:T(8,128)(2,1)S(1)} collective-permute-done((bf16[64,512]{1,0:T(8,128)(2,1)S(1)}, bf16[64,512]{1,0:T(8,128)(2,1)S(1)}, u32[]{:S(2)}, u32[]{:S(2)}) %collective-permute-start.13) | collective-permute-done | bytes 65568 | tf_op jit(solution)/shard_map/ppermute | solution.py:283
  32.4 0.0 collective-permute-start.14
  32.4 0.0 collective-permute-done.15.refs_8_
  32.4 0.5 %collective-permute-start.16 = (bf16[32,512]{1,0:T(8,128)(2,1)S(1)}, bf16[32,512]{1,0:T(8,128)(2,1)S(1)}, u32[]{:S(2)}, u32[]{:S(2)}) collective-permute-start(bf16[32,512]{1,0:T(8,128)(2,1)S(1)} %slice.19), channel_id=1, source_target_pairs={{0,1},{1,0},{2,3},{3,2},{4,5},{5,4},{6,7},{7,6},{8,9},{9,8},{10,11... | collective-permute-start | bytes 98312 | tf_op jit(solution)/shard_map/ppermute | solution.py:275
  32.9 0.0 collective-permute-done.9.refs_2_
  32.9 0.1 collective-permute-start.10
  33.0 1.1 %collective-permute-done.10.refs_3_ = bf16[16,512]{1,0:T(8,128)(2,1)S(1)} collective-permute-done((bf16[16,512]{1,0:T(8,128)(2,1)S(1)}, bf16[16,512]{1,0:T(8,128)(2,1)S(1)}, u32[]{:S(2)}, u32[]{:S(2)}) %collective-permute-start.10) | collective-permute-done | bytes 16416 | tf_op jit(solution)/shard_map/ppermute | solution.py:275
  34.1 0.0 collective-permute-done.12.refs_5_
  34.1 0.0 collective-permute-done.14.refs_7_
  34.1 0.0 collective-permute-done.16.refs_9_
  34.1 0.0 collective-permute-done.8.got_ref
  34.1 1.9 %shard_map.98 = bf16[8,8,1024]{2,1,0:T(8,128)(2,1)} custom-call(s32[64]{0:T(128)S(1)} %bitcast.18, bf16[8,8,1024]{2,1,0:T(8,128)(2,1)S(1)} %copy-done.3, bf16[2,64,512]{2,1,0:T(8,128)(2,1)S(1)} %get-tuple-element.83.keep_ref, bf16[2,64,512]{2,1,0:T(8,128)(2,1)S(1)} %collective-permute-done.8.got_ref, bf16[512,1024]{1,0:T(8,128)(2,1)S(1)} %copy-done.4, ...), custom_call_target="tpu_custom_call" | custom-call | flops 268435456 | bytes 2097152 | tf_op jit(solution)/shard_map/pallas_call | solution.py:359
  (6 shorter events, 0.0 us)
Async XLA Ops:
  0.0 2.6 %collective-permute-start = (bf16[8,8,1024]{2,1,0:T(8,128)(2,1)}, bf16[8,8,1024]{2,1,0:T(8,128)(2,1)S(1)}, u32[]{:S(2)}, u32[]{:S(2)}) collective-permute-start(bf16[8,8,1024]{2,1,0:T(8,128)(2,1)} %own_ref.5), channel_id=1, source_target_pairs={{0,1},{1,0},{2,3},{3,2},{4,5},{5,4},{6,7},{7,6},{8,9},{9,8},{10,11... | collective-permute-start | bytes 393224 | tf_op jit(solution)/shard_map/ppermute | solution.py:275
  0.5 0.9 %copy-start.2 = (bf16[8,8,1024]{2,1,0:T(8,128)(2,1)S(1)}, bf16[8,8,1024]{2,1,0:T(8,128)(2,1)}, u32[]{:S(2)}) copy-start(bf16[8,8,1024]{2,1,0:T(8,128)(2,1)} %own_ref.5) | copy-start | bytes 393220
  1.4 0.7 %copy-start.6 = (s32[64,1]{0,1:T(1,128)S(1)}, s32[64,1]{0,1:T(1,128)}, u32[]{:S(2)}) copy-start(s32[64,1]{0,1:T(1,128)} %param.15) | copy-start | bytes 772
  2.9 11.9 %copy-start.7 = (s32[64,1]{0,1:T(1,128)S(1)}, s32[64,1]{0,1:T(1,128)}, u32[]{:S(2)}) copy-start(s32[64,1]{0,1:T(1,128)} %param.15) | copy-start | bytes 772
  2.9 11.9 %copy-start.8 = (s32[64,32]{0,1:T(8,128)S(1)}, s32[64,32]{0,1:T(8,128)}, u32[]{:S(2)}) copy-start(s32[64,32]{0,1:T(8,128)} %param.17) | copy-start | bytes 24580
  2.9 11.9 %copy-start.9 = (s32[8]{0:T(128)S(1)}, s32[8]{0:T(128)}, u32[]{:S(2)}) copy-start(s32[8]{0:T(128)} %param.16) | copy-start | bytes 100
  2.9 13.3 %copy-start.4 = (bf16[512,1024]{1,0:T(8,128)(2,1)S(1)}, bf16[512,1024]{1,0:T(8,128)(2,1)}, u32[]{:S(2)}) copy-start(bf16[512,1024]{1,0:T(8,128)(2,1)} %w_own_ref) | copy-start | bytes 3145732
  2.9 13.4 %copy-start = (bf16[1,2048,512]{2,1,0:T(8,128)(2,1)S(1)}, bf16[1,2048,512]{2,1,0:T(8,128)(2,1)}, u32[]{:S(2)}) copy-start(bf16[1,2048,512]{2,1,0:T(8,128)(2,1)} %param.13) | copy-start | bytes 6291460
  2.9 13.4 %copy-start.1 = (bf16[1,2048,512]{2,1,0:T(8,128)(2,1)S(1)}, bf16[1,2048,512]{2,1,0:T(8,128)(2,1)}, u32[]{:S(2)}) copy-start(bf16[1,2048,512]{2,1,0:T(8,128)(2,1)} %param.14) | copy-start | bytes 6291460
  2.9 13.4 %copy-start.5 = (bf16[1024]{0:T(1024)(128)(2,1)S(1)}, bf16[1024]{0:T(1024)(128)(2,1)}, u32[]{:S(2)}) copy-start(bf16[1024]{0:T(1024)(128)(2,1)} %param.10) | copy-start | bytes 6148
  3.0 10.9 %collective-permute-start.1 = (bf16[32,1024]{1,0:T(8,128)(2,1)S(1)}, bf16[32,1024]{1,0:T(8,128)(2,1)S(1)}, u32[]{:S(2)}, u32[]{:S(2)}) collective-permute-start(bf16[32,1024]{1,0:T(8,128)(2,1)S(1)} %get-tuple-element.59), channel_id=1, source_target_pairs={{0,12},{1,15},{2,14},{3,13},{4,8},{5,11},{6,10},{7,9},{8,4},{9,7},... | collective-permute-start | bytes 196616 | tf_op jit(solution)/shard_map/ppermute | solution.py:283
  7.6 7.0 %collective-permute-start.2 = (bf16[32,1024]{1,0:T(8,128)(2,1)S(1)}, bf16[32,1024]{1,0:T(8,128)(2,1)S(1)}, u32[]{:S(2)}, u32[]{:S(2)}) collective-permute-start(bf16[32,1024]{1,0:T(8,128)(2,1)S(1)} %get-tuple-element.60), channel_id=1, source_target_pairs={{1,9},{0,10},{3,11},{2,8},{5,13},{4,14},{7,15},{6,12},{9,1},{8,2},... | collective-permute-start | bytes 196616 | tf_op jit(solution)/shard_map/ppermute | solution.py:283
  8.0 6.6 %collective-permute-start.3 = (bf16[32,1024]{1,0:T(8,128)(2,1)S(1)}, bf16[32,1024]{1,0:T(8,128)(2,1)S(1)}, u32[]{:S(2)}, u32[]{:S(2)}) collective-permute-start(bf16[32,1024]{1,0:T(8,128)(2,1)S(1)} %get-tuple-element.61), channel_id=1, source_target_pairs={{1,5},{0,6},{3,7},{2,4},{5,1},{4,2},{7,3},{6,0},{9,13},{8,14},{11,... | collective-permute-start | bytes 196616 | tf_op jit(solution)/shard_map/ppermute | solution.py:283
  9.2 5.5 %collective-permute-start.4 = (bf16[32,1024]{1,0:T(8,128)(2,1)S(1)}, bf16[32,1024]{1,0:T(8,128)(2,1)S(1)}, u32[]{:S(2)}, u32[]{:S(2)}) collective-permute-start(bf16[32,1024]{1,0:T(8,128)(2,1)S(1)} %get-tuple-element.62), channel_id=1, source_target_pairs={{0,2},{2,0},{4,6},{6,4},{8,10},{10,8},{12,14},{14,12},{1,3},{3,1},... | collective-permute-start | bytes 196616 | tf_op jit(solution)/shard_map/ppermute | solution.py:288
  14.7 1.5 %collective-permute-start.5 = (bf16[96,1024]{1,0:T(8,128)(2,1)S(1)}, bf16[96,1024]{1,0:T(8,128)(2,1)S(1)}, u32[]{:S(2)}, u32[]{:S(2)}) collective-permute-start(bf16[96,1024]{1,0:T(8,128)(2,1)S(1)} %shard_map.93), channel_id=1, source_target_pairs={{0,1},{1,0},{2,3},{3,2},{4,5},{5,4},{6,7},{7,6},{8,9},{9,8},{10,11... | collective-permute-start | bytes 589832 | tf_op jit(solution)/shard_map/ppermute | solution.py:275
  16.2 4.5 %collective-permute-start.6 = (bf16[512,1024]{1,0:T(8,128)(2,1)S(1)}, bf16[512,1024]{1,0:T(8,128)(2,1)S(1)}, u32[]{:S(2)}, u32[]{:S(2)}) collective-permute-start(bf16[512,1024]{1,0:T(8,128)(2,1)S(1)} %copy-done.4), channel_id=1, source_target_pairs={{0,1},{1,0},{2,3},{3,2},{4,5},{5,4},{6,7},{7,6},{8,9},{9,8},{10,11... | collective-permute-start | bytes 3145736 | tf_op jit(solution)/shard_map/ppermute | solution.py:275
  16.3 4.8 %copy-start.3 = (bf16[8,8,1024]{2,1,0:T(8,128)(2,1)S(1)}, bf16[8,8,1024]{2,1,0:T(8,128)(2,1)}, u32[]{:S(2)}) copy-start(bf16[8,8,1024]{2,1,0:T(8,128)(2,1)} %own_ref.5) | copy-start | bytes 393220
  20.7 1.4 %collective-permute-start.7 = (bf16[112,512]{1,0:T(8,128)(2,1)S(1)}, bf16[112,512]{1,0:T(8,128)(2,1)S(1)}, u32[]{:S(2)}, u32[]{:S(2)}) collective-permute-start(bf16[112,512]{1,0:T(8,128)(2,1)S(1)} %get-tuple-element.79), channel_id=1, source_target_pairs={{0,1},{1,0},{2,3},{3,2},{4,5},{5,4},{6,7},{7,6},{8,9},{9,8},{10,11... | collective-permute-start | bytes 344072 | tf_op jit(solution)/shard_map/ppermute | solution.py:275
  22.1 12.0 %collective-permute-start.8 = (bf16[2,64,512]{2,1,0:T(8,128)(2,1)S(1)}, bf16[2,64,512]{2,1,0:T(8,128)(2,1)S(1)}, u32[]{:S(2)}, u32[]{:S(2)}) collective-permute-start(bf16[2,64,512]{2,1,0:T(8,128)(2,1)S(1)} %get-tuple-element.84), channel_id=1, source_target_pairs={{0,1},{1,0},{2,3},{3,2},{4,5},{5,4},{6,7},{7,6},{8,9},{9,8},{10,11... | collective-permute-start | bytes 393224 | tf_op jit(solution)/shard_map/ppermute | solution.py:275
  22.5 6.8 %collective-permute-start.11 = (bf16[64,512]{1,0:T(8,128)(2,1)S(1)}, bf16[64,512]{1,0:T(8,128)(2,1)S(1)}, u32[]{:S(2)}, u32[]{:S(2)}) collective-permute-start(bf16[64,512]{1,0:T(8,128)(2,1)S(1)} %get-tuple-element.90), channel_id=1, source_target_pairs={{0,12},{1,15},{2,14},{3,13},{4,8},{5,11},{6,10},{7,9},{8,4},{9,7},... | collective-permute-start | bytes 196616 | tf_op jit(solution)/shard_map/ppermute | solution.py:283
  25.7 6.7 %collective-permute-start.13 = (bf16[64,512]{1,0:T(8,128)(2,1)S(1)}, bf16[64,512]{1,0:T(8,128)(2,1)S(1)}, u32[]{:S(2)}, u32[]{:S(2)}) collective-permute-start(bf16[64,512]{1,0:T(8,128)(2,1)S(1)} %get-tuple-element.91), channel_id=1, source_target_pairs={{1,9},{0,10},{3,11},{2,8},{5,13},{4,14},{7,15},{6,12},{9,1},{8,2},... | collective-permute-start | bytes 196616 | tf_op jit(solution)/shard_map/ppermute | solution.py:283
  25.7 6.7 %collective-permute-start.15 = (bf16[64,512]{1,0:T(8,128)(2,1)S(1)}, bf16[64,512]{1,0:T(8,128)(2,1)S(1)}, u32[]{:S(2)}, u32[]{:S(2)}) collective-permute-start(bf16[64,512]{1,0:T(8,128)(2,1)S(1)} %get-tuple-element.92), channel_id=1, source_target_pairs={{1,5},{0,6},{3,7},{2,4},{5,1},{4,2},{7,3},{6,0},{9,13},{8,14},{11,... | collective-permute-start | bytes 196616 | tf_op jit(solution)/shard_map/ppermute | solution.py:283
  27.8 5.1 %collective-permute-start.9 = (bf16[32,512]{1,0:T(8,128)(2,1)S(1)}, bf16[32,512]{1,0:T(8,128)(2,1)S(1)}, u32[]{:S(2)}, u32[]{:S(2)}) collective-permute-start(bf16[32,512]{1,0:T(8,128)(2,1)S(1)} %get-tuple-element.88), channel_id=1, source_target_pairs={{0,2},{2,0},{4,6},{6,4},{8,10},{10,8},{12,14},{14,12},{1,3},{3,1},... | collective-permute-start | bytes 98312 | tf_op jit(solution)/shard_map/ppermute | solution.py:288
  29.3 4.8 %collective-permute-start.12 = (bf16[32,512]{1,0:T(8,128)(2,1)S(1)}, bf16[32,512]{1,0:T(8,128)(2,1)S(1)}, u32[]{:S(2)}, u32[]{:S(2)}) collective-permute-start(bf16[32,512]{1,0:T(8,128)(2,1)S(1)} %slice.17), channel_id=1, source_target_pairs={{0,1},{1,0},{2,3},{3,2},{4,5},{5,4},{6,7},{7,6},{8,9},{9,8},{10,11... | collective-permute-start | bytes 98312 | tf_op jit(solution)/shard_map/ppermute | solution.py:275
  32.4 1.7 %collective-permute-start.14 = (bf16[32,512]{1,0:T(8,128)(2,1)S(1)}, bf16[32,512]{1,0:T(8,128)(2,1)S(1)}, u32[]{:S(2)}, u32[]{:S(2)}) collective-permute-start(bf16[32,512]{1,0:T(8,128)(2,1)S(1)} %slice.18), channel_id=1, source_target_pairs={{0,1},{1,0},{2,3},{3,2},{4,5},{5,4},{6,7},{7,6},{8,9},{9,8},{10,11... | collective-permute-start | bytes 98312 | tf_op jit(solution)/shard_map/ppermute | solution.py:275
  32.4 1.7 %collective-permute-start.16 = (bf16[32,512]{1,0:T(8,128)(2,1)S(1)}, bf16[32,512]{1,0:T(8,128)(2,1)S(1)}, u32[]{:S(2)}, u32[]{:S(2)}) collective-permute-start(bf16[32,512]{1,0:T(8,128)(2,1)S(1)} %slice.19), channel_id=1, source_target_pairs={{0,1},{1,0},{2,3},{3,2},{4,5},{5,4},{6,7},{7,6},{8,9},{9,8},{10,11... | collective-permute-start | bytes 98312 | tf_op jit(solution)/shard_map/ppermute | solution.py:275
  32.9 1.2 %collective-permute-start.10 = (bf16[16,512]{1,0:T(8,128)(2,1)S(1)}, bf16[16,512]{1,0:T(8,128)(2,1)S(1)}, u32[]{:S(2)}, u32[]{:S(2)}) collective-permute-start(bf16[16,512]{1,0:T(8,128)(2,1)S(1)} %slice.16), channel_id=1, source_target_pairs={{0,1},{1,0},{2,3},{3,2},{4,5},{5,4},{6,7},{7,6},{8,9},{9,8},{10,11... | collective-permute-start | bytes 49160 | tf_op jit(solution)/shard_map/ppermute | solution.py:275

commit v21 on v18

--- a/solution.py
+++ b/solution.py
@@ -196,7 +196,7 @@
     sources = [(ref, 0) for ref in slot_refs] + [(swapped_ref, at * per_owner) for at in range(owners // 2 - 1)]
     targets = [local, [(near_ref, 0, 0, per_owner)]] + [[target] for target in far]
     hist_rows = keys_ref.shape[0]
-    span = min(256, hist_rows)
+    span = min(512, hist_rows)
     per_step = max(1, min(owners, 256 // per_owner))
     gain = gain_row(gain_ref)
     for first in range(0, owners, per_step):

time: 35.5 us -> 36.1 us (1.017)
  Pallas kernels: 8.18 us -> 8.83 us
    pallas_call x1, Pallas kernels: 3.64 us -> 4.29 us  [body(): kernel_call(functools.partial(history_kernel, owners), [bf16((rows_out, w...]
  transfers between devices with their start and end apart: 17 -> 17, of which waited for: 6 -> 6; matrix products, arithmetic and copies ran while one was open for 9% -> 8% of each run, Pallas kernels for 17% -> 19%
where the time goes in v21:
time: 36.1 us; the launch traced here: 36 us
  starting transfers between devices  16.4 us (45%)
  Pallas kernels  8.83 us (24%)
  waiting for transfers between devices  5.85 us (16%)
  local copies, waits for them, and re-layouts  4.64 us (13%)
    ppermute x6, starting transfers between devices, cross(): came.append(lax.ppermute(messages[at], ('cache', 'serve'), pairs))  11.6 us
    pallas_call x1, Pallas kernels, body(): kernel_call(functools.partial(history_kernel, owners), [bf16((rows_out, w...  4.29 us
    ppermute x6, waiting for transfers between devices, cross(): came.append(lax.ppermute(messages[at], ('cache', 'serve'), pairs))  4.2 us
    optimization_barrier x1, local copies, waits for them, and re-layouts, body(): (local, near, *out), w_in = lax.optimization_barrier((out, w_in))  3.02 us
    ppermute x2, starting transfers between devices, to_neighbour(): lax.ppermute(rows, 'cache', [(place, place ^ 1) for place in range(owners)])  2.83 us
    ppermute x9, starting transfers between devices, swap(): return lax.ppermute(rows, 'serve', [(0, 1), (1, 0)])  2.06 us
    pallas_call x1, Pallas kernels, body(): kernel_call(functools.partial(output_kernel, owners), bf16((req_count, ha...  1.86 us
    ppermute x9, waiting for transfers between devices, swap(): return lax.ppermute(rows, 'serve', [(0, 1), (1, 0)])  1.64 us
  transfers between devices with their start and end apart: 17, of which 6 were waited for; matrix products, arithmetic and copies ran while one was open for 8% of the time, Pallas kernels for 19%

profile of v21, /device:TPU:0, one launch (start us, length us, event | category | flops | bytes accessed | tf_op | source)
XLA Modules:
  0.0 36.0 jit_solution(5023799748570950764)
XLA Ops:
  0.0 0.5 %collective-permute-start = (bf16[8,8,1024]{2,1,0:T(8,128)(2,1)}, bf16[8,8,1024]{2,1,0:T(8,128)(2,1)S(1)}, u32[]{:S(2)}, u32[]{:S(2)}) collective-permute-start(bf16[8,8,1024]{2,1,0:T(8,128)(2,1)} %own_ref.5), channel_id=1, source_target_pairs={{0,1},{1,0},{2,3},{3,2},{4,5},{5,4},{6,7},{7,6},{8,9},{9,8},{10,11... | collective-permute-start | bytes 393224 | tf_op jit(solution)/shard_map/ppermute | solution.py:272
  0.5 0.0 copy-start.2
  0.5 0.9 %copy-done.2 = bf16[8,8,1024]{2,1,0:T(8,128)(2,1)S(1)} copy-done((bf16[8,8,1024]{2,1,0:T(8,128)(2,1)S(1)}, bf16[8,8,1024]{2,1,0:T(8,128)(2,1)}, u32[]{:S(2)}) %copy-start.2) | copy-done | bytes 131096
  1.4 0.0 copy-start.6
  1.4 0.7 %copy-done.6 = s32[64,1]{0,1:T(1,128)S(1)} copy-done((s32[64,1]{0,1:T(1,128)S(1)}, s32[64,1]{0,1:T(1,128)}, u32[]{:S(2)}) %copy-start.6) | copy-done | bytes 280
  2.0 0.6 %shard_map.91 = (bf16[160,1024]{1,0:T(8,128)(2,1)S(1)}, bf16[160,64]{1,0:T(8,128)(2,1)S(1)}) custom-call(s32[1,64]{1,0:T(1,128)S(1)} %bitcast.16, bf16[8,8,1024]{2,1,0:T(8,128)(2,1)S(1)} %copy-done.2), custom_call_target="tpu_custom_call" | custom-call | tf_op jit(solution)/shard_map/pallas_call | solution.py:301
  2.6 0.0 collective-permute-done.other_ref
  2.6 0.2 shard_map.92
  2.9 0.0 copy-start.7
  2.9 0.0 copy-start.8
  2.9 0.0 copy-start.9
  2.9 0.0 copy-start.4
  2.9 0.0 copy-start
  2.9 0.0 copy-start.1
  2.9 0.0 copy-start.5
  3.0 4.7 %collective-permute-start.1 = (bf16[32,1024]{1,0:T(8,128)(2,1)S(1)}, bf16[32,1024]{1,0:T(8,128)(2,1)S(1)}, u32[]{:S(2)}, u32[]{:S(2)}) collective-permute-start(bf16[32,1024]{1,0:T(8,128)(2,1)S(1)} %get-tuple-element.59), channel_id=1, source_target_pairs={{0,12},{1,15},{2,14},{3,13},{4,8},{5,11},{6,10},{7,9},{8,4},{9,7},... | collective-permute-start | bytes 196616 | tf_op jit(solution)/shard_map/ppermute | solution.py:280
  7.6 0.4 %collective-permute-start.2 = (bf16[32,1024]{1,0:T(8,128)(2,1)S(1)}, bf16[32,1024]{1,0:T(8,128)(2,1)S(1)}, u32[]{:S(2)}, u32[]{:S(2)}) collective-permute-start(bf16[32,1024]{1,0:T(8,128)(2,1)S(1)} %get-tuple-element.60), channel_id=1, source_target_pairs={{1,9},{0,10},{3,11},{2,8},{5,13},{4,14},{7,15},{6,12},{9,1},{8,2},... | collective-permute-start | bytes 196616 | tf_op jit(solution)/shard_map/ppermute | solution.py:280
  8.0 1.1 %collective-permute-start.3 = (bf16[32,1024]{1,0:T(8,128)(2,1)S(1)}, bf16[32,1024]{1,0:T(8,128)(2,1)S(1)}, u32[]{:S(2)}, u32[]{:S(2)}) collective-permute-start(bf16[32,1024]{1,0:T(8,128)(2,1)S(1)} %get-tuple-element.61), channel_id=1, source_target_pairs={{1,5},{0,6},{3,7},{2,4},{5,1},{4,2},{7,3},{6,0},{9,13},{8,14},{11,... | collective-permute-start | bytes 196616 | tf_op jit(solution)/shard_map/ppermute | solution.py:280
  9.2 1.7 %collective-permute-start.4 = (bf16[32,1024]{1,0:T(8,128)(2,1)S(1)}, bf16[32,1024]{1,0:T(8,128)(2,1)S(1)}, u32[]{:S(2)}, u32[]{:S(2)}) collective-permute-start(bf16[32,1024]{1,0:T(8,128)(2,1)S(1)} %get-tuple-element.62), channel_id=1, source_target_pairs={{0,2},{2,0},{4,6},{6,4},{8,10},{10,8},{12,14},{14,12},{1,3},{3,1},... | collective-permute-start | bytes 196616 | tf_op jit(solution)/shard_map/ppermute | solution.py:285
  10.8 3.0 %copy.12 = bf16[1024,4,512]{2,0,1:T(8,128)(2,1)S(1)} copy(bf16[1024,4,512]{2,1,0:T(4,128)(2,1)} %param.11) | data formatting | bytes 8388608 | tf_op jit(solution)/shard_map/optimization_barrier | solution.py:308
  13.9 0.0 collective-permute-done.1.refs_0_.refs_4_
  13.9 0.8 %collective-permute-done.2.refs_1_.refs_3_ = bf16[32,1024]{1,0:T(8,128)(2,1)S(1)} collective-permute-done((bf16[32,1024]{1,0:T(8,128)(2,1)S(1)}, bf16[32,1024]{1,0:T(8,128)(2,1)S(1)}, u32[]{:S(2)}, u32[]{:S(2)}) %collective-permute-start.2) | collective-permute-done | bytes 65568 | tf_op jit(solution)/shard_map/ppermute | solution.py:280
  14.6 0.0 collective-permute-done.3.refs_2_
  14.7 0.0 collective-permute-done.4.refs_1_
  14.7 0.1 collective-permute-start.5
  14.8 0.0 copy-done.7
  14.8 0.0 copy-done.8
  14.8 0.0 copy-done.9
  14.8 1.0 %shard_map.94 = (bf16[256,128]{1,0:T(8,128)(2,1)S(1)}, bf16[2048,128]{1,0:T(8,128)(2,1)S(1)}) custom-call(s32[1,64]{1,0:T(1,128)S(1)} %bitcast.17, s32[1,8]{1,0:T(1,128)S(1)} %bitcast.20, s32[32,64]{1,0:T(8,128)S(1)} %bitcast.19), custom_call_target="tpu_custom_call" | custom-call | flops 100663296 | tf_op jit(solution)/shard_map/pallas_call | solution.py:314
  15.7 0.4 %collective-permute-done.5.refs_5_ = bf16[96,1024]{1,0:T(8,128)(2,1)S(1)} collective-permute-done((bf16[96,1024]{1,0:T(8,128)(2,1)S(1)}, bf16[96,1024]{1,0:T(8,128)(2,1)S(1)}, u32[]{:S(2)}, u32[]{:S(2)}) %collective-permute-start.5) | collective-permute-done | bytes 196640 | tf_op jit(solution)/shard_map/ppermute | solution.py:272
  16.2 0.0 copy-done.4
  16.2 0.1 collective-permute-start.6
  16.3 0.0 copy-done
  16.3 0.0 copy-done.1
  16.3 0.0 copy-done.5
  16.3 0.0 copy-start.3
  16.3 4.3 %shard_map.95 = (bf16[16,512]{1,0:T(8,128)(2,1)S(1)}, bf16[32,512]{1,0:T(8,128)(2,1)S(1)}, bf16[96,512]{1,0:T(8,128)(2,1)S(1)}, bf16[112,512]{1,0:T(8,128)(2,1)S(1)}) custom-call(bf16[8,128]{1,0:T(8,128)(2,1)S(1)} %bitcast.14, bf16[4,1024,512]{2,1,0:T(8,128)(2,1)S(1)} %bitcast.10, bf16[256,128]{1,0:T(8,128)(2,1)S(1)} %get-tuple-element.71.hide_rows_ref, ...), custom_call_target="tpu_custom_call" | custom-call | flops 2147483648 | bytes 4194304 | tf_op jit(solution)/shard_map/pallas_call | solution.py:323
  20.6 0.0 collective-permute-done.6.w_other_ref
  20.6 0.4 %collective-permute-start.7 = (bf16[112,512]{1,0:T(8,128)(2,1)S(1)}, bf16[112,512]{1,0:T(8,128)(2,1)S(1)}, u32[]{:S(2)}, u32[]{:S(2)}) collective-permute-start(bf16[112,512]{1,0:T(8,128)(2,1)S(1)} %get-tuple-element.79), channel_id=1, source_target_pairs={{0,1},{1,0},{2,3},{3,2},{4,5},{5,4},{6,7},{7,6},{8,9},{9,8},{10,11... | collective-permute-start | bytes 344072 | tf_op jit(solution)/shard_map/ppermute | solution.py:272
  21.1 0.0 copy-done.3
  21.1 0.9 %shard_map.96 = (bf16[2,64,512]{2,1,0:T(8,128)(2,1)S(1)}, bf16[2,64,512]{2,1,0:T(8,128)(2,1)S(1)}) custom-call(bf16[8,8,1024]{2,1,0:T(8,128)(2,1)S(1)} %copy-done.3, bf16[8,8,1024]{2,1,0:T(8,128)(2,1)S(1)} %collective-permute-done.other_ref, bf16[8,128]{1,0:T(8,128)(2,1)S(1)} %bitcast.15, bf16[4,1024,512]{2,1,0:T(8,128)(2,1)S(1)} %bitcast.11), custom_call_target="tpu_custom_call" | custom-call | flops 536870912 | bytes 4194304 | tf_op jit(solution)/shard_map/pallas_call | solution.py:344
  22.0 0.1 collective-permute-done.7.got_ref.refs_1_
  22.1 0.4 collective-permute-start.8
  22.4 3.2 %collective-permute-start.11 = (bf16[64,512]{1,0:T(8,128)(2,1)S(1)}, bf16[64,512]{1,0:T(8,128)(2,1)S(1)}, u32[]{:S(2)}, u32[]{:S(2)}) collective-permute-start(bf16[64,512]{1,0:T(8,128)(2,1)S(1)} %get-tuple-element.90), channel_id=1, source_target_pairs={{0,12},{1,15},{2,14},{3,13},{4,8},{5,11},{6,10},{7,9},{8,4},{9,7},... | collective-permute-start | bytes 196616 | tf_op jit(solution)/shard_map/ppermute | solution.py:280
  25.7 0.0 collective-permute-start.13
  25.7 2.1 %collective-permute-start.15 = (bf16[64,512]{1,0:T(8,128)(2,1)S(1)}, bf16[64,512]{1,0:T(8,128)(2,1)S(1)}, u32[]{:S(2)}, u32[]{:S(2)}) collective-permute-start(bf16[64,512]{1,0:T(8,128)(2,1)S(1)} %get-tuple-element.92), channel_id=1, source_target_pairs={{1,5},{0,6},{3,7},{2,4},{5,1},{4,2},{7,3},{6,0},{9,13},{8,14},{11,... | collective-permute-start | bytes 196616 | tf_op jit(solution)/shard_map/ppermute | solution.py:280
  27.8 1.2 %collective-permute-start.9 = (bf16[32,512]{1,0:T(8,128)(2,1)S(1)}, bf16[32,512]{1,0:T(8,128)(2,1)S(1)}, u32[]{:S(2)}, u32[]{:S(2)}) collective-permute-start(bf16[32,512]{1,0:T(8,128)(2,1)S(1)} %get-tuple-element.88), channel_id=1, source_target_pairs={{0,2},{2,0},{4,6},{6,4},{8,10},{10,8},{12,14},{14,12},{1,3},{3,1},... | collective-permute-start | bytes 98312 | tf_op jit(solution)/shard_map/ppermute | solution.py:285
  28.9 0.3 collective-permute-done.11.refs_4_
  29.3 0.0 collective-permute-start.12
  29.3 3.1 %collective-permute-done.13.refs_6_ = bf16[64,512]{1,0:T(8,128)(2,1)S(1)} collective-permute-done((bf16[64,512]{1,0:T(8,128)(2,1)S(1)}, bf16[64,512]{1,0:T(8,128)(2,1)S(1)}, u32[]{:S(2)}, u32[]{:S(2)}) %collective-permute-start.13) | collective-permute-done | bytes 65568 | tf_op jit(solution)/shard_map/ppermute | solution.py:280
  32.4 0.0 collective-permute-start.14
  32.4 0.0 collective-permute-done.15.refs_8_
  32.4 0.5 %collective-permute-start.16 = (bf16[32,512]{1,0:T(8,128)(2,1)S(1)}, bf16[32,512]{1,0:T(8,128)(2,1)S(1)}, u32[]{:S(2)}, u32[]{:S(2)}) collective-permute-start(bf16[32,512]{1,0:T(8,128)(2,1)S(1)} %slice.19), channel_id=1, source_target_pairs={{0,1},{1,0},{2,3},{3,2},{4,5},{5,4},{6,7},{7,6},{8,9},{9,8},{10,11... | collective-permute-start | bytes 98312 | tf_op jit(solution)/shard_map/ppermute | solution.py:272
  32.9 0.0 collective-permute-done.9.refs_2_
  32.9 0.1 collective-permute-start.10
  33.0 1.1 %collective-permute-done.10.refs_3_ = bf16[16,512]{1,0:T(8,128)(2,1)S(1)} collective-permute-done((bf16[16,512]{1,0:T(8,128)(2,1)S(1)}, bf16[16,512]{1,0:T(8,128)(2,1)S(1)}, u32[]{:S(2)}, u32[]{:S(2)}) %collective-permute-start.10) | collective-permute-done | bytes 16416 | tf_op jit(solution)/shard_map/ppermute | solution.py:272
  34.1 0.0 collective-permute-done.12.refs_5_
  34.1 0.0 collective-permute-done.14.refs_7_
  34.1 0.0 collective-permute-done.16.refs_9_
  34.1 0.0 collective-permute-done.8.got_ref
  34.1 1.9 %shard_map.98 = bf16[8,8,1024]{2,1,0:T(8,128)(2,1)} custom-call(s32[64]{0:T(128)S(1)} %bitcast.18, bf16[8,8,1024]{2,1,0:T(8,128)(2,1)S(1)} %copy-done.3, bf16[2,64,512]{2,1,0:T(8,128)(2,1)S(1)} %get-tuple-element.83.keep_ref, bf16[2,64,512]{2,1,0:T(8,128)(2,1)S(1)} %collective-permute-done.8.got_ref, bf16[512,1024]{1,0:T(8,128)(2,1)S(1)} %copy-done.4, ...), custom_call_target="tpu_custom_call" | custom-call | flops 268435456 | bytes 2097152 | tf_op jit(solution)/shard_map/pallas_call | solution.py:356
  (6 shorter events, 0.0 us)
Async XLA Ops:
  0.0 2.6 %collective-permute-start = (bf16[8,8,1024]{2,1,0:T(8,128)(2,1)}, bf16[8,8,1024]{2,1,0:T(8,128)(2,1)S(1)}, u32[]{:S(2)}, u32[]{:S(2)}) collective-permute-start(bf16[8,8,1024]{2,1,0:T(8,128)(2,1)} %own_ref.5), channel_id=1, source_target_pairs={{0,1},{1,0},{2,3},{3,2},{4,5},{5,4},{6,7},{7,6},{8,9},{9,8},{10,11... | collective-permute-start | bytes 393224 | tf_op jit(solution)/shard_map/ppermute | solution.py:272
  0.5 0.9 %copy-start.2 = (bf16[8,8,1024]{2,1,0:T(8,128)(2,1)S(1)}, bf16[8,8,1024]{2,1,0:T(8,128)(2,1)}, u32[]{:S(2)}) copy-start(bf16[8,8,1024]{2,1,0:T(8,128)(2,1)} %own_ref.5) | copy-start | bytes 393220
  1.4 0.7 %copy-start.6 = (s32[64,1]{0,1:T(1,128)S(1)}, s32[64,1]{0,1:T(1,128)}, u32[]{:S(2)}) copy-start(s32[64,1]{0,1:T(1,128)} %param.15) | copy-start | bytes 772
  2.9 11.9 %copy-start.7 = (s32[64,1]{0,1:T(1,128)S(1)}, s32[64,1]{0,1:T(1,128)}, u32[]{:S(2)}) copy-start(s32[64,1]{0,1:T(1,128)} %param.15) | copy-start | bytes 772
  2.9 11.9 %copy-start.8 = (s32[64,32]{0,1:T(8,128)S(1)}, s32[64,32]{0,1:T(8,128)}, u32[]{:S(2)}) copy-start(s32[64,32]{0,1:T(8,128)} %param.17) | copy-start | bytes 24580
  2.9 11.9 %copy-start.9 = (s32[8]{0:T(128)S(1)}, s32[8]{0:T(128)}, u32[]{:S(2)}) copy-start(s32[8]{0:T(128)} %param.16) | copy-start | bytes 100
  2.9 13.3 %copy-start.4 = (bf16[512,1024]{1,0:T(8,128)(2,1)S(1)}, bf16[512,1024]{1,0:T(8,128)(2,1)}, u32[]{:S(2)}) copy-start(bf16[512,1024]{1,0:T(8,128)(2,1)} %w_own_ref) | copy-start | bytes 3145732
  2.9 13.4 %copy-start = (bf16[1,2048,512]{2,1,0:T(8,128)(2,1)S(1)}, bf16[1,2048,512]{2,1,0:T(8,128)(2,1)}, u32[]{:S(2)}) copy-start(bf16[1,2048,512]{2,1,0:T(8,128)(2,1)} %param.13) | copy-start | bytes 6291460
  2.9 13.4 %copy-start.1 = (bf16[1,2048,512]{2,1,0:T(8,128)(2,1)S(1)}, bf16[1,2048,512]{2,1,0:T(8,128)(2,1)}, u32[]{:S(2)}) copy-start(bf16[1,2048,512]{2,1,0:T(8,128)(2,1)} %param.14) | copy-start | bytes 6291460
  2.9 13.4 %copy-start.5 = (bf16[1024]{0:T(1024)(128)(2,1)S(1)}, bf16[1024]{0:T(1024)(128)(2,1)}, u32[]{:S(2)}) copy-start(bf16[1024]{0:T(1024)(128)(2,1)} %param.10) | copy-start | bytes 6148
  3.0 10.9 %collective-permute-start.1 = (bf16[32,1024]{1,0:T(8,128)(2,1)S(1)}, bf16[32,1024]{1,0:T(8,128)(2,1)S(1)}, u32[]{:S(2)}, u32[]{:S(2)}) collective-permute-start(bf16[32,1024]{1,0:T(8,128)(2,1)S(1)} %get-tuple-element.59), channel_id=1, source_target_pairs={{0,12},{1,15},{2,14},{3,13},{4,8},{5,11},{6,10},{7,9},{8,4},{9,7},... | collective-permute-start | bytes 196616 | tf_op jit(solution)/shard_map/ppermute | solution.py:280
  7.6 7.0 %collective-permute-start.2 = (bf16[32,1024]{1,0:T(8,128)(2,1)S(1)}, bf16[32,1024]{1,0:T(8,128)(2,1)S(1)}, u32[]{:S(2)}, u32[]{:S(2)}) collective-permute-start(bf16[32,1024]{1,0:T(8,128)(2,1)S(1)} %get-tuple-element.60), channel_id=1, source_target_pairs={{1,9},{0,10},{3,11},{2,8},{5,13},{4,14},{7,15},{6,12},{9,1},{8,2},... | collective-permute-start | bytes 196616 | tf_op jit(solution)/shard_map/ppermute | solution.py:280
  8.0 6.6 %collective-permute-start.3 = (bf16[32,1024]{1,0:T(8,128)(2,1)S(1)}, bf16[32,1024]{1,0:T(8,128)(2,1)S(1)}, u32[]{:S(2)}, u32[]{:S(2)}) collective-permute-start(bf16[32,1024]{1,0:T(8,128)(2,1)S(1)} %get-tuple-element.61), channel_id=1, source_target_pairs={{1,5},{0,6},{3,7},{2,4},{5,1},{4,2},{7,3},{6,0},{9,13},{8,14},{11,... | collective-permute-start | bytes 196616 | tf_op jit(solution)/shard_map/ppermute | solution.py:280
  9.2 5.5 %collective-permute-start.4 = (bf16[32,1024]{1,0:T(8,128)(2,1)S(1)}, bf16[32,1024]{1,0:T(8,128)(2,1)S(1)}, u32[]{:S(2)}, u32[]{:S(2)}) collective-permute-start(bf16[32,1024]{1,0:T(8,128)(2,1)S(1)} %get-tuple-element.62), channel_id=1, source_target_pairs={{0,2},{2,0},{4,6},{6,4},{8,10},{10,8},{12,14},{14,12},{1,3},{3,1},... | collective-permute-start | bytes 196616 | tf_op jit(solution)/shard_map/ppermute | solution.py:285
  14.7 1.5 %collective-permute-start.5 = (bf16[96,1024]{1,0:T(8,128)(2,1)S(1)}, bf16[96,1024]{1,0:T(8,128)(2,1)S(1)}, u32[]{:S(2)}, u32[]{:S(2)}) collective-permute-start(bf16[96,1024]{1,0:T(8,128)(2,1)S(1)} %shard_map.93), channel_id=1, source_target_pairs={{0,1},{1,0},{2,3},{3,2},{4,5},{5,4},{6,7},{7,6},{8,9},{9,8},{10,11... | collective-permute-start | bytes 589832 | tf_op jit(solution)/shard_map/ppermute | solution.py:272
  16.2 4.5 %collective-permute-start.6 = (bf16[512,1024]{1,0:T(8,128)(2,1)S(1)}, bf16[512,1024]{1,0:T(8,128)(2,1)S(1)}, u32[]{:S(2)}, u32[]{:S(2)}) collective-permute-start(bf16[512,1024]{1,0:T(8,128)(2,1)S(1)} %copy-done.4), channel_id=1, source_target_pairs={{0,1},{1,0},{2,3},{3,2},{4,5},{5,4},{6,7},{7,6},{8,9},{9,8},{10,11... | collective-permute-start | bytes 3145736 | tf_op jit(solution)/shard_map/ppermute | solution.py:272
  16.3 4.8 %copy-start.3 = (bf16[8,8,1024]{2,1,0:T(8,128)(2,1)S(1)}, bf16[8,8,1024]{2,1,0:T(8,128)(2,1)}, u32[]{:S(2)}) copy-start(bf16[8,8,1024]{2,1,0:T(8,128)(2,1)} %own_ref.5) | copy-start | bytes 393220
  20.6 1.4 %collective-permute-start.7 = (bf16[112,512]{1,0:T(8,128)(2,1)S(1)}, bf16[112,512]{1,0:T(8,128)(2,1)S(1)}, u32[]{:S(2)}, u32[]{:S(2)}) collective-permute-start(bf16[112,512]{1,0:T(8,128)(2,1)S(1)} %get-tuple-element.79), channel_id=1, source_target_pairs={{0,1},{1,0},{2,3},{3,2},{4,5},{5,4},{6,7},{7,6},{8,9},{9,8},{10,11... | collective-permute-start | bytes 344072 | tf_op jit(solution)/shard_map/ppermute | solution.py:272
  22.1 12.0 %collective-permute-start.8 = (bf16[2,64,512]{2,1,0:T(8,128)(2,1)S(1)}, bf16[2,64,512]{2,1,0:T(8,128)(2,1)S(1)}, u32[]{:S(2)}, u32[]{:S(2)}) collective-permute-start(bf16[2,64,512]{2,1,0:T(8,128)(2,1)S(1)} %get-tuple-element.84), channel_id=1, source_target_pairs={{0,1},{1,0},{2,3},{3,2},{4,5},{5,4},{6,7},{7,6},{8,9},{9,8},{10,11... | collective-permute-start | bytes 393224 | tf_op jit(solution)/shard_map/ppermute | solution.py:272
  22.4 6.8 %collective-permute-start.11 = (bf16[64,512]{1,0:T(8,128)(2,1)S(1)}, bf16[64,512]{1,0:T(8,128)(2,1)S(1)}, u32[]{:S(2)}, u32[]{:S(2)}) collective-permute-start(bf16[64,512]{1,0:T(8,128)(2,1)S(1)} %get-tuple-element.90), channel_id=1, source_target_pairs={{0,12},{1,15},{2,14},{3,13},{4,8},{5,11},{6,10},{7,9},{8,4},{9,7},... | collective-permute-start | bytes 196616 | tf_op jit(solution)/shard_map/ppermute | solution.py:280
  25.7 6.7 %collective-permute-start.13 = (bf16[64,512]{1,0:T(8,128)(2,1)S(1)}, bf16[64,512]{1,0:T(8,128)(2,1)S(1)}, u32[]{:S(2)}, u32[]{:S(2)}) collective-permute-start(bf16[64,512]{1,0:T(8,128)(2,1)S(1)} %get-tuple-element.91), channel_id=1, source_target_pairs={{1,9},{0,10},{3,11},{2,8},{5,13},{4,14},{7,15},{6,12},{9,1},{8,2},... | collective-permute-start | bytes 196616 | tf_op jit(solution)/shard_map/ppermute | solution.py:280
  25.7 6.7 %collective-permute-start.15 = (bf16[64,512]{1,0:T(8,128)(2,1)S(1)}, bf16[64,512]{1,0:T(8,128)(2,1)S(1)}, u32[]{:S(2)}, u32[]{:S(2)}) collective-permute-start(bf16[64,512]{1,0:T(8,128)(2,1)S(1)} %get-tuple-element.92), channel_id=1, source_target_pairs={{1,5},{0,6},{3,7},{2,4},{5,1},{4,2},{7,3},{6,0},{9,13},{8,14},{11,... | collective-permute-start | bytes 196616 | tf_op jit(solution)/shard_map/ppermute | solution.py:280
  27.8 5.1 %collective-permute-start.9 = (bf16[32,512]{1,0:T(8,128)(2,1)S(1)}, bf16[32,512]{1,0:T(8,128)(2,1)S(1)}, u32[]{:S(2)}, u32[]{:S(2)}) collective-permute-start(bf16[32,512]{1,0:T(8,128)(2,1)S(1)} %get-tuple-element.88), channel_id=1, source_target_pairs={{0,2},{2,0},{4,6},{6,4},{8,10},{10,8},{12,14},{14,12},{1,3},{3,1},... | collective-permute-start | bytes 98312 | tf_op jit(solution)/shard_map/ppermute | solution.py:285
  29.3 4.8 %collective-permute-start.12 = (bf16[32,512]{1,0:T(8,128)(2,1)S(1)}, bf16[32,512]{1,0:T(8,128)(2,1)S(1)}, u32[]{:S(2)}, u32[]{:S(2)}) collective-permute-start(bf16[32,512]{1,0:T(8,128)(2,1)S(1)} %slice.17), channel_id=1, source_target_pairs={{0,1},{1,0},{2,3},{3,2},{4,5},{5,4},{6,7},{7,6},{8,9},{9,8},{10,11... | collective-permute-start | bytes 98312 | tf_op jit(solution)/shard_map/ppermute | solution.py:272
  32.4 1.7 %collective-permute-start.14 = (bf16[32,512]{1,0:T(8,128)(2,1)S(1)}, bf16[32,512]{1,0:T(8,128)(2,1)S(1)}, u32[]{:S(2)}, u32[]{:S(2)}) collective-permute-start(bf16[32,512]{1,0:T(8,128)(2,1)S(1)} %slice.18), channel_id=1, source_target_pairs={{0,1},{1,0},{2,3},{3,2},{4,5},{5,4},{6,7},{7,6},{8,9},{9,8},{10,11... | collective-permute-start | bytes 98312 | tf_op jit(solution)/shard_map/ppermute | solution.py:272
  32.4 1.7 %collective-permute-start.16 = (bf16[32,512]{1,0:T(8,128)(2,1)S(1)}, bf16[32,512]{1,0:T(8,128)(2,1)S(1)}, u32[]{:S(2)}, u32[]{:S(2)}) collective-permute-start(bf16[32,512]{1,0:T(8,128)(2,1)S(1)} %slice.19), channel_id=1, source_target_pairs={{0,1},{1,0},{2,3},{3,2},{4,5},{5,4},{6,7},{7,6},{8,9},{9,8},{10,11... | collective-permute-start | bytes 98312 | tf_op jit(solution)/shard_map/ppermute | solution.py:272
  32.9 1.2 %collective-permute-start.10 = (bf16[16,512]{1,0:T(8,128)(2,1)S(1)}, bf16[16,512]{1,0:T(8,128)(2,1)S(1)}, u32[]{:S(2)}, u32[]{:S(2)}) collective-permute-start(bf16[16,512]{1,0:T(8,128)(2,1)S(1)} %slice.16), channel_id=1, source_target_pairs={{0,1},{1,0},{2,3},{3,2},{4,5},{5,4},{6,7},{7,6},{8,9},{9,8},{10,11... | collective-permute-start | bytes 49160 | tf_op jit(solution)/shard_map/ppermute | solution.py:272

commit v22 on v18

--- a/solution.py
+++ b/solution.py
@@ -187,12 +187,12 @@
 
 
 def history_kernel(owners, gain_ref, w_ref, hide_rows_ref, hide_cols_ref, keys_ref, values_ref, *refs):
-    *slot_refs, swapped_ref, local_ref, near_ref, keep_ref, give_ref = refs
+    *slot_refs, swapped_ref, local_ref, near_ref, keep_ref, give_ref, hidden_ref = refs
     width = near_ref.shape[1]
     per_owner = near_ref.shape[0]
-    half = per_owner // 2
+    half_rows = per_owner // 2
     far = [(ref, at * per_owner, 0, per_owner) for ref in (keep_ref, give_ref) for at in range(owners // 2 - 1)]
-    local = [(local_ref, 0, 0, half), (give_ref, (owners // 2 - 1) * per_owner, half, half)]
+    local = [(local_ref, 0, 0, half_rows), (give_ref, (owners // 2 - 1) * per_owner, half_rows, half_rows)]
     sources = [(ref, 0) for ref in slot_refs] + [(swapped_ref, at * per_owner) for at in range(owners // 2 - 1)]
     targets = [local, [(near_ref, 0, 0, per_owner)]] + [[target] for target in far]
     hist_rows = keys_ref.shape[0]
@@ -204,15 +204,21 @@
         normed = jnp.concatenate([normed_rows(*sources[at], per_owner, gain) for at in group], axis=0)
         queries = silu(jnp.dot(normed, w_ref[0], preferred_element_type=jnp.float32)).astype(jnp.bfloat16)
         hide_rows = hide_rows_ref[first * per_owner : first * per_owner + queries.shape[0], :]
+        for start in range(0, hist_rows, span):
+            hidden_ref[:, start : start + span] = lax.dot_general(
+                hide_rows, hide_cols_ref[start : start + span, :], (((1,), (1,)), ((), ())), preferred_element_type=jnp.float32
+            )
         for low in range(0, width, HD):
-            lhs = jnp.concatenate([queries[:, low : low + HD], hide_rows], axis=1)
             total = None
             for start in range(0, hist_rows, span):
-                rhs = jnp.concatenate(
-                    [keys_ref[start : start + span, low : low + HD], hide_cols_ref[start : start + span, :]], axis=1
+                scores = lax.dot_general(
+                    queries[:, low : low + HD],
+                    keys_ref[start : start + span, low : low + HD],
+                    (((1,), (1,)), ((), ())),
+                    preferred_element_type=jnp.float32,
                 )
-                scores = lax.dot_general(lhs, rhs, (((1,), (1,)), ((), ())), preferred_element_type=jnp.float32)
-                weights = silu_of_half(scores * (0.5 * SCALE)).astype(jnp.bfloat16)
+                half = scores * (0.5 * SCALE) + hidden_ref[:, start : start + span]
+                weights = silu_of_half(half).astype(jnp.bfloat16)
                 term = jnp.dot(
                     weights, values_ref[start : start + span, low : low + HD], preferred_element_type=jnp.float32
                 )
@@ -324,6 +330,7 @@
         functools.partial(history_kernel, owners),
         [bf16((rows_out, width)) for rows_out in (piece // 2, piece, messages * piece, messages * piece + piece // 2)],
         [vmem] * (6 + owners // 2 + 2),
+        [pltpu.VMEM((min(owners * piece, 256), hist_rows), jnp.float32)],
         flops=8 * owners * piece * hist_rows * width,
         moved=4 * hist_rows * width,
     )(

time: 35.5 us -> 35.7 us (level)
  transfers between devices with their start and end apart: 17 -> 17, of which waited for: 6 -> 6; matrix products, arithmetic and copies ran while one was open for 9% -> 9% of each run, Pallas kernels for 17% -> 18%
where the time goes in v22:
time: 35.7 us; the launch traced here: 35.5 us
  starting transfers between devices  16.4 us (46%)
  Pallas kernels  8.37 us (23%)
  waiting for transfers between devices  5.86 us (16%)
  local copies, waits for them, and re-layouts  4.64 us (13%)
    ppermute x6, starting transfers between devices, cross(): came.append(lax.ppermute(messages[at], ('cache', 'serve'), pairs))  11.6 us
    ppermute x6, waiting for transfers between devices, cross(): came.append(lax.ppermute(messages[at], ('cache', 'serve'), pairs))  4.22 us
    pallas_call x1, Pallas kernels, body(): kernel_call(functools.partial(history_kernel, owners), [bf16((rows_out, w...  3.83 us
    optimization_barrier x1, local copies, waits for them, and re-layouts, body(): (local, near, *out), w_in = lax.optimization_barrier((out, w_in))  3.02 us
    ppermute x2, starting transfers between devices, to_neighbour(): lax.ppermute(rows, 'cache', [(place, place ^ 1) for place in range(owners)])  2.83 us
    ppermute x9, starting transfers between devices, swap(): return lax.ppermute(rows, 'serve', [(0, 1), (1, 0)])  2.04 us
    pallas_call x1, Pallas kernels, body(): kernel_call(functools.partial(output_kernel, owners), bf16((req_count, ha...  1.86 us
    ppermute x9, waiting for transfers between devices, swap(): return lax.ppermute(rows, 'serve', [(0, 1), (1, 0)])  1.64 us
  transfers between devices with their start and end apart: 17, of which 6 were waited for; matrix products, arithmetic and copies ran while one was open for 9% of the time, Pallas kernels for 18%

profile of v22, /device:TPU:0, one launch (start us, length us, event | category | flops | bytes accessed | tf_op | source)
XLA Modules:
  0.0 35.5 jit_solution(14873851473377791519)
XLA Ops:
  0.0 0.5 %collective-permute-start = (bf16[8,8,1024]{2,1,0:T(8,128)(2,1)}, bf16[8,8,1024]{2,1,0:T(8,128)(2,1)S(1)}, u32[]{:S(2)}, u32[]{:S(2)}) collective-permute-start(bf16[8,8,1024]{2,1,0:T(8,128)(2,1)} %own_ref.5), channel_id=1, source_target_pairs={{0,1},{1,0},{2,3},{3,2},{4,5},{5,4},{6,7},{7,6},{8,9},{9,8},{10,11... | collective-permute-start | bytes 393224 | tf_op jit(solution)/shard_map/ppermute | solution.py:278
  0.5 0.0 copy-start.2
  0.5 0.9 %copy-done.2 = bf16[8,8,1024]{2,1,0:T(8,128)(2,1)S(1)} copy-done((bf16[8,8,1024]{2,1,0:T(8,128)(2,1)S(1)}, bf16[8,8,1024]{2,1,0:T(8,128)(2,1)}, u32[]{:S(2)}) %copy-start.2) | copy-done | bytes 131096
  1.4 0.0 copy-start.6
  1.4 0.7 %copy-done.6 = s32[64,1]{0,1:T(1,128)S(1)} copy-done((s32[64,1]{0,1:T(1,128)S(1)}, s32[64,1]{0,1:T(1,128)}, u32[]{:S(2)}) %copy-start.6) | copy-done | bytes 280
  2.0 0.6 %shard_map.91 = (bf16[160,1024]{1,0:T(8,128)(2,1)S(1)}, bf16[160,64]{1,0:T(8,128)(2,1)S(1)}) custom-call(s32[1,64]{1,0:T(1,128)S(1)} %bitcast.16, bf16[8,8,1024]{2,1,0:T(8,128)(2,1)S(1)} %copy-done.2), custom_call_target="tpu_custom_call" | custom-call | tf_op jit(solution)/shard_map/pallas_call | solution.py:307
  2.6 0.0 collective-permute-done.other_ref
  2.6 0.2 shard_map.92
  2.9 0.0 copy-start.7
  2.9 0.0 copy-start.8
  2.9 0.0 copy-start.9
  2.9 0.0 copy-start.4
  2.9 0.0 copy-start
  2.9 0.0 copy-start.1
  2.9 0.0 copy-start.5
  3.0 4.7 %collective-permute-start.1 = (bf16[32,1024]{1,0:T(8,128)(2,1)S(1)}, bf16[32,1024]{1,0:T(8,128)(2,1)S(1)}, u32[]{:S(2)}, u32[]{:S(2)}) collective-permute-start(bf16[32,1024]{1,0:T(8,128)(2,1)S(1)} %get-tuple-element.59), channel_id=1, source_target_pairs={{0,12},{1,15},{2,14},{3,13},{4,8},{5,11},{6,10},{7,9},{8,4},{9,7},... | collective-permute-start | bytes 196616 | tf_op jit(solution)/shard_map/ppermute | solution.py:286
  7.6 0.4 %collective-permute-start.2 = (bf16[32,1024]{1,0:T(8,128)(2,1)S(1)}, bf16[32,1024]{1,0:T(8,128)(2,1)S(1)}, u32[]{:S(2)}, u32[]{:S(2)}) collective-permute-start(bf16[32,1024]{1,0:T(8,128)(2,1)S(1)} %get-tuple-element.60), channel_id=1, source_target_pairs={{1,9},{0,10},{3,11},{2,8},{5,13},{4,14},{7,15},{6,12},{9,1},{8,2},... | collective-permute-start | bytes 196616 | tf_op jit(solution)/shard_map/ppermute | solution.py:286
  8.0 1.1 %collective-permute-start.3 = (bf16[32,1024]{1,0:T(8,128)(2,1)S(1)}, bf16[32,1024]{1,0:T(8,128)(2,1)S(1)}, u32[]{:S(2)}, u32[]{:S(2)}) collective-permute-start(bf16[32,1024]{1,0:T(8,128)(2,1)S(1)} %get-tuple-element.61), channel_id=1, source_target_pairs={{1,5},{0,6},{3,7},{2,4},{5,1},{4,2},{7,3},{6,0},{9,13},{8,14},{11,... | collective-permute-start | bytes 196616 | tf_op jit(solution)/shard_map/ppermute | solution.py:286
  9.2 1.7 %collective-permute-start.4 = (bf16[32,1024]{1,0:T(8,128)(2,1)S(1)}, bf16[32,1024]{1,0:T(8,128)(2,1)S(1)}, u32[]{:S(2)}, u32[]{:S(2)}) collective-permute-start(bf16[32,1024]{1,0:T(8,128)(2,1)S(1)} %get-tuple-element.62), channel_id=1, source_target_pairs={{0,2},{2,0},{4,6},{6,4},{8,10},{10,8},{12,14},{14,12},{1,3},{3,1},... | collective-permute-start | bytes 196616 | tf_op jit(solution)/shard_map/ppermute | solution.py:291
  10.8 3.0 %copy.12 = bf16[1024,4,512]{2,0,1:T(8,128)(2,1)S(1)} copy(bf16[1024,4,512]{2,1,0:T(4,128)(2,1)} %param.11) | data formatting | bytes 8388608 | tf_op jit(solution)/shard_map/optimization_barrier | solution.py:314
  13.9 0.0 collective-permute-done.1.refs_0_.refs_4_
  13.9 0.8 %collective-permute-done.2.refs_1_.refs_3_ = bf16[32,1024]{1,0:T(8,128)(2,1)S(1)} collective-permute-done((bf16[32,1024]{1,0:T(8,128)(2,1)S(1)}, bf16[32,1024]{1,0:T(8,128)(2,1)S(1)}, u32[]{:S(2)}, u32[]{:S(2)}) %collective-permute-start.2) | collective-permute-done | bytes 65568 | tf_op jit(solution)/shard_map/ppermute | solution.py:286
  14.6 0.0 collective-permute-done.3.refs_2_
  14.7 0.0 collective-permute-done.4.refs_1_
  14.7 0.1 collective-permute-start.5
  14.8 0.0 copy-done.7
  14.8 0.0 copy-done.8
  14.8 0.0 copy-done.9
  14.8 1.0 %shard_map.94 = (bf16[256,128]{1,0:T(8,128)(2,1)S(1)}, bf16[2048,128]{1,0:T(8,128)(2,1)S(1)}) custom-call(s32[1,64]{1,0:T(1,128)S(1)} %bitcast.17, s32[1,8]{1,0:T(1,128)S(1)} %bitcast.20, s32[32,64]{1,0:T(8,128)S(1)} %bitcast.19), custom_call_target="tpu_custom_call" | custom-call | flops 100663296 | tf_op jit(solution)/shard_map/pallas_call | solution.py:320
  15.7 0.4 %collective-permute-done.5.refs_5_ = bf16[96,1024]{1,0:T(8,128)(2,1)S(1)} collective-permute-done((bf16[96,1024]{1,0:T(8,128)(2,1)S(1)}, bf16[96,1024]{1,0:T(8,128)(2,1)S(1)}, u32[]{:S(2)}, u32[]{:S(2)}) %collective-permute-start.5) | collective-permute-done | bytes 196640 | tf_op jit(solution)/shard_map/ppermute | solution.py:278
  16.2 0.0 copy-done.4
  16.2 0.1 collective-permute-start.6
  16.3 0.0 copy-done
  16.3 0.0 copy-done.1
  16.3 0.0 copy-done.5
  16.3 0.0 copy-start.3
  16.3 3.8 %shard_map.95 = (bf16[16,512]{1,0:T(8,128)(2,1)S(1)}, bf16[32,512]{1,0:T(8,128)(2,1)S(1)}, bf16[96,512]{1,0:T(8,128)(2,1)S(1)}, bf16[112,512]{1,0:T(8,128)(2,1)S(1)}) custom-call(bf16[8,128]{1,0:T(8,128)(2,1)S(1)} %bitcast.14, bf16[4,1024,512]{2,1,0:T(8,128)(2,1)S(1)} %bitcast.10, bf16[256,128]{1,0:T(8,128)(2,1)S(1)} %get-tuple-element.71.hide_rows_ref, ...), custom_call_target="tpu_custom_call" | custom-call | flops 2147483648 | bytes 4194304 | tf_op jit(solution)/shard_map/pallas_call | solution.py:329
  20.2 0.0 collective-permute-done.6.w_other_ref
  20.2 0.4 %collective-permute-start.7 = (bf16[112,512]{1,0:T(8,128)(2,1)S(1)}, bf16[112,512]{1,0:T(8,128)(2,1)S(1)}, u32[]{:S(2)}, u32[]{:S(2)}) collective-permute-start(bf16[112,512]{1,0:T(8,128)(2,1)S(1)} %get-tuple-element.79), channel_id=1, source_target_pairs={{0,1},{1,0},{2,3},{3,2},{4,5},{5,4},{6,7},{7,6},{8,9},{9,8},{10,11... | collective-permute-start | bytes 344072 | tf_op jit(solution)/shard_map/ppermute | solution.py:278
  20.6 0.0 copy-done.3
  20.6 0.9 %shard_map.96 = (bf16[2,64,512]{2,1,0:T(8,128)(2,1)S(1)}, bf16[2,64,512]{2,1,0:T(8,128)(2,1)S(1)}) custom-call(bf16[8,8,1024]{2,1,0:T(8,128)(2,1)S(1)} %copy-done.3, bf16[8,8,1024]{2,1,0:T(8,128)(2,1)S(1)} %collective-permute-done.other_ref, bf16[8,128]{1,0:T(8,128)(2,1)S(1)} %bitcast.15, bf16[4,1024,512]{2,1,0:T(8,128)(2,1)S(1)} %bitcast.11), custom_call_target="tpu_custom_call" | custom-call | flops 536870912 | bytes 4194304 | tf_op jit(solution)/shard_map/pallas_call | solution.py:351
  21.5 0.1 collective-permute-done.7.got_ref.refs_1_
  21.6 0.4 %collective-permute-start.8 = (bf16[2,64,512]{2,1,0:T(8,128)(2,1)S(1)}, bf16[2,64,512]{2,1,0:T(8,128)(2,1)S(1)}, u32[]{:S(2)}, u32[]{:S(2)}) collective-permute-start(bf16[2,64,512]{2,1,0:T(8,128)(2,1)S(1)} %get-tuple-element.84), channel_id=1, source_target_pairs={{0,1},{1,0},{2,3},{3,2},{4,5},{5,4},{6,7},{7,6},{8,9},{9,8},{10,11... | collective-permute-start | bytes 393224 | tf_op jit(solution)/shard_map/ppermute | solution.py:278
  22.0 3.2 %collective-permute-start.11 = (bf16[64,512]{1,0:T(8,128)(2,1)S(1)}, bf16[64,512]{1,0:T(8,128)(2,1)S(1)}, u32[]{:S(2)}, u32[]{:S(2)}) collective-permute-start(bf16[64,512]{1,0:T(8,128)(2,1)S(1)} %get-tuple-element.90), channel_id=1, source_target_pairs={{0,12},{1,15},{2,14},{3,13},{4,8},{5,11},{6,10},{7,9},{8,4},{9,7},... | collective-permute-start | bytes 196616 | tf_op jit(solution)/shard_map/ppermute | solution.py:286
  25.2 0.0 collective-permute-start.13
  25.2 2.1 %collective-permute-start.15 = (bf16[64,512]{1,0:T(8,128)(2,1)S(1)}, bf16[64,512]{1,0:T(8,128)(2,1)S(1)}, u32[]{:S(2)}, u32[]{:S(2)}) collective-permute-start(bf16[64,512]{1,0:T(8,128)(2,1)S(1)} %get-tuple-element.92), channel_id=1, source_target_pairs={{1,5},{0,6},{3,7},{2,4},{5,1},{4,2},{7,3},{6,0},{9,13},{8,14},{11,... | collective-permute-start | bytes 196616 | tf_op jit(solution)/shard_map/ppermute | solution.py:286
  27.3 1.2 %collective-permute-start.9 = (bf16[32,512]{1,0:T(8,128)(2,1)S(1)}, bf16[32,512]{1,0:T(8,128)(2,1)S(1)}, u32[]{:S(2)}, u32[]{:S(2)}) collective-permute-start(bf16[32,512]{1,0:T(8,128)(2,1)S(1)} %get-tuple-element.88), channel_id=1, source_target_pairs={{0,2},{2,0},{4,6},{6,4},{8,10},{10,8},{12,14},{14,12},{1,3},{3,1},... | collective-permute-start | bytes 98312 | tf_op jit(solution)/shard_map/ppermute | solution.py:291
  28.5 0.3 collective-permute-done.11.refs_4_
  28.8 0.0 collective-permute-start.12
  28.8 3.1 %collective-permute-done.13.refs_6_ = bf16[64,512]{1,0:T(8,128)(2,1)S(1)} collective-permute-done((bf16[64,512]{1,0:T(8,128)(2,1)S(1)}, bf16[64,512]{1,0:T(8,128)(2,1)S(1)}, u32[]{:S(2)}, u32[]{:S(2)}) %collective-permute-start.13) | collective-permute-done | bytes 65568 | tf_op jit(solution)/shard_map/ppermute | solution.py:286
  31.9 0.0 collective-permute-start.14
  31.9 0.0 collective-permute-done.15.refs_8_
  31.9 0.5 %collective-permute-start.16 = (bf16[32,512]{1,0:T(8,128)(2,1)S(1)}, bf16[32,512]{1,0:T(8,128)(2,1)S(1)}, u32[]{:S(2)}, u32[]{:S(2)}) collective-permute-start(bf16[32,512]{1,0:T(8,128)(2,1)S(1)} %slice.19), channel_id=1, source_target_pairs={{0,1},{1,0},{2,3},{3,2},{4,5},{5,4},{6,7},{7,6},{8,9},{9,8},{10,11... | collective-permute-start | bytes 98312 | tf_op jit(solution)/shard_map/ppermute | solution.py:278
  32.4 0.0 collective-permute-done.9.refs_2_
  32.4 0.1 collective-permute-start.10
  32.5 1.1 %collective-permute-done.10.refs_3_ = bf16[16,512]{1,0:T(8,128)(2,1)S(1)} collective-permute-done((bf16[16,512]{1,0:T(8,128)(2,1)S(1)}, bf16[16,512]{1,0:T(8,128)(2,1)S(1)}, u32[]{:S(2)}, u32[]{:S(2)}) %collective-permute-start.10) | collective-permute-done | bytes 16416 | tf_op jit(solution)/shard_map/ppermute | solution.py:278
  33.6 0.0 collective-permute-done.12.refs_5_
  33.6 0.0 collective-permute-done.14.refs_7_
  33.6 0.0 collective-permute-done.16.refs_9_
  33.6 0.0 collective-permute-done.8.got_ref
  33.7 1.9 %shard_map.98 = bf16[8,8,1024]{2,1,0:T(8,128)(2,1)} custom-call(s32[64]{0:T(128)S(1)} %bitcast.18, bf16[8,8,1024]{2,1,0:T(8,128)(2,1)S(1)} %copy-done.3, bf16[2,64,512]{2,1,0:T(8,128)(2,1)S(1)} %get-tuple-element.83.keep_ref, bf16[2,64,512]{2,1,0:T(8,128)(2,1)S(1)} %collective-permute-done.8.got_ref, bf16[512,1024]{1,0:T(8,128)(2,1)S(1)} %copy-done.4, ...), custom_call_target="tpu_custom_call" | custom-call | flops 268435456 | bytes 2097152 | tf_op jit(solution)/shard_map/pallas_call | solution.py:363
  (6 shorter events, 0.0 us)
Async XLA Ops:
  0.0 2.6 %collective-permute-start = (bf16[8,8,1024]{2,1,0:T(8,128)(2,1)}, bf16[8,8,1024]{2,1,0:T(8,128)(2,1)S(1)}, u32[]{:S(2)}, u32[]{:S(2)}) collective-permute-start(bf16[8,8,1024]{2,1,0:T(8,128)(2,1)} %own_ref.5), channel_id=1, source_target_pairs={{0,1},{1,0},{2,3},{3,2},{4,5},{5,4},{6,7},{7,6},{8,9},{9,8},{10,11... | collective-permute-start | bytes 393224 | tf_op jit(solution)/shard_map/ppermute | solution.py:278
  0.5 0.9 %copy-start.2 = (bf16[8,8,1024]{2,1,0:T(8,128)(2,1)S(1)}, bf16[8,8,1024]{2,1,0:T(8,128)(2,1)}, u32[]{:S(2)}) copy-start(bf16[8,8,1024]{2,1,0:T(8,128)(2,1)} %own_ref.5) | copy-start | bytes 393220
  1.4 0.7 %copy-start.6 = (s32[64,1]{0,1:T(1,128)S(1)}, s32[64,1]{0,1:T(1,128)}, u32[]{:S(2)}) copy-start(s32[64,1]{0,1:T(1,128)} %param.15) | copy-start | bytes 772
  2.9 11.9 %copy-start.7 = (s32[64,1]{0,1:T(1,128)S(1)}, s32[64,1]{0,1:T(1,128)}, u32[]{:S(2)}) copy-start(s32[64,1]{0,1:T(1,128)} %param.15) | copy-start | bytes 772
  2.9 11.9 %copy-start.8 = (s32[64,32]{0,1:T(8,128)S(1)}, s32[64,32]{0,1:T(8,128)}, u32[]{:S(2)}) copy-start(s32[64,32]{0,1:T(8,128)} %param.17) | copy-start | bytes 24580
  2.9 11.9 %copy-start.9 = (s32[8]{0:T(128)S(1)}, s32[8]{0:T(128)}, u32[]{:S(2)}) copy-start(s32[8]{0:T(128)} %param.16) | copy-start | bytes 100
  2.9 13.3 %copy-start.4 = (bf16[512,1024]{1,0:T(8,128)(2,1)S(1)}, bf16[512,1024]{1,0:T(8,128)(2,1)}, u32[]{:S(2)}) copy-start(bf16[512,1024]{1,0:T(8,128)(2,1)} %w_own_ref) | copy-start | bytes 3145732
  2.9 13.4 %copy-start = (bf16[1,2048,512]{2,1,0:T(8,128)(2,1)S(1)}, bf16[1,2048,512]{2,1,0:T(8,128)(2,1)}, u32[]{:S(2)}) copy-start(bf16[1,2048,512]{2,1,0:T(8,128)(2,1)} %param.13) | copy-start | bytes 6291460
  2.9 13.4 %copy-start.1 = (bf16[1,2048,512]{2,1,0:T(8,128)(2,1)S(1)}, bf16[1,2048,512]{2,1,0:T(8,128)(2,1)}, u32[]{:S(2)}) copy-start(bf16[1,2048,512]{2,1,0:T(8,128)(2,1)} %param.14) | copy-start | bytes 6291460
  2.9 13.4 %copy-start.5 = (bf16[1024]{0:T(1024)(128)(2,1)S(1)}, bf16[1024]{0:T(1024)(128)(2,1)}, u32[]{:S(2)}) copy-start(bf16[1024]{0:T(1024)(128)(2,1)} %param.10) | copy-start | bytes 6148
  3.0 10.9 %collective-permute-start.1 = (bf16[32,1024]{1,0:T(8,128)(2,1)S(1)}, bf16[32,1024]{1,0:T(8,128)(2,1)S(1)}, u32[]{:S(2)}, u32[]{:S(2)}) collective-permute-start(bf16[32,1024]{1,0:T(8,128)(2,1)S(1)} %get-tuple-element.59), channel_id=1, source_target_pairs={{0,12},{1,15},{2,14},{3,13},{4,8},{5,11},{6,10},{7,9},{8,4},{9,7},... | collective-permute-start | bytes 196616 | tf_op jit(solution)/shard_map/ppermute | solution.py:286
  7.6 7.0 %collective-permute-start.2 = (bf16[32,1024]{1,0:T(8,128)(2,1)S(1)}, bf16[32,1024]{1,0:T(8,128)(2,1)S(1)}, u32[]{:S(2)}, u32[]{:S(2)}) collective-permute-start(bf16[32,1024]{1,0:T(8,128)(2,1)S(1)} %get-tuple-element.60), channel_id=1, source_target_pairs={{1,9},{0,10},{3,11},{2,8},{5,13},{4,14},{7,15},{6,12},{9,1},{8,2},... | collective-permute-start | bytes 196616 | tf_op jit(solution)/shard_map/ppermute | solution.py:286
  8.0 6.6 %collective-permute-start.3 = (bf16[32,1024]{1,0:T(8,128)(2,1)S(1)}, bf16[32,1024]{1,0:T(8,128)(2,1)S(1)}, u32[]{:S(2)}, u32[]{:S(2)}) collective-permute-start(bf16[32,1024]{1,0:T(8,128)(2,1)S(1)} %get-tuple-element.61), channel_id=1, source_target_pairs={{1,5},{0,6},{3,7},{2,4},{5,1},{4,2},{7,3},{6,0},{9,13},{8,14},{11,... | collective-permute-start | bytes 196616 | tf_op jit(solution)/shard_map/ppermute | solution.py:286
  9.2 5.5 %collective-permute-start.4 = (bf16[32,1024]{1,0:T(8,128)(2,1)S(1)}, bf16[32,1024]{1,0:T(8,128)(2,1)S(1)}, u32[]{:S(2)}, u32[]{:S(2)}) collective-permute-start(bf16[32,1024]{1,0:T(8,128)(2,1)S(1)} %get-tuple-element.62), channel_id=1, source_target_pairs={{0,2},{2,0},{4,6},{6,4},{8,10},{10,8},{12,14},{14,12},{1,3},{3,1},... | collective-permute-start | bytes 196616 | tf_op jit(solution)/shard_map/ppermute | solution.py:291
  14.7 1.5 %collective-permute-start.5 = (bf16[96,1024]{1,0:T(8,128)(2,1)S(1)}, bf16[96,1024]{1,0:T(8,128)(2,1)S(1)}, u32[]{:S(2)}, u32[]{:S(2)}) collective-permute-start(bf16[96,1024]{1,0:T(8,128)(2,1)S(1)} %shard_map.93), channel_id=1, source_target_pairs={{0,1},{1,0},{2,3},{3,2},{4,5},{5,4},{6,7},{7,6},{8,9},{9,8},{10,11... | collective-permute-start | bytes 589832 | tf_op jit(solution)/shard_map/ppermute | solution.py:278
  16.2 4.0 %collective-permute-start.6 = (bf16[512,1024]{1,0:T(8,128)(2,1)S(1)}, bf16[512,1024]{1,0:T(8,128)(2,1)S(1)}, u32[]{:S(2)}, u32[]{:S(2)}) collective-permute-start(bf16[512,1024]{1,0:T(8,128)(2,1)S(1)} %copy-done.4), channel_id=1, source_target_pairs={{0,1},{1,0},{2,3},{3,2},{4,5},{5,4},{6,7},{7,6},{8,9},{9,8},{10,11... | collective-permute-start | bytes 3145736 | tf_op jit(solution)/shard_map/ppermute | solution.py:278
  16.3 4.3 %copy-start.3 = (bf16[8,8,1024]{2,1,0:T(8,128)(2,1)S(1)}, bf16[8,8,1024]{2,1,0:T(8,128)(2,1)}, u32[]{:S(2)}) copy-start(bf16[8,8,1024]{2,1,0:T(8,128)(2,1)} %own_ref.5) | copy-start | bytes 393220
  20.2 1.4 %collective-permute-start.7 = (bf16[112,512]{1,0:T(8,128)(2,1)S(1)}, bf16[112,512]{1,0:T(8,128)(2,1)S(1)}, u32[]{:S(2)}, u32[]{:S(2)}) collective-permute-start(bf16[112,512]{1,0:T(8,128)(2,1)S(1)} %get-tuple-element.79), channel_id=1, source_target_pairs={{0,1},{1,0},{2,3},{3,2},{4,5},{5,4},{6,7},{7,6},{8,9},{9,8},{10,11... | collective-permute-start | bytes 344072 | tf_op jit(solution)/shard_map/ppermute | solution.py:278
  21.6 12.1 %collective-permute-start.8 = (bf16[2,64,512]{2,1,0:T(8,128)(2,1)S(1)}, bf16[2,64,512]{2,1,0:T(8,128)(2,1)S(1)}, u32[]{:S(2)}, u32[]{:S(2)}) collective-permute-start(bf16[2,64,512]{2,1,0:T(8,128)(2,1)S(1)} %get-tuple-element.84), channel_id=1, source_target_pairs={{0,1},{1,0},{2,3},{3,2},{4,5},{5,4},{6,7},{7,6},{8,9},{9,8},{10,11... | collective-permute-start | bytes 393224 | tf_op jit(solution)/shard_map/ppermute | solution.py:278
  22.0 6.8 %collective-permute-start.11 = (bf16[64,512]{1,0:T(8,128)(2,1)S(1)}, bf16[64,512]{1,0:T(8,128)(2,1)S(1)}, u32[]{:S(2)}, u32[]{:S(2)}) collective-permute-start(bf16[64,512]{1,0:T(8,128)(2,1)S(1)} %get-tuple-element.90), channel_id=1, source_target_pairs={{0,12},{1,15},{2,14},{3,13},{4,8},{5,11},{6,10},{7,9},{8,4},{9,7},... | collective-permute-start | bytes 196616 | tf_op jit(solution)/shard_map/ppermute | solution.py:286
  25.2 6.7 %collective-permute-start.13 = (bf16[64,512]{1,0:T(8,128)(2,1)S(1)}, bf16[64,512]{1,0:T(8,128)(2,1)S(1)}, u32[]{:S(2)}, u32[]{:S(2)}) collective-permute-start(bf16[64,512]{1,0:T(8,128)(2,1)S(1)} %get-tuple-element.91), channel_id=1, source_target_pairs={{1,9},{0,10},{3,11},{2,8},{5,13},{4,14},{7,15},{6,12},{9,1},{8,2},... | collective-permute-start | bytes 196616 | tf_op jit(solution)/shard_map/ppermute | solution.py:286
  25.2 6.7 %collective-permute-start.15 = (bf16[64,512]{1,0:T(8,128)(2,1)S(1)}, bf16[64,512]{1,0:T(8,128)(2,1)S(1)}, u32[]{:S(2)}, u32[]{:S(2)}) collective-permute-start(bf16[64,512]{1,0:T(8,128)(2,1)S(1)} %get-tuple-element.92), channel_id=1, source_target_pairs={{1,5},{0,6},{3,7},{2,4},{5,1},{4,2},{7,3},{6,0},{9,13},{8,14},{11,... | collective-permute-start | bytes 196616 | tf_op jit(solution)/shard_map/ppermute | solution.py:286
  27.3 5.1 %collective-permute-start.9 = (bf16[32,512]{1,0:T(8,128)(2,1)S(1)}, bf16[32,512]{1,0:T(8,128)(2,1)S(1)}, u32[]{:S(2)}, u32[]{:S(2)}) collective-permute-start(bf16[32,512]{1,0:T(8,128)(2,1)S(1)} %get-tuple-element.88), channel_id=1, source_target_pairs={{0,2},{2,0},{4,6},{6,4},{8,10},{10,8},{12,14},{14,12},{1,3},{3,1},... | collective-permute-start | bytes 98312 | tf_op jit(solution)/shard_map/ppermute | solution.py:291
  28.8 4.8 %collective-permute-start.12 = (bf16[32,512]{1,0:T(8,128)(2,1)S(1)}, bf16[32,512]{1,0:T(8,128)(2,1)S(1)}, u32[]{:S(2)}, u32[]{:S(2)}) collective-permute-start(bf16[32,512]{1,0:T(8,128)(2,1)S(1)} %slice.17), channel_id=1, source_target_pairs={{0,1},{1,0},{2,3},{3,2},{4,5},{5,4},{6,7},{7,6},{8,9},{9,8},{10,11... | collective-permute-start | bytes 98312 | tf_op jit(solution)/shard_map/ppermute | solution.py:278
  31.9 1.7 %collective-permute-start.14 = (bf16[32,512]{1,0:T(8,128)(2,1)S(1)}, bf16[32,512]{1,0:T(8,128)(2,1)S(1)}, u32[]{:S(2)}, u32[]{:S(2)}) collective-permute-start(bf16[32,512]{1,0:T(8,128)(2,1)S(1)} %slice.18), channel_id=1, source_target_pairs={{0,1},{1,0},{2,3},{3,2},{4,5},{5,4},{6,7},{7,6},{8,9},{9,8},{10,11... | collective-permute-start | bytes 98312 | tf_op jit(solution)/shard_map/ppermute | solution.py:278
  31.9 1.7 %collective-permute-start.16 = (bf16[32,512]{1,0:T(8,128)(2,1)S(1)}, bf16[32,512]{1,0:T(8,128)(2,1)S(1)}, u32[]{:S(2)}, u32[]{:S(2)}) collective-permute-start(bf16[32,512]{1,0:T(8,128)(2,1)S(1)} %slice.19), channel_id=1, source_target_pairs={{0,1},{1,0},{2,3},{3,2},{4,5},{5,4},{6,7},{7,6},{8,9},{9,8},{10,11... | collective-permute-start | bytes 98312 | tf_op jit(solution)/shard_map/ppermute | solution.py:278
  32.4 1.2 %collective-permute-start.10 = (bf16[16,512]{1,0:T(8,128)(2,1)S(1)}, bf16[16,512]{1,0:T(8,128)(2,1)S(1)}, u32[]{:S(2)}, u32[]{:S(2)}) collective-permute-start(bf16[16,512]{1,0:T(8,128)(2,1)S(1)} %slice.16), channel_id=1, source_target_pairs={{0,1},{1,0},{2,3},{3,2},{4,5},{5,4},{6,7},{7,6},{8,9},{9,8},{10,11... | collective-permute-start | bytes 49160 | tf_op jit(solution)/shard_map/ppermute | solution.py:278

commit v23 on v21

--- a/solution.py
+++ b/solution.py
@@ -196,7 +196,7 @@
     sources = [(ref, 0) for ref in slot_refs] + [(swapped_ref, at * per_owner) for at in range(owners // 2 - 1)]
     targets = [local, [(near_ref, 0, 0, per_owner)]] + [[target] for target in far]
     hist_rows = keys_ref.shape[0]
-    span = min(512, hist_rows)
+    span = min(128, hist_rows)
     per_step = max(1, min(owners, 256 // per_owner))
     gain = gain_row(gain_ref)
     for first in range(0, owners, per_step):

time: 36.1 us -> 37.2 us (1.030)
  Pallas kernels: 8.83 us -> 9.87 us
    pallas_call x1, Pallas kernels: 4.29 us -> 5.34 us  [body(): kernel_call(functools.partial(history_kernel, owners), [bf16((rows_out, w...]
  transfers between devices with their start and end apart: 17 -> 17, of which waited for: 6 -> 6; matrix products, arithmetic and copies ran while one was open for 8% -> 8% of each run, Pallas kernels for 19% -> 21%
where the time goes in v23:
time: 37.2 us; the launch traced here: 37 us
  starting transfers between devices  16.4 us (44%)
  Pallas kernels  9.87 us (27%)
  waiting for transfers between devices  5.86 us (16%)
  local copies, waits for them, and re-layouts  4.64 us (12%)
    ppermute x6, starting transfers between devices, cross(): came.append(lax.ppermute(messages[at], ('cache', 'serve'), pairs))  11.6 us
    pallas_call x1, Pallas kernels, body(): kernel_call(functools.partial(history_kernel, owners), [bf16((rows_out, w...  5.34 us
    ppermute x6, waiting for transfers between devices, cross(): came.append(lax.ppermute(messages[at], ('cache', 'serve'), pairs))  4.22 us
    optimization_barrier x1, local copies, waits for them, and re-layouts, body(): (local, near, *out), w_in = lax.optimization_barrier((out, w_in))  3.02 us
    ppermute x2, starting transfers between devices, to_neighbour(): lax.ppermute(rows, 'cache', [(place, place ^ 1) for place in range(owners)])  2.83 us
    ppermute x9, starting transfers between devices, swap(): return lax.ppermute(rows, 'serve', [(0, 1), (1, 0)])  2.04 us
    pallas_call x1, Pallas kernels, body(): kernel_call(functools.partial(output_kernel, owners), bf16((req_count, ha...  1.86 us
    ppermute x9, waiting for transfers between devices, swap(): return lax.ppermute(rows, 'serve', [(0, 1), (1, 0)])  1.64 us
  transfers between devices with their start and end apart: 17, of which 6 were waited for; matrix products, arithmetic and copies ran while one was open for 8% of the time, Pallas kernels for 21%

profile of v23, /device:TPU:0, one launch (start us, length us, event | category | flops | bytes accessed | tf_op | source)
XLA Modules:
  0.0 37.0 jit_solution(1113677215022082994)
XLA Ops:
  0.0 0.5 %collective-permute-start = (bf16[8,8,1024]{2,1,0:T(8,128)(2,1)}, bf16[8,8,1024]{2,1,0:T(8,128)(2,1)S(1)}, u32[]{:S(2)}, u32[]{:S(2)}) collective-permute-start(bf16[8,8,1024]{2,1,0:T(8,128)(2,1)} %own_ref.5), channel_id=1, source_target_pairs={{0,1},{1,0},{2,3},{3,2},{4,5},{5,4},{6,7},{7,6},{8,9},{9,8},{10,11... | collective-permute-start | bytes 393224 | tf_op jit(solution)/shard_map/ppermute | solution.py:272
  0.5 0.0 copy-start.2
  0.5 0.9 %copy-done.2 = bf16[8,8,1024]{2,1,0:T(8,128)(2,1)S(1)} copy-done((bf16[8,8,1024]{2,1,0:T(8,128)(2,1)S(1)}, bf16[8,8,1024]{2,1,0:T(8,128)(2,1)}, u32[]{:S(2)}) %copy-start.2) | copy-done | bytes 131096
  1.4 0.0 copy-start.6
  1.4 0.7 %copy-done.6 = s32[64,1]{0,1:T(1,128)S(1)} copy-done((s32[64,1]{0,1:T(1,128)S(1)}, s32[64,1]{0,1:T(1,128)}, u32[]{:S(2)}) %copy-start.6) | copy-done | bytes 280
  2.0 0.6 %shard_map.91 = (bf16[160,1024]{1,0:T(8,128)(2,1)S(1)}, bf16[160,64]{1,0:T(8,128)(2,1)S(1)}) custom-call(s32[1,64]{1,0:T(1,128)S(1)} %bitcast.16, bf16[8,8,1024]{2,1,0:T(8,128)(2,1)S(1)} %copy-done.2), custom_call_target="tpu_custom_call" | custom-call | tf_op jit(solution)/shard_map/pallas_call | solution.py:301
  2.6 0.0 collective-permute-done.other_ref
  2.6 0.2 shard_map.92
  2.9 0.0 copy-start.7
  2.9 0.0 copy-start.8
  2.9 0.0 copy-start.9
  2.9 0.0 copy-start.4
  2.9 0.0 copy-start
  2.9 0.0 copy-start.1
  2.9 0.0 copy-start.5
  3.0 4.7 %collective-permute-start.1 = (bf16[32,1024]{1,0:T(8,128)(2,1)S(1)}, bf16[32,1024]{1,0:T(8,128)(2,1)S(1)}, u32[]{:S(2)}, u32[]{:S(2)}) collective-permute-start(bf16[32,1024]{1,0:T(8,128)(2,1)S(1)} %get-tuple-element.59), channel_id=1, source_target_pairs={{0,12},{1,15},{2,14},{3,13},{4,8},{5,11},{6,10},{7,9},{8,4},{9,7},... | collective-permute-start | bytes 196616 | tf_op jit(solution)/shard_map/ppermute | solution.py:280
  7.6 0.4 %collective-permute-start.2 = (bf16[32,1024]{1,0:T(8,128)(2,1)S(1)}, bf16[32,1024]{1,0:T(8,128)(2,1)S(1)}, u32[]{:S(2)}, u32[]{:S(2)}) collective-permute-start(bf16[32,1024]{1,0:T(8,128)(2,1)S(1)} %get-tuple-element.60), channel_id=1, source_target_pairs={{1,9},{0,10},{3,11},{2,8},{5,13},{4,14},{7,15},{6,12},{9,1},{8,2},... | collective-permute-start | bytes 196616 | tf_op jit(solution)/shard_map/ppermute | solution.py:280
  8.0 1.1 %collective-permute-start.3 = (bf16[32,1024]{1,0:T(8,128)(2,1)S(1)}, bf16[32,1024]{1,0:T(8,128)(2,1)S(1)}, u32[]{:S(2)}, u32[]{:S(2)}) collective-permute-start(bf16[32,1024]{1,0:T(8,128)(2,1)S(1)} %get-tuple-element.61), channel_id=1, source_target_pairs={{1,5},{0,6},{3,7},{2,4},{5,1},{4,2},{7,3},{6,0},{9,13},{8,14},{11,... | collective-permute-start | bytes 196616 | tf_op jit(solution)/shard_map/ppermute | solution.py:280
  9.2 1.7 %collective-permute-start.4 = (bf16[32,1024]{1,0:T(8,128)(2,1)S(1)}, bf16[32,1024]{1,0:T(8,128)(2,1)S(1)}, u32[]{:S(2)}, u32[]{:S(2)}) collective-permute-start(bf16[32,1024]{1,0:T(8,128)(2,1)S(1)} %get-tuple-element.62), channel_id=1, source_target_pairs={{0,2},{2,0},{4,6},{6,4},{8,10},{10,8},{12,14},{14,12},{1,3},{3,1},... | collective-permute-start | bytes 196616 | tf_op jit(solution)/shard_map/ppermute | solution.py:285
  10.8 3.0 %copy.12 = bf16[1024,4,512]{2,0,1:T(8,128)(2,1)S(1)} copy(bf16[1024,4,512]{2,1,0:T(4,128)(2,1)} %param.11) | data formatting | bytes 8388608 | tf_op jit(solution)/shard_map/optimization_barrier | solution.py:308
  13.9 0.0 collective-permute-done.1.refs_0_.refs_4_
  13.9 0.8 %collective-permute-done.2.refs_1_.refs_3_ = bf16[32,1024]{1,0:T(8,128)(2,1)S(1)} collective-permute-done((bf16[32,1024]{1,0:T(8,128)(2,1)S(1)}, bf16[32,1024]{1,0:T(8,128)(2,1)S(1)}, u32[]{:S(2)}, u32[]{:S(2)}) %collective-permute-start.2) | collective-permute-done | bytes 65568 | tf_op jit(solution)/shard_map/ppermute | solution.py:280
  14.6 0.0 collective-permute-done.3.refs_2_
  14.7 0.0 collective-permute-done.4.refs_1_
  14.7 0.1 collective-permute-start.5
  14.8 0.0 copy-done.7
  14.8 0.0 copy-done.8
  14.8 0.0 copy-done.9
  14.8 1.0 %shard_map.94 = (bf16[256,128]{1,0:T(8,128)(2,1)S(1)}, bf16[2048,128]{1,0:T(8,128)(2,1)S(1)}) custom-call(s32[1,64]{1,0:T(1,128)S(1)} %bitcast.17, s32[1,8]{1,0:T(1,128)S(1)} %bitcast.20, s32[32,64]{1,0:T(8,128)S(1)} %bitcast.19), custom_call_target="tpu_custom_call" | custom-call | flops 100663296 | tf_op jit(solution)/shard_map/pallas_call | solution.py:314
  15.7 0.4 %collective-permute-done.5.refs_5_ = bf16[96,1024]{1,0:T(8,128)(2,1)S(1)} collective-permute-done((bf16[96,1024]{1,0:T(8,128)(2,1)S(1)}, bf16[96,1024]{1,0:T(8,128)(2,1)S(1)}, u32[]{:S(2)}, u32[]{:S(2)}) %collective-permute-start.5) | collective-permute-done | bytes 196640 | tf_op jit(solution)/shard_map/ppermute | solution.py:272
  16.2 0.0 copy-done.4
  16.2 0.1 collective-permute-start.6
  16.3 0.0 copy-done
  16.3 0.0 copy-done.1
  16.3 0.0 copy-done.5
  16.3 0.0 copy-start.3
  16.3 5.3 %shard_map.95 = (bf16[16,512]{1,0:T(8,128)(2,1)S(1)}, bf16[32,512]{1,0:T(8,128)(2,1)S(1)}, bf16[96,512]{1,0:T(8,128)(2,1)S(1)}, bf16[112,512]{1,0:T(8,128)(2,1)S(1)}) custom-call(bf16[8,128]{1,0:T(8,128)(2,1)S(1)} %bitcast.14, bf16[4,1024,512]{2,1,0:T(8,128)(2,1)S(1)} %bitcast.10, bf16[256,128]{1,0:T(8,128)(2,1)S(1)} %get-tuple-element.71.hide_rows_ref, ...), custom_call_target="tpu_custom_call" | custom-call | flops 2147483648 | bytes 4194304 | tf_op jit(solution)/shard_map/pallas_call | solution.py:323
  21.7 0.0 collective-permute-done.6.w_other_ref
  21.7 0.4 %collective-permute-start.7 = (bf16[112,512]{1,0:T(8,128)(2,1)S(1)}, bf16[112,512]{1,0:T(8,128)(2,1)S(1)}, u32[]{:S(2)}, u32[]{:S(2)}) collective-permute-start(bf16[112,512]{1,0:T(8,128)(2,1)S(1)} %get-tuple-element.79), channel_id=1, source_target_pairs={{0,1},{1,0},{2,3},{3,2},{4,5},{5,4},{6,7},{7,6},{8,9},{9,8},{10,11... | collective-permute-start | bytes 344072 | tf_op jit(solution)/shard_map/ppermute | solution.py:272
  22.1 0.0 copy-done.3
  22.1 0.9 %shard_map.96 = (bf16[2,64,512]{2,1,0:T(8,128)(2,1)S(1)}, bf16[2,64,512]{2,1,0:T(8,128)(2,1)S(1)}) custom-call(bf16[8,8,1024]{2,1,0:T(8,128)(2,1)S(1)} %copy-done.3, bf16[8,8,1024]{2,1,0:T(8,128)(2,1)S(1)} %collective-permute-done.other_ref, bf16[8,128]{1,0:T(8,128)(2,1)S(1)} %bitcast.15, bf16[4,1024,512]{2,1,0:T(8,128)(2,1)S(1)} %bitcast.11), custom_call_target="tpu_custom_call" | custom-call | flops 536870912 | bytes 4194304 | tf_op jit(solution)/shard_map/pallas_call | solution.py:344
  23.0 0.1 collective-permute-done.7.got_ref.refs_1_
  23.1 0.4 collective-permute-start.8
  23.5 3.2 %collective-permute-start.11 = (bf16[64,512]{1,0:T(8,128)(2,1)S(1)}, bf16[64,512]{1,0:T(8,128)(2,1)S(1)}, u32[]{:S(2)}, u32[]{:S(2)}) collective-permute-start(bf16[64,512]{1,0:T(8,128)(2,1)S(1)} %get-tuple-element.90), channel_id=1, source_target_pairs={{0,12},{1,15},{2,14},{3,13},{4,8},{5,11},{6,10},{7,9},{8,4},{9,7},... | collective-permute-start | bytes 196616 | tf_op jit(solution)/shard_map/ppermute | solution.py:280
  26.7 0.0 collective-permute-start.13
  26.7 2.1 %collective-permute-start.15 = (bf16[64,512]{1,0:T(8,128)(2,1)S(1)}, bf16[64,512]{1,0:T(8,128)(2,1)S(1)}, u32[]{:S(2)}, u32[]{:S(2)}) collective-permute-start(bf16[64,512]{1,0:T(8,128)(2,1)S(1)} %get-tuple-element.92), channel_id=1, source_target_pairs={{1,5},{0,6},{3,7},{2,4},{5,1},{4,2},{7,3},{6,0},{9,13},{8,14},{11,... | collective-permute-start | bytes 196616 | tf_op jit(solution)/shard_map/ppermute | solution.py:280
  28.8 1.2 %collective-permute-start.9 = (bf16[32,512]{1,0:T(8,128)(2,1)S(1)}, bf16[32,512]{1,0:T(8,128)(2,1)S(1)}, u32[]{:S(2)}, u32[]{:S(2)}) collective-permute-start(bf16[32,512]{1,0:T(8,128)(2,1)S(1)} %get-tuple-element.88), channel_id=1, source_target_pairs={{0,2},{2,0},{4,6},{6,4},{8,10},{10,8},{12,14},{14,12},{1,3},{3,1},... | collective-permute-start | bytes 98312 | tf_op jit(solution)/shard_map/ppermute | solution.py:285
  30.0 0.3 collective-permute-done.11.refs_4_
  30.3 0.0 collective-permute-start.12
  30.3 3.1 %collective-permute-done.13.refs_6_ = bf16[64,512]{1,0:T(8,128)(2,1)S(1)} collective-permute-done((bf16[64,512]{1,0:T(8,128)(2,1)S(1)}, bf16[64,512]{1,0:T(8,128)(2,1)S(1)}, u32[]{:S(2)}, u32[]{:S(2)}) %collective-permute-start.13) | collective-permute-done | bytes 65568 | tf_op jit(solution)/shard_map/ppermute | solution.py:280
  33.4 0.0 collective-permute-start.14
  33.4 0.0 collective-permute-done.15.refs_8_
  33.4 0.5 %collective-permute-start.16 = (bf16[32,512]{1,0:T(8,128)(2,1)S(1)}, bf16[32,512]{1,0:T(8,128)(2,1)S(1)}, u32[]{:S(2)}, u32[]{:S(2)}) collective-permute-start(bf16[32,512]{1,0:T(8,128)(2,1)S(1)} %slice.19), channel_id=1, source_target_pairs={{0,1},{1,0},{2,3},{3,2},{4,5},{5,4},{6,7},{7,6},{8,9},{9,8},{10,11... | collective-permute-start | bytes 98312 | tf_op jit(solution)/shard_map/ppermute | solution.py:272
  33.9 0.0 collective-permute-done.9.refs_2_
  33.9 0.1 collective-permute-start.10
  34.0 1.1 %collective-permute-done.10.refs_3_ = bf16[16,512]{1,0:T(8,128)(2,1)S(1)} collective-permute-done((bf16[16,512]{1,0:T(8,128)(2,1)S(1)}, bf16[16,512]{1,0:T(8,128)(2,1)S(1)}, u32[]{:S(2)}, u32[]{:S(2)}) %collective-permute-start.10) | collective-permute-done | bytes 16416 | tf_op jit(solution)/shard_map/ppermute | solution.py:272
  35.1 0.0 collective-permute-done.12.refs_5_
  35.1 0.0 collective-permute-done.14.refs_7_
  35.1 0.0 collective-permute-done.16.refs_9_
  35.1 0.0 collective-permute-done.8.got_ref
  35.2 1.9 %shard_map.98 = bf16[8,8,1024]{2,1,0:T(8,128)(2,1)} custom-call(s32[64]{0:T(128)S(1)} %bitcast.18, bf16[8,8,1024]{2,1,0:T(8,128)(2,1)S(1)} %copy-done.3, bf16[2,64,512]{2,1,0:T(8,128)(2,1)S(1)} %get-tuple-element.83.keep_ref, bf16[2,64,512]{2,1,0:T(8,128)(2,1)S(1)} %collective-permute-done.8.got_ref, bf16[512,1024]{1,0:T(8,128)(2,1)S(1)} %copy-done.4, ...), custom_call_target="tpu_custom_call" | custom-call | flops 268435456 | bytes 2097152 | tf_op jit(solution)/shard_map/pallas_call | solution.py:356
  (6 shorter events, 0.0 us)
Async XLA Ops:
  0.0 2.6 %collective-permute-start = (bf16[8,8,1024]{2,1,0:T(8,128)(2,1)}, bf16[8,8,1024]{2,1,0:T(8,128)(2,1)S(1)}, u32[]{:S(2)}, u32[]{:S(2)}) collective-permute-start(bf16[8,8,1024]{2,1,0:T(8,128)(2,1)} %own_ref.5), channel_id=1, source_target_pairs={{0,1},{1,0},{2,3},{3,2},{4,5},{5,4},{6,7},{7,6},{8,9},{9,8},{10,11... | collective-permute-start | bytes 393224 | tf_op jit(solution)/shard_map/ppermute | solution.py:272
  0.5 0.9 %copy-start.2 = (bf16[8,8,1024]{2,1,0:T(8,128)(2,1)S(1)}, bf16[8,8,1024]{2,1,0:T(8,128)(2,1)}, u32[]{:S(2)}) copy-start(bf16[8,8,1024]{2,1,0:T(8,128)(2,1)} %own_ref.5) | copy-start | bytes 393220
  1.4 0.7 %copy-start.6 = (s32[64,1]{0,1:T(1,128)S(1)}, s32[64,1]{0,1:T(1,128)}, u32[]{:S(2)}) copy-start(s32[64,1]{0,1:T(1,128)} %param.15) | copy-start | bytes 772
  2.9 11.9 %copy-start.7 = (s32[64,1]{0,1:T(1,128)S(1)}, s32[64,1]{0,1:T(1,128)}, u32[]{:S(2)}) copy-start(s32[64,1]{0,1:T(1,128)} %param.15) | copy-start | bytes 772
  2.9 11.9 %copy-start.8 = (s32[64,32]{0,1:T(8,128)S(1)}, s32[64,32]{0,1:T(8,128)}, u32[]{:S(2)}) copy-start(s32[64,32]{0,1:T(8,128)} %param.17) | copy-start | bytes 24580
  2.9 11.9 %copy-start.9 = (s32[8]{0:T(128)S(1)}, s32[8]{0:T(128)}, u32[]{:S(2)}) copy-start(s32[8]{0:T(128)} %param.16) | copy-start | bytes 100
  2.9 13.3 %copy-start.4 = (bf16[512,1024]{1,0:T(8,128)(2,1)S(1)}, bf16[512,1024]{1,0:T(8,128)(2,1)}, u32[]{:S(2)}) copy-start(bf16[512,1024]{1,0:T(8,128)(2,1)} %w_own_ref) | copy-start | bytes 3145732
  2.9 13.4 %copy-start = (bf16[1,2048,512]{2,1,0:T(8,128)(2,1)S(1)}, bf16[1,2048,512]{2,1,0:T(8,128)(2,1)}, u32[]{:S(2)}) copy-start(bf16[1,2048,512]{2,1,0:T(8,128)(2,1)} %param.13) | copy-start | bytes 6291460
  2.9 13.4 %copy-start.1 = (bf16[1,2048,512]{2,1,0:T(8,128)(2,1)S(1)}, bf16[1,2048,512]{2,1,0:T(8,128)(2,1)}, u32[]{:S(2)}) copy-start(bf16[1,2048,512]{2,1,0:T(8,128)(2,1)} %param.14) | copy-start | bytes 6291460
  2.9 13.4 %copy-start.5 = (bf16[1024]{0:T(1024)(128)(2,1)S(1)}, bf16[1024]{0:T(1024)(128)(2,1)}, u32[]{:S(2)}) copy-start(bf16[1024]{0:T(1024)(128)(2,1)} %param.10) | copy-start | bytes 6148
  3.0 10.9 %collective-permute-start.1 = (bf16[32,1024]{1,0:T(8,128)(2,1)S(1)}, bf16[32,1024]{1,0:T(8,128)(2,1)S(1)}, u32[]{:S(2)}, u32[]{:S(2)}) collective-permute-start(bf16[32,1024]{1,0:T(8,128)(2,1)S(1)} %get-tuple-element.59), channel_id=1, source_target_pairs={{0,12},{1,15},{2,14},{3,13},{4,8},{5,11},{6,10},{7,9},{8,4},{9,7},... | collective-permute-start | bytes 196616 | tf_op jit(solution)/shard_map/ppermute | solution.py:280
  7.6 7.0 %collective-permute-start.2 = (bf16[32,1024]{1,0:T(8,128)(2,1)S(1)}, bf16[32,1024]{1,0:T(8,128)(2,1)S(1)}, u32[]{:S(2)}, u32[]{:S(2)}) collective-permute-start(bf16[32,1024]{1,0:T(8,128)(2,1)S(1)} %get-tuple-element.60), channel_id=1, source_target_pairs={{1,9},{0,10},{3,11},{2,8},{5,13},{4,14},{7,15},{6,12},{9,1},{8,2},... | collective-permute-start | bytes 196616 | tf_op jit(solution)/shard_map/ppermute | solution.py:280
  8.0 6.6 %collective-permute-start.3 = (bf16[32,1024]{1,0:T(8,128)(2,1)S(1)}, bf16[32,1024]{1,0:T(8,128)(2,1)S(1)}, u32[]{:S(2)}, u32[]{:S(2)}) collective-permute-start(bf16[32,1024]{1,0:T(8,128)(2,1)S(1)} %get-tuple-element.61), channel_id=1, source_target_pairs={{1,5},{0,6},{3,7},{2,4},{5,1},{4,2},{7,3},{6,0},{9,13},{8,14},{11,... | collective-permute-start | bytes 196616 | tf_op jit(solution)/shard_map/ppermute | solution.py:280
  9.2 5.5 %collective-permute-start.4 = (bf16[32,1024]{1,0:T(8,128)(2,1)S(1)}, bf16[32,1024]{1,0:T(8,128)(2,1)S(1)}, u32[]{:S(2)}, u32[]{:S(2)}) collective-permute-start(bf16[32,1024]{1,0:T(8,128)(2,1)S(1)} %get-tuple-element.62), channel_id=1, source_target_pairs={{0,2},{2,0},{4,6},{6,4},{8,10},{10,8},{12,14},{14,12},{1,3},{3,1},... | collective-permute-start | bytes 196616 | tf_op jit(solution)/shard_map/ppermute | solution.py:285
  14.7 1.5 %collective-permute-start.5 = (bf16[96,1024]{1,0:T(8,128)(2,1)S(1)}, bf16[96,1024]{1,0:T(8,128)(2,1)S(1)}, u32[]{:S(2)}, u32[]{:S(2)}) collective-permute-start(bf16[96,1024]{1,0:T(8,128)(2,1)S(1)} %shard_map.93), channel_id=1, source_target_pairs={{0,1},{1,0},{2,3},{3,2},{4,5},{5,4},{6,7},{7,6},{8,9},{9,8},{10,11... | collective-permute-start | bytes 589832 | tf_op jit(solution)/shard_map/ppermute | solution.py:272
  16.2 5.5 %collective-permute-start.6 = (bf16[512,1024]{1,0:T(8,128)(2,1)S(1)}, bf16[512,1024]{1,0:T(8,128)(2,1)S(1)}, u32[]{:S(2)}, u32[]{:S(2)}) collective-permute-start(bf16[512,1024]{1,0:T(8,128)(2,1)S(1)} %copy-done.4), channel_id=1, source_target_pairs={{0,1},{1,0},{2,3},{3,2},{4,5},{5,4},{6,7},{7,6},{8,9},{9,8},{10,11... | collective-permute-start | bytes 3145736 | tf_op jit(solution)/shard_map/ppermute | solution.py:272
  16.3 5.8 %copy-start.3 = (bf16[8,8,1024]{2,1,0:T(8,128)(2,1)S(1)}, bf16[8,8,1024]{2,1,0:T(8,128)(2,1)}, u32[]{:S(2)}) copy-start(bf16[8,8,1024]{2,1,0:T(8,128)(2,1)} %own_ref.5) | copy-start | bytes 393220
  21.7 1.4 %collective-permute-start.7 = (bf16[112,512]{1,0:T(8,128)(2,1)S(1)}, bf16[112,512]{1,0:T(8,128)(2,1)S(1)}, u32[]{:S(2)}, u32[]{:S(2)}) collective-permute-start(bf16[112,512]{1,0:T(8,128)(2,1)S(1)} %get-tuple-element.79), channel_id=1, source_target_pairs={{0,1},{1,0},{2,3},{3,2},{4,5},{5,4},{6,7},{7,6},{8,9},{9,8},{10,11... | collective-permute-start | bytes 344072 | tf_op jit(solution)/shard_map/ppermute | solution.py:272
  23.1 12.1 %collective-permute-start.8 = (bf16[2,64,512]{2,1,0:T(8,128)(2,1)S(1)}, bf16[2,64,512]{2,1,0:T(8,128)(2,1)S(1)}, u32[]{:S(2)}, u32[]{:S(2)}) collective-permute-start(bf16[2,64,512]{2,1,0:T(8,128)(2,1)S(1)} %get-tuple-element.84), channel_id=1, source_target_pairs={{0,1},{1,0},{2,3},{3,2},{4,5},{5,4},{6,7},{7,6},{8,9},{9,8},{10,11... | collective-permute-start | bytes 393224 | tf_op jit(solution)/shard_map/ppermute | solution.py:272
  23.5 6.8 %collective-permute-start.11 = (bf16[64,512]{1,0:T(8,128)(2,1)S(1)}, bf16[64,512]{1,0:T(8,128)(2,1)S(1)}, u32[]{:S(2)}, u32[]{:S(2)}) collective-permute-start(bf16[64,512]{1,0:T(8,128)(2,1)S(1)} %get-tuple-element.90), channel_id=1, source_target_pairs={{0,12},{1,15},{2,14},{3,13},{4,8},{5,11},{6,10},{7,9},{8,4},{9,7},... | collective-permute-start | bytes 196616 | tf_op jit(solution)/shard_map/ppermute | solution.py:280
  26.7 6.7 %collective-permute-start.13 = (bf16[64,512]{1,0:T(8,128)(2,1)S(1)}, bf16[64,512]{1,0:T(8,128)(2,1)S(1)}, u32[]{:S(2)}, u32[]{:S(2)}) collective-permute-start(bf16[64,512]{1,0:T(8,128)(2,1)S(1)} %get-tuple-element.91), channel_id=1, source_target_pairs={{1,9},{0,10},{3,11},{2,8},{5,13},{4,14},{7,15},{6,12},{9,1},{8,2},... | collective-permute-start | bytes 196616 | tf_op jit(solution)/shard_map/ppermute | solution.py:280
  26.7 6.7 %collective-permute-start.15 = (bf16[64,512]{1,0:T(8,128)(2,1)S(1)}, bf16[64,512]{1,0:T(8,128)(2,1)S(1)}, u32[]{:S(2)}, u32[]{:S(2)}) collective-permute-start(bf16[64,512]{1,0:T(8,128)(2,1)S(1)} %get-tuple-element.92), channel_id=1, source_target_pairs={{1,5},{0,6},{3,7},{2,4},{5,1},{4,2},{7,3},{6,0},{9,13},{8,14},{11,... | collective-permute-start | bytes 196616 | tf_op jit(solution)/shard_map/ppermute | solution.py:280
  28.8 5.1 %collective-permute-start.9 = (bf16[32,512]{1,0:T(8,128)(2,1)S(1)}, bf16[32,512]{1,0:T(8,128)(2,1)S(1)}, u32[]{:S(2)}, u32[]{:S(2)}) collective-permute-start(bf16[32,512]{1,0:T(8,128)(2,1)S(1)} %get-tuple-element.88), channel_id=1, source_target_pairs={{0,2},{2,0},{4,6},{6,4},{8,10},{10,8},{12,14},{14,12},{1,3},{3,1},... | collective-permute-start | bytes 98312 | tf_op jit(solution)/shard_map/ppermute | solution.py:285
  30.3 4.8 %collective-permute-start.12 = (bf16[32,512]{1,0:T(8,128)(2,1)S(1)}, bf16[32,512]{1,0:T(8,128)(2,1)S(1)}, u32[]{:S(2)}, u32[]{:S(2)}) collective-permute-start(bf16[32,512]{1,0:T(8,128)(2,1)S(1)} %slice.17), channel_id=1, source_target_pairs={{0,1},{1,0},{2,3},{3,2},{4,5},{5,4},{6,7},{7,6},{8,9},{9,8},{10,11... | collective-permute-start | bytes 98312 | tf_op jit(solution)/shard_map/ppermute | solution.py:272
  33.4 1.7 %collective-permute-start.14 = (bf16[32,512]{1,0:T(8,128)(2,1)S(1)}, bf16[32,512]{1,0:T(8,128)(2,1)S(1)}, u32[]{:S(2)}, u32[]{:S(2)}) collective-permute-start(bf16[32,512]{1,0:T(8,128)(2,1)S(1)} %slice.18), channel_id=1, source_target_pairs={{0,1},{1,0},{2,3},{3,2},{4,5},{5,4},{6,7},{7,6},{8,9},{9,8},{10,11... | collective-permute-start | bytes 98312 | tf_op jit(solution)/shard_map/ppermute | solution.py:272
  33.4 1.7 %collective-permute-start.16 = (bf16[32,512]{1,0:T(8,128)(2,1)S(1)}, bf16[32,512]{1,0:T(8,128)(2,1)S(1)}, u32[]{:S(2)}, u32[]{:S(2)}) collective-permute-start(bf16[32,512]{1,0:T(8,128)(2,1)S(1)} %slice.19), channel_id=1, source_target_pairs={{0,1},{1,0},{2,3},{3,2},{4,5},{5,4},{6,7},{7,6},{8,9},{9,8},{10,11... | collective-permute-start | bytes 98312 | tf_op jit(solution)/shard_map/ppermute | solution.py:272
  33.9 1.2 %collective-permute-start.10 = (bf16[16,512]{1,0:T(8,128)(2,1)S(1)}, bf16[16,512]{1,0:T(8,128)(2,1)S(1)}, u32[]{:S(2)}, u32[]{:S(2)}) collective-permute-start(bf16[16,512]{1,0:T(8,128)(2,1)S(1)} %slice.16), channel_id=1, source_target_pairs={{0,1},{1,0},{2,3},{3,2},{4,5},{5,4},{6,7},{7,6},{8,9},{9,8},{10,11... | collective-permute-start | bytes 49160 | tf_op jit(solution)/shard_map/ppermute | solution.py:272
